TPU v7x, 32 devices: a whole 2x2x4 slice. The times are simulated.
32 devices in a mesh: group: 2 (over y), row: 4 (over z), col: 4 (over x, core).
Axes of the slice: x: 2, y: 2, z: 4, core: 2. Of those that a mesh axis runs over, the one named last changes fastest.
Arguments:
- pair_acts: bfloat16 [128, 64, 128], P(('group', 'row'), 'col'), parts along dimension 0, may hold values from -6 to 6
- pair_mask: int32 [128, 64], P(('group', 'row'), 'col'), parts along dimension 0, may hold values 0 or 1
- crop_length: int32 [2], P('group'), parts along dimension 0, may hold values from 32 to 64
- cotangent: bfloat16 [128, 64, 128], P(('group', 'row'), 'col'), parts along dimension 0, may hold values from -6 to 6
- in_weights: bfloat16 [128, 640], replicated, may hold values from -0.5 to 0.5
- out_weight: bfloat16 [128, 128], replicated, may hold values from -0.5 to 0.5
Outputs:
- update: bfloat16 [128, 64, 128], P(('group', 'row'), 'col'), parts along dimension 0
- pair_grad: bfloat16 [128, 64, 128], P(('group', 'row'), 'col'), parts along dimension 0
There are 2 independent parts, one for each index of `group`. A program takes and returns all parts, laid end to end along the dimension named above; an argument that names none is the same for every part. Nothing has to cross between parts.
Inputs may be any that keep to these rules, and one draw needn't show every extreme that they name: `pair_mask`: 1 marks a token pair that takes part, 0 one that does not. Tokens at positions crop_length and beyond are padding.
All inputs are finite; a program needn't handle non-finite values. No bound on the sum of `pair_mask` on one device may be relied on, other than what follows from the above.
Results may differ from a plain program's by a relative error of at most 0.014.
Values may be sent and summed in bfloat16 or wider, within the bound.
No kernel may reach another device: no remote copies, remote signals or barrier semaphores. Data moves between devices by JAX's collectives and lax.ppermute only.
A program may use at most 128 MiB of HBM per device.

v0:
```python
import jax
import jax.numpy as jnp
from jax import lax
from jax.sharding import PartitionSpec as P

epsilon = 1e-05


def normalize(values):
    center = values - jnp.mean(values, axis=-1, keepdims=True)
    variance = jnp.mean(center * center, axis=-1, keepdims=True)
    scale = lax.rsqrt(variance + epsilon)
    return (center * scale, scale)


def normalize_back(normed, scale, upstream):
    average = jnp.mean(upstream, axis=-1, keepdims=True)
    project = jnp.mean(upstream * normed, axis=-1, keepdims=True)
    return scale * (upstream - average - normed * project)


def local(pair_acts, pair_mask, crop_length, cotangent, in_weights, out_weight):
    tile_size = pair_acts.shape[0]
    channels = pair_acts.shape[2]
    grid_size = lax.axis_size("row")
    sub_rows = tile_size // grid_size
    offsets = lax.iota(jnp.int32, tile_size)
    row_live = (lax.axis_index("row") * tile_size + offsets < crop_length[0]).astype(jnp.float32)
    col_live = (lax.axis_index("col") * tile_size + offsets < crop_length[0]).astype(jnp.float32)
    pair_keep = (pair_mask.astype(jnp.float32) * row_live[:, None] * col_live[None, :])[:, :, None]
    normed, scale_in = normalize(pair_acts.astype(jnp.float32))
    projected = jnp.dot(
        normed.astype(jnp.bfloat16).reshape(-1, channels),
        in_weights,
        preferred_element_type=jnp.float32,
    ).reshape(tile_size, tile_size, 5, channels)
    left_value = projected[:, :, 0]
    left_gate = projected[:, :, 1]
    right_value = projected[:, :, 2]
    right_gate = projected[:, :, 3]
    out_gate = projected[:, :, 4]
    left_open = jax.nn.sigmoid(left_gate)
    right_open = jax.nn.sigmoid(right_gate)
    out_open = jax.nn.sigmoid(out_gate)
    left_tile = (left_open * left_value * pair_keep).astype(jnp.bfloat16)
    right_tile = (right_open * right_value * pair_keep).astype(jnp.bfloat16)
    mirrored = lax.all_to_all(
        lax.all_to_all(left_tile, "col", split_axis=0, concat_axis=1, tiled=True),
        "row",
        split_axis=1,
        concat_axis=0,
        tiled=True,
    )
    left_panel = lax.all_gather(mirrored, "col", axis=0, tiled=True)
    right_panel = lax.all_gather(right_tile, "row", axis=0, tiled=True)
    left_split = left_panel.reshape(grid_size, grid_size, sub_rows, tile_size, channels)
    right_split = right_panel.reshape(grid_size, grid_size, sub_rows, tile_size, channels)
    triangle = jnp.einsum(
        "pqsic,qpsjc->ijc", left_split, right_split, preferred_element_type=jnp.float32
    )
    tri_normed, tri_scale = normalize(triangle)
    linear = jnp.dot(
        tri_normed.astype(jnp.bfloat16).reshape(-1, channels),
        out_weight,
        preferred_element_type=jnp.float32,
    ).reshape(tile_size, tile_size, channels)
    update = (out_open * linear).astype(jnp.bfloat16)
    upstream = cotangent.astype(jnp.float32)
    lin_grad = (upstream * out_open).astype(jnp.bfloat16)
    out_gate_grad = upstream * linear * out_open * (1.0 - out_open)
    tri_normed_grad = jnp.dot(
        lin_grad.reshape(-1, channels), out_weight.T, preferred_element_type=jnp.float32
    ).reshape(tile_size, tile_size, channels)
    tri_grad = normalize_back(tri_normed, tri_scale, tri_normed_grad).astype(jnp.bfloat16)
    left_terms = jnp.einsum(
        "ijc,qpsjc->pqsic", tri_grad, right_split, preferred_element_type=jnp.float32
    ).reshape(grid_size * tile_size, tile_size, channels)
    left_summed = lax.psum_scatter(
        left_terms.astype(jnp.bfloat16), "col", scatter_dimension=0, tiled=True
    ).astype(jnp.float32)
    left_grad = lax.all_to_all(
        lax.all_to_all(
            left_summed.astype(jnp.bfloat16), "row", split_axis=0, concat_axis=1, tiled=True
        ),
        "col",
        split_axis=1,
        concat_axis=0,
        tiled=True,
    ).astype(left_summed.dtype)
    right_terms = jnp.einsum(
        "ijc,pqsic->qpsjc", tri_grad, left_split, preferred_element_type=jnp.float32
    ).reshape(grid_size * tile_size, tile_size, channels)
    right_grad = lax.psum_scatter(
        right_terms.astype(jnp.bfloat16), "row", scatter_dimension=0, tiled=True
    ).astype(jnp.float32)
    left_back = left_grad * pair_keep
    right_back = right_grad * pair_keep
    grads = jnp.stack(
        [
            left_back * left_open,
            left_back * left_value * left_open * (1.0 - left_open),
            right_back * right_open,
            right_back * right_value * right_open * (1.0 - right_open),
            out_gate_grad,
        ],
        axis=2,
    )
    normed_grad = jnp.dot(
        grads.astype(jnp.bfloat16).reshape(-1, 5 * channels),
        in_weights.T,
        preferred_element_type=jnp.float32,
    ).reshape(tile_size, tile_size, channels)
    pair_grad = normalize_back(normed, scale_in, normed_grad).astype(jnp.bfloat16)
    return (update, pair_grad)


def solution(mesh):
    return jax.shard_map(
        local,
        mesh=mesh,
        in_specs=(
            P(("group", "row"), "col", None),
            P(("group", "row"), "col"),
            P("group"),
            P(("group", "row"), "col", None),
            P(),
            P(),
        ),
        out_specs=(P(("group", "row"), "col", None), P(("group", "row"), "col", None)),
        check_vma=False,
    )
```

profile of v0, /device:TPU:0, one launch (start us, length us, event | category | flops | bytes accessed | tf_op | source)
XLA Modules:
  0.0 141.2 jit_solution(12927319792015184519)
XLA Ops:
  8.0 0.9 convert_reduce_fusion
  9.0 1.0 fusion.13
  10.0 1.1 copy.236
  11.8 1.1 fusion.48
  13.8 8.1 %all_to_all.63 = bf16[16,16,128]{2,1,0:T(8,128)(2,1)S(1)} all-to-all(bf16[16,16,128]{2,1,0:T(8,128)(2,1)S(1)} %get-tuple-element.6), channel_id=1, replica_groups=mesh['group'=2,'row'=4,'col'=4] {'col'}, dimensions={0} | all-to-all | bytes 131072 | tf_op jit(solution)/shard_map/all_to_all | solution.py:48
  22.6 4.9 %all-to-all-start.1 = ((bf16[4,64,128]{2,0,1:T(4,128)(2,1)}), bf16[4,64,128]{2,0,1:T(4,128)(2,1)S(1)}, u32[]{:S(2)}, u32[]{:S(2)}) async-start(bf16[4,64,128]{2,0,1:T(4,128)(2,1)} %copy.243), calls=%async_computation.1 | async-start | bytes 131072 | tf_op jit(solution)/shard_map/all_to_all | solution.py:47
  27.5 14.5 %all_gather.6 = bf16[64,16,128]{2,1,0:T(8,128)(2,1)S(1)} all-gather(bf16[16,16,128]{2,1,0:T(8,128)(2,1)S(1)} %get-tuple-element.7), channel_id=1, replica_groups=mesh['group'=2,'row'=4,'col'=4] {'row'}, dimensions={0}, use_global_device_ids=true | all-gather | bytes 327680 | tf_op jit(solution)/shard_map/all_gather | solution.py:55
  42.0 2.9 %copy.246 = bf16[4,4,4,16,128]{3,2,0,1,4:T(4,128)(2,1)} copy(bf16[4,4,4,16,128]{4,3,2,1,0:T(8,128)(2,1)S(1)} %bitcast.222) | data formatting | bytes 524288 | tf_op jit(solution)/shard_map/reshape | solution.py:57
  44.8 2.9 %copy.255 = bf16[4,4,4,16,128]{3,2,1,0,4:T(4,128)(2,1)} copy(bf16[4,4,4,16,128]{4,3,2,1,0:T(8,128)(2,1)S(1)} %bitcast.223) | data formatting | bytes 524288 | tf_op jit(solution)/shard_map/reshape | solution.py:57
  47.8 5.8 %all_gather.7 = bf16[64,16,128]{2,1,0:T(8,128)(2,1)S(1)} all-gather(bf16[16,16,128]{2,1,0:T(8,128)(2,1)S(1)} %bitcast.229), channel_id=1, replica_groups=mesh['group'=2,'row'=4,'col'=4] {'col'}, dimensions={0}, use_global_device_ids=true | all-gather | bytes 327680 | tf_op jit(solution)/shard_map/all_gather | solution.py:54
  53.6 1.8 %copy.247 = bf16[4,4,4,16,128]{3,2,1,0,4:T(4,128)(2,1)S(1)} copy(bf16[4,4,4,16,128]{4,3,2,1,0:T(8,128)(2,1)S(1)} %bitcast.224) | data formatting | bytes 524288 | tf_op jit(solution)/shard_map/reshape | solution.py:56
  55.4 4.8 %bitcast_reduce_fusion = (f32[16,16]{0,1:T(8,128)S(1)}, f32[128,16,16,1,1]{2,1,4,3,0:T(8,128)}) fusion(bf16[4,4,4,16,128]{3,2,0,1,4:T(4,128)(2,1)} %copy.246, bf16[4,4,4,16,128]{3,2,1,0,4:T(4,128)(2,1)S(1)} %copy.247), kind=kOutput, calls=%fused_computation.2 | convolution fusion | flops 4226816 | bytes 656384 | tf_op jit(solution)/shard_map/pqsic,qpsjc->ijc/dot_general | solution.py:58
  60.2 1.6 %copy.248 = f32[128,16,16]{0,1,2:T(8,128)S(1)} copy(f32[128,16,16]{2,1,0:T(8,128)} %bitcast.227) | data formatting | bytes 262144 | tf_op jit(solution)/shard_map/pqsic,qpsjc->ijc/dot_general | solution.py:58
  63.1 4.6 %convert_bitcast_fusion.1 = bf16[4,4,4,16,128]{3,2,0,1,4:T(4,128)(2,1)} fusion(bf16[4,4,4,16,128]{3,2,1,0,4:T(4,128)(2,1)} %copy.255, bf16[16,16,128,1,1]{1,0,4,3,2:T(8,128)(2,1)S(1)} %copy.274), kind=kOutput, calls=%fused_computation.1 | convolution fusion | flops 4325376 | bytes 589824 | tf_op jit(solution)/shard_map/ijc,qpsjc->pqsic/dot_general | solution.py:75
  67.8 4.1 %copy.257 = bf16[4,4,4,16,128]{4,3,2,1,0:T(8,128)(2,1)} copy(bf16[4,4,4,16,128]{3,2,0,1,4:T(4,128)(2,1)} %convert_bitcast_fusion.1) | data formatting | bytes 524288 | tf_op jit(solution)/shard_map/convert_element_type | solution.py:79
  71.9 20.3 %reduce-scatter.3.cloned.1.call-done = bf16[16,16,128]{2,1,0:T(8,128)(2,1)} async-done(((bf16[64,16,128]{2,1,0:T(8,128)(2,1)}), bf16[16,16,128]{2,1,0:T(8,128)(2,1)}) %reduce-scatter.3.cloned.1.call-update) | async-done | bytes 65552 | tf_op jit(solution)/shard_map/reduce_scatter | solution.py:78
  92.2 4.6 %all-to-all-start.2 = ((bf16[16,16,128]{2,1,0:T(8,128)(2,1)}), bf16[16,16,128]{2,1,0:T(8,128)(2,1)S(1)}, u32[]{:S(2)}, u32[]{:S(2)}) async-start(bf16[16,16,128]{2,1,0:T(8,128)(2,1)} %reduce-scatter.3.cloned.1.call-done), calls=%async_computation.3 | async-start | bytes 131072 | tf_op jit(solution)/shard_map/all_to_all | solution.py:82
  96.8 2.4 %convert_bitcast_fusion = bf16[4,4,4,16,128]{3,2,0,1,4:T(4,128)(2,1)} fusion(bf16[4,4,4,16,128]{3,2,1,0,4:T(4,128)(2,1)S(1)} %copy.247, bf16[16,16,128,1,1]{1,0,4,3,2:T(8,128)(2,1)S(1)} %copy.274), kind=kOutput, calls=%fused_computation | convolution fusion | flops 4325376 | bytes 589824 | tf_op jit(solution)/shard_map/ijc,pqsic->qpsjc/dot_general | solution.py:90
  99.2 3.3 %all-to-all-done.2 = bf16[16,16,128]{2,1,0:T(8,128)(2,1)S(1)} async-done(((bf16[16,16,128]{2,1,0:T(8,128)(2,1)}), bf16[16,16,128]{2,1,0:T(8,128)(2,1)S(1)}, u32[]{:S(2)}, u32[]{:S(2)}) %all-to-all-start.2) | async-done | bytes 65568 | tf_op jit(solution)/shard_map/all_to_all | solution.py:82
  103.2 3.3 %all-to-all-start.3 = ((bf16[4,64,128]{2,0,1:T(4,128)(2,1)}), bf16[4,64,128]{2,0,1:T(4,128)(2,1)S(1)}, u32[]{:S(2)}, u32[]{:S(2)}) async-start(bf16[4,64,128]{2,0,1:T(4,128)(2,1)} %copy.259), calls=%async_computation.4 | async-start | bytes 131072 | tf_op jit(solution)/shard_map/all_to_all | solution.py:81
  107.5 4.2 %copy.267 = bf16[4,4,4,16,128]{4,3,2,1,0:T(8,128)(2,1)} copy(bf16[4,4,4,16,128]{3,2,0,1,4:T(4,128)(2,1)} %convert_bitcast_fusion) | data formatting | bytes 524288 | tf_op jit(solution)/shard_map/convert_element_type | solution.py:94
  112.0 18.5 %reduce-scatter.5.cloned.1.call-done = bf16[16,16,128]{2,1,0:T(8,128)(2,1)} async-done(((bf16[64,16,128]{2,1,0:T(8,128)(2,1)}), bf16[16,16,128]{2,1,0:T(8,128)(2,1)}) %reduce-scatter.5.cloned.1.call-update) | async-done | bytes 65552 | tf_op jit(solution)/shard_map/reduce_scatter | solution.py:93
  130.5 1.0 fusion.40
  131.4 1.0 fusion.42
  (47 shorter events, 6.0 us)
Async XLA Ops:
  8.0 54.2 %copy-start = (bf16[128,128]{1,0:T(8,128)(2,1)S(1)}, bf16[128,128]{1,0:T(8,128)(2,1)}, u32[]{:S(2)}) copy-start(bf16[128,128]{1,0:T(8,128)(2,1)} %param.11) | copy-start | bytes 98308
  22.6 25.1 %all-to-all-start.1 = ((bf16[4,64,128]{2,0,1:T(4,128)(2,1)}), bf16[4,64,128]{2,0,1:T(4,128)(2,1)S(1)}, u32[]{:S(2)}, u32[]{:S(2)}) async-start(bf16[4,64,128]{2,0,1:T(4,128)(2,1)} %copy.243), calls=%async_computation.1 | async-start | bytes 131072 | tf_op jit(solution)/shard_map/all_to_all | solution.py:47
  27.5 64.7 %reduce-scatter.3.cloned.1.call-start = ((), (), s32[]{:S(2)}) async-start(), calls=%async_computation.6 | async-start | bytes 327680 | tf_op jit(solution)/shard_map/reduce_scatter | solution.py:78
  55.4 6.7 %copy-start.3 = (bf16[16,16,128]{2,1,0:T(8,128)(2,1)S(1)}, bf16[16,16,128]{2,1,0:T(8,128)(2,1)}, u32[]{:S(2)}) copy-start(bf16[16,16,128]{2,1,0:T(8,128)(2,1)} %param.9) | copy-start | bytes 196612
  92.2 10.3 %all-to-all-start.2 = ((bf16[16,16,128]{2,1,0:T(8,128)(2,1)}), bf16[16,16,128]{2,1,0:T(8,128)(2,1)S(1)}, u32[]{:S(2)}, u32[]{:S(2)}) async-start(bf16[16,16,128]{2,1,0:T(8,128)(2,1)} %reduce-scatter.3.cloned.1.call-done), calls=%async_computation.3 | async-start | bytes 131072 | tf_op jit(solution)/shard_map/all_to_all | solution.py:82
  103.2 8.4 %all-to-all-start.3 = ((bf16[4,64,128]{2,0,1:T(4,128)(2,1)}), bf16[4,64,128]{2,0,1:T(4,128)(2,1)S(1)}, u32[]{:S(2)}, u32[]{:S(2)}) async-start(bf16[4,64,128]{2,0,1:T(4,128)(2,1)} %copy.259), calls=%async_computation.4 | async-start | bytes 131072 | tf_op jit(solution)/shard_map/all_to_all | solution.py:81
  106.5 23.9 %reduce-scatter.5.cloned.1.call-start = ((), (), s32[]{:S(2)}) async-start(), calls=%async_computation.7 | async-start | bytes 327680 | tf_op jit(solution)/shard_map/reduce_scatter | solution.py:93
  107.5 24.9 %copy-start.4 = (bf16[16,16,128]{2,1,0:T(8,128)(2,1)S(1)}, bf16[16,16,128]{2,1,0:T(8,128)(2,1)}, u32[]{:S(2)}) copy-start(bf16[16,16,128]{2,1,0:T(8,128)(2,1)} %param.9) | copy-start | bytes 196612
  107.5 25.0 %copy-start.1 = (bf16[16,16,128]{2,1,0:T(8,128)(2,1)S(1)}, bf16[16,16,128]{2,1,0:T(8,128)(2,1)}, u32[]{:S(2)}) copy-start(bf16[16,16,128]{2,1,0:T(8,128)(2,1)} %param.6) | copy-start | bytes 196612
  107.5 25.0 %copy-start.2 = (bf16[128,640]{1,0:T(8,128)(2,1)S(1)}, bf16[128,640]{1,0:T(8,128)(2,1)}, u32[]{:S(2)}) copy-start(bf16[128,640]{1,0:T(8,128)(2,1)} %param.10) | copy-start | bytes 491524
Sparse Core Ops, SparseCore 0:
  72.0 20.1 reduce-scatter.2
Sparse Core Ops, SparseCore 1:
  111.8 18.7 reduce-scatter.4
where the time goes:
time: 142 us; the launch traced here: 141 us
  waiting for transfers between devices  42.1 us (30%)
  blocking collectives  28.4 us (20%)
  local copies, waits for them, and re-layouts  20.6 us (15%)
  between operations  16.4 us (12%)
  matrix products  14.5 us (10%)
  starting transfers between devices  12.8 us (9%)
  other arithmetic  6.34 us (4%)
    reduce_scatter x1, waiting for transfers between devices, local(): lax.psum_scatter(left_terms.astype(jnp.bfloat16), 'col', scatter_dimensio...  20.3 us
    reduce_scatter x1, waiting for transfers between devices, local(): lax.psum_scatter(right_terms.astype(jnp.bfloat16), 'row', scatter_dimensi...  18.5 us
    all_gather x1, blocking collectives, local(): right_panel = lax.all_gather(right_tile, 'row', axis=0, tiled=True)  14.5 us
    all_to_all x1, blocking collectives, local(): lax.all_to_all(left_tile, 'col', split_axis=0, concat_axis=1, tiled=True)  8.13 us
    all_gather x1, blocking collectives, local(): left_panel = lax.all_gather(mirrored, 'col', axis=0, tiled=True)  5.79 us
    reshape x2, local copies, waits for them, and re-layouts, local(): right_panel.reshape(grid_size, grid_size, sub_rows, tile_size, channels)  5.77 us
    all_to_all x1, starting transfers between devices, local(): lax.all_to_all(lax.all_to_all(left_tile, 'col', split_axis=0, concat_axis...  4.87 us
    dot_general x1, matrix products, local(): jnp.einsum('pqsic,qpsjc->ijc', left_split, right_split, preferred_element...  4.8 us
  transfers between devices with their start and end apart: 5, of which 3 were waited for; matrix products, arithmetic and copies ran while one was open for 10% of the time, Pallas kernels for 0%

commit v1 on v0

v1 whole, which is shorter than its diff:
```python
import functools

import jax
import jax.numpy as jnp
from jax import lax
from jax.experimental import pallas as pl
from jax.experimental.pallas import tpu as pltpu
from jax.sharding import PartitionSpec as P

epsilon = 1e-05
f32 = jnp.float32
bf16 = jnp.bfloat16


def mean_lanes(values):
    return jnp.sum(values, axis=-1, keepdims=True) * (1.0 / values.shape[-1])


def normalize(values):
    center = values - mean_lanes(values)
    variance = mean_lanes(center * center)
    scale = lax.rsqrt(variance + epsilon)
    return (center * scale, scale)


def normalize_back(normed, scale, upstream):
    average = mean_lanes(upstream)
    project = mean_lanes(upstream * normed)
    return scale * (upstream - average - normed * project)


def sigmoid(values):
    return 1.0 / (1.0 + jnp.exp(-values))


def dot(a, b):
    return jnp.dot(a, b, preferred_element_type=f32)


def dot_t(a, b):
    return lax.dot_general(a, b, (((1,), (1,)), ((), ())), preferred_element_type=f32)


def keep_rows(mask_ref, crop_ref):
    size = mask_ref.shape[0]
    rows = lax.axis_index("row") * size + lax.broadcasted_iota(jnp.int32, (size, size), 0)
    cols = lax.axis_index("col") * size + lax.broadcasted_iota(jnp.int32, (size, size), 1)
    live = jnp.where(jnp.maximum(rows, cols) < crop_ref[0], 1.0, 0.0)
    keep = (mask_ref[...].astype(f32) * live).astype(bf16)
    pair = lax.broadcasted_iota(jnp.int32, (size * size, size), 0)
    lane = lax.broadcasted_iota(jnp.int32, (size * size, size), 1)
    pick_row = jnp.where(pair // size == lane, 1.0, 0.0).astype(bf16)
    pick_col = jnp.where(pair % size == lane, 1.0, 0.0)
    spread = (dot(pick_row, keep) * pick_col).astype(bf16)
    return dot(spread, jnp.ones((size, 128), bf16))


def tiles_kernel(acts_ref, mask_ref, crop_ref, weights_ref, left_ref, right_ref):
    size, _, channels = acts_ref.shape
    normed, _ = normalize(acts_ref[...].astype(f32).reshape(size * size, channels))
    projected = dot(normed.astype(bf16), weights_ref[:, : 4 * channels])
    keep = keep_rows(mask_ref, crop_ref)
    for block, out_ref in ((0, left_ref), (2, right_ref)):
        value = projected[:, block * channels : (block + 1) * channels]
        gate = projected[:, (block + 1) * channels : (block + 2) * channels]
        tile = (sigmoid(gate) * value * keep).astype(bf16)
        out_ref[...] = tile.reshape(size, size, channels)


def factors_kernel(
    acts_ref, mask_ref, crop_ref, cotangent_ref, weights_ref, out_weight_ref,
    normed_ref, scale_ref, factor_ref, open_ref, gate_factor_ref, upstream_ref,
):
    size, _, channels = acts_ref.shape
    pairs = size * size
    normed, scale = normalize(acts_ref[...].astype(f32).reshape(pairs, channels))
    normed_ref[...] = normed
    scale_ref[...] = jnp.broadcast_to(scale, (pairs, channels))
    projected = dot(normed.astype(bf16), weights_ref[...])
    keep = keep_rows(mask_ref, crop_ref)
    for block in (0, 2):
        value = projected[:, block * channels : (block + 1) * channels]
        gate = projected[:, (block + 1) * channels : (block + 2) * channels]
        opened = sigmoid(gate)
        factor_ref[block] = keep * opened
        factor_ref[block + 1] = keep * value * opened * (1.0 - opened)
    out_open = sigmoid(projected[:, 4 * channels :])
    cotangent = cotangent_ref[...].astype(f32).reshape(pairs, channels)
    lin_grad = (cotangent * out_open).astype(bf16)
    open_ref[...] = out_open
    gate_factor_ref[...] = cotangent * out_open * (1.0 - out_open)
    upstream_ref[...] = dot_t(lin_grad, out_weight_ref[...])


def triangle_kernel(grid_size, *refs):
    left_in, right_in = refs[:grid_size], refs[grid_size : 2 * grid_size]
    upstream_ref = refs[2 * grid_size]
    outs = refs[2 * grid_size + 1 :]
    tri_normed_ref = outs[0]
    left_out, right_out = outs[1 : grid_size + 1], outs[grid_size + 1 : 2 * grid_size + 1]
    left, right, grad = outs[2 * grid_size + 1 :]
    size, _, channels = left_in[0].shape
    row, col = lax.axis_index("row"), lax.axis_index("col")
    for shift in range(grid_size):
        start = lax.rem(col + (grid_size - shift), grid_size) * size
        left[pl.ds(start, size)] = left_in[shift][...].astype(f32)
        start = lax.rem(row + (grid_size - shift), grid_size) * size
        right[pl.ds(start, size)] = right_in[shift][...].astype(f32)

    def step(k, sums):
        other = right[k]
        return tuple(sums[i] + left[k, pl.ds(i, 1), :] * other for i in range(size))

    zero = jnp.zeros((size, channels), f32)
    sums = lax.fori_loop(0, grid_size * size, step, (zero,) * size)
    for i in range(size):
        here = pl.ds(i * size, size)
        tri_normed, scale = normalize(sums[i])
        tri_normed_ref[here, :] = tri_normed
        back = normalize_back(tri_normed, scale, upstream_ref[here, :])
        grad[here, :] = back.astype(bf16).astype(f32)

    grads = [grad[pl.ds(i * size, size), :] for i in range(size)]
    for shift in range(grid_size):
        start = lax.rem(row + shift, grid_size) * size
        out = right_out[shift]

        def step(k, _):
            total = left[start + k, pl.ds(0, 1), :] * grads[0]
            for i in range(1, size):
                total = total + left[start + k, pl.ds(i, 1), :] * grads[i]
            out[k] = total.astype(bf16)
            return 0

        lax.fori_loop(0, size, step, 0)

    grads_t = [grad[pl.ds(j, size, stride=size), :] for j in range(size)]
    for shift in range(grid_size):
        start = lax.rem(col + shift, grid_size) * size
        out = left_out[shift]

        def step(k, _):
            total = right[start + k, pl.ds(0, 1), :] * grads_t[0]
            for j in range(1, size):
                total = total + right[start + k, pl.ds(j, 1), :] * grads_t[j]
            out[k] = total.astype(bf16)
            return 0

        lax.fori_loop(0, size, step, 0)


def update_kernel(
    tri_normed_ref, open_ref, gate_factor_ref, weights_ref, out_weight_ref, update_ref, normed_grad_ref
):
    size, _, channels = update_ref.shape
    linear = dot(tri_normed_ref[...].astype(bf16), out_weight_ref[...])
    update = (open_ref[...] * linear).astype(bf16)
    update_ref[...] = update.reshape(size, size, channels)
    out_gate_grad = (gate_factor_ref[...] * linear).astype(bf16)
    normed_grad_ref[...] = dot_t(out_gate_grad, weights_ref[:, 4 * channels :])


def sum_kernel(grid_size, *refs):
    total = refs[0][...].astype(f32)
    for ref in refs[1:grid_size]:
        total = total + ref[...].astype(f32)
    refs[grid_size][...] = total.astype(bf16)


def back_kernel(grid_size, left_ref, *refs):
    right_in = refs[:grid_size]
    normed_ref, scale_ref, factor_ref, partial_ref, weights_ref, out_ref = refs[grid_size:]
    size, _, channels = out_ref.shape
    pairs = size * size
    left = left_ref[...].astype(f32).reshape(pairs, channels)
    right = right_in[0][...].astype(f32)
    for ref in right_in[1:]:
        right = right + ref[...].astype(f32)
    right = right.astype(bf16).astype(f32).reshape(pairs, channels)
    grads = jnp.concatenate(
        [(total * factor_ref[block]).astype(bf16) for block, total in enumerate((left, left, right, right))],
        axis=1,
    )
    normed_grad = partial_ref[...] + dot_t(grads, weights_ref[:, : 4 * channels])
    back = normalize_back(normed_ref[...], scale_ref[...], normed_grad)
    out_ref[...] = back.astype(bf16).reshape(size, size, channels)


def call(kernel, outs, *args, scratch=(), flops=0, smem=()):
    spec = pl.BlockSpec(memory_space=pltpu.VMEM)
    total = sum(a.size * a.dtype.itemsize for a in (*args, *outs))
    return pl.pallas_call(
        kernel,
        out_shape=tuple(outs),
        in_specs=[pl.BlockSpec(memory_space=pltpu.SMEM) if n in smem else spec for n in range(len(args))],
        out_specs=(spec,) * len(outs),
        scratch_shapes=scratch,
        compiler_params=pltpu.CompilerParams(vmem_limit_bytes=24 * 2**20),
        cost_estimate=pl.CostEstimate(flops=flops, bytes_accessed=total, transcendentals=0),
    )(*args)


def local(pair_acts, pair_mask, crop_length, cotangent, in_weights, out_weight):
    size, _, channels = pair_acts.shape
    pairs = size * size
    n = lax.axis_size("row")
    tile = jax.ShapeDtypeStruct((size, size, channels), bf16)
    flat = jax.ShapeDtypeStruct((pairs, channels), f32)

    def shift_by(values, axis, shift):
        if shift == 0:
            return values
        return lax.ppermute(values, axis, [(a, (a + shift) % n) for a in range(n)])

    def mirror(values):
        return lax.ppermute(values, ("row", "col"), [(a * n + b, b * n + a) for a in range(n) for b in range(n)])

    left, right = call(
        tiles_kernel, (tile, tile), pair_acts, pair_mask, crop_length, in_weights,
        smem=(2,), flops=2 * pairs * channels * 4 * channels,
    )
    mirrored = mirror(left)
    rights = [shift_by(right, "row", shift) for shift in range(n)]
    normed, scale, factors, out_open, gate_factor, upstream = call(
        factors_kernel,
        (flat, flat, jax.ShapeDtypeStruct((4, pairs, channels), f32), flat, flat, flat),
        pair_acts, pair_mask, crop_length, cotangent, in_weights, out_weight,
        smem=(2,), flops=2 * pairs * channels * 6 * channels,
    )
    lefts = [shift_by(mirrored, "col", shift) for shift in range(n)]
    tri_normed, *terms = call(
        functools.partial(triangle_kernel, n),
        (flat,) + (tile,) * (2 * n),
        *lefts, *rights, upstream,
        scratch=[
            pltpu.VMEM((n * size, size, channels), f32),
            pltpu.VMEM((n * size, size, channels), f32),
            pltpu.VMEM((pairs, channels), f32),
        ],
        flops=6 * n * size * pairs * channels,
    )
    left_terms = [shift_by(values, "col", shift) for shift, values in enumerate(terms[:n])]
    right_terms = [shift_by(values, "row", shift) for shift, values in enumerate(terms[n:])]
    update, partial = call(
        update_kernel, (tile, flat), tri_normed, out_open, gate_factor, in_weights, out_weight,
        flops=4 * pairs * channels * channels,
    )
    (left_sum,) = call(functools.partial(sum_kernel, n), (tile,), *left_terms)
    left_grad = mirror(left_sum)
    (pair_grad,) = call(
        functools.partial(back_kernel, n), (tile,),
        left_grad, *right_terms, normed, scale, factors, partial, in_weights,
        flops=2 * pairs * channels * 4 * channels,
    )
    return (update, pair_grad)


def solution(mesh):
    return jax.shard_map(
        local,
        mesh=mesh,
        in_specs=(
            P(("group", "row"), "col", None),
            P(("group", "row"), "col"),
            P("group"),
            P(("group", "row"), "col", None),
            P(),
            P(),
        ),
        out_specs=(P(("group", "row"), "col", None), P(("group", "row"), "col", None)),
        check_vma=False,
    )
```

time: 142 us -> 40.7 us (0.29)
  the two profiles are of different devices: /device:TPU:0 before, /device:TPU:6 now
where the time goes in v1:
time: 40.7 us; the launch traced here: 40.4 us
  starting transfers between devices  17.9 us (44%)
  waiting for transfers between devices  11.6 us (29%)
  Pallas kernels  7.09 us (17%)
  local copies, waits for them, and re-layouts  2.46 us (6%)
  between operations  1.36 us (3%)
    ppermute x12, starting transfers between devices, shift_by(): return lax.ppermute(values, axis, [(a, (a + shift) % n) for a in range(n)])  9.91 us
    ppermute x2, starting transfers between devices, mirror(): lax.ppermute(values, ('row', 'col'), [(a * n + b, b * n + a) for a in ran...  8.02 us
    ppermute x2, waiting for transfers between devices, mirror(): lax.ppermute(values, ('row', 'col'), [(a * n + b, b * n + a) for a in ran...  7.46 us
    pallas_call x6, Pallas kernels, call(): pl.pallas_call(kernel, out_shape=tuple(outs), in_specs=[pl.BlockSpec(memo...  7.09 us
    ppermute x12, waiting for transfers between devices, shift_by(): return lax.ppermute(values, axis, [(a, (a + shift) % n) for a in range(n)])  4.13 us
    unnamed x12, local copies, waits for them, and re-layouts  2.46 us
  transfers between devices with their start and end apart: 14, of which 5 were waited for; matrix products, arithmetic and copies ran while one was open for 0% of the time, Pallas kernels for 4%

profile of v1, /device:TPU:6, one launch (start us, length us, event | category | flops | bytes accessed | tf_op | source)
XLA Modules:
  0.0 40.4 jit_solution(1199404556704295618)
XLA Ops:
  1.3 0.9 %copy-done = bf16[128,640]{1,0:T(8,128)(2,1)S(1)} copy-done((bf16[128,640]{1,0:T(8,128)(2,1)S(1)}, bf16[128,640]{1,0:T(8,128)(2,1)}, u32[]{:S(2)}) %copy-start) | copy-done | bytes 163864
  2.2 0.8 %copy-done.2 = bf16[16,16,128]{2,1,0:T(8,128)(2,1)S(1)} copy-done((bf16[16,16,128]{2,1,0:T(8,128)(2,1)S(1)}, bf16[16,16,128]{2,1,0:T(8,128)(2,1)}, u32[]{:S(2)}) %copy-start.2) | copy-done | bytes 65560
  3.0 0.7 %copy-done.5 = s32[16,16]{1,0:T(8,128)S(1)} copy-done((s32[16,16]{1,0:T(8,128)S(1)}, s32[16,16]{1,0:T(8,128)}, u32[]{:S(2)}) %copy-start.5) | copy-done | bytes 1048
  3.7 0.6 %shard_map.77 = (bf16[16,16,128]{2,1,0:T(8,128)(2,1)S(1)}, bf16[16,16,128]{2,1,0:T(8,128)(2,1)S(1)}) custom-call(bf16[16,16,128]{2,1,0:T(8,128)(2,1)S(1)} %copy-done.2, s32[16,16]{1,0:T(8,128)S(1)} %copy-done.5, s32[1]{0:T(128)S(6)} %copy.8.crop_ref, bf16[128,640]{1,0:T(8,128)(2,1)S(1)} %copy-done), custom_call_target="tpu_custom_call" | custom-call | flops 33554432 | bytes 361476 | tf_op jit(solution)/shard_map/pallas_call | solution.py:192
  4.3 4.5 %collective-permute-start = (bf16[16,16,128]{2,1,0:T(8,128)(2,1)S(1)}, bf16[16,16,128]{2,1,0:T(8,128)(2,1)S(1)}, u32[]{:S(2)}, u32[]{:S(2)}) collective-permute-start(bf16[16,16,128]{2,1,0:T(8,128)(2,1)S(1)} %get-tuple-element.21), channel_id=1, source_target_pairs={{0,0},{1,4},{2,8},{3,12},{4,1},{5,5},{6,9},{7,13},{8,2},{9,6},{10,... | collective-permute-start | bytes 196616 | tf_op jit(solution)/shard_map/ppermute | solution.py:216
  8.8 1.1 %collective-permute-start.6 = (bf16[16,16,128]{2,1,0:T(8,128)(2,1)S(1)}, bf16[16,16,128]{2,1,0:T(8,128)(2,1)S(1)}, u32[]{:S(2)}, u32[]{:S(2)}) collective-permute-start(bf16[16,16,128]{2,1,0:T(8,128)(2,1)S(1)} %get-tuple-element.22.refs_4_), channel_id=1, source_target_pairs={{0,12},{4,0},{8,4},{12,8},{1,13},{5,1},{9,5},{13,9},{2,14},{6,2},{... | collective-permute-start | bytes 196616 | tf_op jit(solution)/shard_map/ppermute | solution.py:213
  9.9 0.4 %collective-permute-start.5 = (bf16[16,16,128]{2,1,0:T(8,128)(2,1)S(1)}, bf16[16,16,128]{2,1,0:T(8,128)(2,1)S(1)}, u32[]{:S(2)}, u32[]{:S(2)}) collective-permute-start(bf16[16,16,128]{2,1,0:T(8,128)(2,1)S(1)} %get-tuple-element.22.refs_4_), channel_id=1, source_target_pairs={{0,8},{4,12},{8,0},{12,4},{1,9},{5,13},{9,1},{13,5},{2,10},{6,14},... | collective-permute-start | bytes 196616 | tf_op jit(solution)/shard_map/ppermute | solution.py:213
  10.3 0.6 %collective-permute-start.4 = (bf16[16,16,128]{2,1,0:T(8,128)(2,1)S(1)}, bf16[16,16,128]{2,1,0:T(8,128)(2,1)S(1)}, u32[]{:S(2)}, u32[]{:S(2)}) collective-permute-start(bf16[16,16,128]{2,1,0:T(8,128)(2,1)S(1)} %get-tuple-element.22.refs_4_), channel_id=1, source_target_pairs={{0,4},{4,8},{8,12},{12,0},{1,5},{5,9},{9,13},{13,1},{2,6},{6,10},{... | collective-permute-start | bytes 196616 | tf_op jit(solution)/shard_map/ppermute | solution.py:213
  10.9 3.8 %collective-permute-done.refs_0_ = bf16[16,16,128]{2,1,0:T(8,128)(2,1)S(1)} collective-permute-done((bf16[16,16,128]{2,1,0:T(8,128)(2,1)S(1)}, bf16[16,16,128]{2,1,0:T(8,128)(2,1)S(1)}, u32[]{:S(2)}, u32[]{:S(2)}) %collective-permute-start) | collective-permute-done | bytes 65568 | tf_op jit(solution)/shard_map/ppermute | solution.py:216
  14.6 0.1 collective-permute-start.2
  14.7 0.4 %collective-permute-start.1 = (bf16[16,16,128]{2,1,0:T(8,128)(2,1)S(1)}, bf16[16,16,128]{2,1,0:T(8,128)(2,1)S(1)}, u32[]{:S(2)}, u32[]{:S(2)}) collective-permute-start(bf16[16,16,128]{2,1,0:T(8,128)(2,1)S(1)} %collective-permute-done.refs_0_), channel_id=1, source_target_pairs={{0,1},{1,2},{2,3},{3,0},{4,5},{5,6},{6,7},{7,4},{8,9},{9,10},{10,1... | collective-permute-start | bytes 196616 | tf_op jit(solution)/shard_map/ppermute | solution.py:213
  15.2 0.6 %shard_map.78 = (f32[256,128]{1,0:T(8,128)S(1)}, f32[256,128]{1,0:T(8,128)S(1)}, f32[4,256,128]{2,1,0:T(8,128)S(1)}, f32[256,128]{1,0:T(8,128)S(1)}, f32[256,128]{1,0:T(8,128)S(1)}, /*index=5*/f32[256,128]{1,0:T(8,128)S(1)}) custom-call(bf16[16,16,128]{2,1,0:T(8,128)(2,1)S(1)} %copy-done.2, s32[16,16]{1,0:T(8,128)S(1)} %copy-done.5, s32[1]{0:T(128)S(6)} %copy.8.crop_ref, ...), custom_call_target="tpu_custom_call" | custom-call | flops 50331648 | bytes 1508356 | tf_op jit(solution)/shard_map/pallas_call | solution.py:192
  15.8 2.1 %collective-permute-done.5.refs_6_ = bf16[16,16,128]{2,1,0:T(8,128)(2,1)S(1)} collective-permute-done((bf16[16,16,128]{2,1,0:T(8,128)(2,1)S(1)}, bf16[16,16,128]{2,1,0:T(8,128)(2,1)S(1)}, u32[]{:S(2)}, u32[]{:S(2)}) %collective-permute-start.5) | collective-permute-done | bytes 65568 | tf_op jit(solution)/shard_map/ppermute | solution.py:213
  17.9 1.6 %collective-permute-done.2.refs_2_ = bf16[16,16,128]{2,1,0:T(8,128)(2,1)S(1)} collective-permute-done((bf16[16,16,128]{2,1,0:T(8,128)(2,1)S(1)}, bf16[16,16,128]{2,1,0:T(8,128)(2,1)S(1)}, u32[]{:S(2)}, u32[]{:S(2)}) %collective-permute-start.2) | collective-permute-done | bytes 65568 | tf_op jit(solution)/shard_map/ppermute | solution.py:213
  19.5 0.4 collective-permute-done.1.refs_1_
  19.9 4.1 %shard_map.79 = (f32[256,128]{1,0:T(8,128)S(1)}, bf16[16,16,128]{2,1,0:T(8,128)(2,1)S(1)}, bf16[16,16,128]{2,1,0:T(8,128)(2,1)S(1)}, bf16[16,16,128]{2,1,0:T(8,1...) custom-call(bf16[16,16,128]{2,1,0:T(8,128)(2,1)S(1)} %collective-per, ...), custom_call_target="tpu_custom_call" | custom-call | flops 12582912 | bytes 1310720 | tf_op jit(solution)/shard_map/pallas_call | solution.py:192
  24.1 1.0 %collective-permute-start.8 = (bf16[16,16,128]{2,1,0:T(8,128)(2,1)S(1)}, bf16[16,16,128]{2,1,0:T(8,128)(2,1)S(1)}, u32[]{:S(2)}, u32[]{:S(2)}) collective-permute-start(bf16[16,16,128]{2,1,0:T(8,128)(2,1)S(1)} %get-tuple-element.30), channel_id=1, source_target_pairs={{0,2},{1,3},{2,0},{3,1},{4,6},{5,7},{6,4},{7,5},{8,10},{9,11},{10,... | collective-permute-start | bytes 196616 | tf_op jit(solution)/shard_map/ppermute | solution.py:213
  25.1 1.4 %collective-permute-start.9 = (bf16[16,16,128]{2,1,0:T(8,128)(2,1)S(1)}, bf16[16,16,128]{2,1,0:T(8,128)(2,1)S(1)}, u32[]{:S(2)}, u32[]{:S(2)}) collective-permute-start(bf16[16,16,128]{2,1,0:T(8,128)(2,1)S(1)} %get-tuple-element.31), channel_id=1, source_target_pairs={{0,3},{1,0},{2,1},{3,2},{4,7},{5,4},{6,5},{7,6},{8,11},{9,8},{10,9... | collective-permute-start | bytes 196616 | tf_op jit(solution)/shard_map/ppermute | solution.py:213
  26.5 2.5 %collective-permute-start.11 = (bf16[16,16,128]{2,1,0:T(8,128)(2,1)S(1)}, bf16[16,16,128]{2,1,0:T(8,128)(2,1)S(1)}, u32[]{:S(2)}, u32[]{:S(2)}) collective-permute-start(bf16[16,16,128]{2,1,0:T(8,128)(2,1)S(1)} %get-tuple-element.33), channel_id=1, source_target_pairs={{0,4},{4,8},{8,12},{12,0},{1,5},{5,9},{9,13},{13,1},{2,6},{6,10},{... | collective-permute-start | bytes 196616 | tf_op jit(solution)/shard_map/ppermute | solution.py:213
  29.0 2.4 %collective-permute-start.13 = (bf16[16,16,128]{2,1,0:T(8,128)(2,1)S(1)}, bf16[16,16,128]{2,1,0:T(8,128)(2,1)S(1)}, u32[]{:S(2)}, u32[]{:S(2)}) collective-permute-start(bf16[16,16,128]{2,1,0:T(8,128)(2,1)S(1)} %get-tuple-element.35), channel_id=1, source_target_pairs={{0,12},{4,0},{8,4},{12,8},{1,13},{5,1},{9,5},{13,9},{2,14},{6,2},{... | collective-permute-start | bytes 196616 | tf_op jit(solution)/shard_map/ppermute | solution.py:213
  31.4 3.5 %collective-permute-start.10 = (bf16[16,16,128]{2,1,0:T(8,128)(2,1)S(1)}, bf16[16,16,128]{2,1,0:T(8,128)(2,1)S(1)}, u32[]{:S(2)}, u32[]{:S(2)}) collective-permute-start(bf16[16,16,128]{2,1,0:T(8,128)(2,1)S(1)} %shard_map.81), channel_id=1, source_target_pairs={{0,0},{1,4},{2,8},{3,12},{4,1},{5,5},{6,9},{7,13},{8,2},{9,6},{10,... | collective-permute-start | bytes 196616 | tf_op jit(solution)/shard_map/ppermute | solution.py:216
  34.9 0.8 %shard_map.80 = (bf16[16,16,128]{2,1,0:T(8,128)(2,1)}, f32[256,128]{1,0:T(8,128)S(1)}) custom-call(f32[256,128]{1,0:T(8,128)S(1)} %get-tuple-element.24.tri_normed_ref, f32[256,128]{1,0:T(8,128)S(1)} %get-tuple-element.25.open_ref, f32[256,128]{1,0:T(8,128)S(1)} %get-tuple-element.26.gate_factor_ref, bf16[128,640]{1,0:T(8,128)(2,1)S(1)} %copy-done.1, ...), custom_call_target="tpu_custom_call" | custom-call | flops 16777216 | bytes 786432 | tf_op jit(solution)/shard_map/pallas_call | solution.py:192
  35.8 3.7 %collective-permute-done.10.left_ref = bf16[16,16,128]{2,1,0:T(8,128)(2,1)S(1)} collective-permute-done((bf16[16,16,128]{2,1,0:T(8,128)(2,1)S(1)}, bf16[16,16,128]{2,1,0:T(8,128)(2,1)S(1)}, u32[]{:S(2)}, u32[]{:S(2)}) %collective-permute-start.10) | collective-permute-done | bytes 65568 | tf_op jit(solution)/shard_map/ppermute | solution.py:216
  39.5 1.0 %shard_map.82 = bf16[16,16,128]{2,1,0:T(8,128)(2,1)} custom-call(bf16[16,16,128]{2,1,0:T(8,128)(2,1)S(1)} %collective-permute-done.10.left_ref, bf16[16,16,128]{2,1,0:T(8,128)(2,1)S(1)} %get-tuple-element.32.refs_0_, bf16[16,16,128]{2,1,0:T(8,128)(2,1)S(1)} %collective-permute-done.11.refs_1_, bf16[16,16,128]{2,1,0:T(8,128)(2,1)S(1)} %collective-permute-done.12.refs_2_, ...), custom_call_target="tpu_custom_call" | custom-call | flops 33554432 | bytes 1474560 | tf_op jit(solution)/shard_map/pallas_call | solution.py:192
  (22 shorter events, 0.1 us)
Async XLA Ops:
  1.3 0.9 %copy-start = (bf16[128,640]{1,0:T(8,128)(2,1)S(1)}, bf16[128,640]{1,0:T(8,128)(2,1)}, u32[]{:S(2)}) copy-start(bf16[128,640]{1,0:T(8,128)(2,1)} %refs_8_.1) | copy-start | bytes 491524
  2.2 0.8 %copy-start.2 = (bf16[16,16,128]{2,1,0:T(8,128)(2,1)S(1)}, bf16[16,16,128]{2,1,0:T(8,128)(2,1)}, u32[]{:S(2)}) copy-start(bf16[16,16,128]{2,1,0:T(8,128)(2,1)} %acts_ref.3) | copy-start | bytes 196612
  3.0 0.7 %copy-start.5 = (s32[16,16]{1,0:T(8,128)S(1)}, s32[16,16]{1,0:T(8,128)}, u32[]{:S(2)}) copy-start(s32[16,16]{1,0:T(8,128)} %mask_ref.3) | copy-start | bytes 3076
  3.7 11.4 %copy-start.3 = (bf16[128,128]{1,0:T(8,128)(2,1)S(1)}, bf16[128,128]{1,0:T(8,128)(2,1)}, u32[]{:S(2)}) copy-start(bf16[128,128]{1,0:T(8,128)(2,1)} %out_weight_ref.3) | copy-start | bytes 98308
  3.7 11.4 %copy-start.4 = (bf16[16,16,128]{2,1,0:T(8,128)(2,1)S(1)}, bf16[16,16,128]{2,1,0:T(8,128)(2,1)}, u32[]{:S(2)}) copy-start(bf16[16,16,128]{2,1,0:T(8,128)(2,1)} %cotangent_ref.1) | copy-start | bytes 196612
  4.3 10.3 %collective-permute-start = (bf16[16,16,128]{2,1,0:T(8,128)(2,1)S(1)}, bf16[16,16,128]{2,1,0:T(8,128)(2,1)S(1)}, u32[]{:S(2)}, u32[]{:S(2)}) collective-permute-start(bf16[16,16,128]{2,1,0:T(8,128)(2,1)S(1)} %get-tuple-element.21), channel_id=1, source_target_pairs={{0,0},{1,4},{2,8},{3,12},{4,1},{5,5},{6,9},{7,13},{8,2},{9,6},{10,... | collective-permute-start | bytes 196616 | tf_op jit(solution)/shard_map/ppermute | solution.py:216
  8.8 5.9 %collective-permute-start.6 = (bf16[16,16,128]{2,1,0:T(8,128)(2,1)S(1)}, bf16[16,16,128]{2,1,0:T(8,128)(2,1)S(1)}, u32[]{:S(2)}, u32[]{:S(2)}) collective-permute-start(bf16[16,16,128]{2,1,0:T(8,128)(2,1)S(1)} %get-tuple-element.22.refs_4_), channel_id=1, source_target_pairs={{0,12},{4,0},{8,4},{12,8},{1,13},{5,1},{9,5},{13,9},{2,14},{6,2},{... | collective-permute-start | bytes 196616 | tf_op jit(solution)/shard_map/ppermute | solution.py:213
  9.9 8.0 %collective-permute-start.5 = (bf16[16,16,128]{2,1,0:T(8,128)(2,1)S(1)}, bf16[16,16,128]{2,1,0:T(8,128)(2,1)S(1)}, u32[]{:S(2)}, u32[]{:S(2)}) collective-permute-start(bf16[16,16,128]{2,1,0:T(8,128)(2,1)S(1)} %get-tuple-element.22.refs_4_), channel_id=1, source_target_pairs={{0,8},{4,12},{8,0},{12,4},{1,9},{5,13},{9,1},{13,5},{2,10},{6,14},... | collective-permute-start | bytes 196616 | tf_op jit(solution)/shard_map/ppermute | solution.py:213
  10.3 7.6 %collective-permute-start.4 = (bf16[16,16,128]{2,1,0:T(8,128)(2,1)S(1)}, bf16[16,16,128]{2,1,0:T(8,128)(2,1)S(1)}, u32[]{:S(2)}, u32[]{:S(2)}) collective-permute-start(bf16[16,16,128]{2,1,0:T(8,128)(2,1)S(1)} %get-tuple-element.22.refs_4_), channel_id=1, source_target_pairs={{0,4},{4,8},{8,12},{12,0},{1,5},{5,9},{9,13},{13,1},{2,6},{6,10},{... | collective-permute-start | bytes 196616 | tf_op jit(solution)/shard_map/ppermute | solution.py:213
  14.6 3.2 %collective-permute-start.3 = (bf16[16,16,128]{2,1,0:T(8,128)(2,1)S(1)}, bf16[16,16,128]{2,1,0:T(8,128)(2,1)S(1)}, u32[]{:S(2)}, u32[]{:S(2)}) collective-permute-start(bf16[16,16,128]{2,1,0:T(8,128)(2,1)S(1)} %collective-permute-done.refs_0_), channel_id=1, source_target_pairs={{0,3},{1,0},{2,1},{3,2},{4,7},{5,4},{6,5},{7,6},{8,11},{9,8},{10,9... | collective-permute-start | bytes 196616 | tf_op jit(solution)/shard_map/ppermute | solution.py:213
  14.6 4.9 %collective-permute-start.2 = (bf16[16,16,128]{2,1,0:T(8,128)(2,1)S(1)}, bf16[16,16,128]{2,1,0:T(8,128)(2,1)S(1)}, u32[]{:S(2)}, u32[]{:S(2)}) collective-permute-start(bf16[16,16,128]{2,1,0:T(8,128)(2,1)S(1)} %collective-permute-done.refs_0_), channel_id=1, source_target_pairs={{0,2},{1,3},{2,0},{3,1},{4,6},{5,7},{6,4},{7,5},{8,10},{9,11},{10,... | collective-permute-start | bytes 196616 | tf_op jit(solution)/shard_map/ppermute | solution.py:213
  14.7 5.1 %collective-permute-start.1 = (bf16[16,16,128]{2,1,0:T(8,128)(2,1)S(1)}, bf16[16,16,128]{2,1,0:T(8,128)(2,1)S(1)}, u32[]{:S(2)}, u32[]{:S(2)}) collective-permute-start(bf16[16,16,128]{2,1,0:T(8,128)(2,1)S(1)} %collective-permute-done.refs_0_), channel_id=1, source_target_pairs={{0,1},{1,2},{2,3},{3,0},{4,5},{5,6},{6,7},{7,4},{8,9},{9,10},{10,1... | collective-permute-start | bytes 196616 | tf_op jit(solution)/shard_map/ppermute | solution.py:213
  24.0 5.0 %collective-permute-start.7 = (bf16[16,16,128]{2,1,0:T(8,128)(2,1)S(1)}, bf16[16,16,128]{2,1,0:T(8,128)(2,1)S(1)}, u32[]{:S(2)}, u32[]{:S(2)}) collective-permute-start(bf16[16,16,128]{2,1,0:T(8,128)(2,1)S(1)} %get-tuple-element.29), channel_id=1, source_target_pairs={{0,1},{1,2},{2,3},{3,0},{4,5},{5,6},{6,7},{7,4},{8,9},{9,10},{10,1... | collective-permute-start | bytes 196616 | tf_op jit(solution)/shard_map/ppermute | solution.py:213
  24.1 7.3 %collective-permute-start.8 = (bf16[16,16,128]{2,1,0:T(8,128)(2,1)S(1)}, bf16[16,16,128]{2,1,0:T(8,128)(2,1)S(1)}, u32[]{:S(2)}, u32[]{:S(2)}) collective-permute-start(bf16[16,16,128]{2,1,0:T(8,128)(2,1)S(1)} %get-tuple-element.30), channel_id=1, source_target_pairs={{0,2},{1,3},{2,0},{3,1},{4,6},{5,7},{6,4},{7,5},{8,10},{9,11},{10,... | collective-permute-start | bytes 196616 | tf_op jit(solution)/shard_map/ppermute | solution.py:213
  25.1 6.2 %collective-permute-start.9 = (bf16[16,16,128]{2,1,0:T(8,128)(2,1)S(1)}, bf16[16,16,128]{2,1,0:T(8,128)(2,1)S(1)}, u32[]{:S(2)}, u32[]{:S(2)}) collective-permute-start(bf16[16,16,128]{2,1,0:T(8,128)(2,1)S(1)} %get-tuple-element.31), channel_id=1, source_target_pairs={{0,3},{1,0},{2,1},{3,2},{4,7},{5,4},{6,5},{7,6},{8,11},{9,8},{10,9... | collective-permute-start | bytes 196616 | tf_op jit(solution)/shard_map/ppermute | solution.py:213
  26.5 9.3 %collective-permute-start.11 = (bf16[16,16,128]{2,1,0:T(8,128)(2,1)S(1)}, bf16[16,16,128]{2,1,0:T(8,128)(2,1)S(1)}, u32[]{:S(2)}, u32[]{:S(2)}) collective-permute-start(bf16[16,16,128]{2,1,0:T(8,128)(2,1)S(1)} %get-tuple-element.33), channel_id=1, source_target_pairs={{0,4},{4,8},{8,12},{12,0},{1,5},{5,9},{9,13},{13,1},{2,6},{6,10},{... | collective-permute-start | bytes 196616 | tf_op jit(solution)/shard_map/ppermute | solution.py:213
  28.9 6.8 %collective-permute-start.12 = (bf16[16,16,128]{2,1,0:T(8,128)(2,1)S(1)}, bf16[16,16,128]{2,1,0:T(8,128)(2,1)S(1)}, u32[]{:S(2)}, u32[]{:S(2)}) collective-permute-start(bf16[16,16,128]{2,1,0:T(8,128)(2,1)S(1)} %get-tuple-element.34), channel_id=1, source_target_pairs={{0,8},{4,12},{8,0},{12,4},{1,9},{5,13},{9,1},{13,5},{2,10},{6,14},... | collective-permute-start | bytes 196616 | tf_op jit(solution)/shard_map/ppermute | solution.py:213
  29.0 6.8 %collective-permute-start.13 = (bf16[16,16,128]{2,1,0:T(8,128)(2,1)S(1)}, bf16[16,16,128]{2,1,0:T(8,128)(2,1)S(1)}, u32[]{:S(2)}, u32[]{:S(2)}) collective-permute-start(bf16[16,16,128]{2,1,0:T(8,128)(2,1)S(1)} %get-tuple-element.35), channel_id=1, source_target_pairs={{0,12},{4,0},{8,4},{12,8},{1,13},{5,1},{9,5},{13,9},{2,14},{6,2},{... | collective-permute-start | bytes 196616 | tf_op jit(solution)/shard_map/ppermute | solution.py:213
  31.3 3.6 %copy-start.1 = (bf16[128,640]{1,0:T(8,128)(2,1)S(1)}, bf16[128,640]{1,0:T(8,128)(2,1)}, u32[]{:S(2)}) copy-start(bf16[128,640]{1,0:T(8,128)(2,1)} %refs_8_.1) | copy-start | bytes 491524
  31.4 8.1 %collective-permute-start.10 = (bf16[16,16,128]{2,1,0:T(8,128)(2,1)S(1)}, bf16[16,16,128]{2,1,0:T(8,128)(2,1)S(1)}, u32[]{:S(2)}, u32[]{:S(2)}) collective-permute-start(bf16[16,16,128]{2,1,0:T(8,128)(2,1)S(1)} %shard_map.81), channel_id=1, source_target_pairs={{0,0},{1,4},{2,8},{3,12},{4,1},{5,5},{6,9},{7,13},{8,2},{9,6},{10,... | collective-permute-start | bytes 196616 | tf_op jit(solution)/shard_map/ppermute | solution.py:216

commit v2 on v1

--- a/solution.py
+++ b/solution.py
@@ -55,10 +55,24 @@
     return dot(spread, jnp.ones((size, 128), bf16))
 
 
-def tiles_kernel(acts_ref, mask_ref, crop_ref, weights_ref, left_ref, right_ref):
+def start_copies(sems, *pairs):
+    copies = [pltpu.make_async_copy(src, dst, sems.at[n]) for n, (src, dst) in enumerate(pairs)]
+    for copy in copies:
+        copy.start()
+    return copies
+
+
+def tiles_kernel(
+    acts_in, mask_in, crop_ref, weights_in, left_ref, right_ref, acts_ref, mask_ref, weights_ref, sems
+):
+    copies = start_copies(sems, (acts_in, acts_ref), (weights_in, weights_ref), (mask_in, mask_ref))
     size, _, channels = acts_ref.shape
+    copies[0].wait()
     normed, _ = normalize(acts_ref[...].astype(f32).reshape(size * size, channels))
-    projected = dot(normed.astype(bf16), weights_ref[:, : 4 * channels])
+    normed = normed.astype(bf16)
+    copies[1].wait()
+    copies[2].wait()
+    projected = dot(normed, weights_ref[:, : 4 * channels])
     keep = keep_rows(mask_ref, crop_ref)
     for block, out_ref in ((0, left_ref), (2, right_ref)):
         value = projected[:, block * channels : (block + 1) * channels]
@@ -68,14 +82,22 @@
 
 
 def factors_kernel(
-    acts_ref, mask_ref, crop_ref, cotangent_ref, weights_ref, out_weight_ref,
+    acts_in, mask_in, crop_ref, cotangent_in, weights_in, out_weight_in,
     normed_ref, scale_ref, factor_ref, open_ref, gate_factor_ref, upstream_ref,
+    acts_ref, mask_ref, cotangent_ref, weights_ref, out_weight_ref, sems,
 ):
+    copies = start_copies(
+        sems, (acts_in, acts_ref), (weights_in, weights_ref), (mask_in, mask_ref),
+        (cotangent_in, cotangent_ref), (out_weight_in, out_weight_ref),
+    )
     size, _, channels = acts_ref.shape
     pairs = size * size
+    copies[0].wait()
     normed, scale = normalize(acts_ref[...].astype(f32).reshape(pairs, channels))
     normed_ref[...] = normed
     scale_ref[...] = jnp.broadcast_to(scale, (pairs, channels))
+    for copy in copies[1:]:
+        copy.wait()
     projected = dot(normed.astype(bf16), weights_ref[...])
     keep = keep_rows(mask_ref, crop_ref)
     for block in (0, 2):
@@ -92,20 +114,27 @@
     upstream_ref[...] = dot_t(lin_grad, out_weight_ref[...])
 
 
+def weighted_sums(weights, start, terms, out):
+    def step(k, _):
+        total = weights[start + k, pl.ds(0, 1), :] * terms[0]
+        for n in range(1, len(terms)):
+            total = total + weights[start + k, pl.ds(n, 1), :] * terms[n]
+        out[k] = total.astype(bf16)
+        return 0
+
+    lax.fori_loop(0, out.shape[0], step, 0)
+
+
 def triangle_kernel(grid_size, *refs):
     left_in, right_in = refs[:grid_size], refs[grid_size : 2 * grid_size]
     upstream_ref = refs[2 * grid_size]
-    outs = refs[2 * grid_size + 1 :]
-    tri_normed_ref = outs[0]
-    left_out, right_out = outs[1 : grid_size + 1], outs[grid_size + 1 : 2 * grid_size + 1]
-    left, right, grad = outs[2 * grid_size + 1 :]
+    tri_normed_ref, left, grad, *left_out = refs[2 * grid_size + 1 : -1]
+    right = refs[-1]
     size, _, channels = left_in[0].shape
     row, col = lax.axis_index("row"), lax.axis_index("col")
-    for shift in range(grid_size):
-        start = lax.rem(col + (grid_size - shift), grid_size) * size
-        left[pl.ds(start, size)] = left_in[shift][...].astype(f32)
-        start = lax.rem(row + (grid_size - shift), grid_size) * size
-        right[pl.ds(start, size)] = right_in[shift][...].astype(f32)
+    for step in range(grid_size):
+        left[pl.ds((col ^ step) * size, size)] = left_in[step][...].astype(f32)
+        right[pl.ds((row ^ step) * size, size)] = right_in[step][...].astype(f32)
 
     def step(k, sums):
         other = right[k]
@@ -120,33 +149,17 @@
         back = normalize_back(tri_normed, scale, upstream_ref[here, :])
         grad[here, :] = back.astype(bf16).astype(f32)
 
+    grads = [grad[pl.ds(j, size, stride=size), :] for j in range(size)]
+    for step in range(grid_size):
+        weighted_sums(right, (col ^ step) * size, grads, left_out[step])
+
+
+def right_kernel(grid_size, left, grad, *right_out):
+    size = right_out[0].shape[0]
+    row = lax.axis_index("row")
     grads = [grad[pl.ds(i * size, size), :] for i in range(size)]
-    for shift in range(grid_size):
-        start = lax.rem(row + shift, grid_size) * size
-        out = right_out[shift]
-
-        def step(k, _):
-            total = left[start + k, pl.ds(0, 1), :] * grads[0]
-            for i in range(1, size):
-                total = total + left[start + k, pl.ds(i, 1), :] * grads[i]
-            out[k] = total.astype(bf16)
-            return 0
-
-        lax.fori_loop(0, size, step, 0)
-
-    grads_t = [grad[pl.ds(j, size, stride=size), :] for j in range(size)]
-    for shift in range(grid_size):
-        start = lax.rem(col + shift, grid_size) * size
-        out = left_out[shift]
-
-        def step(k, _):
-            total = right[start + k, pl.ds(0, 1), :] * grads_t[0]
-            for j in range(1, size):
-                total = total + right[start + k, pl.ds(j, 1), :] * grads_t[j]
-            out[k] = total.astype(bf16)
-            return 0
-
-        lax.fori_loop(0, size, step, 0)
+    for step in range(grid_size):
+        weighted_sums(left, (row ^ step) * size, grads, right_out[step])
 
 
 def update_kernel(
@@ -186,13 +199,20 @@
     out_ref[...] = back.astype(bf16).reshape(size, size, channels)
 
 
-def call(kernel, outs, *args, scratch=(), flops=0, smem=()):
+def call(kernel, outs, *args, scratch=(), flops=0, smem=(), hbm=()):
     spec = pl.BlockSpec(memory_space=pltpu.VMEM)
     total = sum(a.size * a.dtype.itemsize for a in (*args, *outs))
+    specs = [spec] * len(args)
+    for n in smem:
+        specs[n] = pl.BlockSpec(memory_space=pltpu.SMEM)
+    args = list(args)
+    for n in hbm:
+        specs[n] = pl.BlockSpec(memory_space=pltpu.HBM)
+        args[n] = pltpu.with_memory_space_constraint(args[n], pltpu.HBM)
     return pl.pallas_call(
         kernel,
         out_shape=tuple(outs),
-        in_specs=[pl.BlockSpec(memory_space=pltpu.SMEM) if n in smem else spec for n in range(len(args))],
+        in_specs=specs,
         out_specs=(spec,) * len(outs),
         scratch_shapes=scratch,
         compiler_params=pltpu.CompilerParams(vmem_limit_bytes=24 * 2**20),
@@ -207,40 +227,53 @@
     tile = jax.ShapeDtypeStruct((size, size, channels), bf16)
     flat = jax.ShapeDtypeStruct((pairs, channels), f32)
 
-    def shift_by(values, axis, shift):
-        if shift == 0:
-            return values
-        return lax.ppermute(values, axis, [(a, (a + shift) % n) for a in range(n)])
+    def swap(values, axis, step):
+        return lax.ppermute(values, axis, [(a, a ^ step) for a in range(n)])
 
     def mirror(values):
         return lax.ppermute(values, ("row", "col"), [(a * n + b, b * n + a) for a in range(n) for b in range(n)])
 
     left, right = call(
         tiles_kernel, (tile, tile), pair_acts, pair_mask, crop_length, in_weights,
-        smem=(2,), flops=2 * pairs * channels * 4 * channels,
+        smem=(2,), hbm=(0, 1, 3), flops=2 * pairs * channels * 4 * channels,
+        scratch=[
+            pltpu.VMEM(pair_acts.shape, bf16),
+            pltpu.VMEM(pair_mask.shape, jnp.int32),
+            pltpu.VMEM(in_weights.shape, bf16),
+            pltpu.SemaphoreType.DMA((3,)),
+        ],
     )
     mirrored = mirror(left)
-    rights = [shift_by(right, "row", shift) for shift in range(n)]
+    rights = [right] + [swap(right, "row", step) for step in range(n - 1, 0, -1)][::-1]
     normed, scale, factors, out_open, gate_factor, upstream = call(
         factors_kernel,
         (flat, flat, jax.ShapeDtypeStruct((4, pairs, channels), f32), flat, flat, flat),
         pair_acts, pair_mask, crop_length, cotangent, in_weights, out_weight,
-        smem=(2,), flops=2 * pairs * channels * 6 * channels,
-    )
-    lefts = [shift_by(mirrored, "col", shift) for shift in range(n)]
-    tri_normed, *terms = call(
+        smem=(2,), hbm=(0, 1, 3, 4, 5), flops=2 * pairs * channels * 6 * channels,
+        scratch=[
+            pltpu.VMEM(pair_acts.shape, bf16),
+            pltpu.VMEM(pair_mask.shape, jnp.int32),
+            pltpu.VMEM(cotangent.shape, bf16),
+            pltpu.VMEM(in_weights.shape, bf16),
+            pltpu.VMEM(out_weight.shape, bf16),
+            pltpu.SemaphoreType.DMA((5,)),
+        ],
+    )
+    lefts = [mirrored] + [swap(mirrored, "col", step) for step in range(1, n)]
+    panel = jax.ShapeDtypeStruct((n * size, size, channels), f32)
+    tri_normed, left_panel, tri_grad, *left_terms = call(
         functools.partial(triangle_kernel, n),
-        (flat,) + (tile,) * (2 * n),
+        (flat, panel, flat) + (tile,) * n,
         *lefts, *rights, upstream,
-        scratch=[
-            pltpu.VMEM((n * size, size, channels), f32),
-            pltpu.VMEM((n * size, size, channels), f32),
-            pltpu.VMEM((pairs, channels), f32),
-        ],
-        flops=6 * n * size * pairs * channels,
-    )
-    left_terms = [shift_by(values, "col", shift) for shift, values in enumerate(terms[:n])]
-    right_terms = [shift_by(values, "row", shift) for shift, values in enumerate(terms[n:])]
+        scratch=[pltpu.VMEM(panel.shape, f32)],
+        flops=4 * n * size * pairs * channels,
+    )
+    left_terms = [left_terms[0]] + [swap(left_terms[step], "col", step) for step in range(1, n)]
+    right_terms = call(
+        functools.partial(right_kernel, n), (tile,) * n, left_panel, tri_grad,
+        flops=2 * n * size * pairs * channels,
+    )
+    right_terms = [right_terms[0]] + [swap(right_terms[step], "row", step) for step in range(1, n)]
     update, partial = call(
         update_kernel, (tile, flat), tri_normed, out_open, gate_factor, in_weights, out_weight,
         flops=4 * pairs * channels * channels,

time: 40.7 us -> 40.9 us (level)
  local copies, waits for them, and re-layouts: 2.46 us -> 0.01 us
  Pallas kernels: 7.09 us -> 8.77 us
  starting transfers between devices: 17.9 us -> 19.2 us
    ppermute x12, starting transfers between devices: 9.91 us -> 12.7 us  [swap(): return lax.ppermute(values, axis, [(a, a ^ step) for a in range(n)])]
    unnamed x12 -> x4, local copies, waits for them, and re-layouts: 2.46 us -> 0.01 us
    pallas_call x6 -> x7, Pallas kernels: 7.09 us -> 8.77 us  [call(): pl.pallas_call(kernel, out_shape=tuple(outs), in_specs=specs, out_specs=(...]
    ppermute x2, starting transfers between devices: 8.02 us -> 6.52 us  [mirror(): lax.ppermute(values, ('row', 'col'), [(a * n + b, b * n + a) for a in ran...]
    ppermute x12, waiting for transfers between devices: 4.13 us -> 2.95 us  [swap(): return lax.ppermute(values, axis, [(a, a ^ step) for a in range(n)])]
    ppermute x2, waiting for transfers between devices: 7.46 us -> 8.38 us  [mirror(): lax.ppermute(values, ('row', 'col'), [(a * n + b, b * n + a) for a in ran...]
  transfers between devices with their start and end apart: 14 -> 14, of which waited for: 5 -> 5; matrix products, arithmetic and copies ran while one was open for 0% -> 0% of each run, Pallas kernels for 4% -> 9%
where the time goes in v2:
time: 40.9 us; the launch traced here: 40.7 us
  starting transfers between devices  19.2 us (47%)
  waiting for transfers between devices  11.3 us (28%)
  Pallas kernels  8.77 us (21%)
  between operations  1.38 us (3%)
    ppermute x12, starting transfers between devices, swap(): return lax.ppermute(values, axis, [(a, a ^ step) for a in range(n)])  12.7 us
    pallas_call x7, Pallas kernels, call(): pl.pallas_call(kernel, out_shape=tuple(outs), in_specs=specs, out_specs=(...  8.77 us
    ppermute x2, waiting for transfers between devices, mirror(): lax.ppermute(values, ('row', 'col'), [(a * n + b, b * n + a) for a in ran...  8.38 us
    ppermute x2, starting transfers between devices, mirror(): lax.ppermute(values, ('row', 'col'), [(a * n + b, b * n + a) for a in ran...  6.52 us
    ppermute x12, waiting for transfers between devices, swap(): return lax.ppermute(values, axis, [(a, a ^ step) for a in range(n)])  2.95 us
  transfers between devices with their start and end apart: 14, of which 5 were waited for; matrix products, arithmetic and copies ran while one was open for 0% of the time, Pallas kernels for 9%

profile of v2, /device:TPU:6, one launch (start us, length us, event | category | flops | bytes accessed | tf_op | source)
XLA Modules:
  0.0 40.7 jit_solution(3822863769810637346)
XLA Ops:
  1.3 1.4 %shard_map.77 = (bf16[16,16,128]{2,1,0:T(8,128)(2,1)S(1)}, bf16[16,16,128]{2,1,0:T(8,128)(2,1)S(1)}) custom-call(bf16[16,16,128]{2,1,0:T(8,128)(2,1)} %acts_in.3, s32[16,16]{1,0:T(8,128)} %mask_in.3, s32[1]{0:T(128)S(6)} %copy.8.crop_ref, bf16[128,640]{1,0:T(8,128)(2,1)} %refs_8_.1), custom_call_target="tpu_custom_call" | custom-call | flops 33554432 | bytes 361476 | tf_op jit(solution)/shard_map/pallas_call | solution.py:212
  2.7 4.5 %collective-permute-start = (bf16[16,16,128]{2,1,0:T(8,128)(2,1)S(1)}, bf16[16,16,128]{2,1,0:T(8,128)(2,1)S(1)}, u32[]{:S(2)}, u32[]{:S(2)}) collective-permute-start(bf16[16,16,128]{2,1,0:T(8,128)(2,1)S(1)} %get-tuple-element.23), channel_id=1, source_target_pairs={{0,0},{1,4},{2,8},{3,12},{4,1},{5,5},{6,9},{7,13},{8,2},{9,6},{10,... | collective-permute-start | bytes 196616 | tf_op jit(solution)/shard_map/ppermute | solution.py:234
  7.2 1.1 %collective-permute-start.6 = (bf16[16,16,128]{2,1,0:T(8,128)(2,1)S(1)}, bf16[16,16,128]{2,1,0:T(8,128)(2,1)S(1)}, u32[]{:S(2)}, u32[]{:S(2)}) collective-permute-start(bf16[16,16,128]{2,1,0:T(8,128)(2,1)S(1)} %get-tuple-element.24.refs_4_), channel_id=1, source_target_pairs={{0,12},{4,8},{8,4},{12,0},{1,13},{5,9},{9,5},{13,1},{2,14},{6,10},... | collective-permute-start | bytes 196616 | tf_op jit(solution)/shard_map/ppermute | solution.py:231
  8.3 0.4 %collective-permute-start.5 = (bf16[16,16,128]{2,1,0:T(8,128)(2,1)S(1)}, bf16[16,16,128]{2,1,0:T(8,128)(2,1)S(1)}, u32[]{:S(2)}, u32[]{:S(2)}) collective-permute-start(bf16[16,16,128]{2,1,0:T(8,128)(2,1)S(1)} %get-tuple-element.24.refs_4_), channel_id=1, source_target_pairs={{0,8},{4,12},{8,0},{12,4},{1,9},{5,13},{9,1},{13,5},{2,10},{6,14},... | collective-permute-start | bytes 196616 | tf_op jit(solution)/shard_map/ppermute | solution.py:231
  8.7 2.9 %collective-permute-start.4 = (bf16[16,16,128]{2,1,0:T(8,128)(2,1)S(1)}, bf16[16,16,128]{2,1,0:T(8,128)(2,1)S(1)}, u32[]{:S(2)}, u32[]{:S(2)}) collective-permute-start(bf16[16,16,128]{2,1,0:T(8,128)(2,1)S(1)} %get-tuple-element.24.refs_4_), channel_id=1, source_target_pairs={{0,4},{4,0},{8,12},{12,8},{1,5},{5,1},{9,13},{13,9},{2,6},{6,2},{1... | collective-permute-start | bytes 196616 | tf_op jit(solution)/shard_map/ppermute | solution.py:231
  11.7 3.8 %collective-permute-done.refs_0_ = bf16[16,16,128]{2,1,0:T(8,128)(2,1)S(1)} collective-permute-done((bf16[16,16,128]{2,1,0:T(8,128)(2,1)S(1)}, bf16[16,16,128]{2,1,0:T(8,128)(2,1)S(1)}, u32[]{:S(2)}, u32[]{:S(2)}) %collective-permute-start) | collective-permute-done | bytes 65568 | tf_op jit(solution)/shard_map/ppermute | solution.py:234
  15.5 1.9 %collective-permute-start.1 = (bf16[16,16,128]{2,1,0:T(8,128)(2,1)S(1)}, bf16[16,16,128]{2,1,0:T(8,128)(2,1)S(1)}, u32[]{:S(2)}, u32[]{:S(2)}) collective-permute-start(bf16[16,16,128]{2,1,0:T(8,128)(2,1)S(1)} %collective-permute-done.refs_0_), channel_id=1, source_target_pairs={{0,1},{1,0},{2,3},{3,2},{4,5},{5,4},{6,7},{7,6},{8,9},{9,8},{10,11... | collective-permute-start | bytes 196616 | tf_op jit(solution)/shard_map/ppermute | solution.py:231
  17.4 1.5 %shard_map.78 = (f32[256,128]{1,0:T(8,128)S(1)}, f32[256,128]{1,0:T(8,128)S(1)}, f32[4,256,128]{2,1,0:T(8,128)S(1)}, f32[256,128]{1,0:T(8,128)S(1)}, f32[256,128]{1,0:T(8,128)S(1)}, /*index=5*/f32[256,128]{1,0:T(8,128)S(1)}) custom-call(bf16[16,16,128]{2,1,0:T(8,128)(2,1)} %acts_in.3, s32[16,16]{1,0:T(8,128)} %mask_in.3, s32[1]{0:T(128)S(6)} %copy.8.crop_ref, ...), custom_call_target="tpu_custom_call" | custom-call | flops 50331648 | bytes 1508356 | tf_op jit(solution)/shard_map/pallas_call | solution.py:212
  18.9 0.5 %collective-permute-done.3.refs_3_ = bf16[16,16,128]{2,1,0:T(8,128)(2,1)S(1)} collective-permute-done((bf16[16,16,128]{2,1,0:T(8,128)(2,1)S(1)}, bf16[16,16,128]{2,1,0:T(8,128)(2,1)S(1)}, u32[]{:S(2)}, u32[]{:S(2)}) %collective-permute-start.3) | collective-permute-done | bytes 65568 | tf_op jit(solution)/shard_map/ppermute | solution.py:231
  19.3 1.1 %collective-permute-done.2.refs_2_ = bf16[16,16,128]{2,1,0:T(8,128)(2,1)S(1)} collective-permute-done((bf16[16,16,128]{2,1,0:T(8,128)(2,1)S(1)}, bf16[16,16,128]{2,1,0:T(8,128)(2,1)S(1)}, u32[]{:S(2)}, u32[]{:S(2)}) %collective-permute-start.2) | collective-permute-done | bytes 65568 | tf_op jit(solution)/shard_map/ppermute | solution.py:231
  20.4 2.8 %shard_map.79 = (f32[256,128]{1,0:T(8,128)S(1)}, f32[64,16,128]{2,1,0:T(8,128)S(1)}, f32[256,128]{1,0:T(8,128)S(1)}, bf16[16,16,128]{2,1,0:T(8,128)(2,1)S(1)}, b...) custom-call(bf16[16,16,128]{2,1,0:T(8,128)(2,1)S(1)} %collective-permute-done.ref, ...), custom_call_target="tpu_custom_call" | custom-call | flops 8388608 | bytes 1703936 | tf_op jit(solution)/shard_map/pallas_call | solution.py:212
  23.3 0.2 collective-permute-start.7
  23.5 0.4 %collective-permute-start.8 = (bf16[16,16,128]{2,1,0:T(8,128)(2,1)S(1)}, bf16[16,16,128]{2,1,0:T(8,128)(2,1)S(1)}, u32[]{:S(2)}, u32[]{:S(2)}) collective-permute-start(bf16[16,16,128]{2,1,0:T(8,128)(2,1)S(1)} %get-tuple-element.32), channel_id=1, source_target_pairs={{0,2},{1,3},{2,0},{3,1},{4,6},{5,7},{6,4},{7,5},{8,10},{9,11},{10,... | collective-permute-start | bytes 196616 | tf_op jit(solution)/shard_map/ppermute | solution.py:231
  23.9 1.3 %collective-permute-start.9 = (bf16[16,16,128]{2,1,0:T(8,128)(2,1)S(1)}, bf16[16,16,128]{2,1,0:T(8,128)(2,1)S(1)}, u32[]{:S(2)}, u32[]{:S(2)}) collective-permute-start(bf16[16,16,128]{2,1,0:T(8,128)(2,1)S(1)} %get-tuple-element.33), channel_id=1, source_target_pairs={{0,3},{1,2},{2,1},{3,0},{4,7},{5,6},{6,5},{7,4},{8,11},{9,10},{10,... | collective-permute-start | bytes 196616 | tf_op jit(solution)/shard_map/ppermute | solution.py:231
  25.2 1.2 %shard_map.82 = (bf16[16,16,128]{2,1,0:T(8,128)(2,1)S(1)}, bf16[16,16,128]{2,1,0:T(8,128)(2,1)S(1)}, bf16[16,16,128]{2,1,0:T(8,128)(2,1)S(1)}, bf16[16,16,128]{2,1,0:T(8,128)(2,1)S(1)}) custom-call(f32[64,16,128]{2,1,0:T(8,128)S(1)} %get-tuple-element.34.left, f32[256,128]{1,0:T(8,128)S(1)} %get-tuple-element.35.grad), custom_call_target="tpu_custom_call" | custom-call | flops 4194304 | bytes 917504 | tf_op jit(solution)/shard_map/pallas_call | solution.py:212
  26.4 0.1 collective-permute-start.11
  26.5 2.3 %collective-permute-start.12 = (bf16[16,16,128]{2,1,0:T(8,128)(2,1)S(1)}, bf16[16,16,128]{2,1,0:T(8,128)(2,1)S(1)}, u32[]{:S(2)}, u32[]{:S(2)}) collective-permute-start(bf16[16,16,128]{2,1,0:T(8,128)(2,1)S(1)} %get-tuple-element.38), channel_id=1, source_target_pairs={{0,8},{4,12},{8,0},{12,4},{1,9},{5,13},{9,1},{13,5},{2,10},{6,14},... | collective-permute-start | bytes 196616 | tf_op jit(solution)/shard_map/ppermute | solution.py:231
  28.8 2.0 %collective-permute-start.13 = (bf16[16,16,128]{2,1,0:T(8,128)(2,1)S(1)}, bf16[16,16,128]{2,1,0:T(8,128)(2,1)S(1)}, u32[]{:S(2)}, u32[]{:S(2)}) collective-permute-start(bf16[16,16,128]{2,1,0:T(8,128)(2,1)S(1)} %get-tuple-element.39), channel_id=1, source_target_pairs={{0,12},{4,8},{8,4},{12,0},{1,13},{5,9},{9,5},{13,1},{2,14},{6,10},... | collective-permute-start | bytes 196616 | tf_op jit(solution)/shard_map/ppermute | solution.py:231
  30.9 0.0 copy-start.1
  30.9 2.1 %collective-permute-start.10 = (bf16[16,16,128]{2,1,0:T(8,128)(2,1)S(1)}, bf16[16,16,128]{2,1,0:T(8,128)(2,1)S(1)}, u32[]{:S(2)}, u32[]{:S(2)}) collective-permute-start(bf16[16,16,128]{2,1,0:T(8,128)(2,1)S(1)} %shard_map.81), channel_id=1, source_target_pairs={{0,0},{1,4},{2,8},{3,12},{4,1},{5,5},{6,9},{7,13},{8,2},{9,6},{10,... | collective-permute-start | bytes 196616 | tf_op jit(solution)/shard_map/ppermute | solution.py:234
  33.0 0.8 %shard_map.80 = (bf16[16,16,128]{2,1,0:T(8,128)(2,1)}, f32[256,128]{1,0:T(8,128)S(1)}) custom-call(f32[256,128]{1,0:T(8,128)S(1)} %get-tuple-element.26.tri_normed_ref, f32[256,128]{1,0:T(8,128)S(1)} %get-tuple-element.27.open_ref, f32[256,128]{1,0:T(8,128)S(1)} %get-tuple-element.28.gate_factor_ref, bf16[128,640]{1,0:T(8,128)(2,1)S(1)} %copy-done, ...), custom_call_target="tpu_custom_call" | custom-call | flops 16777216 | bytes 786432 | tf_op jit(solution)/shard_map/pallas_call | solution.py:212
  33.8 1.4 %collective-permute-done.12.refs_2_ = bf16[16,16,128]{2,1,0:T(8,128)(2,1)S(1)} collective-permute-done((bf16[16,16,128]{2,1,0:T(8,128)(2,1)S(1)}, bf16[16,16,128]{2,1,0:T(8,128)(2,1)S(1)}, u32[]{:S(2)}, u32[]{:S(2)}) %collective-permute-start.12) | collective-permute-done | bytes 65568 | tf_op jit(solution)/shard_map/ppermute | solution.py:231
  35.2 4.5 %collective-permute-done.10.left_ref = bf16[16,16,128]{2,1,0:T(8,128)(2,1)S(1)} collective-permute-done((bf16[16,16,128]{2,1,0:T(8,128)(2,1)S(1)}, bf16[16,16,128]{2,1,0:T(8,128)(2,1)S(1)}, u32[]{:S(2)}, u32[]{:S(2)}) %collective-permute-start.10) | collective-permute-done | bytes 65568 | tf_op jit(solution)/shard_map/ppermute | solution.py:234
  39.7 1.0 %shard_map.83 = bf16[16,16,128]{2,1,0:T(8,128)(2,1)} custom-call(bf16[16,16,128]{2,1,0:T(8,128)(2,1)S(1)} %collective-permute-done.10.left_ref, bf16[16,16,128]{2,1,0:T(8,128)(2,1)S(1)} %get-tuple-element.36.refs_0_, bf16[16,16,128]{2,1,0:T(8,128)(2,1)S(1)} %collective-permute-done.11.refs_1_, bf16[16,16,128]{2,1,0:T(8,128)(2,1)S(1)} %collective-permute-done.12.refs_2_, ...), custom_call_target="tpu_custom_call" | custom-call | flops 33554432 | bytes 1474560 | tf_op jit(solution)/shard_map/pallas_call | solution.py:212
  (15 shorter events, 0.1 us)
Async XLA Ops:
  2.7 12.8 %collective-permute-start = (bf16[16,16,128]{2,1,0:T(8,128)(2,1)S(1)}, bf16[16,16,128]{2,1,0:T(8,128)(2,1)S(1)}, u32[]{:S(2)}, u32[]{:S(2)}) collective-permute-start(bf16[16,16,128]{2,1,0:T(8,128)(2,1)S(1)} %get-tuple-element.23), channel_id=1, source_target_pairs={{0,0},{1,4},{2,8},{3,12},{4,1},{5,5},{6,9},{7,13},{8,2},{9,6},{10,... | collective-permute-start | bytes 196616 | tf_op jit(solution)/shard_map/ppermute | solution.py:234
  7.2 8.3 %collective-permute-start.6 = (bf16[16,16,128]{2,1,0:T(8,128)(2,1)S(1)}, bf16[16,16,128]{2,1,0:T(8,128)(2,1)S(1)}, u32[]{:S(2)}, u32[]{:S(2)}) collective-permute-start(bf16[16,16,128]{2,1,0:T(8,128)(2,1)S(1)} %get-tuple-element.24.refs_4_), channel_id=1, source_target_pairs={{0,12},{4,8},{8,4},{12,0},{1,13},{5,9},{9,5},{13,1},{2,14},{6,10},... | collective-permute-start | bytes 196616 | tf_op jit(solution)/shard_map/ppermute | solution.py:231
  8.3 10.5 %collective-permute-start.5 = (bf16[16,16,128]{2,1,0:T(8,128)(2,1)S(1)}, bf16[16,16,128]{2,1,0:T(8,128)(2,1)S(1)}, u32[]{:S(2)}, u32[]{:S(2)}) collective-permute-start(bf16[16,16,128]{2,1,0:T(8,128)(2,1)S(1)} %get-tuple-element.24.refs_4_), channel_id=1, source_target_pairs={{0,8},{4,12},{8,0},{12,4},{1,9},{5,13},{9,1},{13,5},{2,10},{6,14},... | collective-permute-start | bytes 196616 | tf_op jit(solution)/shard_map/ppermute | solution.py:231
  8.7 10.1 %collective-permute-start.4 = (bf16[16,16,128]{2,1,0:T(8,128)(2,1)S(1)}, bf16[16,16,128]{2,1,0:T(8,128)(2,1)S(1)}, u32[]{:S(2)}, u32[]{:S(2)}) collective-permute-start(bf16[16,16,128]{2,1,0:T(8,128)(2,1)S(1)} %get-tuple-element.24.refs_4_), channel_id=1, source_target_pairs={{0,4},{4,0},{8,12},{12,8},{1,5},{5,1},{9,13},{13,9},{2,6},{6,2},{1... | collective-permute-start | bytes 196616 | tf_op jit(solution)/shard_map/ppermute | solution.py:231
  15.5 3.8 %collective-permute-start.3 = (bf16[16,16,128]{2,1,0:T(8,128)(2,1)S(1)}, bf16[16,16,128]{2,1,0:T(8,128)(2,1)S(1)}, u32[]{:S(2)}, u32[]{:S(2)}) collective-permute-start(bf16[16,16,128]{2,1,0:T(8,128)(2,1)S(1)} %collective-permute-done.refs_0_), channel_id=1, source_target_pairs={{0,3},{1,2},{2,1},{3,0},{4,7},{5,6},{6,5},{7,4},{8,11},{9,10},{10,... | collective-permute-start | bytes 196616 | tf_op jit(solution)/shard_map/ppermute | solution.py:231
  15.5 4.9 %collective-permute-start.2 = (bf16[16,16,128]{2,1,0:T(8,128)(2,1)S(1)}, bf16[16,16,128]{2,1,0:T(8,128)(2,1)S(1)}, u32[]{:S(2)}, u32[]{:S(2)}) collective-permute-start(bf16[16,16,128]{2,1,0:T(8,128)(2,1)S(1)} %collective-permute-done.refs_0_), channel_id=1, source_target_pairs={{0,2},{1,3},{2,0},{3,1},{4,6},{5,7},{6,4},{7,5},{8,10},{9,11},{10,... | collective-permute-start | bytes 196616 | tf_op jit(solution)/shard_map/ppermute | solution.py:231
  15.5 4.9 %collective-permute-start.1 = (bf16[16,16,128]{2,1,0:T(8,128)(2,1)S(1)}, bf16[16,16,128]{2,1,0:T(8,128)(2,1)S(1)}, u32[]{:S(2)}, u32[]{:S(2)}) collective-permute-start(bf16[16,16,128]{2,1,0:T(8,128)(2,1)S(1)} %collective-permute-done.refs_0_), channel_id=1, source_target_pairs={{0,1},{1,0},{2,3},{3,2},{4,5},{5,4},{6,7},{7,6},{8,9},{9,8},{10,11... | collective-permute-start | bytes 196616 | tf_op jit(solution)/shard_map/ppermute | solution.py:231
  23.3 5.6 %collective-permute-start.7 = (bf16[16,16,128]{2,1,0:T(8,128)(2,1)S(1)}, bf16[16,16,128]{2,1,0:T(8,128)(2,1)S(1)}, u32[]{:S(2)}, u32[]{:S(2)}) collective-permute-start(bf16[16,16,128]{2,1,0:T(8,128)(2,1)S(1)} %get-tuple-element.31), channel_id=1, source_target_pairs={{0,1},{1,0},{2,3},{3,2},{4,5},{5,4},{6,7},{7,6},{8,9},{9,8},{10,11... | collective-permute-start | bytes 196616 | tf_op jit(solution)/shard_map/ppermute | solution.py:231
  23.5 7.4 %collective-permute-start.8 = (bf16[16,16,128]{2,1,0:T(8,128)(2,1)S(1)}, bf16[16,16,128]{2,1,0:T(8,128)(2,1)S(1)}, u32[]{:S(2)}, u32[]{:S(2)}) collective-permute-start(bf16[16,16,128]{2,1,0:T(8,128)(2,1)S(1)} %get-tuple-element.32), channel_id=1, source_target_pairs={{0,2},{1,3},{2,0},{3,1},{4,6},{5,7},{6,4},{7,5},{8,10},{9,11},{10,... | collective-permute-start | bytes 196616 | tf_op jit(solution)/shard_map/ppermute | solution.py:231
  23.9 7.0 %collective-permute-start.9 = (bf16[16,16,128]{2,1,0:T(8,128)(2,1)S(1)}, bf16[16,16,128]{2,1,0:T(8,128)(2,1)S(1)}, u32[]{:S(2)}, u32[]{:S(2)}) collective-permute-start(bf16[16,16,128]{2,1,0:T(8,128)(2,1)S(1)} %get-tuple-element.33), channel_id=1, source_target_pairs={{0,3},{1,2},{2,1},{3,0},{4,7},{5,6},{6,5},{7,4},{8,11},{9,10},{10,... | collective-permute-start | bytes 196616 | tf_op jit(solution)/shard_map/ppermute | solution.py:231
  26.4 7.4 %collective-permute-start.11 = (bf16[16,16,128]{2,1,0:T(8,128)(2,1)S(1)}, bf16[16,16,128]{2,1,0:T(8,128)(2,1)S(1)}, u32[]{:S(2)}, u32[]{:S(2)}) collective-permute-start(bf16[16,16,128]{2,1,0:T(8,128)(2,1)S(1)} %get-tuple-element.37), channel_id=1, source_target_pairs={{0,4},{4,0},{8,12},{12,8},{1,5},{5,1},{9,13},{13,9},{2,6},{6,2},{1... | collective-permute-start | bytes 196616 | tf_op jit(solution)/shard_map/ppermute | solution.py:231
  26.5 8.7 %collective-permute-start.12 = (bf16[16,16,128]{2,1,0:T(8,128)(2,1)S(1)}, bf16[16,16,128]{2,1,0:T(8,128)(2,1)S(1)}, u32[]{:S(2)}, u32[]{:S(2)}) collective-permute-start(bf16[16,16,128]{2,1,0:T(8,128)(2,1)S(1)} %get-tuple-element.38), channel_id=1, source_target_pairs={{0,8},{4,12},{8,0},{12,4},{1,9},{5,13},{9,1},{13,5},{2,10},{6,14},... | collective-permute-start | bytes 196616 | tf_op jit(solution)/shard_map/ppermute | solution.py:231
  28.8 6.4 %collective-permute-start.13 = (bf16[16,16,128]{2,1,0:T(8,128)(2,1)S(1)}, bf16[16,16,128]{2,1,0:T(8,128)(2,1)S(1)}, u32[]{:S(2)}, u32[]{:S(2)}) collective-permute-start(bf16[16,16,128]{2,1,0:T(8,128)(2,1)S(1)} %get-tuple-element.39), channel_id=1, source_target_pairs={{0,12},{4,8},{8,4},{12,0},{1,13},{5,9},{9,5},{13,1},{2,14},{6,10},... | collective-permute-start | bytes 196616 | tf_op jit(solution)/shard_map/ppermute | solution.py:231
  30.9 2.1 %copy-start = (bf16[128,640]{1,0:T(8,128)(2,1)S(1)}, bf16[128,640]{1,0:T(8,128)(2,1)}, u32[]{:S(2)}) copy-start(bf16[128,640]{1,0:T(8,128)(2,1)} %refs_8_.1) | copy-start | bytes 491524
  30.9 2.1 %copy-start.1 = (bf16[128,128]{1,0:T(8,128)(2,1)S(1)}, bf16[128,128]{1,0:T(8,128)(2,1)}, u32[]{:S(2)}) copy-start(bf16[128,128]{1,0:T(8,128)(2,1)} %out_weight_ref.1) | copy-start | bytes 98308
  30.9 8.8 %collective-permute-start.10 = (bf16[16,16,128]{2,1,0:T(8,128)(2,1)S(1)}, bf16[16,16,128]{2,1,0:T(8,128)(2,1)S(1)}, u32[]{:S(2)}, u32[]{:S(2)}) collective-permute-start(bf16[16,16,128]{2,1,0:T(8,128)(2,1)S(1)} %shard_map.81), channel_id=1, source_target_pairs={{0,0},{1,4},{2,8},{3,12},{4,1},{5,5},{6,9},{7,13},{8,2},{9,6},{10,... | collective-permute-start | bytes 196616 | tf_op jit(solution)/shard_map/ppermute | solution.py:234

commit v3 on v2

--- a/solution.py
+++ b/solution.py
@@ -114,26 +114,30 @@
     upstream_ref[...] = dot_t(lin_grad, out_weight_ref[...])
 
 
-def weighted_sums(weights, start, terms, out):
+def weighted_sums(weights, start, terms, out, base=None):
     def step(k, _):
         total = weights[start + k, pl.ds(0, 1), :] * terms[0]
         for n in range(1, len(terms)):
             total = total + weights[start + k, pl.ds(n, 1), :] * terms[n]
-        out[k] = total.astype(bf16)
+        if base is not None:
+            total = total + base[k]
+        out[k] = total.astype(out.dtype)
         return 0
 
     lax.fori_loop(0, out.shape[0], step, 0)
+
+
+def flip(grid_size):
+    return lax.rem(lax.axis_index("row"), 2) * (grid_size // 2)
 
 
 def triangle_kernel(grid_size, *refs):
     left_in, right_in = refs[:grid_size], refs[grid_size : 2 * grid_size]
-    upstream_ref = refs[2 * grid_size]
-    tri_normed_ref, left, grad, *left_out = refs[2 * grid_size + 1 : -1]
-    right = refs[-1]
+    upstream_ref, tri_normed_ref, right, grad, left = refs[2 * grid_size :]
     size, _, channels = left_in[0].shape
-    row, col = lax.axis_index("row"), lax.axis_index("col")
+    row, held = lax.axis_index("row"), lax.axis_index("col") ^ flip(grid_size)
     for step in range(grid_size):
-        left[pl.ds((col ^ step) * size, size)] = left_in[step][...].astype(f32)
+        left[pl.ds((held ^ step) * size, size)] = left_in[step][...].astype(f32)
         right[pl.ds((row ^ step) * size, size)] = right_in[step][...].astype(f32)
 
     def step(k, sums):
@@ -147,19 +151,35 @@
         tri_normed, scale = normalize(sums[i])
         tri_normed_ref[here, :] = tri_normed
         back = normalize_back(tri_normed, scale, upstream_ref[here, :])
-        grad[here, :] = back.astype(bf16).astype(f32)
-
+        grad[i] = back.astype(bf16)
+
+
+def left_terms_kernel(grid_size, steps, right, grad_ref, *refs):
+    out, grad = refs[:-1], refs[-1]
+    size, _, channels = grad_ref.shape
+    grad[...] = grad_ref[...].astype(f32).reshape(size * size, channels)
+    held = lax.axis_index("col") ^ flip(grid_size)
     grads = [grad[pl.ds(j, size, stride=size), :] for j in range(size)]
+    for step, ref in zip(steps, out):
+        weighted_sums(right, (held ^ step) * size, grads, ref)
+
+
+def panel_kernel(grid_size, *refs):
+    panel = refs[grid_size]
+    size = refs[0].shape[0]
+    col = lax.axis_index("col")
     for step in range(grid_size):
-        weighted_sums(right, (col ^ step) * size, grads, left_out[step])
-
-
-def right_kernel(grid_size, left, grad, *right_out):
-    size = right_out[0].shape[0]
-    row = lax.axis_index("row")
-    grads = [grad[pl.ds(i * size, size), :] for i in range(size)]
-    for step in range(grid_size):
-        weighted_sums(left, (row ^ step) * size, grads, right_out[step])
+        panel[pl.ds((col ^ step) * size, size)] = refs[step][...].astype(f32)
+
+
+def right_grad_kernel(steps, panel, *refs):
+    grads, refs = refs[: len(steps)], refs[len(steps) :]
+    out, base = refs[-1], refs[0] if len(refs) > 1 else None
+    size = out.shape[0]
+    for step, grad in zip(steps, grads):
+        start = (lax.axis_index("row") ^ step) * size
+        weighted_sums(panel, start, [grad[i].astype(f32) for i in range(size)], out, base)
+        base = out
 
 
 def update_kernel(
@@ -173,23 +193,20 @@
     normed_grad_ref[...] = dot_t(out_gate_grad, weights_ref[:, 4 * channels :])
 
 
-def sum_kernel(grid_size, *refs):
+def sum_kernel(*refs):
     total = refs[0][...].astype(f32)
-    for ref in refs[1:grid_size]:
+    for ref in refs[1:-1]:
         total = total + ref[...].astype(f32)
-    refs[grid_size][...] = total.astype(bf16)
-
-
-def back_kernel(grid_size, left_ref, *refs):
-    right_in = refs[:grid_size]
-    normed_ref, scale_ref, factor_ref, partial_ref, weights_ref, out_ref = refs[grid_size:]
+    refs[-1][...] = total.astype(bf16)
+
+
+def back_kernel(step, left_ref, grad_ref, base, panel, normed_ref, scale_ref, factor_ref, partial_ref, weights_ref,
+                out_ref, right_ref):
+    right_grad_kernel((step,), panel, grad_ref, base, right_ref)
     size, _, channels = out_ref.shape
     pairs = size * size
     left = left_ref[...].astype(f32).reshape(pairs, channels)
-    right = right_in[0][...].astype(f32)
-    for ref in right_in[1:]:
-        right = right + ref[...].astype(f32)
-    right = right.astype(bf16).astype(f32).reshape(pairs, channels)
+    right = right_ref[...].reshape(pairs, channels)
     grads = jnp.concatenate(
         [(total * factor_ref[block]).astype(bf16) for block, total in enumerate((left, left, right, right))],
         axis=1,
@@ -227,11 +244,26 @@
     tile = jax.ShapeDtypeStruct((size, size, channels), bf16)
     flat = jax.ShapeDtypeStruct((pairs, channels), f32)
 
+    wide = jax.ShapeDtypeStruct((size, size, channels), f32)
+    panel = jax.ShapeDtypeStruct((n * size, size, channels), f32)
+
     def swap(values, axis, step):
         return lax.ppermute(values, axis, [(a, a ^ step) for a in range(n)])
 
-    def mirror(values):
-        return lax.ppermute(values, ("row", "col"), [(a * n + b, b * n + a) for a in range(n) for b in range(n)])
+    def gather(values, axis):
+        held = {0: values}
+        bit = n // 2
+        while bit:
+            held.update({step ^ bit: swap(held[step], axis, bit) for step in list(held)})
+            bit //= 2
+        return [held[step] for step in range(n)]
+
+    def seat(a, b):
+        return b * n + (a ^ (b % 2 * (n // 2)))
+
+    def mirror(values, back=False):
+        pairs = [(a * n + b, seat(a, b)) for a in range(n) for b in range(n)]
+        return lax.ppermute(values, ("row", "col"), [(t, s) if back else (s, t) for s, t in pairs])
 
     left, right = call(
         tiles_kernel, (tile, tile), pair_acts, pair_mask, crop_length, in_weights,
@@ -244,7 +276,8 @@
         ],
     )
     mirrored = mirror(left)
-    rights = [right] + [swap(right, "row", step) for step in range(n - 1, 0, -1)][::-1]
+    rights = gather(right, "row")
+    own_lefts = gather(left, "col")
     normed, scale, factors, out_open, gate_factor, upstream = call(
         factors_kernel,
         (flat, flat, jax.ShapeDtypeStruct((4, pairs, channels), f32), flat, flat, flat),
@@ -259,31 +292,40 @@
             pltpu.SemaphoreType.DMA((5,)),
         ],
     )
-    lefts = [mirrored] + [swap(mirrored, "col", step) for step in range(1, n)]
-    panel = jax.ShapeDtypeStruct((n * size, size, channels), f32)
-    tri_normed, left_panel, tri_grad, *left_terms = call(
+    lefts = gather(mirrored, "col")
+    tri_normed, right_panel, tri_grad = call(
         functools.partial(triangle_kernel, n),
-        (flat, panel, flat) + (tile,) * n,
+        (flat, panel, tile),
         *lefts, *rights, upstream,
         scratch=[pltpu.VMEM(panel.shape, f32)],
-        flops=4 * n * size * pairs * channels,
-    )
-    left_terms = [left_terms[0]] + [swap(left_terms[step], "col", step) for step in range(1, n)]
-    right_terms = call(
-        functools.partial(right_kernel, n), (tile,) * n, left_panel, tri_grad,
         flops=2 * n * size * pairs * channels,
     )
-    right_terms = [right_terms[0]] + [swap(right_terms[step], "row", step) for step in range(1, n)]
+    terms = {}
+    for steps in (tuple(range(n - 1, 1, -1)), (1, 0)):
+        outs = call(
+            functools.partial(left_terms_kernel, n, steps), (tile,) * len(steps), right_panel, tri_grad,
+            scratch=[pltpu.VMEM((pairs, channels), f32)],
+            flops=2 * len(steps) * size * pairs * channels,
+        )
+        terms.update({step: swap(out, "col", step) if step else out for step, out in zip(steps, outs)})
+    grads = gather(tri_grad, "row")
+    (own_panel,) = call(functools.partial(panel_kernel, n), (panel,), *own_lefts)
     update, partial = call(
         update_kernel, (tile, flat), tri_normed, out_open, gate_factor, in_weights, out_weight,
         flops=4 * pairs * channels * channels,
     )
-    (left_sum,) = call(functools.partial(sum_kernel, n), (tile,), *left_terms)
-    left_grad = mirror(left_sum)
+    early = tuple(range(n - 1))
+    (right_grad,) = call(
+        functools.partial(right_grad_kernel, early), (wide,), own_panel, *grads[:-1],
+        flops=2 * len(early) * size * pairs * channels,
+    )
+    (left_sum,) = call(sum_kernel, (tile,), *terms.values())
+    left_grad = mirror(left_sum, back=True)
     (pair_grad,) = call(
-        functools.partial(back_kernel, n), (tile,),
-        left_grad, *right_terms, normed, scale, factors, partial, in_weights,
-        flops=2 * pairs * channels * 4 * channels,
+        functools.partial(back_kernel, n - 1), (tile,),
+        left_grad, grads[-1], right_grad, own_panel, normed, scale, factors, partial, in_weights,
+        scratch=[pltpu.VMEM(wide.shape, f32)],
+        flops=2 * pairs * channels * (4 * channels + size),
     )
     return (update, pair_grad)
 

time: 40.9 us -> 40.5 us (level)
  the two profiles are of different devices: /device:TPU:6 before, /device:TPU:0 now
where the time goes in v3:
time: 40.5 us; the launch traced here: 40.3 us
  starting transfers between devices  22.5 us (56%)
  Pallas kernels  9 us (22%)
  waiting for transfers between devices  7.36 us (18%)
  between operations  1.43 us (4%)
    ppermute x15, starting transfers between devices, swap(): return lax.ppermute(values, axis, [(a, a ^ step) for a in range(n)])  21.1 us
    pallas_call x10, Pallas kernels, call(): pl.pallas_call(kernel, out_shape=tuple(outs), in_specs=specs, out_specs=(...  9 us
    ppermute x15, waiting for transfers between devices, swap(): return lax.ppermute(values, axis, [(a, a ^ step) for a in range(n)])  7.35 us
    ppermute x2, starting transfers between devices, mirror(): lax.ppermute(values, ('row', 'col'), [(t, s) if back else (s, t) for s, t...  1.46 us
  transfers between devices with their start and end apart: 17, of which 5 were waited for; matrix products, arithmetic and copies ran while one was open for 0% of the time, Pallas kernels for 16%

profile of v3, /device:TPU:0, one launch (start us, length us, event | category | flops | bytes accessed | tf_op | source)
XLA Modules:
  0.0 40.3 jit_solution(490302923036931698)
XLA Ops:
  1.3 1.4 %shard_map.77 = (bf16[16,16,128]{2,1,0:T(8,128)(2,1)S(1)}, bf16[16,16,128]{2,1,0:T(8,128)(2,1)S(1)}) custom-call(bf16[16,16,128]{2,1,0:T(8,128)(2,1)} %acts_in.3, s32[16,16]{1,0:T(8,128)} %mask_in.3, s32[1]{0:T(128)S(6)} %copy.8.crop_ref, bf16[128,640]{1,0:T(8,128)(2,1)} %weights_ref.3), custom_call_target="tpu_custom_call" | custom-call | flops 33554432 | bytes 361476 | tf_op jit(solution)/shard_map/pallas_call | solution.py:229
  2.7 0.7 %collective-permute-start = (bf16[16,16,128]{2,1,0:T(8,128)(2,1)S(1)}, bf16[16,16,128]{2,1,0:T(8,128)(2,1)S(1)}, u32[]{:S(2)}, u32[]{:S(2)}) collective-permute-start(bf16[16,16,128]{2,1,0:T(8,128)(2,1)S(1)} %get-tuple-element.19.refs_0_), channel_id=1, source_target_pairs={{0,0},{1,6},{2,8},{3,14},{4,1},{5,7},{6,9},{7,15},{8,2},{9,4},{10,... | collective-permute-start | bytes 196616 | tf_op jit(solution)/shard_map/ppermute | solution.py:266
  3.4 6.6 %collective-permute-start.5 = (bf16[16,16,128]{2,1,0:T(8,128)(2,1)S(1)}, bf16[16,16,128]{2,1,0:T(8,128)(2,1)S(1)}, u32[]{:S(2)}, u32[]{:S(2)}) collective-permute-start(bf16[16,16,128]{2,1,0:T(8,128)(2,1)S(1)} %get-tuple-element.20.refs_4_), channel_id=1, source_target_pairs={{0,8},{4,12},{8,0},{12,4},{1,9},{5,13},{9,1},{13,5},{2,10},{6,14},... | collective-permute-start | bytes 196616 | tf_op jit(solution)/shard_map/ppermute | solution.py:251
  10.0 6.1 %collective-permute-start.2 = (bf16[16,16,128]{2,1,0:T(8,128)(2,1)S(1)}, bf16[16,16,128]{2,1,0:T(8,128)(2,1)S(1)}, u32[]{:S(2)}, u32[]{:S(2)}) collective-permute-start(bf16[16,16,128]{2,1,0:T(8,128)(2,1)S(1)} %collective-permute-done.refs_0_), channel_id=1, source_target_pairs={{0,2},{1,3},{2,0},{3,1},{4,6},{5,7},{6,4},{7,5},{8,10},{9,11},{10,... | collective-permute-start | bytes 196616 | tf_op jit(solution)/shard_map/ppermute | solution.py:251
  16.1 2.0 %collective-permute-start.6 = (bf16[16,16,128]{2,1,0:T(8,128)(2,1)S(1)}, bf16[16,16,128]{2,1,0:T(8,128)(2,1)S(1)}, u32[]{:S(2)}, u32[]{:S(2)}) collective-permute-start(bf16[16,16,128]{2,1,0:T(8,128)(2,1)S(1)} %collective-permute-done.5.refs_6_), channel_id=1, source_target_pairs={{0,4},{4,0},{8,12},{12,8},{1,5},{5,1},{9,13},{13,9},{2,6},{6,2},{1... | collective-permute-start | bytes 196616 | tf_op jit(solution)/shard_map/ppermute | solution.py:251
  18.1 0.2 collective-permute-done.2.refs_2_
  18.4 2.0 %collective-permute-start.14 = (bf16[16,16,128]{2,1,0:T(8,128)(2,1)S(1)}, bf16[16,16,128]{2,1,0:T(8,128)(2,1)S(1)}, u32[]{:S(2)}, u32[]{:S(2)}) collective-permute-start(bf16[16,16,128]{2,1,0:T(8,128)(2,1)S(1)} %get-tuple-element.19.refs_0_), channel_id=1, source_target_pairs={{0,2},{1,3},{2,0},{3,1},{4,6},{5,7},{6,4},{7,5},{8,10},{9,11},{10,... | collective-permute-start | bytes 196616 | tf_op jit(solution)/shard_map/ppermute | solution.py:251
  20.4 1.5 %shard_map.78 = (f32[256,128]{1,0:T(8,128)S(1)}, f32[256,128]{1,0:T(8,128)S(1)}, f32[4,256,128]{2,1,0:T(8,128)S(1)}, f32[256,128]{1,0:T(8,128)S(1)}, f32[256,128]{1,0:T(8,128)S(1)}, /*index=5*/f32[256,128]{1,0:T(8,128)S(1)}) custom-call(bf16[16,16,128]{2,1,0:T(8,128)(2,1)} %acts_in.3, s32[16,16]{1,0:T(8,128)} %mask_in.3, s32[1]{0:T(128)S(6)} %copy.8.crop_ref, ...), custom_call_target="tpu_custom_call" | custom-call | flops 50331648 | bytes 1508356 | tf_op jit(solution)/shard_map/pallas_call | solution.py:229
  21.9 1.6 %shard_map.79 = (f32[256,128]{1,0:T(8,128)S(1)}, f32[64,16,128]{2,1,0:T(8,128)S(1)}, bf16[16,16,128]{2,1,0:T(8,128)(2,1)S(1)}) custom-call(bf16[16,16,128]{2,1,0:T(8,128)(2,1)S(1)} %collective-permute-done.refs_0_, bf16[16,16,128]{2,1,0:T(8,128)(2,1)S(1)} %collective-permute-done.1.refs_1_, bf16[16,16,128]{2,1,0:T(8,128)(2,1)S(1)} %collective-permute-done.2.refs_2_, ...), custom_call_target="tpu_custom_call" | custom-call | flops 4194304 | bytes 1376256 | tf_op jit(solution)/shard_map/pallas_call | solution.py:229
  23.5 0.7 %shard_map.81 = (bf16[16,16,128]{2,1,0:T(8,128)(2,1)S(1)}, bf16[16,16,128]{2,1,0:T(8,128)(2,1)S(1)}) custom-call(f32[64,16,128]{2,1,0:T(8,128)S(1)} %get-tuple-element.26.right, bf16[16,16,128]{2,1,0:T(8,128)(2,1)S(1)} %get-tuple-element.27.grad_ref.refs_0_), custom_call_target="tpu_custom_call" | custom-call | flops 2097152 | bytes 720896 | tf_op jit(solution)/shard_map/pallas_call | solution.py:229
  24.4 1.7 %collective-permute-start.8 = (bf16[16,16,128]{2,1,0:T(8,128)(2,1)S(1)}, bf16[16,16,128]{2,1,0:T(8,128)(2,1)S(1)}, u32[]{:S(2)}, u32[]{:S(2)}) collective-permute-start(bf16[16,16,128]{2,1,0:T(8,128)(2,1)S(1)} %get-tuple-element.29), channel_id=1, source_target_pairs={{0,2},{1,3},{2,0},{3,1},{4,6},{5,7},{6,4},{7,5},{8,10},{9,11},{10,... | collective-permute-start | bytes 196616 | tf_op jit(solution)/shard_map/ppermute | solution.py:251
  26.1 0.7 %shard_map.82 = (bf16[16,16,128]{2,1,0:T(8,128)(2,1)S(1)}, bf16[16,16,128]{2,1,0:T(8,128)(2,1)S(1)}) custom-call(f32[64,16,128]{2,1,0:T(8,128)S(1)} %get-tuple-element.26.right, bf16[16,16,128]{2,1,0:T(8,128)(2,1)S(1)} %get-tuple-element.27.grad_ref.refs_0_), custom_call_target="tpu_custom_call" | custom-call | flops 2097152 | bytes 720896 | tf_op jit(solution)/shard_map/pallas_call | solution.py:229
  26.8 0.5 %collective-permute-start.11 = (bf16[16,16,128]{2,1,0:T(8,128)(2,1)S(1)}, bf16[16,16,128]{2,1,0:T(8,128)(2,1)S(1)}, u32[]{:S(2)}, u32[]{:S(2)}) collective-permute-start(bf16[16,16,128]{2,1,0:T(8,128)(2,1)S(1)} %get-tuple-element.27.grad_ref.refs_0_), channel_id=1, source_target_pairs={{0,8},{4,12},{8,0},{12,4},{1,9},{5,13},{9,1},{13,5},{2,10},{6,14},... | collective-permute-start | bytes 196616 | tf_op jit(solution)/shard_map/ppermute | solution.py:251
  27.4 0.9 %collective-permute-done.7.refs_0_ = bf16[16,16,128]{2,1,0:T(8,128)(2,1)S(1)} collective-permute-done((bf16[16,16,128]{2,1,0:T(8,128)(2,1)S(1)}, bf16[16,16,128]{2,1,0:T(8,128)(2,1)S(1)}, u32[]{:S(2)}, u32[]{:S(2)}) %collective-permute-start.7) | collective-permute-done | bytes 65568 | tf_op jit(solution)/shard_map/ppermute | solution.py:251
  28.3 0.5 %collective-permute-start.15 = (bf16[16,16,128]{2,1,0:T(8,128)(2,1)S(1)}, bf16[16,16,128]{2,1,0:T(8,128)(2,1)S(1)}, u32[]{:S(2)}, u32[]{:S(2)}) collective-permute-start(bf16[16,16,128]{2,1,0:T(8,128)(2,1)S(1)} %collective-permute-done.14.refs_2_), channel_id=1, source_target_pairs={{0,1},{1,0},{2,3},{3,2},{4,5},{5,4},{6,7},{7,6},{8,9},{9,8},{10,11... | collective-permute-start | bytes 196616 | tf_op jit(solution)/shard_map/ppermute | solution.py:251
  28.8 1.3 %collective-permute-done.8.refs_1_ = bf16[16,16,128]{2,1,0:T(8,128)(2,1)S(1)} collective-permute-done((bf16[16,16,128]{2,1,0:T(8,128)(2,1)S(1)}, bf16[16,16,128]{2,1,0:T(8,128)(2,1)S(1)}, u32[]{:S(2)}, u32[]{:S(2)}) %collective-permute-start.8) | collective-permute-done | bytes 65568 | tf_op jit(solution)/shard_map/ppermute | solution.py:251
  30.0 0.5 %collective-permute-start.16 = (bf16[16,16,128]{2,1,0:T(8,128)(2,1)S(1)}, bf16[16,16,128]{2,1,0:T(8,128)(2,1)S(1)}, u32[]{:S(2)}, u32[]{:S(2)}) collective-permute-start(bf16[16,16,128]{2,1,0:T(8,128)(2,1)S(1)} %get-tuple-element.27.grad_ref.refs_0_), channel_id=1, source_target_pairs={{0,4},{4,0},{8,12},{12,8},{1,5},{5,1},{9,13},{13,9},{2,6},{6,2},{1... | collective-permute-start | bytes 196616 | tf_op jit(solution)/shard_map/ppermute | solution.py:251
  30.6 0.8 %collective-permute-start.10 = (bf16[16,16,128]{2,1,0:T(8,128)(2,1)S(1)}, bf16[16,16,128]{2,1,0:T(8,128)(2,1)S(1)}, u32[]{:S(2)}, u32[]{:S(2)}) collective-permute-start(bf16[16,16,128]{2,1,0:T(8,128)(2,1)S(1)} %shard_map.83), channel_id=1, source_target_pairs={{0,0},{6,1},{8,2},{14,3},{1,4},{7,5},{9,6},{15,7},{2,8},{4,9},{10,... | collective-permute-start | bytes 196616 | tf_op jit(solution)/shard_map/ppermute | solution.py:266
  31.4 2.0 %collective-permute-done.11.refs_2_ = bf16[16,16,128]{2,1,0:T(8,128)(2,1)S(1)} collective-permute-done((bf16[16,16,128]{2,1,0:T(8,128)(2,1)S(1)}, bf16[16,16,128]{2,1,0:T(8,128)(2,1)S(1)}, u32[]{:S(2)}, u32[]{:S(2)}) %collective-permute-start.11) | collective-permute-done | bytes 65568 | tf_op jit(solution)/shard_map/ppermute | solution.py:251
  33.5 0.8 %collective-permute-start.12 = (bf16[16,16,128]{2,1,0:T(8,128)(2,1)S(1)}, bf16[16,16,128]{2,1,0:T(8,128)(2,1)S(1)}, u32[]{:S(2)}, u32[]{:S(2)}) collective-permute-start(bf16[16,16,128]{2,1,0:T(8,128)(2,1)S(1)} %collective-permute-done.11.refs_2_), channel_id=1, source_target_pairs={{0,4},{4,0},{8,12},{12,8},{1,5},{5,1},{9,13},{13,9},{2,6},{6,2},{1... | collective-permute-start | bytes 196616 | tf_op jit(solution)/shard_map/ppermute | solution.py:251
  34.3 0.8 %shard_map.80 = (bf16[16,16,128]{2,1,0:T(8,128)(2,1)}, f32[256,128]{1,0:T(8,128)S(1)}) custom-call(f32[256,128]{1,0:T(8,128)S(1)} %get-tuple-element.22.tri_normed_ref, f32[256,128]{1,0:T(8,128)S(1)} %get-tuple-element.23.open_ref, f32[256,128]{1,0:T(8,128)S(1)} %get-tuple-element.24.gate_factor_ref, bf16[128,640]{1,0:T(8,128)(2,1)S(1)} %copy-done, ...), custom_call_target="tpu_custom_call" | custom-call | flops 16777216 | bytes 786432 | tf_op jit(solution)/shard_map/pallas_call | solution.py:229
  35.1 1.0 %shard_map.85.base = f32[16,16,128]{2,1,0:T(8,128)S(1)} custom-call(f32[64,16,128]{2,1,0:T(8,128)S(1)} %shard_map.84.panel, bf16[16,16,128]{2,1,0:T(8,128)(2,1)S(1)} %get-tuple-element.27.grad_ref.refs_0_, bf16[16,16,128]{2,1,0:T(8,128)(2,1)S(1)} %collective-permute-done.16.refs_1_, bf16[16,16,128]{2,1,0:T(8,128)(2,1)S(1)} %collective-permute-done.11.refs_2_), custom_call_target="tpu_custom_call" | custom-call | flops 3145728 | bytes 851968 | tf_op jit(solution)/shard_map/pallas_call | solution.py:229
  36.2 2.9 %collective-permute-done.12.grad_ref = bf16[16,16,128]{2,1,0:T(8,128)(2,1)S(1)} collective-permute-done((bf16[16,16,128]{2,1,0:T(8,128)(2,1)S(1)}, bf16[16,16,128]{2,1,0:T(8,128)(2,1)S(1)}, u32[]{:S(2)}, u32[]{:S(2)}) %collective-permute-start.12) | collective-permute-done | bytes 65568 | tf_op jit(solution)/shard_map/ppermute | solution.py:251
  39.1 1.3 %shard_map.86 = bf16[16,16,128]{2,1,0:T(8,128)(2,1)} custom-call(bf16[16,16,128]{2,1,0:T(8,128)(2,1)S(1)} %collective-permute-done.10.left_ref, bf16[16,16,128]{2,1,0:T(8,128)(2,1)S(1)} %collective-permute-done.12.grad_ref, f32[16,16,128]{2,1,0:T(8,128)S(1)} %shard_map.85.base, f32[64,16,128]{2,1,0:T(8,128)S(1)} %shard_map.84.panel, ...), custom_call_target="tpu_custom_call" | custom-call | flops 34603008 | bytes 1933312 | tf_op jit(solution)/shard_map/pallas_call | solution.py:229
  (24 shorter events, 0.4 us)
Async XLA Ops:
  2.7 7.3 %collective-permute-start = (bf16[16,16,128]{2,1,0:T(8,128)(2,1)S(1)}, bf16[16,16,128]{2,1,0:T(8,128)(2,1)S(1)}, u32[]{:S(2)}, u32[]{:S(2)}) collective-permute-start(bf16[16,16,128]{2,1,0:T(8,128)(2,1)S(1)} %get-tuple-element.19.refs_0_), channel_id=1, source_target_pairs={{0,0},{1,6},{2,8},{3,14},{4,1},{5,7},{6,9},{7,15},{8,2},{9,4},{10,... | collective-permute-start | bytes 196616 | tf_op jit(solution)/shard_map/ppermute | solution.py:266
  3.4 12.7 %collective-permute-start.5 = (bf16[16,16,128]{2,1,0:T(8,128)(2,1)S(1)}, bf16[16,16,128]{2,1,0:T(8,128)(2,1)S(1)}, u32[]{:S(2)}, u32[]{:S(2)}) collective-permute-start(bf16[16,16,128]{2,1,0:T(8,128)(2,1)S(1)} %get-tuple-element.20.refs_4_), channel_id=1, source_target_pairs={{0,8},{4,12},{8,0},{12,4},{1,9},{5,13},{9,1},{13,5},{2,10},{6,14},... | collective-permute-start | bytes 196616 | tf_op jit(solution)/shard_map/ppermute | solution.py:251
  10.0 8.3 %collective-permute-start.2 = (bf16[16,16,128]{2,1,0:T(8,128)(2,1)S(1)}, bf16[16,16,128]{2,1,0:T(8,128)(2,1)S(1)}, u32[]{:S(2)}, u32[]{:S(2)}) collective-permute-start(bf16[16,16,128]{2,1,0:T(8,128)(2,1)S(1)} %collective-permute-done.refs_0_), channel_id=1, source_target_pairs={{0,2},{1,3},{2,0},{3,1},{4,6},{5,7},{6,4},{7,5},{8,10},{9,11},{10,... | collective-permute-start | bytes 196616 | tf_op jit(solution)/shard_map/ppermute | solution.py:251
  16.1 5.8 %collective-permute-start.4 = (bf16[16,16,128]{2,1,0:T(8,128)(2,1)S(1)}, bf16[16,16,128]{2,1,0:T(8,128)(2,1)S(1)}, u32[]{:S(2)}, u32[]{:S(2)}) collective-permute-start(bf16[16,16,128]{2,1,0:T(8,128)(2,1)S(1)} %get-tuple-element.20.refs_4_), channel_id=1, source_target_pairs={{0,4},{4,0},{8,12},{12,8},{1,5},{5,1},{9,13},{13,9},{2,6},{6,2},{1... | collective-permute-start | bytes 196616 | tf_op jit(solution)/shard_map/ppermute | solution.py:251
  16.1 5.8 %collective-permute-start.1 = (bf16[16,16,128]{2,1,0:T(8,128)(2,1)S(1)}, bf16[16,16,128]{2,1,0:T(8,128)(2,1)S(1)}, u32[]{:S(2)}, u32[]{:S(2)}) collective-permute-start(bf16[16,16,128]{2,1,0:T(8,128)(2,1)S(1)} %collective-permute-done.refs_0_), channel_id=1, source_target_pairs={{0,1},{1,0},{2,3},{3,2},{4,5},{5,4},{6,7},{7,6},{8,9},{9,8},{10,11... | collective-permute-start | bytes 196616 | tf_op jit(solution)/shard_map/ppermute | solution.py:251
  16.1 5.8 %collective-permute-start.6 = (bf16[16,16,128]{2,1,0:T(8,128)(2,1)S(1)}, bf16[16,16,128]{2,1,0:T(8,128)(2,1)S(1)}, u32[]{:S(2)}, u32[]{:S(2)}) collective-permute-start(bf16[16,16,128]{2,1,0:T(8,128)(2,1)S(1)} %collective-permute-done.5.refs_6_), channel_id=1, source_target_pairs={{0,4},{4,0},{8,12},{12,8},{1,5},{5,1},{9,13},{13,9},{2,6},{6,2},{1... | collective-permute-start | bytes 196616 | tf_op jit(solution)/shard_map/ppermute | solution.py:251
  18.4 3.5 %collective-permute-start.3 = (bf16[16,16,128]{2,1,0:T(8,128)(2,1)S(1)}, bf16[16,16,128]{2,1,0:T(8,128)(2,1)S(1)}, u32[]{:S(2)}, u32[]{:S(2)}) collective-permute-start(bf16[16,16,128]{2,1,0:T(8,128)(2,1)S(1)} %collective-permute-done.2.refs_2_), channel_id=1, source_target_pairs={{0,1},{1,0},{2,3},{3,2},{4,5},{5,4},{6,7},{7,6},{8,9},{9,8},{10,11... | collective-permute-start | bytes 196616 | tf_op jit(solution)/shard_map/ppermute | solution.py:251
  18.4 9.0 %collective-permute-start.14 = (bf16[16,16,128]{2,1,0:T(8,128)(2,1)S(1)}, bf16[16,16,128]{2,1,0:T(8,128)(2,1)S(1)}, u32[]{:S(2)}, u32[]{:S(2)}) collective-permute-start(bf16[16,16,128]{2,1,0:T(8,128)(2,1)S(1)} %get-tuple-element.19.refs_0_), channel_id=1, source_target_pairs={{0,2},{1,3},{2,0},{3,1},{4,6},{5,7},{6,4},{7,5},{8,10},{9,11},{10,... | collective-permute-start | bytes 196616 | tf_op jit(solution)/shard_map/ppermute | solution.py:251
  24.2 4.1 %collective-permute-start.7 = (bf16[16,16,128]{2,1,0:T(8,128)(2,1)S(1)}, bf16[16,16,128]{2,1,0:T(8,128)(2,1)S(1)}, u32[]{:S(2)}, u32[]{:S(2)}) collective-permute-start(bf16[16,16,128]{2,1,0:T(8,128)(2,1)S(1)} %get-tuple-element.28), channel_id=1, source_target_pairs={{0,3},{1,2},{2,1},{3,0},{4,7},{5,6},{6,5},{7,4},{8,11},{9,10},{10,... | collective-permute-start | bytes 196616 | tf_op jit(solution)/shard_map/ppermute | solution.py:251
  24.4 5.7 %collective-permute-start.8 = (bf16[16,16,128]{2,1,0:T(8,128)(2,1)S(1)}, bf16[16,16,128]{2,1,0:T(8,128)(2,1)S(1)}, u32[]{:S(2)}, u32[]{:S(2)}) collective-permute-start(bf16[16,16,128]{2,1,0:T(8,128)(2,1)S(1)} %get-tuple-element.29), channel_id=1, source_target_pairs={{0,2},{1,3},{2,0},{3,1},{4,6},{5,7},{6,4},{7,5},{8,10},{9,11},{10,... | collective-permute-start | bytes 196616 | tf_op jit(solution)/shard_map/ppermute | solution.py:251
  26.7 3.8 %collective-permute-start.9 = (bf16[16,16,128]{2,1,0:T(8,128)(2,1)S(1)}, bf16[16,16,128]{2,1,0:T(8,128)(2,1)S(1)}, u32[]{:S(2)}, u32[]{:S(2)}) collective-permute-start(bf16[16,16,128]{2,1,0:T(8,128)(2,1)S(1)} %get-tuple-element.30), channel_id=1, source_target_pairs={{0,1},{1,0},{2,3},{3,2},{4,5},{5,4},{6,7},{7,6},{8,9},{9,8},{10,11... | collective-permute-start | bytes 196616 | tf_op jit(solution)/shard_map/ppermute | solution.py:251
  26.8 6.6 %collective-permute-start.11 = (bf16[16,16,128]{2,1,0:T(8,128)(2,1)S(1)}, bf16[16,16,128]{2,1,0:T(8,128)(2,1)S(1)}, u32[]{:S(2)}, u32[]{:S(2)}) collective-permute-start(bf16[16,16,128]{2,1,0:T(8,128)(2,1)S(1)} %get-tuple-element.27.grad_ref.refs_0_), channel_id=1, source_target_pairs={{0,8},{4,12},{8,0},{12,4},{1,9},{5,13},{9,1},{13,5},{2,10},{6,14},... | collective-permute-start | bytes 196616 | tf_op jit(solution)/shard_map/ppermute | solution.py:251
  27.4 6.9 %collective-permute-start.13 = (bf16[16,16,128]{2,1,0:T(8,128)(2,1)S(1)}, bf16[16,16,128]{2,1,0:T(8,128)(2,1)S(1)}, u32[]{:S(2)}, u32[]{:S(2)}) collective-permute-start(bf16[16,16,128]{2,1,0:T(8,128)(2,1)S(1)} %get-tuple-element.19.refs_0_), channel_id=1, source_target_pairs={{0,1},{1,0},{2,3},{3,2},{4,5},{5,4},{6,7},{7,6},{8,9},{9,8},{10,11... | collective-permute-start | bytes 196616 | tf_op jit(solution)/shard_map/ppermute | solution.py:251
  28.3 6.0 %collective-permute-start.15 = (bf16[16,16,128]{2,1,0:T(8,128)(2,1)S(1)}, bf16[16,16,128]{2,1,0:T(8,128)(2,1)S(1)}, u32[]{:S(2)}, u32[]{:S(2)}) collective-permute-start(bf16[16,16,128]{2,1,0:T(8,128)(2,1)S(1)} %collective-permute-done.14.refs_2_), channel_id=1, source_target_pairs={{0,1},{1,0},{2,3},{3,2},{4,5},{5,4},{6,7},{7,6},{8,9},{9,8},{10,11... | collective-permute-start | bytes 196616 | tf_op jit(solution)/shard_map/ppermute | solution.py:251
  30.0 5.1 %collective-permute-start.16 = (bf16[16,16,128]{2,1,0:T(8,128)(2,1)S(1)}, bf16[16,16,128]{2,1,0:T(8,128)(2,1)S(1)}, u32[]{:S(2)}, u32[]{:S(2)}) collective-permute-start(bf16[16,16,128]{2,1,0:T(8,128)(2,1)S(1)} %get-tuple-element.27.grad_ref.refs_0_), channel_id=1, source_target_pairs={{0,4},{4,0},{8,12},{12,8},{1,5},{5,1},{9,13},{13,9},{2,6},{6,2},{1... | collective-permute-start | bytes 196616 | tf_op jit(solution)/shard_map/ppermute | solution.py:251
  30.6 3.7 %copy-start = (bf16[128,640]{1,0:T(8,128)(2,1)S(1)}, bf16[128,640]{1,0:T(8,128)(2,1)}, u32[]{:S(2)}) copy-start(bf16[128,640]{1,0:T(8,128)(2,1)} %weights_ref.3) | copy-start | bytes 491524
  30.6 3.7 %copy-start.1 = (bf16[128,128]{1,0:T(8,128)(2,1)S(1)}, bf16[128,128]{1,0:T(8,128)(2,1)}, u32[]{:S(2)}) copy-start(bf16[128,128]{1,0:T(8,128)(2,1)} %out_weight_ref.1) | copy-start | bytes 98308
  30.6 5.5 %collective-permute-start.10 = (bf16[16,16,128]{2,1,0:T(8,128)(2,1)S(1)}, bf16[16,16,128]{2,1,0:T(8,128)(2,1)S(1)}, u32[]{:S(2)}, u32[]{:S(2)}) collective-permute-start(bf16[16,16,128]{2,1,0:T(8,128)(2,1)S(1)} %shard_map.83), channel_id=1, source_target_pairs={{0,0},{6,1},{8,2},{14,3},{1,4},{7,5},{9,6},{15,7},{2,8},{4,9},{10,... | collective-permute-start | bytes 196616 | tf_op jit(solution)/shard_map/ppermute | solution.py:266
  33.5 5.6 %collective-permute-start.12 = (bf16[16,16,128]{2,1,0:T(8,128)(2,1)S(1)}, bf16[16,16,128]{2,1,0:T(8,128)(2,1)S(1)}, u32[]{:S(2)}, u32[]{:S(2)}) collective-permute-start(bf16[16,16,128]{2,1,0:T(8,128)(2,1)S(1)} %collective-permute-done.11.refs_2_), channel_id=1, source_target_pairs={{0,4},{4,0},{8,12},{12,8},{1,5},{5,1},{9,13},{13,9},{2,6},{6,2},{1... | collective-permute-start | bytes 196616 | tf_op jit(solution)/shard_map/ppermute | solution.py:251

commit v4 on v2

--- a/solution.py
+++ b/solution.py
@@ -114,52 +114,74 @@
     upstream_ref[...] = dot_t(lin_grad, out_weight_ref[...])
 
 
-def weighted_sums(weights, start, terms, out):
+def weighted_sums(weights, start, terms, out, base=None):
     def step(k, _):
         total = weights[start + k, pl.ds(0, 1), :] * terms[0]
         for n in range(1, len(terms)):
             total = total + weights[start + k, pl.ds(n, 1), :] * terms[n]
-        out[k] = total.astype(bf16)
+        if base is not None:
+            total = total + base[k]
+        out[k] = total.astype(out.dtype)
         return 0
 
     lax.fori_loop(0, out.shape[0], step, 0)
 
 
-def triangle_kernel(grid_size, *refs):
-    left_in, right_in = refs[:grid_size], refs[grid_size : 2 * grid_size]
-    upstream_ref = refs[2 * grid_size]
-    tri_normed_ref, left, grad, *left_out = refs[2 * grid_size + 1 : -1]
-    right = refs[-1]
-    size, _, channels = left_in[0].shape
+def panel_kernel(grid_size, *refs):
+    col, size, panel = lax.axis_index("col"), refs[0].shape[0], refs[grid_size]
+    for step in range(grid_size):
+        panel[pl.ds((col ^ step) * size, size)] = refs[step][...].astype(f32)
+
+
+def partial_kernel(steps, panel, right_ref, *outs):
+    size, _, channels = right_ref.shape
+    for step, out in zip(steps, outs):
+        start = (lax.axis_index("row") ^ step) * size
+
+        def add(k, sums):
+            other = right_ref[k].astype(f32)
+            return tuple(sums[i] + panel[start + k, pl.ds(i, 1), :] * other for i in range(size))
+
+        zero = jnp.zeros((size, channels), f32)
+        sums = lax.fori_loop(0, size, add, (zero,) * size)
+        for i in range(size):
+            out[i] = sums[i].astype(out.dtype)
+
+
+def triangle_kernel(*refs):
+    upstream_ref, tri_normed_ref, grad_ref = refs[-3:]
+    size = grad_ref.shape[0]
+    for i in range(size):
+        total = refs[0][i]
+        for ref in refs[1:-3]:
+            total = total + ref[i].astype(f32)
+        here = pl.ds(i * size, size)
+        tri_normed, scale = normalize(total)
+        tri_normed_ref[here, :] = tri_normed
+        grad_ref[i] = normalize_back(tri_normed, scale, upstream_ref[here, :]).astype(bf16)
+
+
+def left_terms_kernel(grid_size, steps, right_ref, *refs):
+    grads, outs = refs[:grid_size], refs[grid_size : -2]
+    panel, right = refs[-2:]
+    size, _, channels = right_ref.shape
+    pairs = size * size
     row, col = lax.axis_index("row"), lax.axis_index("col")
     for step in range(grid_size):
-        left[pl.ds((col ^ step) * size, size)] = left_in[step][...].astype(f32)
-        right[pl.ds((row ^ step) * size, size)] = right_in[step][...].astype(f32)
-
-    def step(k, sums):
-        other = right[k]
-        return tuple(sums[i] + left[k, pl.ds(i, 1), :] * other for i in range(size))
-
-    zero = jnp.zeros((size, channels), f32)
-    sums = lax.fori_loop(0, grid_size * size, step, (zero,) * size)
-    for i in range(size):
-        here = pl.ds(i * size, size)
-        tri_normed, scale = normalize(sums[i])
-        tri_normed_ref[here, :] = tri_normed
-        back = normalize_back(tri_normed, scale, upstream_ref[here, :])
-        grad[here, :] = back.astype(bf16).astype(f32)
-
-    grads = [grad[pl.ds(j, size, stride=size), :] for j in range(size)]
-    for step in range(grid_size):
-        weighted_sums(right, (col ^ step) * size, grads, left_out[step])
-
-
-def right_kernel(grid_size, left, grad, *right_out):
-    size = right_out[0].shape[0]
-    row = lax.axis_index("row")
-    grads = [grad[pl.ds(i * size, size), :] for i in range(size)]
-    for step in range(grid_size):
-        weighted_sums(left, (row ^ step) * size, grads, right_out[step])
+        panel[pl.ds((row ^ step) * pairs, pairs), :] = grads[step][...].astype(f32).reshape(pairs, channels)
+    right[...] = right_ref[...].astype(f32)
+    for step, out in zip(steps, outs):
+        start = (col ^ step) * pairs
+        weighted_sums(right, 0, [panel[pl.ds(start + j, size, stride=size), :] for j in range(size)], out)
+
+
+def right_grad_kernel(steps, panel, *refs):
+    out, base = refs[-1], None
+    size = out.shape[0]
+    for step, grad in zip(steps, refs):
+        start = (lax.axis_index("row") ^ step) * size
+        weighted_sums(panel, start, [grad[i].astype(f32) for i in range(size)], out, base)
+        base = out
 
 
 def update_kernel(
@@ -173,23 +195,16 @@
     normed_grad_ref[...] = dot_t(out_gate_grad, weights_ref[:, 4 * channels :])
 
 
-def sum_kernel(grid_size, *refs):
-    total = refs[0][...].astype(f32)
-    for ref in refs[1:grid_size]:
-        total = total + ref[...].astype(f32)
-    refs[grid_size][...] = total.astype(bf16)
-
-
-def back_kernel(grid_size, left_ref, *refs):
-    right_in = refs[:grid_size]
-    normed_ref, scale_ref, factor_ref, partial_ref, weights_ref, out_ref = refs[grid_size:]
+def back_kernel(grid_size, *refs):
+    left_in = refs[:grid_size]
+    right_ref, normed_ref, scale_ref, factor_ref, partial_ref, weights_ref, out_ref = refs[grid_size:]
     size, _, channels = out_ref.shape
     pairs = size * size
-    left = left_ref[...].astype(f32).reshape(pairs, channels)
-    right = right_in[0][...].astype(f32)
-    for ref in right_in[1:]:
-        right = right + ref[...].astype(f32)
-    right = right.astype(bf16).astype(f32).reshape(pairs, channels)
+    left = left_in[0][...]
+    for ref in left_in[1:]:
+        left = left + ref[...].astype(f32)
+    left = left.reshape(pairs, channels)
+    right = right_ref[...].reshape(pairs, channels)
     grads = jnp.concatenate(
         [(total * factor_ref[block]).astype(bf16) for block, total in enumerate((left, left, right, right))],
         axis=1,
@@ -227,11 +242,14 @@
     tile = jax.ShapeDtypeStruct((size, size, channels), bf16)
     flat = jax.ShapeDtypeStruct((pairs, channels), f32)
 
+    wide = jax.ShapeDtypeStruct((size, size, channels), f32)
+    panel = jax.ShapeDtypeStruct((n * size, size, channels), f32)
+
     def swap(values, axis, step):
         return lax.ppermute(values, axis, [(a, a ^ step) for a in range(n)])
 
-    def mirror(values):
-        return lax.ppermute(values, ("row", "col"), [(a * n + b, b * n + a) for a in range(n) for b in range(n)])
+    def swaps(values, axis):
+        return [swap(each, axis, step) if step else each for step, each in enumerate(values)]
 
     left, right = call(
         tiles_kernel, (tile, tile), pair_acts, pair_mask, crop_length, in_weights,
@@ -243,8 +261,17 @@
             pltpu.SemaphoreType.DMA((3,)),
         ],
     )
-    mirrored = mirror(left)
-    rights = [right] + [swap(right, "row", step) for step in range(n - 1, 0, -1)][::-1]
+    lefts = swaps([left] * n, "col")
+    (left_panel,) = call(functools.partial(panel_kernel, n), (panel,), *lefts)
+    parts = [None] * n
+    for steps in [(step,) for step in range(n - 1, 1, -1)] + [(1, 0)]:
+        outs = call(
+            functools.partial(partial_kernel, steps), tuple(tile if step else wide for step in steps),
+            left_panel, right, flops=2 * len(steps) * size * pairs * channels,
+        )
+        for step, out in zip(steps, outs):
+            parts[step] = out
+    parts = swaps(parts, "row")
     normed, scale, factors, out_open, gate_factor, upstream = call(
         factors_kernel,
         (flat, flat, jax.ShapeDtypeStruct((4, pairs, channels), f32), flat, flat, flat),
@@ -259,30 +286,32 @@
             pltpu.SemaphoreType.DMA((5,)),
         ],
     )
-    lefts = [mirrored] + [swap(mirrored, "col", step) for step in range(1, n)]
-    panel = jax.ShapeDtypeStruct((n * size, size, channels), f32)
-    tri_normed, left_panel, tri_grad, *left_terms = call(
-        functools.partial(triangle_kernel, n),
-        (flat, panel, flat) + (tile,) * n,
-        *lefts, *rights, upstream,
-        scratch=[pltpu.VMEM(panel.shape, f32)],
-        flops=4 * n * size * pairs * channels,
-    )
-    left_terms = [left_terms[0]] + [swap(left_terms[step], "col", step) for step in range(1, n)]
-    right_terms = call(
-        functools.partial(right_kernel, n), (tile,) * n, left_panel, tri_grad,
-        flops=2 * n * size * pairs * channels,
-    )
-    right_terms = [right_terms[0]] + [swap(right_terms[step], "row", step) for step in range(1, n)]
+    tri_normed, tri_grad = call(
+        triangle_kernel, (flat, tile), *parts, upstream, flops=20 * pairs * channels,
+    )
+    grads = swaps([tri_grad] * n, "row")
     update, partial = call(
         update_kernel, (tile, flat), tri_normed, out_open, gate_factor, in_weights, out_weight,
         flops=4 * pairs * channels * channels,
     )
-    (left_sum,) = call(functools.partial(sum_kernel, n), (tile,), *left_terms)
-    left_grad = mirror(left_sum)
+    terms = [None] * n
+    for steps in (tuple(range(n - 1, 1, -1)), (1, 0)):
+        outs = call(
+            functools.partial(left_terms_kernel, n, steps), tuple(tile if step else wide for step in steps),
+            right, *grads,
+            scratch=[pltpu.VMEM((n * pairs, channels), f32), pltpu.VMEM(wide.shape, f32)],
+            flops=2 * len(steps) * size * pairs * channels,
+        )
+        for step, out in zip(steps, outs):
+            terms[step] = out
+    terms = swaps(terms, "col")
+    (right_grad,) = call(
+        functools.partial(right_grad_kernel, tuple(range(n))), (wide,), left_panel, *grads,
+        flops=2 * n * size * pairs * channels,
+    )
     (pair_grad,) = call(
         functools.partial(back_kernel, n), (tile,),
-        left_grad, *right_terms, normed, scale, factors, partial, in_weights,
+        *terms, right_grad, normed, scale, factors, partial, in_weights,
         flops=2 * pairs * channels * 4 * channels,
     )
     return (update, pair_grad)

time: 40.9 us -> 37.5 us (0.917)
  the two profiles are of different devices: /device:TPU:6 before, /device:TPU:0 now
where the time goes in v4:
time: 37.5 us; the launch traced here: 37.3 us
  starting transfers between devices  14.3 us (38%)
  waiting for transfers between devices  12.6 us (34%)
  Pallas kernels  9.1 us (24%)
  between operations  1.36 us (4%)
    ppermute x12, starting transfers between devices, swap(): return lax.ppermute(values, axis, [(a, a ^ step) for a in range(n)])  14.3 us
    ppermute x12, waiting for transfers between devices, swap(): return lax.ppermute(values, axis, [(a, a ^ step) for a in range(n)])  12.6 us
    pallas_call x12, Pallas kernels, call(): pl.pallas_call(kernel, out_shape=tuple(outs), in_specs=specs, out_specs=(...  9.1 us
  transfers between devices with their start and end apart: 12, of which 7 were waited for; matrix products, arithmetic and copies ran while one was open for 0% of the time, Pallas kernels for 12%

profile of v4, /device:TPU:0, one launch (start us, length us, event | category | flops | bytes accessed | tf_op | source)
XLA Modules:
  0.0 37.3 jit_solution(9373686704517502301)
XLA Ops:
  1.3 1.4 %shard_map.77 = (bf16[16,16,128]{2,1,0:T(8,128)(2,1)S(1)}, bf16[16,16,128]{2,1,0:T(8,128)(2,1)S(1)}) custom-call(bf16[16,16,128]{2,1,0:T(8,128)(2,1)} %acts_in.3, s32[16,16]{1,0:T(8,128)} %mask_in.3, s32[1]{0:T(128)S(6)} %copy.8.crop_ref, bf16[128,640]{1,0:T(8,128)(2,1)} %refs_9_.1), custom_call_target="tpu_custom_call" | custom-call | flops 33554432 | bytes 361476 | tf_op jit(solution)/shard_map/pallas_call | solution.py:227
  2.7 2.4 %collective-permute-start.2 = (bf16[16,16,128]{2,1,0:T(8,128)(2,1)S(1)}, bf16[16,16,128]{2,1,0:T(8,128)(2,1)S(1)}, u32[]{:S(2)}, u32[]{:S(2)}) collective-permute-start(bf16[16,16,128]{2,1,0:T(8,128)(2,1)S(1)} %get-tuple-element.20.refs_0_), channel_id=1, source_target_pairs={{0,3},{1,2},{2,1},{3,0},{4,7},{5,6},{6,5},{7,4},{8,11},{9,10},{10,... | collective-permute-start | bytes 196616 | tf_op jit(solution)/shard_map/ppermute | solution.py:249
  5.2 0.6 %collective-permute-start.1 = (bf16[16,16,128]{2,1,0:T(8,128)(2,1)S(1)}, bf16[16,16,128]{2,1,0:T(8,128)(2,1)S(1)}, u32[]{:S(2)}, u32[]{:S(2)}) collective-permute-start(bf16[16,16,128]{2,1,0:T(8,128)(2,1)S(1)} %get-tuple-element.20.refs_0_), channel_id=1, source_target_pairs={{0,2},{1,3},{2,0},{3,1},{4,6},{5,7},{6,4},{7,5},{8,10},{9,11},{10,... | collective-permute-start | bytes 196616 | tf_op jit(solution)/shard_map/ppermute | solution.py:249
  5.8 1.8 %collective-permute-done.2.refs_3_ = bf16[16,16,128]{2,1,0:T(8,128)(2,1)S(1)} collective-permute-done((bf16[16,16,128]{2,1,0:T(8,128)(2,1)S(1)}, bf16[16,16,128]{2,1,0:T(8,128)(2,1)S(1)}, u32[]{:S(2)}, u32[]{:S(2)}) %collective-permute-start.2) | collective-permute-done | bytes 65568 | tf_op jit(solution)/shard_map/ppermute | solution.py:249
  7.7 2.2 %collective-permute-done.1.refs_2_ = bf16[16,16,128]{2,1,0:T(8,128)(2,1)S(1)} collective-permute-done((bf16[16,16,128]{2,1,0:T(8,128)(2,1)S(1)}, bf16[16,16,128]{2,1,0:T(8,128)(2,1)S(1)}, u32[]{:S(2)}, u32[]{:S(2)}) %collective-permute-start.1) | collective-permute-done | bytes 65568 | tf_op jit(solution)/shard_map/ppermute | solution.py:249
  9.9 0.3 shard_map.81
  10.5 0.6 %shard_map.79 = (bf16[16,16,128]{2,1,0:T(8,128)(2,1)S(1)}, f32[16,16,128]{2,1,0:T(8,128)S(1)}) custom-call(f32[64,16,128]{2,1,0:T(8,128)S(1)} %shard_map.78.panel, bf16[16,16,128]{2,1,0:T(8,128)(2,1)S(1)} %get-tuple-element.21.right_ref), custom_call_target="tpu_custom_call" | custom-call | flops 2097152 | bytes 786432 | tf_op jit(solution)/shard_map/pallas_call | solution.py:227
  11.2 2.8 %collective-permute-start.4 = (bf16[16,16,128]{2,1,0:T(8,128)(2,1)S(1)}, bf16[16,16,128]{2,1,0:T(8,128)(2,1)S(1)}, u32[]{:S(2)}, u32[]{:S(2)}) collective-permute-start(bf16[16,16,128]{2,1,0:T(8,128)(2,1)S(1)} %shard_map.80), channel_id=1, source_target_pairs={{0,8},{4,12},{8,0},{12,4},{1,9},{5,13},{9,1},{13,5},{2,10},{6,14},... | collective-permute-start | bytes 196616 | tf_op jit(solution)/shard_map/ppermute | solution.py:249
  14.0 1.3 %collective-permute-start.5 = (bf16[16,16,128]{2,1,0:T(8,128)(2,1)S(1)}, bf16[16,16,128]{2,1,0:T(8,128)(2,1)S(1)}, u32[]{:S(2)}, u32[]{:S(2)}) collective-permute-start(bf16[16,16,128]{2,1,0:T(8,128)(2,1)S(1)} %shard_map.81), channel_id=1, source_target_pairs={{0,12},{4,8},{8,4},{12,0},{1,13},{5,9},{9,5},{13,1},{2,14},{6,10},... | collective-permute-start | bytes 196616 | tf_op jit(solution)/shard_map/ppermute | solution.py:249
  15.6 1.5 %shard_map.82 = (f32[256,128]{1,0:T(8,128)S(1)}, f32[256,128]{1,0:T(8,128)S(1)}, f32[4,256,128]{2,1,0:T(8,128)S(1)}, f32[256,128]{1,0:T(8,128)S(1)}, f32[256,128]{1,0:T(8,128)S(1)}, /*index=5*/f32[256,128]{1,0:T(8,128)S(1)}) custom-call(bf16[16,16,128]{2,1,0:T(8,128)(2,1)} %acts_in.3, s32[16,16]{1,0:T(8,128)} %mask_in.3, s32[1]{0:T(128)S(6)} %copy.8.crop_ref, ...), custom_call_target="tpu_custom_call" | custom-call | flops 50331648 | bytes 1508356 | tf_op jit(solution)/shard_map/pallas_call | solution.py:227
  17.1 0.9 %collective-permute-done.4.refs_2_ = bf16[16,16,128]{2,1,0:T(8,128)(2,1)S(1)} collective-permute-done((bf16[16,16,128]{2,1,0:T(8,128)(2,1)S(1)}, bf16[16,16,128]{2,1,0:T(8,128)(2,1)S(1)}, u32[]{:S(2)}, u32[]{:S(2)}) %collective-permute-start.4) | collective-permute-done | bytes 65568 | tf_op jit(solution)/shard_map/ppermute | solution.py:249
  18.0 2.4 %collective-permute-done.5.refs_3_ = bf16[16,16,128]{2,1,0:T(8,128)(2,1)S(1)} collective-permute-done((bf16[16,16,128]{2,1,0:T(8,128)(2,1)S(1)}, bf16[16,16,128]{2,1,0:T(8,128)(2,1)S(1)}, u32[]{:S(2)}, u32[]{:S(2)}) %collective-permute-start.5) | collective-permute-done | bytes 65568 | tf_op jit(solution)/shard_map/ppermute | solution.py:249
  20.7 3.2 %collective-permute-start.8 = (bf16[16,16,128]{2,1,0:T(8,128)(2,1)S(1)}, bf16[16,16,128]{2,1,0:T(8,128)(2,1)S(1)}, u32[]{:S(2)}, u32[]{:S(2)}) collective-permute-start(bf16[16,16,128]{2,1,0:T(8,128)(2,1)S(1)} %get-tuple-element.29.refs_0_), channel_id=1, source_target_pairs={{0,12},{4,8},{8,4},{12,0},{1,13},{5,9},{9,5},{13,1},{2,14},{6,10},... | collective-permute-start | bytes 196616 | tf_op jit(solution)/shard_map/ppermute | solution.py:249
  23.9 1.2 %collective-permute-start.6 = (bf16[16,16,128]{2,1,0:T(8,128)(2,1)S(1)}, bf16[16,16,128]{2,1,0:T(8,128)(2,1)S(1)}, u32[]{:S(2)}, u32[]{:S(2)}) collective-permute-start(bf16[16,16,128]{2,1,0:T(8,128)(2,1)S(1)} %get-tuple-element.29.refs_0_), channel_id=1, source_target_pairs={{0,4},{4,0},{8,12},{12,8},{1,5},{5,1},{9,13},{13,9},{2,6},{6,2},{1... | collective-permute-start | bytes 196616 | tf_op jit(solution)/shard_map/ppermute | solution.py:249
  25.1 2.2 %collective-permute-done.8.refs_3_ = bf16[16,16,128]{2,1,0:T(8,128)(2,1)S(1)} collective-permute-done((bf16[16,16,128]{2,1,0:T(8,128)(2,1)S(1)}, bf16[16,16,128]{2,1,0:T(8,128)(2,1)S(1)}, u32[]{:S(2)}, u32[]{:S(2)}) %collective-permute-start.8) | collective-permute-done | bytes 65568 | tf_op jit(solution)/shard_map/ppermute | solution.py:249
  27.3 2.4 %collective-permute-done.7.refs_2_ = bf16[16,16,128]{2,1,0:T(8,128)(2,1)S(1)} collective-permute-done((bf16[16,16,128]{2,1,0:T(8,128)(2,1)S(1)}, bf16[16,16,128]{2,1,0:T(8,128)(2,1)S(1)}, u32[]{:S(2)}, u32[]{:S(2)}) %collective-permute-start.7) | collective-permute-done | bytes 65568 | tf_op jit(solution)/shard_map/ppermute | solution.py:249
  29.8 0.7 %shard_map.86 = (bf16[16,16,128]{2,1,0:T(8,128)(2,1)S(1)}, bf16[16,16,128]{2,1,0:T(8,128)(2,1)S(1)}) custom-call(bf16[16,16,128]{2,1,0:T(8,128)(2,1)S(1)} %get-tuple-element.21.right_ref, bf16[16,16,128]{2,1,0:T(8,128)(2,1)S(1)} %get-tuple-element.29.refs_0_, bf16[16,16,128]{2,1,0:T(8,128)(2,1)S(1)} %collective-permute-done.6.refs_1_, ...), custom_call_target="tpu_custom_call" | custom-call | flops 2097152 | bytes 458752 | tf_op jit(solution)/shard_map/pallas_call | solution.py:227
  30.5 1.9 %collective-permute-start.10 = (bf16[16,16,128]{2,1,0:T(8,128)(2,1)S(1)}, bf16[16,16,128]{2,1,0:T(8,128)(2,1)S(1)}, u32[]{:S(2)}, u32[]{:S(2)}) collective-permute-start(bf16[16,16,128]{2,1,0:T(8,128)(2,1)S(1)} %get-tuple-element.32), channel_id=1, source_target_pairs={{0,2},{1,3},{2,0},{3,1},{4,6},{5,7},{6,4},{7,5},{8,10},{9,11},{10,... | collective-permute-start | bytes 196616 | tf_op jit(solution)/shard_map/ppermute | solution.py:249
  32.4 0.7 %shard_map.85 = (bf16[16,16,128]{2,1,0:T(8,128)(2,1)S(1)}, f32[16,16,128]{2,1,0:T(8,128)S(1)}) custom-call(bf16[16,16,128]{2,1,0:T(8,128)(2,1)S(1)} %get-tuple-element.21.right_ref, bf16[16,16,128]{2,1,0:T(8,128)(2,1)S(1)} %get-tuple-element.29.refs_0_, bf16[16,16,128]{2,1,0:T(8,128)(2,1)S(1)} %collective-permute-done.6.refs_1_, ...), custom_call_target="tpu_custom_call" | custom-call | flops 2097152 | bytes 524288 | tf_op jit(solution)/shard_map/pallas_call | solution.py:227
  33.1 0.4 %collective-permute-start.9 = (bf16[16,16,128]{2,1,0:T(8,128)(2,1)S(1)}, bf16[16,16,128]{2,1,0:T(8,128)(2,1)S(1)}, u32[]{:S(2)}, u32[]{:S(2)}) collective-permute-start(bf16[16,16,128]{2,1,0:T(8,128)(2,1)S(1)} %get-tuple-element.31), channel_id=1, source_target_pairs={{0,1},{1,0},{2,3},{3,2},{4,5},{5,4},{6,7},{7,6},{8,9},{9,8},{10,11... | collective-permute-start | bytes 196616 | tf_op jit(solution)/shard_map/ppermute | solution.py:249
  33.5 0.8 %shard_map.84 = (bf16[16,16,128]{2,1,0:T(8,128)(2,1)}, f32[256,128]{1,0:T(8,128)S(1)}) custom-call(f32[256,128]{1,0:T(8,128)S(1)} %get-tuple-element.25.tri_normed_ref, f32[256,128]{1,0:T(8,128)S(1)} %get-tuple-element.26.open_ref, f32[256,128]{1,0:T(8,128)S(1)} %get-tuple-element.27.gate_factor_ref, bf16[128,640]{1,0:T(8,128)(2,1)S(1)} %copy-done, ...), custom_call_target="tpu_custom_call" | custom-call | flops 16777216 | bytes 786432 | tf_op jit(solution)/shard_map/pallas_call | solution.py:227
  34.3 1.4 %shard_map.87.refs_4_ = f32[16,16,128]{2,1,0:T(8,128)S(1)} custom-call(f32[64,16,128]{2,1,0:T(8,128)S(1)} %shard_map.78.panel, bf16[16,16,128]{2,1,0:T(8,128)(2,1)S(1)} %get-tuple-element.29.refs_0_, bf16[16,16,128]{2,1,0:T(8,128)(2,1)S(1)} %collective-permute-done.6.refs_1_, bf16[16,16,128]{2,1,0:T(8,128)(2,1)S(1)} %collective-permute-done.7.refs_2_, ...), custom_call_target="tpu_custom_call" | custom-call | flops 4194304 | bytes 917504 | tf_op jit(solution)/shard_map/pallas_call | solution.py:227
  35.7 0.6 %collective-permute-done.11.refs_3_ = bf16[16,16,128]{2,1,0:T(8,128)(2,1)S(1)} collective-permute-done((bf16[16,16,128]{2,1,0:T(8,128)(2,1)S(1)}, bf16[16,16,128]{2,1,0:T(8,128)(2,1)S(1)}, u32[]{:S(2)}, u32[]{:S(2)}) %collective-permute-start.11) | collective-permute-done | bytes 65568 | tf_op jit(solution)/shard_map/ppermute | solution.py:249
  36.3 0.9 %shard_map.88 = bf16[16,16,128]{2,1,0:T(8,128)(2,1)} custom-call(f32[16,16,128]{2,1,0:T(8,128)S(1)} %get-tuple-element.30.refs_0_, bf16[16,16,128]{2,1,0:T(8,128)(2,1)S(1)} %collective-permute-done.9.refs_1_, bf16[16,16,128]{2,1,0:T(8,128)(2,1)S(1)} %collective-permute-done.10.refs_2_, bf16[16,16,128]{2,1,0:T(8,128)(2,1)S(1)} %collective-permute-done.11.refs_3_, ...), custom_call_target="tpu_custom_call" | custom-call | flops 33554432 | bytes 1605632 | tf_op jit(solution)/shard_map/pallas_call | solution.py:227
  (16 shorter events, 1.0 us)
Async XLA Ops:
  2.7 4.9 %collective-permute-start.2 = (bf16[16,16,128]{2,1,0:T(8,128)(2,1)S(1)}, bf16[16,16,128]{2,1,0:T(8,128)(2,1)S(1)}, u32[]{:S(2)}, u32[]{:S(2)}) collective-permute-start(bf16[16,16,128]{2,1,0:T(8,128)(2,1)S(1)} %get-tuple-element.20.refs_0_), channel_id=1, source_target_pairs={{0,3},{1,2},{2,1},{3,0},{4,7},{5,6},{6,5},{7,4},{8,11},{9,10},{10,... | collective-permute-start | bytes 196616 | tf_op jit(solution)/shard_map/ppermute | solution.py:249
  5.2 4.7 %collective-permute-start.1 = (bf16[16,16,128]{2,1,0:T(8,128)(2,1)S(1)}, bf16[16,16,128]{2,1,0:T(8,128)(2,1)S(1)}, u32[]{:S(2)}, u32[]{:S(2)}) collective-permute-start(bf16[16,16,128]{2,1,0:T(8,128)(2,1)S(1)} %get-tuple-element.20.refs_0_), channel_id=1, source_target_pairs={{0,2},{1,3},{2,0},{3,1},{4,6},{5,7},{6,4},{7,5},{8,10},{9,11},{10,... | collective-permute-start | bytes 196616 | tf_op jit(solution)/shard_map/ppermute | solution.py:249
  5.8 4.0 %collective-permute-start = (bf16[16,16,128]{2,1,0:T(8,128)(2,1)S(1)}, bf16[16,16,128]{2,1,0:T(8,128)(2,1)S(1)}, u32[]{:S(2)}, u32[]{:S(2)}) collective-permute-start(bf16[16,16,128]{2,1,0:T(8,128)(2,1)S(1)} %get-tuple-element.20.refs_0_), channel_id=1, source_target_pairs={{0,1},{1,0},{2,3},{3,2},{4,5},{5,4},{6,7},{7,6},{8,9},{9,8},{10,11... | collective-permute-start | bytes 196616 | tf_op jit(solution)/shard_map/ppermute | solution.py:249
  11.2 6.8 %collective-permute-start.4 = (bf16[16,16,128]{2,1,0:T(8,128)(2,1)S(1)}, bf16[16,16,128]{2,1,0:T(8,128)(2,1)S(1)}, u32[]{:S(2)}, u32[]{:S(2)}) collective-permute-start(bf16[16,16,128]{2,1,0:T(8,128)(2,1)S(1)} %shard_map.80), channel_id=1, source_target_pairs={{0,8},{4,12},{8,0},{12,4},{1,9},{5,13},{9,1},{13,5},{2,10},{6,14},... | collective-permute-start | bytes 196616 | tf_op jit(solution)/shard_map/ppermute | solution.py:249
  14.0 6.3 %collective-permute-start.5 = (bf16[16,16,128]{2,1,0:T(8,128)(2,1)S(1)}, bf16[16,16,128]{2,1,0:T(8,128)(2,1)S(1)}, u32[]{:S(2)}, u32[]{:S(2)}) collective-permute-start(bf16[16,16,128]{2,1,0:T(8,128)(2,1)S(1)} %shard_map.81), channel_id=1, source_target_pairs={{0,12},{4,8},{8,4},{12,0},{1,13},{5,9},{9,5},{13,1},{2,14},{6,10},... | collective-permute-start | bytes 196616 | tf_op jit(solution)/shard_map/ppermute | solution.py:249
  15.4 5.0 %collective-permute-start.3 = (bf16[16,16,128]{2,1,0:T(8,128)(2,1)S(1)}, bf16[16,16,128]{2,1,0:T(8,128)(2,1)S(1)}, u32[]{:S(2)}, u32[]{:S(2)}) collective-permute-start(bf16[16,16,128]{2,1,0:T(8,128)(2,1)S(1)} %get-tuple-element.23), channel_id=1, source_target_pairs={{0,4},{4,0},{8,12},{12,8},{1,5},{5,1},{9,13},{13,9},{2,6},{6,2},{1... | collective-permute-start | bytes 196616 | tf_op jit(solution)/shard_map/ppermute | solution.py:249
  20.7 6.6 %collective-permute-start.8 = (bf16[16,16,128]{2,1,0:T(8,128)(2,1)S(1)}, bf16[16,16,128]{2,1,0:T(8,128)(2,1)S(1)}, u32[]{:S(2)}, u32[]{:S(2)}) collective-permute-start(bf16[16,16,128]{2,1,0:T(8,128)(2,1)S(1)} %get-tuple-element.29.refs_0_), channel_id=1, source_target_pairs={{0,12},{4,8},{8,4},{12,0},{1,13},{5,9},{9,5},{13,1},{2,14},{6,10},... | collective-permute-start | bytes 196616 | tf_op jit(solution)/shard_map/ppermute | solution.py:249
  23.9 5.9 %collective-permute-start.7 = (bf16[16,16,128]{2,1,0:T(8,128)(2,1)S(1)}, bf16[16,16,128]{2,1,0:T(8,128)(2,1)S(1)}, u32[]{:S(2)}, u32[]{:S(2)}) collective-permute-start(bf16[16,16,128]{2,1,0:T(8,128)(2,1)S(1)} %get-tuple-element.29.refs_0_), channel_id=1, source_target_pairs={{0,8},{4,12},{8,0},{12,4},{1,9},{5,13},{9,1},{13,5},{2,10},{6,14},... | collective-permute-start | bytes 196616 | tf_op jit(solution)/shard_map/ppermute | solution.py:249
  23.9 5.9 %collective-permute-start.6 = (bf16[16,16,128]{2,1,0:T(8,128)(2,1)S(1)}, bf16[16,16,128]{2,1,0:T(8,128)(2,1)S(1)}, u32[]{:S(2)}, u32[]{:S(2)}) collective-permute-start(bf16[16,16,128]{2,1,0:T(8,128)(2,1)S(1)} %get-tuple-element.29.refs_0_), channel_id=1, source_target_pairs={{0,4},{4,0},{8,12},{12,8},{1,5},{5,1},{9,13},{13,9},{2,6},{6,2},{1... | collective-permute-start | bytes 196616 | tf_op jit(solution)/shard_map/ppermute | solution.py:249
  30.5 5.2 %collective-permute-start.10 = (bf16[16,16,128]{2,1,0:T(8,128)(2,1)S(1)}, bf16[16,16,128]{2,1,0:T(8,128)(2,1)S(1)}, u32[]{:S(2)}, u32[]{:S(2)}) collective-permute-start(bf16[16,16,128]{2,1,0:T(8,128)(2,1)S(1)} %get-tuple-element.32), channel_id=1, source_target_pairs={{0,2},{1,3},{2,0},{3,1},{4,6},{5,7},{6,4},{7,5},{8,10},{9,11},{10,... | collective-permute-start | bytes 196616 | tf_op jit(solution)/shard_map/ppermute | solution.py:249
  32.4 1.2 %copy-start = (bf16[128,640]{1,0:T(8,128)(2,1)S(1)}, bf16[128,640]{1,0:T(8,128)(2,1)}, u32[]{:S(2)}) copy-start(bf16[128,640]{1,0:T(8,128)(2,1)} %refs_9_.1) | copy-start | bytes 491524
  32.4 1.2 %copy-start.1 = (bf16[128,128]{1,0:T(8,128)(2,1)S(1)}, bf16[128,128]{1,0:T(8,128)(2,1)}, u32[]{:S(2)}) copy-start(bf16[128,128]{1,0:T(8,128)(2,1)} %out_weight_ref.1) | copy-start | bytes 98308
  32.4 4.0 %collective-permute-start.11 = (bf16[16,16,128]{2,1,0:T(8,128)(2,1)S(1)}, bf16[16,16,128]{2,1,0:T(8,128)(2,1)S(1)}, u32[]{:S(2)}, u32[]{:S(2)}) collective-permute-start(bf16[16,16,128]{2,1,0:T(8,128)(2,1)S(1)} %get-tuple-element.33), channel_id=1, source_target_pairs={{0,3},{1,2},{2,1},{3,0},{4,7},{5,6},{6,5},{7,4},{8,11},{9,10},{10,... | collective-permute-start | bytes 196616 | tf_op jit(solution)/shard_map/ppermute | solution.py:249
  33.1 3.2 %collective-permute-start.9 = (bf16[16,16,128]{2,1,0:T(8,128)(2,1)S(1)}, bf16[16,16,128]{2,1,0:T(8,128)(2,1)S(1)}, u32[]{:S(2)}, u32[]{:S(2)}) collective-permute-start(bf16[16,16,128]{2,1,0:T(8,128)(2,1)S(1)} %get-tuple-element.31), channel_id=1, source_target_pairs={{0,1},{1,0},{2,3},{3,2},{4,5},{5,4},{6,7},{7,6},{8,9},{9,8},{10,11... | collective-permute-start | bytes 196616 | tf_op jit(solution)/shard_map/ppermute | solution.py:249

commit v5 on v4

--- a/solution.py
+++ b/solution.py
@@ -41,7 +41,7 @@
     return lax.dot_general(a, b, (((1,), (1,)), ((), ())), preferred_element_type=f32)
 
 
-def keep_rows(mask_ref, crop_ref):
+def keep_rows(mask_ref, crop_ref, channels):
     size = mask_ref.shape[0]
     rows = lax.axis_index("row") * size + lax.broadcasted_iota(jnp.int32, (size, size), 0)
     cols = lax.axis_index("col") * size + lax.broadcasted_iota(jnp.int32, (size, size), 1)
@@ -52,7 +52,7 @@
     pick_row = jnp.where(pair // size == lane, 1.0, 0.0).astype(bf16)
     pick_col = jnp.where(pair % size == lane, 1.0, 0.0)
     spread = (dot(pick_row, keep) * pick_col).astype(bf16)
-    return dot(spread, jnp.ones((size, 128), bf16))
+    return dot(spread, jnp.ones((size, channels), bf16))
 
 
 def start_copies(sems, *pairs):
@@ -62,28 +62,30 @@
     return copies
 
 
-def tiles_kernel(
-    acts_in, mask_in, crop_ref, weights_in, left_ref, right_ref, acts_ref, mask_ref, weights_ref, sems
-):
-    copies = start_copies(sems, (acts_in, acts_ref), (weights_in, weights_ref), (mask_in, mask_ref))
+def gated(projected, block, keep):
+    channels = keep.shape[1]
+    value = projected[:, block * channels : (block + 1) * channels]
+    opened = sigmoid(projected[:, (block + 1) * channels : (block + 2) * channels])
+    return (opened * value * keep).astype(bf16), opened, value
+
+
+def left_kernel(acts_in, mask_in, crop_ref, weights_in, left_ref, acts_ref, mask_ref, weights_ref, sems):
     size, _, channels = acts_ref.shape
+    copies = start_copies(
+        sems, (acts_in, acts_ref), (weights_in.at[:, pl.ds(0, 2 * channels)], weights_ref), (mask_in, mask_ref),
+    )
     copies[0].wait()
     normed, _ = normalize(acts_ref[...].astype(f32).reshape(size * size, channels))
     normed = normed.astype(bf16)
-    copies[1].wait()
-    copies[2].wait()
-    projected = dot(normed, weights_ref[:, : 4 * channels])
-    keep = keep_rows(mask_ref, crop_ref)
-    for block, out_ref in ((0, left_ref), (2, right_ref)):
-        value = projected[:, block * channels : (block + 1) * channels]
-        gate = projected[:, (block + 1) * channels : (block + 2) * channels]
-        tile = (sigmoid(gate) * value * keep).astype(bf16)
-        out_ref[...] = tile.reshape(size, size, channels)
+    for copy in copies[1:]:
+        copy.wait()
+    left, _, _ = gated(dot(normed, weights_ref[...]), 0, keep_rows(mask_ref, crop_ref, channels))
+    left_ref[...] = left.reshape(size, size, channels)
 
 
 def factors_kernel(
     acts_in, mask_in, crop_ref, cotangent_in, weights_in, out_weight_in,
-    normed_ref, scale_ref, factor_ref, open_ref, gate_factor_ref, upstream_ref,
+    right_ref, normed_ref, scale_ref, factor_ref, open_ref, gate_factor_ref, upstream_ref,
     acts_ref, mask_ref, cotangent_ref, weights_ref, out_weight_ref, sems,
 ):
     copies = start_copies(
@@ -99,13 +101,12 @@
     for copy in copies[1:]:
         copy.wait()
     projected = dot(normed.astype(bf16), weights_ref[...])
-    keep = keep_rows(mask_ref, crop_ref)
+    keep = keep_rows(mask_ref, crop_ref, channels)
     for block in (0, 2):
-        value = projected[:, block * channels : (block + 1) * channels]
-        gate = projected[:, (block + 1) * channels : (block + 2) * channels]
-        opened = sigmoid(gate)
+        tile, opened, value = gated(projected, block, keep)
         factor_ref[block] = keep * opened
         factor_ref[block + 1] = keep * value * opened * (1.0 - opened)
+    right_ref[...] = tile.reshape(size, size, channels)
     out_open = sigmoid(projected[:, 4 * channels :])
     cotangent = cotangent_ref[...].astype(f32).reshape(pairs, channels)
     lin_grad = (cotangent * out_open).astype(bf16)
@@ -127,10 +128,10 @@
     lax.fori_loop(0, out.shape[0], step, 0)
 
 
-def panel_kernel(grid_size, *refs):
-    col, size, panel = lax.axis_index("col"), refs[0].shape[0], refs[grid_size]
-    for step in range(grid_size):
-        panel[pl.ds((col ^ step) * size, size)] = refs[step][...].astype(f32)
+def panel_kernel(axis, steps, *refs):
+    here, rows, panel = lax.axis_index(axis), refs[0].shape[0], refs[-1]
+    for step, ref in zip(steps, refs):
+        panel[pl.ds((here ^ step) * rows, rows)] = ref[...].astype(f32)
 
 
 def partial_kernel(steps, panel, right_ref, *outs):
@@ -148,31 +149,21 @@
             out[i] = sums[i].astype(out.dtype)
 
 
-def triangle_kernel(*refs):
-    upstream_ref, tri_normed_ref, grad_ref = refs[-3:]
+def triangle_kernel(base, tile_ref, upstream_ref, tri_normed_ref, grad_ref):
     size = grad_ref.shape[0]
     for i in range(size):
-        total = refs[0][i]
-        for ref in refs[1:-3]:
-            total = total + ref[i].astype(f32)
         here = pl.ds(i * size, size)
-        tri_normed, scale = normalize(total)
+        tri_normed, scale = normalize(base[i] + tile_ref[i].astype(f32))
         tri_normed_ref[here, :] = tri_normed
         grad_ref[i] = normalize_back(tri_normed, scale, upstream_ref[here, :]).astype(bf16)
 
 
-def left_terms_kernel(grid_size, steps, right_ref, *refs):
-    grads, outs = refs[:grid_size], refs[grid_size : -2]
-    panel, right = refs[-2:]
+def left_terms_kernel(step, panel, right_ref, out, grad, right):
     size, _, channels = right_ref.shape
-    pairs = size * size
-    row, col = lax.axis_index("row"), lax.axis_index("col")
-    for step in range(grid_size):
-        panel[pl.ds((row ^ step) * pairs, pairs), :] = grads[step][...].astype(f32).reshape(pairs, channels)
     right[...] = right_ref[...].astype(f32)
-    for step, out in zip(steps, outs):
-        start = (col ^ step) * pairs
-        weighted_sums(right, 0, [panel[pl.ds(start + j, size, stride=size), :] for j in range(size)], out)
+    here = panel[pl.ds((lax.axis_index("col") ^ step) * size, size)]
+    grad[...] = here.reshape(size * size, channels)
+    weighted_sums(right, 0, [grad[pl.ds(j, size, stride=size), :] for j in range(size)], out)
 
 
 def right_grad_kernel(steps, panel, *refs):
@@ -182,6 +173,10 @@
         start = (lax.axis_index("row") ^ step) * size
         weighted_sums(panel, start, [grad[i].astype(f32) for i in range(size)], out, base)
         base = out
+
+
+def add_kernel(base, tile_ref, out):
+    out[...] = base[...] + tile_ref[...].astype(f32)
 
 
 def update_kernel(
@@ -195,15 +190,12 @@
     normed_grad_ref[...] = dot_t(out_gate_grad, weights_ref[:, 4 * channels :])
 
 
-def back_kernel(grid_size, *refs):
-    left_in = refs[:grid_size]
-    right_ref, normed_ref, scale_ref, factor_ref, partial_ref, weights_ref, out_ref = refs[grid_size:]
+def back_kernel(
+    base, tile_ref, right_ref, normed_ref, scale_ref, factor_ref, partial_ref, weights_ref, out_ref
+):
     size, _, channels = out_ref.shape
     pairs = size * size
-    left = left_in[0][...]
-    for ref in left_in[1:]:
-        left = left + ref[...].astype(f32)
-    left = left.reshape(pairs, channels)
+    left = (base[...] + tile_ref[...].astype(f32)).reshape(pairs, channels)
     right = right_ref[...].reshape(pairs, channels)
     grads = jnp.concatenate(
         [(total * factor_ref[block]).astype(bf16) for block, total in enumerate((left, left, right, right))],
@@ -231,7 +223,7 @@
         out_specs=(spec,) * len(outs),
         scratch_shapes=scratch,
         compiler_params=pltpu.CompilerParams(vmem_limit_bytes=24 * 2**20),
-        cost_estimate=pl.CostEstimate(flops=flops, bytes_accessed=total, transcendentals=0),
+        cost_estimate=pl.CostEstimate(flops=flops, bytes_accessed=total if flops else 0, transcendentals=0),
     )(*args)
 
 
@@ -244,37 +236,31 @@
 
     wide = jax.ShapeDtypeStruct((size, size, channels), f32)
     panel = jax.ShapeDtypeStruct((n * size, size, channels), f32)
+    work = 2 * size * pairs * channels
+    wait = 2**31
+    steps = [step for bit in range(n.bit_length() - 2, -1, -1) for step in range(2**bit, 2 ** (bit + 1))]
+
 
     def swap(values, axis, step):
         return lax.ppermute(values, axis, [(a, a ^ step) for a in range(n)])
 
-    def swaps(values, axis):
-        return [swap(each, axis, step) if step else each for step, each in enumerate(values)]
-
-    left, right = call(
-        tiles_kernel, (tile, tile), pair_acts, pair_mask, crop_length, in_weights,
-        smem=(2,), hbm=(0, 1, 3), flops=2 * pairs * channels * 4 * channels,
+    def gather(values, axis):
+        return [values] + [swap(values, axis, step) for step in steps]
+
+    (left,) = call(
+        left_kernel, (tile,), pair_acts, pair_mask, crop_length, in_weights,
+        smem=(2,), hbm=(0, 1, 3), flops=2 * pairs * channels * 2 * channels,
         scratch=[
             pltpu.VMEM(pair_acts.shape, bf16),
             pltpu.VMEM(pair_mask.shape, jnp.int32),
-            pltpu.VMEM(in_weights.shape, bf16),
+            pltpu.VMEM((channels, 2 * channels), bf16),
             pltpu.SemaphoreType.DMA((3,)),
         ],
     )
-    lefts = swaps([left] * n, "col")
-    (left_panel,) = call(functools.partial(panel_kernel, n), (panel,), *lefts)
-    parts = [None] * n
-    for steps in [(step,) for step in range(n - 1, 1, -1)] + [(1, 0)]:
-        outs = call(
-            functools.partial(partial_kernel, steps), tuple(tile if step else wide for step in steps),
-            left_panel, right, flops=2 * len(steps) * size * pairs * channels,
-        )
-        for step, out in zip(steps, outs):
-            parts[step] = out
-    parts = swaps(parts, "row")
-    normed, scale, factors, out_open, gate_factor, upstream = call(
+    lefts = gather(left, "col")
+    right, normed, scale, factors, out_open, gate_factor, upstream = call(
         factors_kernel,
-        (flat, flat, jax.ShapeDtypeStruct((4, pairs, channels), f32), flat, flat, flat),
+        (tile, flat, flat, jax.ShapeDtypeStruct((4, pairs, channels), f32), flat, flat, flat),
         pair_acts, pair_mask, crop_length, cotangent, in_weights, out_weight,
         smem=(2,), hbm=(0, 1, 3, 4, 5), flops=2 * pairs * channels * 6 * channels,
         scratch=[
@@ -286,32 +272,45 @@
             pltpu.SemaphoreType.DMA((5,)),
         ],
     )
+    (left_panel,) = call(functools.partial(panel_kernel, "col", [0] + steps), (panel,), *lefts)
+    parts = {}
+    for step in [0] + steps:
+        (parts[step],) = call(
+            functools.partial(partial_kernel, (step,)), (tile if step else wide,), left_panel, right, flops=work,
+        )
+    total = parts[0]
+    for step in steps:
+        part = swap(parts[step], "row", step)
+        if step != steps[-1]:
+            (total,) = call(add_kernel, (wide,), total, part, flops=wait)
     tri_normed, tri_grad = call(
-        triangle_kernel, (flat, tile), *parts, upstream, flops=20 * pairs * channels,
-    )
-    grads = swaps([tri_grad] * n, "row")
+        triangle_kernel, (flat, tile), total, part, upstream, flops=20 * pairs * channels,
+    )
+    grads = gather(tri_grad, "row")
     update, partial = call(
         update_kernel, (tile, flat), tri_normed, out_open, gate_factor, in_weights, out_weight,
         flops=4 * pairs * channels * channels,
     )
-    terms = [None] * n
-    for steps in (tuple(range(n - 1, 1, -1)), (1, 0)):
-        outs = call(
-            functools.partial(left_terms_kernel, n, steps), tuple(tile if step else wide for step in steps),
-            right, *grads,
-            scratch=[pltpu.VMEM((n * pairs, channels), f32), pltpu.VMEM(wide.shape, f32)],
-            flops=2 * len(steps) * size * pairs * channels,
+    right, partial = lax.optimization_barrier((right, partial))
+    (grad_panel,) = call(functools.partial(panel_kernel, "row", [0] + steps), (panel,), *grads)
+    terms = {}
+    for step in [0] + steps:
+        (terms[step],) = call(
+            functools.partial(left_terms_kernel, step), (tile if step else wide,), grad_panel, right,
+            scratch=[pltpu.VMEM((pairs, channels), f32), pltpu.VMEM(wide.shape, f32)], flops=work,
         )
-        for step, out in zip(steps, outs):
-            terms[step] = out
-    terms = swaps(terms, "col")
+    total = terms[0]
+    for step in steps:
+        term = swap(terms[step], "col", step)
+        if step != steps[-1]:
+            (total,) = call(add_kernel, (wide,), total, term, flops=wait)
     (right_grad,) = call(
-        functools.partial(right_grad_kernel, tuple(range(n))), (wide,), left_panel, *grads,
+        functools.partial(right_grad_kernel, [0] + steps), (wide,), left_panel, *grads,
         flops=2 * n * size * pairs * channels,
     )
     (pair_grad,) = call(
-        functools.partial(back_kernel, n), (tile,),
-        *terms, right_grad, normed, scale, factors, partial, in_weights,
+        back_kernel, (tile,),
+        total, term, right_grad, normed, scale, factors, partial, in_weights,
         flops=2 * pairs * channels * 4 * channels,
     )
     return (update, pair_grad)

time: 37.5 us -> 36.6 us (0.976)
  starting transfers between devices: 14.3 us -> 13.5 us
    ppermute x12, starting transfers between devices: 14.3 us -> 13.5 us  [swap(): return lax.ppermute(values, axis, [(a, a ^ step) for a in range(n)])]
    pallas_call x12 -> x20, Pallas kernels: 9.1 us -> 9.08 us  [call(): pl.pallas_call(kernel, out_shape=tuple(outs), in_specs=specs, out_specs=(...]
  transfers between devices with their start and end apart: 12 -> 12, of which waited for: 7 -> 9; matrix products, arithmetic and copies ran while one was open for 0% -> 0% of each run, Pallas kernels for 12% -> 16%
where the time goes in v5:
time: 36.6 us; the launch traced here: 36.4 us
  starting transfers between devices  13.5 us (37%)
  waiting for transfers between devices  12.4 us (34%)
  Pallas kernels  9.08 us (25%)
  between operations  1.41 us (4%)
    ppermute x12, starting transfers between devices, swap(): return lax.ppermute(values, axis, [(a, a ^ step) for a in range(n)])  13.5 us
    ppermute x12, waiting for transfers between devices, swap(): return lax.ppermute(values, axis, [(a, a ^ step) for a in range(n)])  12.4 us
    pallas_call x20, Pallas kernels, call(): pl.pallas_call(kernel, out_shape=tuple(outs), in_specs=specs, out_specs=(...  9.08 us
  transfers between devices with their start and end apart: 12, of which 9 were waited for; matrix products, arithmetic and copies ran while one was open for 0% of the time, Pallas kernels for 16%

profile of v5, /device:TPU:0, one launch (start us, length us, event | category | flops | bytes accessed | tf_op | source)
XLA Modules:
  0.0 36.4 jit_solution(13163487154265414239)
XLA Ops:
  1.3 1.4 %shard_map.77.refs_0_ = bf16[16,16,128]{2,1,0:T(8,128)(2,1)S(1)} custom-call(bf16[16,16,128]{2,1,0:T(8,128)(2,1)} %acts_in.3, s32[16,16]{1,0:T(8,128)} %mask_in.3, s32[1]{0:T(128)S(6)} %copy.8.crop_ref, bf16[128,640]{1,0:T(8,128)(2,1)} %weights_ref.3), custom_call_target="tpu_custom_call" | custom-call | flops 16777216 | bytes 295940 | tf_op jit(solution)/shard_map/pallas_call | solution.py:219
  2.6 3.0 %collective-permute-start = (bf16[16,16,128]{2,1,0:T(8,128)(2,1)S(1)}, bf16[16,16,128]{2,1,0:T(8,128)(2,1)S(1)}, u32[]{:S(2)}, u32[]{:S(2)}) collective-permute-start(bf16[16,16,128]{2,1,0:T(8,128)(2,1)S(1)} %shard_map.77.refs_0_), channel_id=1, source_target_pairs={{0,2},{1,3},{2,0},{3,1},{4,6},{5,7},{6,4},{7,5},{8,10},{9,11},{10,... | collective-permute-start | bytes 196616 | tf_op jit(solution)/shard_map/ppermute | solution.py:245
  5.8 1.5 %shard_map.79 = (bf16[16,16,128]{2,1,0:T(8,128)(2,1)S(1)}, f32[256,128]{1,0:T(8,128)S(1)}, f32[256,128]{1,0:T(8,128)S(1)}, f32[4,256,128]{2,1,0:T(8,128)S(1)}, f...) custom-call(bf16[16,16,128]{2,1,0:T(8,128)(2,1)} %acts_in.3, s32[16,16]{1,0:T(8,128)} %mask_in.3, ...), custom_call_target="tpu_custom_call" | custom-call | flops 50331648 | bytes 1573892 | tf_op jit(solution)/shard_map/pallas_call | solution.py:219
  7.3 0.6 %collective-permute-done.refs_1_ = bf16[16,16,128]{2,1,0:T(8,128)(2,1)S(1)} collective-permute-done((bf16[16,16,128]{2,1,0:T(8,128)(2,1)S(1)}, bf16[16,16,128]{2,1,0:T(8,128)(2,1)S(1)}, u32[]{:S(2)}, u32[]{:S(2)}) %collective-permute-start) | collective-permute-done | bytes 65568 | tf_op jit(solution)/shard_map/ppermute | solution.py:245
  7.9 1.9 %collective-permute-done.1.refs_2_ = bf16[16,16,128]{2,1,0:T(8,128)(2,1)S(1)} collective-permute-done((bf16[16,16,128]{2,1,0:T(8,128)(2,1)S(1)}, bf16[16,16,128]{2,1,0:T(8,128)(2,1)S(1)}, u32[]{:S(2)}, u32[]{:S(2)}) %collective-permute-start.1) | collective-permute-done | bytes 65568 | tf_op jit(solution)/shard_map/ppermute | solution.py:245
  10.2 2.7 %collective-permute-start.3 = (bf16[16,16,128]{2,1,0:T(8,128)(2,1)S(1)}, bf16[16,16,128]{2,1,0:T(8,128)(2,1)S(1)}, u32[]{:S(2)}, u32[]{:S(2)}) collective-permute-start(bf16[16,16,128]{2,1,0:T(8,128)(2,1)S(1)} %shard_map.81), channel_id=1, source_target_pairs={{0,8},{4,12},{8,0},{12,4},{1,9},{5,13},{9,1},{13,5},{2,10},{6,14},... | collective-permute-start | bytes 196616 | tf_op jit(solution)/shard_map/ppermute | solution.py:245
  13.2 1.4 %collective-permute-start.4 = (bf16[16,16,128]{2,1,0:T(8,128)(2,1)S(1)}, bf16[16,16,128]{2,1,0:T(8,128)(2,1)S(1)}, u32[]{:S(2)}, u32[]{:S(2)}) collective-permute-start(bf16[16,16,128]{2,1,0:T(8,128)(2,1)S(1)} %shard_map.83), channel_id=1, source_target_pairs={{0,12},{4,8},{8,4},{12,0},{1,13},{5,9},{9,5},{13,1},{2,14},{6,10},... | collective-permute-start | bytes 196616 | tf_op jit(solution)/shard_map/ppermute | solution.py:245
  15.5 1.5 %collective-permute-done.3.tile_ref = bf16[16,16,128]{2,1,0:T(8,128)(2,1)S(1)} collective-permute-done((bf16[16,16,128]{2,1,0:T(8,128)(2,1)S(1)}, bf16[16,16,128]{2,1,0:T(8,128)(2,1)S(1)}, u32[]{:S(2)}, u32[]{:S(2)}) %collective-permute-start.3) | collective-permute-done | bytes 65568 | tf_op jit(solution)/shard_map/ppermute | solution.py:245
  17.0 2.5 %collective-permute-done.4.tile_ref = bf16[16,16,128]{2,1,0:T(8,128)(2,1)S(1)} collective-permute-done((bf16[16,16,128]{2,1,0:T(8,128)(2,1)S(1)}, bf16[16,16,128]{2,1,0:T(8,128)(2,1)S(1)}, u32[]{:S(2)}, u32[]{:S(2)}) %collective-permute-start.4) | collective-permute-done | bytes 65568 | tf_op jit(solution)/shard_map/ppermute | solution.py:245
  19.5 0.4 %collective-permute-done.5.tile_ref = bf16[16,16,128]{2,1,0:T(8,128)(2,1)S(1)} collective-permute-done((bf16[16,16,128]{2,1,0:T(8,128)(2,1)S(1)}, bf16[16,16,128]{2,1,0:T(8,128)(2,1)S(1)}, u32[]{:S(2)}, u32[]{:S(2)}) %collective-permute-start.5) | collective-permute-done | bytes 65568 | tf_op jit(solution)/shard_map/ppermute | solution.py:245
  20.2 2.1 %collective-permute-start.6 = (bf16[16,16,128]{2,1,0:T(8,128)(2,1)S(1)}, bf16[16,16,128]{2,1,0:T(8,128)(2,1)S(1)}, u32[]{:S(2)}, u32[]{:S(2)}) collective-permute-start(bf16[16,16,128]{2,1,0:T(8,128)(2,1)S(1)} %get-tuple-element.21.refs_0_), channel_id=1, source_target_pairs={{0,8},{4,12},{8,0},{12,4},{1,9},{5,13},{9,1},{13,5},{2,10},{6,14},... | collective-permute-start | bytes 196616 | tf_op jit(solution)/shard_map/ppermute | solution.py:245
  22.3 0.9 %collective-permute-start.7 = (bf16[16,16,128]{2,1,0:T(8,128)(2,1)S(1)}, bf16[16,16,128]{2,1,0:T(8,128)(2,1)S(1)}, u32[]{:S(2)}, u32[]{:S(2)}) collective-permute-start(bf16[16,16,128]{2,1,0:T(8,128)(2,1)S(1)} %get-tuple-element.21.refs_0_), channel_id=1, source_target_pairs={{0,12},{4,8},{8,4},{12,0},{1,13},{5,9},{9,5},{13,1},{2,14},{6,10},... | collective-permute-start | bytes 196616 | tf_op jit(solution)/shard_map/ppermute | solution.py:245
  23.2 0.6 %collective-permute-start.8 = (bf16[16,16,128]{2,1,0:T(8,128)(2,1)S(1)}, bf16[16,16,128]{2,1,0:T(8,128)(2,1)S(1)}, u32[]{:S(2)}, u32[]{:S(2)}) collective-permute-start(bf16[16,16,128]{2,1,0:T(8,128)(2,1)S(1)} %get-tuple-element.21.refs_0_), channel_id=1, source_target_pairs={{0,4},{4,0},{8,12},{12,8},{1,5},{5,1},{9,13},{13,9},{2,6},{6,2},{1... | collective-permute-start | bytes 196616 | tf_op jit(solution)/shard_map/ppermute | solution.py:245
  23.8 0.8 %shard_map.87 = (bf16[16,16,128]{2,1,0:T(8,128)(2,1)}, f32[256,128]{1,0:T(8,128)S(1)}) custom-call(f32[256,128]{1,0:T(8,128)S(1)} %get-tuple-element.17.tri_normed_ref, f32[256,128]{1,0:T(8,128)S(1)} %get-tuple-element.18.open_ref, f32[256,128]{1,0:T(8,128)S(1)} %get-tuple-element.19.gate_factor_ref, bf16[128,640]{1,0:T(8,128)(2,1)S(1)} %copy-done, ...), custom_call_target="tpu_custom_call" | custom-call | flops 16777216 | bytes 786432 | tf_op jit(solution)/shard_map/pallas_call | solution.py:219
  24.6 2.9 %collective-permute-done.6.refs_1_ = bf16[16,16,128]{2,1,0:T(8,128)(2,1)S(1)} collective-permute-done((bf16[16,16,128]{2,1,0:T(8,128)(2,1)S(1)}, bf16[16,16,128]{2,1,0:T(8,128)(2,1)S(1)}, u32[]{:S(2)}, u32[]{:S(2)}) %collective-permute-start.6) | collective-permute-done | bytes 65568 | tf_op jit(solution)/shard_map/ppermute | solution.py:245
  27.5 1.1 %collective-permute-done.7.refs_2_ = bf16[16,16,128]{2,1,0:T(8,128)(2,1)S(1)} collective-permute-done((bf16[16,16,128]{2,1,0:T(8,128)(2,1)S(1)}, bf16[16,16,128]{2,1,0:T(8,128)(2,1)S(1)}, u32[]{:S(2)}, u32[]{:S(2)}) %collective-permute-start.7) | collective-permute-done | bytes 65568 | tf_op jit(solution)/shard_map/ppermute | solution.py:245
  28.5 0.4 %collective-permute-done.8.refs_3_ = bf16[16,16,128]{2,1,0:T(8,128)(2,1)S(1)} collective-permute-done((bf16[16,16,128]{2,1,0:T(8,128)(2,1)S(1)}, bf16[16,16,128]{2,1,0:T(8,128)(2,1)S(1)}, u32[]{:S(2)}, u32[]{:S(2)}) %collective-permute-start.8) | collective-permute-done | bytes 65568 | tf_op jit(solution)/shard_map/ppermute | solution.py:245
  29.0 0.4 shard_map.90
  29.4 1.4 %collective-permute-start.9 = (bf16[16,16,128]{2,1,0:T(8,128)(2,1)S(1)}, bf16[16,16,128]{2,1,0:T(8,128)(2,1)S(1)}, u32[]{:S(2)}, u32[]{:S(2)}) collective-permute-start(bf16[16,16,128]{2,1,0:T(8,128)(2,1)S(1)} %shard_map.90), channel_id=1, source_target_pairs={{0,2},{1,3},{2,0},{3,1},{4,6},{5,7},{6,4},{7,5},{8,10},{9,11},{10,... | collective-permute-start | bytes 196616 | tf_op jit(solution)/shard_map/ppermute | solution.py:245
  31.6 0.8 %collective-permute-start.10 = (bf16[16,16,128]{2,1,0:T(8,128)(2,1)S(1)}, bf16[16,16,128]{2,1,0:T(8,128)(2,1)S(1)}, u32[]{:S(2)}, u32[]{:S(2)}) collective-permute-start(bf16[16,16,128]{2,1,0:T(8,128)(2,1)S(1)} %shard_map.92), channel_id=1, source_target_pairs={{0,3},{1,2},{2,1},{3,0},{4,7},{5,6},{6,5},{7,4},{8,11},{9,10},{10,... | collective-permute-start | bytes 196616 | tf_op jit(solution)/shard_map/ppermute | solution.py:245
  32.4 0.4 %shard_map.89.base = f32[16,16,128]{2,1,0:T(8,128)S(1)} custom-call(f32[64,16,128]{2,1,0:T(8,128)S(1)} %shard_map.88.panel, bf16[16,16,128]{2,1,0:T(8,128)(2,1)S(1)} %get-tuple-element.23.right_ref), custom_call_target="tpu_custom_call" | custom-call | flops 1048576 | bytes 720896 | tf_op jit(solution)/shard_map/pallas_call | solution.py:219
  32.8 1.4 %shard_map.95.right_ref = f32[16,16,128]{2,1,0:T(8,128)S(1)} custom-call(f32[64,16,128]{2,1,0:T(8,128)S(1)} %shard_map.78.panel, bf16[16,16,128]{2,1,0:T(8,128)(2,1)S(1)} %get-tuple-element.21.refs_0_, bf16[16,16,128]{2,1,0:T(8,128)(2,1)S(1)} %collective-permute-done.6.refs_1_, bf16[16,16,128]{2,1,0:T(8,128)(2,1)S(1)} %collective-permute-done.7.refs_2_, ...), custom_call_target="tpu_custom_call" | custom-call | flops 4194304 | bytes 917504 | tf_op jit(solution)/shard_map/pallas_call | solution.py:219
  34.2 1.2 %collective-permute-done.10.tile_ref = bf16[16,16,128]{2,1,0:T(8,128)(2,1)S(1)} collective-permute-done((bf16[16,16,128]{2,1,0:T(8,128)(2,1)S(1)}, bf16[16,16,128]{2,1,0:T(8,128)(2,1)S(1)}, u32[]{:S(2)}, u32[]{:S(2)}) %collective-permute-start.10) | collective-permute-done | bytes 65568 | tf_op jit(solution)/shard_map/ppermute | solution.py:245
  35.4 1.0 %shard_map.96 = bf16[16,16,128]{2,1,0:T(8,128)(2,1)} custom-call(f32[16,16,128]{2,1,0:T(8,128)S(1)} %shard_map.93.base, bf16[16,16,128]{2,1,0:T(8,128)(2,1)S(1)} %collective-permute-done.11.tile_ref, f32[16,16,128]{2,1,0:T(8,128)S(1)} %shard_map.95.right_ref, f32[256,128]{1,0:T(8,128)S(1)} %get-tuple-element.24.normed_ref, ...), custom_call_target="tpu_custom_call" | custom-call | flops 33554432 | bytes 1474560 | tf_op jit(solution)/shard_map/pallas_call | solution.py:219
  (24 shorter events, 3.0 us)
Async XLA Ops:
  2.6 5.2 %collective-permute-start = (bf16[16,16,128]{2,1,0:T(8,128)(2,1)S(1)}, bf16[16,16,128]{2,1,0:T(8,128)(2,1)S(1)}, u32[]{:S(2)}, u32[]{:S(2)}) collective-permute-start(bf16[16,16,128]{2,1,0:T(8,128)(2,1)S(1)} %shard_map.77.refs_0_), channel_id=1, source_target_pairs={{0,2},{1,3},{2,0},{3,1},{4,6},{5,7},{6,4},{7,5},{8,10},{9,11},{10,... | collective-permute-start | bytes 196616 | tf_op jit(solution)/shard_map/ppermute | solution.py:245
  5.6 4.1 %collective-permute-start.1 = (bf16[16,16,128]{2,1,0:T(8,128)(2,1)S(1)}, bf16[16,16,128]{2,1,0:T(8,128)(2,1)S(1)}, u32[]{:S(2)}, u32[]{:S(2)}) collective-permute-start(bf16[16,16,128]{2,1,0:T(8,128)(2,1)S(1)} %shard_map.77.refs_0_), channel_id=1, source_target_pairs={{0,3},{1,2},{2,1},{3,0},{4,7},{5,6},{6,5},{7,4},{8,11},{9,10},{10,... | collective-permute-start | bytes 196616 | tf_op jit(solution)/shard_map/ppermute | solution.py:245
  5.7 4.1 %collective-permute-start.2 = (bf16[16,16,128]{2,1,0:T(8,128)(2,1)S(1)}, bf16[16,16,128]{2,1,0:T(8,128)(2,1)S(1)}, u32[]{:S(2)}, u32[]{:S(2)}) collective-permute-start(bf16[16,16,128]{2,1,0:T(8,128)(2,1)S(1)} %shard_map.77.refs_0_), channel_id=1, source_target_pairs={{0,1},{1,0},{2,3},{3,2},{4,5},{5,4},{6,7},{7,6},{8,9},{9,8},{10,11... | collective-permute-start | bytes 196616 | tf_op jit(solution)/shard_map/ppermute | solution.py:245
  10.2 6.9 %collective-permute-start.3 = (bf16[16,16,128]{2,1,0:T(8,128)(2,1)S(1)}, bf16[16,16,128]{2,1,0:T(8,128)(2,1)S(1)}, u32[]{:S(2)}, u32[]{:S(2)}) collective-permute-start(bf16[16,16,128]{2,1,0:T(8,128)(2,1)S(1)} %shard_map.81), channel_id=1, source_target_pairs={{0,8},{4,12},{8,0},{12,4},{1,9},{5,13},{9,1},{13,5},{2,10},{6,14},... | collective-permute-start | bytes 196616 | tf_op jit(solution)/shard_map/ppermute | solution.py:245
  13.2 6.3 %collective-permute-start.4 = (bf16[16,16,128]{2,1,0:T(8,128)(2,1)S(1)}, bf16[16,16,128]{2,1,0:T(8,128)(2,1)S(1)}, u32[]{:S(2)}, u32[]{:S(2)}) collective-permute-start(bf16[16,16,128]{2,1,0:T(8,128)(2,1)S(1)} %shard_map.83), channel_id=1, source_target_pairs={{0,12},{4,8},{8,4},{12,0},{1,13},{5,9},{9,5},{13,1},{2,14},{6,10},... | collective-permute-start | bytes 196616 | tf_op jit(solution)/shard_map/ppermute | solution.py:245
  14.9 5.0 %collective-permute-start.5 = (bf16[16,16,128]{2,1,0:T(8,128)(2,1)S(1)}, bf16[16,16,128]{2,1,0:T(8,128)(2,1)S(1)}, u32[]{:S(2)}, u32[]{:S(2)}) collective-permute-start(bf16[16,16,128]{2,1,0:T(8,128)(2,1)S(1)} %shard_map.85), channel_id=1, source_target_pairs={{0,4},{4,0},{8,12},{12,8},{1,5},{5,1},{9,13},{13,9},{2,6},{6,2},{1... | collective-permute-start | bytes 196616 | tf_op jit(solution)/shard_map/ppermute | solution.py:245
  19.9 3.8 %copy-start = (bf16[128,640]{1,0:T(8,128)(2,1)S(1)}, bf16[128,640]{1,0:T(8,128)(2,1)}, u32[]{:S(2)}) copy-start(bf16[128,640]{1,0:T(8,128)(2,1)} %weights_ref.3) | copy-start | bytes 491524
  19.9 3.8 %copy-start.1 = (bf16[128,128]{1,0:T(8,128)(2,1)S(1)}, bf16[128,128]{1,0:T(8,128)(2,1)}, u32[]{:S(2)}) copy-start(bf16[128,128]{1,0:T(8,128)(2,1)} %out_weight_ref.1) | copy-start | bytes 98308
  20.2 7.2 %collective-permute-start.6 = (bf16[16,16,128]{2,1,0:T(8,128)(2,1)S(1)}, bf16[16,16,128]{2,1,0:T(8,128)(2,1)S(1)}, u32[]{:S(2)}, u32[]{:S(2)}) collective-permute-start(bf16[16,16,128]{2,1,0:T(8,128)(2,1)S(1)} %get-tuple-element.21.refs_0_), channel_id=1, source_target_pairs={{0,8},{4,12},{8,0},{12,4},{1,9},{5,13},{9,1},{13,5},{2,10},{6,14},... | collective-permute-start | bytes 196616 | tf_op jit(solution)/shard_map/ppermute | solution.py:245
  22.3 6.2 %collective-permute-start.7 = (bf16[16,16,128]{2,1,0:T(8,128)(2,1)S(1)}, bf16[16,16,128]{2,1,0:T(8,128)(2,1)S(1)}, u32[]{:S(2)}, u32[]{:S(2)}) collective-permute-start(bf16[16,16,128]{2,1,0:T(8,128)(2,1)S(1)} %get-tuple-element.21.refs_0_), channel_id=1, source_target_pairs={{0,12},{4,8},{8,4},{12,0},{1,13},{5,9},{9,5},{13,1},{2,14},{6,10},... | collective-permute-start | bytes 196616 | tf_op jit(solution)/shard_map/ppermute | solution.py:245
  23.2 5.7 %collective-permute-start.8 = (bf16[16,16,128]{2,1,0:T(8,128)(2,1)S(1)}, bf16[16,16,128]{2,1,0:T(8,128)(2,1)S(1)}, u32[]{:S(2)}, u32[]{:S(2)}) collective-permute-start(bf16[16,16,128]{2,1,0:T(8,128)(2,1)S(1)} %get-tuple-element.21.refs_0_), channel_id=1, source_target_pairs={{0,4},{4,0},{8,12},{12,8},{1,5},{5,1},{9,13},{13,9},{2,6},{6,2},{1... | collective-permute-start | bytes 196616 | tf_op jit(solution)/shard_map/ppermute | solution.py:245
  29.4 4.8 %collective-permute-start.9 = (bf16[16,16,128]{2,1,0:T(8,128)(2,1)S(1)}, bf16[16,16,128]{2,1,0:T(8,128)(2,1)S(1)}, u32[]{:S(2)}, u32[]{:S(2)}) collective-permute-start(bf16[16,16,128]{2,1,0:T(8,128)(2,1)S(1)} %shard_map.90), channel_id=1, source_target_pairs={{0,2},{1,3},{2,0},{3,1},{4,6},{5,7},{6,4},{7,5},{8,10},{9,11},{10,... | collective-permute-start | bytes 196616 | tf_op jit(solution)/shard_map/ppermute | solution.py:245
  31.1 4.3 %collective-permute-start.11 = (bf16[16,16,128]{2,1,0:T(8,128)(2,1)S(1)}, bf16[16,16,128]{2,1,0:T(8,128)(2,1)S(1)}, u32[]{:S(2)}, u32[]{:S(2)}) collective-permute-start(bf16[16,16,128]{2,1,0:T(8,128)(2,1)S(1)} %shard_map.94), channel_id=1, source_target_pairs={{0,1},{1,0},{2,3},{3,2},{4,5},{5,4},{6,7},{7,6},{8,9},{9,8},{10,11... | collective-permute-start | bytes 196616 | tf_op jit(solution)/shard_map/ppermute | solution.py:245
  31.6 3.8 %collective-permute-start.10 = (bf16[16,16,128]{2,1,0:T(8,128)(2,1)S(1)}, bf16[16,16,128]{2,1,0:T(8,128)(2,1)S(1)}, u32[]{:S(2)}, u32[]{:S(2)}) collective-permute-start(bf16[16,16,128]{2,1,0:T(8,128)(2,1)S(1)} %shard_map.92), channel_id=1, source_target_pairs={{0,3},{1,2},{2,1},{3,0},{4,7},{5,6},{6,5},{7,4},{8,11},{9,10},{10,... | collective-permute-start | bytes 196616 | tf_op jit(solution)/shard_map/ppermute | solution.py:245

commit v6 on v5

--- a/solution.py
+++ b/solution.py
@@ -77,9 +77,10 @@
     copies[0].wait()
     normed, _ = normalize(acts_ref[...].astype(f32).reshape(size * size, channels))
     normed = normed.astype(bf16)
-    for copy in copies[1:]:
-        copy.wait()
-    left, _, _ = gated(dot(normed, weights_ref[...]), 0, keep_rows(mask_ref, crop_ref, channels))
+    copies[2].wait()
+    keep = keep_rows(mask_ref, crop_ref, channels)
+    copies[1].wait()
+    left, _, _ = gated(dot(normed, weights_ref[...]), 0, keep)
     left_ref[...] = left.reshape(size, size, channels)
 
 
@@ -106,7 +107,7 @@
         tile, opened, value = gated(projected, block, keep)
         factor_ref[block] = keep * opened
         factor_ref[block + 1] = keep * value * opened * (1.0 - opened)
-    right_ref[...] = tile.reshape(size, size, channels)
+    right_ref[...] = tile.astype(f32).reshape(size, size, channels)
     out_open = sigmoid(projected[:, 4 * channels :])
     cotangent = cotangent_ref[...].astype(f32).reshape(pairs, channels)
     lin_grad = (cotangent * out_open).astype(bf16)
@@ -125,13 +126,15 @@
         out[k] = total.astype(out.dtype)
         return 0
 
-    lax.fori_loop(0, out.shape[0], step, 0)
+    lax.fori_loop(0, out.shape[0], step, 0, unroll=4)
 
 
 def panel_kernel(axis, steps, *refs):
-    here, rows, panel = lax.axis_index(axis), refs[0].shape[0], refs[-1]
+    here, panel = lax.axis_index(axis), refs[-1]
+    rows = panel.shape[0] // len(steps)
     for step, ref in zip(steps, refs):
-        panel[pl.ds((here ^ step) * rows, rows)] = ref[...].astype(f32)
+        tile = ref[...].astype(f32)
+        panel[pl.ds((here ^ step) * rows, rows)] = tile.reshape((rows,) + panel.shape[1:])
 
 
 def partial_kernel(steps, panel, right_ref, *outs):
@@ -140,11 +143,11 @@
         start = (lax.axis_index("row") ^ step) * size
 
         def add(k, sums):
-            other = right_ref[k].astype(f32)
+            other = right_ref[k]
             return tuple(sums[i] + panel[start + k, pl.ds(i, 1), :] * other for i in range(size))
 
         zero = jnp.zeros((size, channels), f32)
-        sums = lax.fori_loop(0, size, add, (zero,) * size)
+        sums = lax.fori_loop(0, size, add, (zero,) * size, unroll=4)
         for i in range(size):
             out[i] = sums[i].astype(out.dtype)
 
@@ -158,21 +161,28 @@
         grad_ref[i] = normalize_back(tri_normed, scale, upstream_ref[here, :]).astype(bf16)
 
 
-def left_terms_kernel(step, panel, right_ref, out, grad, right):
-    size, _, channels = right_ref.shape
-    right[...] = right_ref[...].astype(f32)
-    here = panel[pl.ds((lax.axis_index("col") ^ step) * size, size)]
-    grad[...] = here.reshape(size * size, channels)
-    weighted_sums(right, 0, [grad[pl.ds(j, size, stride=size), :] for j in range(size)], out)
+def left_terms_kernel(step, panel, right, out):
+    size = out.shape[0]
+    start = (lax.axis_index("col") ^ step) * (size * size)
+    weighted_sums(right, 0, [panel[pl.ds(start + j, size, stride=size), :] for j in range(size)], out)
 
 
 def right_grad_kernel(steps, panel, *refs):
-    out, base = refs[-1], None
+    out, base = refs[-1], refs[len(steps)] if len(refs) > len(steps) + 1 else None
     size = out.shape[0]
     for step, grad in zip(steps, refs):
         start = (lax.axis_index("row") ^ step) * size
         weighted_sums(panel, start, [grad[i].astype(f32) for i in range(size)], out, base)
         base = out
+
+
+def right_back_kernel(steps, panel, *refs):
+    factor_ref, weights_ref, share_ref, out, right_ref = refs[-5:]
+    right_grad_kernel(steps, panel, *refs[: len(steps) + 1], right_ref)
+    pairs, channels = out.shape
+    right = right_ref[...].reshape(pairs, channels)
+    grads = jnp.concatenate([(right * factor_ref[block]).astype(bf16) for block in (2, 3)], axis=1)
+    out[...] = share_ref[...] + dot_t(grads, weights_ref[:, 2 * channels : 4 * channels])
 
 
 def add_kernel(base, tile_ref, out):
@@ -190,23 +200,24 @@
     normed_grad_ref[...] = dot_t(out_gate_grad, weights_ref[:, 4 * channels :])
 
 
-def back_kernel(
-    base, tile_ref, right_ref, normed_ref, scale_ref, factor_ref, partial_ref, weights_ref, out_ref
-):
-    size, _, channels = out_ref.shape
-    pairs = size * size
-    left = (base[...] + tile_ref[...].astype(f32)).reshape(pairs, channels)
-    right = right_ref[...].reshape(pairs, channels)
-    grads = jnp.concatenate(
-        [(total * factor_ref[block]).astype(bf16) for block, total in enumerate((left, left, right, right))],
-        axis=1,
-    )
-    normed_grad = partial_ref[...] + dot_t(grads, weights_ref[:, : 4 * channels])
-    back = normalize_back(normed_ref[...], scale_ref[...], normed_grad)
-    out_ref[...] = back.astype(bf16).reshape(size, size, channels)
-
-
-def call(kernel, outs, *args, scratch=(), flops=0, smem=(), hbm=()):
+def back_kernel(base, tile_ref, normed_ref, scale_ref, factor_ref, share_ref, weights_ref, out, done, sems):
+    size, _, channels = done.shape
+    half = size // 2
+    copies = []
+    for part in range(2):
+        tiles, rows = pl.ds(part * half, half), pl.ds(part * half * size, half * size)
+        left = (base[tiles] + tile_ref[tiles].astype(f32)).reshape(half * size, channels)
+        grads = jnp.concatenate([(left * factor_ref[block, rows]).astype(bf16) for block in (0, 1)], axis=1)
+        normed_grad = share_ref[rows, :] + dot_t(grads, weights_ref[:, : 2 * channels])
+        back = normalize_back(normed_ref[rows, :], scale_ref[rows, :], normed_grad)
+        done[tiles] = back.astype(bf16).reshape(half, size, channels)
+        copies.append(pltpu.make_async_copy(done.at[tiles], out.at[tiles], sems.at[part]))
+        copies[-1].start()
+    for copy in copies:
+        copy.wait()
+
+
+def call(kernel, outs, *args, scratch=(), flops=0, smem=(), hbm=(), out_space=pltpu.VMEM):
     spec = pl.BlockSpec(memory_space=pltpu.VMEM)
     total = sum(a.size * a.dtype.itemsize for a in (*args, *outs))
     specs = [spec] * len(args)
@@ -220,7 +231,7 @@
         kernel,
         out_shape=tuple(outs),
         in_specs=specs,
-        out_specs=(spec,) * len(outs),
+        out_specs=(pl.BlockSpec(memory_space=out_space),) * len(outs),
         scratch_shapes=scratch,
         compiler_params=pltpu.CompilerParams(vmem_limit_bytes=24 * 2**20),
         cost_estimate=pl.CostEstimate(flops=flops, bytes_accessed=total if flops else 0, transcendentals=0),
@@ -260,7 +271,7 @@
     lefts = gather(left, "col")
     right, normed, scale, factors, out_open, gate_factor, upstream = call(
         factors_kernel,
-        (tile, flat, flat, jax.ShapeDtypeStruct((4, pairs, channels), f32), flat, flat, flat),
+        (wide, flat, flat, jax.ShapeDtypeStruct((4, pairs, channels), f32), flat, flat, flat),
         pair_acts, pair_mask, crop_length, cotangent, in_weights, out_weight,
         smem=(2,), hbm=(0, 1, 3, 4, 5), flops=2 * pairs * channels * 6 * channels,
         scratch=[
@@ -291,27 +302,34 @@
         update_kernel, (tile, flat), tri_normed, out_open, gate_factor, in_weights, out_weight,
         flops=4 * pairs * channels * channels,
     )
-    right, partial = lax.optimization_barrier((right, partial))
-    (grad_panel,) = call(functools.partial(panel_kernel, "row", [0] + steps), (panel,), *grads)
+    (right_grad,) = call(functools.partial(right_grad_kernel, [0]), (wide,), left_panel, tri_grad)
+    right, partial, right_grad = lax.optimization_barrier((right, partial, right_grad))
+    (grad_panel,) = call(
+        functools.partial(panel_kernel, "row", [0] + steps), (jax.ShapeDtypeStruct((n * pairs, channels), f32),), *grads
+    )
     terms = {}
-    for step in [0] + steps:
+    for step in steps + [0]:
+        if terms:
+            right, terms[last] = lax.optimization_barrier((right, terms[last]))
+        last = step
         (terms[step],) = call(
             functools.partial(left_terms_kernel, step), (tile if step else wide,), grad_panel, right,
-            scratch=[pltpu.VMEM((pairs, channels), f32), pltpu.VMEM(wide.shape, f32)], flops=work,
+            flops=work,
         )
     total = terms[0]
     for step in steps:
         term = swap(terms[step], "col", step)
         if step != steps[-1]:
             (total,) = call(add_kernel, (wide,), total, term, flops=wait)
-    (right_grad,) = call(
-        functools.partial(right_grad_kernel, [0] + steps), (wide,), left_panel, *grads,
-        flops=2 * n * size * pairs * channels,
+    (share,) = call(
+        functools.partial(right_back_kernel, steps), (flat,),
+        left_panel, *grads[1:], right_grad, factors, in_weights, partial,
+        scratch=[pltpu.VMEM(wide.shape, f32)],
     )
     (pair_grad,) = call(
-        back_kernel, (tile,),
-        total, term, right_grad, normed, scale, factors, partial, in_weights,
-        flops=2 * pairs * channels * 4 * channels,
+        back_kernel, (tile,), total, term, normed, scale, factors, share, in_weights,
+        scratch=[pltpu.VMEM(tile.shape, bf16), pltpu.SemaphoreType.DMA((2,))], out_space=pl.ANY,
+        flops=2 * pairs * channels * 2 * channels,
     )
     return (update, pair_grad)
 

time: 36.6 us -> 36.1 us (0.986)
  Pallas kernels: 9.08 us -> 7.71 us
  waiting for transfers between devices: 12.4 us -> 13.2 us
    pallas_call x20 -> x21, Pallas kernels: 9.08 us -> 7.71 us  [call(): pl.pallas_call(kernel, out_shape=tuple(outs), in_specs=specs, out_specs=(...]
    ppermute x12, waiting for transfers between devices: 12.4 us -> 13.2 us  [swap(): return lax.ppermute(values, axis, [(a, a ^ step) for a in range(n)])]
  transfers between devices with their start and end apart: 12 -> 12, of which waited for: 9 -> 10; matrix products, arithmetic and copies ran while one was open for 0% -> 0% of each run, Pallas kernels for 16% -> 12%
where the time goes in v6:
time: 36.1 us; the launch traced here: 35.9 us
  starting transfers between devices  13.5 us (37%)
  waiting for transfers between devices  13.2 us (37%)
  Pallas kernels  7.71 us (21%)
  between operations  1.42 us (4%)
    ppermute x12, starting transfers between devices, swap(): return lax.ppermute(values, axis, [(a, a ^ step) for a in range(n)])  13.5 us
    ppermute x12, waiting for transfers between devices, swap(): return lax.ppermute(values, axis, [(a, a ^ step) for a in range(n)])  13.2 us
    pallas_call x21, Pallas kernels, call(): pl.pallas_call(kernel, out_shape=tuple(outs), in_specs=specs, out_specs=(...  7.71 us
  transfers between devices with their start and end apart: 12, of which 10 were waited for; matrix products, arithmetic and copies ran while one was open for 0% of the time, Pallas kernels for 12%

profile of v6, /device:TPU:0, one launch (start us, length us, event | category | flops | bytes accessed | tf_op | source)
XLA Modules:
  0.0 35.9 jit_solution(11942569637147377613)
XLA Ops:
  1.3 1.5 %shard_map.77.refs_0_ = bf16[16,16,128]{2,1,0:T(8,128)(2,1)S(1)} custom-call(bf16[16,16,128]{2,1,0:T(8,128)(2,1)} %acts_in.3, s32[16,16]{1,0:T(8,128)} %mask_in.3, s32[1]{0:T(128)S(6)} %copy.8.crop_ref, bf16[128,640]{1,0:T(8,128)(2,1)} %weights_ref.3), custom_call_target="tpu_custom_call" | custom-call | flops 16777216 | bytes 295940 | tf_op jit(solution)/shard_map/pallas_call | solution.py:230
  2.8 3.0 %collective-permute-start = (bf16[16,16,128]{2,1,0:T(8,128)(2,1)S(1)}, bf16[16,16,128]{2,1,0:T(8,128)(2,1)S(1)}, u32[]{:S(2)}, u32[]{:S(2)}) collective-permute-start(bf16[16,16,128]{2,1,0:T(8,128)(2,1)S(1)} %shard_map.77.refs_0_), channel_id=1, source_target_pairs={{0,2},{1,3},{2,0},{3,1},{4,6},{5,7},{6,4},{7,5},{8,10},{9,11},{10,... | collective-permute-start | bytes 196616 | tf_op jit(solution)/shard_map/ppermute | solution.py:256
  6.0 1.5 %shard_map.79 = (f32[16,16,128]{2,1,0:T(8,128)S(1)}, f32[256,128]{1,0:T(8,128)S(1)}, f32[256,128]{1,0:T(8,128)S(1)}, f32[4,256,128]{2,1,0:T(8,128)S(1)}, f32[256...) custom-call(bf16[16,16,128]{2,1,0:T(8,128)(2,1)} %acts_in.3, s32[16,16]{1,0:T(8,128)} %mask_in.3, ...), custom_call_target="tpu_custom_call" | custom-call | flops 50331648 | bytes 1639428 | tf_op jit(solution)/shard_map/pallas_call | solution.py:230
  7.5 0.6 %collective-permute-done.refs_1_ = bf16[16,16,128]{2,1,0:T(8,128)(2,1)S(1)} collective-permute-done((bf16[16,16,128]{2,1,0:T(8,128)(2,1)S(1)}, bf16[16,16,128]{2,1,0:T(8,128)(2,1)S(1)}, u32[]{:S(2)}, u32[]{:S(2)}) %collective-permute-start) | collective-permute-done | bytes 65568 | tf_op jit(solution)/shard_map/ppermute | solution.py:256
  8.1 1.9 %collective-permute-done.1.refs_2_ = bf16[16,16,128]{2,1,0:T(8,128)(2,1)S(1)} collective-permute-done((bf16[16,16,128]{2,1,0:T(8,128)(2,1)S(1)}, bf16[16,16,128]{2,1,0:T(8,128)(2,1)S(1)}, u32[]{:S(2)}, u32[]{:S(2)}) %collective-permute-start.1) | collective-permute-done | bytes 65568 | tf_op jit(solution)/shard_map/ppermute | solution.py:256
  10.2 2.7 %collective-permute-start.3 = (bf16[16,16,128]{2,1,0:T(8,128)(2,1)S(1)}, bf16[16,16,128]{2,1,0:T(8,128)(2,1)S(1)}, u32[]{:S(2)}, u32[]{:S(2)}) collective-permute-start(bf16[16,16,128]{2,1,0:T(8,128)(2,1)S(1)} %shard_map.81), channel_id=1, source_target_pairs={{0,8},{4,12},{8,0},{12,4},{1,9},{5,13},{9,1},{13,5},{2,10},{6,14},... | collective-permute-start | bytes 196616 | tf_op jit(solution)/shard_map/ppermute | solution.py:256
  13.1 1.4 %collective-permute-start.4 = (bf16[16,16,128]{2,1,0:T(8,128)(2,1)S(1)}, bf16[16,16,128]{2,1,0:T(8,128)(2,1)S(1)}, u32[]{:S(2)}, u32[]{:S(2)}) collective-permute-start(bf16[16,16,128]{2,1,0:T(8,128)(2,1)S(1)} %shard_map.83), channel_id=1, source_target_pairs={{0,12},{4,8},{8,4},{12,0},{1,13},{5,9},{9,5},{13,1},{2,14},{6,10},... | collective-permute-start | bytes 196616 | tf_op jit(solution)/shard_map/ppermute | solution.py:256
  14.7 0.3 collective-permute-start.5
  15.2 1.9 %collective-permute-done.3.tile_ref = bf16[16,16,128]{2,1,0:T(8,128)(2,1)S(1)} collective-permute-done((bf16[16,16,128]{2,1,0:T(8,128)(2,1)S(1)}, bf16[16,16,128]{2,1,0:T(8,128)(2,1)S(1)}, u32[]{:S(2)}, u32[]{:S(2)}) %collective-permute-start.3) | collective-permute-done | bytes 65568 | tf_op jit(solution)/shard_map/ppermute | solution.py:256
  17.1 2.3 %collective-permute-done.4.tile_ref = bf16[16,16,128]{2,1,0:T(8,128)(2,1)S(1)} collective-permute-done((bf16[16,16,128]{2,1,0:T(8,128)(2,1)S(1)}, bf16[16,16,128]{2,1,0:T(8,128)(2,1)S(1)}, u32[]{:S(2)}, u32[]{:S(2)}) %collective-permute-start.4) | collective-permute-done | bytes 65568 | tf_op jit(solution)/shard_map/ppermute | solution.py:256
  19.5 0.3 collective-permute-done.5.tile_ref
  19.7 0.3 shard_map.86
  20.0 2.4 %collective-permute-start.6 = (bf16[16,16,128]{2,1,0:T(8,128)(2,1)S(1)}, bf16[16,16,128]{2,1,0:T(8,128)(2,1)S(1)}, u32[]{:S(2)}, u32[]{:S(2)}) collective-permute-start(bf16[16,16,128]{2,1,0:T(8,128)(2,1)S(1)} %get-tuple-element.28.refs_0_), channel_id=1, source_target_pairs={{0,8},{4,12},{8,0},{12,4},{1,9},{5,13},{9,1},{13,5},{2,10},{6,14},... | collective-permute-start | bytes 196616 | tf_op jit(solution)/shard_map/ppermute | solution.py:256
  22.4 0.8 %collective-permute-start.7 = (bf16[16,16,128]{2,1,0:T(8,128)(2,1)S(1)}, bf16[16,16,128]{2,1,0:T(8,128)(2,1)S(1)}, u32[]{:S(2)}, u32[]{:S(2)}) collective-permute-start(bf16[16,16,128]{2,1,0:T(8,128)(2,1)S(1)} %get-tuple-element.28.refs_0_), channel_id=1, source_target_pairs={{0,12},{4,8},{8,4},{12,0},{1,13},{5,9},{9,5},{13,1},{2,14},{6,10},... | collective-permute-start | bytes 196616 | tf_op jit(solution)/shard_map/ppermute | solution.py:256
  23.2 0.5 %collective-permute-start.8 = (bf16[16,16,128]{2,1,0:T(8,128)(2,1)S(1)}, bf16[16,16,128]{2,1,0:T(8,128)(2,1)S(1)}, u32[]{:S(2)}, u32[]{:S(2)}) collective-permute-start(bf16[16,16,128]{2,1,0:T(8,128)(2,1)S(1)} %get-tuple-element.28.refs_0_), channel_id=1, source_target_pairs={{0,4},{4,0},{8,12},{12,8},{1,5},{5,1},{9,13},{13,9},{2,6},{6,2},{1... | collective-permute-start | bytes 196616 | tf_op jit(solution)/shard_map/ppermute | solution.py:256
  23.9 0.8 %shard_map.87 = (bf16[16,16,128]{2,1,0:T(8,128)(2,1)}, f32[256,128]{1,0:T(8,128)S(1)}) custom-call(f32[256,128]{1,0:T(8,128)S(1)} %get-tuple-element.24.tri_normed_ref, f32[256,128]{1,0:T(8,128)S(1)} %get-tuple-element.25.open_ref, f32[256,128]{1,0:T(8,128)S(1)} %get-tuple-element.26.gate_factor_ref, bf16[128,640]{1,0:T(8,128)(2,1)S(1)} %copy-done, ...), custom_call_target="tpu_custom_call" | custom-call | flops 16777216 | bytes 786432 | tf_op jit(solution)/shard_map/pallas_call | solution.py:230
  24.7 2.5 %collective-permute-done.6.refs_1_.refs_0_ = bf16[16,16,128]{2,1,0:T(8,128)(2,1)S(1)} collective-permute-done((bf16[16,16,128]{2,1,0:T(8,128)(2,1)S(1)}, bf16[16,16,128]{2,1,0:T(8,128)(2,1)S(1)}, u32[]{:S(2)}, u32[]{:S(2)}) %collective-permute-start.6) | collective-permute-done | bytes 65568 | tf_op jit(solution)/shard_map/ppermute | solution.py:256
  27.2 1.4 %collective-permute-done.7.refs_2_.refs_1_ = bf16[16,16,128]{2,1,0:T(8,128)(2,1)S(1)} collective-permute-done((bf16[16,16,128]{2,1,0:T(8,128)(2,1)S(1)}, bf16[16,16,128]{2,1,0:T(8,128)(2,1)S(1)}, u32[]{:S(2)}, u32[]{:S(2)}) %collective-permute-start.7) | collective-permute-done | bytes 65568 | tf_op jit(solution)/shard_map/ppermute | solution.py:256
  29.0 1.7 %collective-permute-start.9 = (bf16[16,16,128]{2,1,0:T(8,128)(2,1)S(1)}, bf16[16,16,128]{2,1,0:T(8,128)(2,1)S(1)}, u32[]{:S(2)}, u32[]{:S(2)}) collective-permute-start(bf16[16,16,128]{2,1,0:T(8,128)(2,1)S(1)} %shard_map.90), channel_id=1, source_target_pairs={{0,2},{1,3},{2,0},{3,1},{4,6},{5,7},{6,4},{7,5},{8,10},{9,11},{10,... | collective-permute-start | bytes 196616 | tf_op jit(solution)/shard_map/ppermute | solution.py:256
  31.2 0.5 %collective-permute-start.11 = (bf16[16,16,128]{2,1,0:T(8,128)(2,1)S(1)}, bf16[16,16,128]{2,1,0:T(8,128)(2,1)S(1)}, u32[]{:S(2)}, u32[]{:S(2)}) collective-permute-start(bf16[16,16,128]{2,1,0:T(8,128)(2,1)S(1)} %shard_map.92), channel_id=1, source_target_pairs={{0,1},{1,0},{2,3},{3,2},{4,5},{5,4},{6,7},{7,6},{8,9},{9,8},{10,11... | collective-permute-start | bytes 196616 | tf_op jit(solution)/shard_map/ppermute | solution.py:256
  31.7 0.7 %shard_map.96.share_ref = f32[256,128]{1,0:T(8,128)S(1)} custom-call(f32[64,16,128]{2,1,0:T(8,128)S(1)} %shard_map.78.panel, bf16[16,16,128]{2,1,0:T(8,128)(2,1)S(1)} %collective-permute-done.6.refs_1_.refs_0_, bf16[16,16,128]{2,1,0:T(8,128)(2,1)S(1)} %collective-permute-done.7.refs_2_.refs_1_, ...), custom_call_target="tpu_custom_call" | custom-call | tf_op jit(solution)/shard_map/pallas_call | solution.py:230
  32.7 0.7 %collective-permute-done.9.tile_ref = bf16[16,16,128]{2,1,0:T(8,128)(2,1)S(1)} collective-permute-done((bf16[16,16,128]{2,1,0:T(8,128)(2,1)S(1)}, bf16[16,16,128]{2,1,0:T(8,128)(2,1)S(1)}, u32[]{:S(2)}, u32[]{:S(2)}) %collective-permute-start.9) | collective-permute-done | bytes 65568 | tf_op jit(solution)/shard_map/ppermute | solution.py:256
  33.3 1.6 %collective-permute-done.10.tile_ref = bf16[16,16,128]{2,1,0:T(8,128)(2,1)S(1)} collective-permute-done((bf16[16,16,128]{2,1,0:T(8,128)(2,1)S(1)}, bf16[16,16,128]{2,1,0:T(8,128)(2,1)S(1)}, u32[]{:S(2)}, u32[]{:S(2)}) %collective-permute-start.10) | collective-permute-done | bytes 65568 | tf_op jit(solution)/shard_map/ppermute | solution.py:256
  34.9 0.9 %shard_map.97 = bf16[16,16,128]{2,1,0:T(8,128)(2,1)} custom-call(f32[16,16,128]{2,1,0:T(8,128)S(1)} %shard_map.95.base, bf16[16,16,128]{2,1,0:T(8,128)(2,1)S(1)} %collective-permute-done.11.tile_ref, f32[256,128]{1,0:T(8,128)S(1)} %get-tuple-element.37.normed_ref, f32[256,128]{1,0:T(8,128)S(1)} %get-tuple-element.38.scale_ref, ...), custom_call_target="tpu_custom_call" | custom-call | flops 16777216 | bytes 1343488 | tf_op jit(solution)/shard_map/pallas_call | solution.py:230
  (25 shorter events, 2.3 us)
Async XLA Ops:
  2.8 5.3 %collective-permute-start = (bf16[16,16,128]{2,1,0:T(8,128)(2,1)S(1)}, bf16[16,16,128]{2,1,0:T(8,128)(2,1)S(1)}, u32[]{:S(2)}, u32[]{:S(2)}) collective-permute-start(bf16[16,16,128]{2,1,0:T(8,128)(2,1)S(1)} %shard_map.77.refs_0_), channel_id=1, source_target_pairs={{0,2},{1,3},{2,0},{3,1},{4,6},{5,7},{6,4},{7,5},{8,10},{9,11},{10,... | collective-permute-start | bytes 196616 | tf_op jit(solution)/shard_map/ppermute | solution.py:256
  5.8 4.1 %collective-permute-start.1 = (bf16[16,16,128]{2,1,0:T(8,128)(2,1)S(1)}, bf16[16,16,128]{2,1,0:T(8,128)(2,1)S(1)}, u32[]{:S(2)}, u32[]{:S(2)}) collective-permute-start(bf16[16,16,128]{2,1,0:T(8,128)(2,1)S(1)} %shard_map.77.refs_0_), channel_id=1, source_target_pairs={{0,3},{1,2},{2,1},{3,0},{4,7},{5,6},{6,5},{7,4},{8,11},{9,10},{10,... | collective-permute-start | bytes 196616 | tf_op jit(solution)/shard_map/ppermute | solution.py:256
  5.8 4.1 %collective-permute-start.2 = (bf16[16,16,128]{2,1,0:T(8,128)(2,1)S(1)}, bf16[16,16,128]{2,1,0:T(8,128)(2,1)S(1)}, u32[]{:S(2)}, u32[]{:S(2)}) collective-permute-start(bf16[16,16,128]{2,1,0:T(8,128)(2,1)S(1)} %shard_map.77.refs_0_), channel_id=1, source_target_pairs={{0,1},{1,0},{2,3},{3,2},{4,5},{5,4},{6,7},{7,6},{8,9},{9,8},{10,11... | collective-permute-start | bytes 196616 | tf_op jit(solution)/shard_map/ppermute | solution.py:256
  10.2 6.9 %collective-permute-start.3 = (bf16[16,16,128]{2,1,0:T(8,128)(2,1)S(1)}, bf16[16,16,128]{2,1,0:T(8,128)(2,1)S(1)}, u32[]{:S(2)}, u32[]{:S(2)}) collective-permute-start(bf16[16,16,128]{2,1,0:T(8,128)(2,1)S(1)} %shard_map.81), channel_id=1, source_target_pairs={{0,8},{4,12},{8,0},{12,4},{1,9},{5,13},{9,1},{13,5},{2,10},{6,14},... | collective-permute-start | bytes 196616 | tf_op jit(solution)/shard_map/ppermute | solution.py:256
  13.1 6.4 %collective-permute-start.4 = (bf16[16,16,128]{2,1,0:T(8,128)(2,1)S(1)}, bf16[16,16,128]{2,1,0:T(8,128)(2,1)S(1)}, u32[]{:S(2)}, u32[]{:S(2)}) collective-permute-start(bf16[16,16,128]{2,1,0:T(8,128)(2,1)S(1)} %shard_map.83), channel_id=1, source_target_pairs={{0,12},{4,8},{8,4},{12,0},{1,13},{5,9},{9,5},{13,1},{2,14},{6,10},... | collective-permute-start | bytes 196616 | tf_op jit(solution)/shard_map/ppermute | solution.py:256
  14.7 5.0 %collective-permute-start.5 = (bf16[16,16,128]{2,1,0:T(8,128)(2,1)S(1)}, bf16[16,16,128]{2,1,0:T(8,128)(2,1)S(1)}, u32[]{:S(2)}, u32[]{:S(2)}) collective-permute-start(bf16[16,16,128]{2,1,0:T(8,128)(2,1)S(1)} %shard_map.85), channel_id=1, source_target_pairs={{0,4},{4,0},{8,12},{12,8},{1,5},{5,1},{9,13},{13,9},{2,6},{6,2},{1... | collective-permute-start | bytes 196616 | tf_op jit(solution)/shard_map/ppermute | solution.py:256
  20.0 3.8 %copy-start = (bf16[128,640]{1,0:T(8,128)(2,1)S(1)}, bf16[128,640]{1,0:T(8,128)(2,1)}, u32[]{:S(2)}) copy-start(bf16[128,640]{1,0:T(8,128)(2,1)} %weights_ref.3) | copy-start | bytes 491524
  20.0 3.8 %copy-start.1 = (bf16[128,128]{1,0:T(8,128)(2,1)S(1)}, bf16[128,128]{1,0:T(8,128)(2,1)}, u32[]{:S(2)}) copy-start(bf16[128,128]{1,0:T(8,128)(2,1)} %out_weight_ref.1) | copy-start | bytes 98308
  20.0 7.2 %collective-permute-start.6 = (bf16[16,16,128]{2,1,0:T(8,128)(2,1)S(1)}, bf16[16,16,128]{2,1,0:T(8,128)(2,1)S(1)}, u32[]{:S(2)}, u32[]{:S(2)}) collective-permute-start(bf16[16,16,128]{2,1,0:T(8,128)(2,1)S(1)} %get-tuple-element.28.refs_0_), channel_id=1, source_target_pairs={{0,8},{4,12},{8,0},{12,4},{1,9},{5,13},{9,1},{13,5},{2,10},{6,14},... | collective-permute-start | bytes 196616 | tf_op jit(solution)/shard_map/ppermute | solution.py:256
  22.4 6.2 %collective-permute-start.7 = (bf16[16,16,128]{2,1,0:T(8,128)(2,1)S(1)}, bf16[16,16,128]{2,1,0:T(8,128)(2,1)S(1)}, u32[]{:S(2)}, u32[]{:S(2)}) collective-permute-start(bf16[16,16,128]{2,1,0:T(8,128)(2,1)S(1)} %get-tuple-element.28.refs_0_), channel_id=1, source_target_pairs={{0,12},{4,8},{8,4},{12,0},{1,13},{5,9},{9,5},{13,1},{2,14},{6,10},... | collective-permute-start | bytes 196616 | tf_op jit(solution)/shard_map/ppermute | solution.py:256
  23.2 5.5 %collective-permute-start.8 = (bf16[16,16,128]{2,1,0:T(8,128)(2,1)S(1)}, bf16[16,16,128]{2,1,0:T(8,128)(2,1)S(1)}, u32[]{:S(2)}, u32[]{:S(2)}) collective-permute-start(bf16[16,16,128]{2,1,0:T(8,128)(2,1)S(1)} %get-tuple-element.28.refs_0_), channel_id=1, source_target_pairs={{0,4},{4,0},{8,12},{12,8},{1,5},{5,1},{9,13},{13,9},{2,6},{6,2},{1... | collective-permute-start | bytes 196616 | tf_op jit(solution)/shard_map/ppermute | solution.py:256
  29.0 4.3 %collective-permute-start.9 = (bf16[16,16,128]{2,1,0:T(8,128)(2,1)S(1)}, bf16[16,16,128]{2,1,0:T(8,128)(2,1)S(1)}, u32[]{:S(2)}, u32[]{:S(2)}) collective-permute-start(bf16[16,16,128]{2,1,0:T(8,128)(2,1)S(1)} %shard_map.90), channel_id=1, source_target_pairs={{0,2},{1,3},{2,0},{3,1},{4,6},{5,7},{6,4},{7,5},{8,10},{9,11},{10,... | collective-permute-start | bytes 196616 | tf_op jit(solution)/shard_map/ppermute | solution.py:256
  31.2 3.8 %collective-permute-start.10 = (bf16[16,16,128]{2,1,0:T(8,128)(2,1)S(1)}, bf16[16,16,128]{2,1,0:T(8,128)(2,1)S(1)}, u32[]{:S(2)}, u32[]{:S(2)}) collective-permute-start(bf16[16,16,128]{2,1,0:T(8,128)(2,1)S(1)} %shard_map.91), channel_id=1, source_target_pairs={{0,3},{1,2},{2,1},{3,0},{4,7},{5,6},{6,5},{7,4},{8,11},{9,10},{10,... | collective-permute-start | bytes 196616 | tf_op jit(solution)/shard_map/ppermute | solution.py:256
  31.2 3.7 %collective-permute-start.11 = (bf16[16,16,128]{2,1,0:T(8,128)(2,1)S(1)}, bf16[16,16,128]{2,1,0:T(8,128)(2,1)S(1)}, u32[]{:S(2)}, u32[]{:S(2)}) collective-permute-start(bf16[16,16,128]{2,1,0:T(8,128)(2,1)S(1)} %shard_map.92), channel_id=1, source_target_pairs={{0,1},{1,0},{2,3},{3,2},{4,5},{5,4},{6,7},{7,6},{8,9},{9,8},{10,11... | collective-permute-start | bytes 196616 | tf_op jit(solution)/shard_map/ppermute | solution.py:256

commit v7 on v6

--- a/solution.py
+++ b/solution.py
@@ -77,10 +77,9 @@
     copies[0].wait()
     normed, _ = normalize(acts_ref[...].astype(f32).reshape(size * size, channels))
     normed = normed.astype(bf16)
-    copies[2].wait()
-    keep = keep_rows(mask_ref, crop_ref, channels)
-    copies[1].wait()
-    left, _, _ = gated(dot(normed, weights_ref[...]), 0, keep)
+    for copy in copies[1:]:
+        copy.wait()
+    left, _, _ = gated(dot(normed, weights_ref[...]), 0, keep_rows(mask_ref, crop_ref, channels))
     left_ref[...] = left.reshape(size, size, channels)
 
 
@@ -161,10 +160,11 @@
         grad_ref[i] = normalize_back(tri_normed, scale, upstream_ref[here, :]).astype(bf16)
 
 
-def left_terms_kernel(step, panel, right, out):
-    size = out.shape[0]
-    start = (lax.axis_index("col") ^ step) * (size * size)
-    weighted_sums(right, 0, [panel[pl.ds(start + j, size, stride=size), :] for j in range(size)], out)
+def left_terms_kernel(steps, panel, right, *outs):
+    size = right.shape[0]
+    for step, out in zip(steps, outs):
+        start = (lax.axis_index("col") ^ step) * (size * size)
+        weighted_sums(right, 0, [panel[pl.ds(start + j, size, stride=size), :] for j in range(size)], out)
 
 
 def right_grad_kernel(steps, panel, *refs):
@@ -200,24 +200,21 @@
     normed_grad_ref[...] = dot_t(out_gate_grad, weights_ref[:, 4 * channels :])
 
 
-def back_kernel(base, tile_ref, normed_ref, scale_ref, factor_ref, share_ref, weights_ref, out, done, sems):
-    size, _, channels = done.shape
-    half = size // 2
-    copies = []
-    for part in range(2):
-        tiles, rows = pl.ds(part * half, half), pl.ds(part * half * size, half * size)
-        left = (base[tiles] + tile_ref[tiles].astype(f32)).reshape(half * size, channels)
-        grads = jnp.concatenate([(left * factor_ref[block, rows]).astype(bf16) for block in (0, 1)], axis=1)
-        normed_grad = share_ref[rows, :] + dot_t(grads, weights_ref[:, : 2 * channels])
-        back = normalize_back(normed_ref[rows, :], scale_ref[rows, :], normed_grad)
-        done[tiles] = back.astype(bf16).reshape(half, size, channels)
-        copies.append(pltpu.make_async_copy(done.at[tiles], out.at[tiles], sems.at[part]))
-        copies[-1].start()
-    for copy in copies:
-        copy.wait()
-
-
-def call(kernel, outs, *args, scratch=(), flops=0, smem=(), hbm=(), out_space=pltpu.VMEM):
+def back_kernel(base, *refs):
+    *tiles, normed_ref, scale_ref, factor_ref, share_ref, weights_ref, out = refs
+    size, _, channels = out.shape
+    pairs = size * size
+    left = base[...]
+    for ref in tiles:
+        left = left + ref[...].astype(f32)
+    left = left.reshape(pairs, channels)
+    grads = jnp.concatenate([(left * factor_ref[block]).astype(bf16) for block in (0, 1)], axis=1)
+    normed_grad = share_ref[...] + dot_t(grads, weights_ref[:, : 2 * channels])
+    back = normalize_back(normed_ref[...], scale_ref[...], normed_grad)
+    out[...] = back.astype(bf16).reshape(size, size, channels)
+
+
+def call(kernel, outs, *args, scratch=(), flops=0, smem=(), hbm=()):
     spec = pl.BlockSpec(memory_space=pltpu.VMEM)
     total = sum(a.size * a.dtype.itemsize for a in (*args, *outs))
     specs = [spec] * len(args)
@@ -231,7 +228,7 @@
         kernel,
         out_shape=tuple(outs),
         in_specs=specs,
-        out_specs=(pl.BlockSpec(memory_space=out_space),) * len(outs),
+        out_specs=(spec,) * len(outs),
         scratch_shapes=scratch,
         compiler_params=pltpu.CompilerParams(vmem_limit_bytes=24 * 2**20),
         cost_estimate=pl.CostEstimate(flops=flops, bytes_accessed=total if flops else 0, transcendentals=0),
@@ -250,12 +247,13 @@
     work = 2 * size * pairs * channels
     wait = 2**31
     steps = [step for bit in range(n.bit_length() - 2, -1, -1) for step in range(2**bit, 2 ** (bit + 1))]
+    row_steps = [n // 2] + [step for step in range(1, n) if step != n // 2]
 
 
     def swap(values, axis, step):
         return lax.ppermute(values, axis, [(a, a ^ step) for a in range(n)])
 
-    def gather(values, axis):
+    def gather(values, axis, steps):
         return [values] + [swap(values, axis, step) for step in steps]
 
     (left,) = call(
@@ -268,7 +266,7 @@
             pltpu.SemaphoreType.DMA((3,)),
         ],
     )
-    lefts = gather(left, "col")
+    lefts = gather(left, "col", steps)
     right, normed, scale, factors, out_open, gate_factor, upstream = call(
         factors_kernel,
         (wide, flat, flat, jax.ShapeDtypeStruct((4, pairs, channels), f32), flat, flat, flat),
@@ -285,19 +283,19 @@
     )
     (left_panel,) = call(functools.partial(panel_kernel, "col", [0] + steps), (panel,), *lefts)
     parts = {}
-    for step in [0] + steps:
+    for step in [0] + row_steps:
         (parts[step],) = call(
             functools.partial(partial_kernel, (step,)), (tile if step else wide,), left_panel, right, flops=work,
         )
     total = parts[0]
-    for step in steps:
+    for step in row_steps:
         part = swap(parts[step], "row", step)
-        if step != steps[-1]:
+        if step != row_steps[-1]:
             (total,) = call(add_kernel, (wide,), total, part, flops=wait)
     tri_normed, tri_grad = call(
         triangle_kernel, (flat, tile), total, part, upstream, flops=20 * pairs * channels,
     )
-    grads = gather(tri_grad, "row")
+    grads = gather(tri_grad, "row", row_steps)
     update, partial = call(
         update_kernel, (tile, flat), tri_normed, out_open, gate_factor, in_weights, out_weight,
         flops=4 * pairs * channels * channels,
@@ -305,30 +303,32 @@
     (right_grad,) = call(functools.partial(right_grad_kernel, [0]), (wide,), left_panel, tri_grad)
     right, partial, right_grad = lax.optimization_barrier((right, partial, right_grad))
     (grad_panel,) = call(
-        functools.partial(panel_kernel, "row", [0] + steps), (jax.ShapeDtypeStruct((n * pairs, channels), f32),), *grads
+        functools.partial(panel_kernel, "row", [0] + row_steps), (jax.ShapeDtypeStruct((n * pairs, channels), f32),), *grads
     )
     terms = {}
-    for step in steps + [0]:
+    for group in (steps, [0]):
         if terms:
             right, terms[last] = lax.optimization_barrier((right, terms[last]))
-        last = step
-        (terms[step],) = call(
-            functools.partial(left_terms_kernel, step), (tile if step else wide,), grad_panel, right,
-            flops=work,
+        last = group[-1]
+        outs = call(
+            functools.partial(left_terms_kernel, group), (wide if group == [0] else tile,) * len(group),
+            grad_panel, right, flops=work,
         )
-    total = terms[0]
+        terms.update(zip(group, outs))
+    total, last = terms[0], []
     for step in steps:
         term = swap(terms[step], "col", step)
-        if step != steps[-1]:
+        if step == steps[-1]:
+            last.append(term)
+        else:
             (total,) = call(add_kernel, (wide,), total, term, flops=wait)
     (share,) = call(
-        functools.partial(right_back_kernel, steps), (flat,),
+        functools.partial(right_back_kernel, row_steps), (flat,),
         left_panel, *grads[1:], right_grad, factors, in_weights, partial,
         scratch=[pltpu.VMEM(wide.shape, f32)],
     )
     (pair_grad,) = call(
-        back_kernel, (tile,), total, term, normed, scale, factors, share, in_weights,
-        scratch=[pltpu.VMEM(tile.shape, bf16), pltpu.SemaphoreType.DMA((2,))], out_space=pl.ANY,
+        back_kernel, (tile,), total, *last[::-1], normed, scale, factors, share, in_weights,
         flops=2 * pairs * channels * 2 * channels,
     )
     return (update, pair_grad)

time: 36.1 us -> 36.1 us (level)
  starting transfers between devices: 13.5 us -> 14.4 us
  waiting for transfers between devices: 13.2 us -> 12.6 us
    ppermute x12, starting transfers between devices: 13.5 us -> 14.4 us  [swap(): return lax.ppermute(values, axis, [(a, a ^ step) for a in range(n)])]
    ppermute x12, waiting for transfers between devices: 13.2 us -> 12.6 us  [swap(): return lax.ppermute(values, axis, [(a, a ^ step) for a in range(n)])]
    pallas_call x21 -> x19, Pallas kernels: 7.71 us -> 7.48 us  [call(): pl.pallas_call(kernel, out_shape=tuple(outs), in_specs=specs, out_specs=(...]
  transfers between devices with their start and end apart: 12 -> 12, of which waited for: 10 -> 9; matrix products, arithmetic and copies ran while one was open for 0% -> 0% of each run, Pallas kernels for 12% -> 11%
where the time goes in v7:
time: 36.1 us; the launch traced here: 35.9 us
  starting transfers between devices  14.4 us (40%)
  waiting for transfers between devices  12.6 us (35%)
  Pallas kernels  7.48 us (21%)
  between operations  1.41 us (4%)
    ppermute x12, starting transfers between devices, swap(): return lax.ppermute(values, axis, [(a, a ^ step) for a in range(n)])  14.4 us
    ppermute x12, waiting for transfers between devices, swap(): return lax.ppermute(values, axis, [(a, a ^ step) for a in range(n)])  12.6 us
    pallas_call x19, Pallas kernels, call(): pl.pallas_call(kernel, out_shape=tuple(outs), in_specs=specs, out_specs=(...  7.48 us
  transfers between devices with their start and end apart: 12, of which 9 were waited for; matrix products, arithmetic and copies ran while one was open for 0% of the time, Pallas kernels for 11%

profile of v7, /device:TPU:0, one launch (start us, length us, event | category | flops | bytes accessed | tf_op | source)
XLA Modules:
  0.0 35.9 jit_solution(357853390288462324)
XLA Ops:
  1.3 1.4 %shard_map.77.refs_0_ = bf16[16,16,128]{2,1,0:T(8,128)(2,1)S(1)} custom-call(bf16[16,16,128]{2,1,0:T(8,128)(2,1)} %acts_in.3, s32[16,16]{1,0:T(8,128)} %mask_in.3, s32[1]{0:T(128)S(6)} %copy.8.crop_ref, bf16[128,640]{1,0:T(8,128)(2,1)} %refs_5_.3), custom_call_target="tpu_custom_call" | custom-call | flops 16777216 | bytes 295940 | tf_op jit(solution)/shard_map/pallas_call | solution.py:227
  2.6 3.0 %collective-permute-start = (bf16[16,16,128]{2,1,0:T(8,128)(2,1)S(1)}, bf16[16,16,128]{2,1,0:T(8,128)(2,1)S(1)}, u32[]{:S(2)}, u32[]{:S(2)}) collective-permute-start(bf16[16,16,128]{2,1,0:T(8,128)(2,1)S(1)} %shard_map.77.refs_0_), channel_id=1, source_target_pairs={{0,2},{1,3},{2,0},{3,1},{4,6},{5,7},{6,4},{7,5},{8,10},{9,11},{10,... | collective-permute-start | bytes 196616 | tf_op jit(solution)/shard_map/ppermute | solution.py:254
  5.8 1.5 %shard_map.79 = (f32[16,16,128]{2,1,0:T(8,128)S(1)}, f32[256,128]{1,0:T(8,128)S(1)}, f32[256,128]{1,0:T(8,128)S(1)}, f32[4,256,128]{2,1,0:T(8,128)S(1)}, f32[256...) custom-call(bf16[16,16,128]{2,1,0:T(8,128)(2,1)} %acts_in.3, s32[16,16]{1,0:T(8,128)} %mask_in.3, ...), custom_call_target="tpu_custom_call" | custom-call | flops 50331648 | bytes 1639428 | tf_op jit(solution)/shard_map/pallas_call | solution.py:227
  7.3 0.6 %collective-permute-done.refs_1_ = bf16[16,16,128]{2,1,0:T(8,128)(2,1)S(1)} collective-permute-done((bf16[16,16,128]{2,1,0:T(8,128)(2,1)S(1)}, bf16[16,16,128]{2,1,0:T(8,128)(2,1)S(1)}, u32[]{:S(2)}, u32[]{:S(2)}) %collective-permute-start) | collective-permute-done | bytes 65568 | tf_op jit(solution)/shard_map/ppermute | solution.py:254
  7.9 1.9 %collective-permute-done.1.refs_2_ = bf16[16,16,128]{2,1,0:T(8,128)(2,1)S(1)} collective-permute-done((bf16[16,16,128]{2,1,0:T(8,128)(2,1)S(1)}, bf16[16,16,128]{2,1,0:T(8,128)(2,1)S(1)}, u32[]{:S(2)}, u32[]{:S(2)}) %collective-permute-start.1) | collective-permute-done | bytes 65568 | tf_op jit(solution)/shard_map/ppermute | solution.py:254
  10.0 2.7 %collective-permute-start.3 = (bf16[16,16,128]{2,1,0:T(8,128)(2,1)S(1)}, bf16[16,16,128]{2,1,0:T(8,128)(2,1)S(1)}, u32[]{:S(2)}, u32[]{:S(2)}) collective-permute-start(bf16[16,16,128]{2,1,0:T(8,128)(2,1)S(1)} %shard_map.81), channel_id=1, source_target_pairs={{0,8},{4,12},{8,0},{12,4},{1,9},{5,13},{9,1},{13,5},{2,10},{6,14},... | collective-permute-start | bytes 196616 | tf_op jit(solution)/shard_map/ppermute | solution.py:254
  12.9 1.6 %collective-permute-start.4 = (bf16[16,16,128]{2,1,0:T(8,128)(2,1)S(1)}, bf16[16,16,128]{2,1,0:T(8,128)(2,1)S(1)}, u32[]{:S(2)}, u32[]{:S(2)}) collective-permute-start(bf16[16,16,128]{2,1,0:T(8,128)(2,1)S(1)} %shard_map.83), channel_id=1, source_target_pairs={{0,4},{4,0},{8,12},{12,8},{1,5},{5,1},{9,13},{13,9},{2,6},{6,2},{1... | collective-permute-start | bytes 196616 | tf_op jit(solution)/shard_map/ppermute | solution.py:254
  15.2 1.1 %collective-permute-done.3.tile_ref = bf16[16,16,128]{2,1,0:T(8,128)(2,1)S(1)} collective-permute-done((bf16[16,16,128]{2,1,0:T(8,128)(2,1)S(1)}, bf16[16,16,128]{2,1,0:T(8,128)(2,1)S(1)}, u32[]{:S(2)}, u32[]{:S(2)}) %collective-permute-start.3) | collective-permute-done | bytes 65568 | tf_op jit(solution)/shard_map/ppermute | solution.py:254
  16.3 0.9 %collective-permute-done.4.tile_ref = bf16[16,16,128]{2,1,0:T(8,128)(2,1)S(1)} collective-permute-done((bf16[16,16,128]{2,1,0:T(8,128)(2,1)S(1)}, bf16[16,16,128]{2,1,0:T(8,128)(2,1)S(1)}, u32[]{:S(2)}, u32[]{:S(2)}) %collective-permute-start.4) | collective-permute-done | bytes 65568 | tf_op jit(solution)/shard_map/ppermute | solution.py:254
  17.3 3.6 %collective-permute-done.5.tile_ref = bf16[16,16,128]{2,1,0:T(8,128)(2,1)S(1)} collective-permute-done((bf16[16,16,128]{2,1,0:T(8,128)(2,1)S(1)}, bf16[16,16,128]{2,1,0:T(8,128)(2,1)S(1)}, u32[]{:S(2)}, u32[]{:S(2)}) %collective-permute-start.5) | collective-permute-done | bytes 65568 | tf_op jit(solution)/shard_map/ppermute | solution.py:254
  20.9 0.3 shard_map.86
  21.2 0.9 %collective-permute-start.6 = (bf16[16,16,128]{2,1,0:T(8,128)(2,1)S(1)}, bf16[16,16,128]{2,1,0:T(8,128)(2,1)S(1)}, u32[]{:S(2)}, u32[]{:S(2)}) collective-permute-start(bf16[16,16,128]{2,1,0:T(8,128)(2,1)S(1)} %get-tuple-element.27.refs_0_), channel_id=1, source_target_pairs={{0,8},{4,12},{8,0},{12,4},{1,9},{5,13},{9,1},{13,5},{2,10},{6,14},... | collective-permute-start | bytes 196616 | tf_op jit(solution)/shard_map/ppermute | solution.py:254
  22.1 0.5 %collective-permute-start.7 = (bf16[16,16,128]{2,1,0:T(8,128)(2,1)S(1)}, bf16[16,16,128]{2,1,0:T(8,128)(2,1)S(1)}, u32[]{:S(2)}, u32[]{:S(2)}) collective-permute-start(bf16[16,16,128]{2,1,0:T(8,128)(2,1)S(1)} %get-tuple-element.27.refs_0_), channel_id=1, source_target_pairs={{0,4},{4,0},{8,12},{12,8},{1,5},{5,1},{9,13},{13,9},{2,6},{6,2},{1... | collective-permute-start | bytes 196616 | tf_op jit(solution)/shard_map/ppermute | solution.py:254
  22.6 3.0 %collective-permute-start.8 = (bf16[16,16,128]{2,1,0:T(8,128)(2,1)S(1)}, bf16[16,16,128]{2,1,0:T(8,128)(2,1)S(1)}, u32[]{:S(2)}, u32[]{:S(2)}) collective-permute-start(bf16[16,16,128]{2,1,0:T(8,128)(2,1)S(1)} %get-tuple-element.27.refs_0_), channel_id=1, source_target_pairs={{0,12},{4,8},{8,4},{12,0},{1,13},{5,9},{9,5},{13,1},{2,14},{6,10},... | collective-permute-start | bytes 196616 | tf_op jit(solution)/shard_map/ppermute | solution.py:254
  25.8 0.8 %shard_map.87 = (bf16[16,16,128]{2,1,0:T(8,128)(2,1)}, f32[256,128]{1,0:T(8,128)S(1)}) custom-call(f32[256,128]{1,0:T(8,128)S(1)} %get-tuple-element.23.tri_normed_ref, f32[256,128]{1,0:T(8,128)S(1)} %get-tuple-element.24.open_ref, f32[256,128]{1,0:T(8,128)S(1)} %get-tuple-element.25.gate_factor_ref, bf16[128,640]{1,0:T(8,128)(2,1)S(1)} %copy-done, ...), custom_call_target="tpu_custom_call" | custom-call | flops 16777216 | bytes 786432 | tf_op jit(solution)/shard_map/pallas_call | solution.py:227
  26.6 1.1 %collective-permute-done.6.refs_1_.refs_0_ = bf16[16,16,128]{2,1,0:T(8,128)(2,1)S(1)} collective-permute-done((bf16[16,16,128]{2,1,0:T(8,128)(2,1)S(1)}, bf16[16,16,128]{2,1,0:T(8,128)(2,1)S(1)}, u32[]{:S(2)}, u32[]{:S(2)}) %collective-permute-start.6) | collective-permute-done | bytes 65568 | tf_op jit(solution)/shard_map/ppermute | solution.py:254
  27.8 1.0 %collective-permute-done.8.refs_3_.refs_2_ = bf16[16,16,128]{2,1,0:T(8,128)(2,1)S(1)} collective-permute-done((bf16[16,16,128]{2,1,0:T(8,128)(2,1)S(1)}, bf16[16,16,128]{2,1,0:T(8,128)(2,1)S(1)}, u32[]{:S(2)}, u32[]{:S(2)}) %collective-permute-start.8) | collective-permute-done | bytes 65568 | tf_op jit(solution)/shard_map/ppermute | solution.py:254
  28.9 0.6 %shard_map.90 = (bf16[16,16,128]{2,1,0:T(8,128)(2,1)S(1)}, bf16[16,16,128]{2,1,0:T(8,128)(2,1)S(1)}, bf16[16,16,128]{2,1,0:T(8,128)(2,1)S(1)}) custom-call(f32[1024,128]{1,0:T(8,128)S(1)} %shard_map.88.panel, f32[16,16,128]{2,1,0:T(8,128)S(1)} %get-tuple-element.31.right_ref.right), custom_call_target="tpu_custom_call" | custom-call | flops 1048576 | bytes 851968 | tf_op jit(solution)/shard_map/pallas_call | solution.py:227
  29.5 1.1 %collective-permute-start.9 = (bf16[16,16,128]{2,1,0:T(8,128)(2,1)S(1)}, bf16[16,16,128]{2,1,0:T(8,128)(2,1)S(1)}, u32[]{:S(2)}, u32[]{:S(2)}) collective-permute-start(bf16[16,16,128]{2,1,0:T(8,128)(2,1)S(1)} %get-tuple-element.32), channel_id=1, source_target_pairs={{0,2},{1,3},{2,0},{3,1},{4,6},{5,7},{6,4},{7,5},{8,10},{9,11},{10,... | collective-permute-start | bytes 196616 | tf_op jit(solution)/shard_map/ppermute | solution.py:254
  30.6 1.1 %collective-permute-start.11 = (bf16[16,16,128]{2,1,0:T(8,128)(2,1)S(1)}, bf16[16,16,128]{2,1,0:T(8,128)(2,1)S(1)}, u32[]{:S(2)}, u32[]{:S(2)}) collective-permute-start(bf16[16,16,128]{2,1,0:T(8,128)(2,1)S(1)} %get-tuple-element.34), channel_id=1, source_target_pairs={{0,1},{1,0},{2,3},{3,2},{4,5},{5,4},{6,7},{7,6},{8,9},{9,8},{10,11... | collective-permute-start | bytes 196616 | tf_op jit(solution)/shard_map/ppermute | solution.py:254
  31.7 0.7 %shard_map.94.refs_4_ = f32[256,128]{1,0:T(8,128)S(1)} custom-call(f32[64,16,128]{2,1,0:T(8,128)S(1)} %shard_map.78.panel, bf16[16,16,128]{2,1,0:T(8,128)(2,1)S(1)} %collective-permute-done.6.refs_1_.refs_0_, bf16[16,16,128]{2,1,0:T(8,128)(2,1)S(1)} %collective-permute-done.7.refs_2_.refs_1_, ...), custom_call_target="tpu_custom_call" | custom-call | tf_op jit(solution)/shard_map/pallas_call | solution.py:227
  32.6 1.5 %collective-permute-done.9.tile_ref = bf16[16,16,128]{2,1,0:T(8,128)(2,1)S(1)} collective-permute-done((bf16[16,16,128]{2,1,0:T(8,128)(2,1)S(1)}, bf16[16,16,128]{2,1,0:T(8,128)(2,1)S(1)}, u32[]{:S(2)}, u32[]{:S(2)}) %collective-permute-start.9) | collective-permute-done | bytes 65568 | tf_op jit(solution)/shard_map/ppermute | solution.py:254
  34.1 0.8 %collective-permute-done.10.tile_ref = bf16[16,16,128]{2,1,0:T(8,128)(2,1)S(1)} collective-permute-done((bf16[16,16,128]{2,1,0:T(8,128)(2,1)S(1)}, bf16[16,16,128]{2,1,0:T(8,128)(2,1)S(1)}, u32[]{:S(2)}, u32[]{:S(2)}) %collective-permute-start.10) | collective-permute-done | bytes 65568 | tf_op jit(solution)/shard_map/ppermute | solution.py:254
  34.9 0.9 %shard_map.95 = bf16[16,16,128]{2,1,0:T(8,128)(2,1)} custom-call(f32[16,16,128]{2,1,0:T(8,128)S(1)} %shard_map.93.base, bf16[16,16,128]{2,1,0:T(8,128)(2,1)S(1)} %collective-permute-done.11.refs_0_, f32[256,128]{1,0:T(8,128)S(1)} %get-tuple-element.35.refs_1_, f32[256,128]{1,0:T(8,128)S(1)} %get-tuple-element.36.refs_2_, ...), custom_call_target="tpu_custom_call" | custom-call | flops 16777216 | bytes 1343488 | tf_op jit(solution)/shard_map/pallas_call | solution.py:227
  (23 shorter events, 1.8 us)
Async XLA Ops:
  2.6 5.2 %collective-permute-start = (bf16[16,16,128]{2,1,0:T(8,128)(2,1)S(1)}, bf16[16,16,128]{2,1,0:T(8,128)(2,1)S(1)}, u32[]{:S(2)}, u32[]{:S(2)}) collective-permute-start(bf16[16,16,128]{2,1,0:T(8,128)(2,1)S(1)} %shard_map.77.refs_0_), channel_id=1, source_target_pairs={{0,2},{1,3},{2,0},{3,1},{4,6},{5,7},{6,4},{7,5},{8,10},{9,11},{10,... | collective-permute-start | bytes 196616 | tf_op jit(solution)/shard_map/ppermute | solution.py:254
  5.6 4.1 %collective-permute-start.1 = (bf16[16,16,128]{2,1,0:T(8,128)(2,1)S(1)}, bf16[16,16,128]{2,1,0:T(8,128)(2,1)S(1)}, u32[]{:S(2)}, u32[]{:S(2)}) collective-permute-start(bf16[16,16,128]{2,1,0:T(8,128)(2,1)S(1)} %shard_map.77.refs_0_), channel_id=1, source_target_pairs={{0,3},{1,2},{2,1},{3,0},{4,7},{5,6},{6,5},{7,4},{8,11},{9,10},{10,... | collective-permute-start | bytes 196616 | tf_op jit(solution)/shard_map/ppermute | solution.py:254
  5.7 4.1 %collective-permute-start.2 = (bf16[16,16,128]{2,1,0:T(8,128)(2,1)S(1)}, bf16[16,16,128]{2,1,0:T(8,128)(2,1)S(1)}, u32[]{:S(2)}, u32[]{:S(2)}) collective-permute-start(bf16[16,16,128]{2,1,0:T(8,128)(2,1)S(1)} %shard_map.77.refs_0_), channel_id=1, source_target_pairs={{0,1},{1,0},{2,3},{3,2},{4,5},{5,4},{6,7},{7,6},{8,9},{9,8},{10,11... | collective-permute-start | bytes 196616 | tf_op jit(solution)/shard_map/ppermute | solution.py:254
  10.0 6.3 %collective-permute-start.3 = (bf16[16,16,128]{2,1,0:T(8,128)(2,1)S(1)}, bf16[16,16,128]{2,1,0:T(8,128)(2,1)S(1)}, u32[]{:S(2)}, u32[]{:S(2)}) collective-permute-start(bf16[16,16,128]{2,1,0:T(8,128)(2,1)S(1)} %shard_map.81), channel_id=1, source_target_pairs={{0,8},{4,12},{8,0},{12,4},{1,9},{5,13},{9,1},{13,5},{2,10},{6,14},... | collective-permute-start | bytes 196616 | tf_op jit(solution)/shard_map/ppermute | solution.py:254
  12.9 4.3 %collective-permute-start.4 = (bf16[16,16,128]{2,1,0:T(8,128)(2,1)S(1)}, bf16[16,16,128]{2,1,0:T(8,128)(2,1)S(1)}, u32[]{:S(2)}, u32[]{:S(2)}) collective-permute-start(bf16[16,16,128]{2,1,0:T(8,128)(2,1)S(1)} %shard_map.83), channel_id=1, source_target_pairs={{0,4},{4,0},{8,12},{12,8},{1,5},{5,1},{9,13},{13,9},{2,6},{6,2},{1... | collective-permute-start | bytes 196616 | tf_op jit(solution)/shard_map/ppermute | solution.py:254
  14.7 6.1 %collective-permute-start.5 = (bf16[16,16,128]{2,1,0:T(8,128)(2,1)S(1)}, bf16[16,16,128]{2,1,0:T(8,128)(2,1)S(1)}, u32[]{:S(2)}, u32[]{:S(2)}) collective-permute-start(bf16[16,16,128]{2,1,0:T(8,128)(2,1)S(1)} %shard_map.85), channel_id=1, source_target_pairs={{0,12},{4,8},{8,4},{12,0},{1,13},{5,9},{9,5},{13,1},{2,14},{6,10},... | collective-permute-start | bytes 196616 | tf_op jit(solution)/shard_map/ppermute | solution.py:254
  21.2 4.7 %copy-start = (bf16[128,640]{1,0:T(8,128)(2,1)S(1)}, bf16[128,640]{1,0:T(8,128)(2,1)}, u32[]{:S(2)}) copy-start(bf16[128,640]{1,0:T(8,128)(2,1)} %refs_5_.3) | copy-start | bytes 491524
  21.2 4.7 %copy-start.1 = (bf16[128,128]{1,0:T(8,128)(2,1)S(1)}, bf16[128,128]{1,0:T(8,128)(2,1)}, u32[]{:S(2)}) copy-start(bf16[128,128]{1,0:T(8,128)(2,1)} %out_weight_ref.1) | copy-start | bytes 98308
  21.2 6.6 %collective-permute-start.6 = (bf16[16,16,128]{2,1,0:T(8,128)(2,1)S(1)}, bf16[16,16,128]{2,1,0:T(8,128)(2,1)S(1)}, u32[]{:S(2)}, u32[]{:S(2)}) collective-permute-start(bf16[16,16,128]{2,1,0:T(8,128)(2,1)S(1)} %get-tuple-element.27.refs_0_), channel_id=1, source_target_pairs={{0,8},{4,12},{8,0},{12,4},{1,9},{5,13},{9,1},{13,5},{2,10},{6,14},... | collective-permute-start | bytes 196616 | tf_op jit(solution)/shard_map/ppermute | solution.py:254
  22.1 5.7 %collective-permute-start.7 = (bf16[16,16,128]{2,1,0:T(8,128)(2,1)S(1)}, bf16[16,16,128]{2,1,0:T(8,128)(2,1)S(1)}, u32[]{:S(2)}, u32[]{:S(2)}) collective-permute-start(bf16[16,16,128]{2,1,0:T(8,128)(2,1)S(1)} %get-tuple-element.27.refs_0_), channel_id=1, source_target_pairs={{0,4},{4,0},{8,12},{12,8},{1,5},{5,1},{9,13},{13,9},{2,6},{6,2},{1... | collective-permute-start | bytes 196616 | tf_op jit(solution)/shard_map/ppermute | solution.py:254
  22.6 6.2 %collective-permute-start.8 = (bf16[16,16,128]{2,1,0:T(8,128)(2,1)S(1)}, bf16[16,16,128]{2,1,0:T(8,128)(2,1)S(1)}, u32[]{:S(2)}, u32[]{:S(2)}) collective-permute-start(bf16[16,16,128]{2,1,0:T(8,128)(2,1)S(1)} %get-tuple-element.27.refs_0_), channel_id=1, source_target_pairs={{0,12},{4,8},{8,4},{12,0},{1,13},{5,9},{9,5},{13,1},{2,14},{6,10},... | collective-permute-start | bytes 196616 | tf_op jit(solution)/shard_map/ppermute | solution.py:254
  29.5 4.6 %collective-permute-start.9 = (bf16[16,16,128]{2,1,0:T(8,128)(2,1)S(1)}, bf16[16,16,128]{2,1,0:T(8,128)(2,1)S(1)}, u32[]{:S(2)}, u32[]{:S(2)}) collective-permute-start(bf16[16,16,128]{2,1,0:T(8,128)(2,1)S(1)} %get-tuple-element.32), channel_id=1, source_target_pairs={{0,2},{1,3},{2,0},{3,1},{4,6},{5,7},{6,4},{7,5},{8,10},{9,11},{10,... | collective-permute-start | bytes 196616 | tf_op jit(solution)/shard_map/ppermute | solution.py:254
  30.6 4.3 %collective-permute-start.10 = (bf16[16,16,128]{2,1,0:T(8,128)(2,1)S(1)}, bf16[16,16,128]{2,1,0:T(8,128)(2,1)S(1)}, u32[]{:S(2)}, u32[]{:S(2)}) collective-permute-start(bf16[16,16,128]{2,1,0:T(8,128)(2,1)S(1)} %get-tuple-element.33), channel_id=1, source_target_pairs={{0,3},{1,2},{2,1},{3,0},{4,7},{5,6},{6,5},{7,4},{8,11},{9,10},{10,... | collective-permute-start | bytes 196616 | tf_op jit(solution)/shard_map/ppermute | solution.py:254
  30.6 4.3 %collective-permute-start.11 = (bf16[16,16,128]{2,1,0:T(8,128)(2,1)S(1)}, bf16[16,16,128]{2,1,0:T(8,128)(2,1)S(1)}, u32[]{:S(2)}, u32[]{:S(2)}) collective-permute-start(bf16[16,16,128]{2,1,0:T(8,128)(2,1)S(1)} %get-tuple-element.34), channel_id=1, source_target_pairs={{0,1},{1,0},{2,3},{3,2},{4,5},{5,4},{6,7},{7,6},{8,9},{9,8},{10,11... | collective-permute-start | bytes 196616 | tf_op jit(solution)/shard_map/ppermute | solution.py:254

commit v8 on v7

--- a/solution.py
+++ b/solution.py
@@ -41,18 +41,20 @@
     return lax.dot_general(a, b, (((1,), (1,)), ((), ())), preferred_element_type=f32)
 
 
-def keep_rows(mask_ref, crop_ref, channels):
-    size = mask_ref.shape[0]
-    rows = lax.axis_index("row") * size + lax.broadcasted_iota(jnp.int32, (size, size), 0)
-    cols = lax.axis_index("col") * size + lax.broadcasted_iota(jnp.int32, (size, size), 1)
-    live = jnp.where(jnp.maximum(rows, cols) < crop_ref[0], 1.0, 0.0)
-    keep = (mask_ref[...].astype(f32) * live).astype(bf16)
+def live_pairs(crop_ref, row, col, shape):
+    rows = row * shape[0] + lax.broadcasted_iota(jnp.int32, shape, 0)
+    cols = col * shape[1] + lax.broadcasted_iota(jnp.int32, shape, 1)
+    return jnp.where(jnp.maximum(rows, cols) < crop_ref[0], 1.0, 0.0)
+
+
+def spread(mask, channels):
+    size = mask.shape[0]
     pair = lax.broadcasted_iota(jnp.int32, (size * size, size), 0)
     lane = lax.broadcasted_iota(jnp.int32, (size * size, size), 1)
     pick_row = jnp.where(pair // size == lane, 1.0, 0.0).astype(bf16)
     pick_col = jnp.where(pair % size == lane, 1.0, 0.0)
-    spread = (dot(pick_row, keep) * pick_col).astype(bf16)
-    return dot(spread, jnp.ones((size, channels), bf16))
+    picked = (dot(pick_row, mask.astype(bf16)) * pick_col).astype(bf16)
+    return dot(picked, jnp.ones((size, channels), bf16))
 
 
 def start_copies(sems, *pairs):
@@ -69,7 +71,7 @@
     return (opened * value * keep).astype(bf16), opened, value
 
 
-def left_kernel(acts_in, mask_in, crop_ref, weights_in, left_ref, acts_ref, mask_ref, weights_ref, sems):
+def left_kernel(acts_in, mask_in, weights_in, left_ref, acts_ref, mask_ref, weights_ref, sems):
     size, _, channels = acts_ref.shape
     copies = start_copies(
         sems, (acts_in, acts_ref), (weights_in.at[:, pl.ds(0, 2 * channels)], weights_ref), (mask_in, mask_ref),
@@ -79,7 +81,7 @@
     normed = normed.astype(bf16)
     for copy in copies[1:]:
         copy.wait()
-    left, _, _ = gated(dot(normed, weights_ref[...]), 0, keep_rows(mask_ref, crop_ref, channels))
+    left, _, _ = gated(dot(normed, weights_ref[...]), 0, spread(mask_ref[...].astype(f32), channels))
     left_ref[...] = left.reshape(size, size, channels)
 
 
@@ -101,7 +103,8 @@
     for copy in copies[1:]:
         copy.wait()
     projected = dot(normed.astype(bf16), weights_ref[...])
-    keep = keep_rows(mask_ref, crop_ref, channels)
+    live = live_pairs(crop_ref, lax.axis_index("row"), lax.axis_index("col"), (size, size))
+    keep = spread(mask_ref[...].astype(f32) * live, channels)
     for block in (0, 2):
         tile, opened, value = gated(projected, block, keep)
         factor_ref[block] = keep * opened
@@ -134,6 +137,15 @@
     for step, ref in zip(steps, refs):
         tile = ref[...].astype(f32)
         panel[pl.ds((here ^ step) * rows, rows)] = tile.reshape((rows,) + panel.shape[1:])
+
+
+def left_panel_kernel(steps, crop_ref, *refs):
+    row, col, panel = lax.axis_index("row"), lax.axis_index("col"), refs[-1]
+    size = refs[0].shape[0]
+    for step, ref in zip(steps, refs):
+        place = col ^ step
+        live = live_pairs(crop_ref, row, place, ref.shape)
+        panel[pl.ds(place * size, size)] = ref[...].astype(f32) * live
 
 
 def partial_kernel(steps, panel, right_ref, *outs):
@@ -257,8 +269,8 @@
         return [values] + [swap(values, axis, step) for step in steps]
 
     (left,) = call(
-        left_kernel, (tile,), pair_acts, pair_mask, crop_length, in_weights,
-        smem=(2,), hbm=(0, 1, 3), flops=2 * pairs * channels * 2 * channels,
+        left_kernel, (tile,), pair_acts, pair_mask, in_weights,
+        hbm=(0, 1, 2), flops=2 * pairs * channels * 2 * channels,
         scratch=[
             pltpu.VMEM(pair_acts.shape, bf16),
             pltpu.VMEM(pair_mask.shape, jnp.int32),
@@ -281,7 +293,9 @@
             pltpu.SemaphoreType.DMA((5,)),
         ],
     )
-    (left_panel,) = call(functools.partial(panel_kernel, "col", [0] + steps), (panel,), *lefts)
+    (left_panel,) = call(
+        functools.partial(left_panel_kernel, [0] + steps), (panel,), crop_length, *lefts, smem=(0,)
+    )
     parts = {}
     for step in [0] + row_steps:
         (parts[step],) = call(

time: 36.1 us -> 35.5 us (0.983)
  waiting for transfers between devices: 12.6 us -> 11.9 us
    ppermute x12, waiting for transfers between devices: 12.6 us -> 11.9 us  [swap(): return lax.ppermute(values, axis, [(a, a ^ step) for a in range(n)])]
  transfers between devices with their start and end apart: 12 -> 12, of which waited for: 9 -> 8; matrix products, arithmetic and copies ran while one was open for 0% -> 0% of each run, Pallas kernels for 11% -> 11%
where the time goes in v8:
time: 35.5 us; the launch traced here: 35.3 us
  starting transfers between devices  14.4 us (41%)
  waiting for transfers between devices  11.9 us (34%)
  Pallas kernels  7.57 us (21%)
  between operations  1.42 us (4%)
    ppermute x12, starting transfers between devices, swap(): return lax.ppermute(values, axis, [(a, a ^ step) for a in range(n)])  14.4 us
    ppermute x12, waiting for transfers between devices, swap(): return lax.ppermute(values, axis, [(a, a ^ step) for a in range(n)])  11.9 us
    pallas_call x19, Pallas kernels, call(): pl.pallas_call(kernel, out_shape=tuple(outs), in_specs=specs, out_specs=(...  7.57 us
  transfers between devices with their start and end apart: 12, of which 8 were waited for; matrix products, arithmetic and copies ran while one was open for 0% of the time, Pallas kernels for 11%

profile of v8, /device:TPU:0, one launch (start us, length us, event | category | flops | bytes accessed | tf_op | source)
XLA Modules:
  0.0 35.3 jit_solution(3935706751268238110)
XLA Ops:
  0.6 1.3 %shard_map.77.refs_0_ = bf16[16,16,128]{2,1,0:T(8,128)(2,1)S(1)} custom-call(bf16[16,16,128]{2,1,0:T(8,128)(2,1)} %acts_in.3, s32[16,16]{1,0:T(8,128)} %mask_in.3, bf16[128,640]{1,0:T(8,128)(2,1)} %refs_5_.3), custom_call_target="tpu_custom_call" | custom-call | flops 16777216 | bytes 295936 | tf_op jit(solution)/shard_map/pallas_call | solution.py:239
  2.0 3.0 %collective-permute-start = (bf16[16,16,128]{2,1,0:T(8,128)(2,1)S(1)}, bf16[16,16,128]{2,1,0:T(8,128)(2,1)S(1)}, u32[]{:S(2)}, u32[]{:S(2)}) collective-permute-start(bf16[16,16,128]{2,1,0:T(8,128)(2,1)S(1)} %shard_map.77.refs_0_), channel_id=1, source_target_pairs={{0,2},{1,3},{2,0},{3,1},{4,6},{5,7},{6,4},{7,5},{8,10},{9,11},{10,... | collective-permute-start | bytes 196616 | tf_op jit(solution)/shard_map/ppermute | solution.py:266
  5.8 1.5 %shard_map.79 = (f32[16,16,128]{2,1,0:T(8,128)S(1)}, f32[256,128]{1,0:T(8,128)S(1)}, f32[256,128]{1,0:T(8,128)S(1)}, f32[4,256,128]{2,1,0:T(8,128)S(1)}, f32[256...) custom-call(bf16[16,16,128]{2,1,0:T(8,128)(2,1)} %acts_in.3, s32[16,16]{1,0:T(8,128)} %mask_in.3, ...), custom_call_target="tpu_custom_call" | custom-call | flops 50331648 | bytes 1639428 | tf_op jit(solution)/shard_map/pallas_call | solution.py:239
  7.3 1.8 %collective-permute-done.1.refs_2_ = bf16[16,16,128]{2,1,0:T(8,128)(2,1)S(1)} collective-permute-done((bf16[16,16,128]{2,1,0:T(8,128)(2,1)S(1)}, bf16[16,16,128]{2,1,0:T(8,128)(2,1)S(1)}, u32[]{:S(2)}, u32[]{:S(2)}) %collective-permute-start.1) | collective-permute-done | bytes 65568 | tf_op jit(solution)/shard_map/ppermute | solution.py:266
  9.5 2.7 %collective-permute-start.3 = (bf16[16,16,128]{2,1,0:T(8,128)(2,1)S(1)}, bf16[16,16,128]{2,1,0:T(8,128)(2,1)S(1)}, u32[]{:S(2)}, u32[]{:S(2)}) collective-permute-start(bf16[16,16,128]{2,1,0:T(8,128)(2,1)S(1)} %shard_map.81), channel_id=1, source_target_pairs={{0,8},{4,12},{8,0},{12,4},{1,9},{5,13},{9,1},{13,5},{2,10},{6,14},... | collective-permute-start | bytes 196616 | tf_op jit(solution)/shard_map/ppermute | solution.py:266
  12.4 1.6 %collective-permute-start.4 = (bf16[16,16,128]{2,1,0:T(8,128)(2,1)S(1)}, bf16[16,16,128]{2,1,0:T(8,128)(2,1)S(1)}, u32[]{:S(2)}, u32[]{:S(2)}) collective-permute-start(bf16[16,16,128]{2,1,0:T(8,128)(2,1)S(1)} %shard_map.83), channel_id=1, source_target_pairs={{0,4},{4,0},{8,12},{12,8},{1,5},{5,1},{9,13},{13,9},{2,6},{6,2},{1... | collective-permute-start | bytes 196616 | tf_op jit(solution)/shard_map/ppermute | solution.py:266
  14.2 0.2 collective-permute-start.5
  14.6 1.1 %collective-permute-done.3.tile_ref = bf16[16,16,128]{2,1,0:T(8,128)(2,1)S(1)} collective-permute-done((bf16[16,16,128]{2,1,0:T(8,128)(2,1)S(1)}, bf16[16,16,128]{2,1,0:T(8,128)(2,1)S(1)}, u32[]{:S(2)}, u32[]{:S(2)}) %collective-permute-start.3) | collective-permute-done | bytes 65568 | tf_op jit(solution)/shard_map/ppermute | solution.py:266
  15.8 0.9 %collective-permute-done.4.tile_ref = bf16[16,16,128]{2,1,0:T(8,128)(2,1)S(1)} collective-permute-done((bf16[16,16,128]{2,1,0:T(8,128)(2,1)S(1)}, bf16[16,16,128]{2,1,0:T(8,128)(2,1)S(1)}, u32[]{:S(2)}, u32[]{:S(2)}) %collective-permute-start.4) | collective-permute-done | bytes 65568 | tf_op jit(solution)/shard_map/ppermute | solution.py:266
  16.7 3.6 %collective-permute-done.5.tile_ref = bf16[16,16,128]{2,1,0:T(8,128)(2,1)S(1)} collective-permute-done((bf16[16,16,128]{2,1,0:T(8,128)(2,1)S(1)}, bf16[16,16,128]{2,1,0:T(8,128)(2,1)S(1)}, u32[]{:S(2)}, u32[]{:S(2)}) %collective-permute-start.5) | collective-permute-done | bytes 65568 | tf_op jit(solution)/shard_map/ppermute | solution.py:266
  20.3 0.3 shard_map.86
  20.6 0.9 %collective-permute-start.6 = (bf16[16,16,128]{2,1,0:T(8,128)(2,1)S(1)}, bf16[16,16,128]{2,1,0:T(8,128)(2,1)S(1)}, u32[]{:S(2)}, u32[]{:S(2)}) collective-permute-start(bf16[16,16,128]{2,1,0:T(8,128)(2,1)S(1)} %get-tuple-element.27.refs_0_), channel_id=1, source_target_pairs={{0,8},{4,12},{8,0},{12,4},{1,9},{5,13},{9,1},{13,5},{2,10},{6,14},... | collective-permute-start | bytes 196616 | tf_op jit(solution)/shard_map/ppermute | solution.py:266
  21.6 0.5 %collective-permute-start.7 = (bf16[16,16,128]{2,1,0:T(8,128)(2,1)S(1)}, bf16[16,16,128]{2,1,0:T(8,128)(2,1)S(1)}, u32[]{:S(2)}, u32[]{:S(2)}) collective-permute-start(bf16[16,16,128]{2,1,0:T(8,128)(2,1)S(1)} %get-tuple-element.27.refs_0_), channel_id=1, source_target_pairs={{0,4},{4,0},{8,12},{12,8},{1,5},{5,1},{9,13},{13,9},{2,6},{6,2},{1... | collective-permute-start | bytes 196616 | tf_op jit(solution)/shard_map/ppermute | solution.py:266
  22.1 3.0 %collective-permute-start.8 = (bf16[16,16,128]{2,1,0:T(8,128)(2,1)S(1)}, bf16[16,16,128]{2,1,0:T(8,128)(2,1)S(1)}, u32[]{:S(2)}, u32[]{:S(2)}) collective-permute-start(bf16[16,16,128]{2,1,0:T(8,128)(2,1)S(1)} %get-tuple-element.27.refs_0_), channel_id=1, source_target_pairs={{0,12},{4,8},{8,4},{12,0},{1,13},{5,9},{9,5},{13,1},{2,14},{6,10},... | collective-permute-start | bytes 196616 | tf_op jit(solution)/shard_map/ppermute | solution.py:266
  25.3 0.8 %shard_map.87 = (bf16[16,16,128]{2,1,0:T(8,128)(2,1)}, f32[256,128]{1,0:T(8,128)S(1)}) custom-call(f32[256,128]{1,0:T(8,128)S(1)} %get-tuple-element.23.tri_normed_ref, f32[256,128]{1,0:T(8,128)S(1)} %get-tuple-element.24.open_ref, f32[256,128]{1,0:T(8,128)S(1)} %get-tuple-element.25.gate_factor_ref, bf16[128,640]{1,0:T(8,128)(2,1)S(1)} %copy-done, ...), custom_call_target="tpu_custom_call" | custom-call | flops 16777216 | bytes 786432 | tf_op jit(solution)/shard_map/pallas_call | solution.py:239
  26.1 1.1 %collective-permute-done.6.refs_1_.refs_0_ = bf16[16,16,128]{2,1,0:T(8,128)(2,1)S(1)} collective-permute-done((bf16[16,16,128]{2,1,0:T(8,128)(2,1)S(1)}, bf16[16,16,128]{2,1,0:T(8,128)(2,1)S(1)}, u32[]{:S(2)}, u32[]{:S(2)}) %collective-permute-start.6) | collective-permute-done | bytes 65568 | tf_op jit(solution)/shard_map/ppermute | solution.py:266
  27.2 1.0 %collective-permute-done.8.refs_3_.refs_2_ = bf16[16,16,128]{2,1,0:T(8,128)(2,1)S(1)} collective-permute-done((bf16[16,16,128]{2,1,0:T(8,128)(2,1)S(1)}, bf16[16,16,128]{2,1,0:T(8,128)(2,1)S(1)}, u32[]{:S(2)}, u32[]{:S(2)}) %collective-permute-start.8) | collective-permute-done | bytes 65568 | tf_op jit(solution)/shard_map/ppermute | solution.py:266
  28.3 0.6 %shard_map.90 = (bf16[16,16,128]{2,1,0:T(8,128)(2,1)S(1)}, bf16[16,16,128]{2,1,0:T(8,128)(2,1)S(1)}, bf16[16,16,128]{2,1,0:T(8,128)(2,1)S(1)}) custom-call(f32[1024,128]{1,0:T(8,128)S(1)} %shard_map.88.panel, f32[16,16,128]{2,1,0:T(8,128)S(1)} %get-tuple-element.31.right_ref.right), custom_call_target="tpu_custom_call" | custom-call | flops 1048576 | bytes 851968 | tf_op jit(solution)/shard_map/pallas_call | solution.py:239
  28.9 1.1 %collective-permute-start.9 = (bf16[16,16,128]{2,1,0:T(8,128)(2,1)S(1)}, bf16[16,16,128]{2,1,0:T(8,128)(2,1)S(1)}, u32[]{:S(2)}, u32[]{:S(2)}) collective-permute-start(bf16[16,16,128]{2,1,0:T(8,128)(2,1)S(1)} %get-tuple-element.32), channel_id=1, source_target_pairs={{0,2},{1,3},{2,0},{3,1},{4,6},{5,7},{6,4},{7,5},{8,10},{9,11},{10,... | collective-permute-start | bytes 196616 | tf_op jit(solution)/shard_map/ppermute | solution.py:266
  30.1 1.1 %collective-permute-start.11 = (bf16[16,16,128]{2,1,0:T(8,128)(2,1)S(1)}, bf16[16,16,128]{2,1,0:T(8,128)(2,1)S(1)}, u32[]{:S(2)}, u32[]{:S(2)}) collective-permute-start(bf16[16,16,128]{2,1,0:T(8,128)(2,1)S(1)} %get-tuple-element.34), channel_id=1, source_target_pairs={{0,1},{1,0},{2,3},{3,2},{4,5},{5,4},{6,7},{7,6},{8,9},{9,8},{10,11... | collective-permute-start | bytes 196616 | tf_op jit(solution)/shard_map/ppermute | solution.py:266
  31.1 0.7 %shard_map.94.refs_4_ = f32[256,128]{1,0:T(8,128)S(1)} custom-call(f32[64,16,128]{2,1,0:T(8,128)S(1)} %shard_map.78.panel, bf16[16,16,128]{2,1,0:T(8,128)(2,1)S(1)} %collective-permute-done.6.refs_1_.refs_0_, bf16[16,16,128]{2,1,0:T(8,128)(2,1)S(1)} %collective-permute-done.7.refs_2_.refs_1_, ...), custom_call_target="tpu_custom_call" | custom-call | tf_op jit(solution)/shard_map/pallas_call | solution.py:239
  32.1 1.5 %collective-permute-done.9.tile_ref = bf16[16,16,128]{2,1,0:T(8,128)(2,1)S(1)} collective-permute-done((bf16[16,16,128]{2,1,0:T(8,128)(2,1)S(1)}, bf16[16,16,128]{2,1,0:T(8,128)(2,1)S(1)}, u32[]{:S(2)}, u32[]{:S(2)}) %collective-permute-start.9) | collective-permute-done | bytes 65568 | tf_op jit(solution)/shard_map/ppermute | solution.py:266
  33.6 0.8 %collective-permute-done.10.tile_ref = bf16[16,16,128]{2,1,0:T(8,128)(2,1)S(1)} collective-permute-done((bf16[16,16,128]{2,1,0:T(8,128)(2,1)S(1)}, bf16[16,16,128]{2,1,0:T(8,128)(2,1)S(1)}, u32[]{:S(2)}, u32[]{:S(2)}) %collective-permute-start.10) | collective-permute-done | bytes 65568 | tf_op jit(solution)/shard_map/ppermute | solution.py:266
  34.4 0.9 %shard_map.95 = bf16[16,16,128]{2,1,0:T(8,128)(2,1)} custom-call(f32[16,16,128]{2,1,0:T(8,128)S(1)} %shard_map.93.base, bf16[16,16,128]{2,1,0:T(8,128)(2,1)S(1)} %collective-permute-done.11.refs_0_, f32[256,128]{1,0:T(8,128)S(1)} %get-tuple-element.35.refs_1_, f32[256,128]{1,0:T(8,128)S(1)} %get-tuple-element.36.refs_2_, ...), custom_call_target="tpu_custom_call" | custom-call | flops 16777216 | bytes 1343488 | tf_op jit(solution)/shard_map/pallas_call | solution.py:239
  (23 shorter events, 1.6 us)
Async XLA Ops:
  2.0 5.3 %collective-permute-start = (bf16[16,16,128]{2,1,0:T(8,128)(2,1)S(1)}, bf16[16,16,128]{2,1,0:T(8,128)(2,1)S(1)}, u32[]{:S(2)}, u32[]{:S(2)}) collective-permute-start(bf16[16,16,128]{2,1,0:T(8,128)(2,1)S(1)} %shard_map.77.refs_0_), channel_id=1, source_target_pairs={{0,2},{1,3},{2,0},{3,1},{4,6},{5,7},{6,4},{7,5},{8,10},{9,11},{10,... | collective-permute-start | bytes 196616 | tf_op jit(solution)/shard_map/ppermute | solution.py:266
  5.0 4.1 %collective-permute-start.1 = (bf16[16,16,128]{2,1,0:T(8,128)(2,1)S(1)}, bf16[16,16,128]{2,1,0:T(8,128)(2,1)S(1)}, u32[]{:S(2)}, u32[]{:S(2)}) collective-permute-start(bf16[16,16,128]{2,1,0:T(8,128)(2,1)S(1)} %shard_map.77.refs_0_), channel_id=1, source_target_pairs={{0,3},{1,2},{2,1},{3,0},{4,7},{5,6},{6,5},{7,4},{8,11},{9,10},{10,... | collective-permute-start | bytes 196616 | tf_op jit(solution)/shard_map/ppermute | solution.py:266
  5.0 4.1 %collective-permute-start.2 = (bf16[16,16,128]{2,1,0:T(8,128)(2,1)S(1)}, bf16[16,16,128]{2,1,0:T(8,128)(2,1)S(1)}, u32[]{:S(2)}, u32[]{:S(2)}) collective-permute-start(bf16[16,16,128]{2,1,0:T(8,128)(2,1)S(1)} %shard_map.77.refs_0_), channel_id=1, source_target_pairs={{0,1},{1,0},{2,3},{3,2},{4,5},{5,4},{6,7},{7,6},{8,9},{9,8},{10,11... | collective-permute-start | bytes 196616 | tf_op jit(solution)/shard_map/ppermute | solution.py:266
  9.5 6.3 %collective-permute-start.3 = (bf16[16,16,128]{2,1,0:T(8,128)(2,1)S(1)}, bf16[16,16,128]{2,1,0:T(8,128)(2,1)S(1)}, u32[]{:S(2)}, u32[]{:S(2)}) collective-permute-start(bf16[16,16,128]{2,1,0:T(8,128)(2,1)S(1)} %shard_map.81), channel_id=1, source_target_pairs={{0,8},{4,12},{8,0},{12,4},{1,9},{5,13},{9,1},{13,5},{2,10},{6,14},... | collective-permute-start | bytes 196616 | tf_op jit(solution)/shard_map/ppermute | solution.py:266
  12.4 4.3 %collective-permute-start.4 = (bf16[16,16,128]{2,1,0:T(8,128)(2,1)S(1)}, bf16[16,16,128]{2,1,0:T(8,128)(2,1)S(1)}, u32[]{:S(2)}, u32[]{:S(2)}) collective-permute-start(bf16[16,16,128]{2,1,0:T(8,128)(2,1)S(1)} %shard_map.83), channel_id=1, source_target_pairs={{0,4},{4,0},{8,12},{12,8},{1,5},{5,1},{9,13},{13,9},{2,6},{6,2},{1... | collective-permute-start | bytes 196616 | tf_op jit(solution)/shard_map/ppermute | solution.py:266
  14.2 6.1 %collective-permute-start.5 = (bf16[16,16,128]{2,1,0:T(8,128)(2,1)S(1)}, bf16[16,16,128]{2,1,0:T(8,128)(2,1)S(1)}, u32[]{:S(2)}, u32[]{:S(2)}) collective-permute-start(bf16[16,16,128]{2,1,0:T(8,128)(2,1)S(1)} %shard_map.85), channel_id=1, source_target_pairs={{0,12},{4,8},{8,4},{12,0},{1,13},{5,9},{9,5},{13,1},{2,14},{6,10},... | collective-permute-start | bytes 196616 | tf_op jit(solution)/shard_map/ppermute | solution.py:266
  20.6 4.7 %copy-start = (bf16[128,640]{1,0:T(8,128)(2,1)S(1)}, bf16[128,640]{1,0:T(8,128)(2,1)}, u32[]{:S(2)}) copy-start(bf16[128,640]{1,0:T(8,128)(2,1)} %refs_5_.3) | copy-start | bytes 491524
  20.6 4.7 %copy-start.1 = (bf16[128,128]{1,0:T(8,128)(2,1)S(1)}, bf16[128,128]{1,0:T(8,128)(2,1)}, u32[]{:S(2)}) copy-start(bf16[128,128]{1,0:T(8,128)(2,1)} %out_weight_ref.1) | copy-start | bytes 98308
  20.6 6.6 %collective-permute-start.6 = (bf16[16,16,128]{2,1,0:T(8,128)(2,1)S(1)}, bf16[16,16,128]{2,1,0:T(8,128)(2,1)S(1)}, u32[]{:S(2)}, u32[]{:S(2)}) collective-permute-start(bf16[16,16,128]{2,1,0:T(8,128)(2,1)S(1)} %get-tuple-element.27.refs_0_), channel_id=1, source_target_pairs={{0,8},{4,12},{8,0},{12,4},{1,9},{5,13},{9,1},{13,5},{2,10},{6,14},... | collective-permute-start | bytes 196616 | tf_op jit(solution)/shard_map/ppermute | solution.py:266
  21.6 5.7 %collective-permute-start.7 = (bf16[16,16,128]{2,1,0:T(8,128)(2,1)S(1)}, bf16[16,16,128]{2,1,0:T(8,128)(2,1)S(1)}, u32[]{:S(2)}, u32[]{:S(2)}) collective-permute-start(bf16[16,16,128]{2,1,0:T(8,128)(2,1)S(1)} %get-tuple-element.27.refs_0_), channel_id=1, source_target_pairs={{0,4},{4,0},{8,12},{12,8},{1,5},{5,1},{9,13},{13,9},{2,6},{6,2},{1... | collective-permute-start | bytes 196616 | tf_op jit(solution)/shard_map/ppermute | solution.py:266
  22.1 6.2 %collective-permute-start.8 = (bf16[16,16,128]{2,1,0:T(8,128)(2,1)S(1)}, bf16[16,16,128]{2,1,0:T(8,128)(2,1)S(1)}, u32[]{:S(2)}, u32[]{:S(2)}) collective-permute-start(bf16[16,16,128]{2,1,0:T(8,128)(2,1)S(1)} %get-tuple-element.27.refs_0_), channel_id=1, source_target_pairs={{0,12},{4,8},{8,4},{12,0},{1,13},{5,9},{9,5},{13,1},{2,14},{6,10},... | collective-permute-start | bytes 196616 | tf_op jit(solution)/shard_map/ppermute | solution.py:266
  28.9 4.6 %collective-permute-start.9 = (bf16[16,16,128]{2,1,0:T(8,128)(2,1)S(1)}, bf16[16,16,128]{2,1,0:T(8,128)(2,1)S(1)}, u32[]{:S(2)}, u32[]{:S(2)}) collective-permute-start(bf16[16,16,128]{2,1,0:T(8,128)(2,1)S(1)} %get-tuple-element.32), channel_id=1, source_target_pairs={{0,2},{1,3},{2,0},{3,1},{4,6},{5,7},{6,4},{7,5},{8,10},{9,11},{10,... | collective-permute-start | bytes 196616 | tf_op jit(solution)/shard_map/ppermute | solution.py:266
  30.0 4.3 %collective-permute-start.10 = (bf16[16,16,128]{2,1,0:T(8,128)(2,1)S(1)}, bf16[16,16,128]{2,1,0:T(8,128)(2,1)S(1)}, u32[]{:S(2)}, u32[]{:S(2)}) collective-permute-start(bf16[16,16,128]{2,1,0:T(8,128)(2,1)S(1)} %get-tuple-element.33), channel_id=1, source_target_pairs={{0,3},{1,2},{2,1},{3,0},{4,7},{5,6},{6,5},{7,4},{8,11},{9,10},{10,... | collective-permute-start | bytes 196616 | tf_op jit(solution)/shard_map/ppermute | solution.py:266
  30.1 4.3 %collective-permute-start.11 = (bf16[16,16,128]{2,1,0:T(8,128)(2,1)S(1)}, bf16[16,16,128]{2,1,0:T(8,128)(2,1)S(1)}, u32[]{:S(2)}, u32[]{:S(2)}) collective-permute-start(bf16[16,16,128]{2,1,0:T(8,128)(2,1)S(1)} %get-tuple-element.34), channel_id=1, source_target_pairs={{0,1},{1,0},{2,3},{3,2},{4,5},{5,4},{6,7},{7,6},{8,9},{9,8},{10,11... | collective-permute-start | bytes 196616 | tf_op jit(solution)/shard_map/ppermute | solution.py:266

commit v9 on v8

--- a/solution.py
+++ b/solution.py
@@ -141,11 +141,14 @@
 
 def left_panel_kernel(steps, crop_ref, *refs):
     row, col, panel = lax.axis_index("row"), lax.axis_index("col"), refs[-1]
-    size = refs[0].shape[0]
+    size, _, channels = refs[0].shape
+    rows = row * size + lax.broadcasted_iota(jnp.int32, (size, 1, channels), 0)
+    row_live = jnp.where(rows < crop_ref[0], 1.0, 0.0)
     for step, ref in zip(steps, refs):
         place = col ^ step
-        live = live_pairs(crop_ref, row, place, ref.shape)
-        panel[pl.ds(place * size, size)] = ref[...].astype(f32) * live
+        cols = place * size + lax.broadcasted_iota(jnp.int32, (1, size, channels), 1)
+        col_live = jnp.where(cols < crop_ref[0], 1.0, 0.0)
+        panel[pl.ds(place * size, size)] = ref[...].astype(f32) * (row_live * col_live)
 
 
 def partial_kernel(steps, panel, right_ref, *outs):
@@ -259,7 +262,7 @@
     work = 2 * size * pairs * channels
     wait = 2**31
     steps = [step for bit in range(n.bit_length() - 2, -1, -1) for step in range(2**bit, 2 ** (bit + 1))]
-    row_steps = [n // 2] + [step for step in range(1, n) if step != n // 2]
+    row_steps = list(range(n - 1, 0, -1))
 
 
     def swap(values, axis, step):
@@ -320,7 +323,7 @@
         functools.partial(panel_kernel, "row", [0] + row_steps), (jax.ShapeDtypeStruct((n * pairs, channels), f32),), *grads
     )
     terms = {}
-    for group in (steps, [0]):
+    for group in (steps[: n // 2], steps[n // 2 :], [0]):
         if terms:
             right, terms[last] = lax.optimization_barrier((right, terms[last]))
         last = group[-1]

time: 35.5 us -> 35.5 us (level)
    pallas_call x19 -> x20, Pallas kernels: 7.57 us -> 7.55 us  [call(): pl.pallas_call(kernel, out_shape=tuple(outs), in_specs=specs, out_specs=(...]
  transfers between devices with their start and end apart: 12 -> 12, of which waited for: 8 -> 8; matrix products, arithmetic and copies ran while one was open for 0% -> 0% of each run, Pallas kernels for 11% -> 12%
where the time goes in v9:
time: 35.5 us; the launch traced here: 35.3 us
  starting transfers between devices  14.5 us (41%)
  waiting for transfers between devices  11.9 us (34%)
  Pallas kernels  7.55 us (21%)
  between operations  1.44 us (4%)
    ppermute x12, starting transfers between devices, swap(): return lax.ppermute(values, axis, [(a, a ^ step) for a in range(n)])  14.5 us
    ppermute x12, waiting for transfers between devices, swap(): return lax.ppermute(values, axis, [(a, a ^ step) for a in range(n)])  11.9 us
    pallas_call x20, Pallas kernels, call(): pl.pallas_call(kernel, out_shape=tuple(outs), in_specs=specs, out_specs=(...  7.55 us
  transfers between devices with their start and end apart: 12, of which 8 were waited for; matrix products, arithmetic and copies ran while one was open for 0% of the time, Pallas kernels for 12%

profile of v9, /device:TPU:0, one launch (start us, length us, event | category | flops | bytes accessed | tf_op | source)
XLA Modules:
  0.0 35.3 jit_solution(1773415436507401822)
XLA Ops:
  0.6 1.3 %shard_map.77.refs_0_ = bf16[16,16,128]{2,1,0:T(8,128)(2,1)S(1)} custom-call(bf16[16,16,128]{2,1,0:T(8,128)(2,1)} %acts_in.3, s32[16,16]{1,0:T(8,128)} %mask_in.3, bf16[128,640]{1,0:T(8,128)(2,1)} %refs_5_.3), custom_call_target="tpu_custom_call" | custom-call | flops 16777216 | bytes 295936 | tf_op jit(solution)/shard_map/pallas_call | solution.py:242
  2.0 3.0 %collective-permute-start = (bf16[16,16,128]{2,1,0:T(8,128)(2,1)S(1)}, bf16[16,16,128]{2,1,0:T(8,128)(2,1)S(1)}, u32[]{:S(2)}, u32[]{:S(2)}) collective-permute-start(bf16[16,16,128]{2,1,0:T(8,128)(2,1)S(1)} %shard_map.77.refs_0_), channel_id=1, source_target_pairs={{0,2},{1,3},{2,0},{3,1},{4,6},{5,7},{6,4},{7,5},{8,10},{9,11},{10,... | collective-permute-start | bytes 196616 | tf_op jit(solution)/shard_map/ppermute | solution.py:269
  5.8 1.5 %shard_map.79 = (f32[16,16,128]{2,1,0:T(8,128)S(1)}, f32[256,128]{1,0:T(8,128)S(1)}, f32[256,128]{1,0:T(8,128)S(1)}, f32[4,256,128]{2,1,0:T(8,128)S(1)}, f32[256...) custom-call(bf16[16,16,128]{2,1,0:T(8,128)(2,1)} %acts_in.3, s32[16,16]{1,0:T(8,128)} %mask_in.3, ...), custom_call_target="tpu_custom_call" | custom-call | flops 50331648 | bytes 1639428 | tf_op jit(solution)/shard_map/pallas_call | solution.py:242
  7.3 1.8 %collective-permute-done.1.refs_2_ = bf16[16,16,128]{2,1,0:T(8,128)(2,1)S(1)} collective-permute-done((bf16[16,16,128]{2,1,0:T(8,128)(2,1)S(1)}, bf16[16,16,128]{2,1,0:T(8,128)(2,1)S(1)}, u32[]{:S(2)}, u32[]{:S(2)}) %collective-permute-start.1) | collective-permute-done | bytes 65568 | tf_op jit(solution)/shard_map/ppermute | solution.py:269
  9.4 3.7 %collective-permute-start.3 = (bf16[16,16,128]{2,1,0:T(8,128)(2,1)S(1)}, bf16[16,16,128]{2,1,0:T(8,128)(2,1)S(1)}, u32[]{:S(2)}, u32[]{:S(2)}) collective-permute-start(bf16[16,16,128]{2,1,0:T(8,128)(2,1)S(1)} %shard_map.81), channel_id=1, source_target_pairs={{0,12},{4,8},{8,4},{12,0},{1,13},{5,9},{9,5},{13,1},{2,14},{6,10},... | collective-permute-start | bytes 196616 | tf_op jit(solution)/shard_map/ppermute | solution.py:269
  13.4 0.2 shard_map.85
  13.6 0.8 %collective-permute-start.5 = (bf16[16,16,128]{2,1,0:T(8,128)(2,1)S(1)}, bf16[16,16,128]{2,1,0:T(8,128)(2,1)S(1)}, u32[]{:S(2)}, u32[]{:S(2)}) collective-permute-start(bf16[16,16,128]{2,1,0:T(8,128)(2,1)S(1)} %shard_map.85), channel_id=1, source_target_pairs={{0,4},{4,0},{8,12},{12,8},{1,5},{5,1},{9,13},{13,9},{2,6},{6,2},{1... | collective-permute-start | bytes 196616 | tf_op jit(solution)/shard_map/ppermute | solution.py:269
  14.6 1.1 %collective-permute-done.3.tile_ref = bf16[16,16,128]{2,1,0:T(8,128)(2,1)S(1)} collective-permute-done((bf16[16,16,128]{2,1,0:T(8,128)(2,1)S(1)}, bf16[16,16,128]{2,1,0:T(8,128)(2,1)S(1)}, u32[]{:S(2)}, u32[]{:S(2)}) %collective-permute-start.3) | collective-permute-done | bytes 65568 | tf_op jit(solution)/shard_map/ppermute | solution.py:269
  15.7 3.2 %collective-permute-done.4.tile_ref = bf16[16,16,128]{2,1,0:T(8,128)(2,1)S(1)} collective-permute-done((bf16[16,16,128]{2,1,0:T(8,128)(2,1)S(1)}, bf16[16,16,128]{2,1,0:T(8,128)(2,1)S(1)}, u32[]{:S(2)}, u32[]{:S(2)}) %collective-permute-start.4) | collective-permute-done | bytes 65568 | tf_op jit(solution)/shard_map/ppermute | solution.py:269
  19.1 0.3 shard_map.86
  19.4 2.5 %collective-permute-start.6 = (bf16[16,16,128]{2,1,0:T(8,128)(2,1)S(1)}, bf16[16,16,128]{2,1,0:T(8,128)(2,1)S(1)}, u32[]{:S(2)}, u32[]{:S(2)}) collective-permute-start(bf16[16,16,128]{2,1,0:T(8,128)(2,1)S(1)} %get-tuple-element.28.refs_0_), channel_id=1, source_target_pairs={{0,12},{4,8},{8,4},{12,0},{1,13},{5,9},{9,5},{13,1},{2,14},{6,10},... | collective-permute-start | bytes 196616 | tf_op jit(solution)/shard_map/ppermute | solution.py:269
  21.9 2.0 %collective-permute-start.8 = (bf16[16,16,128]{2,1,0:T(8,128)(2,1)S(1)}, bf16[16,16,128]{2,1,0:T(8,128)(2,1)S(1)}, u32[]{:S(2)}, u32[]{:S(2)}) collective-permute-start(bf16[16,16,128]{2,1,0:T(8,128)(2,1)S(1)} %get-tuple-element.28.refs_0_), channel_id=1, source_target_pairs={{0,4},{4,0},{8,12},{12,8},{1,5},{5,1},{9,13},{13,9},{2,6},{6,2},{1... | collective-permute-start | bytes 196616 | tf_op jit(solution)/shard_map/ppermute | solution.py:269
  24.1 0.8 %shard_map.87 = (bf16[16,16,128]{2,1,0:T(8,128)(2,1)}, f32[256,128]{1,0:T(8,128)S(1)}) custom-call(f32[256,128]{1,0:T(8,128)S(1)} %get-tuple-element.24.tri_normed_ref, f32[256,128]{1,0:T(8,128)S(1)} %get-tuple-element.25.open_ref, f32[256,128]{1,0:T(8,128)S(1)} %get-tuple-element.26.gate_factor_ref, bf16[128,640]{1,0:T(8,128)(2,1)S(1)} %copy-done, ...), custom_call_target="tpu_custom_call" | custom-call | flops 16777216 | bytes 786432 | tf_op jit(solution)/shard_map/pallas_call | solution.py:242
  24.9 0.7 %collective-permute-done.6.refs_1_.refs_0_ = bf16[16,16,128]{2,1,0:T(8,128)(2,1)S(1)} collective-permute-done((bf16[16,16,128]{2,1,0:T(8,128)(2,1)S(1)}, bf16[16,16,128]{2,1,0:T(8,128)(2,1)S(1)}, u32[]{:S(2)}, u32[]{:S(2)}) %collective-permute-start.6) | collective-permute-done | bytes 65568 | tf_op jit(solution)/shard_map/ppermute | solution.py:269
  25.5 2.6 %collective-permute-done.7.refs_2_.refs_1_ = bf16[16,16,128]{2,1,0:T(8,128)(2,1)S(1)} collective-permute-done((bf16[16,16,128]{2,1,0:T(8,128)(2,1)S(1)}, bf16[16,16,128]{2,1,0:T(8,128)(2,1)S(1)}, u32[]{:S(2)}, u32[]{:S(2)}) %collective-permute-start.7) | collective-permute-done | bytes 65568 | tf_op jit(solution)/shard_map/ppermute | solution.py:269
  28.2 0.4 %shard_map.90 = (bf16[16,16,128]{2,1,0:T(8,128)(2,1)S(1)}, bf16[16,16,128]{2,1,0:T(8,128)(2,1)S(1)}) custom-call(f32[1024,128]{1,0:T(8,128)S(1)} %shard_map.88.panel, f32[16,16,128]{2,1,0:T(8,128)S(1)} %get-tuple-element.33.right_ref.right), custom_call_target="tpu_custom_call" | custom-call | flops 1048576 | bytes 786432 | tf_op jit(solution)/shard_map/pallas_call | solution.py:242
  28.6 1.5 %collective-permute-start.9 = (bf16[16,16,128]{2,1,0:T(8,128)(2,1)S(1)}, bf16[16,16,128]{2,1,0:T(8,128)(2,1)S(1)}, u32[]{:S(2)}, u32[]{:S(2)}) collective-permute-start(bf16[16,16,128]{2,1,0:T(8,128)(2,1)S(1)} %get-tuple-element.34), channel_id=1, source_target_pairs={{0,2},{1,3},{2,0},{3,1},{4,6},{5,7},{6,4},{7,5},{8,10},{9,11},{10,... | collective-permute-start | bytes 196616 | tf_op jit(solution)/shard_map/ppermute | solution.py:269
  30.1 0.2 shard_map.91
  30.4 0.7 %collective-permute-start.11 = (bf16[16,16,128]{2,1,0:T(8,128)(2,1)S(1)}, bf16[16,16,128]{2,1,0:T(8,128)(2,1)S(1)}, u32[]{:S(2)}, u32[]{:S(2)}) collective-permute-start(bf16[16,16,128]{2,1,0:T(8,128)(2,1)S(1)} %shard_map.91), channel_id=1, source_target_pairs={{0,1},{1,0},{2,3},{3,2},{4,5},{5,4},{6,7},{7,6},{8,9},{9,8},{10,11... | collective-permute-start | bytes 196616 | tf_op jit(solution)/shard_map/ppermute | solution.py:269
  31.1 0.7 %shard_map.95.refs_4_ = f32[256,128]{1,0:T(8,128)S(1)} custom-call(f32[64,16,128]{2,1,0:T(8,128)S(1)} %shard_map.78.panel, bf16[16,16,128]{2,1,0:T(8,128)(2,1)S(1)} %collective-permute-done.6.refs_1_.refs_0_, bf16[16,16,128]{2,1,0:T(8,128)(2,1)S(1)} %collective-permute-done.7.refs_2_.refs_1_, ...), custom_call_target="tpu_custom_call" | custom-call | tf_op jit(solution)/shard_map/pallas_call | solution.py:242
  31.9 0.2 shard_map.92.base
  32.1 0.9 %collective-permute-done.9.tile_ref = bf16[16,16,128]{2,1,0:T(8,128)(2,1)S(1)} collective-permute-done((bf16[16,16,128]{2,1,0:T(8,128)(2,1)S(1)}, bf16[16,16,128]{2,1,0:T(8,128)(2,1)S(1)}, u32[]{:S(2)}, u32[]{:S(2)}) %collective-permute-start.9) | collective-permute-done | bytes 65568 | tf_op jit(solution)/shard_map/ppermute | solution.py:269
  33.0 1.4 %collective-permute-done.10.tile_ref = bf16[16,16,128]{2,1,0:T(8,128)(2,1)S(1)} collective-permute-done((bf16[16,16,128]{2,1,0:T(8,128)(2,1)S(1)}, bf16[16,16,128]{2,1,0:T(8,128)(2,1)S(1)}, u32[]{:S(2)}, u32[]{:S(2)}) %collective-permute-start.10) | collective-permute-done | bytes 65568 | tf_op jit(solution)/shard_map/ppermute | solution.py:269
  34.4 0.9 %shard_map.96 = bf16[16,16,128]{2,1,0:T(8,128)(2,1)} custom-call(f32[16,16,128]{2,1,0:T(8,128)S(1)} %shard_map.94.base, bf16[16,16,128]{2,1,0:T(8,128)(2,1)S(1)} %collective-permute-done.11.refs_0_, f32[256,128]{1,0:T(8,128)S(1)} %get-tuple-element.37.refs_1_, f32[256,128]{1,0:T(8,128)S(1)} %get-tuple-element.38.refs_2_, ...), custom_call_target="tpu_custom_call" | custom-call | flops 16777216 | bytes 1343488 | tf_op jit(solution)/shard_map/pallas_call | solution.py:242
  (24 shorter events, 1.4 us)
Async XLA Ops:
  2.0 5.3 %collective-permute-start = (bf16[16,16,128]{2,1,0:T(8,128)(2,1)S(1)}, bf16[16,16,128]{2,1,0:T(8,128)(2,1)S(1)}, u32[]{:S(2)}, u32[]{:S(2)}) collective-permute-start(bf16[16,16,128]{2,1,0:T(8,128)(2,1)S(1)} %shard_map.77.refs_0_), channel_id=1, source_target_pairs={{0,2},{1,3},{2,0},{3,1},{4,6},{5,7},{6,4},{7,5},{8,10},{9,11},{10,... | collective-permute-start | bytes 196616 | tf_op jit(solution)/shard_map/ppermute | solution.py:269
  5.0 4.1 %collective-permute-start.1 = (bf16[16,16,128]{2,1,0:T(8,128)(2,1)S(1)}, bf16[16,16,128]{2,1,0:T(8,128)(2,1)S(1)}, u32[]{:S(2)}, u32[]{:S(2)}) collective-permute-start(bf16[16,16,128]{2,1,0:T(8,128)(2,1)S(1)} %shard_map.77.refs_0_), channel_id=1, source_target_pairs={{0,3},{1,2},{2,1},{3,0},{4,7},{5,6},{6,5},{7,4},{8,11},{9,10},{10,... | collective-permute-start | bytes 196616 | tf_op jit(solution)/shard_map/ppermute | solution.py:269
  5.0 4.1 %collective-permute-start.2 = (bf16[16,16,128]{2,1,0:T(8,128)(2,1)S(1)}, bf16[16,16,128]{2,1,0:T(8,128)(2,1)S(1)}, u32[]{:S(2)}, u32[]{:S(2)}) collective-permute-start(bf16[16,16,128]{2,1,0:T(8,128)(2,1)S(1)} %shard_map.77.refs_0_), channel_id=1, source_target_pairs={{0,1},{1,0},{2,3},{3,2},{4,5},{5,4},{6,7},{7,6},{8,9},{9,8},{10,11... | collective-permute-start | bytes 196616 | tf_op jit(solution)/shard_map/ppermute | solution.py:269
  9.4 6.3 %collective-permute-start.3 = (bf16[16,16,128]{2,1,0:T(8,128)(2,1)S(1)}, bf16[16,16,128]{2,1,0:T(8,128)(2,1)S(1)}, u32[]{:S(2)}, u32[]{:S(2)}) collective-permute-start(bf16[16,16,128]{2,1,0:T(8,128)(2,1)S(1)} %shard_map.81), channel_id=1, source_target_pairs={{0,12},{4,8},{8,4},{12,0},{1,13},{5,9},{9,5},{13,1},{2,14},{6,10},... | collective-permute-start | bytes 196616 | tf_op jit(solution)/shard_map/ppermute | solution.py:269
  13.3 5.6 %collective-permute-start.4 = (bf16[16,16,128]{2,1,0:T(8,128)(2,1)S(1)}, bf16[16,16,128]{2,1,0:T(8,128)(2,1)S(1)}, u32[]{:S(2)}, u32[]{:S(2)}) collective-permute-start(bf16[16,16,128]{2,1,0:T(8,128)(2,1)S(1)} %shard_map.83), channel_id=1, source_target_pairs={{0,8},{4,12},{8,0},{12,4},{1,9},{5,13},{9,1},{13,5},{2,10},{6,14},... | collective-permute-start | bytes 196616 | tf_op jit(solution)/shard_map/ppermute | solution.py:269
  13.6 5.5 %collective-permute-start.5 = (bf16[16,16,128]{2,1,0:T(8,128)(2,1)S(1)}, bf16[16,16,128]{2,1,0:T(8,128)(2,1)S(1)}, u32[]{:S(2)}, u32[]{:S(2)}) collective-permute-start(bf16[16,16,128]{2,1,0:T(8,128)(2,1)S(1)} %shard_map.85), channel_id=1, source_target_pairs={{0,4},{4,0},{8,12},{12,8},{1,5},{5,1},{9,13},{13,9},{2,6},{6,2},{1... | collective-permute-start | bytes 196616 | tf_op jit(solution)/shard_map/ppermute | solution.py:269
  19.4 4.7 %copy-start = (bf16[128,640]{1,0:T(8,128)(2,1)S(1)}, bf16[128,640]{1,0:T(8,128)(2,1)}, u32[]{:S(2)}) copy-start(bf16[128,640]{1,0:T(8,128)(2,1)} %refs_5_.3) | copy-start | bytes 491524
  19.4 4.7 %copy-start.1 = (bf16[128,128]{1,0:T(8,128)(2,1)S(1)}, bf16[128,128]{1,0:T(8,128)(2,1)}, u32[]{:S(2)}) copy-start(bf16[128,128]{1,0:T(8,128)(2,1)} %out_weight_ref.1) | copy-start | bytes 98308
  19.4 6.1 %collective-permute-start.6 = (bf16[16,16,128]{2,1,0:T(8,128)(2,1)S(1)}, bf16[16,16,128]{2,1,0:T(8,128)(2,1)S(1)}, u32[]{:S(2)}, u32[]{:S(2)}) collective-permute-start(bf16[16,16,128]{2,1,0:T(8,128)(2,1)S(1)} %get-tuple-element.28.refs_0_), channel_id=1, source_target_pairs={{0,12},{4,8},{8,4},{12,0},{1,13},{5,9},{9,5},{13,1},{2,14},{6,10},... | collective-permute-start | bytes 196616 | tf_op jit(solution)/shard_map/ppermute | solution.py:269
  21.9 6.3 %collective-permute-start.7 = (bf16[16,16,128]{2,1,0:T(8,128)(2,1)S(1)}, bf16[16,16,128]{2,1,0:T(8,128)(2,1)S(1)}, u32[]{:S(2)}, u32[]{:S(2)}) collective-permute-start(bf16[16,16,128]{2,1,0:T(8,128)(2,1)S(1)} %get-tuple-element.28.refs_0_), channel_id=1, source_target_pairs={{0,8},{4,12},{8,0},{12,4},{1,9},{5,13},{9,1},{13,5},{2,10},{6,14},... | collective-permute-start | bytes 196616 | tf_op jit(solution)/shard_map/ppermute | solution.py:269
  21.9 6.3 %collective-permute-start.8 = (bf16[16,16,128]{2,1,0:T(8,128)(2,1)S(1)}, bf16[16,16,128]{2,1,0:T(8,128)(2,1)S(1)}, u32[]{:S(2)}, u32[]{:S(2)}) collective-permute-start(bf16[16,16,128]{2,1,0:T(8,128)(2,1)S(1)} %get-tuple-element.28.refs_0_), channel_id=1, source_target_pairs={{0,4},{4,0},{8,12},{12,8},{1,5},{5,1},{9,13},{13,9},{2,6},{6,2},{1... | collective-permute-start | bytes 196616 | tf_op jit(solution)/shard_map/ppermute | solution.py:269
  28.6 4.3 %collective-permute-start.9 = (bf16[16,16,128]{2,1,0:T(8,128)(2,1)S(1)}, bf16[16,16,128]{2,1,0:T(8,128)(2,1)S(1)}, u32[]{:S(2)}, u32[]{:S(2)}) collective-permute-start(bf16[16,16,128]{2,1,0:T(8,128)(2,1)S(1)} %get-tuple-element.34), channel_id=1, source_target_pairs={{0,2},{1,3},{2,0},{3,1},{4,6},{5,7},{6,4},{7,5},{8,10},{9,11},{10,... | collective-permute-start | bytes 196616 | tf_op jit(solution)/shard_map/ppermute | solution.py:269
  30.3 4.1 %collective-permute-start.10 = (bf16[16,16,128]{2,1,0:T(8,128)(2,1)S(1)}, bf16[16,16,128]{2,1,0:T(8,128)(2,1)S(1)}, u32[]{:S(2)}, u32[]{:S(2)}) collective-permute-start(bf16[16,16,128]{2,1,0:T(8,128)(2,1)S(1)} %get-tuple-element.35), channel_id=1, source_target_pairs={{0,3},{1,2},{2,1},{3,0},{4,7},{5,6},{6,5},{7,4},{8,11},{9,10},{10,... | collective-permute-start | bytes 196616 | tf_op jit(solution)/shard_map/ppermute | solution.py:269
  30.4 4.0 %collective-permute-start.11 = (bf16[16,16,128]{2,1,0:T(8,128)(2,1)S(1)}, bf16[16,16,128]{2,1,0:T(8,128)(2,1)S(1)}, u32[]{:S(2)}, u32[]{:S(2)}) collective-permute-start(bf16[16,16,128]{2,1,0:T(8,128)(2,1)S(1)} %shard_map.91), channel_id=1, source_target_pairs={{0,1},{1,0},{2,3},{3,2},{4,5},{5,4},{6,7},{7,6},{8,9},{9,8},{10,11... | collective-permute-start | bytes 196616 | tf_op jit(solution)/shard_map/ppermute | solution.py:269

commit v10 on v9

--- a/solution.py
+++ b/solution.py
@@ -131,14 +131,6 @@
     lax.fori_loop(0, out.shape[0], step, 0, unroll=4)
 
 
-def panel_kernel(axis, steps, *refs):
-    here, panel = lax.axis_index(axis), refs[-1]
-    rows = panel.shape[0] // len(steps)
-    for step, ref in zip(steps, refs):
-        tile = ref[...].astype(f32)
-        panel[pl.ds((here ^ step) * rows, rows)] = tile.reshape((rows,) + panel.shape[1:])
-
-
 def left_panel_kernel(steps, crop_ref, *refs):
     row, col, panel = lax.axis_index("row"), lax.axis_index("col"), refs[-1]
     size, _, channels = refs[0].shape
@@ -151,19 +143,35 @@
         panel[pl.ds(place * size, size)] = ref[...].astype(f32) * (row_live * col_live)
 
 
-def partial_kernel(steps, panel, right_ref, *outs):
+def partial_kernel(steps, crop_ref, *refs):
+    count = len(steps)
+    lefts, right_ref, outs, left = refs[:count], refs[count], refs[count + 1 : -1], refs[-1]
     size, _, channels = right_ref.shape
-    for step, out in zip(steps, outs):
-        start = (lax.axis_index("row") ^ step) * size
+    rows = lax.axis_index("row") * size + lax.broadcasted_iota(jnp.int32, (size, 1, channels), 0)
+    row_live = jnp.where(rows < crop_ref[0], 1.0, 0.0)
+    for step, left_ref, out in zip(steps, lefts, outs):
+        cols = (lax.axis_index("col") ^ step) * size + lax.broadcasted_iota(jnp.int32, (1, size, channels), 1)
+        left[...] = left_ref[...].astype(f32) * (row_live * jnp.where(cols < crop_ref[0], 1.0, 0.0))
 
         def add(k, sums):
             other = right_ref[k]
-            return tuple(sums[i] + panel[start + k, pl.ds(i, 1), :] * other for i in range(size))
+            return tuple(sums[i] + left[k, pl.ds(i, 1), :] * other for i in range(size))
 
         zero = jnp.zeros((size, channels), f32)
         sums = lax.fori_loop(0, size, add, (zero,) * size, unroll=4)
         for i in range(size):
-            out[i] = sums[i].astype(out.dtype)
+            out[i] = sums[i]
+
+
+def pick_kernel(steps, *refs):
+    here = lax.axis_index("row") ^ lax.axis_index("col")
+    tiles, outs = refs[: len(steps)], refs[len(steps) :]
+    for step, out in zip(steps, outs):
+        for other, tile in enumerate(tiles):
+
+            @pl.when((here ^ step) == other)
+            def _():
+                out[...] = tile[...].astype(out.dtype)
 
 
 def triangle_kernel(base, tile_ref, upstream_ref, tri_normed_ref, grad_ref):
@@ -175,11 +183,10 @@
         grad_ref[i] = normalize_back(tri_normed, scale, upstream_ref[here, :]).astype(bf16)
 
 
-def left_terms_kernel(steps, panel, right, *outs):
-    size = right.shape[0]
-    for step, out in zip(steps, outs):
-        start = (lax.axis_index("col") ^ step) * (size * size)
-        weighted_sums(right, 0, [panel[pl.ds(start + j, size, stride=size), :] for j in range(size)], out)
+def left_terms_kernel(grad_ref, right, out, grad):
+    size, _, channels = out.shape
+    grad[...] = grad_ref[...].astype(f32).reshape(size * size, channels)
+    weighted_sums(right, 0, [grad[pl.ds(j, size, stride=size), :] for j in range(size)], out)
 
 
 def right_grad_kernel(steps, panel, *refs):
@@ -262,7 +269,7 @@
     work = 2 * size * pairs * channels
     wait = 2**31
     steps = [step for bit in range(n.bit_length() - 2, -1, -1) for step in range(2**bit, 2 ** (bit + 1))]
-    row_steps = list(range(n - 1, 0, -1))
+    row_steps = [n // 2] + [step for step in range(1, n) if step != n // 2]
 
 
     def swap(values, axis, step):
@@ -296,17 +303,24 @@
             pltpu.SemaphoreType.DMA((5,)),
         ],
     )
+    parts = []
+    order = [0] + steps
+    for group in [[at] for at in range(n - 2)] + [[n - 2, n - 1]]:
+        parts += call(
+            functools.partial(partial_kernel, [order[at] for at in group]), (wide,) * len(group),
+            crop_length, *(lefts[at] for at in group), right, smem=(0,), flops=work,
+            scratch=[pltpu.VMEM(wide.shape, f32)],
+        )
+    parts = [part for _, part in sorted(zip(order, parts), key=lambda each: each[0])]
+    total, *parts = call(
+        functools.partial(pick_kernel, [0] + row_steps), (wide,) + (tile,) * (n - 1), *parts,
+        flops=pairs * channels,
+    )
     (left_panel,) = call(
         functools.partial(left_panel_kernel, [0] + steps), (panel,), crop_length, *lefts, smem=(0,)
     )
-    parts = {}
-    for step in [0] + row_steps:
-        (parts[step],) = call(
-            functools.partial(partial_kernel, (step,)), (tile if step else wide,), left_panel, right, flops=work,
-        )
-    total = parts[0]
-    for step in row_steps:
-        part = swap(parts[step], "row", step)
+    for step, part in zip(row_steps, parts):
+        part = swap(part, "row", step)
         if step != row_steps[-1]:
             (total,) = call(add_kernel, (wide,), total, part, flops=wait)
     tri_normed, tri_grad = call(
@@ -319,25 +333,17 @@
     )
     (right_grad,) = call(functools.partial(right_grad_kernel, [0]), (wide,), left_panel, tri_grad)
     right, partial, right_grad = lax.optimization_barrier((right, partial, right_grad))
-    (grad_panel,) = call(
-        functools.partial(panel_kernel, "row", [0] + row_steps), (jax.ShapeDtypeStruct((n * pairs, channels), f32),), *grads
-    )
-    terms = {}
-    for group in (steps[: n // 2], steps[n // 2 :], [0]):
-        if terms:
-            right, terms[last] = lax.optimization_barrier((right, terms[last]))
-        last = group[-1]
-        outs = call(
-            functools.partial(left_terms_kernel, group), (wide if group == [0] else tile,) * len(group),
-            grad_panel, right, flops=work,
+    terms = [None] * n
+    for step, grad in zip([0] + row_steps, grads):
+        (terms[step],) = call(
+            left_terms_kernel, (wide,), grad, right, scratch=[pltpu.VMEM((pairs, channels), f32)], flops=work,
         )
-        terms.update(zip(group, outs))
-    total, last = terms[0], []
-    for step in steps:
-        term = swap(terms[step], "col", step)
-        if step == steps[-1]:
-            last.append(term)
-        else:
+    total, *terms = call(
+        functools.partial(pick_kernel, [0] + steps), (wide,) + (tile,) * (n - 1), *terms, flops=pairs * channels,
+    )
+    for step, term in zip(steps, terms):
+        term = swap(term, "col", step)
+        if step != steps[-1]:
             (total,) = call(add_kernel, (wide,), total, term, flops=wait)
     (share,) = call(
         functools.partial(right_back_kernel, row_steps), (flat,),
@@ -345,7 +351,7 @@
         scratch=[pltpu.VMEM(wide.shape, f32)],
     )
     (pair_grad,) = call(
-        back_kernel, (tile,), total, *last[::-1], normed, scale, factors, share, in_weights,
+        back_kernel, (tile,), total, term, normed, scale, factors, share, in_weights,
         flops=2 * pairs * channels * 2 * channels,
     )
     return (update, pair_grad)

time: 35.5 us -> 35.5 us (level)
  waiting for transfers between devices: 11.9 us -> 11 us
  local copies, waits for them, and re-layouts: 0.01 us -> 0.71 us
    ppermute x12, waiting for transfers between devices: 11.9 us -> 11 us  [swap(): return lax.ppermute(values, axis, [(a, a ^ step) for a in range(n)])]
    unnamed x4, local copies, waits for them, and re-layouts: 0.01 us -> 0.71 us
    pallas_call x20 -> x21, Pallas kernels: 7.55 us -> 7.81 us  [call(): pl.pallas_call(kernel, out_shape=tuple(outs), in_specs=specs, out_specs=(...]
  transfers between devices with their start and end apart: 12 -> 12, of which waited for: 8 -> 8; matrix products, arithmetic and copies ran while one was open for 0% -> 0% of each run, Pallas kernels for 12% -> 13%
where the time goes in v10:
time: 35.5 us; the launch traced here: 35.3 us
  starting transfers between devices  14.3 us (40%)
  waiting for transfers between devices  11 us (31%)
  Pallas kernels  7.81 us (22%)
  between operations  1.43 us (4%)
  local copies, waits for them, and re-layouts  0.71 us (2%)
    ppermute x12, starting transfers between devices, swap(): return lax.ppermute(values, axis, [(a, a ^ step) for a in range(n)])  14.3 us
    ppermute x12, waiting for transfers between devices, swap(): return lax.ppermute(values, axis, [(a, a ^ step) for a in range(n)])  11 us
    pallas_call x21, Pallas kernels, call(): pl.pallas_call(kernel, out_shape=tuple(outs), in_specs=specs, out_specs=(...  7.81 us
    unnamed x4, local copies, waits for them, and re-layouts  0.71 us
  transfers between devices with their start and end apart: 12, of which 8 were waited for; matrix products, arithmetic and copies ran while one was open for 0% of the time, Pallas kernels for 13%

profile of v10, /device:TPU:0, one launch (start us, length us, event | category | flops | bytes accessed | tf_op | source)
XLA Modules:
  0.0 35.3 jit_solution(9382925764672350308)
XLA Ops:
  0.6 1.3 %shard_map.77.refs_0_ = bf16[16,16,128]{2,1,0:T(8,128)(2,1)S(1)} custom-call(bf16[16,16,128]{2,1,0:T(8,128)(2,1)} %acts_in.3, s32[16,16]{1,0:T(8,128)} %mask_in.3, bf16[128,640]{1,0:T(8,128)(2,1)} %refs_5_.3), custom_call_target="tpu_custom_call" | custom-call | flops 16777216 | bytes 295936 | tf_op jit(solution)/shard_map/pallas_call | solution.py:249
  2.0 3.0 %collective-permute-start.2 = (bf16[16,16,128]{2,1,0:T(8,128)(2,1)S(1)}, bf16[16,16,128]{2,1,0:T(8,128)(2,1)S(1)}, u32[]{:S(2)}, u32[]{:S(2)}) collective-permute-start(bf16[16,16,128]{2,1,0:T(8,128)(2,1)S(1)} %shard_map.77.refs_0_), channel_id=1, source_target_pairs={{0,2},{1,3},{2,0},{3,1},{4,6},{5,7},{6,4},{7,5},{8,10},{9,11},{10,... | collective-permute-start | bytes 196616 | tf_op jit(solution)/shard_map/ppermute | solution.py:276
  5.8 1.5 %shard_map.78 = (f32[16,16,128]{2,1,0:T(8,128)S(1)}, f32[256,128]{1,0:T(8,128)S(1)}, f32[256,128]{1,0:T(8,128)S(1)}, f32[4,256,128]{2,1,0:T(8,128)S(1)}, f32[256...) custom-call(bf16[16,16,128]{2,1,0:T(8,128)(2,1)} %acts_in.3, s32[16,16]{1,0:T(8,128)} %mask_in.3, ...), custom_call_target="tpu_custom_call" | custom-call | flops 50331648 | bytes 1639428 | tf_op jit(solution)/shard_map/pallas_call | solution.py:249
  7.8 1.4 %collective-permute-done.refs_0_.refs_2_ = bf16[16,16,128]{2,1,0:T(8,128)(2,1)S(1)} collective-permute-done((bf16[16,16,128]{2,1,0:T(8,128)(2,1)S(1)}, bf16[16,16,128]{2,1,0:T(8,128)(2,1)S(1)}, u32[]{:S(2)}, u32[]{:S(2)}) %collective-permute-start) | collective-permute-done | bytes 65568 | tf_op jit(solution)/shard_map/ppermute | solution.py:276
  9.1 0.4 %shard_map.80 = (f32[16,16,128]{2,1,0:T(8,128)S(1)}, f32[16,16,128]{2,1,0:T(8,128)S(1)}) custom-call(s32[1]{0:T(128)S(6)} %copy.8.crop_ref, bf16[16,16,128]{2,1,0:T(8,128)(2,1)S(1)} %collective-permute-done.refs_0_.refs_2_, bf16[16,16,128]{2,1,0:T(8,128)(2,1)S(1)} %collective-permute-done.1.refs_1_.refs_3_, ...), custom_call_target="tpu_custom_call" | custom-call | flops 1048576 | bytes 524292 | tf_op jit(solution)/shard_map/pallas_call | solution.py:249
  9.6 2.7 %collective-permute-start.3 = (bf16[16,16,128]{2,1,0:T(8,128)(2,1)S(1)}, bf16[16,16,128]{2,1,0:T(8,128)(2,1)S(1)}, u32[]{:S(2)}, u32[]{:S(2)}) collective-permute-start(bf16[16,16,128]{2,1,0:T(8,128)(2,1)S(1)} %get-tuple-element.30), channel_id=1, source_target_pairs={{0,8},{4,12},{8,0},{12,4},{1,9},{5,13},{9,1},{13,5},{2,10},{6,14},... | collective-permute-start | bytes 196616 | tf_op jit(solution)/shard_map/ppermute | solution.py:276
  12.3 1.6 %collective-permute-start.4 = (bf16[16,16,128]{2,1,0:T(8,128)(2,1)S(1)}, bf16[16,16,128]{2,1,0:T(8,128)(2,1)S(1)}, u32[]{:S(2)}, u32[]{:S(2)}) collective-permute-start(bf16[16,16,128]{2,1,0:T(8,128)(2,1)S(1)} %get-tuple-element.31), channel_id=1, source_target_pairs={{0,4},{4,0},{8,12},{12,8},{1,5},{5,1},{9,13},{13,9},{2,6},{6,2},{1... | collective-permute-start | bytes 196616 | tf_op jit(solution)/shard_map/ppermute | solution.py:276
  14.1 1.8 %collective-permute-done.3.tile_ref = bf16[16,16,128]{2,1,0:T(8,128)(2,1)S(1)} collective-permute-done((bf16[16,16,128]{2,1,0:T(8,128)(2,1)S(1)}, bf16[16,16,128]{2,1,0:T(8,128)(2,1)S(1)}, u32[]{:S(2)}, u32[]{:S(2)}) %collective-permute-start.3) | collective-permute-done | bytes 65568 | tf_op jit(solution)/shard_map/ppermute | solution.py:276
  15.9 0.7 %collective-permute-done.4.tile_ref = bf16[16,16,128]{2,1,0:T(8,128)(2,1)S(1)} collective-permute-done((bf16[16,16,128]{2,1,0:T(8,128)(2,1)S(1)}, bf16[16,16,128]{2,1,0:T(8,128)(2,1)S(1)}, u32[]{:S(2)}, u32[]{:S(2)}) %collective-permute-start.4) | collective-permute-done | bytes 65568 | tf_op jit(solution)/shard_map/ppermute | solution.py:276
  16.6 3.4 %collective-permute-done.5.tile_ref = bf16[16,16,128]{2,1,0:T(8,128)(2,1)S(1)} collective-permute-done((bf16[16,16,128]{2,1,0:T(8,128)(2,1)S(1)}, bf16[16,16,128]{2,1,0:T(8,128)(2,1)S(1)}, u32[]{:S(2)}, u32[]{:S(2)}) %collective-permute-start.5) | collective-permute-done | bytes 65568 | tf_op jit(solution)/shard_map/ppermute | solution.py:276
  20.0 0.3 shard_map.85
  20.3 1.4 %collective-permute-start.8 = (bf16[16,16,128]{2,1,0:T(8,128)(2,1)S(1)}, bf16[16,16,128]{2,1,0:T(8,128)(2,1)S(1)}, u32[]{:S(2)}, u32[]{:S(2)}) collective-permute-start(bf16[16,16,128]{2,1,0:T(8,128)(2,1)S(1)} %get-tuple-element.38.refs_0_.grad_ref), channel_id=1, source_target_pairs={{0,12},{4,8},{8,4},{12,0},{1,13},{5,9},{9,5},{13,1},{2,14},{6,10},... | collective-permute-start | bytes 196616 | tf_op jit(solution)/shard_map/ppermute | solution.py:276
  21.8 2.9 %collective-permute-start.6 = (bf16[16,16,128]{2,1,0:T(8,128)(2,1)S(1)}, bf16[16,16,128]{2,1,0:T(8,128)(2,1)S(1)}, u32[]{:S(2)}, u32[]{:S(2)}) collective-permute-start(bf16[16,16,128]{2,1,0:T(8,128)(2,1)S(1)} %get-tuple-element.38.refs_0_.grad_ref), channel_id=1, source_target_pairs={{0,4},{4,0},{8,12},{12,8},{1,5},{5,1},{9,13},{13,9},{2,6},{6,2},{1... | collective-permute-start | bytes 196616 | tf_op jit(solution)/shard_map/ppermute | solution.py:276
  25.0 0.7 %copy-done = bf16[128,640]{1,0:T(8,128)(2,1)S(1)} copy-done((bf16[128,640]{1,0:T(8,128)(2,1)S(1)}, bf16[128,640]{1,0:T(8,128)(2,1)}, u32[]{:S(2)}) %copy-start) | copy-done | bytes 163864
  25.7 0.8 %shard_map.86 = (bf16[16,16,128]{2,1,0:T(8,128)(2,1)}, f32[256,128]{1,0:T(8,128)S(1)}) custom-call(f32[256,128]{1,0:T(8,128)S(1)} %get-tuple-element.34.tri_normed_ref, f32[256,128]{1,0:T(8,128)S(1)} %get-tuple-element.35.open_ref, f32[256,128]{1,0:T(8,128)S(1)} %get-tuple-element.36.gate_factor_ref, bf16[128,640]{1,0:T(8,128)(2,1)S(1)} %copy-done, ...), custom_call_target="tpu_custom_call" | custom-call | flops 16777216 | bytes 786432 | tf_op jit(solution)/shard_map/pallas_call | solution.py:249
  26.5 0.2 shard_map.89.refs_0_
  27.1 0.9 %collective-permute-done.7.grad_ref.refs_0_ = bf16[16,16,128]{2,1,0:T(8,128)(2,1)S(1)} collective-permute-done((bf16[16,16,128]{2,1,0:T(8,128)(2,1)S(1)}, bf16[16,16,128]{2,1,0:T(8,128)(2,1)S(1)}, u32[]{:S(2)}, u32[]{:S(2)}) %collective-permute-start.7) | collective-permute-done | bytes 65568 | tf_op jit(solution)/shard_map/ppermute | solution.py:276
  28.2 0.2 shard_map.90.refs_1_
  28.6 1.7 %collective-permute-start.9 = (bf16[16,16,128]{2,1,0:T(8,128)(2,1)S(1)}, bf16[16,16,128]{2,1,0:T(8,128)(2,1)S(1)}, u32[]{:S(2)}, u32[]{:S(2)}) collective-permute-start(bf16[16,16,128]{2,1,0:T(8,128)(2,1)S(1)} %get-tuple-element.42), channel_id=1, source_target_pairs={{0,2},{1,3},{2,0},{3,1},{4,6},{5,7},{6,4},{7,5},{8,10},{9,11},{10,... | collective-permute-start | bytes 196616 | tf_op jit(solution)/shard_map/ppermute | solution.py:276
  30.2 0.5 %collective-permute-start.11 = (bf16[16,16,128]{2,1,0:T(8,128)(2,1)S(1)}, bf16[16,16,128]{2,1,0:T(8,128)(2,1)S(1)}, u32[]{:S(2)}, u32[]{:S(2)}) collective-permute-start(bf16[16,16,128]{2,1,0:T(8,128)(2,1)S(1)} %get-tuple-element.44), channel_id=1, source_target_pairs={{0,1},{1,0},{2,3},{3,2},{4,5},{5,4},{6,7},{7,6},{8,9},{9,8},{10,11... | collective-permute-start | bytes 196616 | tf_op jit(solution)/shard_map/ppermute | solution.py:276
  30.8 0.7 %shard_map.96.refs_4_ = f32[256,128]{1,0:T(8,128)S(1)} custom-call(f32[64,16,128]{2,1,0:T(8,128)S(1)} %shard_map.87.panel, bf16[16,16,128]{2,1,0:T(8,128)(2,1)S(1)} %collective-permute-done.7.grad_ref.refs_0_, bf16[16,16,128]{2,1,0:T(8,128)(2,1)S(1)} %collective-permute-done.6.grad_ref.refs_1_, ...), custom_call_target="tpu_custom_call" | custom-call | tf_op jit(solution)/shard_map/pallas_call | solution.py:249
  31.5 1.4 %collective-permute-done.9.tile_ref = bf16[16,16,128]{2,1,0:T(8,128)(2,1)S(1)} collective-permute-done((bf16[16,16,128]{2,1,0:T(8,128)(2,1)S(1)}, bf16[16,16,128]{2,1,0:T(8,128)(2,1)S(1)}, u32[]{:S(2)}, u32[]{:S(2)}) %collective-permute-start.9) | collective-permute-done | bytes 65568 | tf_op jit(solution)/shard_map/ppermute | solution.py:276
  32.9 1.4 %collective-permute-done.10.tile_ref = bf16[16,16,128]{2,1,0:T(8,128)(2,1)S(1)} collective-permute-done((bf16[16,16,128]{2,1,0:T(8,128)(2,1)S(1)}, bf16[16,16,128]{2,1,0:T(8,128)(2,1)S(1)}, u32[]{:S(2)}, u32[]{:S(2)}) %collective-permute-start.10) | collective-permute-done | bytes 65568 | tf_op jit(solution)/shard_map/ppermute | solution.py:276
  34.3 0.9 %shard_map.97 = bf16[16,16,128]{2,1,0:T(8,128)(2,1)} custom-call(f32[16,16,128]{2,1,0:T(8,128)S(1)} %shard_map.95.base, bf16[16,16,128]{2,1,0:T(8,128)(2,1)S(1)} %collective-permute-done.11.refs_0_, f32[256,128]{1,0:T(8,128)S(1)} %get-tuple-element.45.refs_1_, f32[256,128]{1,0:T(8,128)S(1)} %get-tuple-element.46.refs_2_, ...), custom_call_target="tpu_custom_call" | custom-call | flops 16777216 | bytes 1343488 | tf_op jit(solution)/shard_map/pallas_call | solution.py:249
  (25 shorter events, 2.0 us)
Async XLA Ops:
  2.0 5.6 %collective-permute-start.2 = (bf16[16,16,128]{2,1,0:T(8,128)(2,1)S(1)}, bf16[16,16,128]{2,1,0:T(8,128)(2,1)S(1)}, u32[]{:S(2)}, u32[]{:S(2)}) collective-permute-start(bf16[16,16,128]{2,1,0:T(8,128)(2,1)S(1)} %shard_map.77.refs_0_), channel_id=1, source_target_pairs={{0,2},{1,3},{2,0},{3,1},{4,6},{5,7},{6,4},{7,5},{8,10},{9,11},{10,... | collective-permute-start | bytes 196616 | tf_op jit(solution)/shard_map/ppermute | solution.py:276
  5.0 4.1 %collective-permute-start = (bf16[16,16,128]{2,1,0:T(8,128)(2,1)S(1)}, bf16[16,16,128]{2,1,0:T(8,128)(2,1)S(1)}, u32[]{:S(2)}, u32[]{:S(2)}) collective-permute-start(bf16[16,16,128]{2,1,0:T(8,128)(2,1)S(1)} %shard_map.77.refs_0_), channel_id=1, source_target_pairs={{0,3},{1,2},{2,1},{3,0},{4,7},{5,6},{6,5},{7,4},{8,11},{9,10},{10,... | collective-permute-start | bytes 196616 | tf_op jit(solution)/shard_map/ppermute | solution.py:276
  5.0 4.1 %collective-permute-start.1 = (bf16[16,16,128]{2,1,0:T(8,128)(2,1)S(1)}, bf16[16,16,128]{2,1,0:T(8,128)(2,1)S(1)}, u32[]{:S(2)}, u32[]{:S(2)}) collective-permute-start(bf16[16,16,128]{2,1,0:T(8,128)(2,1)S(1)} %shard_map.77.refs_0_), channel_id=1, source_target_pairs={{0,1},{1,0},{2,3},{3,2},{4,5},{5,4},{6,7},{7,6},{8,9},{9,8},{10,11... | collective-permute-start | bytes 196616 | tf_op jit(solution)/shard_map/ppermute | solution.py:276
  9.6 6.3 %collective-permute-start.3 = (bf16[16,16,128]{2,1,0:T(8,128)(2,1)S(1)}, bf16[16,16,128]{2,1,0:T(8,128)(2,1)S(1)}, u32[]{:S(2)}, u32[]{:S(2)}) collective-permute-start(bf16[16,16,128]{2,1,0:T(8,128)(2,1)S(1)} %get-tuple-element.30), channel_id=1, source_target_pairs={{0,8},{4,12},{8,0},{12,4},{1,9},{5,13},{9,1},{13,5},{2,10},{6,14},... | collective-permute-start | bytes 196616 | tf_op jit(solution)/shard_map/ppermute | solution.py:276
  12.3 4.3 %collective-permute-start.4 = (bf16[16,16,128]{2,1,0:T(8,128)(2,1)S(1)}, bf16[16,16,128]{2,1,0:T(8,128)(2,1)S(1)}, u32[]{:S(2)}, u32[]{:S(2)}) collective-permute-start(bf16[16,16,128]{2,1,0:T(8,128)(2,1)S(1)} %get-tuple-element.31), channel_id=1, source_target_pairs={{0,4},{4,0},{8,12},{12,8},{1,5},{5,1},{9,13},{13,9},{2,6},{6,2},{1... | collective-permute-start | bytes 196616 | tf_op jit(solution)/shard_map/ppermute | solution.py:276
  13.9 6.1 %collective-permute-start.5 = (bf16[16,16,128]{2,1,0:T(8,128)(2,1)S(1)}, bf16[16,16,128]{2,1,0:T(8,128)(2,1)S(1)}, u32[]{:S(2)}, u32[]{:S(2)}) collective-permute-start(bf16[16,16,128]{2,1,0:T(8,128)(2,1)S(1)} %get-tuple-element.32), channel_id=1, source_target_pairs={{0,12},{4,8},{8,4},{12,0},{1,13},{5,9},{9,5},{13,1},{2,14},{6,10},... | collective-permute-start | bytes 196616 | tf_op jit(solution)/shard_map/ppermute | solution.py:276
  20.3 6.6 %collective-permute-start.8 = (bf16[16,16,128]{2,1,0:T(8,128)(2,1)S(1)}, bf16[16,16,128]{2,1,0:T(8,128)(2,1)S(1)}, u32[]{:S(2)}, u32[]{:S(2)}) collective-permute-start(bf16[16,16,128]{2,1,0:T(8,128)(2,1)S(1)} %get-tuple-element.38.refs_0_.grad_ref), channel_id=1, source_target_pairs={{0,12},{4,8},{8,4},{12,0},{1,13},{5,9},{9,5},{13,1},{2,14},{6,10},... | collective-permute-start | bytes 196616 | tf_op jit(solution)/shard_map/ppermute | solution.py:276
  21.6 6.4 %collective-permute-start.7 = (bf16[16,16,128]{2,1,0:T(8,128)(2,1)S(1)}, bf16[16,16,128]{2,1,0:T(8,128)(2,1)S(1)}, u32[]{:S(2)}, u32[]{:S(2)}) collective-permute-start(bf16[16,16,128]{2,1,0:T(8,128)(2,1)S(1)} %get-tuple-element.38.refs_0_.grad_ref), channel_id=1, source_target_pairs={{0,8},{4,12},{8,0},{12,4},{1,9},{5,13},{9,1},{13,5},{2,10},{6,14},... | collective-permute-start | bytes 196616 | tf_op jit(solution)/shard_map/ppermute | solution.py:276
  21.8 6.4 %collective-permute-start.6 = (bf16[16,16,128]{2,1,0:T(8,128)(2,1)S(1)}, bf16[16,16,128]{2,1,0:T(8,128)(2,1)S(1)}, u32[]{:S(2)}, u32[]{:S(2)}) collective-permute-start(bf16[16,16,128]{2,1,0:T(8,128)(2,1)S(1)} %get-tuple-element.38.refs_0_.grad_ref), channel_id=1, source_target_pairs={{0,4},{4,0},{8,12},{12,8},{1,5},{5,1},{9,13},{13,9},{2,6},{6,2},{1... | collective-permute-start | bytes 196616 | tf_op jit(solution)/shard_map/ppermute | solution.py:276
  24.8 0.9 %copy-start = (bf16[128,640]{1,0:T(8,128)(2,1)S(1)}, bf16[128,640]{1,0:T(8,128)(2,1)}, u32[]{:S(2)}) copy-start(bf16[128,640]{1,0:T(8,128)(2,1)} %refs_5_.3) | copy-start | bytes 491524
  24.8 0.9 %copy-start.1 = (bf16[128,128]{1,0:T(8,128)(2,1)S(1)}, bf16[128,128]{1,0:T(8,128)(2,1)}, u32[]{:S(2)}) copy-start(bf16[128,128]{1,0:T(8,128)(2,1)} %out_weight_ref.1) | copy-start | bytes 98308
  28.6 4.3 %collective-permute-start.9 = (bf16[16,16,128]{2,1,0:T(8,128)(2,1)S(1)}, bf16[16,16,128]{2,1,0:T(8,128)(2,1)S(1)}, u32[]{:S(2)}, u32[]{:S(2)}) collective-permute-start(bf16[16,16,128]{2,1,0:T(8,128)(2,1)S(1)} %get-tuple-element.42), channel_id=1, source_target_pairs={{0,2},{1,3},{2,0},{3,1},{4,6},{5,7},{6,4},{7,5},{8,10},{9,11},{10,... | collective-permute-start | bytes 196616 | tf_op jit(solution)/shard_map/ppermute | solution.py:276
  30.2 4.1 %collective-permute-start.10 = (bf16[16,16,128]{2,1,0:T(8,128)(2,1)S(1)}, bf16[16,16,128]{2,1,0:T(8,128)(2,1)S(1)}, u32[]{:S(2)}, u32[]{:S(2)}) collective-permute-start(bf16[16,16,128]{2,1,0:T(8,128)(2,1)S(1)} %get-tuple-element.43), channel_id=1, source_target_pairs={{0,3},{1,2},{2,1},{3,0},{4,7},{5,6},{6,5},{7,4},{8,11},{9,10},{10,... | collective-permute-start | bytes 196616 | tf_op jit(solution)/shard_map/ppermute | solution.py:276
  30.2 4.1 %collective-permute-start.11 = (bf16[16,16,128]{2,1,0:T(8,128)(2,1)S(1)}, bf16[16,16,128]{2,1,0:T(8,128)(2,1)S(1)}, u32[]{:S(2)}, u32[]{:S(2)}) collective-permute-start(bf16[16,16,128]{2,1,0:T(8,128)(2,1)S(1)} %get-tuple-element.44), channel_id=1, source_target_pairs={{0,1},{1,0},{2,3},{3,2},{4,5},{5,4},{6,7},{7,6},{8,9},{9,8},{10,11... | collective-permute-start | bytes 196616 | tf_op jit(solution)/shard_map/ppermute | solution.py:276

commit v11 on v5

v11 whole, which is shorter than its diff:
```python
import functools

import jax
import jax.numpy as jnp
from jax import lax
from jax.experimental import pallas as pl
from jax.experimental.pallas import tpu as pltpu
from jax.sharding import PartitionSpec as P

epsilon = 1e-05
f32 = jnp.float32
bf16 = jnp.bfloat16


def mean_lanes(values):
    return jnp.sum(values, axis=-1, keepdims=True) * (1.0 / values.shape[-1])


def normalize(values):
    center = values - mean_lanes(values)
    variance = mean_lanes(center * center)
    scale = lax.rsqrt(variance + epsilon)
    return (center * scale, scale)


def normalize_back(normed, scale, upstream):
    average = mean_lanes(upstream)
    project = mean_lanes(upstream * normed)
    return scale * (upstream - average - normed * project)


def sigmoid(values):
    return 1.0 / (1.0 + jnp.exp(-values))


def dot(a, b):
    return jnp.dot(a, b, preferred_element_type=f32)


def dot_t(a, b):
    return lax.dot_general(a, b, (((1,), (1,)), ((), ())), preferred_element_type=f32)


def live_factor(crop_ref, row, col, shape):
    rows = row * shape[0] + lax.broadcasted_iota(jnp.int32, (shape[0], 1, shape[2]), 0)
    cols = col * shape[1] + lax.broadcasted_iota(jnp.int32, (1, shape[1], shape[2]), 1)
    return jnp.where(rows < crop_ref[0], 1.0, 0.0) * jnp.where(cols < crop_ref[0], 1.0, 0.0)


def spread(mask, channels):
    size = mask.shape[0]
    pair = lax.broadcasted_iota(jnp.int32, (size * size, size), 0)
    lane = lax.broadcasted_iota(jnp.int32, (size * size, size), 1)
    pick_row = jnp.where(pair // size == lane, 1.0, 0.0).astype(bf16)
    pick_col = jnp.where(pair % size == lane, 1.0, 0.0)
    picked = (dot(pick_row, mask.astype(bf16)) * pick_col).astype(bf16)
    return dot(picked, jnp.ones((size, channels), bf16))


def start_copies(sems, *pairs):
    copies = [pltpu.make_async_copy(src, dst, sems.at[n]) for n, (src, dst) in enumerate(pairs)]
    for copy in copies:
        copy.start()
    return copies


def gated(projected, block, keep):
    channels = keep.shape[1]
    value = projected[:, block * channels : (block + 1) * channels]
    opened = sigmoid(projected[:, (block + 1) * channels : (block + 2) * channels])
    return (opened * value * keep).astype(bf16), opened, value


def tiles_kernel(acts_in, mask_in, weights_in, left_ref, right_ref, acts_ref, mask_ref, weights_ref, sems):
    size, _, channels = acts_ref.shape
    copies = start_copies(
        sems, (acts_in, acts_ref), (weights_in.at[:, pl.ds(0, 4 * channels)], weights_ref), (mask_in, mask_ref)
    )
    copies[0].wait()
    normed, _ = normalize(acts_ref[...].astype(f32).reshape(size * size, channels))
    normed = normed.astype(bf16)
    for copy in copies[1:]:
        copy.wait()
    projected = dot(normed, weights_ref[...])
    mask = spread(mask_ref[...].astype(f32), channels)
    for block, out in ((0, left_ref), (2, right_ref)):
        tile, _, _ = gated(projected, block, mask)
        out[...] = tile.reshape(size, size, channels)


def factors_kernel(
    acts_in, mask_in, crop_ref, cotangent_in, weights_in, out_weight_in, _,
    normed_ref, scale_ref, factor_ref, open_ref, gate_factor_ref, upstream_ref,
    acts_ref, mask_ref, cotangent_ref, weights_ref, out_weight_ref, sems,
):
    copies = start_copies(
        sems, (acts_in, acts_ref), (weights_in, weights_ref), (mask_in, mask_ref),
        (cotangent_in, cotangent_ref), (out_weight_in, out_weight_ref),
    )
    size, _, channels = acts_ref.shape
    pairs = size * size
    copies[0].wait()
    normed, scale = normalize(acts_ref[...].astype(f32).reshape(pairs, channels))
    normed_ref[...] = normed
    scale_ref[...] = jnp.broadcast_to(scale, (pairs, channels))
    for copy in copies[1:]:
        copy.wait()
    projected = dot(normed.astype(bf16), weights_ref[...])
    live = live_factor(crop_ref, lax.axis_index("row"), lax.axis_index("col"), acts_ref.shape)
    keep = spread(mask_ref[...].astype(f32), channels) * live.reshape(pairs, channels)
    for block in (0, 2):
        _, opened, value = gated(projected, block, keep)
        factor_ref[block] = keep * opened
        factor_ref[block + 1] = keep * value * opened * (1.0 - opened)
    out_open = sigmoid(projected[:, 4 * channels :])
    cotangent = cotangent_ref[...].astype(f32).reshape(pairs, channels)
    lin_grad = (cotangent * out_open).astype(bf16)
    open_ref[...] = out_open
    gate_factor_ref[...] = cotangent * out_open * (1.0 - out_open)
    upstream_ref[...] = dot_t(lin_grad, out_weight_ref[...])


def weighted_sums(weights, start, terms, out, base=None):
    def step(k, _):
        total = weights[start + k, pl.ds(0, 1), :] * terms[0]
        for n in range(1, len(terms)):
            total = total + weights[start + k, pl.ds(n, 1), :] * terms[n]
        if base is not None:
            total = total + base[k]
        out[k] = total.astype(out.dtype)
        return 0

    lax.fori_loop(0, out.shape[0], step, 0, unroll=4)


def place():
    row, col = lax.axis_index("row"), lax.axis_index("col")
    return row, col, row ^ col, (row ^ col) & 1


def panel_kernel(steps, crop_ref, *refs):
    row, col, _, _ = place()
    panel, size = refs[-1], refs[0].shape[0]
    for at, (step, ref) in enumerate(zip(steps, refs)):
        live = live_factor(crop_ref, row, col ^ step, ref.shape)
        panel[at * size : (at + 1) * size] = ref[...].astype(f32) * live


def left_panel_kernel(steps, crop_ref, *refs):
    row, col, _, _ = place()
    panel, size = refs[-1], refs[0].shape[0]
    for step, ref in zip(steps, refs):
        live = live_factor(crop_ref, row, col ^ step, ref.shape)
        panel[pl.ds(((col ^ step) // 2) * size, size)] = ref[...].astype(f32) * live


def partial_kernel(step, crop_ref, left_ref, rights, out, left):
    row, col, _, _ = place()
    size, _, channels = left_ref.shape
    left[...] = left_ref[...].astype(f32) * live_factor(crop_ref, row, col ^ step, left_ref.shape)
    for half in range(2):

        def add(k, sums):
            other = rights[half * size + k]
            return tuple(sums[i] + left[k, pl.ds(i, 1), :] * other for i in range(size))

        zero = jnp.zeros((size, channels), f32)
        sums = lax.fori_loop(0, size, add, (zero,) * size, unroll=4)
        for i in range(size):
            out[half, i] = sums[i]


def pick_parts_kernel(steps, *refs):
    _, _, away, differ = place()
    tiles, outs = refs[: -len(steps)], refs[-len(steps) :]
    for step, out in zip(steps, outs):
        for at, tile in enumerate(tiles):

            @pl.when((away ^ step) == 2 * at)
            def _():
                out[...] = tile[...].astype(out.dtype)

        if step == 0:

            @pl.when(differ == 1)
            def _():
                out[...] = jnp.zeros(out.shape, out.dtype)


def pick_terms_kernel(steps, *refs):
    _, _, away, differ = place()
    tiles, outs = refs[: -len(steps)], refs[-len(steps) :]
    for step, out in zip(steps, outs):
        for at, tile in enumerate(tiles):

            @pl.when((away ^ differ ^ step) == 2 * at)
            def _():
                out[...] = tile[...].astype(out.dtype)


def triangle_kernel(base, tile_ref, normed_ref, scale_ref, own_ref, other_ref):
    size, _, channels = own_ref.shape
    for half, out in enumerate((own_ref, other_ref)):
        for i in range(size):
            tri_normed, scale = normalize(base[half, i] + tile_ref[half, i].astype(f32))
            normed_ref[half, i] = tri_normed
            scale_ref[half, i] = jnp.broadcast_to(scale, (size, channels))
            out[i] = tri_normed.astype(bf16)


def triangle_back_kernel(normed_ref, scale_ref, upstream_ref, other_ref, grad_ref):
    size = grad_ref.shape[1]
    for half, upstream in enumerate((upstream_ref, other_ref)):
        for i in range(size):
            rows = pl.ds(i * size, size)
            grad_ref[half, i] = normalize_back(normed_ref[half, i], scale_ref[half, i], upstream[rows, :]).astype(bf16)


def select_grads(same_ref, differ_ref, out):
    _, _, _, differ = place()

    @pl.when(differ == 0)
    def _():
        out[...] = same_ref[...].astype(f32).reshape(out.shape)

    @pl.when(differ == 1)
    def _():
        out[...] = differ_ref[...].astype(f32).reshape(out.shape)


def left_terms_kernel(differ_ref, same_ref, rights, *refs):
    out, grad = refs[-2:]
    size, pairs = out.shape[0], out.shape[0] ** 2
    select_grads(same_ref, differ_ref, grad)
    for half in range(2):
        rows = [grad[pl.ds(half * pairs + j, size, stride=size), :] for j in range(size)]
        weighted_sums(rights, half * size, rows, out, out if half else None)


def right_grad_kernel(slot, panel, same_ref, differ_ref, *refs):
    outs, grad = refs[-3:-1], refs[-1]
    size = outs[0].shape[0]
    row, _, _, differ = place()
    select_grads(same_ref, differ_ref, grad)
    start = ((row ^ slot ^ differ) // 2) * size
    for half, out in enumerate(outs):
        rows = [grad[half, i] for i in range(size)]
        weighted_sums(panel, start, rows, out, refs[half] if len(refs) > 3 else None)


def add_kernel(base, tile_ref, out):
    out[...] = base[...] + tile_ref[...].astype(f32)


def update_kernel(
    normed_ref, other_ref, open_ref, gate_factor_ref, weights_ref, out_weight_ref, update_ref, share_ref, tri_normed
):
    size, _, channels = update_ref.shape
    _, _, _, differ = place()
    for parity, ref in enumerate((normed_ref, other_ref)):

        @pl.when(differ == parity)
        def _():
            tri_normed[...] = ref[...].reshape(tri_normed.shape)

    linear = dot(tri_normed[...], out_weight_ref[...])
    update = (open_ref[...] * linear).astype(bf16)
    update_ref[...] = update.reshape(size, size, channels)
    out_gate_grad = (gate_factor_ref[...] * linear).astype(bf16)
    share_ref[...] = dot_t(out_gate_grad, weights_ref[:, 4 * channels :])


def back_kernel(
    left_ref, right_ref, other_ref, normed_ref, scale_ref, factor_ref, share_ref, weights_ref, out
):
    size, _, channels = out.shape
    pairs = size * size
    left = left_ref[...].reshape(pairs, channels)
    right = (right_ref[...] + other_ref[...].astype(f32)).reshape(pairs, channels)
    grads = jnp.concatenate(
        [(total * factor_ref[block]).astype(bf16) for block, total in enumerate((left, left, right, right))],
        axis=1,
    )
    normed_grad = share_ref[...] + dot_t(grads, weights_ref[:, : 4 * channels])
    back = normalize_back(normed_ref[...], scale_ref[...], normed_grad)
    out[...] = back.astype(bf16).reshape(size, size, channels)


def call(kernel, outs, *args, scratch=(), flops=0, smem=(), hbm=()):
    spec = pl.BlockSpec(memory_space=pltpu.VMEM)
    total = sum(a.size * a.dtype.itemsize for a in (*args, *outs))
    specs = [spec] * len(args)
    for n in smem:
        specs[n] = pl.BlockSpec(memory_space=pltpu.SMEM)
    args = list(args)
    for n in hbm:
        specs[n] = pl.BlockSpec(memory_space=pltpu.HBM)
        args[n] = pltpu.with_memory_space_constraint(args[n], pltpu.HBM)
    return pl.pallas_call(
        kernel,
        out_shape=tuple(outs),
        in_specs=specs,
        out_specs=(spec,) * len(outs),
        scratch_shapes=scratch,
        compiler_params=pltpu.CompilerParams(vmem_limit_bytes=24 * 2**20),
        cost_estimate=pl.CostEstimate(flops=flops, bytes_accessed=total if flops else 0, transcendentals=0),
    )(*args)


def local(pair_acts, pair_mask, crop_length, cotangent, in_weights, out_weight):
    size, _, channels = pair_acts.shape
    pairs = size * size
    n = lax.axis_size("row")
    tile = jax.ShapeDtypeStruct((size, size, channels), bf16)
    flat = jax.ShapeDtypeStruct((pairs, channels), f32)

    wide = jax.ShapeDtypeStruct((size, size, channels), f32)
    work = 2 * size * pairs * channels
    wait = 2**31
    near = list(range(0, n, 2))
    row_steps = list(range(n - 1, 0, -2)) + list(range(n - 2, 0, -2))
    pair = jax.ShapeDtypeStruct((2, size, size, channels), bf16)
    wide_pair = jax.ShapeDtypeStruct(pair.shape, f32)
    pair_panel = jax.ShapeDtypeStruct((2 * size, size, channels), f32)
    left_panel = jax.ShapeDtypeStruct((n // 2 * size, size, channels), f32)

    def swap(values, step):
        return lax.ppermute(values, "col", [(a, a ^ step) for a in range(n)])

    def send(values, step, parity):
        pairs = [(a * n + b, (a ^ step) * n + b) for a in range(n) for b in range(n) if (a ^ b) % 2 == parity]
        return lax.ppermute(values, ("row", "col"), pairs)

    left, right = call(
        tiles_kernel, (tile, tile), pair_acts, pair_mask, in_weights,
        hbm=(0, 1, 2), flops=2 * pairs * channels * 4 * channels,
        scratch=[
            pltpu.VMEM(pair_acts.shape, bf16),
            pltpu.VMEM(pair_mask.shape, jnp.int32),
            pltpu.VMEM((channels, 4 * channels), bf16),
            pltpu.SemaphoreType.DMA((3,)),
        ],
    )
    lefts = [left] + [swap(left, step) for step in near[1:]]
    other_right = swap(right, 1)
    (rights,) = call(
        functools.partial(panel_kernel, (0, 1)), (pair_panel,), crop_length, right, other_right, smem=(0,)
    )
    parts = [
        call(
            functools.partial(partial_kernel, step), (wide_pair,), crop_length, tile_of, rights, smem=(0,),
            flops=work, scratch=[pltpu.VMEM(wide.shape, f32)],
        )[0]
        for step, tile_of in zip(near, lefts)
    ]
    total, *parts = call(
        functools.partial(pick_parts_kernel, [0] + row_steps), (wide_pair,) + (pair,) * (n - 1), *parts,
        flops=pairs * channels,
    )
    normed, scale, factors, out_open, gate_factor, upstream = call(
        factors_kernel,
        (flat, flat, jax.ShapeDtypeStruct((4, pairs, channels), f32), flat, flat, flat),
        pair_acts, pair_mask, crop_length, cotangent, in_weights, out_weight, total,
        smem=(2,), hbm=(0, 1, 3, 4, 5), flops=2 * pairs * channels * 6 * channels,
        scratch=[
            pltpu.VMEM(pair_acts.shape, bf16),
            pltpu.VMEM(pair_mask.shape, jnp.int32),
            pltpu.VMEM(cotangent.shape, bf16),
            pltpu.VMEM(in_weights.shape, bf16),
            pltpu.VMEM(out_weight.shape, bf16),
            pltpu.SemaphoreType.DMA((5,)),
        ],
    )
    other_upstream = swap(upstream, 1)
    (left_panel,) = call(
        functools.partial(left_panel_kernel, near), (left_panel,), crop_length, *lefts, smem=(0,)
    )
    for step, part in zip(row_steps, parts):
        part = send(part, step, step % 2)
        if step != row_steps[-1]:
            (total,) = call(add_kernel, (wide_pair,), total, part, flops=wait)
    wide_normed, wide_scale, tri_normed, other_normed = call(
        triangle_kernel, (wide_pair, wide_pair, tile, tile), total, part, flops=wait,
    )
    (tri_grad,) = call(
        triangle_back_kernel, (pair,), wide_normed, wide_scale, upstream, other_upstream,
        flops=20 * pairs * channels,
    )
    grads = {0: tri_grad}
    for step in row_steps:
        grads[step] = send(tri_grad, step, 0)
    other_normed = swap(other_normed, 1)
    update, share = call(
        update_kernel, (tile, flat), tri_normed, other_normed, out_open, gate_factor, in_weights, out_weight,
        flops=4 * pairs * channels * channels, scratch=[pltpu.VMEM((pairs, channels), bf16)],
    )
    terms = [
        call(
            left_terms_kernel, (wide,), grads[slot + 1], grads[slot], rights, share, left_panel,
            scratch=[pltpu.VMEM((2 * pairs, channels), f32)], flops=work,
        )[0]
        for slot in near[::-1]
    ][::-1]
    total, *terms = call(
        functools.partial(pick_terms_kernel, near), (wide,) + (tile,) * (n // 2 - 1), *terms, flops=pairs * channels
    )
    right_grads = ()
    for slot in near:
        right_grads = call(
            functools.partial(right_grad_kernel, slot), (wide, tile if slot == near[-1] else wide),
            left_panel, grads[slot], grads[slot + 1], *right_grads,
            scratch=[pltpu.VMEM(wide_pair.shape, f32)],
        )
    right_grad, other_grad = right_grads
    other_grad = swap(other_grad, 1)
    for step, term in zip(near[1:], terms):
        (total,) = call(add_kernel, (wide,), total, swap(term, step), flops=wait)
    (pair_grad,) = call(
        back_kernel, (tile,), total, right_grad, other_grad, normed, scale, factors, share, in_weights,
        flops=2 * pairs * channels * 4 * channels,
    )
    return (update, pair_grad)


def solution(mesh):
    return jax.shard_map(
        local,
        mesh=mesh,
        in_specs=(
            P(("group", "row"), "col", None),
            P(("group", "row"), "col"),
            P("group"),
            P(("group", "row"), "col", None),
            P(),
            P(),
        ),
        out_specs=(P(("group", "row"), "col", None), P(("group", "row"), "col", None)),
        check_vma=False,
    )
```

time: 36.6 us -> 38 us (1.038)
  starting transfers between devices: 13.5 us -> 18.3 us
  waiting for transfers between devices: 12.4 us -> 10 us
  Pallas kernels: 9.08 us -> 7.87 us
    ppermute x12, starting transfers between devices: 13.5 us -> 18.3 us  [the longest x6 13.4 us: send(): return lax.ppermute(values, ('row', 'col'), pairs)]
    ppermute x12, waiting for transfers between devices: 12.4 us -> 10 us  [the longest x6 5.32 us: send(): return lax.ppermute(values, ('row', 'col'), pairs)]
    pallas_call x20 -> x19, Pallas kernels: 9.08 us -> 7.87 us  [call(): pl.pallas_call(kernel, out_shape=tuple(outs), in_specs=specs, out_specs=(...]
  transfers between devices with their start and end apart: 12 -> 12, of which waited for: 9 -> 6; matrix products, arithmetic and copies ran while one was open for 0% -> 0% of each run, Pallas kernels for 16% -> 11%
where the time goes in v11:
time: 38 us; the launch traced here: 37.7 us
  starting transfers between devices  18.3 us (48%)
  waiting for transfers between devices  10 us (26%)
  Pallas kernels  7.87 us (21%)
  between operations  1.52 us (4%)
    ppermute x6, starting transfers between devices, send(): return lax.ppermute(values, ('row', 'col'), pairs)  13.4 us
    pallas_call x19, Pallas kernels, call(): pl.pallas_call(kernel, out_shape=tuple(outs), in_specs=specs, out_specs=(...  7.87 us
    ppermute x6, waiting for transfers between devices, send(): return lax.ppermute(values, ('row', 'col'), pairs)  5.32 us
    ppermute x6, starting transfers between devices, swap(): return lax.ppermute(values, 'col', [(a, a ^ step) for a in range(n)])  4.85 us
    ppermute x6, waiting for transfers between devices, swap(): return lax.ppermute(values, 'col', [(a, a ^ step) for a in range(n)])  4.68 us
  transfers between devices with their start and end apart: 12, of which 6 were waited for; matrix products, arithmetic and copies ran while one was open for 0% of the time, Pallas kernels for 11%

profile of v11, /device:TPU:0, one launch (start us, length us, event | category | flops | bytes accessed | tf_op | source)
XLA Modules:
  0.0 37.7 jit_solution(4341283868127522485)
XLA Ops:
  0.6 1.4 %shard_map.77 = (bf16[16,16,128]{2,1,0:T(8,128)(2,1)S(1)}, bf16[16,16,128]{2,1,0:T(8,128)(2,1)S(1)}) custom-call(bf16[16,16,128]{2,1,0:T(8,128)(2,1)} %acts_in.3, s32[16,16]{1,0:T(8,128)} %mask_in.3, bf16[128,640]{1,0:T(8,128)(2,1)} %weights_ref.3), custom_call_target="tpu_custom_call" | custom-call | flops 33554432 | bytes 361472 | tf_op jit(solution)/shard_map/pallas_call | solution.py:299
  2.1 0.5 %collective-permute-start = (bf16[16,16,128]{2,1,0:T(8,128)(2,1)S(1)}, bf16[16,16,128]{2,1,0:T(8,128)(2,1)S(1)}, u32[]{:S(2)}, u32[]{:S(2)}) collective-permute-start(bf16[16,16,128]{2,1,0:T(8,128)(2,1)S(1)} %get-tuple-element.27.refs_0_), channel_id=1, source_target_pairs={{0,1},{1,0},{2,3},{3,2},{4,5},{5,4},{6,7},{7,6},{8,9},{9,8},{10,11... | collective-permute-start | bytes 196616 | tf_op jit(solution)/shard_map/ppermute | solution.py:328
  2.6 2.6 %collective-permute-start.1 = (bf16[16,16,128]{2,1,0:T(8,128)(2,1)S(1)}, bf16[16,16,128]{2,1,0:T(8,128)(2,1)S(1)}, u32[]{:S(2)}, u32[]{:S(2)}) collective-permute-start(bf16[16,16,128]{2,1,0:T(8,128)(2,1)S(1)} %get-tuple-element.26.left_ref.refs_0_), channel_id=1, source_target_pairs={{0,2},{1,3},{2,0},{3,1},{4,6},{5,7},{6,4},{7,5},{8,10},{9,11},{10,... | collective-permute-start | bytes 196616 | tf_op jit(solution)/shard_map/ppermute | solution.py:328
  5.9 0.4 %shard_map.79.refs_0_ = f32[2,16,16,128]{3,2,1,0:T(8,128)S(1)} custom-call(s32[1]{0:T(128)S(6)} %copy.8.crop_ref, bf16[16,16,128]{2,1,0:T(8,128)(2,1)S(1)} %get-tuple-element.26.left_ref.refs_0_, f32[32,16,128]{2,1,0:T(8,128)S(1)} %shard_map.78.rights), custom_call_target="tpu_custom_call" | custom-call | flops 1048576 | bytes 589828 | tf_op jit(solution)/shard_map/pallas_call | solution.py:299
  6.3 1.6 %collective-permute-done.1.left_ref.refs_1_ = bf16[16,16,128]{2,1,0:T(8,128)(2,1)S(1)} collective-permute-done((bf16[16,16,128]{2,1,0:T(8,128)(2,1)S(1)}, bf16[16,16,128]{2,1,0:T(8,128)(2,1)S(1)}, u32[]{:S(2)}, u32[]{:S(2)}) %collective-permute-start.1) | collective-permute-done | bytes 65568 | tf_op jit(solution)/shard_map/ppermute | solution.py:328
  7.8 0.4 %shard_map.80.refs_1_ = f32[2,16,16,128]{3,2,1,0:T(8,128)S(1)} custom-call(s32[1]{0:T(128)S(6)} %copy.8.crop_ref, bf16[16,16,128]{2,1,0:T(8,128)(2,1)S(1)} %collective-permute-done.1.left_ref.refs_1_, f32[32,16,128]{2,1,0:T(8,128)S(1)} %shard_map.78.rights), custom_call_target="tpu_custom_call" | custom-call | flops 1048576 | bytes 589828 | tf_op jit(solution)/shard_map/pallas_call | solution.py:299
  8.3 1.3 %collective-permute-start.2 = (bf16[2,16,16,128]{3,2,1,0:T(8,128)(2,1)S(1)}, bf16[2,16,16,128]{3,2,1,0:T(8,128)(2,1)S(1)}, u32[]{:S(2)}, u32[]{:S(2)}) collective-permute-start(bf16[2,16,16,128]{3,2,1,0:T(8,128)(2,1)S(1)} %get-tuple-element.29), channel_id=1, source_target_pairs={{1,13},{3,15},{4,8},{6,10},{9,5},{11,7},{12,0},{14,2},{17,29},{19,... | collective-permute-start | bytes 393224 | tf_op jit(solution)/shard_map/ppermute | solution.py:332
  9.6 1.3 %collective-permute-start.3 = (bf16[2,16,16,128]{3,2,1,0:T(8,128)(2,1)S(1)}, bf16[2,16,16,128]{3,2,1,0:T(8,128)(2,1)S(1)}, u32[]{:S(2)}, u32[]{:S(2)}) collective-permute-start(bf16[2,16,16,128]{3,2,1,0:T(8,128)(2,1)S(1)} %get-tuple-element.30), channel_id=1, source_target_pairs={{1,5},{3,7},{4,0},{6,2},{9,13},{11,15},{12,8},{14,10},{17,21},{19,... | collective-permute-start | bytes 393224 | tf_op jit(solution)/shard_map/ppermute | solution.py:332
  10.9 4.8 %collective-permute-start.4 = (bf16[2,16,16,128]{3,2,1,0:T(8,128)(2,1)S(1)}, bf16[2,16,16,128]{3,2,1,0:T(8,128)(2,1)S(1)}, u32[]{:S(2)}, u32[]{:S(2)}) collective-permute-start(bf16[2,16,16,128]{3,2,1,0:T(8,128)(2,1)S(1)} %get-tuple-element.31), channel_id=1, source_target_pairs={{0,8},{2,10},{5,13},{7,15},{8,0},{10,2},{13,5},{15,7},{16,24},{18,... | collective-permute-start | bytes 393224 | tf_op jit(solution)/shard_map/ppermute | solution.py:332
  15.7 1.5 %shard_map.85 = (f32[256,128]{1,0:T(8,128)S(1)}, f32[256,128]{1,0:T(8,128)S(1)}, f32[4,256,128]{2,1,0:T(8,128)S(1)}, f32[256,128]{1,0:T(8,128)S(1)}, f32[256,128]{1,0:T(8,128)S(1)}, /*index=5*/f32[256,128]{1,0:T(8,128)S(1)}) custom-call(bf16[16,16,128]{2,1,0:T(8,128)(2,1)} %acts_in.3, s32[16,16]{1,0:T(8,128)} %mask_in.3, s32[1]{0:T(128)S(6)} %copy.8.crop_ref, ...), custom_call_target="tpu_custom_call" | custom-call | flops 50331648 | bytes 1770500 | tf_op jit(solution)/shard_map/pallas_call | solution.py:299
  17.3 2.1 %collective-permute-done.3.tile_ref = bf16[2,16,16,128]{3,2,1,0:T(8,128)(2,1)S(1)} collective-permute-done((bf16[2,16,16,128]{3,2,1,0:T(8,128)(2,1)S(1)}, bf16[2,16,16,128]{3,2,1,0:T(8,128)(2,1)S(1)}, u32[]{:S(2)}, u32[]{:S(2)}) %collective-permute-start.3) | collective-permute-done | bytes 131104 | tf_op jit(solution)/shard_map/ppermute | solution.py:332
  19.4 0.6 %collective-permute-done.4.tile_ref = bf16[2,16,16,128]{3,2,1,0:T(8,128)(2,1)S(1)} collective-permute-done((bf16[2,16,16,128]{3,2,1,0:T(8,128)(2,1)S(1)}, bf16[2,16,16,128]{3,2,1,0:T(8,128)(2,1)S(1)}, u32[]{:S(2)}, u32[]{:S(2)}) %collective-permute-start.4) | collective-permute-done | bytes 131104 | tf_op jit(solution)/shard_map/ppermute | solution.py:332
  20.6 1.3 %collective-permute-start.7 = (bf16[2,16,16,128]{3,2,1,0:T(8,128)(2,1)S(1)}, bf16[2,16,16,128]{3,2,1,0:T(8,128)(2,1)S(1)}, u32[]{:S(2)}, u32[]{:S(2)}) collective-permute-start(bf16[2,16,16,128]{3,2,1,0:T(8,128)(2,1)S(1)} %shard_map.87.same_ref), channel_id=1, source_target_pairs={{0,4},{2,6},{5,1},{7,3},{8,12},{10,14},{13,9},{15,11},{16,20},{18,... | collective-permute-start | bytes 393224 | tf_op jit(solution)/shard_map/ppermute | solution.py:332
  21.9 1.5 %collective-permute-start.8 = (bf16[2,16,16,128]{3,2,1,0:T(8,128)(2,1)S(1)}, bf16[2,16,16,128]{3,2,1,0:T(8,128)(2,1)S(1)}, u32[]{:S(2)}, u32[]{:S(2)}) collective-permute-start(bf16[2,16,16,128]{3,2,1,0:T(8,128)(2,1)S(1)} %shard_map.87.same_ref), channel_id=1, source_target_pairs={{0,12},{2,14},{5,9},{7,11},{8,4},{10,6},{13,1},{15,3},{16,28},{18,... | collective-permute-start | bytes 393224 | tf_op jit(solution)/shard_map/ppermute | solution.py:332
  23.4 3.3 %collective-permute-start.9 = (bf16[2,16,16,128]{3,2,1,0:T(8,128)(2,1)S(1)}, bf16[2,16,16,128]{3,2,1,0:T(8,128)(2,1)S(1)}, u32[]{:S(2)}, u32[]{:S(2)}) collective-permute-start(bf16[2,16,16,128]{3,2,1,0:T(8,128)(2,1)S(1)} %shard_map.87.same_ref), channel_id=1, source_target_pairs={{0,8},{2,10},{5,13},{7,15},{8,0},{10,2},{13,5},{15,7},{16,24},{18,... | collective-permute-start | bytes 393224 | tf_op jit(solution)/shard_map/ppermute | solution.py:332
  26.8 1.2 %collective-permute-done.5.other_ref = bf16[16,16,128]{2,1,0:T(8,128)(2,1)S(1)} collective-permute-done((bf16[16,16,128]{2,1,0:T(8,128)(2,1)S(1)}, bf16[16,16,128]{2,1,0:T(8,128)(2,1)S(1)}, u32[]{:S(2)}, u32[]{:S(2)}) %collective-permute-start.5) | collective-permute-done | bytes 65568 | tf_op jit(solution)/shard_map/ppermute | solution.py:328
  28.0 0.8 %shard_map.86 = (bf16[16,16,128]{2,1,0:T(8,128)(2,1)}, f32[256,128]{1,0:T(8,128)S(1)}) custom-call(bf16[16,16,128]{2,1,0:T(8,128)(2,1)S(1)} %get-tuple-element.32.normed_ref, bf16[16,16,128]{2,1,0:T(8,128)(2,1)S(1)} %collective-permute-done.5.other_ref, f32[256,128]{1,0:T(8,128)S(1)} %get-tuple-element.34.open_ref, ...), custom_call_target="tpu_custom_call" | custom-call | flops 16777216 | bytes 786432 | tf_op jit(solution)/shard_map/pallas_call | solution.py:299
  28.8 0.4 %shard_map.89.refs_0_ = f32[16,16,128]{2,1,0:T(8,128)S(1)} custom-call(bf16[2,16,16,128]{3,2,1,0:T(8,128)(2,1)S(1)} %collective-permute-done.7.differ_ref, bf16[2,16,16,128]{3,2,1,0:T(8,128)(2,1)S(1)} %shard_map.87.same_ref, f32[32,16,128]{2,1,0:T(8,128)S(1)} %shard_map.78.rights, f32[256,128]{1,0:T(8,128)S(1)} %get-tuple-element.40.refs_0_.share_ref, ...), custom_call_target="tpu_custom_call" | custom-call | flops 1048576 | bytes 1048576 | tf_op jit(solution)/shard_map/pallas_call | solution.py:299
  29.3 2.6 %collective-permute-done.9.same_ref = bf16[2,16,16,128]{3,2,1,0:T(8,128)(2,1)S(1)} collective-permute-done((bf16[2,16,16,128]{3,2,1,0:T(8,128)(2,1)S(1)}, bf16[2,16,16,128]{3,2,1,0:T(8,128)(2,1)S(1)}, u32[]{:S(2)}, u32[]{:S(2)}) %collective-permute-start.9) | collective-permute-done | bytes 131104 | tf_op jit(solution)/shard_map/ppermute | solution.py:332
  31.9 0.4 %shard_map.90.refs_1_ = f32[16,16,128]{2,1,0:T(8,128)S(1)} custom-call(bf16[2,16,16,128]{3,2,1,0:T(8,128)(2,1)S(1)} %collective-permute-done.8.differ_ref, bf16[2,16,16,128]{3,2,1,0:T(8,128)(2,1)S(1)} %collective-permute-done.9.same_ref, f32[32,16,128]{2,1,0:T(8,128)S(1)} %shard_map.78.rights, f32[256,128]{1,0:T(8,128)S(1)} %get-tuple-element.40.refs_0_.share_ref, ...), custom_call_target="tpu_custom_call" | custom-call | flops 1048576 | bytes 1048576 | tf_op jit(solution)/shard_map/pallas_call | solution.py:299
  32.4 1.6 %collective-permute-start.10 = (bf16[16,16,128]{2,1,0:T(8,128)(2,1)S(1)}, bf16[16,16,128]{2,1,0:T(8,128)(2,1)S(1)}, u32[]{:S(2)}, u32[]{:S(2)}) collective-permute-start(bf16[16,16,128]{2,1,0:T(8,128)(2,1)S(1)} %get-tuple-element.42), channel_id=1, source_target_pairs={{0,2},{1,3},{2,0},{3,1},{4,6},{5,7},{6,4},{7,5},{8,10},{9,11},{10,... | collective-permute-start | bytes 196616 | tf_op jit(solution)/shard_map/ppermute | solution.py:328
  34.3 0.4 %shard_map.94 = (f32[16,16,128]{2,1,0:T(8,128)S(1)}, bf16[16,16,128]{2,1,0:T(8,128)(2,1)S(1)}) custom-call(f32[32,16,128]{2,1,0:T(8,128)S(1)} %shard_map.88.refs_1_.panel, bf16[2,16,16,128]{3,2,1,0:T(8,128)(2,1)S(1)} %collective-permute-done.9.same_ref, bf16[2,16,16,128]{3,2,1,0:T(8,128)(2,1)S(1)} %collective-permute-done.8.differ_ref, ...), custom_call_target="tpu_custom_call" | custom-call | tf_op jit(solution)/shard_map/pallas_call | solution.py:299
  34.8 1.9 %collective-permute-done.10.tile_ref = bf16[16,16,128]{2,1,0:T(8,128)(2,1)S(1)} collective-permute-done((bf16[16,16,128]{2,1,0:T(8,128)(2,1)S(1)}, bf16[16,16,128]{2,1,0:T(8,128)(2,1)S(1)}, u32[]{:S(2)}, u32[]{:S(2)}) %collective-permute-start.10) | collective-permute-done | bytes 65568 | tf_op jit(solution)/shard_map/ppermute | solution.py:328
  36.7 1.0 %shard_map.95 = bf16[16,16,128]{2,1,0:T(8,128)(2,1)} custom-call(f32[16,16,128]{2,1,0:T(8,128)S(1)} %shard_map.92.left_ref, f32[16,16,128]{2,1,0:T(8,128)S(1)} %get-tuple-element.45.right_ref, bf16[16,16,128]{2,1,0:T(8,128)(2,1)S(1)} %collective-permute-done.11.other_ref, f32[256,128]{1,0:T(8,128)S(1)} %get-tuple-element.47.normed_ref, ...), custom_call_target="tpu_custom_call" | custom-call | flops 33554432 | bytes 1474560 | tf_op jit(solution)/shard_map/pallas_call | solution.py:299
  (23 shorter events, 1.4 us)
Async XLA Ops:
  2.1 3.7 %collective-permute-start = (bf16[16,16,128]{2,1,0:T(8,128)(2,1)S(1)}, bf16[16,16,128]{2,1,0:T(8,128)(2,1)S(1)}, u32[]{:S(2)}, u32[]{:S(2)}) collective-permute-start(bf16[16,16,128]{2,1,0:T(8,128)(2,1)S(1)} %get-tuple-element.27.refs_0_), channel_id=1, source_target_pairs={{0,1},{1,0},{2,3},{3,2},{4,5},{5,4},{6,7},{7,6},{8,9},{9,8},{10,11... | collective-permute-start | bytes 196616 | tf_op jit(solution)/shard_map/ppermute | solution.py:328
  2.6 5.2 %collective-permute-start.1 = (bf16[16,16,128]{2,1,0:T(8,128)(2,1)S(1)}, bf16[16,16,128]{2,1,0:T(8,128)(2,1)S(1)}, u32[]{:S(2)}, u32[]{:S(2)}) collective-permute-start(bf16[16,16,128]{2,1,0:T(8,128)(2,1)S(1)} %get-tuple-element.26.left_ref.refs_0_), channel_id=1, source_target_pairs={{0,2},{1,3},{2,0},{3,1},{4,6},{5,7},{6,4},{7,5},{8,10},{9,11},{10,... | collective-permute-start | bytes 196616 | tf_op jit(solution)/shard_map/ppermute | solution.py:328
  8.3 8.9 %collective-permute-start.2 = (bf16[2,16,16,128]{3,2,1,0:T(8,128)(2,1)S(1)}, bf16[2,16,16,128]{3,2,1,0:T(8,128)(2,1)S(1)}, u32[]{:S(2)}, u32[]{:S(2)}) collective-permute-start(bf16[2,16,16,128]{3,2,1,0:T(8,128)(2,1)S(1)} %get-tuple-element.29), channel_id=1, source_target_pairs={{1,13},{3,15},{4,8},{6,10},{9,5},{11,7},{12,0},{14,2},{17,29},{19,... | collective-permute-start | bytes 393224 | tf_op jit(solution)/shard_map/ppermute | solution.py:332
  9.6 9.8 %collective-permute-start.3 = (bf16[2,16,16,128]{3,2,1,0:T(8,128)(2,1)S(1)}, bf16[2,16,16,128]{3,2,1,0:T(8,128)(2,1)S(1)}, u32[]{:S(2)}, u32[]{:S(2)}) collective-permute-start(bf16[2,16,16,128]{3,2,1,0:T(8,128)(2,1)S(1)} %get-tuple-element.30), channel_id=1, source_target_pairs={{1,5},{3,7},{4,0},{6,2},{9,13},{11,15},{12,8},{14,10},{17,21},{19,... | collective-permute-start | bytes 393224 | tf_op jit(solution)/shard_map/ppermute | solution.py:332
  10.9 9.1 %collective-permute-start.4 = (bf16[2,16,16,128]{3,2,1,0:T(8,128)(2,1)S(1)}, bf16[2,16,16,128]{3,2,1,0:T(8,128)(2,1)S(1)}, u32[]{:S(2)}, u32[]{:S(2)}) collective-permute-start(bf16[2,16,16,128]{3,2,1,0:T(8,128)(2,1)S(1)} %get-tuple-element.31), channel_id=1, source_target_pairs={{0,8},{2,10},{5,13},{7,15},{8,0},{10,2},{13,5},{15,7},{16,24},{18,... | collective-permute-start | bytes 393224 | tf_op jit(solution)/shard_map/ppermute | solution.py:332
  17.2 3.2 %collective-permute-start.6 = (f32[256,128]{1,0:T(8,128)S(1)}, f32[256,128]{1,0:T(8,128)S(1)}, u32[]{:S(2)}, u32[]{:S(2)}) collective-permute-start(f32[256,128]{1,0:T(8,128)S(1)} %get-tuple-element.39.upstream_ref), channel_id=1, source_target_pairs={{0,1},{1,0},{2,3},{3,2},{4,5},{5,4},{6,7},{7,6},{8,9},{9,8},{10,11... | collective-permute-start | bytes 393224 | tf_op jit(solution)/shard_map/ppermute | solution.py:328
  20.6 8.3 %collective-permute-start.7 = (bf16[2,16,16,128]{3,2,1,0:T(8,128)(2,1)S(1)}, bf16[2,16,16,128]{3,2,1,0:T(8,128)(2,1)S(1)}, u32[]{:S(2)}, u32[]{:S(2)}) collective-permute-start(bf16[2,16,16,128]{3,2,1,0:T(8,128)(2,1)S(1)} %shard_map.87.same_ref), channel_id=1, source_target_pairs={{0,4},{2,6},{5,1},{7,3},{8,12},{10,14},{13,9},{15,11},{16,20},{18,... | collective-permute-start | bytes 393224 | tf_op jit(solution)/shard_map/ppermute | solution.py:332
  21.9 7.4 %collective-permute-start.8 = (bf16[2,16,16,128]{3,2,1,0:T(8,128)(2,1)S(1)}, bf16[2,16,16,128]{3,2,1,0:T(8,128)(2,1)S(1)}, u32[]{:S(2)}, u32[]{:S(2)}) collective-permute-start(bf16[2,16,16,128]{3,2,1,0:T(8,128)(2,1)S(1)} %shard_map.87.same_ref), channel_id=1, source_target_pairs={{0,12},{2,14},{5,9},{7,11},{8,4},{10,6},{13,1},{15,3},{16,28},{18,... | collective-permute-start | bytes 393224 | tf_op jit(solution)/shard_map/ppermute | solution.py:332
  23.4 8.5 %collective-permute-start.9 = (bf16[2,16,16,128]{3,2,1,0:T(8,128)(2,1)S(1)}, bf16[2,16,16,128]{3,2,1,0:T(8,128)(2,1)S(1)}, u32[]{:S(2)}, u32[]{:S(2)}) collective-permute-start(bf16[2,16,16,128]{3,2,1,0:T(8,128)(2,1)S(1)} %shard_map.87.same_ref), channel_id=1, source_target_pairs={{0,8},{2,10},{5,13},{7,15},{8,0},{10,2},{13,5},{15,7},{16,24},{18,... | collective-permute-start | bytes 393224 | tf_op jit(solution)/shard_map/ppermute | solution.py:332
  26.7 1.3 %copy-start = (bf16[128,640]{1,0:T(8,128)(2,1)S(1)}, bf16[128,640]{1,0:T(8,128)(2,1)}, u32[]{:S(2)}) copy-start(bf16[128,640]{1,0:T(8,128)(2,1)} %weights_ref.3) | copy-start | bytes 491524
  26.7 1.3 %copy-start.1 = (bf16[128,128]{1,0:T(8,128)(2,1)S(1)}, bf16[128,128]{1,0:T(8,128)(2,1)}, u32[]{:S(2)}) copy-start(bf16[128,128]{1,0:T(8,128)(2,1)} %out_weight_ref.1) | copy-start | bytes 98308
  26.7 1.3 %collective-permute-start.5 = (bf16[16,16,128]{2,1,0:T(8,128)(2,1)S(1)}, bf16[16,16,128]{2,1,0:T(8,128)(2,1)S(1)}, u32[]{:S(2)}, u32[]{:S(2)}) collective-permute-start(bf16[16,16,128]{2,1,0:T(8,128)(2,1)S(1)} %get-tuple-element.33), channel_id=1, source_target_pairs={{0,1},{1,0},{2,3},{3,2},{4,5},{5,4},{6,7},{7,6},{8,9},{9,8},{10,11... | collective-permute-start | bytes 196616 | tf_op jit(solution)/shard_map/ppermute | solution.py:328
  32.4 4.3 %collective-permute-start.10 = (bf16[16,16,128]{2,1,0:T(8,128)(2,1)S(1)}, bf16[16,16,128]{2,1,0:T(8,128)(2,1)S(1)}, u32[]{:S(2)}, u32[]{:S(2)}) collective-permute-start(bf16[16,16,128]{2,1,0:T(8,128)(2,1)S(1)} %get-tuple-element.42), channel_id=1, source_target_pairs={{0,2},{1,3},{2,0},{3,1},{4,6},{5,7},{6,4},{7,5},{8,10},{9,11},{10,... | collective-permute-start | bytes 196616 | tf_op jit(solution)/shard_map/ppermute | solution.py:328
  34.7 2.0 %collective-permute-start.11 = (bf16[16,16,128]{2,1,0:T(8,128)(2,1)S(1)}, bf16[16,16,128]{2,1,0:T(8,128)(2,1)S(1)}, u32[]{:S(2)}, u32[]{:S(2)}) collective-permute-start(bf16[16,16,128]{2,1,0:T(8,128)(2,1)S(1)} %get-tuple-element.46), channel_id=1, source_target_pairs={{0,1},{1,0},{2,3},{3,2},{4,5},{5,4},{6,7},{7,6},{8,9},{9,8},{10,11... | collective-permute-start | bytes 196616 | tf_op jit(solution)/shard_map/ppermute | solution.py:328

commit v12 on v10

--- a/solution.py
+++ b/solution.py
@@ -269,7 +269,7 @@
     work = 2 * size * pairs * channels
     wait = 2**31
     steps = [step for bit in range(n.bit_length() - 2, -1, -1) for step in range(2**bit, 2 ** (bit + 1))]
-    row_steps = [n // 2] + [step for step in range(1, n) if step != n // 2]
+    row_steps = list(range(n - 1, 0, -1))
 
 
     def swap(values, axis, step):

time: 35.5 us -> 35.9 us (1.011)
  waiting for transfers between devices: 11 us -> 11.4 us
    ppermute x12, waiting for transfers between devices: 11 us -> 11.4 us  [swap(): return lax.ppermute(values, axis, [(a, a ^ step) for a in range(n)])]
  transfers between devices with their start and end apart: 12 -> 12, of which waited for: 8 -> 7; matrix products, arithmetic and copies ran while one was open for 0% -> 0% of each run, Pallas kernels for 13% -> 12%
where the time goes in v12:
time: 35.9 us; the launch traced here: 35.7 us
  starting transfers between devices  14.3 us (40%)
  waiting for transfers between devices  11.4 us (32%)
  Pallas kernels  7.82 us (22%)
  between operations  1.44 us (4%)
  local copies, waits for them, and re-layouts  0.71 us (2%)
    ppermute x12, starting transfers between devices, swap(): return lax.ppermute(values, axis, [(a, a ^ step) for a in range(n)])  14.3 us
    ppermute x12, waiting for transfers between devices, swap(): return lax.ppermute(values, axis, [(a, a ^ step) for a in range(n)])  11.4 us
    pallas_call x21, Pallas kernels, call(): pl.pallas_call(kernel, out_shape=tuple(outs), in_specs=specs, out_specs=(...  7.82 us
  transfers between devices with their start and end apart: 12, of which 7 were waited for; matrix products, arithmetic and copies ran while one was open for 0% of the time, Pallas kernels for 12%

profile of v12, /device:TPU:0, one launch (start us, length us, event | category | flops | bytes accessed | tf_op | source)
XLA Modules:
  0.0 35.7 jit_solution(12252269227820405762)
XLA Ops:
  0.6 1.3 %shard_map.77.refs_0_ = bf16[16,16,128]{2,1,0:T(8,128)(2,1)S(1)} custom-call(bf16[16,16,128]{2,1,0:T(8,128)(2,1)} %acts_in.3, s32[16,16]{1,0:T(8,128)} %mask_in.3, bf16[128,640]{1,0:T(8,128)(2,1)} %refs_5_.3), custom_call_target="tpu_custom_call" | custom-call | flops 16777216 | bytes 295936 | tf_op jit(solution)/shard_map/pallas_call | solution.py:249
  2.0 3.0 %collective-permute-start.2 = (bf16[16,16,128]{2,1,0:T(8,128)(2,1)S(1)}, bf16[16,16,128]{2,1,0:T(8,128)(2,1)S(1)}, u32[]{:S(2)}, u32[]{:S(2)}) collective-permute-start(bf16[16,16,128]{2,1,0:T(8,128)(2,1)S(1)} %shard_map.77.refs_0_), channel_id=1, source_target_pairs={{0,2},{1,3},{2,0},{3,1},{4,6},{5,7},{6,4},{7,5},{8,10},{9,11},{10,... | collective-permute-start | bytes 196616 | tf_op jit(solution)/shard_map/ppermute | solution.py:276
  5.8 1.5 %shard_map.78 = (f32[16,16,128]{2,1,0:T(8,128)S(1)}, f32[256,128]{1,0:T(8,128)S(1)}, f32[256,128]{1,0:T(8,128)S(1)}, f32[4,256,128]{2,1,0:T(8,128)S(1)}, f32[256...) custom-call(bf16[16,16,128]{2,1,0:T(8,128)(2,1)} %acts_in.3, s32[16,16]{1,0:T(8,128)} %mask_in.3, ...), custom_call_target="tpu_custom_call" | custom-call | flops 50331648 | bytes 1639428 | tf_op jit(solution)/shard_map/pallas_call | solution.py:249
  7.8 1.4 %collective-permute-done.refs_0_.refs_2_ = bf16[16,16,128]{2,1,0:T(8,128)(2,1)S(1)} collective-permute-done((bf16[16,16,128]{2,1,0:T(8,128)(2,1)S(1)}, bf16[16,16,128]{2,1,0:T(8,128)(2,1)S(1)}, u32[]{:S(2)}, u32[]{:S(2)}) %collective-permute-start) | collective-permute-done | bytes 65568 | tf_op jit(solution)/shard_map/ppermute | solution.py:276
  9.1 0.4 %shard_map.80 = (f32[16,16,128]{2,1,0:T(8,128)S(1)}, f32[16,16,128]{2,1,0:T(8,128)S(1)}) custom-call(s32[1]{0:T(128)S(6)} %copy.8.crop_ref, bf16[16,16,128]{2,1,0:T(8,128)(2,1)S(1)} %collective-permute-done.refs_0_.refs_2_, bf16[16,16,128]{2,1,0:T(8,128)(2,1)S(1)} %collective-permute-done.1.refs_1_.refs_3_, ...), custom_call_target="tpu_custom_call" | custom-call | flops 1048576 | bytes 524292 | tf_op jit(solution)/shard_map/pallas_call | solution.py:249
  9.6 3.7 %collective-permute-start.3 = (bf16[16,16,128]{2,1,0:T(8,128)(2,1)S(1)}, bf16[16,16,128]{2,1,0:T(8,128)(2,1)S(1)}, u32[]{:S(2)}, u32[]{:S(2)}) collective-permute-start(bf16[16,16,128]{2,1,0:T(8,128)(2,1)S(1)} %get-tuple-element.30), channel_id=1, source_target_pairs={{0,12},{4,8},{8,4},{12,0},{1,13},{5,9},{9,5},{13,1},{2,14},{6,10},... | collective-permute-start | bytes 196616 | tf_op jit(solution)/shard_map/ppermute | solution.py:276
  13.4 0.7 %collective-permute-start.5 = (bf16[16,16,128]{2,1,0:T(8,128)(2,1)S(1)}, bf16[16,16,128]{2,1,0:T(8,128)(2,1)S(1)}, u32[]{:S(2)}, u32[]{:S(2)}) collective-permute-start(bf16[16,16,128]{2,1,0:T(8,128)(2,1)S(1)} %get-tuple-element.32), channel_id=1, source_target_pairs={{0,4},{4,0},{8,12},{12,8},{1,5},{5,1},{9,13},{13,9},{2,6},{6,2},{1... | collective-permute-start | bytes 196616 | tf_op jit(solution)/shard_map/ppermute | solution.py:276
  14.1 2.1 %collective-permute-done.3.tile_ref = bf16[16,16,128]{2,1,0:T(8,128)(2,1)S(1)} collective-permute-done((bf16[16,16,128]{2,1,0:T(8,128)(2,1)S(1)}, bf16[16,16,128]{2,1,0:T(8,128)(2,1)S(1)}, u32[]{:S(2)}, u32[]{:S(2)}) %collective-permute-start.3) | collective-permute-done | bytes 65568 | tf_op jit(solution)/shard_map/ppermute | solution.py:276
  16.2 2.8 %collective-permute-done.4.tile_ref = bf16[16,16,128]{2,1,0:T(8,128)(2,1)S(1)} collective-permute-done((bf16[16,16,128]{2,1,0:T(8,128)(2,1)S(1)}, bf16[16,16,128]{2,1,0:T(8,128)(2,1)S(1)}, u32[]{:S(2)}, u32[]{:S(2)}) %collective-permute-start.4) | collective-permute-done | bytes 65568 | tf_op jit(solution)/shard_map/ppermute | solution.py:276
  19.1 0.3 shard_map.85
  19.3 2.7 %collective-permute-start.8 = (bf16[16,16,128]{2,1,0:T(8,128)(2,1)S(1)}, bf16[16,16,128]{2,1,0:T(8,128)(2,1)S(1)}, u32[]{:S(2)}, u32[]{:S(2)}) collective-permute-start(bf16[16,16,128]{2,1,0:T(8,128)(2,1)S(1)} %get-tuple-element.38.refs_0_.grad_ref), channel_id=1, source_target_pairs={{0,12},{4,8},{8,4},{12,0},{1,13},{5,9},{9,5},{13,1},{2,14},{6,10},... | collective-permute-start | bytes 196616 | tf_op jit(solution)/shard_map/ppermute | solution.py:276
  22.1 1.7 %collective-permute-start.6 = (bf16[16,16,128]{2,1,0:T(8,128)(2,1)S(1)}, bf16[16,16,128]{2,1,0:T(8,128)(2,1)S(1)}, u32[]{:S(2)}, u32[]{:S(2)}) collective-permute-start(bf16[16,16,128]{2,1,0:T(8,128)(2,1)S(1)} %get-tuple-element.38.refs_0_.grad_ref), channel_id=1, source_target_pairs={{0,4},{4,0},{8,12},{12,8},{1,5},{5,1},{9,13},{13,9},{2,6},{6,2},{1... | collective-permute-start | bytes 196616 | tf_op jit(solution)/shard_map/ppermute | solution.py:276
  24.1 0.7 %copy-done = bf16[128,640]{1,0:T(8,128)(2,1)S(1)} copy-done((bf16[128,640]{1,0:T(8,128)(2,1)S(1)}, bf16[128,640]{1,0:T(8,128)(2,1)}, u32[]{:S(2)}) %copy-start) | copy-done | bytes 163864
  24.8 0.8 %shard_map.86 = (bf16[16,16,128]{2,1,0:T(8,128)(2,1)}, f32[256,128]{1,0:T(8,128)S(1)}) custom-call(f32[256,128]{1,0:T(8,128)S(1)} %get-tuple-element.34.tri_normed_ref, f32[256,128]{1,0:T(8,128)S(1)} %get-tuple-element.35.open_ref, f32[256,128]{1,0:T(8,128)S(1)} %get-tuple-element.36.gate_factor_ref, bf16[128,640]{1,0:T(8,128)(2,1)S(1)} %copy-done, ...), custom_call_target="tpu_custom_call" | custom-call | flops 16777216 | bytes 786432 | tf_op jit(solution)/shard_map/pallas_call | solution.py:249
  25.6 0.2 shard_map.89.refs_0_
  25.9 0.2 shard_map.92.refs_3_
  26.2 2.2 %collective-permute-done.7.grad_ref.refs_1_ = bf16[16,16,128]{2,1,0:T(8,128)(2,1)S(1)} collective-permute-done((bf16[16,16,128]{2,1,0:T(8,128)(2,1)S(1)}, bf16[16,16,128]{2,1,0:T(8,128)(2,1)S(1)}, u32[]{:S(2)}, u32[]{:S(2)}) %collective-permute-start.7) | collective-permute-done | bytes 65568 | tf_op jit(solution)/shard_map/ppermute | solution.py:276
  28.6 0.2 shard_map.90.refs_1_
  29.0 1.4 %collective-permute-start.9 = (bf16[16,16,128]{2,1,0:T(8,128)(2,1)S(1)}, bf16[16,16,128]{2,1,0:T(8,128)(2,1)S(1)}, u32[]{:S(2)}, u32[]{:S(2)}) collective-permute-start(bf16[16,16,128]{2,1,0:T(8,128)(2,1)S(1)} %get-tuple-element.42), channel_id=1, source_target_pairs={{0,2},{1,3},{2,0},{3,1},{4,6},{5,7},{6,4},{7,5},{8,10},{9,11},{10,... | collective-permute-start | bytes 196616 | tf_op jit(solution)/shard_map/ppermute | solution.py:276
  30.4 0.8 %collective-permute-start.11 = (bf16[16,16,128]{2,1,0:T(8,128)(2,1)S(1)}, bf16[16,16,128]{2,1,0:T(8,128)(2,1)S(1)}, u32[]{:S(2)}, u32[]{:S(2)}) collective-permute-start(bf16[16,16,128]{2,1,0:T(8,128)(2,1)S(1)} %get-tuple-element.44), channel_id=1, source_target_pairs={{0,1},{1,0},{2,3},{3,2},{4,5},{5,4},{6,7},{7,6},{8,9},{9,8},{10,11... | collective-permute-start | bytes 196616 | tf_op jit(solution)/shard_map/ppermute | solution.py:276
  31.2 0.7 %shard_map.96.refs_4_ = f32[256,128]{1,0:T(8,128)S(1)} custom-call(f32[64,16,128]{2,1,0:T(8,128)S(1)} %shard_map.87.panel, bf16[16,16,128]{2,1,0:T(8,128)(2,1)S(1)} %collective-permute-done.8.grad_ref.refs_0_, bf16[16,16,128]{2,1,0:T(8,128)(2,1)S(1)} %collective-permute-done.7.grad_ref.refs_1_, ...), custom_call_target="tpu_custom_call" | custom-call | tf_op jit(solution)/shard_map/pallas_call | solution.py:249
  31.9 1.4 %collective-permute-done.9.tile_ref = bf16[16,16,128]{2,1,0:T(8,128)(2,1)S(1)} collective-permute-done((bf16[16,16,128]{2,1,0:T(8,128)(2,1)S(1)}, bf16[16,16,128]{2,1,0:T(8,128)(2,1)S(1)}, u32[]{:S(2)}, u32[]{:S(2)}) %collective-permute-start.9) | collective-permute-done | bytes 65568 | tf_op jit(solution)/shard_map/ppermute | solution.py:276
  33.3 1.4 %collective-permute-done.10.tile_ref = bf16[16,16,128]{2,1,0:T(8,128)(2,1)S(1)} collective-permute-done((bf16[16,16,128]{2,1,0:T(8,128)(2,1)S(1)}, bf16[16,16,128]{2,1,0:T(8,128)(2,1)S(1)}, u32[]{:S(2)}, u32[]{:S(2)}) %collective-permute-start.10) | collective-permute-done | bytes 65568 | tf_op jit(solution)/shard_map/ppermute | solution.py:276
  34.7 0.9 %shard_map.97 = bf16[16,16,128]{2,1,0:T(8,128)(2,1)} custom-call(f32[16,16,128]{2,1,0:T(8,128)S(1)} %shard_map.95.base, bf16[16,16,128]{2,1,0:T(8,128)(2,1)S(1)} %collective-permute-done.11.refs_0_, f32[256,128]{1,0:T(8,128)S(1)} %get-tuple-element.45.refs_1_, f32[256,128]{1,0:T(8,128)S(1)} %get-tuple-element.46.refs_2_, ...), custom_call_target="tpu_custom_call" | custom-call | flops 16777216 | bytes 1343488 | tf_op jit(solution)/shard_map/pallas_call | solution.py:249
  (25 shorter events, 1.5 us)
Async XLA Ops:
  2.0 5.6 %collective-permute-start.2 = (bf16[16,16,128]{2,1,0:T(8,128)(2,1)S(1)}, bf16[16,16,128]{2,1,0:T(8,128)(2,1)S(1)}, u32[]{:S(2)}, u32[]{:S(2)}) collective-permute-start(bf16[16,16,128]{2,1,0:T(8,128)(2,1)S(1)} %shard_map.77.refs_0_), channel_id=1, source_target_pairs={{0,2},{1,3},{2,0},{3,1},{4,6},{5,7},{6,4},{7,5},{8,10},{9,11},{10,... | collective-permute-start | bytes 196616 | tf_op jit(solution)/shard_map/ppermute | solution.py:276
  5.0 4.1 %collective-permute-start = (bf16[16,16,128]{2,1,0:T(8,128)(2,1)S(1)}, bf16[16,16,128]{2,1,0:T(8,128)(2,1)S(1)}, u32[]{:S(2)}, u32[]{:S(2)}) collective-permute-start(bf16[16,16,128]{2,1,0:T(8,128)(2,1)S(1)} %shard_map.77.refs_0_), channel_id=1, source_target_pairs={{0,3},{1,2},{2,1},{3,0},{4,7},{5,6},{6,5},{7,4},{8,11},{9,10},{10,... | collective-permute-start | bytes 196616 | tf_op jit(solution)/shard_map/ppermute | solution.py:276
  5.0 4.1 %collective-permute-start.1 = (bf16[16,16,128]{2,1,0:T(8,128)(2,1)S(1)}, bf16[16,16,128]{2,1,0:T(8,128)(2,1)S(1)}, u32[]{:S(2)}, u32[]{:S(2)}) collective-permute-start(bf16[16,16,128]{2,1,0:T(8,128)(2,1)S(1)} %shard_map.77.refs_0_), channel_id=1, source_target_pairs={{0,1},{1,0},{2,3},{3,2},{4,5},{5,4},{6,7},{7,6},{8,9},{9,8},{10,11... | collective-permute-start | bytes 196616 | tf_op jit(solution)/shard_map/ppermute | solution.py:276
  9.6 6.6 %collective-permute-start.3 = (bf16[16,16,128]{2,1,0:T(8,128)(2,1)S(1)}, bf16[16,16,128]{2,1,0:T(8,128)(2,1)S(1)}, u32[]{:S(2)}, u32[]{:S(2)}) collective-permute-start(bf16[16,16,128]{2,1,0:T(8,128)(2,1)S(1)} %get-tuple-element.30), channel_id=1, source_target_pairs={{0,12},{4,8},{8,4},{12,0},{1,13},{5,9},{9,5},{13,1},{2,14},{6,10},... | collective-permute-start | bytes 196616 | tf_op jit(solution)/shard_map/ppermute | solution.py:276
  13.3 5.7 %collective-permute-start.4 = (bf16[16,16,128]{2,1,0:T(8,128)(2,1)S(1)}, bf16[16,16,128]{2,1,0:T(8,128)(2,1)S(1)}, u32[]{:S(2)}, u32[]{:S(2)}) collective-permute-start(bf16[16,16,128]{2,1,0:T(8,128)(2,1)S(1)} %get-tuple-element.31), channel_id=1, source_target_pairs={{0,8},{4,12},{8,0},{12,4},{1,9},{5,13},{9,1},{13,5},{2,10},{6,14},... | collective-permute-start | bytes 196616 | tf_op jit(solution)/shard_map/ppermute | solution.py:276
  13.4 5.7 %collective-permute-start.5 = (bf16[16,16,128]{2,1,0:T(8,128)(2,1)S(1)}, bf16[16,16,128]{2,1,0:T(8,128)(2,1)S(1)}, u32[]{:S(2)}, u32[]{:S(2)}) collective-permute-start(bf16[16,16,128]{2,1,0:T(8,128)(2,1)S(1)} %get-tuple-element.32), channel_id=1, source_target_pairs={{0,4},{4,0},{8,12},{12,8},{1,5},{5,1},{9,13},{13,9},{2,6},{6,2},{1... | collective-permute-start | bytes 196616 | tf_op jit(solution)/shard_map/ppermute | solution.py:276
  19.3 6.6 %collective-permute-start.8 = (bf16[16,16,128]{2,1,0:T(8,128)(2,1)S(1)}, bf16[16,16,128]{2,1,0:T(8,128)(2,1)S(1)}, u32[]{:S(2)}, u32[]{:S(2)}) collective-permute-start(bf16[16,16,128]{2,1,0:T(8,128)(2,1)S(1)} %get-tuple-element.38.refs_0_.grad_ref), channel_id=1, source_target_pairs={{0,12},{4,8},{8,4},{12,0},{1,13},{5,9},{9,5},{13,1},{2,14},{6,10},... | collective-permute-start | bytes 196616 | tf_op jit(solution)/shard_map/ppermute | solution.py:276
  22.1 6.3 %collective-permute-start.7 = (bf16[16,16,128]{2,1,0:T(8,128)(2,1)S(1)}, bf16[16,16,128]{2,1,0:T(8,128)(2,1)S(1)}, u32[]{:S(2)}, u32[]{:S(2)}) collective-permute-start(bf16[16,16,128]{2,1,0:T(8,128)(2,1)S(1)} %get-tuple-element.38.refs_0_.grad_ref), channel_id=1, source_target_pairs={{0,8},{4,12},{8,0},{12,4},{1,9},{5,13},{9,1},{13,5},{2,10},{6,14},... | collective-permute-start | bytes 196616 | tf_op jit(solution)/shard_map/ppermute | solution.py:276
  22.1 6.5 %collective-permute-start.6 = (bf16[16,16,128]{2,1,0:T(8,128)(2,1)S(1)}, bf16[16,16,128]{2,1,0:T(8,128)(2,1)S(1)}, u32[]{:S(2)}, u32[]{:S(2)}) collective-permute-start(bf16[16,16,128]{2,1,0:T(8,128)(2,1)S(1)} %get-tuple-element.38.refs_0_.grad_ref), channel_id=1, source_target_pairs={{0,4},{4,0},{8,12},{12,8},{1,5},{5,1},{9,13},{13,9},{2,6},{6,2},{1... | collective-permute-start | bytes 196616 | tf_op jit(solution)/shard_map/ppermute | solution.py:276
  23.9 0.9 %copy-start = (bf16[128,640]{1,0:T(8,128)(2,1)S(1)}, bf16[128,640]{1,0:T(8,128)(2,1)}, u32[]{:S(2)}) copy-start(bf16[128,640]{1,0:T(8,128)(2,1)} %refs_5_.3) | copy-start | bytes 491524
  23.9 0.9 %copy-start.1 = (bf16[128,128]{1,0:T(8,128)(2,1)S(1)}, bf16[128,128]{1,0:T(8,128)(2,1)}, u32[]{:S(2)}) copy-start(bf16[128,128]{1,0:T(8,128)(2,1)} %out_weight_ref.1) | copy-start | bytes 98308
  29.0 4.3 %collective-permute-start.9 = (bf16[16,16,128]{2,1,0:T(8,128)(2,1)S(1)}, bf16[16,16,128]{2,1,0:T(8,128)(2,1)S(1)}, u32[]{:S(2)}, u32[]{:S(2)}) collective-permute-start(bf16[16,16,128]{2,1,0:T(8,128)(2,1)S(1)} %get-tuple-element.42), channel_id=1, source_target_pairs={{0,2},{1,3},{2,0},{3,1},{4,6},{5,7},{6,4},{7,5},{8,10},{9,11},{10,... | collective-permute-start | bytes 196616 | tf_op jit(solution)/shard_map/ppermute | solution.py:276
  30.4 4.3 %collective-permute-start.10 = (bf16[16,16,128]{2,1,0:T(8,128)(2,1)S(1)}, bf16[16,16,128]{2,1,0:T(8,128)(2,1)S(1)}, u32[]{:S(2)}, u32[]{:S(2)}) collective-permute-start(bf16[16,16,128]{2,1,0:T(8,128)(2,1)S(1)} %get-tuple-element.43), channel_id=1, source_target_pairs={{0,3},{1,2},{2,1},{3,0},{4,7},{5,6},{6,5},{7,4},{8,11},{9,10},{10,... | collective-permute-start | bytes 196616 | tf_op jit(solution)/shard_map/ppermute | solution.py:276
  30.4 4.3 %collective-permute-start.11 = (bf16[16,16,128]{2,1,0:T(8,128)(2,1)S(1)}, bf16[16,16,128]{2,1,0:T(8,128)(2,1)S(1)}, u32[]{:S(2)}, u32[]{:S(2)}) collective-permute-start(bf16[16,16,128]{2,1,0:T(8,128)(2,1)S(1)} %get-tuple-element.44), channel_id=1, source_target_pairs={{0,1},{1,0},{2,3},{3,2},{4,5},{5,4},{6,7},{7,6},{8,9},{9,8},{10,11... | collective-permute-start | bytes 196616 | tf_op jit(solution)/shard_map/ppermute | solution.py:276

commit v13 on v8

--- a/solution.py
+++ b/solution.py
@@ -319,8 +319,9 @@
     (grad_panel,) = call(
         functools.partial(panel_kernel, "row", [0] + row_steps), (jax.ShapeDtypeStruct((n * pairs, channels), f32),), *grads
     )
+    last_steps = list(range(n - 1, 0, -1))
     terms = {}
-    for group in (steps, [0]):
+    for group in (last_steps, [0]):
         if terms:
             right, terms[last] = lax.optimization_barrier((right, terms[last]))
         last = group[-1]
@@ -330,9 +331,9 @@
         )
         terms.update(zip(group, outs))
     total, last = terms[0], []
-    for step in steps:
+    for step in last_steps:
         term = swap(terms[step], "col", step)
-        if step == steps[-1]:
+        if step == last_steps[-1]:
             last.append(term)
         else:
             (total,) = call(add_kernel, (wide,), total, term, flops=wait)

time: 35.5 us -> 35.2 us (level)
  no operation moved by 1% of the time
where the time goes in v13:
time: 35.2 us; the launch traced here: 35.1 us
  starting transfers between devices  14.2 us (40%)
  waiting for transfers between devices  11.9 us (34%)
  Pallas kernels  7.58 us (22%)
  between operations  1.42 us (4%)
    ppermute x12, starting transfers between devices, swap(): return lax.ppermute(values, axis, [(a, a ^ step) for a in range(n)])  14.2 us
    ppermute x12, waiting for transfers between devices, swap(): return lax.ppermute(values, axis, [(a, a ^ step) for a in range(n)])  11.9 us
    pallas_call x19, Pallas kernels, call(): pl.pallas_call(kernel, out_shape=tuple(outs), in_specs=specs, out_specs=(...  7.58 us
  transfers between devices with their start and end apart: 12, of which 8 were waited for; matrix products, arithmetic and copies ran while one was open for 0% of the time, Pallas kernels for 11%

profile of v13, /device:TPU:0, one launch (start us, length us, event | category | flops | bytes accessed | tf_op | source)
XLA Modules:
  0.0 35.1 jit_solution(7079004897067950927)
XLA Ops:
  0.6 1.3 %shard_map.77.refs_0_ = bf16[16,16,128]{2,1,0:T(8,128)(2,1)S(1)} custom-call(bf16[16,16,128]{2,1,0:T(8,128)(2,1)} %acts_in.3, s32[16,16]{1,0:T(8,128)} %mask_in.3, bf16[128,640]{1,0:T(8,128)(2,1)} %refs_5_.3), custom_call_target="tpu_custom_call" | custom-call | flops 16777216 | bytes 295936 | tf_op jit(solution)/shard_map/pallas_call | solution.py:239
  2.0 3.0 %collective-permute-start = (bf16[16,16,128]{2,1,0:T(8,128)(2,1)S(1)}, bf16[16,16,128]{2,1,0:T(8,128)(2,1)S(1)}, u32[]{:S(2)}, u32[]{:S(2)}) collective-permute-start(bf16[16,16,128]{2,1,0:T(8,128)(2,1)S(1)} %shard_map.77.refs_0_), channel_id=1, source_target_pairs={{0,2},{1,3},{2,0},{3,1},{4,6},{5,7},{6,4},{7,5},{8,10},{9,11},{10,... | collective-permute-start | bytes 196616 | tf_op jit(solution)/shard_map/ppermute | solution.py:266
  5.8 1.5 %shard_map.79 = (f32[16,16,128]{2,1,0:T(8,128)S(1)}, f32[256,128]{1,0:T(8,128)S(1)}, f32[256,128]{1,0:T(8,128)S(1)}, f32[4,256,128]{2,1,0:T(8,128)S(1)}, f32[256...) custom-call(bf16[16,16,128]{2,1,0:T(8,128)(2,1)} %acts_in.3, s32[16,16]{1,0:T(8,128)} %mask_in.3, ...), custom_call_target="tpu_custom_call" | custom-call | flops 50331648 | bytes 1639428 | tf_op jit(solution)/shard_map/pallas_call | solution.py:239
  7.3 1.8 %collective-permute-done.1.refs_2_ = bf16[16,16,128]{2,1,0:T(8,128)(2,1)S(1)} collective-permute-done((bf16[16,16,128]{2,1,0:T(8,128)(2,1)S(1)}, bf16[16,16,128]{2,1,0:T(8,128)(2,1)S(1)}, u32[]{:S(2)}, u32[]{:S(2)}) %collective-permute-start.1) | collective-permute-done | bytes 65568 | tf_op jit(solution)/shard_map/ppermute | solution.py:266
  9.5 2.7 %collective-permute-start.3 = (bf16[16,16,128]{2,1,0:T(8,128)(2,1)S(1)}, bf16[16,16,128]{2,1,0:T(8,128)(2,1)S(1)}, u32[]{:S(2)}, u32[]{:S(2)}) collective-permute-start(bf16[16,16,128]{2,1,0:T(8,128)(2,1)S(1)} %shard_map.81), channel_id=1, source_target_pairs={{0,8},{4,12},{8,0},{12,4},{1,9},{5,13},{9,1},{13,5},{2,10},{6,14},... | collective-permute-start | bytes 196616 | tf_op jit(solution)/shard_map/ppermute | solution.py:266
  12.4 1.6 %collective-permute-start.4 = (bf16[16,16,128]{2,1,0:T(8,128)(2,1)S(1)}, bf16[16,16,128]{2,1,0:T(8,128)(2,1)S(1)}, u32[]{:S(2)}, u32[]{:S(2)}) collective-permute-start(bf16[16,16,128]{2,1,0:T(8,128)(2,1)S(1)} %shard_map.83), channel_id=1, source_target_pairs={{0,4},{4,0},{8,12},{12,8},{1,5},{5,1},{9,13},{13,9},{2,6},{6,2},{1... | collective-permute-start | bytes 196616 | tf_op jit(solution)/shard_map/ppermute | solution.py:266
  14.2 0.2 collective-permute-start.5
  14.6 1.1 %collective-permute-done.3.tile_ref = bf16[16,16,128]{2,1,0:T(8,128)(2,1)S(1)} collective-permute-done((bf16[16,16,128]{2,1,0:T(8,128)(2,1)S(1)}, bf16[16,16,128]{2,1,0:T(8,128)(2,1)S(1)}, u32[]{:S(2)}, u32[]{:S(2)}) %collective-permute-start.3) | collective-permute-done | bytes 65568 | tf_op jit(solution)/shard_map/ppermute | solution.py:266
  15.8 0.9 %collective-permute-done.4.tile_ref = bf16[16,16,128]{2,1,0:T(8,128)(2,1)S(1)} collective-permute-done((bf16[16,16,128]{2,1,0:T(8,128)(2,1)S(1)}, bf16[16,16,128]{2,1,0:T(8,128)(2,1)S(1)}, u32[]{:S(2)}, u32[]{:S(2)}) %collective-permute-start.4) | collective-permute-done | bytes 65568 | tf_op jit(solution)/shard_map/ppermute | solution.py:266
  16.7 3.6 %collective-permute-done.5.tile_ref = bf16[16,16,128]{2,1,0:T(8,128)(2,1)S(1)} collective-permute-done((bf16[16,16,128]{2,1,0:T(8,128)(2,1)S(1)}, bf16[16,16,128]{2,1,0:T(8,128)(2,1)S(1)}, u32[]{:S(2)}, u32[]{:S(2)}) %collective-permute-start.5) | collective-permute-done | bytes 65568 | tf_op jit(solution)/shard_map/ppermute | solution.py:266
  20.3 0.3 shard_map.86
  20.6 0.9 %collective-permute-start.6 = (bf16[16,16,128]{2,1,0:T(8,128)(2,1)S(1)}, bf16[16,16,128]{2,1,0:T(8,128)(2,1)S(1)}, u32[]{:S(2)}, u32[]{:S(2)}) collective-permute-start(bf16[16,16,128]{2,1,0:T(8,128)(2,1)S(1)} %get-tuple-element.27.refs_0_), channel_id=1, source_target_pairs={{0,8},{4,12},{8,0},{12,4},{1,9},{5,13},{9,1},{13,5},{2,10},{6,14},... | collective-permute-start | bytes 196616 | tf_op jit(solution)/shard_map/ppermute | solution.py:266
  21.6 0.5 %collective-permute-start.7 = (bf16[16,16,128]{2,1,0:T(8,128)(2,1)S(1)}, bf16[16,16,128]{2,1,0:T(8,128)(2,1)S(1)}, u32[]{:S(2)}, u32[]{:S(2)}) collective-permute-start(bf16[16,16,128]{2,1,0:T(8,128)(2,1)S(1)} %get-tuple-element.27.refs_0_), channel_id=1, source_target_pairs={{0,4},{4,0},{8,12},{12,8},{1,5},{5,1},{9,13},{13,9},{2,6},{6,2},{1... | collective-permute-start | bytes 196616 | tf_op jit(solution)/shard_map/ppermute | solution.py:266
  22.1 3.0 %collective-permute-start.8 = (bf16[16,16,128]{2,1,0:T(8,128)(2,1)S(1)}, bf16[16,16,128]{2,1,0:T(8,128)(2,1)S(1)}, u32[]{:S(2)}, u32[]{:S(2)}) collective-permute-start(bf16[16,16,128]{2,1,0:T(8,128)(2,1)S(1)} %get-tuple-element.27.refs_0_), channel_id=1, source_target_pairs={{0,12},{4,8},{8,4},{12,0},{1,13},{5,9},{9,5},{13,1},{2,14},{6,10},... | collective-permute-start | bytes 196616 | tf_op jit(solution)/shard_map/ppermute | solution.py:266
  25.3 0.8 %shard_map.87 = (bf16[16,16,128]{2,1,0:T(8,128)(2,1)}, f32[256,128]{1,0:T(8,128)S(1)}) custom-call(f32[256,128]{1,0:T(8,128)S(1)} %get-tuple-element.23.tri_normed_ref, f32[256,128]{1,0:T(8,128)S(1)} %get-tuple-element.24.open_ref, f32[256,128]{1,0:T(8,128)S(1)} %get-tuple-element.25.gate_factor_ref, bf16[128,640]{1,0:T(8,128)(2,1)S(1)} %copy-done, ...), custom_call_target="tpu_custom_call" | custom-call | flops 16777216 | bytes 786432 | tf_op jit(solution)/shard_map/pallas_call | solution.py:239
  26.1 1.1 %collective-permute-done.6.refs_1_.refs_0_ = bf16[16,16,128]{2,1,0:T(8,128)(2,1)S(1)} collective-permute-done((bf16[16,16,128]{2,1,0:T(8,128)(2,1)S(1)}, bf16[16,16,128]{2,1,0:T(8,128)(2,1)S(1)}, u32[]{:S(2)}, u32[]{:S(2)}) %collective-permute-start.6) | collective-permute-done | bytes 65568 | tf_op jit(solution)/shard_map/ppermute | solution.py:266
  27.2 1.0 %collective-permute-done.8.refs_3_.refs_2_ = bf16[16,16,128]{2,1,0:T(8,128)(2,1)S(1)} collective-permute-done((bf16[16,16,128]{2,1,0:T(8,128)(2,1)S(1)}, bf16[16,16,128]{2,1,0:T(8,128)(2,1)S(1)}, u32[]{:S(2)}, u32[]{:S(2)}) %collective-permute-start.8) | collective-permute-done | bytes 65568 | tf_op jit(solution)/shard_map/ppermute | solution.py:266
  28.3 0.6 %shard_map.90 = (bf16[16,16,128]{2,1,0:T(8,128)(2,1)S(1)}, bf16[16,16,128]{2,1,0:T(8,128)(2,1)S(1)}, bf16[16,16,128]{2,1,0:T(8,128)(2,1)S(1)}) custom-call(f32[1024,128]{1,0:T(8,128)S(1)} %shard_map.88.panel, f32[16,16,128]{2,1,0:T(8,128)S(1)} %get-tuple-element.31.right_ref.right), custom_call_target="tpu_custom_call" | custom-call | flops 1048576 | bytes 851968 | tf_op jit(solution)/shard_map/pallas_call | solution.py:239
  29.0 1.1 %collective-permute-start.10 = (bf16[16,16,128]{2,1,0:T(8,128)(2,1)S(1)}, bf16[16,16,128]{2,1,0:T(8,128)(2,1)S(1)}, u32[]{:S(2)}, u32[]{:S(2)}) collective-permute-start(bf16[16,16,128]{2,1,0:T(8,128)(2,1)S(1)} %get-tuple-element.33), channel_id=1, source_target_pairs={{0,2},{1,3},{2,0},{3,1},{4,6},{5,7},{6,4},{7,5},{8,10},{9,11},{10,... | collective-permute-start | bytes 196616 | tf_op jit(solution)/shard_map/ppermute | solution.py:266
  30.1 0.7 %collective-permute-start.11 = (bf16[16,16,128]{2,1,0:T(8,128)(2,1)S(1)}, bf16[16,16,128]{2,1,0:T(8,128)(2,1)S(1)}, u32[]{:S(2)}, u32[]{:S(2)}) collective-permute-start(bf16[16,16,128]{2,1,0:T(8,128)(2,1)S(1)} %get-tuple-element.34), channel_id=1, source_target_pairs={{0,1},{1,0},{2,3},{3,2},{4,5},{5,4},{6,7},{7,6},{8,9},{9,8},{10,11... | collective-permute-start | bytes 196616 | tf_op jit(solution)/shard_map/ppermute | solution.py:266
  30.9 0.7 %shard_map.94.refs_4_ = f32[256,128]{1,0:T(8,128)S(1)} custom-call(f32[64,16,128]{2,1,0:T(8,128)S(1)} %shard_map.78.panel, bf16[16,16,128]{2,1,0:T(8,128)(2,1)S(1)} %collective-permute-done.6.refs_1_.refs_0_, bf16[16,16,128]{2,1,0:T(8,128)(2,1)S(1)} %collective-permute-done.7.refs_2_.refs_1_, ...), custom_call_target="tpu_custom_call" | custom-call | tf_op jit(solution)/shard_map/pallas_call | solution.py:239
  31.8 1.5 %collective-permute-done.9.tile_ref = bf16[16,16,128]{2,1,0:T(8,128)(2,1)S(1)} collective-permute-done((bf16[16,16,128]{2,1,0:T(8,128)(2,1)S(1)}, bf16[16,16,128]{2,1,0:T(8,128)(2,1)S(1)}, u32[]{:S(2)}, u32[]{:S(2)}) %collective-permute-start.9) | collective-permute-done | bytes 65568 | tf_op jit(solution)/shard_map/ppermute | solution.py:266
  33.3 0.8 %collective-permute-done.10.tile_ref = bf16[16,16,128]{2,1,0:T(8,128)(2,1)S(1)} collective-permute-done((bf16[16,16,128]{2,1,0:T(8,128)(2,1)S(1)}, bf16[16,16,128]{2,1,0:T(8,128)(2,1)S(1)}, u32[]{:S(2)}, u32[]{:S(2)}) %collective-permute-start.10) | collective-permute-done | bytes 65568 | tf_op jit(solution)/shard_map/ppermute | solution.py:266
  34.1 0.9 %shard_map.95 = bf16[16,16,128]{2,1,0:T(8,128)(2,1)} custom-call(f32[16,16,128]{2,1,0:T(8,128)S(1)} %shard_map.93.base, bf16[16,16,128]{2,1,0:T(8,128)(2,1)S(1)} %collective-permute-done.11.refs_0_, f32[256,128]{1,0:T(8,128)S(1)} %get-tuple-element.35.refs_1_, f32[256,128]{1,0:T(8,128)S(1)} %get-tuple-element.36.refs_2_, ...), custom_call_target="tpu_custom_call" | custom-call | flops 16777216 | bytes 1343488 | tf_op jit(solution)/shard_map/pallas_call | solution.py:239
  (23 shorter events, 1.7 us)
Async XLA Ops:
  2.0 5.3 %collective-permute-start = (bf16[16,16,128]{2,1,0:T(8,128)(2,1)S(1)}, bf16[16,16,128]{2,1,0:T(8,128)(2,1)S(1)}, u32[]{:S(2)}, u32[]{:S(2)}) collective-permute-start(bf16[16,16,128]{2,1,0:T(8,128)(2,1)S(1)} %shard_map.77.refs_0_), channel_id=1, source_target_pairs={{0,2},{1,3},{2,0},{3,1},{4,6},{5,7},{6,4},{7,5},{8,10},{9,11},{10,... | collective-permute-start | bytes 196616 | tf_op jit(solution)/shard_map/ppermute | solution.py:266
  5.0 4.1 %collective-permute-start.1 = (bf16[16,16,128]{2,1,0:T(8,128)(2,1)S(1)}, bf16[16,16,128]{2,1,0:T(8,128)(2,1)S(1)}, u32[]{:S(2)}, u32[]{:S(2)}) collective-permute-start(bf16[16,16,128]{2,1,0:T(8,128)(2,1)S(1)} %shard_map.77.refs_0_), channel_id=1, source_target_pairs={{0,3},{1,2},{2,1},{3,0},{4,7},{5,6},{6,5},{7,4},{8,11},{9,10},{10,... | collective-permute-start | bytes 196616 | tf_op jit(solution)/shard_map/ppermute | solution.py:266
  5.0 4.1 %collective-permute-start.2 = (bf16[16,16,128]{2,1,0:T(8,128)(2,1)S(1)}, bf16[16,16,128]{2,1,0:T(8,128)(2,1)S(1)}, u32[]{:S(2)}, u32[]{:S(2)}) collective-permute-start(bf16[16,16,128]{2,1,0:T(8,128)(2,1)S(1)} %shard_map.77.refs_0_), channel_id=1, source_target_pairs={{0,1},{1,0},{2,3},{3,2},{4,5},{5,4},{6,7},{7,6},{8,9},{9,8},{10,11... | collective-permute-start | bytes 196616 | tf_op jit(solution)/shard_map/ppermute | solution.py:266
  9.5 6.3 %collective-permute-start.3 = (bf16[16,16,128]{2,1,0:T(8,128)(2,1)S(1)}, bf16[16,16,128]{2,1,0:T(8,128)(2,1)S(1)}, u32[]{:S(2)}, u32[]{:S(2)}) collective-permute-start(bf16[16,16,128]{2,1,0:T(8,128)(2,1)S(1)} %shard_map.81), channel_id=1, source_target_pairs={{0,8},{4,12},{8,0},{12,4},{1,9},{5,13},{9,1},{13,5},{2,10},{6,14},... | collective-permute-start | bytes 196616 | tf_op jit(solution)/shard_map/ppermute | solution.py:266
  12.4 4.3 %collective-permute-start.4 = (bf16[16,16,128]{2,1,0:T(8,128)(2,1)S(1)}, bf16[16,16,128]{2,1,0:T(8,128)(2,1)S(1)}, u32[]{:S(2)}, u32[]{:S(2)}) collective-permute-start(bf16[16,16,128]{2,1,0:T(8,128)(2,1)S(1)} %shard_map.83), channel_id=1, source_target_pairs={{0,4},{4,0},{8,12},{12,8},{1,5},{5,1},{9,13},{13,9},{2,6},{6,2},{1... | collective-permute-start | bytes 196616 | tf_op jit(solution)/shard_map/ppermute | solution.py:266
  14.2 6.1 %collective-permute-start.5 = (bf16[16,16,128]{2,1,0:T(8,128)(2,1)S(1)}, bf16[16,16,128]{2,1,0:T(8,128)(2,1)S(1)}, u32[]{:S(2)}, u32[]{:S(2)}) collective-permute-start(bf16[16,16,128]{2,1,0:T(8,128)(2,1)S(1)} %shard_map.85), channel_id=1, source_target_pairs={{0,12},{4,8},{8,4},{12,0},{1,13},{5,9},{9,5},{13,1},{2,14},{6,10},... | collective-permute-start | bytes 196616 | tf_op jit(solution)/shard_map/ppermute | solution.py:266
  20.6 4.7 %copy-start = (bf16[128,640]{1,0:T(8,128)(2,1)S(1)}, bf16[128,640]{1,0:T(8,128)(2,1)}, u32[]{:S(2)}) copy-start(bf16[128,640]{1,0:T(8,128)(2,1)} %refs_5_.3) | copy-start | bytes 491524
  20.6 4.7 %copy-start.1 = (bf16[128,128]{1,0:T(8,128)(2,1)S(1)}, bf16[128,128]{1,0:T(8,128)(2,1)}, u32[]{:S(2)}) copy-start(bf16[128,128]{1,0:T(8,128)(2,1)} %out_weight_ref.1) | copy-start | bytes 98308
  20.6 6.6 %collective-permute-start.6 = (bf16[16,16,128]{2,1,0:T(8,128)(2,1)S(1)}, bf16[16,16,128]{2,1,0:T(8,128)(2,1)S(1)}, u32[]{:S(2)}, u32[]{:S(2)}) collective-permute-start(bf16[16,16,128]{2,1,0:T(8,128)(2,1)S(1)} %get-tuple-element.27.refs_0_), channel_id=1, source_target_pairs={{0,8},{4,12},{8,0},{12,4},{1,9},{5,13},{9,1},{13,5},{2,10},{6,14},... | collective-permute-start | bytes 196616 | tf_op jit(solution)/shard_map/ppermute | solution.py:266
  21.6 5.7 %collective-permute-start.7 = (bf16[16,16,128]{2,1,0:T(8,128)(2,1)S(1)}, bf16[16,16,128]{2,1,0:T(8,128)(2,1)S(1)}, u32[]{:S(2)}, u32[]{:S(2)}) collective-permute-start(bf16[16,16,128]{2,1,0:T(8,128)(2,1)S(1)} %get-tuple-element.27.refs_0_), channel_id=1, source_target_pairs={{0,4},{4,0},{8,12},{12,8},{1,5},{5,1},{9,13},{13,9},{2,6},{6,2},{1... | collective-permute-start | bytes 196616 | tf_op jit(solution)/shard_map/ppermute | solution.py:266
  22.1 6.2 %collective-permute-start.8 = (bf16[16,16,128]{2,1,0:T(8,128)(2,1)S(1)}, bf16[16,16,128]{2,1,0:T(8,128)(2,1)S(1)}, u32[]{:S(2)}, u32[]{:S(2)}) collective-permute-start(bf16[16,16,128]{2,1,0:T(8,128)(2,1)S(1)} %get-tuple-element.27.refs_0_), channel_id=1, source_target_pairs={{0,12},{4,8},{8,4},{12,0},{1,13},{5,9},{9,5},{13,1},{2,14},{6,10},... | collective-permute-start | bytes 196616 | tf_op jit(solution)/shard_map/ppermute | solution.py:266
  28.9 4.4 %collective-permute-start.9 = (bf16[16,16,128]{2,1,0:T(8,128)(2,1)S(1)}, bf16[16,16,128]{2,1,0:T(8,128)(2,1)S(1)}, u32[]{:S(2)}, u32[]{:S(2)}) collective-permute-start(bf16[16,16,128]{2,1,0:T(8,128)(2,1)S(1)} %get-tuple-element.32), channel_id=1, source_target_pairs={{0,3},{1,2},{2,1},{3,0},{4,7},{5,6},{6,5},{7,4},{8,11},{9,10},{10,... | collective-permute-start | bytes 196616 | tf_op jit(solution)/shard_map/ppermute | solution.py:266
  29.0 5.1 %collective-permute-start.10 = (bf16[16,16,128]{2,1,0:T(8,128)(2,1)S(1)}, bf16[16,16,128]{2,1,0:T(8,128)(2,1)S(1)}, u32[]{:S(2)}, u32[]{:S(2)}) collective-permute-start(bf16[16,16,128]{2,1,0:T(8,128)(2,1)S(1)} %get-tuple-element.33), channel_id=1, source_target_pairs={{0,2},{1,3},{2,0},{3,1},{4,6},{5,7},{6,4},{7,5},{8,10},{9,11},{10,... | collective-permute-start | bytes 196616 | tf_op jit(solution)/shard_map/ppermute | solution.py:266
  30.1 4.0 %collective-permute-start.11 = (bf16[16,16,128]{2,1,0:T(8,128)(2,1)S(1)}, bf16[16,16,128]{2,1,0:T(8,128)(2,1)S(1)}, u32[]{:S(2)}, u32[]{:S(2)}) collective-permute-start(bf16[16,16,128]{2,1,0:T(8,128)(2,1)S(1)} %get-tuple-element.34), channel_id=1, source_target_pairs={{0,1},{1,0},{2,3},{3,2},{4,5},{5,4},{6,7},{7,6},{8,9},{9,8},{10,11... | collective-permute-start | bytes 196616 | tf_op jit(solution)/shard_map/ppermute | solution.py:266

commit v14 on v9

--- a/solution.py
+++ b/solution.py
@@ -263,6 +263,7 @@
     wait = 2**31
     steps = [step for bit in range(n.bit_length() - 2, -1, -1) for step in range(2**bit, 2 ** (bit + 1))]
     row_steps = list(range(n - 1, 0, -1))
+    gather_steps = [n - 1] + list(range(1, n - 1))
 
 
     def swap(values, axis, step):
@@ -312,7 +313,7 @@
     tri_normed, tri_grad = call(
         triangle_kernel, (flat, tile), total, part, upstream, flops=20 * pairs * channels,
     )
-    grads = gather(tri_grad, "row", row_steps)
+    grads = gather(tri_grad, "row", gather_steps)
     update, partial = call(
         update_kernel, (tile, flat), tri_normed, out_open, gate_factor, in_weights, out_weight,
         flops=4 * pairs * channels * channels,
@@ -320,10 +321,10 @@
     (right_grad,) = call(functools.partial(right_grad_kernel, [0]), (wide,), left_panel, tri_grad)
     right, partial, right_grad = lax.optimization_barrier((right, partial, right_grad))
     (grad_panel,) = call(
-        functools.partial(panel_kernel, "row", [0] + row_steps), (jax.ShapeDtypeStruct((n * pairs, channels), f32),), *grads
+        functools.partial(panel_kernel, "row", [0] + gather_steps), (jax.ShapeDtypeStruct((n * pairs, channels), f32),), *grads
     )
     terms = {}
-    for group in (steps[: n // 2], steps[n // 2 :], [0]):
+    for group in (steps, [0]):
         if terms:
             right, terms[last] = lax.optimization_barrier((right, terms[last]))
         last = group[-1]
@@ -340,7 +341,7 @@
         else:
             (total,) = call(add_kernel, (wide,), total, term, flops=wait)
     (share,) = call(
-        functools.partial(right_back_kernel, row_steps), (flat,),
+        functools.partial(right_back_kernel, gather_steps), (flat,),
         left_panel, *grads[1:], right_grad, factors, in_weights, partial,
         scratch=[pltpu.VMEM(wide.shape, f32)],
     )

time: 35.5 us -> 35.1 us (0.989)
  waiting for transfers between devices: 11.9 us -> 11.5 us
    pallas_call x20 -> x19, Pallas kernels: 7.55 us -> 7.53 us  [call(): pl.pallas_call(kernel, out_shape=tuple(outs), in_specs=specs, out_specs=(...]
  transfers between devices with their start and end apart: 12 -> 12, of which waited for: 8 -> 9; matrix products, arithmetic and copies ran while one was open for 0% -> 0% of each run, Pallas kernels for 12% -> 12%
where the time goes in v14:
time: 35.1 us; the launch traced here: 34.9 us
  starting transfers between devices  14.4 us (41%)
  waiting for transfers between devices  11.5 us (33%)
  Pallas kernels  7.53 us (21%)
  between operations  1.43 us (4%)
    ppermute x12, starting transfers between devices, swap(): return lax.ppermute(values, axis, [(a, a ^ step) for a in range(n)])  14.4 us
    ppermute x12, waiting for transfers between devices, swap(): return lax.ppermute(values, axis, [(a, a ^ step) for a in range(n)])  11.5 us
    pallas_call x19, Pallas kernels, call(): pl.pallas_call(kernel, out_shape=tuple(outs), in_specs=specs, out_specs=(...  7.53 us
  transfers between devices with their start and end apart: 12, of which 9 were waited for; matrix products, arithmetic and copies ran while one was open for 0% of the time, Pallas kernels for 12%

profile of v14, /device:TPU:0, one launch (start us, length us, event | category | flops | bytes accessed | tf_op | source)
XLA Modules:
  0.0 34.9 jit_solution(14542680668274613603)
XLA Ops:
  0.6 1.3 %shard_map.77.refs_0_ = bf16[16,16,128]{2,1,0:T(8,128)(2,1)S(1)} custom-call(bf16[16,16,128]{2,1,0:T(8,128)(2,1)} %acts_in.3, s32[16,16]{1,0:T(8,128)} %mask_in.3, bf16[128,640]{1,0:T(8,128)(2,1)} %refs_5_.3), custom_call_target="tpu_custom_call" | custom-call | flops 16777216 | bytes 295936 | tf_op jit(solution)/shard_map/pallas_call | solution.py:242
  2.0 3.0 %collective-permute-start = (bf16[16,16,128]{2,1,0:T(8,128)(2,1)S(1)}, bf16[16,16,128]{2,1,0:T(8,128)(2,1)S(1)}, u32[]{:S(2)}, u32[]{:S(2)}) collective-permute-start(bf16[16,16,128]{2,1,0:T(8,128)(2,1)S(1)} %shard_map.77.refs_0_), channel_id=1, source_target_pairs={{0,2},{1,3},{2,0},{3,1},{4,6},{5,7},{6,4},{7,5},{8,10},{9,11},{10,... | collective-permute-start | bytes 196616 | tf_op jit(solution)/shard_map/ppermute | solution.py:270
  5.8 1.5 %shard_map.79 = (f32[16,16,128]{2,1,0:T(8,128)S(1)}, f32[256,128]{1,0:T(8,128)S(1)}, f32[256,128]{1,0:T(8,128)S(1)}, f32[4,256,128]{2,1,0:T(8,128)S(1)}, f32[256...) custom-call(bf16[16,16,128]{2,1,0:T(8,128)(2,1)} %acts_in.3, s32[16,16]{1,0:T(8,128)} %mask_in.3, ...), custom_call_target="tpu_custom_call" | custom-call | flops 50331648 | bytes 1639428 | tf_op jit(solution)/shard_map/pallas_call | solution.py:242
  7.3 1.8 %collective-permute-done.1.refs_2_ = bf16[16,16,128]{2,1,0:T(8,128)(2,1)S(1)} collective-permute-done((bf16[16,16,128]{2,1,0:T(8,128)(2,1)S(1)}, bf16[16,16,128]{2,1,0:T(8,128)(2,1)S(1)}, u32[]{:S(2)}, u32[]{:S(2)}) %collective-permute-start.1) | collective-permute-done | bytes 65568 | tf_op jit(solution)/shard_map/ppermute | solution.py:270
  9.4 3.7 %collective-permute-start.3 = (bf16[16,16,128]{2,1,0:T(8,128)(2,1)S(1)}, bf16[16,16,128]{2,1,0:T(8,128)(2,1)S(1)}, u32[]{:S(2)}, u32[]{:S(2)}) collective-permute-start(bf16[16,16,128]{2,1,0:T(8,128)(2,1)S(1)} %shard_map.81), channel_id=1, source_target_pairs={{0,12},{4,8},{8,4},{12,0},{1,13},{5,9},{9,5},{13,1},{2,14},{6,10},... | collective-permute-start | bytes 196616 | tf_op jit(solution)/shard_map/ppermute | solution.py:270
  13.4 0.2 shard_map.85
  13.6 0.8 %collective-permute-start.5 = (bf16[16,16,128]{2,1,0:T(8,128)(2,1)S(1)}, bf16[16,16,128]{2,1,0:T(8,128)(2,1)S(1)}, u32[]{:S(2)}, u32[]{:S(2)}) collective-permute-start(bf16[16,16,128]{2,1,0:T(8,128)(2,1)S(1)} %shard_map.85), channel_id=1, source_target_pairs={{0,4},{4,0},{8,12},{12,8},{1,5},{5,1},{9,13},{13,9},{2,6},{6,2},{1... | collective-permute-start | bytes 196616 | tf_op jit(solution)/shard_map/ppermute | solution.py:270
  14.6 1.1 %collective-permute-done.3.tile_ref = bf16[16,16,128]{2,1,0:T(8,128)(2,1)S(1)} collective-permute-done((bf16[16,16,128]{2,1,0:T(8,128)(2,1)S(1)}, bf16[16,16,128]{2,1,0:T(8,128)(2,1)S(1)}, u32[]{:S(2)}, u32[]{:S(2)}) %collective-permute-start.3) | collective-permute-done | bytes 65568 | tf_op jit(solution)/shard_map/ppermute | solution.py:270
  15.7 3.2 %collective-permute-done.4.tile_ref = bf16[16,16,128]{2,1,0:T(8,128)(2,1)S(1)} collective-permute-done((bf16[16,16,128]{2,1,0:T(8,128)(2,1)S(1)}, bf16[16,16,128]{2,1,0:T(8,128)(2,1)S(1)}, u32[]{:S(2)}, u32[]{:S(2)}) %collective-permute-start.4) | collective-permute-done | bytes 65568 | tf_op jit(solution)/shard_map/ppermute | solution.py:270
  19.1 0.3 shard_map.86
  19.4 2.5 %collective-permute-start.6 = (bf16[16,16,128]{2,1,0:T(8,128)(2,1)S(1)}, bf16[16,16,128]{2,1,0:T(8,128)(2,1)S(1)}, u32[]{:S(2)}, u32[]{:S(2)}) collective-permute-start(bf16[16,16,128]{2,1,0:T(8,128)(2,1)S(1)} %get-tuple-element.27.refs_0_), channel_id=1, source_target_pairs={{0,12},{4,8},{8,4},{12,0},{1,13},{5,9},{9,5},{13,1},{2,14},{6,10},... | collective-permute-start | bytes 196616 | tf_op jit(solution)/shard_map/ppermute | solution.py:270
  21.9 2.0 %collective-permute-start.8 = (bf16[16,16,128]{2,1,0:T(8,128)(2,1)S(1)}, bf16[16,16,128]{2,1,0:T(8,128)(2,1)S(1)}, u32[]{:S(2)}, u32[]{:S(2)}) collective-permute-start(bf16[16,16,128]{2,1,0:T(8,128)(2,1)S(1)} %get-tuple-element.27.refs_0_), channel_id=1, source_target_pairs={{0,8},{4,12},{8,0},{12,4},{1,9},{5,13},{9,1},{13,5},{2,10},{6,14},... | collective-permute-start | bytes 196616 | tf_op jit(solution)/shard_map/ppermute | solution.py:270
  24.1 0.8 %shard_map.87 = (bf16[16,16,128]{2,1,0:T(8,128)(2,1)}, f32[256,128]{1,0:T(8,128)S(1)}) custom-call(f32[256,128]{1,0:T(8,128)S(1)} %get-tuple-element.23.tri_normed_ref, f32[256,128]{1,0:T(8,128)S(1)} %get-tuple-element.24.open_ref, f32[256,128]{1,0:T(8,128)S(1)} %get-tuple-element.25.gate_factor_ref, bf16[128,640]{1,0:T(8,128)(2,1)S(1)} %copy-done, ...), custom_call_target="tpu_custom_call" | custom-call | flops 16777216 | bytes 786432 | tf_op jit(solution)/shard_map/pallas_call | solution.py:242
  24.9 0.8 %collective-permute-done.6.refs_1_.refs_0_ = bf16[16,16,128]{2,1,0:T(8,128)(2,1)S(1)} collective-permute-done((bf16[16,16,128]{2,1,0:T(8,128)(2,1)S(1)}, bf16[16,16,128]{2,1,0:T(8,128)(2,1)S(1)}, u32[]{:S(2)}, u32[]{:S(2)}) %collective-permute-start.6) | collective-permute-done | bytes 65568 | tf_op jit(solution)/shard_map/ppermute | solution.py:270
  25.7 1.3 %collective-permute-done.7.refs_2_.refs_1_ = bf16[16,16,128]{2,1,0:T(8,128)(2,1)S(1)} collective-permute-done((bf16[16,16,128]{2,1,0:T(8,128)(2,1)S(1)}, bf16[16,16,128]{2,1,0:T(8,128)(2,1)S(1)}, u32[]{:S(2)}, u32[]{:S(2)}) %collective-permute-start.7) | collective-permute-done | bytes 65568 | tf_op jit(solution)/shard_map/ppermute | solution.py:270
  26.9 0.6 %collective-permute-done.8.refs_3_.refs_2_ = bf16[16,16,128]{2,1,0:T(8,128)(2,1)S(1)} collective-permute-done((bf16[16,16,128]{2,1,0:T(8,128)(2,1)S(1)}, bf16[16,16,128]{2,1,0:T(8,128)(2,1)S(1)}, u32[]{:S(2)}, u32[]{:S(2)}) %collective-permute-start.8) | collective-permute-done | bytes 65568 | tf_op jit(solution)/shard_map/ppermute | solution.py:270
  27.6 0.6 %shard_map.90 = (bf16[16,16,128]{2,1,0:T(8,128)(2,1)S(1)}, bf16[16,16,128]{2,1,0:T(8,128)(2,1)S(1)}, bf16[16,16,128]{2,1,0:T(8,128)(2,1)S(1)}) custom-call(f32[1024,128]{1,0:T(8,128)S(1)} %shard_map.88.panel, f32[16,16,128]{2,1,0:T(8,128)S(1)} %get-tuple-element.31.right_ref.right), custom_call_target="tpu_custom_call" | custom-call | flops 1048576 | bytes 851968 | tf_op jit(solution)/shard_map/pallas_call | solution.py:242
  28.2 1.5 %collective-permute-start.9 = (bf16[16,16,128]{2,1,0:T(8,128)(2,1)S(1)}, bf16[16,16,128]{2,1,0:T(8,128)(2,1)S(1)}, u32[]{:S(2)}, u32[]{:S(2)}) collective-permute-start(bf16[16,16,128]{2,1,0:T(8,128)(2,1)S(1)} %get-tuple-element.32), channel_id=1, source_target_pairs={{0,2},{1,3},{2,0},{3,1},{4,6},{5,7},{6,4},{7,5},{8,10},{9,11},{10,... | collective-permute-start | bytes 196616 | tf_op jit(solution)/shard_map/ppermute | solution.py:270
  29.8 0.7 %collective-permute-start.11 = (bf16[16,16,128]{2,1,0:T(8,128)(2,1)S(1)}, bf16[16,16,128]{2,1,0:T(8,128)(2,1)S(1)}, u32[]{:S(2)}, u32[]{:S(2)}) collective-permute-start(bf16[16,16,128]{2,1,0:T(8,128)(2,1)S(1)} %get-tuple-element.34), channel_id=1, source_target_pairs={{0,1},{1,0},{2,3},{3,2},{4,5},{5,4},{6,7},{7,6},{8,9},{9,8},{10,11... | collective-permute-start | bytes 196616 | tf_op jit(solution)/shard_map/ppermute | solution.py:270
  30.4 0.7 %shard_map.94.refs_4_ = f32[256,128]{1,0:T(8,128)S(1)} custom-call(f32[64,16,128]{2,1,0:T(8,128)S(1)} %shard_map.78.panel, bf16[16,16,128]{2,1,0:T(8,128)(2,1)S(1)} %collective-permute-done.6.refs_1_.refs_0_, bf16[16,16,128]{2,1,0:T(8,128)(2,1)S(1)} %collective-permute-done.7.refs_2_.refs_1_, ...), custom_call_target="tpu_custom_call" | custom-call | tf_op jit(solution)/shard_map/pallas_call | solution.py:242
  31.2 0.2 shard_map.91.base
  31.4 1.2 %collective-permute-done.9.tile_ref = bf16[16,16,128]{2,1,0:T(8,128)(2,1)S(1)} collective-permute-done((bf16[16,16,128]{2,1,0:T(8,128)(2,1)S(1)}, bf16[16,16,128]{2,1,0:T(8,128)(2,1)S(1)}, u32[]{:S(2)}, u32[]{:S(2)}) %collective-permute-start.9) | collective-permute-done | bytes 65568 | tf_op jit(solution)/shard_map/ppermute | solution.py:270
  32.6 1.4 %collective-permute-done.10.tile_ref = bf16[16,16,128]{2,1,0:T(8,128)(2,1)S(1)} collective-permute-done((bf16[16,16,128]{2,1,0:T(8,128)(2,1)S(1)}, bf16[16,16,128]{2,1,0:T(8,128)(2,1)S(1)}, u32[]{:S(2)}, u32[]{:S(2)}) %collective-permute-start.10) | collective-permute-done | bytes 65568 | tf_op jit(solution)/shard_map/ppermute | solution.py:270
  34.0 0.9 %shard_map.95 = bf16[16,16,128]{2,1,0:T(8,128)(2,1)} custom-call(f32[16,16,128]{2,1,0:T(8,128)S(1)} %shard_map.93.base, bf16[16,16,128]{2,1,0:T(8,128)(2,1)S(1)} %collective-permute-done.11.refs_0_, f32[256,128]{1,0:T(8,128)S(1)} %get-tuple-element.35.refs_1_, f32[256,128]{1,0:T(8,128)S(1)} %get-tuple-element.36.refs_2_, ...), custom_call_target="tpu_custom_call" | custom-call | flops 16777216 | bytes 1343488 | tf_op jit(solution)/shard_map/pallas_call | solution.py:242
  (23 shorter events, 1.4 us)
Async XLA Ops:
  2.0 5.3 %collective-permute-start = (bf16[16,16,128]{2,1,0:T(8,128)(2,1)S(1)}, bf16[16,16,128]{2,1,0:T(8,128)(2,1)S(1)}, u32[]{:S(2)}, u32[]{:S(2)}) collective-permute-start(bf16[16,16,128]{2,1,0:T(8,128)(2,1)S(1)} %shard_map.77.refs_0_), channel_id=1, source_target_pairs={{0,2},{1,3},{2,0},{3,1},{4,6},{5,7},{6,4},{7,5},{8,10},{9,11},{10,... | collective-permute-start | bytes 196616 | tf_op jit(solution)/shard_map/ppermute | solution.py:270
  5.0 4.1 %collective-permute-start.1 = (bf16[16,16,128]{2,1,0:T(8,128)(2,1)S(1)}, bf16[16,16,128]{2,1,0:T(8,128)(2,1)S(1)}, u32[]{:S(2)}, u32[]{:S(2)}) collective-permute-start(bf16[16,16,128]{2,1,0:T(8,128)(2,1)S(1)} %shard_map.77.refs_0_), channel_id=1, source_target_pairs={{0,3},{1,2},{2,1},{3,0},{4,7},{5,6},{6,5},{7,4},{8,11},{9,10},{10,... | collective-permute-start | bytes 196616 | tf_op jit(solution)/shard_map/ppermute | solution.py:270
  5.0 4.1 %collective-permute-start.2 = (bf16[16,16,128]{2,1,0:T(8,128)(2,1)S(1)}, bf16[16,16,128]{2,1,0:T(8,128)(2,1)S(1)}, u32[]{:S(2)}, u32[]{:S(2)}) collective-permute-start(bf16[16,16,128]{2,1,0:T(8,128)(2,1)S(1)} %shard_map.77.refs_0_), channel_id=1, source_target_pairs={{0,1},{1,0},{2,3},{3,2},{4,5},{5,4},{6,7},{7,6},{8,9},{9,8},{10,11... | collective-permute-start | bytes 196616 | tf_op jit(solution)/shard_map/ppermute | solution.py:270
  9.4 6.3 %collective-permute-start.3 = (bf16[16,16,128]{2,1,0:T(8,128)(2,1)S(1)}, bf16[16,16,128]{2,1,0:T(8,128)(2,1)S(1)}, u32[]{:S(2)}, u32[]{:S(2)}) collective-permute-start(bf16[16,16,128]{2,1,0:T(8,128)(2,1)S(1)} %shard_map.81), channel_id=1, source_target_pairs={{0,12},{4,8},{8,4},{12,0},{1,13},{5,9},{9,5},{13,1},{2,14},{6,10},... | collective-permute-start | bytes 196616 | tf_op jit(solution)/shard_map/ppermute | solution.py:270
  13.3 5.6 %collective-permute-start.4 = (bf16[16,16,128]{2,1,0:T(8,128)(2,1)S(1)}, bf16[16,16,128]{2,1,0:T(8,128)(2,1)S(1)}, u32[]{:S(2)}, u32[]{:S(2)}) collective-permute-start(bf16[16,16,128]{2,1,0:T(8,128)(2,1)S(1)} %shard_map.83), channel_id=1, source_target_pairs={{0,8},{4,12},{8,0},{12,4},{1,9},{5,13},{9,1},{13,5},{2,10},{6,14},... | collective-permute-start | bytes 196616 | tf_op jit(solution)/shard_map/ppermute | solution.py:270
  13.6 5.5 %collective-permute-start.5 = (bf16[16,16,128]{2,1,0:T(8,128)(2,1)S(1)}, bf16[16,16,128]{2,1,0:T(8,128)(2,1)S(1)}, u32[]{:S(2)}, u32[]{:S(2)}) collective-permute-start(bf16[16,16,128]{2,1,0:T(8,128)(2,1)S(1)} %shard_map.85), channel_id=1, source_target_pairs={{0,4},{4,0},{8,12},{12,8},{1,5},{5,1},{9,13},{13,9},{2,6},{6,2},{1... | collective-permute-start | bytes 196616 | tf_op jit(solution)/shard_map/ppermute | solution.py:270
  19.4 4.7 %copy-start = (bf16[128,640]{1,0:T(8,128)(2,1)S(1)}, bf16[128,640]{1,0:T(8,128)(2,1)}, u32[]{:S(2)}) copy-start(bf16[128,640]{1,0:T(8,128)(2,1)} %refs_5_.3) | copy-start | bytes 491524
  19.4 4.7 %copy-start.1 = (bf16[128,128]{1,0:T(8,128)(2,1)S(1)}, bf16[128,128]{1,0:T(8,128)(2,1)}, u32[]{:S(2)}) copy-start(bf16[128,128]{1,0:T(8,128)(2,1)} %out_weight_ref.1) | copy-start | bytes 98308
  19.4 6.2 %collective-permute-start.6 = (bf16[16,16,128]{2,1,0:T(8,128)(2,1)S(1)}, bf16[16,16,128]{2,1,0:T(8,128)(2,1)S(1)}, u32[]{:S(2)}, u32[]{:S(2)}) collective-permute-start(bf16[16,16,128]{2,1,0:T(8,128)(2,1)S(1)} %get-tuple-element.27.refs_0_), channel_id=1, source_target_pairs={{0,12},{4,8},{8,4},{12,0},{1,13},{5,9},{9,5},{13,1},{2,14},{6,10},... | collective-permute-start | bytes 196616 | tf_op jit(solution)/shard_map/ppermute | solution.py:270
  21.9 5.0 %collective-permute-start.7 = (bf16[16,16,128]{2,1,0:T(8,128)(2,1)S(1)}, bf16[16,16,128]{2,1,0:T(8,128)(2,1)S(1)}, u32[]{:S(2)}, u32[]{:S(2)}) collective-permute-start(bf16[16,16,128]{2,1,0:T(8,128)(2,1)S(1)} %get-tuple-element.27.refs_0_), channel_id=1, source_target_pairs={{0,4},{4,0},{8,12},{12,8},{1,5},{5,1},{9,13},{13,9},{2,6},{6,2},{1... | collective-permute-start | bytes 196616 | tf_op jit(solution)/shard_map/ppermute | solution.py:270
  21.9 5.7 %collective-permute-start.8 = (bf16[16,16,128]{2,1,0:T(8,128)(2,1)S(1)}, bf16[16,16,128]{2,1,0:T(8,128)(2,1)S(1)}, u32[]{:S(2)}, u32[]{:S(2)}) collective-permute-start(bf16[16,16,128]{2,1,0:T(8,128)(2,1)S(1)} %get-tuple-element.27.refs_0_), channel_id=1, source_target_pairs={{0,8},{4,12},{8,0},{12,4},{1,9},{5,13},{9,1},{13,5},{2,10},{6,14},... | collective-permute-start | bytes 196616 | tf_op jit(solution)/shard_map/ppermute | solution.py:270
  28.2 4.3 %collective-permute-start.9 = (bf16[16,16,128]{2,1,0:T(8,128)(2,1)S(1)}, bf16[16,16,128]{2,1,0:T(8,128)(2,1)S(1)}, u32[]{:S(2)}, u32[]{:S(2)}) collective-permute-start(bf16[16,16,128]{2,1,0:T(8,128)(2,1)S(1)} %get-tuple-element.32), channel_id=1, source_target_pairs={{0,2},{1,3},{2,0},{3,1},{4,6},{5,7},{6,4},{7,5},{8,10},{9,11},{10,... | collective-permute-start | bytes 196616 | tf_op jit(solution)/shard_map/ppermute | solution.py:270
  29.8 4.2 %collective-permute-start.10 = (bf16[16,16,128]{2,1,0:T(8,128)(2,1)S(1)}, bf16[16,16,128]{2,1,0:T(8,128)(2,1)S(1)}, u32[]{:S(2)}, u32[]{:S(2)}) collective-permute-start(bf16[16,16,128]{2,1,0:T(8,128)(2,1)S(1)} %get-tuple-element.33), channel_id=1, source_target_pairs={{0,3},{1,2},{2,1},{3,0},{4,7},{5,6},{6,5},{7,4},{8,11},{9,10},{10,... | collective-permute-start | bytes 196616 | tf_op jit(solution)/shard_map/ppermute | solution.py:270
  29.8 4.2 %collective-permute-start.11 = (bf16[16,16,128]{2,1,0:T(8,128)(2,1)S(1)}, bf16[16,16,128]{2,1,0:T(8,128)(2,1)S(1)}, u32[]{:S(2)}, u32[]{:S(2)}) collective-permute-start(bf16[16,16,128]{2,1,0:T(8,128)(2,1)S(1)} %get-tuple-element.34), channel_id=1, source_target_pairs={{0,1},{1,0},{2,3},{3,2},{4,5},{5,4},{6,7},{7,6},{8,9},{9,8},{10,11... | collective-permute-start | bytes 196616 | tf_op jit(solution)/shard_map/ppermute | solution.py:270

commit v15 on v14

--- a/solution.py
+++ b/solution.py
@@ -151,19 +151,35 @@
         panel[pl.ds(place * size, size)] = ref[...].astype(f32) * (row_live * col_live)
 
 
-def partial_kernel(steps, panel, right_ref, *outs):
+def partial_kernel(steps, crop_ref, *refs):
+    count = len(steps)
+    lefts, right_ref, outs, left = refs[:count], refs[count], refs[count + 1 : -1], refs[-1]
     size, _, channels = right_ref.shape
-    for step, out in zip(steps, outs):
-        start = (lax.axis_index("row") ^ step) * size
+    rows = lax.axis_index("row") * size + lax.broadcasted_iota(jnp.int32, (size, 1, channels), 0)
+    row_live = jnp.where(rows < crop_ref[0], 1.0, 0.0)
+    for step, left_ref, out in zip(steps, lefts, outs):
+        cols = (lax.axis_index("col") ^ step) * size + lax.broadcasted_iota(jnp.int32, (1, size, channels), 1)
+        left[...] = left_ref[...].astype(f32) * (row_live * jnp.where(cols < crop_ref[0], 1.0, 0.0))
 
         def add(k, sums):
             other = right_ref[k]
-            return tuple(sums[i] + panel[start + k, pl.ds(i, 1), :] * other for i in range(size))
+            return tuple(sums[i] + left[k, pl.ds(i, 1), :] * other for i in range(size))
 
         zero = jnp.zeros((size, channels), f32)
         sums = lax.fori_loop(0, size, add, (zero,) * size, unroll=4)
         for i in range(size):
-            out[i] = sums[i].astype(out.dtype)
+            out[i] = sums[i]
+
+
+def pick_kernel(steps, *refs):
+    here = lax.axis_index("row") ^ lax.axis_index("col")
+    tiles, outs = refs[: len(steps)], refs[len(steps) :]
+    for step, out in zip(steps, outs):
+        for other, tile in enumerate(tiles):
+
+            @pl.when((here ^ step) == other)
+            def _():
+                out[...] = tile[...].astype(out.dtype)
 
 
 def triangle_kernel(base, tile_ref, upstream_ref, tri_normed_ref, grad_ref):
@@ -297,17 +313,24 @@
             pltpu.SemaphoreType.DMA((5,)),
         ],
     )
+    parts = []
+    order = [0] + steps
+    for group in [[at] for at in range(n - 2)] + [[n - 2, n - 1]]:
+        parts += call(
+            functools.partial(partial_kernel, [order[at] for at in group]), (wide,) * len(group),
+            crop_length, *(lefts[at] for at in group), right, smem=(0,), flops=work,
+            scratch=[pltpu.VMEM(wide.shape, f32)],
+        )
+    parts = [part for _, part in sorted(zip(order, parts), key=lambda each: each[0])]
+    total, *parts = call(
+        functools.partial(pick_kernel, [0] + row_steps), (wide,) + (tile,) * (n - 1), *parts,
+        flops=pairs * channels,
+    )
     (left_panel,) = call(
         functools.partial(left_panel_kernel, [0] + steps), (panel,), crop_length, *lefts, smem=(0,)
     )
-    parts = {}
-    for step in [0] + row_steps:
-        (parts[step],) = call(
-            functools.partial(partial_kernel, (step,)), (tile if step else wide,), left_panel, right, flops=work,
-        )
-    total = parts[0]
-    for step in row_steps:
-        part = swap(parts[step], "row", step)
+    for step, part in zip(row_steps, parts):
+        part = swap(part, "row", step)
         if step != row_steps[-1]:
             (total,) = call(add_kernel, (wide,), total, part, flops=wait)
     tri_normed, tri_grad = call(
@@ -324,7 +347,7 @@
         functools.partial(panel_kernel, "row", [0] + gather_steps), (jax.ShapeDtypeStruct((n * pairs, channels), f32),), *grads
     )
     terms = {}
-    for group in (steps, [0]):
+    for group in (steps[:1], steps[1:], [0]):
         if terms:
             right, terms[last] = lax.optimization_barrier((right, terms[last]))
         last = group[-1]

time: 35.1 us -> 35 us (level)
  waiting for transfers between devices: 11.5 us -> 10.6 us
  local copies, waits for them, and re-layouts: 0.01 us -> 0.71 us
    ppermute x12, waiting for transfers between devices: 11.5 us -> 10.6 us  [swap(): return lax.ppermute(values, axis, [(a, a ^ step) for a in range(n)])]
    unnamed x4, local copies, waits for them, and re-layouts: 0.01 us -> 0.71 us
    pallas_call x19 -> x20, Pallas kernels: 7.53 us -> 7.71 us  [call(): pl.pallas_call(kernel, out_shape=tuple(outs), in_specs=specs, out_specs=(...]
  transfers between devices with their start and end apart: 12 -> 12, of which waited for: 9 -> 8; matrix products, arithmetic and copies ran while one was open for 0% -> 0% of each run, Pallas kernels for 12% -> 13%
where the time goes in v15:
time: 35 us; the launch traced here: 34.8 us
  starting transfers between devices  14.4 us (41%)
  waiting for transfers between devices  10.6 us (30%)
  Pallas kernels  7.71 us (22%)
  between operations  1.44 us (4%)
  local copies, waits for them, and re-layouts  0.71 us (2%)
    ppermute x12, starting transfers between devices, swap(): return lax.ppermute(values, axis, [(a, a ^ step) for a in range(n)])  14.4 us
    ppermute x12, waiting for transfers between devices, swap(): return lax.ppermute(values, axis, [(a, a ^ step) for a in range(n)])  10.6 us
    pallas_call x20, Pallas kernels, call(): pl.pallas_call(kernel, out_shape=tuple(outs), in_specs=specs, out_specs=(...  7.71 us
    unnamed x4, local copies, waits for them, and re-layouts  0.71 us
  transfers between devices with their start and end apart: 12, of which 8 were waited for; matrix products, arithmetic and copies ran while one was open for 0% of the time, Pallas kernels for 13%

profile of v15, /device:TPU:0, one launch (start us, length us, event | category | flops | bytes accessed | tf_op | source)
XLA Modules:
  0.0 34.8 jit_solution(16853641097944837820)
XLA Ops:
  0.6 1.3 %shard_map.77.refs_0_ = bf16[16,16,128]{2,1,0:T(8,128)(2,1)S(1)} custom-call(bf16[16,16,128]{2,1,0:T(8,128)(2,1)} %acts_in.3, s32[16,16]{1,0:T(8,128)} %mask_in.3, bf16[128,640]{1,0:T(8,128)(2,1)} %refs_5_.3), custom_call_target="tpu_custom_call" | custom-call | flops 16777216 | bytes 295936 | tf_op jit(solution)/shard_map/pallas_call | solution.py:258
  2.0 3.0 %collective-permute-start.2 = (bf16[16,16,128]{2,1,0:T(8,128)(2,1)S(1)}, bf16[16,16,128]{2,1,0:T(8,128)(2,1)S(1)}, u32[]{:S(2)}, u32[]{:S(2)}) collective-permute-start(bf16[16,16,128]{2,1,0:T(8,128)(2,1)S(1)} %shard_map.77.refs_0_), channel_id=1, source_target_pairs={{0,2},{1,3},{2,0},{3,1},{4,6},{5,7},{6,4},{7,5},{8,10},{9,11},{10,... | collective-permute-start | bytes 196616 | tf_op jit(solution)/shard_map/ppermute | solution.py:286
  5.8 1.5 %shard_map.78 = (f32[16,16,128]{2,1,0:T(8,128)S(1)}, f32[256,128]{1,0:T(8,128)S(1)}, f32[256,128]{1,0:T(8,128)S(1)}, f32[4,256,128]{2,1,0:T(8,128)S(1)}, f32[256...) custom-call(bf16[16,16,128]{2,1,0:T(8,128)(2,1)} %acts_in.3, s32[16,16]{1,0:T(8,128)} %mask_in.3, ...), custom_call_target="tpu_custom_call" | custom-call | flops 50331648 | bytes 1639428 | tf_op jit(solution)/shard_map/pallas_call | solution.py:258
  7.8 1.4 %collective-permute-done.refs_0_.refs_2_ = bf16[16,16,128]{2,1,0:T(8,128)(2,1)S(1)} collective-permute-done((bf16[16,16,128]{2,1,0:T(8,128)(2,1)S(1)}, bf16[16,16,128]{2,1,0:T(8,128)(2,1)S(1)}, u32[]{:S(2)}, u32[]{:S(2)}) %collective-permute-start) | collective-permute-done | bytes 65568 | tf_op jit(solution)/shard_map/ppermute | solution.py:286
  9.1 0.4 %shard_map.80 = (f32[16,16,128]{2,1,0:T(8,128)S(1)}, f32[16,16,128]{2,1,0:T(8,128)S(1)}) custom-call(s32[1]{0:T(128)S(6)} %copy.8.crop_ref, bf16[16,16,128]{2,1,0:T(8,128)(2,1)S(1)} %collective-permute-done.refs_0_.refs_2_, bf16[16,16,128]{2,1,0:T(8,128)(2,1)S(1)} %collective-permute-done.1.refs_1_.refs_3_, ...), custom_call_target="tpu_custom_call" | custom-call | flops 1048576 | bytes 524292 | tf_op jit(solution)/shard_map/pallas_call | solution.py:258
  9.6 3.7 %collective-permute-start.3 = (bf16[16,16,128]{2,1,0:T(8,128)(2,1)S(1)}, bf16[16,16,128]{2,1,0:T(8,128)(2,1)S(1)}, u32[]{:S(2)}, u32[]{:S(2)}) collective-permute-start(bf16[16,16,128]{2,1,0:T(8,128)(2,1)S(1)} %get-tuple-element.32), channel_id=1, source_target_pairs={{0,12},{4,8},{8,4},{12,0},{1,13},{5,9},{9,5},{13,1},{2,14},{6,10},... | collective-permute-start | bytes 196616 | tf_op jit(solution)/shard_map/ppermute | solution.py:286
  13.4 0.7 %collective-permute-start.5 = (bf16[16,16,128]{2,1,0:T(8,128)(2,1)S(1)}, bf16[16,16,128]{2,1,0:T(8,128)(2,1)S(1)}, u32[]{:S(2)}, u32[]{:S(2)}) collective-permute-start(bf16[16,16,128]{2,1,0:T(8,128)(2,1)S(1)} %get-tuple-element.34), channel_id=1, source_target_pairs={{0,4},{4,0},{8,12},{12,8},{1,5},{5,1},{9,13},{13,9},{2,6},{6,2},{1... | collective-permute-start | bytes 196616 | tf_op jit(solution)/shard_map/ppermute | solution.py:286
  14.1 2.1 %collective-permute-done.3.tile_ref = bf16[16,16,128]{2,1,0:T(8,128)(2,1)S(1)} collective-permute-done((bf16[16,16,128]{2,1,0:T(8,128)(2,1)S(1)}, bf16[16,16,128]{2,1,0:T(8,128)(2,1)S(1)}, u32[]{:S(2)}, u32[]{:S(2)}) %collective-permute-start.3) | collective-permute-done | bytes 65568 | tf_op jit(solution)/shard_map/ppermute | solution.py:286
  16.2 2.8 %collective-permute-done.4.tile_ref = bf16[16,16,128]{2,1,0:T(8,128)(2,1)S(1)} collective-permute-done((bf16[16,16,128]{2,1,0:T(8,128)(2,1)S(1)}, bf16[16,16,128]{2,1,0:T(8,128)(2,1)S(1)}, u32[]{:S(2)}, u32[]{:S(2)}) %collective-permute-start.4) | collective-permute-done | bytes 65568 | tf_op jit(solution)/shard_map/ppermute | solution.py:286
  19.1 0.3 shard_map.85
  19.3 2.7 %collective-permute-start.6 = (bf16[16,16,128]{2,1,0:T(8,128)(2,1)S(1)}, bf16[16,16,128]{2,1,0:T(8,128)(2,1)S(1)}, u32[]{:S(2)}, u32[]{:S(2)}) collective-permute-start(bf16[16,16,128]{2,1,0:T(8,128)(2,1)S(1)} %get-tuple-element.40.refs_0_), channel_id=1, source_target_pairs={{0,12},{4,8},{8,4},{12,0},{1,13},{5,9},{9,5},{13,1},{2,14},{6,10},... | collective-permute-start | bytes 196616 | tf_op jit(solution)/shard_map/ppermute | solution.py:286
  22.1 1.7 %collective-permute-start.8 = (bf16[16,16,128]{2,1,0:T(8,128)(2,1)S(1)}, bf16[16,16,128]{2,1,0:T(8,128)(2,1)S(1)}, u32[]{:S(2)}, u32[]{:S(2)}) collective-permute-start(bf16[16,16,128]{2,1,0:T(8,128)(2,1)S(1)} %get-tuple-element.40.refs_0_), channel_id=1, source_target_pairs={{0,8},{4,12},{8,0},{12,4},{1,9},{5,13},{9,1},{13,5},{2,10},{6,14},... | collective-permute-start | bytes 196616 | tf_op jit(solution)/shard_map/ppermute | solution.py:286
  24.1 0.7 %copy-done = bf16[128,640]{1,0:T(8,128)(2,1)S(1)} copy-done((bf16[128,640]{1,0:T(8,128)(2,1)S(1)}, bf16[128,640]{1,0:T(8,128)(2,1)}, u32[]{:S(2)}) %copy-start) | copy-done | bytes 163864
  24.8 0.8 %shard_map.86 = (bf16[16,16,128]{2,1,0:T(8,128)(2,1)}, f32[256,128]{1,0:T(8,128)S(1)}) custom-call(f32[256,128]{1,0:T(8,128)S(1)} %get-tuple-element.36.tri_normed_ref, f32[256,128]{1,0:T(8,128)S(1)} %get-tuple-element.37.open_ref, f32[256,128]{1,0:T(8,128)S(1)} %get-tuple-element.38.gate_factor_ref, bf16[128,640]{1,0:T(8,128)(2,1)S(1)} %copy-done, ...), custom_call_target="tpu_custom_call" | custom-call | flops 16777216 | bytes 786432 | tf_op jit(solution)/shard_map/pallas_call | solution.py:258
  25.6 0.3 collective-permute-done.6.refs_1_.refs_0_
  25.9 0.8 %collective-permute-done.7.refs_2_.refs_1_ = bf16[16,16,128]{2,1,0:T(8,128)(2,1)S(1)} collective-permute-done((bf16[16,16,128]{2,1,0:T(8,128)(2,1)S(1)}, bf16[16,16,128]{2,1,0:T(8,128)(2,1)S(1)}, u32[]{:S(2)}, u32[]{:S(2)}) %collective-permute-start.7) | collective-permute-done | bytes 65568 | tf_op jit(solution)/shard_map/ppermute | solution.py:286
  26.7 1.0 %collective-permute-done.8.refs_3_.refs_2_ = bf16[16,16,128]{2,1,0:T(8,128)(2,1)S(1)} collective-permute-done((bf16[16,16,128]{2,1,0:T(8,128)(2,1)S(1)}, bf16[16,16,128]{2,1,0:T(8,128)(2,1)S(1)}, u32[]{:S(2)}, u32[]{:S(2)}) %collective-permute-start.8) | collective-permute-done | bytes 65568 | tf_op jit(solution)/shard_map/ppermute | solution.py:286
  27.9 1.5 %collective-permute-start.9 = (bf16[16,16,128]{2,1,0:T(8,128)(2,1)S(1)}, bf16[16,16,128]{2,1,0:T(8,128)(2,1)S(1)}, u32[]{:S(2)}, u32[]{:S(2)}) collective-permute-start(bf16[16,16,128]{2,1,0:T(8,128)(2,1)S(1)} %shard_map.90), channel_id=1, source_target_pairs={{0,2},{1,3},{2,0},{3,1},{4,6},{5,7},{6,4},{7,5},{8,10},{9,11},{10,... | collective-permute-start | bytes 196616 | tf_op jit(solution)/shard_map/ppermute | solution.py:286
  29.5 0.4 %shard_map.91 = (bf16[16,16,128]{2,1,0:T(8,128)(2,1)S(1)}, bf16[16,16,128]{2,1,0:T(8,128)(2,1)S(1)}) custom-call(f32[1024,128]{1,0:T(8,128)S(1)} %shard_map.87.panel, f32[16,16,128]{2,1,0:T(8,128)S(1)} %get-tuple-element.45.refs_1_.refs_2_.right), custom_call_target="tpu_custom_call" | custom-call | flops 1048576 | bytes 786432 | tf_op jit(solution)/shard_map/pallas_call | solution.py:258
  30.0 0.7 %collective-permute-start.11 = (bf16[16,16,128]{2,1,0:T(8,128)(2,1)S(1)}, bf16[16,16,128]{2,1,0:T(8,128)(2,1)S(1)}, u32[]{:S(2)}, u32[]{:S(2)}) collective-permute-start(bf16[16,16,128]{2,1,0:T(8,128)(2,1)S(1)} %get-tuple-element.48), channel_id=1, source_target_pairs={{0,1},{1,0},{2,3},{3,2},{4,5},{5,4},{6,7},{7,6},{8,9},{9,8},{10,11... | collective-permute-start | bytes 196616 | tf_op jit(solution)/shard_map/ppermute | solution.py:286
  30.6 0.7 %shard_map.95.refs_4_ = f32[256,128]{1,0:T(8,128)S(1)} custom-call(f32[64,16,128]{2,1,0:T(8,128)S(1)} %shard_map.88.panel, bf16[16,16,128]{2,1,0:T(8,128)(2,1)S(1)} %collective-permute-done.6.refs_1_.refs_0_, bf16[16,16,128]{2,1,0:T(8,128)(2,1)S(1)} %collective-permute-done.7.refs_2_.refs_1_, ...), custom_call_target="tpu_custom_call" | custom-call | tf_op jit(solution)/shard_map/pallas_call | solution.py:258
  31.6 0.7 %collective-permute-done.9.tile_ref = bf16[16,16,128]{2,1,0:T(8,128)(2,1)S(1)} collective-permute-done((bf16[16,16,128]{2,1,0:T(8,128)(2,1)S(1)}, bf16[16,16,128]{2,1,0:T(8,128)(2,1)S(1)}, u32[]{:S(2)}, u32[]{:S(2)}) %collective-permute-start.9) | collective-permute-done | bytes 65568 | tf_op jit(solution)/shard_map/ppermute | solution.py:286
  32.3 1.6 %collective-permute-done.10.tile_ref = bf16[16,16,128]{2,1,0:T(8,128)(2,1)S(1)} collective-permute-done((bf16[16,16,128]{2,1,0:T(8,128)(2,1)S(1)}, bf16[16,16,128]{2,1,0:T(8,128)(2,1)S(1)}, u32[]{:S(2)}, u32[]{:S(2)}) %collective-permute-start.10) | collective-permute-done | bytes 65568 | tf_op jit(solution)/shard_map/ppermute | solution.py:286
  33.9 0.9 %shard_map.96 = bf16[16,16,128]{2,1,0:T(8,128)(2,1)} custom-call(f32[16,16,128]{2,1,0:T(8,128)S(1)} %shard_map.94.base, bf16[16,16,128]{2,1,0:T(8,128)(2,1)S(1)} %collective-permute-done.11.refs_0_, f32[256,128]{1,0:T(8,128)S(1)} %get-tuple-element.49.refs_1_, f32[256,128]{1,0:T(8,128)S(1)} %get-tuple-element.50.refs_2_, ...), custom_call_target="tpu_custom_call" | custom-call | flops 16777216 | bytes 1343488 | tf_op jit(solution)/shard_map/pallas_call | solution.py:258
  (24 shorter events, 1.6 us)
Async XLA Ops:
  2.0 5.6 %collective-permute-start.2 = (bf16[16,16,128]{2,1,0:T(8,128)(2,1)S(1)}, bf16[16,16,128]{2,1,0:T(8,128)(2,1)S(1)}, u32[]{:S(2)}, u32[]{:S(2)}) collective-permute-start(bf16[16,16,128]{2,1,0:T(8,128)(2,1)S(1)} %shard_map.77.refs_0_), channel_id=1, source_target_pairs={{0,2},{1,3},{2,0},{3,1},{4,6},{5,7},{6,4},{7,5},{8,10},{9,11},{10,... | collective-permute-start | bytes 196616 | tf_op jit(solution)/shard_map/ppermute | solution.py:286
  5.0 4.1 %collective-permute-start = (bf16[16,16,128]{2,1,0:T(8,128)(2,1)S(1)}, bf16[16,16,128]{2,1,0:T(8,128)(2,1)S(1)}, u32[]{:S(2)}, u32[]{:S(2)}) collective-permute-start(bf16[16,16,128]{2,1,0:T(8,128)(2,1)S(1)} %shard_map.77.refs_0_), channel_id=1, source_target_pairs={{0,3},{1,2},{2,1},{3,0},{4,7},{5,6},{6,5},{7,4},{8,11},{9,10},{10,... | collective-permute-start | bytes 196616 | tf_op jit(solution)/shard_map/ppermute | solution.py:286
  5.0 4.1 %collective-permute-start.1 = (bf16[16,16,128]{2,1,0:T(8,128)(2,1)S(1)}, bf16[16,16,128]{2,1,0:T(8,128)(2,1)S(1)}, u32[]{:S(2)}, u32[]{:S(2)}) collective-permute-start(bf16[16,16,128]{2,1,0:T(8,128)(2,1)S(1)} %shard_map.77.refs_0_), channel_id=1, source_target_pairs={{0,1},{1,0},{2,3},{3,2},{4,5},{5,4},{6,7},{7,6},{8,9},{9,8},{10,11... | collective-permute-start | bytes 196616 | tf_op jit(solution)/shard_map/ppermute | solution.py:286
  9.6 6.6 %collective-permute-start.3 = (bf16[16,16,128]{2,1,0:T(8,128)(2,1)S(1)}, bf16[16,16,128]{2,1,0:T(8,128)(2,1)S(1)}, u32[]{:S(2)}, u32[]{:S(2)}) collective-permute-start(bf16[16,16,128]{2,1,0:T(8,128)(2,1)S(1)} %get-tuple-element.32), channel_id=1, source_target_pairs={{0,12},{4,8},{8,4},{12,0},{1,13},{5,9},{9,5},{13,1},{2,14},{6,10},... | collective-permute-start | bytes 196616 | tf_op jit(solution)/shard_map/ppermute | solution.py:286
  13.3 5.7 %collective-permute-start.4 = (bf16[16,16,128]{2,1,0:T(8,128)(2,1)S(1)}, bf16[16,16,128]{2,1,0:T(8,128)(2,1)S(1)}, u32[]{:S(2)}, u32[]{:S(2)}) collective-permute-start(bf16[16,16,128]{2,1,0:T(8,128)(2,1)S(1)} %get-tuple-element.33), channel_id=1, source_target_pairs={{0,8},{4,12},{8,0},{12,4},{1,9},{5,13},{9,1},{13,5},{2,10},{6,14},... | collective-permute-start | bytes 196616 | tf_op jit(solution)/shard_map/ppermute | solution.py:286
  13.4 5.7 %collective-permute-start.5 = (bf16[16,16,128]{2,1,0:T(8,128)(2,1)S(1)}, bf16[16,16,128]{2,1,0:T(8,128)(2,1)S(1)}, u32[]{:S(2)}, u32[]{:S(2)}) collective-permute-start(bf16[16,16,128]{2,1,0:T(8,128)(2,1)S(1)} %get-tuple-element.34), channel_id=1, source_target_pairs={{0,4},{4,0},{8,12},{12,8},{1,5},{5,1},{9,13},{13,9},{2,6},{6,2},{1... | collective-permute-start | bytes 196616 | tf_op jit(solution)/shard_map/ppermute | solution.py:286
  19.3 6.6 %collective-permute-start.6 = (bf16[16,16,128]{2,1,0:T(8,128)(2,1)S(1)}, bf16[16,16,128]{2,1,0:T(8,128)(2,1)S(1)}, u32[]{:S(2)}, u32[]{:S(2)}) collective-permute-start(bf16[16,16,128]{2,1,0:T(8,128)(2,1)S(1)} %get-tuple-element.40.refs_0_), channel_id=1, source_target_pairs={{0,12},{4,8},{8,4},{12,0},{1,13},{5,9},{9,5},{13,1},{2,14},{6,10},... | collective-permute-start | bytes 196616 | tf_op jit(solution)/shard_map/ppermute | solution.py:286
  22.1 4.6 %collective-permute-start.7 = (bf16[16,16,128]{2,1,0:T(8,128)(2,1)S(1)}, bf16[16,16,128]{2,1,0:T(8,128)(2,1)S(1)}, u32[]{:S(2)}, u32[]{:S(2)}) collective-permute-start(bf16[16,16,128]{2,1,0:T(8,128)(2,1)S(1)} %get-tuple-element.40.refs_0_), channel_id=1, source_target_pairs={{0,4},{4,0},{8,12},{12,8},{1,5},{5,1},{9,13},{13,9},{2,6},{6,2},{1... | collective-permute-start | bytes 196616 | tf_op jit(solution)/shard_map/ppermute | solution.py:286
  22.1 5.6 %collective-permute-start.8 = (bf16[16,16,128]{2,1,0:T(8,128)(2,1)S(1)}, bf16[16,16,128]{2,1,0:T(8,128)(2,1)S(1)}, u32[]{:S(2)}, u32[]{:S(2)}) collective-permute-start(bf16[16,16,128]{2,1,0:T(8,128)(2,1)S(1)} %get-tuple-element.40.refs_0_), channel_id=1, source_target_pairs={{0,8},{4,12},{8,0},{12,4},{1,9},{5,13},{9,1},{13,5},{2,10},{6,14},... | collective-permute-start | bytes 196616 | tf_op jit(solution)/shard_map/ppermute | solution.py:286
  23.9 0.9 %copy-start = (bf16[128,640]{1,0:T(8,128)(2,1)S(1)}, bf16[128,640]{1,0:T(8,128)(2,1)}, u32[]{:S(2)}) copy-start(bf16[128,640]{1,0:T(8,128)(2,1)} %refs_5_.3) | copy-start | bytes 491524
  23.9 0.9 %copy-start.1 = (bf16[128,128]{1,0:T(8,128)(2,1)S(1)}, bf16[128,128]{1,0:T(8,128)(2,1)}, u32[]{:S(2)}) copy-start(bf16[128,128]{1,0:T(8,128)(2,1)} %out_weight_ref.1) | copy-start | bytes 98308
  27.9 4.3 %collective-permute-start.9 = (bf16[16,16,128]{2,1,0:T(8,128)(2,1)S(1)}, bf16[16,16,128]{2,1,0:T(8,128)(2,1)S(1)}, u32[]{:S(2)}, u32[]{:S(2)}) collective-permute-start(bf16[16,16,128]{2,1,0:T(8,128)(2,1)S(1)} %shard_map.90), channel_id=1, source_target_pairs={{0,2},{1,3},{2,0},{3,1},{4,6},{5,7},{6,4},{7,5},{8,10},{9,11},{10,... | collective-permute-start | bytes 196616 | tf_op jit(solution)/shard_map/ppermute | solution.py:286
  29.9 4.0 %collective-permute-start.10 = (bf16[16,16,128]{2,1,0:T(8,128)(2,1)S(1)}, bf16[16,16,128]{2,1,0:T(8,128)(2,1)S(1)}, u32[]{:S(2)}, u32[]{:S(2)}) collective-permute-start(bf16[16,16,128]{2,1,0:T(8,128)(2,1)S(1)} %get-tuple-element.47), channel_id=1, source_target_pairs={{0,3},{1,2},{2,1},{3,0},{4,7},{5,6},{6,5},{7,4},{8,11},{9,10},{10,... | collective-permute-start | bytes 196616 | tf_op jit(solution)/shard_map/ppermute | solution.py:286
  30.0 3.9 %collective-permute-start.11 = (bf16[16,16,128]{2,1,0:T(8,128)(2,1)S(1)}, bf16[16,16,128]{2,1,0:T(8,128)(2,1)S(1)}, u32[]{:S(2)}, u32[]{:S(2)}) collective-permute-start(bf16[16,16,128]{2,1,0:T(8,128)(2,1)S(1)} %get-tuple-element.48), channel_id=1, source_target_pairs={{0,1},{1,0},{2,3},{3,2},{4,5},{5,4},{6,7},{7,6},{8,9},{9,8},{10,11... | collective-permute-start | bytes 196616 | tf_op jit(solution)/shard_map/ppermute | solution.py:286

commit v16 on v12

--- a/solution.py
+++ b/solution.py
@@ -183,7 +183,8 @@
         grad_ref[i] = normalize_back(tri_normed, scale, upstream_ref[here, :]).astype(bf16)
 
 
-def left_terms_kernel(grad_ref, right, out, grad):
+def left_terms_kernel(grad_ref, right, *refs):
+    out, grad = refs[-2:]
     size, _, channels = out.shape
     grad[...] = grad_ref[...].astype(f32).reshape(size * size, channels)
     weighted_sums(right, 0, [grad[pl.ds(j, size, stride=size), :] for j in range(size)], out)
@@ -270,6 +271,7 @@
     wait = 2**31
     steps = [step for bit in range(n.bit_length() - 2, -1, -1) for step in range(2**bit, 2 ** (bit + 1))]
     row_steps = list(range(n - 1, 0, -1))
+    gather_steps = [n - 1] + list(range(1, n - 1))
 
 
     def swap(values, axis, step):
@@ -326,18 +328,19 @@
     tri_normed, tri_grad = call(
         triangle_kernel, (flat, tile), total, part, upstream, flops=20 * pairs * channels,
     )
-    grads = gather(tri_grad, "row", row_steps)
+    grads = gather(tri_grad, "row", gather_steps)
     update, partial = call(
         update_kernel, (tile, flat), tri_normed, out_open, gate_factor, in_weights, out_weight,
         flops=4 * pairs * channels * channels,
     )
     (right_grad,) = call(functools.partial(right_grad_kernel, [0]), (wide,), left_panel, tri_grad)
-    right, partial, right_grad = lax.optimization_barrier((right, partial, right_grad))
-    terms = [None] * n
-    for step, grad in zip([0] + row_steps, grads):
-        (terms[step],) = call(
-            left_terms_kernel, (wide,), grad, right, scratch=[pltpu.VMEM((pairs, channels), f32)], flops=work,
+    terms, before = [None] * n, (partial, right_grad)
+    for step, grad in zip([0] + gather_steps, grads):
+        before = call(
+            left_terms_kernel, (wide,), grad, right, *before,
+            scratch=[pltpu.VMEM((pairs, channels), f32)], flops=work,
         )
+        terms[step] = before[0]
     total, *terms = call(
         functools.partial(pick_kernel, [0] + steps), (wide,) + (tile,) * (n - 1), *terms, flops=pairs * channels,
     )
@@ -346,7 +349,7 @@
         if step != steps[-1]:
             (total,) = call(add_kernel, (wide,), total, term, flops=wait)
     (share,) = call(
-        functools.partial(right_back_kernel, row_steps), (flat,),
+        functools.partial(right_back_kernel, gather_steps), (flat,),
         left_panel, *grads[1:], right_grad, factors, in_weights, partial,
         scratch=[pltpu.VMEM(wide.shape, f32)],
     )

time: 35.9 us -> 34.9 us (0.972)
  waiting for transfers between devices: 11.4 us -> 10.4 us
    ppermute x12, waiting for transfers between devices: 11.4 us -> 10.4 us  [swap(): return lax.ppermute(values, axis, [(a, a ^ step) for a in range(n)])]
  transfers between devices with their start and end apart: 12 -> 12, of which waited for: 7 -> 8; matrix products, arithmetic and copies ran while one was open for 0% -> 0% of each run, Pallas kernels for 12% -> 13%
where the time goes in v16:
time: 34.9 us; the launch traced here: 34.7 us
  starting transfers between devices  14.3 us (41%)
  waiting for transfers between devices  10.4 us (30%)
  Pallas kernels  7.81 us (22%)
  between operations  1.43 us (4%)
  local copies, waits for them, and re-layouts  0.71 us (2%)
    ppermute x12, starting transfers between devices, swap(): return lax.ppermute(values, axis, [(a, a ^ step) for a in range(n)])  14.3 us
    ppermute x12, waiting for transfers between devices, swap(): return lax.ppermute(values, axis, [(a, a ^ step) for a in range(n)])  10.4 us
    pallas_call x21, Pallas kernels, call(): pl.pallas_call(kernel, out_shape=tuple(outs), in_specs=specs, out_specs=(...  7.81 us
    unnamed x4, local copies, waits for them, and re-layouts  0.71 us
  transfers between devices with their start and end apart: 12, of which 8 were waited for; matrix products, arithmetic and copies ran while one was open for 0% of the time, Pallas kernels for 13%

profile of v16, /device:TPU:0, one launch (start us, length us, event | category | flops | bytes accessed | tf_op | source)
XLA Modules:
  0.0 34.7 jit_solution(15004852000558326133)
XLA Ops:
  0.6 1.3 %shard_map.77.refs_0_ = bf16[16,16,128]{2,1,0:T(8,128)(2,1)S(1)} custom-call(bf16[16,16,128]{2,1,0:T(8,128)(2,1)} %acts_in.3, s32[16,16]{1,0:T(8,128)} %mask_in.3, bf16[128,640]{1,0:T(8,128)(2,1)} %refs_5_.3), custom_call_target="tpu_custom_call" | custom-call | flops 16777216 | bytes 295936 | tf_op jit(solution)/shard_map/pallas_call | solution.py:250
  2.0 3.0 %collective-permute-start.2 = (bf16[16,16,128]{2,1,0:T(8,128)(2,1)S(1)}, bf16[16,16,128]{2,1,0:T(8,128)(2,1)S(1)}, u32[]{:S(2)}, u32[]{:S(2)}) collective-permute-start(bf16[16,16,128]{2,1,0:T(8,128)(2,1)S(1)} %shard_map.77.refs_0_), channel_id=1, source_target_pairs={{0,2},{1,3},{2,0},{3,1},{4,6},{5,7},{6,4},{7,5},{8,10},{9,11},{10,... | collective-permute-start | bytes 196616 | tf_op jit(solution)/shard_map/ppermute | solution.py:278
  5.8 1.5 %shard_map.78 = (f32[16,16,128]{2,1,0:T(8,128)S(1)}, f32[256,128]{1,0:T(8,128)S(1)}, f32[256,128]{1,0:T(8,128)S(1)}, f32[4,256,128]{2,1,0:T(8,128)S(1)}, f32[256...) custom-call(bf16[16,16,128]{2,1,0:T(8,128)(2,1)} %acts_in.3, s32[16,16]{1,0:T(8,128)} %mask_in.3, ...), custom_call_target="tpu_custom_call" | custom-call | flops 50331648 | bytes 1639428 | tf_op jit(solution)/shard_map/pallas_call | solution.py:250
  7.8 1.4 %collective-permute-done.refs_0_.refs_2_ = bf16[16,16,128]{2,1,0:T(8,128)(2,1)S(1)} collective-permute-done((bf16[16,16,128]{2,1,0:T(8,128)(2,1)S(1)}, bf16[16,16,128]{2,1,0:T(8,128)(2,1)S(1)}, u32[]{:S(2)}, u32[]{:S(2)}) %collective-permute-start) | collective-permute-done | bytes 65568 | tf_op jit(solution)/shard_map/ppermute | solution.py:278
  9.1 0.4 %shard_map.80 = (f32[16,16,128]{2,1,0:T(8,128)S(1)}, f32[16,16,128]{2,1,0:T(8,128)S(1)}) custom-call(s32[1]{0:T(128)S(6)} %copy.8.crop_ref, bf16[16,16,128]{2,1,0:T(8,128)(2,1)S(1)} %collective-permute-done.refs_0_.refs_2_, bf16[16,16,128]{2,1,0:T(8,128)(2,1)S(1)} %collective-permute-done.1.refs_1_.refs_3_, ...), custom_call_target="tpu_custom_call" | custom-call | flops 1048576 | bytes 524292 | tf_op jit(solution)/shard_map/pallas_call | solution.py:250
  9.6 3.7 %collective-permute-start.3 = (bf16[16,16,128]{2,1,0:T(8,128)(2,1)S(1)}, bf16[16,16,128]{2,1,0:T(8,128)(2,1)S(1)}, u32[]{:S(2)}, u32[]{:S(2)}) collective-permute-start(bf16[16,16,128]{2,1,0:T(8,128)(2,1)S(1)} %get-tuple-element.27), channel_id=1, source_target_pairs={{0,12},{4,8},{8,4},{12,0},{1,13},{5,9},{9,5},{13,1},{2,14},{6,10},... | collective-permute-start | bytes 196616 | tf_op jit(solution)/shard_map/ppermute | solution.py:278
  13.4 0.7 %collective-permute-start.5 = (bf16[16,16,128]{2,1,0:T(8,128)(2,1)S(1)}, bf16[16,16,128]{2,1,0:T(8,128)(2,1)S(1)}, u32[]{:S(2)}, u32[]{:S(2)}) collective-permute-start(bf16[16,16,128]{2,1,0:T(8,128)(2,1)S(1)} %get-tuple-element.29), channel_id=1, source_target_pairs={{0,4},{4,0},{8,12},{12,8},{1,5},{5,1},{9,13},{13,9},{2,6},{6,2},{1... | collective-permute-start | bytes 196616 | tf_op jit(solution)/shard_map/ppermute | solution.py:278
  14.1 2.1 %collective-permute-done.3.tile_ref = bf16[16,16,128]{2,1,0:T(8,128)(2,1)S(1)} collective-permute-done((bf16[16,16,128]{2,1,0:T(8,128)(2,1)S(1)}, bf16[16,16,128]{2,1,0:T(8,128)(2,1)S(1)}, u32[]{:S(2)}, u32[]{:S(2)}) %collective-permute-start.3) | collective-permute-done | bytes 65568 | tf_op jit(solution)/shard_map/ppermute | solution.py:278
  16.2 2.8 %collective-permute-done.4.tile_ref = bf16[16,16,128]{2,1,0:T(8,128)(2,1)S(1)} collective-permute-done((bf16[16,16,128]{2,1,0:T(8,128)(2,1)S(1)}, bf16[16,16,128]{2,1,0:T(8,128)(2,1)S(1)}, u32[]{:S(2)}, u32[]{:S(2)}) %collective-permute-start.4) | collective-permute-done | bytes 65568 | tf_op jit(solution)/shard_map/ppermute | solution.py:278
  19.1 0.3 shard_map.85
  19.3 2.7 %collective-permute-start.7 = (bf16[16,16,128]{2,1,0:T(8,128)(2,1)S(1)}, bf16[16,16,128]{2,1,0:T(8,128)(2,1)S(1)}, u32[]{:S(2)}, u32[]{:S(2)}) collective-permute-start(bf16[16,16,128]{2,1,0:T(8,128)(2,1)S(1)} %get-tuple-element.35.refs_0_.grad_ref), channel_id=1, source_target_pairs={{0,12},{4,8},{8,4},{12,0},{1,13},{5,9},{9,5},{13,1},{2,14},{6,10},... | collective-permute-start | bytes 196616 | tf_op jit(solution)/shard_map/ppermute | solution.py:278
  22.1 1.7 %collective-permute-start.8 = (bf16[16,16,128]{2,1,0:T(8,128)(2,1)S(1)}, bf16[16,16,128]{2,1,0:T(8,128)(2,1)S(1)}, u32[]{:S(2)}, u32[]{:S(2)}) collective-permute-start(bf16[16,16,128]{2,1,0:T(8,128)(2,1)S(1)} %get-tuple-element.35.refs_0_.grad_ref), channel_id=1, source_target_pairs={{0,8},{4,12},{8,0},{12,4},{1,9},{5,13},{9,1},{13,5},{2,10},{6,14},... | collective-permute-start | bytes 196616 | tf_op jit(solution)/shard_map/ppermute | solution.py:278
  24.1 0.7 %copy-done = bf16[128,640]{1,0:T(8,128)(2,1)S(1)} copy-done((bf16[128,640]{1,0:T(8,128)(2,1)S(1)}, bf16[128,640]{1,0:T(8,128)(2,1)}, u32[]{:S(2)}) %copy-start) | copy-done | bytes 163864
  24.8 0.8 %shard_map.86 = (bf16[16,16,128]{2,1,0:T(8,128)(2,1)}, f32[256,128]{1,0:T(8,128)S(1)}) custom-call(f32[256,128]{1,0:T(8,128)S(1)} %get-tuple-element.31.tri_normed_ref, f32[256,128]{1,0:T(8,128)S(1)} %get-tuple-element.32.open_ref, f32[256,128]{1,0:T(8,128)S(1)} %get-tuple-element.33.gate_factor_ref, bf16[128,640]{1,0:T(8,128)(2,1)S(1)} %copy-done, ...), custom_call_target="tpu_custom_call" | custom-call | flops 16777216 | bytes 786432 | tf_op jit(solution)/shard_map/pallas_call | solution.py:250
  25.6 0.2 shard_map.89.refs_0_
  26.1 0.6 %collective-permute-done.6.grad_ref.refs_1_ = bf16[16,16,128]{2,1,0:T(8,128)(2,1)S(1)} collective-permute-done((bf16[16,16,128]{2,1,0:T(8,128)(2,1)S(1)}, bf16[16,16,128]{2,1,0:T(8,128)(2,1)S(1)}, u32[]{:S(2)}, u32[]{:S(2)}) %collective-permute-start.6) | collective-permute-done | bytes 65568 | tf_op jit(solution)/shard_map/ppermute | solution.py:278
  26.7 0.2 shard_map.91.refs_0_.refs_1_
  26.9 0.7 %collective-permute-done.8.grad_ref.refs_2_ = bf16[16,16,128]{2,1,0:T(8,128)(2,1)S(1)} collective-permute-done((bf16[16,16,128]{2,1,0:T(8,128)(2,1)S(1)}, bf16[16,16,128]{2,1,0:T(8,128)(2,1)S(1)}, u32[]{:S(2)}, u32[]{:S(2)}) %collective-permute-start.8) | collective-permute-done | bytes 65568 | tf_op jit(solution)/shard_map/ppermute | solution.py:278
  28.0 1.8 %collective-permute-start.9 = (bf16[16,16,128]{2,1,0:T(8,128)(2,1)S(1)}, bf16[16,16,128]{2,1,0:T(8,128)(2,1)S(1)}, u32[]{:S(2)}, u32[]{:S(2)}) collective-permute-start(bf16[16,16,128]{2,1,0:T(8,128)(2,1)S(1)} %get-tuple-element.38), channel_id=1, source_target_pairs={{0,2},{1,3},{2,0},{3,1},{4,6},{5,7},{6,4},{7,5},{8,10},{9,11},{10,... | collective-permute-start | bytes 196616 | tf_op jit(solution)/shard_map/ppermute | solution.py:278
  29.8 0.4 %collective-permute-start.11 = (bf16[16,16,128]{2,1,0:T(8,128)(2,1)S(1)}, bf16[16,16,128]{2,1,0:T(8,128)(2,1)S(1)}, u32[]{:S(2)}, u32[]{:S(2)}) collective-permute-start(bf16[16,16,128]{2,1,0:T(8,128)(2,1)S(1)} %get-tuple-element.40), channel_id=1, source_target_pairs={{0,1},{1,0},{2,3},{3,2},{4,5},{5,4},{6,7},{7,6},{8,9},{9,8},{10,11... | collective-permute-start | bytes 196616 | tf_op jit(solution)/shard_map/ppermute | solution.py:278
  30.2 0.7 %shard_map.96.refs_4_ = f32[256,128]{1,0:T(8,128)S(1)} custom-call(f32[64,16,128]{2,1,0:T(8,128)S(1)} %shard_map.87.panel, bf16[16,16,128]{2,1,0:T(8,128)(2,1)S(1)} %collective-permute-done.7.grad_ref.refs_0_, bf16[16,16,128]{2,1,0:T(8,128)(2,1)S(1)} %collective-permute-done.6.grad_ref.refs_1_, ...), custom_call_target="tpu_custom_call" | custom-call | tf_op jit(solution)/shard_map/pallas_call | solution.py:250
  31.0 1.4 %collective-permute-done.9.tile_ref = bf16[16,16,128]{2,1,0:T(8,128)(2,1)S(1)} collective-permute-done((bf16[16,16,128]{2,1,0:T(8,128)(2,1)S(1)}, bf16[16,16,128]{2,1,0:T(8,128)(2,1)S(1)}, u32[]{:S(2)}, u32[]{:S(2)}) %collective-permute-start.9) | collective-permute-done | bytes 65568 | tf_op jit(solution)/shard_map/ppermute | solution.py:278
  32.4 1.4 %collective-permute-done.10.tile_ref = bf16[16,16,128]{2,1,0:T(8,128)(2,1)S(1)} collective-permute-done((bf16[16,16,128]{2,1,0:T(8,128)(2,1)S(1)}, bf16[16,16,128]{2,1,0:T(8,128)(2,1)S(1)}, u32[]{:S(2)}, u32[]{:S(2)}) %collective-permute-start.10) | collective-permute-done | bytes 65568 | tf_op jit(solution)/shard_map/ppermute | solution.py:278
  33.8 0.9 %shard_map.97 = bf16[16,16,128]{2,1,0:T(8,128)(2,1)} custom-call(f32[16,16,128]{2,1,0:T(8,128)S(1)} %shard_map.95.base, bf16[16,16,128]{2,1,0:T(8,128)(2,1)S(1)} %collective-permute-done.11.refs_0_, f32[256,128]{1,0:T(8,128)S(1)} %get-tuple-element.41.refs_1_, f32[256,128]{1,0:T(8,128)S(1)} %get-tuple-element.42.refs_2_, ...), custom_call_target="tpu_custom_call" | custom-call | flops 16777216 | bytes 1343488 | tf_op jit(solution)/shard_map/pallas_call | solution.py:250
  (25 shorter events, 1.7 us)
Async XLA Ops:
  2.0 5.6 %collective-permute-start.2 = (bf16[16,16,128]{2,1,0:T(8,128)(2,1)S(1)}, bf16[16,16,128]{2,1,0:T(8,128)(2,1)S(1)}, u32[]{:S(2)}, u32[]{:S(2)}) collective-permute-start(bf16[16,16,128]{2,1,0:T(8,128)(2,1)S(1)} %shard_map.77.refs_0_), channel_id=1, source_target_pairs={{0,2},{1,3},{2,0},{3,1},{4,6},{5,7},{6,4},{7,5},{8,10},{9,11},{10,... | collective-permute-start | bytes 196616 | tf_op jit(solution)/shard_map/ppermute | solution.py:278
  5.0 4.1 %collective-permute-start = (bf16[16,16,128]{2,1,0:T(8,128)(2,1)S(1)}, bf16[16,16,128]{2,1,0:T(8,128)(2,1)S(1)}, u32[]{:S(2)}, u32[]{:S(2)}) collective-permute-start(bf16[16,16,128]{2,1,0:T(8,128)(2,1)S(1)} %shard_map.77.refs_0_), channel_id=1, source_target_pairs={{0,3},{1,2},{2,1},{3,0},{4,7},{5,6},{6,5},{7,4},{8,11},{9,10},{10,... | collective-permute-start | bytes 196616 | tf_op jit(solution)/shard_map/ppermute | solution.py:278
  5.0 4.1 %collective-permute-start.1 = (bf16[16,16,128]{2,1,0:T(8,128)(2,1)S(1)}, bf16[16,16,128]{2,1,0:T(8,128)(2,1)S(1)}, u32[]{:S(2)}, u32[]{:S(2)}) collective-permute-start(bf16[16,16,128]{2,1,0:T(8,128)(2,1)S(1)} %shard_map.77.refs_0_), channel_id=1, source_target_pairs={{0,1},{1,0},{2,3},{3,2},{4,5},{5,4},{6,7},{7,6},{8,9},{9,8},{10,11... | collective-permute-start | bytes 196616 | tf_op jit(solution)/shard_map/ppermute | solution.py:278
  9.6 6.6 %collective-permute-start.3 = (bf16[16,16,128]{2,1,0:T(8,128)(2,1)S(1)}, bf16[16,16,128]{2,1,0:T(8,128)(2,1)S(1)}, u32[]{:S(2)}, u32[]{:S(2)}) collective-permute-start(bf16[16,16,128]{2,1,0:T(8,128)(2,1)S(1)} %get-tuple-element.27), channel_id=1, source_target_pairs={{0,12},{4,8},{8,4},{12,0},{1,13},{5,9},{9,5},{13,1},{2,14},{6,10},... | collective-permute-start | bytes 196616 | tf_op jit(solution)/shard_map/ppermute | solution.py:278
  13.3 5.7 %collective-permute-start.4 = (bf16[16,16,128]{2,1,0:T(8,128)(2,1)S(1)}, bf16[16,16,128]{2,1,0:T(8,128)(2,1)S(1)}, u32[]{:S(2)}, u32[]{:S(2)}) collective-permute-start(bf16[16,16,128]{2,1,0:T(8,128)(2,1)S(1)} %get-tuple-element.28), channel_id=1, source_target_pairs={{0,8},{4,12},{8,0},{12,4},{1,9},{5,13},{9,1},{13,5},{2,10},{6,14},... | collective-permute-start | bytes 196616 | tf_op jit(solution)/shard_map/ppermute | solution.py:278
  13.4 5.7 %collective-permute-start.5 = (bf16[16,16,128]{2,1,0:T(8,128)(2,1)S(1)}, bf16[16,16,128]{2,1,0:T(8,128)(2,1)S(1)}, u32[]{:S(2)}, u32[]{:S(2)}) collective-permute-start(bf16[16,16,128]{2,1,0:T(8,128)(2,1)S(1)} %get-tuple-element.29), channel_id=1, source_target_pairs={{0,4},{4,0},{8,12},{12,8},{1,5},{5,1},{9,13},{13,9},{2,6},{6,2},{1... | collective-permute-start | bytes 196616 | tf_op jit(solution)/shard_map/ppermute | solution.py:278
  19.3 6.6 %collective-permute-start.7 = (bf16[16,16,128]{2,1,0:T(8,128)(2,1)S(1)}, bf16[16,16,128]{2,1,0:T(8,128)(2,1)S(1)}, u32[]{:S(2)}, u32[]{:S(2)}) collective-permute-start(bf16[16,16,128]{2,1,0:T(8,128)(2,1)S(1)} %get-tuple-element.35.refs_0_.grad_ref), channel_id=1, source_target_pairs={{0,12},{4,8},{8,4},{12,0},{1,13},{5,9},{9,5},{13,1},{2,14},{6,10},... | collective-permute-start | bytes 196616 | tf_op jit(solution)/shard_map/ppermute | solution.py:278
  22.1 4.6 %collective-permute-start.6 = (bf16[16,16,128]{2,1,0:T(8,128)(2,1)S(1)}, bf16[16,16,128]{2,1,0:T(8,128)(2,1)S(1)}, u32[]{:S(2)}, u32[]{:S(2)}) collective-permute-start(bf16[16,16,128]{2,1,0:T(8,128)(2,1)S(1)} %get-tuple-element.35.refs_0_.grad_ref), channel_id=1, source_target_pairs={{0,4},{4,0},{8,12},{12,8},{1,5},{5,1},{9,13},{13,9},{2,6},{6,2},{1... | collective-permute-start | bytes 196616 | tf_op jit(solution)/shard_map/ppermute | solution.py:278
  22.1 5.6 %collective-permute-start.8 = (bf16[16,16,128]{2,1,0:T(8,128)(2,1)S(1)}, bf16[16,16,128]{2,1,0:T(8,128)(2,1)S(1)}, u32[]{:S(2)}, u32[]{:S(2)}) collective-permute-start(bf16[16,16,128]{2,1,0:T(8,128)(2,1)S(1)} %get-tuple-element.35.refs_0_.grad_ref), channel_id=1, source_target_pairs={{0,8},{4,12},{8,0},{12,4},{1,9},{5,13},{9,1},{13,5},{2,10},{6,14},... | collective-permute-start | bytes 196616 | tf_op jit(solution)/shard_map/ppermute | solution.py:278
  23.9 0.9 %copy-start = (bf16[128,640]{1,0:T(8,128)(2,1)S(1)}, bf16[128,640]{1,0:T(8,128)(2,1)}, u32[]{:S(2)}) copy-start(bf16[128,640]{1,0:T(8,128)(2,1)} %refs_5_.3) | copy-start | bytes 491524
  23.9 0.9 %copy-start.1 = (bf16[128,128]{1,0:T(8,128)(2,1)S(1)}, bf16[128,128]{1,0:T(8,128)(2,1)}, u32[]{:S(2)}) copy-start(bf16[128,128]{1,0:T(8,128)(2,1)} %out_weight_ref.1) | copy-start | bytes 98308
  28.0 4.3 %collective-permute-start.9 = (bf16[16,16,128]{2,1,0:T(8,128)(2,1)S(1)}, bf16[16,16,128]{2,1,0:T(8,128)(2,1)S(1)}, u32[]{:S(2)}, u32[]{:S(2)}) collective-permute-start(bf16[16,16,128]{2,1,0:T(8,128)(2,1)S(1)} %get-tuple-element.38), channel_id=1, source_target_pairs={{0,2},{1,3},{2,0},{3,1},{4,6},{5,7},{6,4},{7,5},{8,10},{9,11},{10,... | collective-permute-start | bytes 196616 | tf_op jit(solution)/shard_map/ppermute | solution.py:278
  29.8 4.0 %collective-permute-start.10 = (bf16[16,16,128]{2,1,0:T(8,128)(2,1)S(1)}, bf16[16,16,128]{2,1,0:T(8,128)(2,1)S(1)}, u32[]{:S(2)}, u32[]{:S(2)}) collective-permute-start(bf16[16,16,128]{2,1,0:T(8,128)(2,1)S(1)} %get-tuple-element.39), channel_id=1, source_target_pairs={{0,3},{1,2},{2,1},{3,0},{4,7},{5,6},{6,5},{7,4},{8,11},{9,10},{10,... | collective-permute-start | bytes 196616 | tf_op jit(solution)/shard_map/ppermute | solution.py:278
  29.8 4.0 %collective-permute-start.11 = (bf16[16,16,128]{2,1,0:T(8,128)(2,1)S(1)}, bf16[16,16,128]{2,1,0:T(8,128)(2,1)S(1)}, u32[]{:S(2)}, u32[]{:S(2)}) collective-permute-start(bf16[16,16,128]{2,1,0:T(8,128)(2,1)S(1)} %get-tuple-element.40), channel_id=1, source_target_pairs={{0,1},{1,0},{2,3},{3,2},{4,5},{5,4},{6,7},{7,6},{8,9},{9,8},{10,11... | collective-permute-start | bytes 196616 | tf_op jit(solution)/shard_map/ppermute | solution.py:278

commit v17 on v16

--- a/solution.py
+++ b/solution.py
@@ -271,7 +271,7 @@
     wait = 2**31
     steps = [step for bit in range(n.bit_length() - 2, -1, -1) for step in range(2**bit, 2 ** (bit + 1))]
     row_steps = list(range(n - 1, 0, -1))
-    gather_steps = [n - 1] + list(range(1, n - 1))
+    gather_steps = steps
 
 
     def swap(values, axis, step):

time: 34.9 us -> 35 us (level)
  waiting for transfers between devices: 10.4 us -> 11.4 us
  starting transfers between devices: 14.3 us -> 13.4 us
    ppermute x12, waiting for transfers between devices: 10.4 us -> 11.4 us  [swap(): return lax.ppermute(values, axis, [(a, a ^ step) for a in range(n)])]
    ppermute x12, starting transfers between devices: 14.3 us -> 13.4 us  [swap(): return lax.ppermute(values, axis, [(a, a ^ step) for a in range(n)])]
  transfers between devices with their start and end apart: 12 -> 12, of which waited for: 8 -> 7; matrix products, arithmetic and copies ran while one was open for 0% -> 0% of each run, Pallas kernels for 13% -> 13%
where the time goes in v17:
time: 35 us; the launch traced here: 34.8 us
  starting transfers between devices  13.4 us (38%)
  waiting for transfers between devices  11.4 us (33%)
  Pallas kernels  7.82 us (22%)
  between operations  1.44 us (4%)
  local copies, waits for them, and re-layouts  0.71 us (2%)
    ppermute x12, starting transfers between devices, swap(): return lax.ppermute(values, axis, [(a, a ^ step) for a in range(n)])  13.4 us
    ppermute x12, waiting for transfers between devices, swap(): return lax.ppermute(values, axis, [(a, a ^ step) for a in range(n)])  11.4 us
    pallas_call x21, Pallas kernels, call(): pl.pallas_call(kernel, out_shape=tuple(outs), in_specs=specs, out_specs=(...  7.82 us
    unnamed x4, local copies, waits for them, and re-layouts  0.71 us
  transfers between devices with their start and end apart: 12, of which 7 were waited for; matrix products, arithmetic and copies ran while one was open for 0% of the time, Pallas kernels for 13%

profile of v17, /device:TPU:0, one launch (start us, length us, event | category | flops | bytes accessed | tf_op | source)
XLA Modules:
  0.0 34.8 jit_solution(7026597576265923391)
XLA Ops:
  0.6 1.3 %shard_map.77.refs_0_ = bf16[16,16,128]{2,1,0:T(8,128)(2,1)S(1)} custom-call(bf16[16,16,128]{2,1,0:T(8,128)(2,1)} %acts_in.3, s32[16,16]{1,0:T(8,128)} %mask_in.3, bf16[128,640]{1,0:T(8,128)(2,1)} %refs_5_.3), custom_call_target="tpu_custom_call" | custom-call | flops 16777216 | bytes 295936 | tf_op jit(solution)/shard_map/pallas_call | solution.py:250
  2.0 3.0 %collective-permute-start.2 = (bf16[16,16,128]{2,1,0:T(8,128)(2,1)S(1)}, bf16[16,16,128]{2,1,0:T(8,128)(2,1)S(1)}, u32[]{:S(2)}, u32[]{:S(2)}) collective-permute-start(bf16[16,16,128]{2,1,0:T(8,128)(2,1)S(1)} %shard_map.77.refs_0_), channel_id=1, source_target_pairs={{0,2},{1,3},{2,0},{3,1},{4,6},{5,7},{6,4},{7,5},{8,10},{9,11},{10,... | collective-permute-start | bytes 196616 | tf_op jit(solution)/shard_map/ppermute | solution.py:278
  5.8 1.5 %shard_map.78 = (f32[16,16,128]{2,1,0:T(8,128)S(1)}, f32[256,128]{1,0:T(8,128)S(1)}, f32[256,128]{1,0:T(8,128)S(1)}, f32[4,256,128]{2,1,0:T(8,128)S(1)}, f32[256...) custom-call(bf16[16,16,128]{2,1,0:T(8,128)(2,1)} %acts_in.3, s32[16,16]{1,0:T(8,128)} %mask_in.3, ...), custom_call_target="tpu_custom_call" | custom-call | flops 50331648 | bytes 1639428 | tf_op jit(solution)/shard_map/pallas_call | solution.py:250
  7.8 1.4 %collective-permute-done.refs_0_.refs_2_ = bf16[16,16,128]{2,1,0:T(8,128)(2,1)S(1)} collective-permute-done((bf16[16,16,128]{2,1,0:T(8,128)(2,1)S(1)}, bf16[16,16,128]{2,1,0:T(8,128)(2,1)S(1)}, u32[]{:S(2)}, u32[]{:S(2)}) %collective-permute-start) | collective-permute-done | bytes 65568 | tf_op jit(solution)/shard_map/ppermute | solution.py:278
  9.1 0.4 %shard_map.80 = (f32[16,16,128]{2,1,0:T(8,128)S(1)}, f32[16,16,128]{2,1,0:T(8,128)S(1)}) custom-call(s32[1]{0:T(128)S(6)} %copy.8.crop_ref, bf16[16,16,128]{2,1,0:T(8,128)(2,1)S(1)} %collective-permute-done.refs_0_.refs_2_, bf16[16,16,128]{2,1,0:T(8,128)(2,1)S(1)} %collective-permute-done.1.refs_1_.refs_3_, ...), custom_call_target="tpu_custom_call" | custom-call | flops 1048576 | bytes 524292 | tf_op jit(solution)/shard_map/pallas_call | solution.py:250
  9.6 3.7 %collective-permute-start.3 = (bf16[16,16,128]{2,1,0:T(8,128)(2,1)S(1)}, bf16[16,16,128]{2,1,0:T(8,128)(2,1)S(1)}, u32[]{:S(2)}, u32[]{:S(2)}) collective-permute-start(bf16[16,16,128]{2,1,0:T(8,128)(2,1)S(1)} %get-tuple-element.27), channel_id=1, source_target_pairs={{0,12},{4,8},{8,4},{12,0},{1,13},{5,9},{9,5},{13,1},{2,14},{6,10},... | collective-permute-start | bytes 196616 | tf_op jit(solution)/shard_map/ppermute | solution.py:278
  13.4 0.7 %collective-permute-start.5 = (bf16[16,16,128]{2,1,0:T(8,128)(2,1)S(1)}, bf16[16,16,128]{2,1,0:T(8,128)(2,1)S(1)}, u32[]{:S(2)}, u32[]{:S(2)}) collective-permute-start(bf16[16,16,128]{2,1,0:T(8,128)(2,1)S(1)} %get-tuple-element.29), channel_id=1, source_target_pairs={{0,4},{4,0},{8,12},{12,8},{1,5},{5,1},{9,13},{13,9},{2,6},{6,2},{1... | collective-permute-start | bytes 196616 | tf_op jit(solution)/shard_map/ppermute | solution.py:278
  14.1 2.1 %collective-permute-done.3.tile_ref = bf16[16,16,128]{2,1,0:T(8,128)(2,1)S(1)} collective-permute-done((bf16[16,16,128]{2,1,0:T(8,128)(2,1)S(1)}, bf16[16,16,128]{2,1,0:T(8,128)(2,1)S(1)}, u32[]{:S(2)}, u32[]{:S(2)}) %collective-permute-start.3) | collective-permute-done | bytes 65568 | tf_op jit(solution)/shard_map/ppermute | solution.py:278
  16.2 2.8 %collective-permute-done.4.tile_ref = bf16[16,16,128]{2,1,0:T(8,128)(2,1)S(1)} collective-permute-done((bf16[16,16,128]{2,1,0:T(8,128)(2,1)S(1)}, bf16[16,16,128]{2,1,0:T(8,128)(2,1)S(1)}, u32[]{:S(2)}, u32[]{:S(2)}) %collective-permute-start.4) | collective-permute-done | bytes 65568 | tf_op jit(solution)/shard_map/ppermute | solution.py:278
  19.1 0.3 shard_map.85
  19.3 1.5 %collective-permute-start.8 = (bf16[16,16,128]{2,1,0:T(8,128)(2,1)S(1)}, bf16[16,16,128]{2,1,0:T(8,128)(2,1)S(1)}, u32[]{:S(2)}, u32[]{:S(2)}) collective-permute-start(bf16[16,16,128]{2,1,0:T(8,128)(2,1)S(1)} %get-tuple-element.35.refs_0_.grad_ref), channel_id=1, source_target_pairs={{0,8},{4,12},{8,0},{12,4},{1,9},{5,13},{9,1},{13,5},{2,10},{6,14},... | collective-permute-start | bytes 196616 | tf_op jit(solution)/shard_map/ppermute | solution.py:278
  20.9 1.9 %collective-permute-start.7 = (bf16[16,16,128]{2,1,0:T(8,128)(2,1)S(1)}, bf16[16,16,128]{2,1,0:T(8,128)(2,1)S(1)}, u32[]{:S(2)}, u32[]{:S(2)}) collective-permute-start(bf16[16,16,128]{2,1,0:T(8,128)(2,1)S(1)} %get-tuple-element.35.refs_0_.grad_ref), channel_id=1, source_target_pairs={{0,12},{4,8},{8,4},{12,0},{1,13},{5,9},{9,5},{13,1},{2,14},{6,10},... | collective-permute-start | bytes 196616 | tf_op jit(solution)/shard_map/ppermute | solution.py:278
  23.2 0.7 %copy-done = bf16[128,640]{1,0:T(8,128)(2,1)S(1)} copy-done((bf16[128,640]{1,0:T(8,128)(2,1)S(1)}, bf16[128,640]{1,0:T(8,128)(2,1)}, u32[]{:S(2)}) %copy-start) | copy-done | bytes 163864
  23.9 0.8 %shard_map.86 = (bf16[16,16,128]{2,1,0:T(8,128)(2,1)}, f32[256,128]{1,0:T(8,128)S(1)}) custom-call(f32[256,128]{1,0:T(8,128)S(1)} %get-tuple-element.31.tri_normed_ref, f32[256,128]{1,0:T(8,128)S(1)} %get-tuple-element.32.open_ref, f32[256,128]{1,0:T(8,128)S(1)} %get-tuple-element.33.gate_factor_ref, bf16[128,640]{1,0:T(8,128)(2,1)S(1)} %copy-done, ...), custom_call_target="tpu_custom_call" | custom-call | flops 16777216 | bytes 786432 | tf_op jit(solution)/shard_map/pallas_call | solution.py:250
  24.7 0.2 shard_map.89.refs_0_
  24.9 2.2 %collective-permute-done.8.grad_ref.refs_0_ = bf16[16,16,128]{2,1,0:T(8,128)(2,1)S(1)} collective-permute-done((bf16[16,16,128]{2,1,0:T(8,128)(2,1)S(1)}, bf16[16,16,128]{2,1,0:T(8,128)(2,1)S(1)}, u32[]{:S(2)}, u32[]{:S(2)}) %collective-permute-start.8) | collective-permute-done | bytes 65568 | tf_op jit(solution)/shard_map/ppermute | solution.py:278
  27.2 0.2 shard_map.90.refs_0_.refs_2_
  27.4 0.2 shard_map.91.refs_0_.refs_3_
  28.1 1.3 %collective-permute-start.9 = (bf16[16,16,128]{2,1,0:T(8,128)(2,1)S(1)}, bf16[16,16,128]{2,1,0:T(8,128)(2,1)S(1)}, u32[]{:S(2)}, u32[]{:S(2)}) collective-permute-start(bf16[16,16,128]{2,1,0:T(8,128)(2,1)S(1)} %get-tuple-element.38), channel_id=1, source_target_pairs={{0,2},{1,3},{2,0},{3,1},{4,6},{5,7},{6,4},{7,5},{8,10},{9,11},{10,... | collective-permute-start | bytes 196616 | tf_op jit(solution)/shard_map/ppermute | solution.py:278
  29.5 0.9 %collective-permute-start.11 = (bf16[16,16,128]{2,1,0:T(8,128)(2,1)S(1)}, bf16[16,16,128]{2,1,0:T(8,128)(2,1)S(1)}, u32[]{:S(2)}, u32[]{:S(2)}) collective-permute-start(bf16[16,16,128]{2,1,0:T(8,128)(2,1)S(1)} %get-tuple-element.40), channel_id=1, source_target_pairs={{0,1},{1,0},{2,3},{3,2},{4,5},{5,4},{6,7},{7,6},{8,9},{9,8},{10,11... | collective-permute-start | bytes 196616 | tf_op jit(solution)/shard_map/ppermute | solution.py:278
  30.4 0.7 %shard_map.96.refs_4_ = f32[256,128]{1,0:T(8,128)S(1)} custom-call(f32[64,16,128]{2,1,0:T(8,128)S(1)} %shard_map.87.panel, bf16[16,16,128]{2,1,0:T(8,128)(2,1)S(1)} %collective-permute-done.8.grad_ref.refs_0_, bf16[16,16,128]{2,1,0:T(8,128)(2,1)S(1)} %collective-permute-done.7.grad_ref.refs_1_, ...), custom_call_target="tpu_custom_call" | custom-call | tf_op jit(solution)/shard_map/pallas_call | solution.py:250
  31.1 1.5 %collective-permute-done.9.tile_ref = bf16[16,16,128]{2,1,0:T(8,128)(2,1)S(1)} collective-permute-done((bf16[16,16,128]{2,1,0:T(8,128)(2,1)S(1)}, bf16[16,16,128]{2,1,0:T(8,128)(2,1)S(1)}, u32[]{:S(2)}, u32[]{:S(2)}) %collective-permute-start.9) | collective-permute-done | bytes 65568 | tf_op jit(solution)/shard_map/ppermute | solution.py:278
  32.6 1.2 %collective-permute-done.10.tile_ref = bf16[16,16,128]{2,1,0:T(8,128)(2,1)S(1)} collective-permute-done((bf16[16,16,128]{2,1,0:T(8,128)(2,1)S(1)}, bf16[16,16,128]{2,1,0:T(8,128)(2,1)S(1)}, u32[]{:S(2)}, u32[]{:S(2)}) %collective-permute-start.10) | collective-permute-done | bytes 65568 | tf_op jit(solution)/shard_map/ppermute | solution.py:278
  33.8 0.9 %shard_map.97 = bf16[16,16,128]{2,1,0:T(8,128)(2,1)} custom-call(f32[16,16,128]{2,1,0:T(8,128)S(1)} %shard_map.95.base, bf16[16,16,128]{2,1,0:T(8,128)(2,1)S(1)} %collective-permute-done.11.refs_0_, f32[256,128]{1,0:T(8,128)S(1)} %get-tuple-element.41.refs_1_, f32[256,128]{1,0:T(8,128)S(1)} %get-tuple-element.42.refs_2_, ...), custom_call_target="tpu_custom_call" | custom-call | flops 16777216 | bytes 1343488 | tf_op jit(solution)/shard_map/pallas_call | solution.py:250
  (25 shorter events, 1.7 us)
Async XLA Ops:
  2.0 5.6 %collective-permute-start.2 = (bf16[16,16,128]{2,1,0:T(8,128)(2,1)S(1)}, bf16[16,16,128]{2,1,0:T(8,128)(2,1)S(1)}, u32[]{:S(2)}, u32[]{:S(2)}) collective-permute-start(bf16[16,16,128]{2,1,0:T(8,128)(2,1)S(1)} %shard_map.77.refs_0_), channel_id=1, source_target_pairs={{0,2},{1,3},{2,0},{3,1},{4,6},{5,7},{6,4},{7,5},{8,10},{9,11},{10,... | collective-permute-start | bytes 196616 | tf_op jit(solution)/shard_map/ppermute | solution.py:278
  5.0 4.1 %collective-permute-start = (bf16[16,16,128]{2,1,0:T(8,128)(2,1)S(1)}, bf16[16,16,128]{2,1,0:T(8,128)(2,1)S(1)}, u32[]{:S(2)}, u32[]{:S(2)}) collective-permute-start(bf16[16,16,128]{2,1,0:T(8,128)(2,1)S(1)} %shard_map.77.refs_0_), channel_id=1, source_target_pairs={{0,3},{1,2},{2,1},{3,0},{4,7},{5,6},{6,5},{7,4},{8,11},{9,10},{10,... | collective-permute-start | bytes 196616 | tf_op jit(solution)/shard_map/ppermute | solution.py:278
  5.0 4.1 %collective-permute-start.1 = (bf16[16,16,128]{2,1,0:T(8,128)(2,1)S(1)}, bf16[16,16,128]{2,1,0:T(8,128)(2,1)S(1)}, u32[]{:S(2)}, u32[]{:S(2)}) collective-permute-start(bf16[16,16,128]{2,1,0:T(8,128)(2,1)S(1)} %shard_map.77.refs_0_), channel_id=1, source_target_pairs={{0,1},{1,0},{2,3},{3,2},{4,5},{5,4},{6,7},{7,6},{8,9},{9,8},{10,11... | collective-permute-start | bytes 196616 | tf_op jit(solution)/shard_map/ppermute | solution.py:278
  9.6 6.6 %collective-permute-start.3 = (bf16[16,16,128]{2,1,0:T(8,128)(2,1)S(1)}, bf16[16,16,128]{2,1,0:T(8,128)(2,1)S(1)}, u32[]{:S(2)}, u32[]{:S(2)}) collective-permute-start(bf16[16,16,128]{2,1,0:T(8,128)(2,1)S(1)} %get-tuple-element.27), channel_id=1, source_target_pairs={{0,12},{4,8},{8,4},{12,0},{1,13},{5,9},{9,5},{13,1},{2,14},{6,10},... | collective-permute-start | bytes 196616 | tf_op jit(solution)/shard_map/ppermute | solution.py:278
  13.3 5.7 %collective-permute-start.4 = (bf16[16,16,128]{2,1,0:T(8,128)(2,1)S(1)}, bf16[16,16,128]{2,1,0:T(8,128)(2,1)S(1)}, u32[]{:S(2)}, u32[]{:S(2)}) collective-permute-start(bf16[16,16,128]{2,1,0:T(8,128)(2,1)S(1)} %get-tuple-element.28), channel_id=1, source_target_pairs={{0,8},{4,12},{8,0},{12,4},{1,9},{5,13},{9,1},{13,5},{2,10},{6,14},... | collective-permute-start | bytes 196616 | tf_op jit(solution)/shard_map/ppermute | solution.py:278
  13.4 5.7 %collective-permute-start.5 = (bf16[16,16,128]{2,1,0:T(8,128)(2,1)S(1)}, bf16[16,16,128]{2,1,0:T(8,128)(2,1)S(1)}, u32[]{:S(2)}, u32[]{:S(2)}) collective-permute-start(bf16[16,16,128]{2,1,0:T(8,128)(2,1)S(1)} %get-tuple-element.29), channel_id=1, source_target_pairs={{0,4},{4,0},{8,12},{12,8},{1,5},{5,1},{9,13},{13,9},{2,6},{6,2},{1... | collective-permute-start | bytes 196616 | tf_op jit(solution)/shard_map/ppermute | solution.py:278
  19.3 7.8 %collective-permute-start.8 = (bf16[16,16,128]{2,1,0:T(8,128)(2,1)S(1)}, bf16[16,16,128]{2,1,0:T(8,128)(2,1)S(1)}, u32[]{:S(2)}, u32[]{:S(2)}) collective-permute-start(bf16[16,16,128]{2,1,0:T(8,128)(2,1)S(1)} %get-tuple-element.35.refs_0_.grad_ref), channel_id=1, source_target_pairs={{0,8},{4,12},{8,0},{12,4},{1,9},{5,13},{9,1},{13,5},{2,10},{6,14},... | collective-permute-start | bytes 196616 | tf_op jit(solution)/shard_map/ppermute | solution.py:278
  20.9 6.5 %collective-permute-start.7 = (bf16[16,16,128]{2,1,0:T(8,128)(2,1)S(1)}, bf16[16,16,128]{2,1,0:T(8,128)(2,1)S(1)}, u32[]{:S(2)}, u32[]{:S(2)}) collective-permute-start(bf16[16,16,128]{2,1,0:T(8,128)(2,1)S(1)} %get-tuple-element.35.refs_0_.grad_ref), channel_id=1, source_target_pairs={{0,12},{4,8},{8,4},{12,0},{1,13},{5,9},{9,5},{13,1},{2,14},{6,10},... | collective-permute-start | bytes 196616 | tf_op jit(solution)/shard_map/ppermute | solution.py:278
  22.8 5.0 %collective-permute-start.6 = (bf16[16,16,128]{2,1,0:T(8,128)(2,1)S(1)}, bf16[16,16,128]{2,1,0:T(8,128)(2,1)S(1)}, u32[]{:S(2)}, u32[]{:S(2)}) collective-permute-start(bf16[16,16,128]{2,1,0:T(8,128)(2,1)S(1)} %get-tuple-element.35.refs_0_.grad_ref), channel_id=1, source_target_pairs={{0,4},{4,0},{8,12},{12,8},{1,5},{5,1},{9,13},{13,9},{2,6},{6,2},{1... | collective-permute-start | bytes 196616 | tf_op jit(solution)/shard_map/ppermute | solution.py:278
  23.0 0.9 %copy-start = (bf16[128,640]{1,0:T(8,128)(2,1)S(1)}, bf16[128,640]{1,0:T(8,128)(2,1)}, u32[]{:S(2)}) copy-start(bf16[128,640]{1,0:T(8,128)(2,1)} %refs_5_.3) | copy-start | bytes 491524
  23.0 0.9 %copy-start.1 = (bf16[128,128]{1,0:T(8,128)(2,1)S(1)}, bf16[128,128]{1,0:T(8,128)(2,1)}, u32[]{:S(2)}) copy-start(bf16[128,128]{1,0:T(8,128)(2,1)} %out_weight_ref.1) | copy-start | bytes 98308
  28.1 4.4 %collective-permute-start.9 = (bf16[16,16,128]{2,1,0:T(8,128)(2,1)S(1)}, bf16[16,16,128]{2,1,0:T(8,128)(2,1)S(1)}, u32[]{:S(2)}, u32[]{:S(2)}) collective-permute-start(bf16[16,16,128]{2,1,0:T(8,128)(2,1)S(1)} %get-tuple-element.38), channel_id=1, source_target_pairs={{0,2},{1,3},{2,0},{3,1},{4,6},{5,7},{6,4},{7,5},{8,10},{9,11},{10,... | collective-permute-start | bytes 196616 | tf_op jit(solution)/shard_map/ppermute | solution.py:278
  29.5 4.3 %collective-permute-start.10 = (bf16[16,16,128]{2,1,0:T(8,128)(2,1)S(1)}, bf16[16,16,128]{2,1,0:T(8,128)(2,1)S(1)}, u32[]{:S(2)}, u32[]{:S(2)}) collective-permute-start(bf16[16,16,128]{2,1,0:T(8,128)(2,1)S(1)} %get-tuple-element.39), channel_id=1, source_target_pairs={{0,3},{1,2},{2,1},{3,0},{4,7},{5,6},{6,5},{7,4},{8,11},{9,10},{10,... | collective-permute-start | bytes 196616 | tf_op jit(solution)/shard_map/ppermute | solution.py:278
  29.5 4.4 %collective-permute-start.11 = (bf16[16,16,128]{2,1,0:T(8,128)(2,1)S(1)}, bf16[16,16,128]{2,1,0:T(8,128)(2,1)S(1)}, u32[]{:S(2)}, u32[]{:S(2)}) collective-permute-start(bf16[16,16,128]{2,1,0:T(8,128)(2,1)S(1)} %get-tuple-element.40), channel_id=1, source_target_pairs={{0,1},{1,0},{2,3},{3,2},{4,5},{5,4},{6,7},{7,6},{8,9},{9,8},{10,11... | collective-permute-start | bytes 196616 | tf_op jit(solution)/shard_map/ppermute | solution.py:278

commit v18 on v16

--- a/solution.py
+++ b/solution.py
@@ -270,7 +270,7 @@
     work = 2 * size * pairs * channels
     wait = 2**31
     steps = [step for bit in range(n.bit_length() - 2, -1, -1) for step in range(2**bit, 2 ** (bit + 1))]
-    row_steps = list(range(n - 1, 0, -1))
+    row_steps = steps
     gather_steps = [n - 1] + list(range(1, n - 1))
 
 

time: 34.9 us -> 34.8 us (level)
  no operation moved by 1% of the time
where the time goes in v18:
time: 34.8 us; the launch traced here: 34.6 us
  starting transfers between devices  14.1 us (41%)
  waiting for transfers between devices  10.5 us (30%)
  Pallas kernels  7.81 us (22%)
  between operations  1.43 us (4%)
  local copies, waits for them, and re-layouts  0.71 us (2%)
    ppermute x12, starting transfers between devices, swap(): return lax.ppermute(values, axis, [(a, a ^ step) for a in range(n)])  14.1 us
    ppermute x12, waiting for transfers between devices, swap(): return lax.ppermute(values, axis, [(a, a ^ step) for a in range(n)])  10.5 us
    pallas_call x21, Pallas kernels, call(): pl.pallas_call(kernel, out_shape=tuple(outs), in_specs=specs, out_specs=(...  7.81 us
    unnamed x4, local copies, waits for them, and re-layouts  0.71 us
  transfers between devices with their start and end apart: 12, of which 8 were waited for; matrix products, arithmetic and copies ran while one was open for 0% of the time, Pallas kernels for 13%

profile of v18, /device:TPU:0, one launch (start us, length us, event | category | flops | bytes accessed | tf_op | source)
XLA Modules:
  0.0 34.6 jit_solution(3993649326222990509)
XLA Ops:
  0.6 1.3 %shard_map.77.refs_0_ = bf16[16,16,128]{2,1,0:T(8,128)(2,1)S(1)} custom-call(bf16[16,16,128]{2,1,0:T(8,128)(2,1)} %acts_in.3, s32[16,16]{1,0:T(8,128)} %mask_in.3, bf16[128,640]{1,0:T(8,128)(2,1)} %refs_5_.3), custom_call_target="tpu_custom_call" | custom-call | flops 16777216 | bytes 295936 | tf_op jit(solution)/shard_map/pallas_call | solution.py:250
  2.0 3.0 %collective-permute-start.2 = (bf16[16,16,128]{2,1,0:T(8,128)(2,1)S(1)}, bf16[16,16,128]{2,1,0:T(8,128)(2,1)S(1)}, u32[]{:S(2)}, u32[]{:S(2)}) collective-permute-start(bf16[16,16,128]{2,1,0:T(8,128)(2,1)S(1)} %shard_map.77.refs_0_), channel_id=1, source_target_pairs={{0,2},{1,3},{2,0},{3,1},{4,6},{5,7},{6,4},{7,5},{8,10},{9,11},{10,... | collective-permute-start | bytes 196616 | tf_op jit(solution)/shard_map/ppermute | solution.py:278
  5.8 1.5 %shard_map.78 = (f32[16,16,128]{2,1,0:T(8,128)S(1)}, f32[256,128]{1,0:T(8,128)S(1)}, f32[256,128]{1,0:T(8,128)S(1)}, f32[4,256,128]{2,1,0:T(8,128)S(1)}, f32[256...) custom-call(bf16[16,16,128]{2,1,0:T(8,128)(2,1)} %acts_in.3, s32[16,16]{1,0:T(8,128)} %mask_in.3, ...), custom_call_target="tpu_custom_call" | custom-call | flops 50331648 | bytes 1639428 | tf_op jit(solution)/shard_map/pallas_call | solution.py:250
  7.8 1.4 %collective-permute-done.refs_0_.refs_2_ = bf16[16,16,128]{2,1,0:T(8,128)(2,1)S(1)} collective-permute-done((bf16[16,16,128]{2,1,0:T(8,128)(2,1)S(1)}, bf16[16,16,128]{2,1,0:T(8,128)(2,1)S(1)}, u32[]{:S(2)}, u32[]{:S(2)}) %collective-permute-start) | collective-permute-done | bytes 65568 | tf_op jit(solution)/shard_map/ppermute | solution.py:278
  9.1 0.4 %shard_map.80 = (f32[16,16,128]{2,1,0:T(8,128)S(1)}, f32[16,16,128]{2,1,0:T(8,128)S(1)}) custom-call(s32[1]{0:T(128)S(6)} %copy.8.crop_ref, bf16[16,16,128]{2,1,0:T(8,128)(2,1)S(1)} %collective-permute-done.refs_0_.refs_2_, bf16[16,16,128]{2,1,0:T(8,128)(2,1)S(1)} %collective-permute-done.1.refs_1_.refs_3_, ...), custom_call_target="tpu_custom_call" | custom-call | flops 1048576 | bytes 524292 | tf_op jit(solution)/shard_map/pallas_call | solution.py:250
  9.6 2.7 %collective-permute-start.3 = (bf16[16,16,128]{2,1,0:T(8,128)(2,1)S(1)}, bf16[16,16,128]{2,1,0:T(8,128)(2,1)S(1)}, u32[]{:S(2)}, u32[]{:S(2)}) collective-permute-start(bf16[16,16,128]{2,1,0:T(8,128)(2,1)S(1)} %get-tuple-element.27), channel_id=1, source_target_pairs={{0,8},{4,12},{8,0},{12,4},{1,9},{5,13},{9,1},{13,5},{2,10},{6,14},... | collective-permute-start | bytes 196616 | tf_op jit(solution)/shard_map/ppermute | solution.py:278
  12.3 1.3 %collective-permute-start.4 = (bf16[16,16,128]{2,1,0:T(8,128)(2,1)S(1)}, bf16[16,16,128]{2,1,0:T(8,128)(2,1)S(1)}, u32[]{:S(2)}, u32[]{:S(2)}) collective-permute-start(bf16[16,16,128]{2,1,0:T(8,128)(2,1)S(1)} %get-tuple-element.28), channel_id=1, source_target_pairs={{0,12},{4,8},{8,4},{12,0},{1,13},{5,9},{9,5},{13,1},{2,14},{6,10},... | collective-permute-start | bytes 196616 | tf_op jit(solution)/shard_map/ppermute | solution.py:278
  13.7 0.2 collective-permute-start.5
  13.9 3.3 %collective-permute-done.3.tile_ref = bf16[16,16,128]{2,1,0:T(8,128)(2,1)S(1)} collective-permute-done((bf16[16,16,128]{2,1,0:T(8,128)(2,1)S(1)}, bf16[16,16,128]{2,1,0:T(8,128)(2,1)S(1)}, u32[]{:S(2)}, u32[]{:S(2)}) %collective-permute-start.3) | collective-permute-done | bytes 65568 | tf_op jit(solution)/shard_map/ppermute | solution.py:278
  17.3 1.4 %collective-permute-done.4.tile_ref = bf16[16,16,128]{2,1,0:T(8,128)(2,1)S(1)} collective-permute-done((bf16[16,16,128]{2,1,0:T(8,128)(2,1)S(1)}, bf16[16,16,128]{2,1,0:T(8,128)(2,1)S(1)}, u32[]{:S(2)}, u32[]{:S(2)}) %collective-permute-start.4) | collective-permute-done | bytes 65568 | tf_op jit(solution)/shard_map/ppermute | solution.py:278
  18.8 0.3 shard_map.85
  19.1 3.0 %collective-permute-start.7 = (bf16[16,16,128]{2,1,0:T(8,128)(2,1)S(1)}, bf16[16,16,128]{2,1,0:T(8,128)(2,1)S(1)}, u32[]{:S(2)}, u32[]{:S(2)}) collective-permute-start(bf16[16,16,128]{2,1,0:T(8,128)(2,1)S(1)} %get-tuple-element.35.refs_0_.grad_ref), channel_id=1, source_target_pairs={{0,12},{4,8},{8,4},{12,0},{1,13},{5,9},{9,5},{13,1},{2,14},{6,10},... | collective-permute-start | bytes 196616 | tf_op jit(solution)/shard_map/ppermute | solution.py:278
  22.3 1.2 %collective-permute-start.8 = (bf16[16,16,128]{2,1,0:T(8,128)(2,1)S(1)}, bf16[16,16,128]{2,1,0:T(8,128)(2,1)S(1)}, u32[]{:S(2)}, u32[]{:S(2)}) collective-permute-start(bf16[16,16,128]{2,1,0:T(8,128)(2,1)S(1)} %get-tuple-element.35.refs_0_.grad_ref), channel_id=1, source_target_pairs={{0,8},{4,12},{8,0},{12,4},{1,9},{5,13},{9,1},{13,5},{2,10},{6,14},... | collective-permute-start | bytes 196616 | tf_op jit(solution)/shard_map/ppermute | solution.py:278
  23.9 0.7 %copy-done = bf16[128,640]{1,0:T(8,128)(2,1)S(1)} copy-done((bf16[128,640]{1,0:T(8,128)(2,1)S(1)}, bf16[128,640]{1,0:T(8,128)(2,1)}, u32[]{:S(2)}) %copy-start) | copy-done | bytes 163864
  24.6 0.8 %shard_map.86 = (bf16[16,16,128]{2,1,0:T(8,128)(2,1)}, f32[256,128]{1,0:T(8,128)S(1)}) custom-call(f32[256,128]{1,0:T(8,128)S(1)} %get-tuple-element.31.tri_normed_ref, f32[256,128]{1,0:T(8,128)S(1)} %get-tuple-element.32.open_ref, f32[256,128]{1,0:T(8,128)S(1)} %get-tuple-element.33.gate_factor_ref, bf16[128,640]{1,0:T(8,128)(2,1)S(1)} %copy-done, ...), custom_call_target="tpu_custom_call" | custom-call | flops 16777216 | bytes 786432 | tf_op jit(solution)/shard_map/pallas_call | solution.py:250
  25.6 0.2 shard_map.90.refs_0_.refs_3_
  25.8 0.8 %collective-permute-done.6.grad_ref.refs_1_ = bf16[16,16,128]{2,1,0:T(8,128)(2,1)S(1)} collective-permute-done((bf16[16,16,128]{2,1,0:T(8,128)(2,1)S(1)}, bf16[16,16,128]{2,1,0:T(8,128)(2,1)S(1)}, u32[]{:S(2)}, u32[]{:S(2)}) %collective-permute-start.6) | collective-permute-done | bytes 65568 | tf_op jit(solution)/shard_map/ppermute | solution.py:278
  26.8 0.7 %collective-permute-done.8.grad_ref.refs_2_ = bf16[16,16,128]{2,1,0:T(8,128)(2,1)S(1)} collective-permute-done((bf16[16,16,128]{2,1,0:T(8,128)(2,1)S(1)}, bf16[16,16,128]{2,1,0:T(8,128)(2,1)S(1)}, u32[]{:S(2)}, u32[]{:S(2)}) %collective-permute-start.8) | collective-permute-done | bytes 65568 | tf_op jit(solution)/shard_map/ppermute | solution.py:278
  27.9 1.9 %collective-permute-start.9 = (bf16[16,16,128]{2,1,0:T(8,128)(2,1)S(1)}, bf16[16,16,128]{2,1,0:T(8,128)(2,1)S(1)}, u32[]{:S(2)}, u32[]{:S(2)}) collective-permute-start(bf16[16,16,128]{2,1,0:T(8,128)(2,1)S(1)} %get-tuple-element.38), channel_id=1, source_target_pairs={{0,2},{1,3},{2,0},{3,1},{4,6},{5,7},{6,4},{7,5},{8,10},{9,11},{10,... | collective-permute-start | bytes 196616 | tf_op jit(solution)/shard_map/ppermute | solution.py:278
  29.8 0.3 collective-permute-start.11
  30.1 0.7 %shard_map.96.refs_4_ = f32[256,128]{1,0:T(8,128)S(1)} custom-call(f32[64,16,128]{2,1,0:T(8,128)S(1)} %shard_map.87.panel, bf16[16,16,128]{2,1,0:T(8,128)(2,1)S(1)} %collective-permute-done.7.grad_ref.refs_0_, bf16[16,16,128]{2,1,0:T(8,128)(2,1)S(1)} %collective-permute-done.6.grad_ref.refs_1_, ...), custom_call_target="tpu_custom_call" | custom-call | tf_op jit(solution)/shard_map/pallas_call | solution.py:250
  30.8 1.4 %collective-permute-done.9.tile_ref = bf16[16,16,128]{2,1,0:T(8,128)(2,1)S(1)} collective-permute-done((bf16[16,16,128]{2,1,0:T(8,128)(2,1)S(1)}, bf16[16,16,128]{2,1,0:T(8,128)(2,1)S(1)}, u32[]{:S(2)}, u32[]{:S(2)}) %collective-permute-start.9) | collective-permute-done | bytes 65568 | tf_op jit(solution)/shard_map/ppermute | solution.py:278
  32.2 1.4 %collective-permute-done.10.tile_ref = bf16[16,16,128]{2,1,0:T(8,128)(2,1)S(1)} collective-permute-done((bf16[16,16,128]{2,1,0:T(8,128)(2,1)S(1)}, bf16[16,16,128]{2,1,0:T(8,128)(2,1)S(1)}, u32[]{:S(2)}, u32[]{:S(2)}) %collective-permute-start.10) | collective-permute-done | bytes 65568 | tf_op jit(solution)/shard_map/ppermute | solution.py:278
  33.6 0.9 %shard_map.97 = bf16[16,16,128]{2,1,0:T(8,128)(2,1)} custom-call(f32[16,16,128]{2,1,0:T(8,128)S(1)} %shard_map.95.base, bf16[16,16,128]{2,1,0:T(8,128)(2,1)S(1)} %collective-permute-done.11.refs_0_, f32[256,128]{1,0:T(8,128)S(1)} %get-tuple-element.41.refs_1_, f32[256,128]{1,0:T(8,128)S(1)} %get-tuple-element.42.refs_2_, ...), custom_call_target="tpu_custom_call" | custom-call | flops 16777216 | bytes 1343488 | tf_op jit(solution)/shard_map/pallas_call | solution.py:250
  (25 shorter events, 2.2 us)
Async XLA Ops:
  2.0 5.6 %collective-permute-start.2 = (bf16[16,16,128]{2,1,0:T(8,128)(2,1)S(1)}, bf16[16,16,128]{2,1,0:T(8,128)(2,1)S(1)}, u32[]{:S(2)}, u32[]{:S(2)}) collective-permute-start(bf16[16,16,128]{2,1,0:T(8,128)(2,1)S(1)} %shard_map.77.refs_0_), channel_id=1, source_target_pairs={{0,2},{1,3},{2,0},{3,1},{4,6},{5,7},{6,4},{7,5},{8,10},{9,11},{10,... | collective-permute-start | bytes 196616 | tf_op jit(solution)/shard_map/ppermute | solution.py:278
  5.0 4.1 %collective-permute-start = (bf16[16,16,128]{2,1,0:T(8,128)(2,1)S(1)}, bf16[16,16,128]{2,1,0:T(8,128)(2,1)S(1)}, u32[]{:S(2)}, u32[]{:S(2)}) collective-permute-start(bf16[16,16,128]{2,1,0:T(8,128)(2,1)S(1)} %shard_map.77.refs_0_), channel_id=1, source_target_pairs={{0,3},{1,2},{2,1},{3,0},{4,7},{5,6},{6,5},{7,4},{8,11},{9,10},{10,... | collective-permute-start | bytes 196616 | tf_op jit(solution)/shard_map/ppermute | solution.py:278
  5.0 4.1 %collective-permute-start.1 = (bf16[16,16,128]{2,1,0:T(8,128)(2,1)S(1)}, bf16[16,16,128]{2,1,0:T(8,128)(2,1)S(1)}, u32[]{:S(2)}, u32[]{:S(2)}) collective-permute-start(bf16[16,16,128]{2,1,0:T(8,128)(2,1)S(1)} %shard_map.77.refs_0_), channel_id=1, source_target_pairs={{0,1},{1,0},{2,3},{3,2},{4,5},{5,4},{6,7},{7,6},{8,9},{9,8},{10,11... | collective-permute-start | bytes 196616 | tf_op jit(solution)/shard_map/ppermute | solution.py:278
  9.6 7.6 %collective-permute-start.3 = (bf16[16,16,128]{2,1,0:T(8,128)(2,1)S(1)}, bf16[16,16,128]{2,1,0:T(8,128)(2,1)S(1)}, u32[]{:S(2)}, u32[]{:S(2)}) collective-permute-start(bf16[16,16,128]{2,1,0:T(8,128)(2,1)S(1)} %get-tuple-element.27), channel_id=1, source_target_pairs={{0,8},{4,12},{8,0},{12,4},{1,9},{5,13},{9,1},{13,5},{2,10},{6,14},... | collective-permute-start | bytes 196616 | tf_op jit(solution)/shard_map/ppermute | solution.py:278
  12.3 6.3 %collective-permute-start.4 = (bf16[16,16,128]{2,1,0:T(8,128)(2,1)S(1)}, bf16[16,16,128]{2,1,0:T(8,128)(2,1)S(1)}, u32[]{:S(2)}, u32[]{:S(2)}) collective-permute-start(bf16[16,16,128]{2,1,0:T(8,128)(2,1)S(1)} %get-tuple-element.28), channel_id=1, source_target_pairs={{0,12},{4,8},{8,4},{12,0},{1,13},{5,9},{9,5},{13,1},{2,14},{6,10},... | collective-permute-start | bytes 196616 | tf_op jit(solution)/shard_map/ppermute | solution.py:278
  13.7 5.1 %collective-permute-start.5 = (bf16[16,16,128]{2,1,0:T(8,128)(2,1)S(1)}, bf16[16,16,128]{2,1,0:T(8,128)(2,1)S(1)}, u32[]{:S(2)}, u32[]{:S(2)}) collective-permute-start(bf16[16,16,128]{2,1,0:T(8,128)(2,1)S(1)} %get-tuple-element.29), channel_id=1, source_target_pairs={{0,4},{4,0},{8,12},{12,8},{1,5},{5,1},{9,13},{13,9},{2,6},{6,2},{1... | collective-permute-start | bytes 196616 | tf_op jit(solution)/shard_map/ppermute | solution.py:278
  19.1 6.5 %collective-permute-start.7 = (bf16[16,16,128]{2,1,0:T(8,128)(2,1)S(1)}, bf16[16,16,128]{2,1,0:T(8,128)(2,1)S(1)}, u32[]{:S(2)}, u32[]{:S(2)}) collective-permute-start(bf16[16,16,128]{2,1,0:T(8,128)(2,1)S(1)} %get-tuple-element.35.refs_0_.grad_ref), channel_id=1, source_target_pairs={{0,12},{4,8},{8,4},{12,0},{1,13},{5,9},{9,5},{13,1},{2,14},{6,10},... | collective-permute-start | bytes 196616 | tf_op jit(solution)/shard_map/ppermute | solution.py:278
  22.1 4.5 %collective-permute-start.6 = (bf16[16,16,128]{2,1,0:T(8,128)(2,1)S(1)}, bf16[16,16,128]{2,1,0:T(8,128)(2,1)S(1)}, u32[]{:S(2)}, u32[]{:S(2)}) collective-permute-start(bf16[16,16,128]{2,1,0:T(8,128)(2,1)S(1)} %get-tuple-element.35.refs_0_.grad_ref), channel_id=1, source_target_pairs={{0,4},{4,0},{8,12},{12,8},{1,5},{5,1},{9,13},{13,9},{2,6},{6,2},{1... | collective-permute-start | bytes 196616 | tf_op jit(solution)/shard_map/ppermute | solution.py:278
  22.3 5.2 %collective-permute-start.8 = (bf16[16,16,128]{2,1,0:T(8,128)(2,1)S(1)}, bf16[16,16,128]{2,1,0:T(8,128)(2,1)S(1)}, u32[]{:S(2)}, u32[]{:S(2)}) collective-permute-start(bf16[16,16,128]{2,1,0:T(8,128)(2,1)S(1)} %get-tuple-element.35.refs_0_.grad_ref), channel_id=1, source_target_pairs={{0,8},{4,12},{8,0},{12,4},{1,9},{5,13},{9,1},{13,5},{2,10},{6,14},... | collective-permute-start | bytes 196616 | tf_op jit(solution)/shard_map/ppermute | solution.py:278
  23.6 0.9 %copy-start = (bf16[128,640]{1,0:T(8,128)(2,1)S(1)}, bf16[128,640]{1,0:T(8,128)(2,1)}, u32[]{:S(2)}) copy-start(bf16[128,640]{1,0:T(8,128)(2,1)} %refs_5_.3) | copy-start | bytes 491524
  23.6 0.9 %copy-start.1 = (bf16[128,128]{1,0:T(8,128)(2,1)S(1)}, bf16[128,128]{1,0:T(8,128)(2,1)}, u32[]{:S(2)}) copy-start(bf16[128,128]{1,0:T(8,128)(2,1)} %out_weight_ref.1) | copy-start | bytes 98308
  27.9 4.3 %collective-permute-start.9 = (bf16[16,16,128]{2,1,0:T(8,128)(2,1)S(1)}, bf16[16,16,128]{2,1,0:T(8,128)(2,1)S(1)}, u32[]{:S(2)}, u32[]{:S(2)}) collective-permute-start(bf16[16,16,128]{2,1,0:T(8,128)(2,1)S(1)} %get-tuple-element.38), channel_id=1, source_target_pairs={{0,2},{1,3},{2,0},{3,1},{4,6},{5,7},{6,4},{7,5},{8,10},{9,11},{10,... | collective-permute-start | bytes 196616 | tf_op jit(solution)/shard_map/ppermute | solution.py:278
  29.8 3.8 %collective-permute-start.10 = (bf16[16,16,128]{2,1,0:T(8,128)(2,1)S(1)}, bf16[16,16,128]{2,1,0:T(8,128)(2,1)S(1)}, u32[]{:S(2)}, u32[]{:S(2)}) collective-permute-start(bf16[16,16,128]{2,1,0:T(8,128)(2,1)S(1)} %get-tuple-element.39), channel_id=1, source_target_pairs={{0,3},{1,2},{2,1},{3,0},{4,7},{5,6},{6,5},{7,4},{8,11},{9,10},{10,... | collective-permute-start | bytes 196616 | tf_op jit(solution)/shard_map/ppermute | solution.py:278
  29.8 3.8 %collective-permute-start.11 = (bf16[16,16,128]{2,1,0:T(8,128)(2,1)S(1)}, bf16[16,16,128]{2,1,0:T(8,128)(2,1)S(1)}, u32[]{:S(2)}, u32[]{:S(2)}) collective-permute-start(bf16[16,16,128]{2,1,0:T(8,128)(2,1)S(1)} %get-tuple-element.40), channel_id=1, source_target_pairs={{0,1},{1,0},{2,3},{3,2},{4,5},{5,4},{6,7},{7,6},{8,9},{9,8},{10,11... | collective-permute-start | bytes 196616 | tf_op jit(solution)/shard_map/ppermute | solution.py:278

commit v19 on v18

--- a/solution.py
+++ b/solution.py
@@ -49,12 +49,11 @@
 
 def spread(mask, channels):
     size = mask.shape[0]
-    pair = lax.broadcasted_iota(jnp.int32, (size * size, size), 0)
-    lane = lax.broadcasted_iota(jnp.int32, (size * size, size), 1)
-    pick_row = jnp.where(pair // size == lane, 1.0, 0.0).astype(bf16)
-    pick_col = jnp.where(pair % size == lane, 1.0, 0.0)
-    picked = (dot(pick_row, mask.astype(bf16)) * pick_col).astype(bf16)
-    return dot(picked, jnp.ones((size, channels), bf16))
+    shape = (size, size, size)
+    diagonal = lax.broadcasted_iota(jnp.int32, shape, 1) == lax.broadcasted_iota(jnp.int32, shape, 2)
+    picked = jnp.where(diagonal, jnp.broadcast_to(mask[:, None, :], shape), 0.0)
+    rows = jnp.sum(picked, axis=-1, keepdims=True)
+    return jnp.broadcast_to(rows, (size, size, channels)).reshape(size * size, channels)
 
 
 def start_copies(sems, *pairs):
@@ -174,6 +173,15 @@
                 out[...] = tile[...].astype(out.dtype)
 
 
+def last_partial_kernel(steps, early, row_steps, crop_ref, *refs):
+    count, known = len(steps), len(early)
+    left, parts = refs[-2:]
+    partial_kernel(steps, crop_ref, *refs[: count + 1], *(parts.at[at] for at in range(count)), left)
+    tiles = dict(zip(early, refs[count + 1 : count + 1 + known]))
+    tiles.update((step, parts.at[at]) for at, step in enumerate(steps))
+    pick_kernel(row_steps, *(tiles[step] for step in range(count + known)), *refs[count + 1 + known : -2])
+
+
 def triangle_kernel(base, tile_ref, upstream_ref, tri_normed_ref, grad_ref):
     size = grad_ref.shape[0]
     for i in range(size):
@@ -188,6 +196,15 @@
     size, _, channels = out.shape
     grad[...] = grad_ref[...].astype(f32).reshape(size * size, channels)
     weighted_sums(right, 0, [grad[pl.ds(j, size, stride=size), :] for j in range(size)], out)
+
+
+def last_terms_kernel(early, last, steps, grad_ref, right, *refs):
+    known = len(early)
+    term, grad = refs[-2:]
+    left_terms_kernel(grad_ref, right, term, grad)
+    tiles = dict(zip(early, refs[:known]))
+    tiles[last] = term
+    pick_kernel(steps, *(tiles[step] for step in range(known + 1)), *refs[known:-2])
 
 
 def right_grad_kernel(steps, panel, *refs):
@@ -305,18 +322,18 @@
             pltpu.SemaphoreType.DMA((5,)),
         ],
     )
-    parts = []
     order = [0] + steps
-    for group in [[at] for at in range(n - 2)] + [[n - 2, n - 1]]:
-        parts += call(
-            functools.partial(partial_kernel, [order[at] for at in group]), (wide,) * len(group),
-            crop_length, *(lefts[at] for at in group), right, smem=(0,), flops=work,
-            scratch=[pltpu.VMEM(wide.shape, f32)],
-        )
-    parts = [part for _, part in sorted(zip(order, parts), key=lambda each: each[0])]
+    parts = [
+        call(
+            functools.partial(partial_kernel, [order[at]]), (wide,), crop_length, lefts[at], right, smem=(0,),
+            flops=work, scratch=[pltpu.VMEM(wide.shape, f32)],
+        )[0]
+        for at in range(n - 2)
+    ]
     total, *parts = call(
-        functools.partial(pick_kernel, [0] + row_steps), (wide,) + (tile,) * (n - 1), *parts,
-        flops=pairs * channels,
+        functools.partial(last_partial_kernel, order[-2:], order[:-2], [0] + row_steps),
+        (wide,) + (tile,) * (n - 1), crop_length, *lefts[-2:], right, *parts, smem=(0,), flops=work,
+        scratch=[pltpu.VMEM(wide.shape, f32), pltpu.VMEM((2,) + wide.shape, f32)],
     )
     (left_panel,) = call(
         functools.partial(left_panel_kernel, [0] + steps), (panel,), crop_length, *lefts, smem=(0,)
@@ -334,15 +351,17 @@
         flops=4 * pairs * channels * channels,
     )
     (right_grad,) = call(functools.partial(right_grad_kernel, [0]), (wide,), left_panel, tri_grad)
-    terms, before = [None] * n, (partial, right_grad)
-    for step, grad in zip([0] + gather_steps, grads):
+    terms, before = [], (partial, right_grad)
+    for grad in grads[:-1]:
         before = call(
             left_terms_kernel, (wide,), grad, right, *before,
             scratch=[pltpu.VMEM((pairs, channels), f32)], flops=work,
         )
-        terms[step] = before[0]
+        terms += before
     total, *terms = call(
-        functools.partial(pick_kernel, [0] + steps), (wide,) + (tile,) * (n - 1), *terms, flops=pairs * channels,
+        functools.partial(last_terms_kernel, [0] + gather_steps[:-1], gather_steps[-1], [0] + steps),
+        (wide,) + (tile,) * (n - 1), grads[-1], right, *terms, flops=work,
+        scratch=[pltpu.VMEM(wide.shape, f32), pltpu.VMEM((pairs, channels), f32)],
     )
     for step, term in zip(steps, terms):
         term = swap(term, "col", step)

time: 34.8 us -> 34.6 us (level)
    pallas_call x21 -> x19, Pallas kernels: 7.81 us -> 7.69 us  [call(): pl.pallas_call(kernel, out_shape=tuple(outs), in_specs=specs, out_specs=(...]
where the time goes in v19:
time: 34.6 us; the launch traced here: 34.4 us
  starting transfers between devices  14.1 us (41%)
  waiting for transfers between devices  10.5 us (30%)
  Pallas kernels  7.69 us (22%)
  between operations  1.42 us (4%)
  local copies, waits for them, and re-layouts  0.71 us (2%)
    ppermute x12, starting transfers between devices, swap(): return lax.ppermute(values, axis, [(a, a ^ step) for a in range(n)])  14.1 us
    ppermute x12, waiting for transfers between devices, swap(): return lax.ppermute(values, axis, [(a, a ^ step) for a in range(n)])  10.5 us
    pallas_call x19, Pallas kernels, call(): pl.pallas_call(kernel, out_shape=tuple(outs), in_specs=specs, out_specs=(...  7.69 us
    unnamed x4, local copies, waits for them, and re-layouts  0.71 us
  transfers between devices with their start and end apart: 12, of which 8 were waited for; matrix products, arithmetic and copies ran while one was open for 0% of the time, Pallas kernels for 13%

profile of v19, /device:TPU:0, one launch (start us, length us, event | category | flops | bytes accessed | tf_op | source)
XLA Modules:
  0.0 34.4 jit_solution(9309656462965743652)
XLA Ops:
  0.6 1.3 %shard_map.77.refs_0_ = bf16[16,16,128]{2,1,0:T(8,128)(2,1)S(1)} custom-call(bf16[16,16,128]{2,1,0:T(8,128)(2,1)} %acts_in.3, s32[16,16]{1,0:T(8,128)} %mask_in.3, bf16[128,640]{1,0:T(8,128)(2,1)} %refs_5_.3), custom_call_target="tpu_custom_call" | custom-call | flops 16777216 | bytes 295936 | tf_op jit(solution)/shard_map/pallas_call | solution.py:267
  1.9 3.0 %collective-permute-start.2 = (bf16[16,16,128]{2,1,0:T(8,128)(2,1)S(1)}, bf16[16,16,128]{2,1,0:T(8,128)(2,1)S(1)}, u32[]{:S(2)}, u32[]{:S(2)}) collective-permute-start(bf16[16,16,128]{2,1,0:T(8,128)(2,1)S(1)} %shard_map.77.refs_0_), channel_id=1, source_target_pairs={{0,2},{1,3},{2,0},{3,1},{4,6},{5,7},{6,4},{7,5},{8,10},{9,11},{10,... | collective-permute-start | bytes 196616 | tf_op jit(solution)/shard_map/ppermute | solution.py:295
  5.8 1.5 %shard_map.78 = (f32[16,16,128]{2,1,0:T(8,128)S(1)}, f32[256,128]{1,0:T(8,128)S(1)}, f32[256,128]{1,0:T(8,128)S(1)}, f32[4,256,128]{2,1,0:T(8,128)S(1)}, f32[256...) custom-call(bf16[16,16,128]{2,1,0:T(8,128)(2,1)} %acts_in.3, s32[16,16]{1,0:T(8,128)} %mask_in.3, ...), custom_call_target="tpu_custom_call" | custom-call | flops 50331648 | bytes 1639428 | tf_op jit(solution)/shard_map/pallas_call | solution.py:267
  7.7 1.4 %collective-permute-done.refs_0_.refs_2_ = bf16[16,16,128]{2,1,0:T(8,128)(2,1)S(1)} collective-permute-done((bf16[16,16,128]{2,1,0:T(8,128)(2,1)S(1)}, bf16[16,16,128]{2,1,0:T(8,128)(2,1)S(1)}, u32[]{:S(2)}, u32[]{:S(2)}) %collective-permute-start) | collective-permute-done | bytes 65568 | tf_op jit(solution)/shard_map/ppermute | solution.py:295
  9.0 0.5 %shard_map.81 = (f32[16,16,128]{2,1,0:T(8,128)S(1)}, bf16[16,16,128]{2,1,0:T(8,128)(2,1)S(1)}, bf16[16,16,128]{2,1,0:T(8,128)(2,1)S(1)}, bf16[16,16,128]{2,1,0:T(8,128)(2,1)S(1)}) custom-call(s32[1]{0:T(128)S(6)} %copy.8.crop_ref, bf16[16,16,128]{2,1,0:T(8,128)(2,1)S(1)} %collective-permute-done.refs_0_.refs_2_, ...), custom_call_target="tpu_custom_call" | custom-call | flops 1048576 | bytes 851972 | tf_op jit(solution)/shard_map/pallas_call | solution.py:267
  9.5 2.7 %collective-permute-start.3 = (bf16[16,16,128]{2,1,0:T(8,128)(2,1)S(1)}, bf16[16,16,128]{2,1,0:T(8,128)(2,1)S(1)}, u32[]{:S(2)}, u32[]{:S(2)}) collective-permute-start(bf16[16,16,128]{2,1,0:T(8,128)(2,1)S(1)} %get-tuple-element.23), channel_id=1, source_target_pairs={{0,8},{4,12},{8,0},{12,4},{1,9},{5,13},{9,1},{13,5},{2,10},{6,14},... | collective-permute-start | bytes 196616 | tf_op jit(solution)/shard_map/ppermute | solution.py:295
  12.2 1.3 %collective-permute-start.4 = (bf16[16,16,128]{2,1,0:T(8,128)(2,1)S(1)}, bf16[16,16,128]{2,1,0:T(8,128)(2,1)S(1)}, u32[]{:S(2)}, u32[]{:S(2)}) collective-permute-start(bf16[16,16,128]{2,1,0:T(8,128)(2,1)S(1)} %get-tuple-element.24), channel_id=1, source_target_pairs={{0,12},{4,8},{8,4},{12,0},{1,13},{5,9},{9,5},{13,1},{2,14},{6,10},... | collective-permute-start | bytes 196616 | tf_op jit(solution)/shard_map/ppermute | solution.py:295
  13.6 0.2 collective-permute-start.5
  13.8 3.3 %collective-permute-done.3.tile_ref = bf16[16,16,128]{2,1,0:T(8,128)(2,1)S(1)} collective-permute-done((bf16[16,16,128]{2,1,0:T(8,128)(2,1)S(1)}, bf16[16,16,128]{2,1,0:T(8,128)(2,1)S(1)}, u32[]{:S(2)}, u32[]{:S(2)}) %collective-permute-start.3) | collective-permute-done | bytes 65568 | tf_op jit(solution)/shard_map/ppermute | solution.py:295
  17.2 1.4 %collective-permute-done.4.tile_ref = bf16[16,16,128]{2,1,0:T(8,128)(2,1)S(1)} collective-permute-done((bf16[16,16,128]{2,1,0:T(8,128)(2,1)S(1)}, bf16[16,16,128]{2,1,0:T(8,128)(2,1)S(1)}, u32[]{:S(2)}, u32[]{:S(2)}) %collective-permute-start.4) | collective-permute-done | bytes 65568 | tf_op jit(solution)/shard_map/ppermute | solution.py:295
  18.7 0.3 shard_map.84
  19.0 3.0 %collective-permute-start.7 = (bf16[16,16,128]{2,1,0:T(8,128)(2,1)S(1)}, bf16[16,16,128]{2,1,0:T(8,128)(2,1)S(1)}, u32[]{:S(2)}, u32[]{:S(2)}) collective-permute-start(bf16[16,16,128]{2,1,0:T(8,128)(2,1)S(1)} %get-tuple-element.31.refs_0_.grad_ref), channel_id=1, source_target_pairs={{0,12},{4,8},{8,4},{12,0},{1,13},{5,9},{9,5},{13,1},{2,14},{6,10},... | collective-permute-start | bytes 196616 | tf_op jit(solution)/shard_map/ppermute | solution.py:295
  22.2 1.2 %collective-permute-start.6 = (bf16[16,16,128]{2,1,0:T(8,128)(2,1)S(1)}, bf16[16,16,128]{2,1,0:T(8,128)(2,1)S(1)}, u32[]{:S(2)}, u32[]{:S(2)}) collective-permute-start(bf16[16,16,128]{2,1,0:T(8,128)(2,1)S(1)} %get-tuple-element.31.refs_0_.grad_ref), channel_id=1, source_target_pairs={{0,8},{4,12},{8,0},{12,4},{1,9},{5,13},{9,1},{13,5},{2,10},{6,14},... | collective-permute-start | bytes 196616 | tf_op jit(solution)/shard_map/ppermute | solution.py:295
  23.7 0.7 %copy-done = bf16[128,640]{1,0:T(8,128)(2,1)S(1)} copy-done((bf16[128,640]{1,0:T(8,128)(2,1)S(1)}, bf16[128,640]{1,0:T(8,128)(2,1)}, u32[]{:S(2)}) %copy-start) | copy-done | bytes 163864
  24.5 0.8 %shard_map.85 = (bf16[16,16,128]{2,1,0:T(8,128)(2,1)}, f32[256,128]{1,0:T(8,128)S(1)}) custom-call(f32[256,128]{1,0:T(8,128)S(1)} %get-tuple-element.27.tri_normed_ref, f32[256,128]{1,0:T(8,128)S(1)} %get-tuple-element.28.open_ref, f32[256,128]{1,0:T(8,128)S(1)} %get-tuple-element.29.gate_factor_ref, bf16[128,640]{1,0:T(8,128)(2,1)S(1)} %copy-done, ...), custom_call_target="tpu_custom_call" | custom-call | flops 16777216 | bytes 786432 | tf_op jit(solution)/shard_map/pallas_call | solution.py:267
  25.7 0.8 %collective-permute-done.8.grad_ref.refs_1_ = bf16[16,16,128]{2,1,0:T(8,128)(2,1)S(1)} collective-permute-done((bf16[16,16,128]{2,1,0:T(8,128)(2,1)S(1)}, bf16[16,16,128]{2,1,0:T(8,128)(2,1)S(1)}, u32[]{:S(2)}, u32[]{:S(2)}) %collective-permute-start.8) | collective-permute-done | bytes 65568 | tf_op jit(solution)/shard_map/ppermute | solution.py:295
  26.7 0.7 %collective-permute-done.6.grad_ref.refs_2_ = bf16[16,16,128]{2,1,0:T(8,128)(2,1)S(1)} collective-permute-done((bf16[16,16,128]{2,1,0:T(8,128)(2,1)S(1)}, bf16[16,16,128]{2,1,0:T(8,128)(2,1)S(1)}, u32[]{:S(2)}, u32[]{:S(2)}) %collective-permute-start.6) | collective-permute-done | bytes 65568 | tf_op jit(solution)/shard_map/ppermute | solution.py:295
  27.4 0.3 shard_map.91
  27.7 1.9 %collective-permute-start.9 = (bf16[16,16,128]{2,1,0:T(8,128)(2,1)S(1)}, bf16[16,16,128]{2,1,0:T(8,128)(2,1)S(1)}, u32[]{:S(2)}, u32[]{:S(2)}) collective-permute-start(bf16[16,16,128]{2,1,0:T(8,128)(2,1)S(1)} %get-tuple-element.34), channel_id=1, source_target_pairs={{0,2},{1,3},{2,0},{3,1},{4,6},{5,7},{6,4},{7,5},{8,10},{9,11},{10,... | collective-permute-start | bytes 196616 | tf_op jit(solution)/shard_map/ppermute | solution.py:295
  29.6 0.3 collective-permute-start.11
  29.9 0.7 %shard_map.94.refs_4_ = f32[256,128]{1,0:T(8,128)S(1)} custom-call(f32[64,16,128]{2,1,0:T(8,128)S(1)} %shard_map.86.panel, bf16[16,16,128]{2,1,0:T(8,128)(2,1)S(1)} %collective-permute-done.7.grad_ref.refs_0_, bf16[16,16,128]{2,1,0:T(8,128)(2,1)S(1)} %collective-permute-done.8.grad_ref.refs_1_, ...), custom_call_target="tpu_custom_call" | custom-call | tf_op jit(solution)/shard_map/pallas_call | solution.py:267
  30.7 1.4 %collective-permute-done.9.tile_ref = bf16[16,16,128]{2,1,0:T(8,128)(2,1)S(1)} collective-permute-done((bf16[16,16,128]{2,1,0:T(8,128)(2,1)S(1)}, bf16[16,16,128]{2,1,0:T(8,128)(2,1)S(1)}, u32[]{:S(2)}, u32[]{:S(2)}) %collective-permute-start.9) | collective-permute-done | bytes 65568 | tf_op jit(solution)/shard_map/ppermute | solution.py:295
  32.1 1.4 %collective-permute-done.10.tile_ref = bf16[16,16,128]{2,1,0:T(8,128)(2,1)S(1)} collective-permute-done((bf16[16,16,128]{2,1,0:T(8,128)(2,1)S(1)}, bf16[16,16,128]{2,1,0:T(8,128)(2,1)S(1)}, u32[]{:S(2)}, u32[]{:S(2)}) %collective-permute-start.10) | collective-permute-done | bytes 65568 | tf_op jit(solution)/shard_map/ppermute | solution.py:295
  33.5 0.9 %shard_map.95 = bf16[16,16,128]{2,1,0:T(8,128)(2,1)} custom-call(f32[16,16,128]{2,1,0:T(8,128)S(1)} %shard_map.93.base, bf16[16,16,128]{2,1,0:T(8,128)(2,1)S(1)} %collective-permute-done.11.refs_0_, f32[256,128]{1,0:T(8,128)S(1)} %get-tuple-element.37.refs_1_, f32[256,128]{1,0:T(8,128)S(1)} %get-tuple-element.38.refs_2_, ...), custom_call_target="tpu_custom_call" | custom-call | flops 16777216 | bytes 1343488 | tf_op jit(solution)/shard_map/pallas_call | solution.py:267
  (23 shorter events, 2.0 us)
Async XLA Ops:
  1.9 5.5 %collective-permute-start.2 = (bf16[16,16,128]{2,1,0:T(8,128)(2,1)S(1)}, bf16[16,16,128]{2,1,0:T(8,128)(2,1)S(1)}, u32[]{:S(2)}, u32[]{:S(2)}) collective-permute-start(bf16[16,16,128]{2,1,0:T(8,128)(2,1)S(1)} %shard_map.77.refs_0_), channel_id=1, source_target_pairs={{0,2},{1,3},{2,0},{3,1},{4,6},{5,7},{6,4},{7,5},{8,10},{9,11},{10,... | collective-permute-start | bytes 196616 | tf_op jit(solution)/shard_map/ppermute | solution.py:295
  4.9 4.1 %collective-permute-start = (bf16[16,16,128]{2,1,0:T(8,128)(2,1)S(1)}, bf16[16,16,128]{2,1,0:T(8,128)(2,1)S(1)}, u32[]{:S(2)}, u32[]{:S(2)}) collective-permute-start(bf16[16,16,128]{2,1,0:T(8,128)(2,1)S(1)} %shard_map.77.refs_0_), channel_id=1, source_target_pairs={{0,3},{1,2},{2,1},{3,0},{4,7},{5,6},{6,5},{7,4},{8,11},{9,10},{10,... | collective-permute-start | bytes 196616 | tf_op jit(solution)/shard_map/ppermute | solution.py:295
  4.9 4.1 %collective-permute-start.1 = (bf16[16,16,128]{2,1,0:T(8,128)(2,1)S(1)}, bf16[16,16,128]{2,1,0:T(8,128)(2,1)S(1)}, u32[]{:S(2)}, u32[]{:S(2)}) collective-permute-start(bf16[16,16,128]{2,1,0:T(8,128)(2,1)S(1)} %shard_map.77.refs_0_), channel_id=1, source_target_pairs={{0,1},{1,0},{2,3},{3,2},{4,5},{5,4},{6,7},{7,6},{8,9},{9,8},{10,11... | collective-permute-start | bytes 196616 | tf_op jit(solution)/shard_map/ppermute | solution.py:295
  9.5 7.6 %collective-permute-start.3 = (bf16[16,16,128]{2,1,0:T(8,128)(2,1)S(1)}, bf16[16,16,128]{2,1,0:T(8,128)(2,1)S(1)}, u32[]{:S(2)}, u32[]{:S(2)}) collective-permute-start(bf16[16,16,128]{2,1,0:T(8,128)(2,1)S(1)} %get-tuple-element.23), channel_id=1, source_target_pairs={{0,8},{4,12},{8,0},{12,4},{1,9},{5,13},{9,1},{13,5},{2,10},{6,14},... | collective-permute-start | bytes 196616 | tf_op jit(solution)/shard_map/ppermute | solution.py:295
  12.2 6.3 %collective-permute-start.4 = (bf16[16,16,128]{2,1,0:T(8,128)(2,1)S(1)}, bf16[16,16,128]{2,1,0:T(8,128)(2,1)S(1)}, u32[]{:S(2)}, u32[]{:S(2)}) collective-permute-start(bf16[16,16,128]{2,1,0:T(8,128)(2,1)S(1)} %get-tuple-element.24), channel_id=1, source_target_pairs={{0,12},{4,8},{8,4},{12,0},{1,13},{5,9},{9,5},{13,1},{2,14},{6,10},... | collective-permute-start | bytes 196616 | tf_op jit(solution)/shard_map/ppermute | solution.py:295
  13.6 5.1 %collective-permute-start.5 = (bf16[16,16,128]{2,1,0:T(8,128)(2,1)S(1)}, bf16[16,16,128]{2,1,0:T(8,128)(2,1)S(1)}, u32[]{:S(2)}, u32[]{:S(2)}) collective-permute-start(bf16[16,16,128]{2,1,0:T(8,128)(2,1)S(1)} %get-tuple-element.25), channel_id=1, source_target_pairs={{0,4},{4,0},{8,12},{12,8},{1,5},{5,1},{9,13},{13,9},{2,6},{6,2},{1... | collective-permute-start | bytes 196616 | tf_op jit(solution)/shard_map/ppermute | solution.py:295
  19.0 6.5 %collective-permute-start.7 = (bf16[16,16,128]{2,1,0:T(8,128)(2,1)S(1)}, bf16[16,16,128]{2,1,0:T(8,128)(2,1)S(1)}, u32[]{:S(2)}, u32[]{:S(2)}) collective-permute-start(bf16[16,16,128]{2,1,0:T(8,128)(2,1)S(1)} %get-tuple-element.31.refs_0_.grad_ref), channel_id=1, source_target_pairs={{0,12},{4,8},{8,4},{12,0},{1,13},{5,9},{9,5},{13,1},{2,14},{6,10},... | collective-permute-start | bytes 196616 | tf_op jit(solution)/shard_map/ppermute | solution.py:295
  22.0 4.5 %collective-permute-start.8 = (bf16[16,16,128]{2,1,0:T(8,128)(2,1)S(1)}, bf16[16,16,128]{2,1,0:T(8,128)(2,1)S(1)}, u32[]{:S(2)}, u32[]{:S(2)}) collective-permute-start(bf16[16,16,128]{2,1,0:T(8,128)(2,1)S(1)} %get-tuple-element.31.refs_0_.grad_ref), channel_id=1, source_target_pairs={{0,4},{4,0},{8,12},{12,8},{1,5},{5,1},{9,13},{13,9},{2,6},{6,2},{1... | collective-permute-start | bytes 196616 | tf_op jit(solution)/shard_map/ppermute | solution.py:295
  22.2 5.2 %collective-permute-start.6 = (bf16[16,16,128]{2,1,0:T(8,128)(2,1)S(1)}, bf16[16,16,128]{2,1,0:T(8,128)(2,1)S(1)}, u32[]{:S(2)}, u32[]{:S(2)}) collective-permute-start(bf16[16,16,128]{2,1,0:T(8,128)(2,1)S(1)} %get-tuple-element.31.refs_0_.grad_ref), channel_id=1, source_target_pairs={{0,8},{4,12},{8,0},{12,4},{1,9},{5,13},{9,1},{13,5},{2,10},{6,14},... | collective-permute-start | bytes 196616 | tf_op jit(solution)/shard_map/ppermute | solution.py:295
  23.5 0.9 %copy-start = (bf16[128,640]{1,0:T(8,128)(2,1)S(1)}, bf16[128,640]{1,0:T(8,128)(2,1)}, u32[]{:S(2)}) copy-start(bf16[128,640]{1,0:T(8,128)(2,1)} %refs_5_.3) | copy-start | bytes 491524
  23.5 0.9 %copy-start.1 = (bf16[128,128]{1,0:T(8,128)(2,1)S(1)}, bf16[128,128]{1,0:T(8,128)(2,1)}, u32[]{:S(2)}) copy-start(bf16[128,128]{1,0:T(8,128)(2,1)} %out_weight_ref.1) | copy-start | bytes 98308
  27.7 4.3 %collective-permute-start.9 = (bf16[16,16,128]{2,1,0:T(8,128)(2,1)S(1)}, bf16[16,16,128]{2,1,0:T(8,128)(2,1)S(1)}, u32[]{:S(2)}, u32[]{:S(2)}) collective-permute-start(bf16[16,16,128]{2,1,0:T(8,128)(2,1)S(1)} %get-tuple-element.34), channel_id=1, source_target_pairs={{0,2},{1,3},{2,0},{3,1},{4,6},{5,7},{6,4},{7,5},{8,10},{9,11},{10,... | collective-permute-start | bytes 196616 | tf_op jit(solution)/shard_map/ppermute | solution.py:295
  29.6 3.8 %collective-permute-start.10 = (bf16[16,16,128]{2,1,0:T(8,128)(2,1)S(1)}, bf16[16,16,128]{2,1,0:T(8,128)(2,1)S(1)}, u32[]{:S(2)}, u32[]{:S(2)}) collective-permute-start(bf16[16,16,128]{2,1,0:T(8,128)(2,1)S(1)} %get-tuple-element.35), channel_id=1, source_target_pairs={{0,3},{1,2},{2,1},{3,0},{4,7},{5,6},{6,5},{7,4},{8,11},{9,10},{10,... | collective-permute-start | bytes 196616 | tf_op jit(solution)/shard_map/ppermute | solution.py:295
  29.6 3.8 %collective-permute-start.11 = (bf16[16,16,128]{2,1,0:T(8,128)(2,1)S(1)}, bf16[16,16,128]{2,1,0:T(8,128)(2,1)S(1)}, u32[]{:S(2)}, u32[]{:S(2)}) collective-permute-start(bf16[16,16,128]{2,1,0:T(8,128)(2,1)S(1)} %get-tuple-element.36), channel_id=1, source_target_pairs={{0,1},{1,0},{2,3},{3,2},{4,5},{5,4},{6,7},{7,6},{8,9},{9,8},{10,11... | collective-permute-start | bytes 196616 | tf_op jit(solution)/shard_map/ppermute | solution.py:295

commit v20 on v19

--- a/solution.py
+++ b/solution.py
@@ -114,7 +114,8 @@
     lin_grad = (cotangent * out_open).astype(bf16)
     open_ref[...] = out_open
     gate_factor_ref[...] = cotangent * out_open * (1.0 - out_open)
-    upstream_ref[...] = dot_t(lin_grad, out_weight_ref[...])
+    upstream = dot_t(lin_grad, out_weight_ref[...])
+    upstream_ref[...] = upstream - mean_lanes(upstream)
 
 
 def weighted_sums(weights, start, terms, out, base=None):
@@ -182,13 +183,21 @@
     pick_kernel(row_steps, *(tiles[step] for step in range(count + known)), *refs[count + 1 + known : -2])
 
 
-def triangle_kernel(base, tile_ref, upstream_ref, tri_normed_ref, grad_ref):
+def triangle_kernel(base, *refs):
+    *tiles, upstream_ref, tri_normed_ref, grad_ref = refs
     size = grad_ref.shape[0]
     for i in range(size):
+        total = base[i]
+        for ref in tiles:
+            total = total + ref[i].astype(f32)
         here = pl.ds(i * size, size)
-        tri_normed, scale = normalize(base[i] + tile_ref[i].astype(f32))
+        upstream = upstream_ref[here, :]
+        center = total - mean_lanes(total)
+        scale = lax.rsqrt(mean_lanes(center * center) + epsilon)
+        tri_normed = center * scale
         tri_normed_ref[here, :] = tri_normed
-        grad_ref[i] = normalize_back(tri_normed, scale, upstream_ref[here, :]).astype(bf16)
+        project = mean_lanes(center * upstream) * scale
+        grad_ref[i] = (scale * (upstream - tri_normed * project)).astype(bf16)
 
 
 def left_terms_kernel(grad_ref, right, *refs):
@@ -217,12 +226,22 @@
 
 
 def right_back_kernel(steps, panel, *refs):
-    factor_ref, weights_ref, share_ref, out, right_ref = refs[-5:]
+    factor_ref, weights_ref, share_ref, normed_ref, scale_ref, out, right_ref = refs[-7:]
     right_grad_kernel(steps, panel, *refs[: len(steps) + 1], right_ref)
     pairs, channels = out.shape
     right = right_ref[...].reshape(pairs, channels)
     grads = jnp.concatenate([(right * factor_ref[block]).astype(bf16) for block in (2, 3)], axis=1)
-    out[...] = share_ref[...] + dot_t(grads, weights_ref[:, 2 * channels : 4 * channels])
+    share = share_ref[...] + dot_t(grads, weights_ref[:, 2 * channels : 4 * channels])
+    out[...] = normalize_back(normed_ref[...], scale_ref[...], share)
+
+
+def slopes_kernel(normed_ref, weights_ref, mean_ref, slope_ref):
+    channels = normed_ref.shape[1]
+    weights = weights_ref[:, : 2 * channels].astype(f32)
+    mean = jnp.sum(weights, axis=0, keepdims=True) * (1.0 / channels)
+    mean_ref[...] = jnp.broadcast_to(mean, mean_ref.shape)
+    slope = jnp.dot(normed_ref[...], weights, precision=lax.Precision.HIGHEST, preferred_element_type=f32)
+    slope_ref[...] = slope * (1.0 / channels)
 
 
 def add_kernel(base, tile_ref, out):
@@ -241,7 +260,7 @@
 
 
 def back_kernel(base, *refs):
-    *tiles, normed_ref, scale_ref, factor_ref, share_ref, weights_ref, out = refs
+    *tiles, normed_ref, scale_ref, factor_ref, done_ref, mean_ref, slope_ref, weights_ref, out = refs
     size, _, channels = out.shape
     pairs = size * size
     left = base[...]
@@ -249,8 +268,11 @@
         left = left + ref[...].astype(f32)
     left = left.reshape(pairs, channels)
     grads = jnp.concatenate([(left * factor_ref[block]).astype(bf16) for block in (0, 1)], axis=1)
-    normed_grad = share_ref[...] + dot_t(grads, weights_ref[:, : 2 * channels])
-    back = normalize_back(normed_ref[...], scale_ref[...], normed_grad)
+    normed_grad = dot_t(grads, weights_ref[:, : 2 * channels])
+    wide_grads = grads.astype(f32)
+    average = jnp.sum(wide_grads * mean_ref[0:1, :], axis=-1, keepdims=True)
+    project = jnp.sum(wide_grads * slope_ref[...], axis=-1, keepdims=True)
+    back = done_ref[...] + scale_ref[...] * (normed_grad - average - normed_ref[...] * project)
     out[...] = back.astype(bf16).reshape(size, size, channels)
 
 
@@ -338,20 +360,27 @@
     (left_panel,) = call(
         functools.partial(left_panel_kernel, [0] + steps), (panel,), crop_length, *lefts, smem=(0,)
     )
+    last = []
     for step, part in zip(row_steps, parts):
         part = swap(part, "row", step)
-        if step != row_steps[-1]:
+        if step in row_steps[-2:]:
+            last.append(part)
+        else:
             (total,) = call(add_kernel, (wide,), total, part, flops=wait)
     tri_normed, tri_grad = call(
-        triangle_kernel, (flat, tile), total, part, upstream, flops=20 * pairs * channels,
+        triangle_kernel, (flat, tile), total, *last, upstream, flops=20 * pairs * channels,
     )
     grads = gather(tri_grad, "row", gather_steps)
     update, partial = call(
         update_kernel, (tile, flat), tri_normed, out_open, gate_factor, in_weights, out_weight,
         flops=4 * pairs * channels * channels,
     )
+    means, slopes = call(
+        slopes_kernel, (jax.ShapeDtypeStruct((8, 2 * channels), f32), jax.ShapeDtypeStruct((pairs, 2 * channels), f32)),
+        normed, in_weights,
+    )
     (right_grad,) = call(functools.partial(right_grad_kernel, [0]), (wide,), left_panel, tri_grad)
-    terms, before = [], (partial, right_grad)
+    terms, before = [], (partial, right_grad, slopes)
     for grad in grads[:-1]:
         before = call(
             left_terms_kernel, (wide,), grad, right, *before,
@@ -363,17 +392,20 @@
         (wide,) + (tile,) * (n - 1), grads[-1], right, *terms, flops=work,
         scratch=[pltpu.VMEM(wide.shape, f32), pltpu.VMEM((pairs, channels), f32)],
     )
+    last = []
     for step, term in zip(steps, terms):
         term = swap(term, "col", step)
-        if step != steps[-1]:
+        if step in steps[-2:]:
+            last.append(term)
+        else:
             (total,) = call(add_kernel, (wide,), total, term, flops=wait)
-    (share,) = call(
+    (done,) = call(
         functools.partial(right_back_kernel, gather_steps), (flat,),
-        left_panel, *grads[1:], right_grad, factors, in_weights, partial,
+        left_panel, *grads[1:], right_grad, factors, in_weights, partial, normed, scale,
         scratch=[pltpu.VMEM(wide.shape, f32)],
     )
     (pair_grad,) = call(
-        back_kernel, (tile,), total, term, normed, scale, factors, share, in_weights,
+        back_kernel, (tile,), total, *last, normed, scale, factors, done, means, slopes, in_weights,
         flops=2 * pairs * channels * 2 * channels,
     )
     return (update, pair_grad)

time: 34.6 us -> 34.5 us (level)
  waiting for transfers between devices: 10.5 us -> 10 us
  Pallas kernels: 7.69 us -> 8.08 us
    ppermute x12, waiting for transfers between devices: 10.5 us -> 10 us  [swap(): return lax.ppermute(values, axis, [(a, a ^ step) for a in range(n)])]
    pallas_call x19 -> x18, Pallas kernels: 7.69 us -> 8.08 us  [call(): pl.pallas_call(kernel, out_shape=tuple(outs), in_specs=specs, out_specs=(...]
  transfers between devices with their start and end apart: 12 -> 12, of which waited for: 8 -> 8; matrix products, arithmetic and copies ran while one was open for 0% -> 0% of each run, Pallas kernels for 13% -> 14%
where the time goes in v20:
time: 34.5 us; the launch traced here: 34.2 us
  starting transfers between devices  14.1 us (41%)
  waiting for transfers between devices  10 us (29%)
  Pallas kernels  8.08 us (23%)
  between operations  1.41 us (4%)
  local copies, waits for them, and re-layouts  0.57 us (2%)
    ppermute x12, starting transfers between devices, swap(): return lax.ppermute(values, axis, [(a, a ^ step) for a in range(n)])  14.1 us
    ppermute x12, waiting for transfers between devices, swap(): return lax.ppermute(values, axis, [(a, a ^ step) for a in range(n)])  10 us
    pallas_call x18, Pallas kernels, call(): pl.pallas_call(kernel, out_shape=tuple(outs), in_specs=specs, out_specs=(...  8.08 us
  transfers between devices with their start and end apart: 12, of which 8 were waited for; matrix products, arithmetic and copies ran while one was open for 0% of the time, Pallas kernels for 14%

profile of v20, /device:TPU:0, one launch (start us, length us, event | category | flops | bytes accessed | tf_op | source)
XLA Modules:
  0.0 34.2 jit_solution(2493178214616502110)
XLA Ops:
  0.6 1.3 %shard_map.77.refs_0_ = bf16[16,16,128]{2,1,0:T(8,128)(2,1)S(1)} custom-call(bf16[16,16,128]{2,1,0:T(8,128)(2,1)} %acts_in.3, s32[16,16]{1,0:T(8,128)} %mask_in.3, bf16[128,640]{1,0:T(8,128)(2,1)} %refs_8_.1), custom_call_target="tpu_custom_call" | custom-call | flops 16777216 | bytes 295936 | tf_op jit(solution)/shard_map/pallas_call | solution.py:289
  1.9 3.0 %collective-permute-start.2 = (bf16[16,16,128]{2,1,0:T(8,128)(2,1)S(1)}, bf16[16,16,128]{2,1,0:T(8,128)(2,1)S(1)}, u32[]{:S(2)}, u32[]{:S(2)}) collective-permute-start(bf16[16,16,128]{2,1,0:T(8,128)(2,1)S(1)} %shard_map.77.refs_0_), channel_id=1, source_target_pairs={{0,2},{1,3},{2,0},{3,1},{4,6},{5,7},{6,4},{7,5},{8,10},{9,11},{10,... | collective-permute-start | bytes 196616 | tf_op jit(solution)/shard_map/ppermute | solution.py:317
  5.8 1.6 %shard_map.78 = (f32[16,16,128]{2,1,0:T(8,128)S(1)}, f32[256,128]{1,0:T(8,128)S(1)}, f32[256,128]{1,0:T(8,128)S(1)}, f32[4,256,128]{2,1,0:T(8,128)S(1)}, f32[256...) custom-call(bf16[16,16,128]{2,1,0:T(8,128)(2,1)} %acts_in.3, s32[16,16]{1,0:T(8,128)} %mask_in.3, ...), custom_call_target="tpu_custom_call" | custom-call | flops 50331648 | bytes 1639428 | tf_op jit(solution)/shard_map/pallas_call | solution.py:289
  7.7 1.3 %collective-permute-done.refs_0_.refs_2_ = bf16[16,16,128]{2,1,0:T(8,128)(2,1)S(1)} collective-permute-done((bf16[16,16,128]{2,1,0:T(8,128)(2,1)S(1)}, bf16[16,16,128]{2,1,0:T(8,128)(2,1)S(1)}, u32[]{:S(2)}, u32[]{:S(2)}) %collective-permute-start) | collective-permute-done | bytes 65568 | tf_op jit(solution)/shard_map/ppermute | solution.py:317
  9.0 0.5 %shard_map.81 = (f32[16,16,128]{2,1,0:T(8,128)S(1)}, bf16[16,16,128]{2,1,0:T(8,128)(2,1)S(1)}, bf16[16,16,128]{2,1,0:T(8,128)(2,1)S(1)}, bf16[16,16,128]{2,1,0:T(8,128)(2,1)S(1)}) custom-call(s32[1]{0:T(128)S(6)} %copy.8.crop_ref, bf16[16,16,128]{2,1,0:T(8,128)(2,1)S(1)} %collective-permute-done.refs_0_.refs_2_, ...), custom_call_target="tpu_custom_call" | custom-call | flops 1048576 | bytes 851972 | tf_op jit(solution)/shard_map/pallas_call | solution.py:289
  9.5 2.7 %collective-permute-start.3 = (bf16[16,16,128]{2,1,0:T(8,128)(2,1)S(1)}, bf16[16,16,128]{2,1,0:T(8,128)(2,1)S(1)}, u32[]{:S(2)}, u32[]{:S(2)}) collective-permute-start(bf16[16,16,128]{2,1,0:T(8,128)(2,1)S(1)} %get-tuple-element.25), channel_id=1, source_target_pairs={{0,8},{4,12},{8,0},{12,4},{1,9},{5,13},{9,1},{13,5},{2,10},{6,14},... | collective-permute-start | bytes 196616 | tf_op jit(solution)/shard_map/ppermute | solution.py:317
  12.2 1.3 %collective-permute-start.4 = (bf16[16,16,128]{2,1,0:T(8,128)(2,1)S(1)}, bf16[16,16,128]{2,1,0:T(8,128)(2,1)S(1)}, u32[]{:S(2)}, u32[]{:S(2)}) collective-permute-start(bf16[16,16,128]{2,1,0:T(8,128)(2,1)S(1)} %get-tuple-element.26), channel_id=1, source_target_pairs={{0,12},{4,8},{8,4},{12,0},{1,13},{5,9},{9,5},{13,1},{2,14},{6,10},... | collective-permute-start | bytes 196616 | tf_op jit(solution)/shard_map/ppermute | solution.py:317
  13.6 0.2 collective-permute-start.5
  13.8 3.3 %collective-permute-done.3.tile_ref = bf16[16,16,128]{2,1,0:T(8,128)(2,1)S(1)} collective-permute-done((bf16[16,16,128]{2,1,0:T(8,128)(2,1)S(1)}, bf16[16,16,128]{2,1,0:T(8,128)(2,1)S(1)}, u32[]{:S(2)}, u32[]{:S(2)}) %collective-permute-start.3) | collective-permute-done | bytes 65568 | tf_op jit(solution)/shard_map/ppermute | solution.py:317
  17.2 1.4 %collective-permute-done.4.refs_0_ = bf16[16,16,128]{2,1,0:T(8,128)(2,1)S(1)} collective-permute-done((bf16[16,16,128]{2,1,0:T(8,128)(2,1)S(1)}, bf16[16,16,128]{2,1,0:T(8,128)(2,1)S(1)}, u32[]{:S(2)}, u32[]{:S(2)}) %collective-permute-start.4) | collective-permute-done | bytes 65568 | tf_op jit(solution)/shard_map/ppermute | solution.py:317
  18.9 3.0 %collective-permute-start.7 = (bf16[16,16,128]{2,1,0:T(8,128)(2,1)S(1)}, bf16[16,16,128]{2,1,0:T(8,128)(2,1)S(1)}, u32[]{:S(2)}, u32[]{:S(2)}) collective-permute-start(bf16[16,16,128]{2,1,0:T(8,128)(2,1)S(1)} %get-tuple-element.33.refs_0_.grad_ref), channel_id=1, source_target_pairs={{0,12},{4,8},{8,4},{12,0},{1,13},{5,9},{9,5},{13,1},{2,14},{6,10},... | collective-permute-start | bytes 196616 | tf_op jit(solution)/shard_map/ppermute | solution.py:317
  22.2 1.2 %collective-permute-start.6 = (bf16[16,16,128]{2,1,0:T(8,128)(2,1)S(1)}, bf16[16,16,128]{2,1,0:T(8,128)(2,1)S(1)}, u32[]{:S(2)}, u32[]{:S(2)}) collective-permute-start(bf16[16,16,128]{2,1,0:T(8,128)(2,1)S(1)} %get-tuple-element.33.refs_0_.grad_ref), channel_id=1, source_target_pairs={{0,8},{4,12},{8,0},{12,4},{1,9},{5,13},{9,1},{13,5},{2,10},{6,14},... | collective-permute-start | bytes 196616 | tf_op jit(solution)/shard_map/ppermute | solution.py:317
  23.4 0.4 %shard_map.87 = (f32[8,256]{1,0:T(8,128)S(1)}, f32[256,256]{1,0:T(8,128)S(1)}) custom-call(f32[256,128]{1,0:T(8,128)S(1)} %get-tuple-element.35.normed_ref.refs_7_.refs_2_, bf16[128,640]{1,0:T(8,128)(2,1)S(1)} %copy-done), custom_call_target="tpu_custom_call" | custom-call | tf_op jit(solution)/shard_map/pallas_call | solution.py:289
  24.1 0.6 %copy-done.1 = bf16[128,128]{1,0:T(8,128)(2,1)S(1)} copy-done((bf16[128,128]{1,0:T(8,128)(2,1)S(1)}, bf16[128,128]{1,0:T(8,128)(2,1)}, u32[]{:S(2)}) %copy-start.1) | copy-done | bytes 32792
  24.6 0.8 %shard_map.84 = (bf16[16,16,128]{2,1,0:T(8,128)(2,1)}, f32[256,128]{1,0:T(8,128)S(1)}) custom-call(f32[256,128]{1,0:T(8,128)S(1)} %get-tuple-element.29.tri_normed_ref, f32[256,128]{1,0:T(8,128)S(1)} %get-tuple-element.30.open_ref, f32[256,128]{1,0:T(8,128)S(1)} %get-tuple-element.31.gate_factor_ref, bf16[128,640]{1,0:T(8,128)(2,1)S(1)} %copy-done, ...), custom_call_target="tpu_custom_call" | custom-call | flops 16777216 | bytes 786432 | tf_op jit(solution)/shard_map/pallas_call | solution.py:289
  25.9 0.6 %collective-permute-done.8.grad_ref.refs_1_ = bf16[16,16,128]{2,1,0:T(8,128)(2,1)S(1)} collective-permute-done((bf16[16,16,128]{2,1,0:T(8,128)(2,1)S(1)}, bf16[16,16,128]{2,1,0:T(8,128)(2,1)S(1)}, u32[]{:S(2)}, u32[]{:S(2)}) %collective-permute-start.8) | collective-permute-done | bytes 65568 | tf_op jit(solution)/shard_map/ppermute | solution.py:317
  26.7 0.6 %collective-permute-done.6.grad_ref.refs_2_ = bf16[16,16,128]{2,1,0:T(8,128)(2,1)S(1)} collective-permute-done((bf16[16,16,128]{2,1,0:T(8,128)(2,1)S(1)}, bf16[16,16,128]{2,1,0:T(8,128)(2,1)S(1)}, u32[]{:S(2)}, u32[]{:S(2)}) %collective-permute-start.6) | collective-permute-done | bytes 65568 | tf_op jit(solution)/shard_map/ppermute | solution.py:317
  27.3 0.3 shard_map.91
  27.7 1.9 %collective-permute-start.9 = (bf16[16,16,128]{2,1,0:T(8,128)(2,1)S(1)}, bf16[16,16,128]{2,1,0:T(8,128)(2,1)S(1)}, u32[]{:S(2)}, u32[]{:S(2)}) collective-permute-start(bf16[16,16,128]{2,1,0:T(8,128)(2,1)S(1)} %get-tuple-element.38), channel_id=1, source_target_pairs={{0,2},{1,3},{2,0},{3,1},{4,6},{5,7},{6,4},{7,5},{8,10},{9,11},{10,... | collective-permute-start | bytes 196616 | tf_op jit(solution)/shard_map/ppermute | solution.py:317
  29.6 0.3 collective-permute-start.11
  29.9 0.8 %shard_map.93.refs_5_ = f32[256,128]{1,0:T(8,128)S(1)} custom-call(f32[64,16,128]{2,1,0:T(8,128)S(1)} %shard_map.85.panel, bf16[16,16,128]{2,1,0:T(8,128)(2,1)S(1)} %collective-permute-done.7.grad_ref.refs_0_, bf16[16,16,128]{2,1,0:T(8,128)(2,1)S(1)} %collective-permute-done.8.grad_ref.refs_1_, ...), custom_call_target="tpu_custom_call" | custom-call | tf_op jit(solution)/shard_map/pallas_call | solution.py:289
  30.7 1.3 %collective-permute-done.9.tile_ref = bf16[16,16,128]{2,1,0:T(8,128)(2,1)S(1)} collective-permute-done((bf16[16,16,128]{2,1,0:T(8,128)(2,1)S(1)}, bf16[16,16,128]{2,1,0:T(8,128)(2,1)S(1)}, u32[]{:S(2)}, u32[]{:S(2)}) %collective-permute-start.9) | collective-permute-done | bytes 65568 | tf_op jit(solution)/shard_map/ppermute | solution.py:317
  32.0 1.4 %collective-permute-done.10.refs_0_ = bf16[16,16,128]{2,1,0:T(8,128)(2,1)S(1)} collective-permute-done((bf16[16,16,128]{2,1,0:T(8,128)(2,1)S(1)}, bf16[16,16,128]{2,1,0:T(8,128)(2,1)S(1)}, u32[]{:S(2)}, u32[]{:S(2)}) %collective-permute-start.10) | collective-permute-done | bytes 65568 | tf_op jit(solution)/shard_map/ppermute | solution.py:317
  33.4 0.8 %shard_map.94 = bf16[16,16,128]{2,1,0:T(8,128)(2,1)} custom-call(f32[16,16,128]{2,1,0:T(8,128)S(1)} %shard_map.92.base, bf16[16,16,128]{2,1,0:T(8,128)(2,1)S(1)} %collective-permute-done.10.refs_0_, bf16[16,16,128]{2,1,0:T(8,128)(2,1)S(1)} %collective-permute-done.11.refs_1_, f32[256,128]{1,0:T(8,128)S(1)} %get-tuple-element.35.normed_ref.refs_7_.refs_2_, ...), custom_call_target="tpu_custom_call" | custom-call | flops 16777216 | bytes 1679360 | tf_op jit(solution)/shard_map/pallas_call | solution.py:289
  (22 shorter events, 2.2 us)
Async XLA Ops:
  1.9 5.6 %collective-permute-start.2 = (bf16[16,16,128]{2,1,0:T(8,128)(2,1)S(1)}, bf16[16,16,128]{2,1,0:T(8,128)(2,1)S(1)}, u32[]{:S(2)}, u32[]{:S(2)}) collective-permute-start(bf16[16,16,128]{2,1,0:T(8,128)(2,1)S(1)} %shard_map.77.refs_0_), channel_id=1, source_target_pairs={{0,2},{1,3},{2,0},{3,1},{4,6},{5,7},{6,4},{7,5},{8,10},{9,11},{10,... | collective-permute-start | bytes 196616 | tf_op jit(solution)/shard_map/ppermute | solution.py:317
  4.9 4.1 %collective-permute-start = (bf16[16,16,128]{2,1,0:T(8,128)(2,1)S(1)}, bf16[16,16,128]{2,1,0:T(8,128)(2,1)S(1)}, u32[]{:S(2)}, u32[]{:S(2)}) collective-permute-start(bf16[16,16,128]{2,1,0:T(8,128)(2,1)S(1)} %shard_map.77.refs_0_), channel_id=1, source_target_pairs={{0,3},{1,2},{2,1},{3,0},{4,7},{5,6},{6,5},{7,4},{8,11},{9,10},{10,... | collective-permute-start | bytes 196616 | tf_op jit(solution)/shard_map/ppermute | solution.py:317
  4.9 4.1 %collective-permute-start.1 = (bf16[16,16,128]{2,1,0:T(8,128)(2,1)S(1)}, bf16[16,16,128]{2,1,0:T(8,128)(2,1)S(1)}, u32[]{:S(2)}, u32[]{:S(2)}) collective-permute-start(bf16[16,16,128]{2,1,0:T(8,128)(2,1)S(1)} %shard_map.77.refs_0_), channel_id=1, source_target_pairs={{0,1},{1,0},{2,3},{3,2},{4,5},{5,4},{6,7},{7,6},{8,9},{9,8},{10,11... | collective-permute-start | bytes 196616 | tf_op jit(solution)/shard_map/ppermute | solution.py:317
  9.5 7.6 %collective-permute-start.3 = (bf16[16,16,128]{2,1,0:T(8,128)(2,1)S(1)}, bf16[16,16,128]{2,1,0:T(8,128)(2,1)S(1)}, u32[]{:S(2)}, u32[]{:S(2)}) collective-permute-start(bf16[16,16,128]{2,1,0:T(8,128)(2,1)S(1)} %get-tuple-element.25), channel_id=1, source_target_pairs={{0,8},{4,12},{8,0},{12,4},{1,9},{5,13},{9,1},{13,5},{2,10},{6,14},... | collective-permute-start | bytes 196616 | tf_op jit(solution)/shard_map/ppermute | solution.py:317
  12.2 6.3 %collective-permute-start.4 = (bf16[16,16,128]{2,1,0:T(8,128)(2,1)S(1)}, bf16[16,16,128]{2,1,0:T(8,128)(2,1)S(1)}, u32[]{:S(2)}, u32[]{:S(2)}) collective-permute-start(bf16[16,16,128]{2,1,0:T(8,128)(2,1)S(1)} %get-tuple-element.26), channel_id=1, source_target_pairs={{0,12},{4,8},{8,4},{12,0},{1,13},{5,9},{9,5},{13,1},{2,14},{6,10},... | collective-permute-start | bytes 196616 | tf_op jit(solution)/shard_map/ppermute | solution.py:317
  13.6 5.1 %collective-permute-start.5 = (bf16[16,16,128]{2,1,0:T(8,128)(2,1)S(1)}, bf16[16,16,128]{2,1,0:T(8,128)(2,1)S(1)}, u32[]{:S(2)}, u32[]{:S(2)}) collective-permute-start(bf16[16,16,128]{2,1,0:T(8,128)(2,1)S(1)} %get-tuple-element.27), channel_id=1, source_target_pairs={{0,4},{4,0},{8,12},{12,8},{1,5},{5,1},{9,13},{13,9},{2,6},{6,2},{1... | collective-permute-start | bytes 196616 | tf_op jit(solution)/shard_map/ppermute | solution.py:317
  18.7 4.7 %copy-start = (bf16[128,640]{1,0:T(8,128)(2,1)S(1)}, bf16[128,640]{1,0:T(8,128)(2,1)}, u32[]{:S(2)}) copy-start(bf16[128,640]{1,0:T(8,128)(2,1)} %refs_8_.1) | copy-start | bytes 491524
  18.9 6.7 %collective-permute-start.7 = (bf16[16,16,128]{2,1,0:T(8,128)(2,1)S(1)}, bf16[16,16,128]{2,1,0:T(8,128)(2,1)S(1)}, u32[]{:S(2)}, u32[]{:S(2)}) collective-permute-start(bf16[16,16,128]{2,1,0:T(8,128)(2,1)S(1)} %get-tuple-element.33.refs_0_.grad_ref), channel_id=1, source_target_pairs={{0,12},{4,8},{8,4},{12,0},{1,13},{5,9},{9,5},{13,1},{2,14},{6,10},... | collective-permute-start | bytes 196616 | tf_op jit(solution)/shard_map/ppermute | solution.py:317
  22.0 4.5 %collective-permute-start.8 = (bf16[16,16,128]{2,1,0:T(8,128)(2,1)S(1)}, bf16[16,16,128]{2,1,0:T(8,128)(2,1)S(1)}, u32[]{:S(2)}, u32[]{:S(2)}) collective-permute-start(bf16[16,16,128]{2,1,0:T(8,128)(2,1)S(1)} %get-tuple-element.33.refs_0_.grad_ref), channel_id=1, source_target_pairs={{0,4},{4,0},{8,12},{12,8},{1,5},{5,1},{9,13},{13,9},{2,6},{6,2},{1... | collective-permute-start | bytes 196616 | tf_op jit(solution)/shard_map/ppermute | solution.py:317
  22.2 5.2 %collective-permute-start.6 = (bf16[16,16,128]{2,1,0:T(8,128)(2,1)S(1)}, bf16[16,16,128]{2,1,0:T(8,128)(2,1)S(1)}, u32[]{:S(2)}, u32[]{:S(2)}) collective-permute-start(bf16[16,16,128]{2,1,0:T(8,128)(2,1)S(1)} %get-tuple-element.33.refs_0_.grad_ref), channel_id=1, source_target_pairs={{0,8},{4,12},{8,0},{12,4},{1,9},{5,13},{9,1},{13,5},{2,10},{6,14},... | collective-permute-start | bytes 196616 | tf_op jit(solution)/shard_map/ppermute | solution.py:317
  23.9 0.8 %copy-start.1 = (bf16[128,128]{1,0:T(8,128)(2,1)S(1)}, bf16[128,128]{1,0:T(8,128)(2,1)}, u32[]{:S(2)}) copy-start(bf16[128,128]{1,0:T(8,128)(2,1)} %out_weight_ref.1) | copy-start | bytes 98308
  27.7 4.3 %collective-permute-start.9 = (bf16[16,16,128]{2,1,0:T(8,128)(2,1)S(1)}, bf16[16,16,128]{2,1,0:T(8,128)(2,1)S(1)}, u32[]{:S(2)}, u32[]{:S(2)}) collective-permute-start(bf16[16,16,128]{2,1,0:T(8,128)(2,1)S(1)} %get-tuple-element.38), channel_id=1, source_target_pairs={{0,2},{1,3},{2,0},{3,1},{4,6},{5,7},{6,4},{7,5},{8,10},{9,11},{10,... | collective-permute-start | bytes 196616 | tf_op jit(solution)/shard_map/ppermute | solution.py:317
  29.6 3.8 %collective-permute-start.10 = (bf16[16,16,128]{2,1,0:T(8,128)(2,1)S(1)}, bf16[16,16,128]{2,1,0:T(8,128)(2,1)S(1)}, u32[]{:S(2)}, u32[]{:S(2)}) collective-permute-start(bf16[16,16,128]{2,1,0:T(8,128)(2,1)S(1)} %get-tuple-element.39), channel_id=1, source_target_pairs={{0,3},{1,2},{2,1},{3,0},{4,7},{5,6},{6,5},{7,4},{8,11},{9,10},{10,... | collective-permute-start | bytes 196616 | tf_op jit(solution)/shard_map/ppermute | solution.py:317
  29.6 3.8 %collective-permute-start.11 = (bf16[16,16,128]{2,1,0:T(8,128)(2,1)S(1)}, bf16[16,16,128]{2,1,0:T(8,128)(2,1)S(1)}, u32[]{:S(2)}, u32[]{:S(2)}) collective-permute-start(bf16[16,16,128]{2,1,0:T(8,128)(2,1)S(1)} %get-tuple-element.40), channel_id=1, source_target_pairs={{0,1},{1,0},{2,3},{3,2},{4,5},{5,4},{6,7},{7,6},{8,9},{9,8},{10,11... | collective-permute-start | bytes 196616 | tf_op jit(solution)/shard_map/ppermute | solution.py:317

commit v21 on v20

--- a/solution.py
+++ b/solution.py
@@ -310,7 +310,7 @@
     wait = 2**31
     steps = [step for bit in range(n.bit_length() - 2, -1, -1) for step in range(2**bit, 2 ** (bit + 1))]
     row_steps = steps
-    gather_steps = [n - 1] + list(range(1, n - 1))
+    gather_steps = steps
 
 
     def swap(values, axis, step):

time: 34.5 us -> 35.2 us (1.020)
  waiting for transfers between devices: 10 us -> 11.6 us
  starting transfers between devices: 14.1 us -> 13.3 us
    ppermute x12, waiting for transfers between devices: 10 us -> 11.6 us  [swap(): return lax.ppermute(values, axis, [(a, a ^ step) for a in range(n)])]
    ppermute x12, starting transfers between devices: 14.1 us -> 13.3 us  [swap(): return lax.ppermute(values, axis, [(a, a ^ step) for a in range(n)])]
where the time goes in v21:
time: 35.2 us; the launch traced here: 34.9 us
  starting transfers between devices  13.3 us (38%)
  waiting for transfers between devices  11.6 us (33%)
  Pallas kernels  8.08 us (23%)
  between operations  1.41 us (4%)
  local copies, waits for them, and re-layouts  0.57 us (2%)
    ppermute x12, starting transfers between devices, swap(): return lax.ppermute(values, axis, [(a, a ^ step) for a in range(n)])  13.3 us
    ppermute x12, waiting for transfers between devices, swap(): return lax.ppermute(values, axis, [(a, a ^ step) for a in range(n)])  11.6 us
    pallas_call x18, Pallas kernels, call(): pl.pallas_call(kernel, out_shape=tuple(outs), in_specs=specs, out_specs=(...  8.08 us
  transfers between devices with their start and end apart: 12, of which 8 were waited for; matrix products, arithmetic and copies ran while one was open for 0% of the time, Pallas kernels for 14%

profile of v21, /device:TPU:0, one launch (start us, length us, event | category | flops | bytes accessed | tf_op | source)
XLA Modules:
  0.0 34.9 jit_solution(17734181403528687747)
XLA Ops:
  0.6 1.3 %shard_map.77.refs_0_ = bf16[16,16,128]{2,1,0:T(8,128)(2,1)S(1)} custom-call(bf16[16,16,128]{2,1,0:T(8,128)(2,1)} %acts_in.3, s32[16,16]{1,0:T(8,128)} %mask_in.3, bf16[128,640]{1,0:T(8,128)(2,1)} %refs_8_.1), custom_call_target="tpu_custom_call" | custom-call | flops 16777216 | bytes 295936 | tf_op jit(solution)/shard_map/pallas_call | solution.py:289
  1.9 3.0 %collective-permute-start.2 = (bf16[16,16,128]{2,1,0:T(8,128)(2,1)S(1)}, bf16[16,16,128]{2,1,0:T(8,128)(2,1)S(1)}, u32[]{:S(2)}, u32[]{:S(2)}) collective-permute-start(bf16[16,16,128]{2,1,0:T(8,128)(2,1)S(1)} %shard_map.77.refs_0_), channel_id=1, source_target_pairs={{0,2},{1,3},{2,0},{3,1},{4,6},{5,7},{6,4},{7,5},{8,10},{9,11},{10,... | collective-permute-start | bytes 196616 | tf_op jit(solution)/shard_map/ppermute | solution.py:317
  5.8 1.6 %shard_map.78 = (f32[16,16,128]{2,1,0:T(8,128)S(1)}, f32[256,128]{1,0:T(8,128)S(1)}, f32[256,128]{1,0:T(8,128)S(1)}, f32[4,256,128]{2,1,0:T(8,128)S(1)}, f32[256...) custom-call(bf16[16,16,128]{2,1,0:T(8,128)(2,1)} %acts_in.3, s32[16,16]{1,0:T(8,128)} %mask_in.3, ...), custom_call_target="tpu_custom_call" | custom-call | flops 50331648 | bytes 1639428 | tf_op jit(solution)/shard_map/pallas_call | solution.py:289
  7.7 1.3 %collective-permute-done.refs_0_.refs_2_ = bf16[16,16,128]{2,1,0:T(8,128)(2,1)S(1)} collective-permute-done((bf16[16,16,128]{2,1,0:T(8,128)(2,1)S(1)}, bf16[16,16,128]{2,1,0:T(8,128)(2,1)S(1)}, u32[]{:S(2)}, u32[]{:S(2)}) %collective-permute-start) | collective-permute-done | bytes 65568 | tf_op jit(solution)/shard_map/ppermute | solution.py:317
  9.0 0.5 %shard_map.81 = (f32[16,16,128]{2,1,0:T(8,128)S(1)}, bf16[16,16,128]{2,1,0:T(8,128)(2,1)S(1)}, bf16[16,16,128]{2,1,0:T(8,128)(2,1)S(1)}, bf16[16,16,128]{2,1,0:T(8,128)(2,1)S(1)}) custom-call(s32[1]{0:T(128)S(6)} %copy.8.crop_ref, bf16[16,16,128]{2,1,0:T(8,128)(2,1)S(1)} %collective-permute-done.refs_0_.refs_2_, ...), custom_call_target="tpu_custom_call" | custom-call | flops 1048576 | bytes 851972 | tf_op jit(solution)/shard_map/pallas_call | solution.py:289
  9.5 2.7 %collective-permute-start.3 = (bf16[16,16,128]{2,1,0:T(8,128)(2,1)S(1)}, bf16[16,16,128]{2,1,0:T(8,128)(2,1)S(1)}, u32[]{:S(2)}, u32[]{:S(2)}) collective-permute-start(bf16[16,16,128]{2,1,0:T(8,128)(2,1)S(1)} %get-tuple-element.25), channel_id=1, source_target_pairs={{0,8},{4,12},{8,0},{12,4},{1,9},{5,13},{9,1},{13,5},{2,10},{6,14},... | collective-permute-start | bytes 196616 | tf_op jit(solution)/shard_map/ppermute | solution.py:317
  12.2 1.3 %collective-permute-start.4 = (bf16[16,16,128]{2,1,0:T(8,128)(2,1)S(1)}, bf16[16,16,128]{2,1,0:T(8,128)(2,1)S(1)}, u32[]{:S(2)}, u32[]{:S(2)}) collective-permute-start(bf16[16,16,128]{2,1,0:T(8,128)(2,1)S(1)} %get-tuple-element.26), channel_id=1, source_target_pairs={{0,12},{4,8},{8,4},{12,0},{1,13},{5,9},{9,5},{13,1},{2,14},{6,10},... | collective-permute-start | bytes 196616 | tf_op jit(solution)/shard_map/ppermute | solution.py:317
  13.8 3.3 %collective-permute-done.3.tile_ref = bf16[16,16,128]{2,1,0:T(8,128)(2,1)S(1)} collective-permute-done((bf16[16,16,128]{2,1,0:T(8,128)(2,1)S(1)}, bf16[16,16,128]{2,1,0:T(8,128)(2,1)S(1)}, u32[]{:S(2)}, u32[]{:S(2)}) %collective-permute-start.3) | collective-permute-done | bytes 65568 | tf_op jit(solution)/shard_map/ppermute | solution.py:317
  17.2 1.4 %collective-permute-done.4.refs_0_ = bf16[16,16,128]{2,1,0:T(8,128)(2,1)S(1)} collective-permute-done((bf16[16,16,128]{2,1,0:T(8,128)(2,1)S(1)}, bf16[16,16,128]{2,1,0:T(8,128)(2,1)S(1)}, u32[]{:S(2)}, u32[]{:S(2)}) %collective-permute-start.4) | collective-permute-done | bytes 65568 | tf_op jit(solution)/shard_map/ppermute | solution.py:317
  18.9 2.7 %collective-permute-start.7 = (bf16[16,16,128]{2,1,0:T(8,128)(2,1)S(1)}, bf16[16,16,128]{2,1,0:T(8,128)(2,1)S(1)}, u32[]{:S(2)}, u32[]{:S(2)}) collective-permute-start(bf16[16,16,128]{2,1,0:T(8,128)(2,1)S(1)} %get-tuple-element.33.refs_0_.grad_ref), channel_id=1, source_target_pairs={{0,8},{4,12},{8,0},{12,4},{1,9},{5,13},{9,1},{13,5},{2,10},{6,14},... | collective-permute-start | bytes 196616 | tf_op jit(solution)/shard_map/ppermute | solution.py:317
  21.6 0.6 %collective-permute-start.8 = (bf16[16,16,128]{2,1,0:T(8,128)(2,1)S(1)}, bf16[16,16,128]{2,1,0:T(8,128)(2,1)S(1)}, u32[]{:S(2)}, u32[]{:S(2)}) collective-permute-start(bf16[16,16,128]{2,1,0:T(8,128)(2,1)S(1)} %get-tuple-element.33.refs_0_.grad_ref), channel_id=1, source_target_pairs={{0,12},{4,8},{8,4},{12,0},{1,13},{5,9},{9,5},{13,1},{2,14},{6,10},... | collective-permute-start | bytes 196616 | tf_op jit(solution)/shard_map/ppermute | solution.py:317
  22.2 0.3 collective-permute-start.6
  22.5 0.4 %shard_map.87 = (f32[8,256]{1,0:T(8,128)S(1)}, f32[256,256]{1,0:T(8,128)S(1)}) custom-call(f32[256,128]{1,0:T(8,128)S(1)} %get-tuple-element.35.normed_ref.refs_7_.refs_2_, bf16[128,640]{1,0:T(8,128)(2,1)S(1)} %copy-done), custom_call_target="tpu_custom_call" | custom-call | tf_op jit(solution)/shard_map/pallas_call | solution.py:289
  23.2 0.6 %copy-done.1 = bf16[128,128]{1,0:T(8,128)(2,1)S(1)} copy-done((bf16[128,128]{1,0:T(8,128)(2,1)S(1)}, bf16[128,128]{1,0:T(8,128)(2,1)}, u32[]{:S(2)}) %copy-start.1) | copy-done | bytes 32792
  23.8 0.8 %shard_map.84 = (bf16[16,16,128]{2,1,0:T(8,128)(2,1)}, f32[256,128]{1,0:T(8,128)S(1)}) custom-call(f32[256,128]{1,0:T(8,128)S(1)} %get-tuple-element.29.tri_normed_ref, f32[256,128]{1,0:T(8,128)S(1)} %get-tuple-element.30.open_ref, f32[256,128]{1,0:T(8,128)S(1)} %get-tuple-element.31.gate_factor_ref, bf16[128,640]{1,0:T(8,128)(2,1)S(1)} %copy-done, ...), custom_call_target="tpu_custom_call" | custom-call | flops 16777216 | bytes 786432 | tf_op jit(solution)/shard_map/pallas_call | solution.py:289
  24.8 1.5 %collective-permute-done.7.grad_ref.refs_0_ = bf16[16,16,128]{2,1,0:T(8,128)(2,1)S(1)} collective-permute-done((bf16[16,16,128]{2,1,0:T(8,128)(2,1)S(1)}, bf16[16,16,128]{2,1,0:T(8,128)(2,1)S(1)}, u32[]{:S(2)}, u32[]{:S(2)}) %collective-permute-start.7) | collective-permute-done | bytes 65568 | tf_op jit(solution)/shard_map/ppermute | solution.py:317
  26.6 1.2 %collective-permute-done.8.grad_ref.refs_1_ = bf16[16,16,128]{2,1,0:T(8,128)(2,1)S(1)} collective-permute-done((bf16[16,16,128]{2,1,0:T(8,128)(2,1)S(1)}, bf16[16,16,128]{2,1,0:T(8,128)(2,1)S(1)}, u32[]{:S(2)}, u32[]{:S(2)}) %collective-permute-start.8) | collective-permute-done | bytes 65568 | tf_op jit(solution)/shard_map/ppermute | solution.py:317
  28.0 0.3 shard_map.91
  28.3 1.6 %collective-permute-start.9 = (bf16[16,16,128]{2,1,0:T(8,128)(2,1)S(1)}, bf16[16,16,128]{2,1,0:T(8,128)(2,1)S(1)}, u32[]{:S(2)}, u32[]{:S(2)}) collective-permute-start(bf16[16,16,128]{2,1,0:T(8,128)(2,1)S(1)} %get-tuple-element.38), channel_id=1, source_target_pairs={{0,2},{1,3},{2,0},{3,1},{4,6},{5,7},{6,4},{7,5},{8,10},{9,11},{10,... | collective-permute-start | bytes 196616 | tf_op jit(solution)/shard_map/ppermute | solution.py:317
  29.9 0.6 %collective-permute-start.11 = (bf16[16,16,128]{2,1,0:T(8,128)(2,1)S(1)}, bf16[16,16,128]{2,1,0:T(8,128)(2,1)S(1)}, u32[]{:S(2)}, u32[]{:S(2)}) collective-permute-start(bf16[16,16,128]{2,1,0:T(8,128)(2,1)S(1)} %get-tuple-element.40), channel_id=1, source_target_pairs={{0,1},{1,0},{2,3},{3,2},{4,5},{5,4},{6,7},{7,6},{8,9},{9,8},{10,11... | collective-permute-start | bytes 196616 | tf_op jit(solution)/shard_map/ppermute | solution.py:317
  30.5 0.8 %shard_map.93.refs_5_ = f32[256,128]{1,0:T(8,128)S(1)} custom-call(f32[64,16,128]{2,1,0:T(8,128)S(1)} %shard_map.85.panel, bf16[16,16,128]{2,1,0:T(8,128)(2,1)S(1)} %collective-permute-done.7.grad_ref.refs_0_, bf16[16,16,128]{2,1,0:T(8,128)(2,1)S(1)} %collective-permute-done.8.grad_ref.refs_1_, ...), custom_call_target="tpu_custom_call" | custom-call | tf_op jit(solution)/shard_map/pallas_call | solution.py:289
  31.4 1.3 %collective-permute-done.9.tile_ref = bf16[16,16,128]{2,1,0:T(8,128)(2,1)S(1)} collective-permute-done((bf16[16,16,128]{2,1,0:T(8,128)(2,1)S(1)}, bf16[16,16,128]{2,1,0:T(8,128)(2,1)S(1)}, u32[]{:S(2)}, u32[]{:S(2)}) %collective-permute-start.9) | collective-permute-done | bytes 65568 | tf_op jit(solution)/shard_map/ppermute | solution.py:317
  32.7 1.4 %collective-permute-done.10.refs_0_ = bf16[16,16,128]{2,1,0:T(8,128)(2,1)S(1)} collective-permute-done((bf16[16,16,128]{2,1,0:T(8,128)(2,1)S(1)}, bf16[16,16,128]{2,1,0:T(8,128)(2,1)S(1)}, u32[]{:S(2)}, u32[]{:S(2)}) %collective-permute-start.10) | collective-permute-done | bytes 65568 | tf_op jit(solution)/shard_map/ppermute | solution.py:317
  34.1 0.8 %shard_map.94 = bf16[16,16,128]{2,1,0:T(8,128)(2,1)} custom-call(f32[16,16,128]{2,1,0:T(8,128)S(1)} %shard_map.92.base, bf16[16,16,128]{2,1,0:T(8,128)(2,1)S(1)} %collective-permute-done.10.refs_0_, bf16[16,16,128]{2,1,0:T(8,128)(2,1)S(1)} %collective-permute-done.11.refs_1_, f32[256,128]{1,0:T(8,128)S(1)} %get-tuple-element.35.normed_ref.refs_7_.refs_2_, ...), custom_call_target="tpu_custom_call" | custom-call | flops 16777216 | bytes 1679360 | tf_op jit(solution)/shard_map/pallas_call | solution.py:289
  (22 shorter events, 2.2 us)
Async XLA Ops:
  1.9 5.6 %collective-permute-start.2 = (bf16[16,16,128]{2,1,0:T(8,128)(2,1)S(1)}, bf16[16,16,128]{2,1,0:T(8,128)(2,1)S(1)}, u32[]{:S(2)}, u32[]{:S(2)}) collective-permute-start(bf16[16,16,128]{2,1,0:T(8,128)(2,1)S(1)} %shard_map.77.refs_0_), channel_id=1, source_target_pairs={{0,2},{1,3},{2,0},{3,1},{4,6},{5,7},{6,4},{7,5},{8,10},{9,11},{10,... | collective-permute-start | bytes 196616 | tf_op jit(solution)/shard_map/ppermute | solution.py:317
  4.9 4.1 %collective-permute-start = (bf16[16,16,128]{2,1,0:T(8,128)(2,1)S(1)}, bf16[16,16,128]{2,1,0:T(8,128)(2,1)S(1)}, u32[]{:S(2)}, u32[]{:S(2)}) collective-permute-start(bf16[16,16,128]{2,1,0:T(8,128)(2,1)S(1)} %shard_map.77.refs_0_), channel_id=1, source_target_pairs={{0,3},{1,2},{2,1},{3,0},{4,7},{5,6},{6,5},{7,4},{8,11},{9,10},{10,... | collective-permute-start | bytes 196616 | tf_op jit(solution)/shard_map/ppermute | solution.py:317
  4.9 4.1 %collective-permute-start.1 = (bf16[16,16,128]{2,1,0:T(8,128)(2,1)S(1)}, bf16[16,16,128]{2,1,0:T(8,128)(2,1)S(1)}, u32[]{:S(2)}, u32[]{:S(2)}) collective-permute-start(bf16[16,16,128]{2,1,0:T(8,128)(2,1)S(1)} %shard_map.77.refs_0_), channel_id=1, source_target_pairs={{0,1},{1,0},{2,3},{3,2},{4,5},{5,4},{6,7},{7,6},{8,9},{9,8},{10,11... | collective-permute-start | bytes 196616 | tf_op jit(solution)/shard_map/ppermute | solution.py:317
  9.5 7.6 %collective-permute-start.3 = (bf16[16,16,128]{2,1,0:T(8,128)(2,1)S(1)}, bf16[16,16,128]{2,1,0:T(8,128)(2,1)S(1)}, u32[]{:S(2)}, u32[]{:S(2)}) collective-permute-start(bf16[16,16,128]{2,1,0:T(8,128)(2,1)S(1)} %get-tuple-element.25), channel_id=1, source_target_pairs={{0,8},{4,12},{8,0},{12,4},{1,9},{5,13},{9,1},{13,5},{2,10},{6,14},... | collective-permute-start | bytes 196616 | tf_op jit(solution)/shard_map/ppermute | solution.py:317
  12.2 6.3 %collective-permute-start.4 = (bf16[16,16,128]{2,1,0:T(8,128)(2,1)S(1)}, bf16[16,16,128]{2,1,0:T(8,128)(2,1)S(1)}, u32[]{:S(2)}, u32[]{:S(2)}) collective-permute-start(bf16[16,16,128]{2,1,0:T(8,128)(2,1)S(1)} %get-tuple-element.26), channel_id=1, source_target_pairs={{0,12},{4,8},{8,4},{12,0},{1,13},{5,9},{9,5},{13,1},{2,14},{6,10},... | collective-permute-start | bytes 196616 | tf_op jit(solution)/shard_map/ppermute | solution.py:317
  13.6 5.1 %collective-permute-start.5 = (bf16[16,16,128]{2,1,0:T(8,128)(2,1)S(1)}, bf16[16,16,128]{2,1,0:T(8,128)(2,1)S(1)}, u32[]{:S(2)}, u32[]{:S(2)}) collective-permute-start(bf16[16,16,128]{2,1,0:T(8,128)(2,1)S(1)} %get-tuple-element.27), channel_id=1, source_target_pairs={{0,4},{4,0},{8,12},{12,8},{1,5},{5,1},{9,13},{13,9},{2,6},{6,2},{1... | collective-permute-start | bytes 196616 | tf_op jit(solution)/shard_map/ppermute | solution.py:317
  18.7 3.8 %copy-start = (bf16[128,640]{1,0:T(8,128)(2,1)S(1)}, bf16[128,640]{1,0:T(8,128)(2,1)}, u32[]{:S(2)}) copy-start(bf16[128,640]{1,0:T(8,128)(2,1)} %refs_8_.1) | copy-start | bytes 491524
  18.9 7.4 %collective-permute-start.7 = (bf16[16,16,128]{2,1,0:T(8,128)(2,1)S(1)}, bf16[16,16,128]{2,1,0:T(8,128)(2,1)S(1)}, u32[]{:S(2)}, u32[]{:S(2)}) collective-permute-start(bf16[16,16,128]{2,1,0:T(8,128)(2,1)S(1)} %get-tuple-element.33.refs_0_.grad_ref), channel_id=1, source_target_pairs={{0,8},{4,12},{8,0},{12,4},{1,9},{5,13},{9,1},{13,5},{2,10},{6,14},... | collective-permute-start | bytes 196616 | tf_op jit(solution)/shard_map/ppermute | solution.py:317
  21.6 6.2 %collective-permute-start.8 = (bf16[16,16,128]{2,1,0:T(8,128)(2,1)S(1)}, bf16[16,16,128]{2,1,0:T(8,128)(2,1)S(1)}, u32[]{:S(2)}, u32[]{:S(2)}) collective-permute-start(bf16[16,16,128]{2,1,0:T(8,128)(2,1)S(1)} %get-tuple-element.33.refs_0_.grad_ref), channel_id=1, source_target_pairs={{0,12},{4,8},{8,4},{12,0},{1,13},{5,9},{9,5},{13,1},{2,14},{6,10},... | collective-permute-start | bytes 196616 | tf_op jit(solution)/shard_map/ppermute | solution.py:317
  22.2 5.8 %collective-permute-start.6 = (bf16[16,16,128]{2,1,0:T(8,128)(2,1)S(1)}, bf16[16,16,128]{2,1,0:T(8,128)(2,1)S(1)}, u32[]{:S(2)}, u32[]{:S(2)}) collective-permute-start(bf16[16,16,128]{2,1,0:T(8,128)(2,1)S(1)} %get-tuple-element.33.refs_0_.grad_ref), channel_id=1, source_target_pairs={{0,4},{4,0},{8,12},{12,8},{1,5},{5,1},{9,13},{13,9},{2,6},{6,2},{1... | collective-permute-start | bytes 196616 | tf_op jit(solution)/shard_map/ppermute | solution.py:317
  23.0 0.8 %copy-start.1 = (bf16[128,128]{1,0:T(8,128)(2,1)S(1)}, bf16[128,128]{1,0:T(8,128)(2,1)}, u32[]{:S(2)}) copy-start(bf16[128,128]{1,0:T(8,128)(2,1)} %out_weight_ref.1) | copy-start | bytes 98308
  28.3 4.3 %collective-permute-start.9 = (bf16[16,16,128]{2,1,0:T(8,128)(2,1)S(1)}, bf16[16,16,128]{2,1,0:T(8,128)(2,1)S(1)}, u32[]{:S(2)}, u32[]{:S(2)}) collective-permute-start(bf16[16,16,128]{2,1,0:T(8,128)(2,1)S(1)} %get-tuple-element.38), channel_id=1, source_target_pairs={{0,2},{1,3},{2,0},{3,1},{4,6},{5,7},{6,4},{7,5},{8,10},{9,11},{10,... | collective-permute-start | bytes 196616 | tf_op jit(solution)/shard_map/ppermute | solution.py:317
  29.9 4.2 %collective-permute-start.10 = (bf16[16,16,128]{2,1,0:T(8,128)(2,1)S(1)}, bf16[16,16,128]{2,1,0:T(8,128)(2,1)S(1)}, u32[]{:S(2)}, u32[]{:S(2)}) collective-permute-start(bf16[16,16,128]{2,1,0:T(8,128)(2,1)S(1)} %get-tuple-element.39), channel_id=1, source_target_pairs={{0,3},{1,2},{2,1},{3,0},{4,7},{5,6},{6,5},{7,4},{8,11},{9,10},{10,... | collective-permute-start | bytes 196616 | tf_op jit(solution)/shard_map/ppermute | solution.py:317
  29.9 4.2 %collective-permute-start.11 = (bf16[16,16,128]{2,1,0:T(8,128)(2,1)S(1)}, bf16[16,16,128]{2,1,0:T(8,128)(2,1)S(1)}, u32[]{:S(2)}, u32[]{:S(2)}) collective-permute-start(bf16[16,16,128]{2,1,0:T(8,128)(2,1)S(1)} %get-tuple-element.40), channel_id=1, source_target_pairs={{0,1},{1,0},{2,3},{3,2},{4,5},{5,4},{6,7},{7,6},{8,9},{9,8},{10,11... | collective-permute-start | bytes 196616 | tf_op jit(solution)/shard_map/ppermute | solution.py:317

commit v22 on v20

--- a/solution.py
+++ b/solution.py
@@ -128,7 +128,7 @@
         out[k] = total.astype(out.dtype)
         return 0
 
-    lax.fori_loop(0, out.shape[0], step, 0, unroll=4)
+    lax.fori_loop(0, out.shape[0], step, 0, unroll=8)
 
 
 def left_panel_kernel(steps, crop_ref, *refs):
@@ -158,9 +158,9 @@
             return tuple(sums[i] + left[k, pl.ds(i, 1), :] * other for i in range(size))
 
         zero = jnp.zeros((size, channels), f32)
-        sums = lax.fori_loop(0, size, add, (zero,) * size, unroll=4)
+        sums = lax.fori_loop(0, size, add, (zero,) * size, unroll=8)
         for i in range(size):
-            out[i] = sums[i]
+            out[i] = sums[i].astype(out.dtype)
 
 
 def pick_kernel(steps, *refs):
@@ -347,7 +347,7 @@
     order = [0] + steps
     parts = [
         call(
-            functools.partial(partial_kernel, [order[at]]), (wide,), crop_length, lefts[at], right, smem=(0,),
+            functools.partial(partial_kernel, [order[at]]), (tile,), crop_length, lefts[at], right, smem=(0,),
             flops=work, scratch=[pltpu.VMEM(wide.shape, f32)],
         )[0]
         for at in range(n - 2)
@@ -355,7 +355,7 @@
     total, *parts = call(
         functools.partial(last_partial_kernel, order[-2:], order[:-2], [0] + row_steps),
         (wide,) + (tile,) * (n - 1), crop_length, *lefts[-2:], right, *parts, smem=(0,), flops=work,
-        scratch=[pltpu.VMEM(wide.shape, f32), pltpu.VMEM((2,) + wide.shape, f32)],
+        scratch=[pltpu.VMEM(wide.shape, f32), pltpu.VMEM((2,) + wide.shape, bf16)],
     )
     (left_panel,) = call(
         functools.partial(left_panel_kernel, [0] + steps), (panel,), crop_length, *lefts, smem=(0,)
@@ -383,14 +383,14 @@
     terms, before = [], (partial, right_grad, slopes)
     for grad in grads[:-1]:
         before = call(
-            left_terms_kernel, (wide,), grad, right, *before,
+            left_terms_kernel, (tile,), grad, right, *before,
             scratch=[pltpu.VMEM((pairs, channels), f32)], flops=work,
         )
         terms += before
     total, *terms = call(
         functools.partial(last_terms_kernel, [0] + gather_steps[:-1], gather_steps[-1], [0] + steps),
         (wide,) + (tile,) * (n - 1), grads[-1], right, *terms, flops=work,
-        scratch=[pltpu.VMEM(wide.shape, f32), pltpu.VMEM((pairs, channels), f32)],
+        scratch=[pltpu.VMEM(tile.shape, bf16), pltpu.VMEM((pairs, channels), f32)],
     )
     last = []
     for step, term in zip(steps, terms):

time: 34.5 us -> 34.4 us (level)
  no operation moved by 1% of the time
where the time goes in v22:
time: 34.4 us; the launch traced here: 34.2 us
  starting transfers between devices  14.1 us (41%)
  waiting for transfers between devices  10.2 us (30%)
  Pallas kernels  7.85 us (23%)
  between operations  1.41 us (4%)
  local copies, waits for them, and re-layouts  0.58 us (2%)
    ppermute x12, starting transfers between devices, swap(): return lax.ppermute(values, axis, [(a, a ^ step) for a in range(n)])  14.1 us
    ppermute x12, waiting for transfers between devices, swap(): return lax.ppermute(values, axis, [(a, a ^ step) for a in range(n)])  10.2 us
    pallas_call x18, Pallas kernels, call(): pl.pallas_call(kernel, out_shape=tuple(outs), in_specs=specs, out_specs=(...  7.85 us
  transfers between devices with their start and end apart: 12, of which 8 were waited for; matrix products, arithmetic and copies ran while one was open for 0% of the time, Pallas kernels for 14%

profile of v22, /device:TPU:0, one launch (start us, length us, event | category | flops | bytes accessed | tf_op | source)
XLA Modules:
  0.0 34.2 jit_solution(8994503782290216431)
XLA Ops:
  0.6 1.3 %shard_map.77.refs_0_ = bf16[16,16,128]{2,1,0:T(8,128)(2,1)S(1)} custom-call(bf16[16,16,128]{2,1,0:T(8,128)(2,1)} %acts_in.3, s32[16,16]{1,0:T(8,128)} %mask_in.3, bf16[128,640]{1,0:T(8,128)(2,1)} %refs_8_.1), custom_call_target="tpu_custom_call" | custom-call | flops 16777216 | bytes 295936 | tf_op jit(solution)/shard_map/pallas_call | solution.py:289
  1.9 3.0 %collective-permute-start.2 = (bf16[16,16,128]{2,1,0:T(8,128)(2,1)S(1)}, bf16[16,16,128]{2,1,0:T(8,128)(2,1)S(1)}, u32[]{:S(2)}, u32[]{:S(2)}) collective-permute-start(bf16[16,16,128]{2,1,0:T(8,128)(2,1)S(1)} %shard_map.77.refs_0_), channel_id=1, source_target_pairs={{0,2},{1,3},{2,0},{3,1},{4,6},{5,7},{6,4},{7,5},{8,10},{9,11},{10,... | collective-permute-start | bytes 196616 | tf_op jit(solution)/shard_map/ppermute | solution.py:317
  5.8 1.6 %shard_map.78 = (f32[16,16,128]{2,1,0:T(8,128)S(1)}, f32[256,128]{1,0:T(8,128)S(1)}, f32[256,128]{1,0:T(8,128)S(1)}, f32[4,256,128]{2,1,0:T(8,128)S(1)}, f32[256...) custom-call(bf16[16,16,128]{2,1,0:T(8,128)(2,1)} %acts_in.3, s32[16,16]{1,0:T(8,128)} %mask_in.3, ...), custom_call_target="tpu_custom_call" | custom-call | flops 50331648 | bytes 1639428 | tf_op jit(solution)/shard_map/pallas_call | solution.py:289
  7.7 1.3 %collective-permute-done.refs_0_.refs_2_ = bf16[16,16,128]{2,1,0:T(8,128)(2,1)S(1)} collective-permute-done((bf16[16,16,128]{2,1,0:T(8,128)(2,1)S(1)}, bf16[16,16,128]{2,1,0:T(8,128)(2,1)S(1)}, u32[]{:S(2)}, u32[]{:S(2)}) %collective-permute-start) | collective-permute-done | bytes 65568 | tf_op jit(solution)/shard_map/ppermute | solution.py:317
  9.0 0.4 %shard_map.81 = (f32[16,16,128]{2,1,0:T(8,128)S(1)}, bf16[16,16,128]{2,1,0:T(8,128)(2,1)S(1)}, bf16[16,16,128]{2,1,0:T(8,128)(2,1)S(1)}, bf16[16,16,128]{2,1,0:T(8,128)(2,1)S(1)}) custom-call(s32[1]{0:T(128)S(6)} %copy.8.crop_ref, bf16[16,16,128]{2,1,0:T(8,128)(2,1)S(1)} %collective-permute-done.refs_0_.refs_2_, ...), custom_call_target="tpu_custom_call" | custom-call | flops 1048576 | bytes 720900 | tf_op jit(solution)/shard_map/pallas_call | solution.py:289
  9.5 2.7 %collective-permute-start.3 = (bf16[16,16,128]{2,1,0:T(8,128)(2,1)S(1)}, bf16[16,16,128]{2,1,0:T(8,128)(2,1)S(1)}, u32[]{:S(2)}, u32[]{:S(2)}) collective-permute-start(bf16[16,16,128]{2,1,0:T(8,128)(2,1)S(1)} %get-tuple-element.25), channel_id=1, source_target_pairs={{0,8},{4,12},{8,0},{12,4},{1,9},{5,13},{9,1},{13,5},{2,10},{6,14},... | collective-permute-start | bytes 196616 | tf_op jit(solution)/shard_map/ppermute | solution.py:317
  12.2 1.4 %collective-permute-start.4 = (bf16[16,16,128]{2,1,0:T(8,128)(2,1)S(1)}, bf16[16,16,128]{2,1,0:T(8,128)(2,1)S(1)}, u32[]{:S(2)}, u32[]{:S(2)}) collective-permute-start(bf16[16,16,128]{2,1,0:T(8,128)(2,1)S(1)} %get-tuple-element.26), channel_id=1, source_target_pairs={{0,12},{4,8},{8,4},{12,0},{1,13},{5,9},{9,5},{13,1},{2,14},{6,10},... | collective-permute-start | bytes 196616 | tf_op jit(solution)/shard_map/ppermute | solution.py:317
  13.8 3.3 %collective-permute-done.3.tile_ref = bf16[16,16,128]{2,1,0:T(8,128)(2,1)S(1)} collective-permute-done((bf16[16,16,128]{2,1,0:T(8,128)(2,1)S(1)}, bf16[16,16,128]{2,1,0:T(8,128)(2,1)S(1)}, u32[]{:S(2)}, u32[]{:S(2)}) %collective-permute-start.3) | collective-permute-done | bytes 65568 | tf_op jit(solution)/shard_map/ppermute | solution.py:317
  17.1 1.3 %collective-permute-done.4.refs_0_ = bf16[16,16,128]{2,1,0:T(8,128)(2,1)S(1)} collective-permute-done((bf16[16,16,128]{2,1,0:T(8,128)(2,1)S(1)}, bf16[16,16,128]{2,1,0:T(8,128)(2,1)S(1)}, u32[]{:S(2)}, u32[]{:S(2)}) %collective-permute-start.4) | collective-permute-done | bytes 65568 | tf_op jit(solution)/shard_map/ppermute | solution.py:317
  18.7 0.2 shard_map.83
  18.9 3.0 %collective-permute-start.7 = (bf16[16,16,128]{2,1,0:T(8,128)(2,1)S(1)}, bf16[16,16,128]{2,1,0:T(8,128)(2,1)S(1)}, u32[]{:S(2)}, u32[]{:S(2)}) collective-permute-start(bf16[16,16,128]{2,1,0:T(8,128)(2,1)S(1)} %get-tuple-element.33.refs_0_.grad_ref), channel_id=1, source_target_pairs={{0,12},{4,8},{8,4},{12,0},{1,13},{5,9},{9,5},{13,1},{2,14},{6,10},... | collective-permute-start | bytes 196616 | tf_op jit(solution)/shard_map/ppermute | solution.py:317
  22.1 1.2 %collective-permute-start.6 = (bf16[16,16,128]{2,1,0:T(8,128)(2,1)S(1)}, bf16[16,16,128]{2,1,0:T(8,128)(2,1)S(1)}, u32[]{:S(2)}, u32[]{:S(2)}) collective-permute-start(bf16[16,16,128]{2,1,0:T(8,128)(2,1)S(1)} %get-tuple-element.33.refs_0_.grad_ref), channel_id=1, source_target_pairs={{0,8},{4,12},{8,0},{12,4},{1,9},{5,13},{9,1},{13,5},{2,10},{6,14},... | collective-permute-start | bytes 196616 | tf_op jit(solution)/shard_map/ppermute | solution.py:317
  23.3 0.4 %shard_map.87 = (f32[8,256]{1,0:T(8,128)S(1)}, f32[256,256]{1,0:T(8,128)S(1)}) custom-call(f32[256,128]{1,0:T(8,128)S(1)} %get-tuple-element.35.normed_ref.refs_7_.refs_2_, bf16[128,640]{1,0:T(8,128)(2,1)S(1)} %copy-done), custom_call_target="tpu_custom_call" | custom-call | tf_op jit(solution)/shard_map/pallas_call | solution.py:289
  24.0 0.6 %copy-done.1 = bf16[128,128]{1,0:T(8,128)(2,1)S(1)} copy-done((bf16[128,128]{1,0:T(8,128)(2,1)S(1)}, bf16[128,128]{1,0:T(8,128)(2,1)}, u32[]{:S(2)}) %copy-start.1) | copy-done | bytes 32792
  24.6 0.8 %shard_map.84 = (bf16[16,16,128]{2,1,0:T(8,128)(2,1)}, f32[256,128]{1,0:T(8,128)S(1)}) custom-call(f32[256,128]{1,0:T(8,128)S(1)} %get-tuple-element.29.tri_normed_ref, f32[256,128]{1,0:T(8,128)S(1)} %get-tuple-element.30.open_ref, f32[256,128]{1,0:T(8,128)S(1)} %get-tuple-element.31.gate_factor_ref, bf16[128,640]{1,0:T(8,128)(2,1)S(1)} %copy-done, ...), custom_call_target="tpu_custom_call" | custom-call | flops 16777216 | bytes 786432 | tf_op jit(solution)/shard_map/pallas_call | solution.py:289
  25.8 0.6 %collective-permute-done.8.grad_ref.refs_1_ = bf16[16,16,128]{2,1,0:T(8,128)(2,1)S(1)} collective-permute-done((bf16[16,16,128]{2,1,0:T(8,128)(2,1)S(1)}, bf16[16,16,128]{2,1,0:T(8,128)(2,1)S(1)}, u32[]{:S(2)}, u32[]{:S(2)}) %collective-permute-start.8) | collective-permute-done | bytes 65568 | tf_op jit(solution)/shard_map/ppermute | solution.py:317
  26.6 0.7 %collective-permute-done.6.grad_ref.refs_2_ = bf16[16,16,128]{2,1,0:T(8,128)(2,1)S(1)} collective-permute-done((bf16[16,16,128]{2,1,0:T(8,128)(2,1)S(1)}, bf16[16,16,128]{2,1,0:T(8,128)(2,1)S(1)}, u32[]{:S(2)}, u32[]{:S(2)}) %collective-permute-start.6) | collective-permute-done | bytes 65568 | tf_op jit(solution)/shard_map/ppermute | solution.py:317
  27.3 0.3 shard_map.91
  27.6 1.9 %collective-permute-start.9 = (bf16[16,16,128]{2,1,0:T(8,128)(2,1)S(1)}, bf16[16,16,128]{2,1,0:T(8,128)(2,1)S(1)}, u32[]{:S(2)}, u32[]{:S(2)}) collective-permute-start(bf16[16,16,128]{2,1,0:T(8,128)(2,1)S(1)} %get-tuple-element.38), channel_id=1, source_target_pairs={{0,2},{1,3},{2,0},{3,1},{4,6},{5,7},{6,4},{7,5},{8,10},{9,11},{10,... | collective-permute-start | bytes 196616 | tf_op jit(solution)/shard_map/ppermute | solution.py:317
  29.5 0.3 collective-permute-start.11
  29.8 0.8 %shard_map.93.refs_5_ = f32[256,128]{1,0:T(8,128)S(1)} custom-call(f32[64,16,128]{2,1,0:T(8,128)S(1)} %shard_map.85.panel, bf16[16,16,128]{2,1,0:T(8,128)(2,1)S(1)} %collective-permute-done.7.grad_ref.refs_0_, bf16[16,16,128]{2,1,0:T(8,128)(2,1)S(1)} %collective-permute-done.8.grad_ref.refs_1_, ...), custom_call_target="tpu_custom_call" | custom-call | tf_op jit(solution)/shard_map/pallas_call | solution.py:289
  30.6 1.3 %collective-permute-done.9.tile_ref = bf16[16,16,128]{2,1,0:T(8,128)(2,1)S(1)} collective-permute-done((bf16[16,16,128]{2,1,0:T(8,128)(2,1)S(1)}, bf16[16,16,128]{2,1,0:T(8,128)(2,1)S(1)}, u32[]{:S(2)}, u32[]{:S(2)}) %collective-permute-start.9) | collective-permute-done | bytes 65568 | tf_op jit(solution)/shard_map/ppermute | solution.py:317
  31.9 1.4 %collective-permute-done.10.refs_0_ = bf16[16,16,128]{2,1,0:T(8,128)(2,1)S(1)} collective-permute-done((bf16[16,16,128]{2,1,0:T(8,128)(2,1)S(1)}, bf16[16,16,128]{2,1,0:T(8,128)(2,1)S(1)}, u32[]{:S(2)}, u32[]{:S(2)}) %collective-permute-start.10) | collective-permute-done | bytes 65568 | tf_op jit(solution)/shard_map/ppermute | solution.py:317
  33.3 0.8 %shard_map.94 = bf16[16,16,128]{2,1,0:T(8,128)(2,1)} custom-call(f32[16,16,128]{2,1,0:T(8,128)S(1)} %shard_map.92.base, bf16[16,16,128]{2,1,0:T(8,128)(2,1)S(1)} %collective-permute-done.10.refs_0_, bf16[16,16,128]{2,1,0:T(8,128)(2,1)S(1)} %collective-permute-done.11.refs_1_, f32[256,128]{1,0:T(8,128)S(1)} %get-tuple-element.35.normed_ref.refs_7_.refs_2_, ...), custom_call_target="tpu_custom_call" | custom-call | flops 16777216 | bytes 1679360 | tf_op jit(solution)/shard_map/pallas_call | solution.py:289
  (22 shorter events, 2.1 us)
Async XLA Ops:
  1.9 5.6 %collective-permute-start.2 = (bf16[16,16,128]{2,1,0:T(8,128)(2,1)S(1)}, bf16[16,16,128]{2,1,0:T(8,128)(2,1)S(1)}, u32[]{:S(2)}, u32[]{:S(2)}) collective-permute-start(bf16[16,16,128]{2,1,0:T(8,128)(2,1)S(1)} %shard_map.77.refs_0_), channel_id=1, source_target_pairs={{0,2},{1,3},{2,0},{3,1},{4,6},{5,7},{6,4},{7,5},{8,10},{9,11},{10,... | collective-permute-start | bytes 196616 | tf_op jit(solution)/shard_map/ppermute | solution.py:317
  4.9 4.1 %collective-permute-start = (bf16[16,16,128]{2,1,0:T(8,128)(2,1)S(1)}, bf16[16,16,128]{2,1,0:T(8,128)(2,1)S(1)}, u32[]{:S(2)}, u32[]{:S(2)}) collective-permute-start(bf16[16,16,128]{2,1,0:T(8,128)(2,1)S(1)} %shard_map.77.refs_0_), channel_id=1, source_target_pairs={{0,3},{1,2},{2,1},{3,0},{4,7},{5,6},{6,5},{7,4},{8,11},{9,10},{10,... | collective-permute-start | bytes 196616 | tf_op jit(solution)/shard_map/ppermute | solution.py:317
  4.9 4.1 %collective-permute-start.1 = (bf16[16,16,128]{2,1,0:T(8,128)(2,1)S(1)}, bf16[16,16,128]{2,1,0:T(8,128)(2,1)S(1)}, u32[]{:S(2)}, u32[]{:S(2)}) collective-permute-start(bf16[16,16,128]{2,1,0:T(8,128)(2,1)S(1)} %shard_map.77.refs_0_), channel_id=1, source_target_pairs={{0,1},{1,0},{2,3},{3,2},{4,5},{5,4},{6,7},{7,6},{8,9},{9,8},{10,11... | collective-permute-start | bytes 196616 | tf_op jit(solution)/shard_map/ppermute | solution.py:317
  9.5 7.6 %collective-permute-start.3 = (bf16[16,16,128]{2,1,0:T(8,128)(2,1)S(1)}, bf16[16,16,128]{2,1,0:T(8,128)(2,1)S(1)}, u32[]{:S(2)}, u32[]{:S(2)}) collective-permute-start(bf16[16,16,128]{2,1,0:T(8,128)(2,1)S(1)} %get-tuple-element.25), channel_id=1, source_target_pairs={{0,8},{4,12},{8,0},{12,4},{1,9},{5,13},{9,1},{13,5},{2,10},{6,14},... | collective-permute-start | bytes 196616 | tf_op jit(solution)/shard_map/ppermute | solution.py:317
  12.2 6.3 %collective-permute-start.4 = (bf16[16,16,128]{2,1,0:T(8,128)(2,1)S(1)}, bf16[16,16,128]{2,1,0:T(8,128)(2,1)S(1)}, u32[]{:S(2)}, u32[]{:S(2)}) collective-permute-start(bf16[16,16,128]{2,1,0:T(8,128)(2,1)S(1)} %get-tuple-element.26), channel_id=1, source_target_pairs={{0,12},{4,8},{8,4},{12,0},{1,13},{5,9},{9,5},{13,1},{2,14},{6,10},... | collective-permute-start | bytes 196616 | tf_op jit(solution)/shard_map/ppermute | solution.py:317
  13.5 5.1 %collective-permute-start.5 = (bf16[16,16,128]{2,1,0:T(8,128)(2,1)S(1)}, bf16[16,16,128]{2,1,0:T(8,128)(2,1)S(1)}, u32[]{:S(2)}, u32[]{:S(2)}) collective-permute-start(bf16[16,16,128]{2,1,0:T(8,128)(2,1)S(1)} %get-tuple-element.27), channel_id=1, source_target_pairs={{0,4},{4,0},{8,12},{12,8},{1,5},{5,1},{9,13},{13,9},{2,6},{6,2},{1... | collective-permute-start | bytes 196616 | tf_op jit(solution)/shard_map/ppermute | solution.py:317
  18.7 4.7 %copy-start = (bf16[128,640]{1,0:T(8,128)(2,1)S(1)}, bf16[128,640]{1,0:T(8,128)(2,1)}, u32[]{:S(2)}) copy-start(bf16[128,640]{1,0:T(8,128)(2,1)} %refs_8_.1) | copy-start | bytes 491524
  18.9 6.7 %collective-permute-start.7 = (bf16[16,16,128]{2,1,0:T(8,128)(2,1)S(1)}, bf16[16,16,128]{2,1,0:T(8,128)(2,1)S(1)}, u32[]{:S(2)}, u32[]{:S(2)}) collective-permute-start(bf16[16,16,128]{2,1,0:T(8,128)(2,1)S(1)} %get-tuple-element.33.refs_0_.grad_ref), channel_id=1, source_target_pairs={{0,12},{4,8},{8,4},{12,0},{1,13},{5,9},{9,5},{13,1},{2,14},{6,10},... | collective-permute-start | bytes 196616 | tf_op jit(solution)/shard_map/ppermute | solution.py:317
  21.9 4.5 %collective-permute-start.8 = (bf16[16,16,128]{2,1,0:T(8,128)(2,1)S(1)}, bf16[16,16,128]{2,1,0:T(8,128)(2,1)S(1)}, u32[]{:S(2)}, u32[]{:S(2)}) collective-permute-start(bf16[16,16,128]{2,1,0:T(8,128)(2,1)S(1)} %get-tuple-element.33.refs_0_.grad_ref), channel_id=1, source_target_pairs={{0,4},{4,0},{8,12},{12,8},{1,5},{5,1},{9,13},{13,9},{2,6},{6,2},{1... | collective-permute-start | bytes 196616 | tf_op jit(solution)/shard_map/ppermute | solution.py:317
  22.1 5.2 %collective-permute-start.6 = (bf16[16,16,128]{2,1,0:T(8,128)(2,1)S(1)}, bf16[16,16,128]{2,1,0:T(8,128)(2,1)S(1)}, u32[]{:S(2)}, u32[]{:S(2)}) collective-permute-start(bf16[16,16,128]{2,1,0:T(8,128)(2,1)S(1)} %get-tuple-element.33.refs_0_.grad_ref), channel_id=1, source_target_pairs={{0,8},{4,12},{8,0},{12,4},{1,9},{5,13},{9,1},{13,5},{2,10},{6,14},... | collective-permute-start | bytes 196616 | tf_op jit(solution)/shard_map/ppermute | solution.py:317
  23.8 0.8 %copy-start.1 = (bf16[128,128]{1,0:T(8,128)(2,1)S(1)}, bf16[128,128]{1,0:T(8,128)(2,1)}, u32[]{:S(2)}) copy-start(bf16[128,128]{1,0:T(8,128)(2,1)} %out_weight_ref.1) | copy-start | bytes 98308
  27.6 4.3 %collective-permute-start.9 = (bf16[16,16,128]{2,1,0:T(8,128)(2,1)S(1)}, bf16[16,16,128]{2,1,0:T(8,128)(2,1)S(1)}, u32[]{:S(2)}, u32[]{:S(2)}) collective-permute-start(bf16[16,16,128]{2,1,0:T(8,128)(2,1)S(1)} %get-tuple-element.38), channel_id=1, source_target_pairs={{0,2},{1,3},{2,0},{3,1},{4,6},{5,7},{6,4},{7,5},{8,10},{9,11},{10,... | collective-permute-start | bytes 196616 | tf_op jit(solution)/shard_map/ppermute | solution.py:317
  29.5 3.8 %collective-permute-start.10 = (bf16[16,16,128]{2,1,0:T(8,128)(2,1)S(1)}, bf16[16,16,128]{2,1,0:T(8,128)(2,1)S(1)}, u32[]{:S(2)}, u32[]{:S(2)}) collective-permute-start(bf16[16,16,128]{2,1,0:T(8,128)(2,1)S(1)} %get-tuple-element.39), channel_id=1, source_target_pairs={{0,3},{1,2},{2,1},{3,0},{4,7},{5,6},{6,5},{7,4},{8,11},{9,10},{10,... | collective-permute-start | bytes 196616 | tf_op jit(solution)/shard_map/ppermute | solution.py:317
  29.5 3.8 %collective-permute-start.11 = (bf16[16,16,128]{2,1,0:T(8,128)(2,1)S(1)}, bf16[16,16,128]{2,1,0:T(8,128)(2,1)S(1)}, u32[]{:S(2)}, u32[]{:S(2)}) collective-permute-start(bf16[16,16,128]{2,1,0:T(8,128)(2,1)S(1)} %get-tuple-element.40), channel_id=1, source_target_pairs={{0,1},{1,0},{2,3},{3,2},{4,5},{5,4},{6,7},{7,6},{8,9},{9,8},{10,11... | collective-permute-start | bytes 196616 | tf_op jit(solution)/shard_map/ppermute | solution.py:317

commit v23 on v22

--- a/solution.py
+++ b/solution.py
@@ -128,7 +128,7 @@
         out[k] = total.astype(out.dtype)
         return 0
 
-    lax.fori_loop(0, out.shape[0], step, 0, unroll=8)
+    lax.fori_loop(0, out.shape[0], step, 0, unroll=16)
 
 
 def left_panel_kernel(steps, crop_ref, *refs):
@@ -158,7 +158,7 @@
             return tuple(sums[i] + left[k, pl.ds(i, 1), :] * other for i in range(size))
 
         zero = jnp.zeros((size, channels), f32)
-        sums = lax.fori_loop(0, size, add, (zero,) * size, unroll=8)
+        sums = lax.fori_loop(0, size, add, (zero,) * size, unroll=16)
         for i in range(size):
             out[i] = sums[i].astype(out.dtype)
 

time: 34.4 us -> 34.3 us (level)
  Pallas kernels: 7.85 us -> 7.5 us
    pallas_call x18, Pallas kernels: 7.85 us -> 7.5 us  [call(): pl.pallas_call(kernel, out_shape=tuple(outs), in_specs=specs, out_specs=(...]
  transfers between devices with their start and end apart: 12 -> 12, of which waited for: 8 -> 8; matrix products, arithmetic and copies ran while one was open for 0% -> 0% of each run, Pallas kernels for 14% -> 13%
where the time goes in v23:
time: 34.3 us; the launch traced here: 34.1 us
  starting transfers between devices  14.1 us (41%)
  waiting for transfers between devices  10.4 us (30%)
  Pallas kernels  7.5 us (22%)
  between operations  1.41 us (4%)
  local copies, waits for them, and re-layouts  0.6 us (2%)
    ppermute x12, starting transfers between devices, swap(): return lax.ppermute(values, axis, [(a, a ^ step) for a in range(n)])  14.1 us
    ppermute x12, waiting for transfers between devices, swap(): return lax.ppermute(values, axis, [(a, a ^ step) for a in range(n)])  10.4 us
    pallas_call x18, Pallas kernels, call(): pl.pallas_call(kernel, out_shape=tuple(outs), in_specs=specs, out_specs=(...  7.5 us
  transfers between devices with their start and end apart: 12, of which 8 were waited for; matrix products, arithmetic and copies ran while one was open for 0% of the time, Pallas kernels for 13%

profile of v23, /device:TPU:0, one launch (start us, length us, event | category | flops | bytes accessed | tf_op | source)
XLA Modules:
  0.0 34.1 jit_solution(10961546097245878024)
XLA Ops:
  0.6 1.3 %shard_map.77.refs_0_ = bf16[16,16,128]{2,1,0:T(8,128)(2,1)S(1)} custom-call(bf16[16,16,128]{2,1,0:T(8,128)(2,1)} %acts_in.3, s32[16,16]{1,0:T(8,128)} %mask_in.3, bf16[128,640]{1,0:T(8,128)(2,1)} %refs_8_.1), custom_call_target="tpu_custom_call" | custom-call | flops 16777216 | bytes 295936 | tf_op jit(solution)/shard_map/pallas_call | solution.py:289
  1.9 3.0 %collective-permute-start.2 = (bf16[16,16,128]{2,1,0:T(8,128)(2,1)S(1)}, bf16[16,16,128]{2,1,0:T(8,128)(2,1)S(1)}, u32[]{:S(2)}, u32[]{:S(2)}) collective-permute-start(bf16[16,16,128]{2,1,0:T(8,128)(2,1)S(1)} %shard_map.77.refs_0_), channel_id=1, source_target_pairs={{0,2},{1,3},{2,0},{3,1},{4,6},{5,7},{6,4},{7,5},{8,10},{9,11},{10,... | collective-permute-start | bytes 196616 | tf_op jit(solution)/shard_map/ppermute | solution.py:317
  5.8 1.6 %shard_map.78 = (f32[16,16,128]{2,1,0:T(8,128)S(1)}, f32[256,128]{1,0:T(8,128)S(1)}, f32[256,128]{1,0:T(8,128)S(1)}, f32[4,256,128]{2,1,0:T(8,128)S(1)}, f32[256...) custom-call(bf16[16,16,128]{2,1,0:T(8,128)(2,1)} %acts_in.3, s32[16,16]{1,0:T(8,128)} %mask_in.3, ...), custom_call_target="tpu_custom_call" | custom-call | flops 50331648 | bytes 1639428 | tf_op jit(solution)/shard_map/pallas_call | solution.py:289
  7.7 1.4 %collective-permute-done.refs_0_.refs_2_ = bf16[16,16,128]{2,1,0:T(8,128)(2,1)S(1)} collective-permute-done((bf16[16,16,128]{2,1,0:T(8,128)(2,1)S(1)}, bf16[16,16,128]{2,1,0:T(8,128)(2,1)S(1)}, u32[]{:S(2)}, u32[]{:S(2)}) %collective-permute-start) | collective-permute-done | bytes 65568 | tf_op jit(solution)/shard_map/ppermute | solution.py:317
  9.0 0.4 %shard_map.81 = (f32[16,16,128]{2,1,0:T(8,128)S(1)}, bf16[16,16,128]{2,1,0:T(8,128)(2,1)S(1)}, bf16[16,16,128]{2,1,0:T(8,128)(2,1)S(1)}, bf16[16,16,128]{2,1,0:T(8,128)(2,1)S(1)}) custom-call(s32[1]{0:T(128)S(6)} %copy.8.crop_ref, bf16[16,16,128]{2,1,0:T(8,128)(2,1)S(1)} %collective-permute-done.refs_0_.refs_2_, ...), custom_call_target="tpu_custom_call" | custom-call | flops 1048576 | bytes 720900 | tf_op jit(solution)/shard_map/pallas_call | solution.py:289
  9.4 2.7 %collective-permute-start.3 = (bf16[16,16,128]{2,1,0:T(8,128)(2,1)S(1)}, bf16[16,16,128]{2,1,0:T(8,128)(2,1)S(1)}, u32[]{:S(2)}, u32[]{:S(2)}) collective-permute-start(bf16[16,16,128]{2,1,0:T(8,128)(2,1)S(1)} %get-tuple-element.25), channel_id=1, source_target_pairs={{0,8},{4,12},{8,0},{12,4},{1,9},{5,13},{9,1},{13,5},{2,10},{6,14},... | collective-permute-start | bytes 196616 | tf_op jit(solution)/shard_map/ppermute | solution.py:317
  12.1 1.4 %collective-permute-start.4 = (bf16[16,16,128]{2,1,0:T(8,128)(2,1)S(1)}, bf16[16,16,128]{2,1,0:T(8,128)(2,1)S(1)}, u32[]{:S(2)}, u32[]{:S(2)}) collective-permute-start(bf16[16,16,128]{2,1,0:T(8,128)(2,1)S(1)} %get-tuple-element.26), channel_id=1, source_target_pairs={{0,12},{4,8},{8,4},{12,0},{1,13},{5,9},{9,5},{13,1},{2,14},{6,10},... | collective-permute-start | bytes 196616 | tf_op jit(solution)/shard_map/ppermute | solution.py:317
  13.5 0.2 collective-permute-start.5
  13.7 3.3 %collective-permute-done.3.tile_ref = bf16[16,16,128]{2,1,0:T(8,128)(2,1)S(1)} collective-permute-done((bf16[16,16,128]{2,1,0:T(8,128)(2,1)S(1)}, bf16[16,16,128]{2,1,0:T(8,128)(2,1)S(1)}, u32[]{:S(2)}, u32[]{:S(2)}) %collective-permute-start.3) | collective-permute-done | bytes 65568 | tf_op jit(solution)/shard_map/ppermute | solution.py:317
  17.1 1.3 %collective-permute-done.4.refs_0_ = bf16[16,16,128]{2,1,0:T(8,128)(2,1)S(1)} collective-permute-done((bf16[16,16,128]{2,1,0:T(8,128)(2,1)S(1)}, bf16[16,16,128]{2,1,0:T(8,128)(2,1)S(1)}, u32[]{:S(2)}, u32[]{:S(2)}) %collective-permute-start.4) | collective-permute-done | bytes 65568 | tf_op jit(solution)/shard_map/ppermute | solution.py:317
  18.8 3.0 %collective-permute-start.7 = (bf16[16,16,128]{2,1,0:T(8,128)(2,1)S(1)}, bf16[16,16,128]{2,1,0:T(8,128)(2,1)S(1)}, u32[]{:S(2)}, u32[]{:S(2)}) collective-permute-start(bf16[16,16,128]{2,1,0:T(8,128)(2,1)S(1)} %get-tuple-element.33.refs_0_.grad_ref), channel_id=1, source_target_pairs={{0,12},{4,8},{8,4},{12,0},{1,13},{5,9},{9,5},{13,1},{2,14},{6,10},... | collective-permute-start | bytes 196616 | tf_op jit(solution)/shard_map/ppermute | solution.py:317
  22.1 1.2 %collective-permute-start.6 = (bf16[16,16,128]{2,1,0:T(8,128)(2,1)S(1)}, bf16[16,16,128]{2,1,0:T(8,128)(2,1)S(1)}, u32[]{:S(2)}, u32[]{:S(2)}) collective-permute-start(bf16[16,16,128]{2,1,0:T(8,128)(2,1)S(1)} %get-tuple-element.33.refs_0_.grad_ref), channel_id=1, source_target_pairs={{0,8},{4,12},{8,0},{12,4},{1,9},{5,13},{9,1},{13,5},{2,10},{6,14},... | collective-permute-start | bytes 196616 | tf_op jit(solution)/shard_map/ppermute | solution.py:317
  23.3 0.4 %shard_map.87 = (f32[8,256]{1,0:T(8,128)S(1)}, f32[256,256]{1,0:T(8,128)S(1)}) custom-call(f32[256,128]{1,0:T(8,128)S(1)} %get-tuple-element.35.normed_ref.refs_7_.refs_2_, bf16[128,640]{1,0:T(8,128)(2,1)S(1)} %copy-done), custom_call_target="tpu_custom_call" | custom-call | tf_op jit(solution)/shard_map/pallas_call | solution.py:289
  23.9 0.6 %copy-done.1 = bf16[128,128]{1,0:T(8,128)(2,1)S(1)} copy-done((bf16[128,128]{1,0:T(8,128)(2,1)S(1)}, bf16[128,128]{1,0:T(8,128)(2,1)}, u32[]{:S(2)}) %copy-start.1) | copy-done | bytes 32792
  24.5 0.8 %shard_map.84 = (bf16[16,16,128]{2,1,0:T(8,128)(2,1)}, f32[256,128]{1,0:T(8,128)S(1)}) custom-call(f32[256,128]{1,0:T(8,128)S(1)} %get-tuple-element.29.tri_normed_ref, f32[256,128]{1,0:T(8,128)S(1)} %get-tuple-element.30.open_ref, f32[256,128]{1,0:T(8,128)S(1)} %get-tuple-element.31.gate_factor_ref, bf16[128,640]{1,0:T(8,128)(2,1)S(1)} %copy-done, ...), custom_call_target="tpu_custom_call" | custom-call | flops 16777216 | bytes 786432 | tf_op jit(solution)/shard_map/pallas_call | solution.py:289
  25.7 0.7 %collective-permute-done.8.grad_ref.refs_1_ = bf16[16,16,128]{2,1,0:T(8,128)(2,1)S(1)} collective-permute-done((bf16[16,16,128]{2,1,0:T(8,128)(2,1)S(1)}, bf16[16,16,128]{2,1,0:T(8,128)(2,1)S(1)}, u32[]{:S(2)}, u32[]{:S(2)}) %collective-permute-start.8) | collective-permute-done | bytes 65568 | tf_op jit(solution)/shard_map/ppermute | solution.py:317
  26.6 0.7 %collective-permute-done.6.grad_ref.refs_2_ = bf16[16,16,128]{2,1,0:T(8,128)(2,1)S(1)} collective-permute-done((bf16[16,16,128]{2,1,0:T(8,128)(2,1)S(1)}, bf16[16,16,128]{2,1,0:T(8,128)(2,1)S(1)}, u32[]{:S(2)}, u32[]{:S(2)}) %collective-permute-start.6) | collective-permute-done | bytes 65568 | tf_op jit(solution)/shard_map/ppermute | solution.py:317
  27.2 0.3 shard_map.91
  27.5 2.0 %collective-permute-start.9 = (bf16[16,16,128]{2,1,0:T(8,128)(2,1)S(1)}, bf16[16,16,128]{2,1,0:T(8,128)(2,1)S(1)}, u32[]{:S(2)}, u32[]{:S(2)}) collective-permute-start(bf16[16,16,128]{2,1,0:T(8,128)(2,1)S(1)} %get-tuple-element.38), channel_id=1, source_target_pairs={{0,2},{1,3},{2,0},{3,1},{4,6},{5,7},{6,4},{7,5},{8,10},{9,11},{10,... | collective-permute-start | bytes 196616 | tf_op jit(solution)/shard_map/ppermute | solution.py:317
  29.5 0.2 collective-permute-start.11
  29.7 0.6 %shard_map.93.refs_5_ = f32[256,128]{1,0:T(8,128)S(1)} custom-call(f32[64,16,128]{2,1,0:T(8,128)S(1)} %shard_map.85.panel, bf16[16,16,128]{2,1,0:T(8,128)(2,1)S(1)} %collective-permute-done.7.grad_ref.refs_0_, bf16[16,16,128]{2,1,0:T(8,128)(2,1)S(1)} %collective-permute-done.8.grad_ref.refs_1_, ...), custom_call_target="tpu_custom_call" | custom-call | tf_op jit(solution)/shard_map/pallas_call | solution.py:289
  30.4 1.5 %collective-permute-done.9.tile_ref = bf16[16,16,128]{2,1,0:T(8,128)(2,1)S(1)} collective-permute-done((bf16[16,16,128]{2,1,0:T(8,128)(2,1)S(1)}, bf16[16,16,128]{2,1,0:T(8,128)(2,1)S(1)}, u32[]{:S(2)}, u32[]{:S(2)}) %collective-permute-start.9) | collective-permute-done | bytes 65568 | tf_op jit(solution)/shard_map/ppermute | solution.py:317
  31.9 1.4 %collective-permute-done.10.refs_0_ = bf16[16,16,128]{2,1,0:T(8,128)(2,1)S(1)} collective-permute-done((bf16[16,16,128]{2,1,0:T(8,128)(2,1)S(1)}, bf16[16,16,128]{2,1,0:T(8,128)(2,1)S(1)}, u32[]{:S(2)}, u32[]{:S(2)}) %collective-permute-start.10) | collective-permute-done | bytes 65568 | tf_op jit(solution)/shard_map/ppermute | solution.py:317
  33.2 0.8 %shard_map.94 = bf16[16,16,128]{2,1,0:T(8,128)(2,1)} custom-call(f32[16,16,128]{2,1,0:T(8,128)S(1)} %shard_map.92.base, bf16[16,16,128]{2,1,0:T(8,128)(2,1)S(1)} %collective-permute-done.10.refs_0_, bf16[16,16,128]{2,1,0:T(8,128)(2,1)S(1)} %collective-permute-done.11.refs_1_, f32[256,128]{1,0:T(8,128)S(1)} %get-tuple-element.35.normed_ref.refs_7_.refs_2_, ...), custom_call_target="tpu_custom_call" | custom-call | flops 16777216 | bytes 1679360 | tf_op jit(solution)/shard_map/pallas_call | solution.py:289
  (22 shorter events, 2.0 us)
Async XLA Ops:
  1.9 5.6 %collective-permute-start.2 = (bf16[16,16,128]{2,1,0:T(8,128)(2,1)S(1)}, bf16[16,16,128]{2,1,0:T(8,128)(2,1)S(1)}, u32[]{:S(2)}, u32[]{:S(2)}) collective-permute-start(bf16[16,16,128]{2,1,0:T(8,128)(2,1)S(1)} %shard_map.77.refs_0_), channel_id=1, source_target_pairs={{0,2},{1,3},{2,0},{3,1},{4,6},{5,7},{6,4},{7,5},{8,10},{9,11},{10,... | collective-permute-start | bytes 196616 | tf_op jit(solution)/shard_map/ppermute | solution.py:317
  4.9 4.1 %collective-permute-start = (bf16[16,16,128]{2,1,0:T(8,128)(2,1)S(1)}, bf16[16,16,128]{2,1,0:T(8,128)(2,1)S(1)}, u32[]{:S(2)}, u32[]{:S(2)}) collective-permute-start(bf16[16,16,128]{2,1,0:T(8,128)(2,1)S(1)} %shard_map.77.refs_0_), channel_id=1, source_target_pairs={{0,3},{1,2},{2,1},{3,0},{4,7},{5,6},{6,5},{7,4},{8,11},{9,10},{10,... | collective-permute-start | bytes 196616 | tf_op jit(solution)/shard_map/ppermute | solution.py:317
  4.9 4.1 %collective-permute-start.1 = (bf16[16,16,128]{2,1,0:T(8,128)(2,1)S(1)}, bf16[16,16,128]{2,1,0:T(8,128)(2,1)S(1)}, u32[]{:S(2)}, u32[]{:S(2)}) collective-permute-start(bf16[16,16,128]{2,1,0:T(8,128)(2,1)S(1)} %shard_map.77.refs_0_), channel_id=1, source_target_pairs={{0,1},{1,0},{2,3},{3,2},{4,5},{5,4},{6,7},{7,6},{8,9},{9,8},{10,11... | collective-permute-start | bytes 196616 | tf_op jit(solution)/shard_map/ppermute | solution.py:317
  9.4 7.6 %collective-permute-start.3 = (bf16[16,16,128]{2,1,0:T(8,128)(2,1)S(1)}, bf16[16,16,128]{2,1,0:T(8,128)(2,1)S(1)}, u32[]{:S(2)}, u32[]{:S(2)}) collective-permute-start(bf16[16,16,128]{2,1,0:T(8,128)(2,1)S(1)} %get-tuple-element.25), channel_id=1, source_target_pairs={{0,8},{4,12},{8,0},{12,4},{1,9},{5,13},{9,1},{13,5},{2,10},{6,14},... | collective-permute-start | bytes 196616 | tf_op jit(solution)/shard_map/ppermute | solution.py:317
  12.1 6.3 %collective-permute-start.4 = (bf16[16,16,128]{2,1,0:T(8,128)(2,1)S(1)}, bf16[16,16,128]{2,1,0:T(8,128)(2,1)S(1)}, u32[]{:S(2)}, u32[]{:S(2)}) collective-permute-start(bf16[16,16,128]{2,1,0:T(8,128)(2,1)S(1)} %get-tuple-element.26), channel_id=1, source_target_pairs={{0,12},{4,8},{8,4},{12,0},{1,13},{5,9},{9,5},{13,1},{2,14},{6,10},... | collective-permute-start | bytes 196616 | tf_op jit(solution)/shard_map/ppermute | solution.py:317
  13.5 5.1 %collective-permute-start.5 = (bf16[16,16,128]{2,1,0:T(8,128)(2,1)S(1)}, bf16[16,16,128]{2,1,0:T(8,128)(2,1)S(1)}, u32[]{:S(2)}, u32[]{:S(2)}) collective-permute-start(bf16[16,16,128]{2,1,0:T(8,128)(2,1)S(1)} %get-tuple-element.27), channel_id=1, source_target_pairs={{0,4},{4,0},{8,12},{12,8},{1,5},{5,1},{9,13},{13,9},{2,6},{6,2},{1... | collective-permute-start | bytes 196616 | tf_op jit(solution)/shard_map/ppermute | solution.py:317
  18.6 4.7 %copy-start = (bf16[128,640]{1,0:T(8,128)(2,1)S(1)}, bf16[128,640]{1,0:T(8,128)(2,1)}, u32[]{:S(2)}) copy-start(bf16[128,640]{1,0:T(8,128)(2,1)} %refs_8_.1) | copy-start | bytes 491524
  18.8 6.7 %collective-permute-start.7 = (bf16[16,16,128]{2,1,0:T(8,128)(2,1)S(1)}, bf16[16,16,128]{2,1,0:T(8,128)(2,1)S(1)}, u32[]{:S(2)}, u32[]{:S(2)}) collective-permute-start(bf16[16,16,128]{2,1,0:T(8,128)(2,1)S(1)} %get-tuple-element.33.refs_0_.grad_ref), channel_id=1, source_target_pairs={{0,12},{4,8},{8,4},{12,0},{1,13},{5,9},{9,5},{13,1},{2,14},{6,10},... | collective-permute-start | bytes 196616 | tf_op jit(solution)/shard_map/ppermute | solution.py:317
  21.9 4.5 %collective-permute-start.8 = (bf16[16,16,128]{2,1,0:T(8,128)(2,1)S(1)}, bf16[16,16,128]{2,1,0:T(8,128)(2,1)S(1)}, u32[]{:S(2)}, u32[]{:S(2)}) collective-permute-start(bf16[16,16,128]{2,1,0:T(8,128)(2,1)S(1)} %get-tuple-element.33.refs_0_.grad_ref), channel_id=1, source_target_pairs={{0,4},{4,0},{8,12},{12,8},{1,5},{5,1},{9,13},{13,9},{2,6},{6,2},{1... | collective-permute-start | bytes 196616 | tf_op jit(solution)/shard_map/ppermute | solution.py:317
  22.1 5.2 %collective-permute-start.6 = (bf16[16,16,128]{2,1,0:T(8,128)(2,1)S(1)}, bf16[16,16,128]{2,1,0:T(8,128)(2,1)S(1)}, u32[]{:S(2)}, u32[]{:S(2)}) collective-permute-start(bf16[16,16,128]{2,1,0:T(8,128)(2,1)S(1)} %get-tuple-element.33.refs_0_.grad_ref), channel_id=1, source_target_pairs={{0,8},{4,12},{8,0},{12,4},{1,9},{5,13},{9,1},{13,5},{2,10},{6,14},... | collective-permute-start | bytes 196616 | tf_op jit(solution)/shard_map/ppermute | solution.py:317
  23.8 0.8 %copy-start.1 = (bf16[128,128]{1,0:T(8,128)(2,1)S(1)}, bf16[128,128]{1,0:T(8,128)(2,1)}, u32[]{:S(2)}) copy-start(bf16[128,128]{1,0:T(8,128)(2,1)} %out_weight_ref.1) | copy-start | bytes 98308
  27.5 4.3 %collective-permute-start.9 = (bf16[16,16,128]{2,1,0:T(8,128)(2,1)S(1)}, bf16[16,16,128]{2,1,0:T(8,128)(2,1)S(1)}, u32[]{:S(2)}, u32[]{:S(2)}) collective-permute-start(bf16[16,16,128]{2,1,0:T(8,128)(2,1)S(1)} %get-tuple-element.38), channel_id=1, source_target_pairs={{0,2},{1,3},{2,0},{3,1},{4,6},{5,7},{6,4},{7,5},{8,10},{9,11},{10,... | collective-permute-start | bytes 196616 | tf_op jit(solution)/shard_map/ppermute | solution.py:317
  29.5 3.8 %collective-permute-start.10 = (bf16[16,16,128]{2,1,0:T(8,128)(2,1)S(1)}, bf16[16,16,128]{2,1,0:T(8,128)(2,1)S(1)}, u32[]{:S(2)}, u32[]{:S(2)}) collective-permute-start(bf16[16,16,128]{2,1,0:T(8,128)(2,1)S(1)} %get-tuple-element.39), channel_id=1, source_target_pairs={{0,3},{1,2},{2,1},{3,0},{4,7},{5,6},{6,5},{7,4},{8,11},{9,10},{10,... | collective-permute-start | bytes 196616 | tf_op jit(solution)/shard_map/ppermute | solution.py:317
  29.5 3.8 %collective-permute-start.11 = (bf16[16,16,128]{2,1,0:T(8,128)(2,1)S(1)}, bf16[16,16,128]{2,1,0:T(8,128)(2,1)S(1)}, u32[]{:S(2)}, u32[]{:S(2)}) collective-permute-start(bf16[16,16,128]{2,1,0:T(8,128)(2,1)S(1)} %get-tuple-element.40), channel_id=1, source_target_pairs={{0,1},{1,0},{2,3},{3,2},{4,5},{5,4},{6,7},{7,6},{8,9},{9,8},{10,11... | collective-permute-start | bytes 196616 | tf_op jit(solution)/shard_map/ppermute | solution.py:317

commit v24 on v23

--- a/solution.py
+++ b/solution.py
@@ -235,13 +235,14 @@
     out[...] = normalize_back(normed_ref[...], scale_ref[...], share)
 
 
-def slopes_kernel(normed_ref, weights_ref, mean_ref, slope_ref):
+def slopes_kernel(normed_ref, weights_ref, mean_ref, slope_ref, turned_ref):
     channels = normed_ref.shape[1]
     weights = weights_ref[:, : 2 * channels].astype(f32)
     mean = jnp.sum(weights, axis=0, keepdims=True) * (1.0 / channels)
     mean_ref[...] = jnp.broadcast_to(mean, mean_ref.shape)
     slope = jnp.dot(normed_ref[...], weights, precision=lax.Precision.HIGHEST, preferred_element_type=f32)
     slope_ref[...] = slope * (1.0 / channels)
+    turned_ref[...] = weights.T.astype(bf16)
 
 
 def add_kernel(base, tile_ref, out):
@@ -260,7 +261,7 @@
 
 
 def back_kernel(base, *refs):
-    *tiles, normed_ref, scale_ref, factor_ref, done_ref, mean_ref, slope_ref, weights_ref, out = refs
+    *tiles, normed_ref, scale_ref, factor_ref, done_ref, mean_ref, slope_ref, turned_ref, out = refs
     size, _, channels = out.shape
     pairs = size * size
     left = base[...]
@@ -268,7 +269,7 @@
         left = left + ref[...].astype(f32)
     left = left.reshape(pairs, channels)
     grads = jnp.concatenate([(left * factor_ref[block]).astype(bf16) for block in (0, 1)], axis=1)
-    normed_grad = dot_t(grads, weights_ref[:, : 2 * channels])
+    normed_grad = dot(grads, turned_ref[...])
     wide_grads = grads.astype(f32)
     average = jnp.sum(wide_grads * mean_ref[0:1, :], axis=-1, keepdims=True)
     project = jnp.sum(wide_grads * slope_ref[...], axis=-1, keepdims=True)
@@ -375,8 +376,13 @@
         update_kernel, (tile, flat), tri_normed, out_open, gate_factor, in_weights, out_weight,
         flops=4 * pairs * channels * channels,
     )
-    means, slopes = call(
-        slopes_kernel, (jax.ShapeDtypeStruct((8, 2 * channels), f32), jax.ShapeDtypeStruct((pairs, 2 * channels), f32)),
+    means, slopes, turned = call(
+        slopes_kernel,
+        (
+            jax.ShapeDtypeStruct((8, 2 * channels), f32),
+            jax.ShapeDtypeStruct((pairs, 2 * channels), f32),
+            jax.ShapeDtypeStruct((2 * channels, channels), bf16),
+        ),
         normed, in_weights,
     )
     (right_grad,) = call(functools.partial(right_grad_kernel, [0]), (wide,), left_panel, tri_grad)
@@ -405,7 +411,7 @@
         scratch=[pltpu.VMEM(wide.shape, f32)],
     )
     (pair_grad,) = call(
-        back_kernel, (tile,), total, *last, normed, scale, factors, done, means, slopes, in_weights,
+        back_kernel, (tile,), total, *last, normed, scale, factors, done, means, slopes, turned,
         flops=2 * pairs * channels * 2 * channels,
     )
     return (update, pair_grad)

time: 34.3 us -> 34.3 us (level)
  no operation moved by 1% of the time
where the time goes in v24:
time: 34.3 us; the launch traced here: 34.1 us
  starting transfers between devices  14.1 us (41%)
  waiting for transfers between devices  10.4 us (30%)
  Pallas kernels  7.5 us (22%)
  between operations  1.41 us (4%)
  local copies, waits for them, and re-layouts  0.6 us (2%)
    ppermute x12, starting transfers between devices, swap(): return lax.ppermute(values, axis, [(a, a ^ step) for a in range(n)])  14.1 us
    ppermute x12, waiting for transfers between devices, swap(): return lax.ppermute(values, axis, [(a, a ^ step) for a in range(n)])  10.4 us
    pallas_call x18, Pallas kernels, call(): pl.pallas_call(kernel, out_shape=tuple(outs), in_specs=specs, out_specs=(...  7.5 us
  transfers between devices with their start and end apart: 12, of which 8 were waited for; matrix products, arithmetic and copies ran while one was open for 0% of the time, Pallas kernels for 13%

profile of v24, /device:TPU:0, one launch (start us, length us, event | category | flops | bytes accessed | tf_op | source)
XLA Modules:
  0.0 34.1 jit_solution(3310142792077978567)
XLA Ops:
  0.6 1.3 %shard_map.77.refs_0_ = bf16[16,16,128]{2,1,0:T(8,128)(2,1)S(1)} custom-call(bf16[16,16,128]{2,1,0:T(8,128)(2,1)} %acts_in.3, s32[16,16]{1,0:T(8,128)} %mask_in.3, bf16[128,640]{1,0:T(8,128)(2,1)} %refs_5_.1), custom_call_target="tpu_custom_call" | custom-call | flops 16777216 | bytes 295936 | tf_op jit(solution)/shard_map/pallas_call | solution.py:290
  1.9 3.0 %collective-permute-start.2 = (bf16[16,16,128]{2,1,0:T(8,128)(2,1)S(1)}, bf16[16,16,128]{2,1,0:T(8,128)(2,1)S(1)}, u32[]{:S(2)}, u32[]{:S(2)}) collective-permute-start(bf16[16,16,128]{2,1,0:T(8,128)(2,1)S(1)} %shard_map.77.refs_0_), channel_id=1, source_target_pairs={{0,2},{1,3},{2,0},{3,1},{4,6},{5,7},{6,4},{7,5},{8,10},{9,11},{10,... | collective-permute-start | bytes 196616 | tf_op jit(solution)/shard_map/ppermute | solution.py:318
  5.8 1.6 %shard_map.78 = (f32[16,16,128]{2,1,0:T(8,128)S(1)}, f32[256,128]{1,0:T(8,128)S(1)}, f32[256,128]{1,0:T(8,128)S(1)}, f32[4,256,128]{2,1,0:T(8,128)S(1)}, f32[256...) custom-call(bf16[16,16,128]{2,1,0:T(8,128)(2,1)} %acts_in.3, s32[16,16]{1,0:T(8,128)} %mask_in.3, ...), custom_call_target="tpu_custom_call" | custom-call | flops 50331648 | bytes 1639428 | tf_op jit(solution)/shard_map/pallas_call | solution.py:290
  7.7 1.4 %collective-permute-done.refs_0_.refs_2_ = bf16[16,16,128]{2,1,0:T(8,128)(2,1)S(1)} collective-permute-done((bf16[16,16,128]{2,1,0:T(8,128)(2,1)S(1)}, bf16[16,16,128]{2,1,0:T(8,128)(2,1)S(1)}, u32[]{:S(2)}, u32[]{:S(2)}) %collective-permute-start) | collective-permute-done | bytes 65568 | tf_op jit(solution)/shard_map/ppermute | solution.py:318
  9.0 0.4 %shard_map.81 = (f32[16,16,128]{2,1,0:T(8,128)S(1)}, bf16[16,16,128]{2,1,0:T(8,128)(2,1)S(1)}, bf16[16,16,128]{2,1,0:T(8,128)(2,1)S(1)}, bf16[16,16,128]{2,1,0:T(8,128)(2,1)S(1)}) custom-call(s32[1]{0:T(128)S(6)} %copy.8.crop_ref, bf16[16,16,128]{2,1,0:T(8,128)(2,1)S(1)} %collective-permute-done.refs_0_.refs_2_, ...), custom_call_target="tpu_custom_call" | custom-call | flops 1048576 | bytes 720900 | tf_op jit(solution)/shard_map/pallas_call | solution.py:290
  9.4 2.7 %collective-permute-start.3 = (bf16[16,16,128]{2,1,0:T(8,128)(2,1)S(1)}, bf16[16,16,128]{2,1,0:T(8,128)(2,1)S(1)}, u32[]{:S(2)}, u32[]{:S(2)}) collective-permute-start(bf16[16,16,128]{2,1,0:T(8,128)(2,1)S(1)} %get-tuple-element.26), channel_id=1, source_target_pairs={{0,8},{4,12},{8,0},{12,4},{1,9},{5,13},{9,1},{13,5},{2,10},{6,14},... | collective-permute-start | bytes 196616 | tf_op jit(solution)/shard_map/ppermute | solution.py:318
  12.1 1.4 %collective-permute-start.4 = (bf16[16,16,128]{2,1,0:T(8,128)(2,1)S(1)}, bf16[16,16,128]{2,1,0:T(8,128)(2,1)S(1)}, u32[]{:S(2)}, u32[]{:S(2)}) collective-permute-start(bf16[16,16,128]{2,1,0:T(8,128)(2,1)S(1)} %get-tuple-element.27), channel_id=1, source_target_pairs={{0,12},{4,8},{8,4},{12,0},{1,13},{5,9},{9,5},{13,1},{2,14},{6,10},... | collective-permute-start | bytes 196616 | tf_op jit(solution)/shard_map/ppermute | solution.py:318
  13.5 0.2 collective-permute-start.5
  13.7 3.3 %collective-permute-done.3.tile_ref = bf16[16,16,128]{2,1,0:T(8,128)(2,1)S(1)} collective-permute-done((bf16[16,16,128]{2,1,0:T(8,128)(2,1)S(1)}, bf16[16,16,128]{2,1,0:T(8,128)(2,1)S(1)}, u32[]{:S(2)}, u32[]{:S(2)}) %collective-permute-start.3) | collective-permute-done | bytes 65568 | tf_op jit(solution)/shard_map/ppermute | solution.py:318
  17.1 1.3 %collective-permute-done.4.refs_0_ = bf16[16,16,128]{2,1,0:T(8,128)(2,1)S(1)} collective-permute-done((bf16[16,16,128]{2,1,0:T(8,128)(2,1)S(1)}, bf16[16,16,128]{2,1,0:T(8,128)(2,1)S(1)}, u32[]{:S(2)}, u32[]{:S(2)}) %collective-permute-start.4) | collective-permute-done | bytes 65568 | tf_op jit(solution)/shard_map/ppermute | solution.py:318
  18.8 3.0 %collective-permute-start.7 = (bf16[16,16,128]{2,1,0:T(8,128)(2,1)S(1)}, bf16[16,16,128]{2,1,0:T(8,128)(2,1)S(1)}, u32[]{:S(2)}, u32[]{:S(2)}) collective-permute-start(bf16[16,16,128]{2,1,0:T(8,128)(2,1)S(1)} %get-tuple-element.34.refs_0_.grad_ref), channel_id=1, source_target_pairs={{0,12},{4,8},{8,4},{12,0},{1,13},{5,9},{9,5},{13,1},{2,14},{6,10},... | collective-permute-start | bytes 196616 | tf_op jit(solution)/shard_map/ppermute | solution.py:318
  22.1 1.2 %collective-permute-start.6 = (bf16[16,16,128]{2,1,0:T(8,128)(2,1)S(1)}, bf16[16,16,128]{2,1,0:T(8,128)(2,1)S(1)}, u32[]{:S(2)}, u32[]{:S(2)}) collective-permute-start(bf16[16,16,128]{2,1,0:T(8,128)(2,1)S(1)} %get-tuple-element.34.refs_0_.grad_ref), channel_id=1, source_target_pairs={{0,8},{4,12},{8,0},{12,4},{1,9},{5,13},{9,1},{13,5},{2,10},{6,14},... | collective-permute-start | bytes 196616 | tf_op jit(solution)/shard_map/ppermute | solution.py:318
  23.3 0.4 %shard_map.87 = (f32[8,256]{1,0:T(8,128)S(1)}, f32[256,256]{1,0:T(8,128)S(1)}, bf16[256,128]{1,0:T(8,128)(2,1)S(1)}) custom-call(f32[256,128]{1,0:T(8,128)S(1)} %get-tuple-element.36.normed_ref.refs_7_.refs_2_, bf16[128,640]{1,0:T(8,128)(2,1)S(1)} %copy-done), custom_call_target="tpu_custom_call" | custom-call | tf_op jit(solution)/shard_map/pallas_call | solution.py:290
  23.9 0.6 %copy-done.1 = bf16[128,128]{1,0:T(8,128)(2,1)S(1)} copy-done((bf16[128,128]{1,0:T(8,128)(2,1)S(1)}, bf16[128,128]{1,0:T(8,128)(2,1)}, u32[]{:S(2)}) %copy-start.1) | copy-done | bytes 32792
  24.5 0.8 %shard_map.84 = (bf16[16,16,128]{2,1,0:T(8,128)(2,1)}, f32[256,128]{1,0:T(8,128)S(1)}) custom-call(f32[256,128]{1,0:T(8,128)S(1)} %get-tuple-element.30.tri_normed_ref, f32[256,128]{1,0:T(8,128)S(1)} %get-tuple-element.31.open_ref, f32[256,128]{1,0:T(8,128)S(1)} %get-tuple-element.32.gate_factor_ref, bf16[128,640]{1,0:T(8,128)(2,1)S(1)} %copy-done, ...), custom_call_target="tpu_custom_call" | custom-call | flops 16777216 | bytes 786432 | tf_op jit(solution)/shard_map/pallas_call | solution.py:290
  25.7 0.7 %collective-permute-done.8.grad_ref.refs_1_ = bf16[16,16,128]{2,1,0:T(8,128)(2,1)S(1)} collective-permute-done((bf16[16,16,128]{2,1,0:T(8,128)(2,1)S(1)}, bf16[16,16,128]{2,1,0:T(8,128)(2,1)S(1)}, u32[]{:S(2)}, u32[]{:S(2)}) %collective-permute-start.8) | collective-permute-done | bytes 65568 | tf_op jit(solution)/shard_map/ppermute | solution.py:318
  26.6 0.7 %collective-permute-done.6.grad_ref.refs_2_ = bf16[16,16,128]{2,1,0:T(8,128)(2,1)S(1)} collective-permute-done((bf16[16,16,128]{2,1,0:T(8,128)(2,1)S(1)}, bf16[16,16,128]{2,1,0:T(8,128)(2,1)S(1)}, u32[]{:S(2)}, u32[]{:S(2)}) %collective-permute-start.6) | collective-permute-done | bytes 65568 | tf_op jit(solution)/shard_map/ppermute | solution.py:318
  27.2 0.3 shard_map.91
  27.5 2.0 %collective-permute-start.9 = (bf16[16,16,128]{2,1,0:T(8,128)(2,1)S(1)}, bf16[16,16,128]{2,1,0:T(8,128)(2,1)S(1)}, u32[]{:S(2)}, u32[]{:S(2)}) collective-permute-start(bf16[16,16,128]{2,1,0:T(8,128)(2,1)S(1)} %get-tuple-element.39), channel_id=1, source_target_pairs={{0,2},{1,3},{2,0},{3,1},{4,6},{5,7},{6,4},{7,5},{8,10},{9,11},{10,... | collective-permute-start | bytes 196616 | tf_op jit(solution)/shard_map/ppermute | solution.py:318
  29.5 0.2 collective-permute-start.11
  29.7 0.6 %shard_map.93.refs_5_ = f32[256,128]{1,0:T(8,128)S(1)} custom-call(f32[64,16,128]{2,1,0:T(8,128)S(1)} %shard_map.85.panel, bf16[16,16,128]{2,1,0:T(8,128)(2,1)S(1)} %collective-permute-done.7.grad_ref.refs_0_, bf16[16,16,128]{2,1,0:T(8,128)(2,1)S(1)} %collective-permute-done.8.grad_ref.refs_1_, ...), custom_call_target="tpu_custom_call" | custom-call | tf_op jit(solution)/shard_map/pallas_call | solution.py:290
  30.4 1.5 %collective-permute-done.9.tile_ref = bf16[16,16,128]{2,1,0:T(8,128)(2,1)S(1)} collective-permute-done((bf16[16,16,128]{2,1,0:T(8,128)(2,1)S(1)}, bf16[16,16,128]{2,1,0:T(8,128)(2,1)S(1)}, u32[]{:S(2)}, u32[]{:S(2)}) %collective-permute-start.9) | collective-permute-done | bytes 65568 | tf_op jit(solution)/shard_map/ppermute | solution.py:318
  31.9 1.4 %collective-permute-done.10.refs_0_ = bf16[16,16,128]{2,1,0:T(8,128)(2,1)S(1)} collective-permute-done((bf16[16,16,128]{2,1,0:T(8,128)(2,1)S(1)}, bf16[16,16,128]{2,1,0:T(8,128)(2,1)S(1)}, u32[]{:S(2)}, u32[]{:S(2)}) %collective-permute-start.10) | collective-permute-done | bytes 65568 | tf_op jit(solution)/shard_map/ppermute | solution.py:318
  33.2 0.8 %shard_map.94 = bf16[16,16,128]{2,1,0:T(8,128)(2,1)} custom-call(f32[16,16,128]{2,1,0:T(8,128)S(1)} %shard_map.92.base, bf16[16,16,128]{2,1,0:T(8,128)(2,1)S(1)} %collective-permute-done.10.refs_0_, bf16[16,16,128]{2,1,0:T(8,128)(2,1)S(1)} %collective-permute-done.11.refs_1_, f32[256,128]{1,0:T(8,128)S(1)} %get-tuple-element.36.normed_ref.refs_7_.refs_2_, ...), custom_call_target="tpu_custom_call" | custom-call | flops 16777216 | bytes 1581056 | tf_op jit(solution)/shard_map/pallas_call | solution.py:290
  (22 shorter events, 2.0 us)
Async XLA Ops:
  1.9 5.6 %collective-permute-start.2 = (bf16[16,16,128]{2,1,0:T(8,128)(2,1)S(1)}, bf16[16,16,128]{2,1,0:T(8,128)(2,1)S(1)}, u32[]{:S(2)}, u32[]{:S(2)}) collective-permute-start(bf16[16,16,128]{2,1,0:T(8,128)(2,1)S(1)} %shard_map.77.refs_0_), channel_id=1, source_target_pairs={{0,2},{1,3},{2,0},{3,1},{4,6},{5,7},{6,4},{7,5},{8,10},{9,11},{10,... | collective-permute-start | bytes 196616 | tf_op jit(solution)/shard_map/ppermute | solution.py:318
  4.9 4.1 %collective-permute-start = (bf16[16,16,128]{2,1,0:T(8,128)(2,1)S(1)}, bf16[16,16,128]{2,1,0:T(8,128)(2,1)S(1)}, u32[]{:S(2)}, u32[]{:S(2)}) collective-permute-start(bf16[16,16,128]{2,1,0:T(8,128)(2,1)S(1)} %shard_map.77.refs_0_), channel_id=1, source_target_pairs={{0,3},{1,2},{2,1},{3,0},{4,7},{5,6},{6,5},{7,4},{8,11},{9,10},{10,... | collective-permute-start | bytes 196616 | tf_op jit(solution)/shard_map/ppermute | solution.py:318
  4.9 4.1 %collective-permute-start.1 = (bf16[16,16,128]{2,1,0:T(8,128)(2,1)S(1)}, bf16[16,16,128]{2,1,0:T(8,128)(2,1)S(1)}, u32[]{:S(2)}, u32[]{:S(2)}) collective-permute-start(bf16[16,16,128]{2,1,0:T(8,128)(2,1)S(1)} %shard_map.77.refs_0_), channel_id=1, source_target_pairs={{0,1},{1,0},{2,3},{3,2},{4,5},{5,4},{6,7},{7,6},{8,9},{9,8},{10,11... | collective-permute-start | bytes 196616 | tf_op jit(solution)/shard_map/ppermute | solution.py:318
  9.4 7.6 %collective-permute-start.3 = (bf16[16,16,128]{2,1,0:T(8,128)(2,1)S(1)}, bf16[16,16,128]{2,1,0:T(8,128)(2,1)S(1)}, u32[]{:S(2)}, u32[]{:S(2)}) collective-permute-start(bf16[16,16,128]{2,1,0:T(8,128)(2,1)S(1)} %get-tuple-element.26), channel_id=1, source_target_pairs={{0,8},{4,12},{8,0},{12,4},{1,9},{5,13},{9,1},{13,5},{2,10},{6,14},... | collective-permute-start | bytes 196616 | tf_op jit(solution)/shard_map/ppermute | solution.py:318
  12.1 6.3 %collective-permute-start.4 = (bf16[16,16,128]{2,1,0:T(8,128)(2,1)S(1)}, bf16[16,16,128]{2,1,0:T(8,128)(2,1)S(1)}, u32[]{:S(2)}, u32[]{:S(2)}) collective-permute-start(bf16[16,16,128]{2,1,0:T(8,128)(2,1)S(1)} %get-tuple-element.27), channel_id=1, source_target_pairs={{0,12},{4,8},{8,4},{12,0},{1,13},{5,9},{9,5},{13,1},{2,14},{6,10},... | collective-permute-start | bytes 196616 | tf_op jit(solution)/shard_map/ppermute | solution.py:318
  13.5 5.1 %collective-permute-start.5 = (bf16[16,16,128]{2,1,0:T(8,128)(2,1)S(1)}, bf16[16,16,128]{2,1,0:T(8,128)(2,1)S(1)}, u32[]{:S(2)}, u32[]{:S(2)}) collective-permute-start(bf16[16,16,128]{2,1,0:T(8,128)(2,1)S(1)} %get-tuple-element.28), channel_id=1, source_target_pairs={{0,4},{4,0},{8,12},{12,8},{1,5},{5,1},{9,13},{13,9},{2,6},{6,2},{1... | collective-permute-start | bytes 196616 | tf_op jit(solution)/shard_map/ppermute | solution.py:318
  18.6 4.7 %copy-start = (bf16[128,640]{1,0:T(8,128)(2,1)S(1)}, bf16[128,640]{1,0:T(8,128)(2,1)}, u32[]{:S(2)}) copy-start(bf16[128,640]{1,0:T(8,128)(2,1)} %refs_5_.1) | copy-start | bytes 491524
  18.8 6.7 %collective-permute-start.7 = (bf16[16,16,128]{2,1,0:T(8,128)(2,1)S(1)}, bf16[16,16,128]{2,1,0:T(8,128)(2,1)S(1)}, u32[]{:S(2)}, u32[]{:S(2)}) collective-permute-start(bf16[16,16,128]{2,1,0:T(8,128)(2,1)S(1)} %get-tuple-element.34.refs_0_.grad_ref), channel_id=1, source_target_pairs={{0,12},{4,8},{8,4},{12,0},{1,13},{5,9},{9,5},{13,1},{2,14},{6,10},... | collective-permute-start | bytes 196616 | tf_op jit(solution)/shard_map/ppermute | solution.py:318
  21.9 4.5 %collective-permute-start.8 = (bf16[16,16,128]{2,1,0:T(8,128)(2,1)S(1)}, bf16[16,16,128]{2,1,0:T(8,128)(2,1)S(1)}, u32[]{:S(2)}, u32[]{:S(2)}) collective-permute-start(bf16[16,16,128]{2,1,0:T(8,128)(2,1)S(1)} %get-tuple-element.34.refs_0_.grad_ref), channel_id=1, source_target_pairs={{0,4},{4,0},{8,12},{12,8},{1,5},{5,1},{9,13},{13,9},{2,6},{6,2},{1... | collective-permute-start | bytes 196616 | tf_op jit(solution)/shard_map/ppermute | solution.py:318
  22.1 5.2 %collective-permute-start.6 = (bf16[16,16,128]{2,1,0:T(8,128)(2,1)S(1)}, bf16[16,16,128]{2,1,0:T(8,128)(2,1)S(1)}, u32[]{:S(2)}, u32[]{:S(2)}) collective-permute-start(bf16[16,16,128]{2,1,0:T(8,128)(2,1)S(1)} %get-tuple-element.34.refs_0_.grad_ref), channel_id=1, source_target_pairs={{0,8},{4,12},{8,0},{12,4},{1,9},{5,13},{9,1},{13,5},{2,10},{6,14},... | collective-permute-start | bytes 196616 | tf_op jit(solution)/shard_map/ppermute | solution.py:318
  23.8 0.8 %copy-start.1 = (bf16[128,128]{1,0:T(8,128)(2,1)S(1)}, bf16[128,128]{1,0:T(8,128)(2,1)}, u32[]{:S(2)}) copy-start(bf16[128,128]{1,0:T(8,128)(2,1)} %out_weight_ref.1) | copy-start | bytes 98308
  27.5 4.3 %collective-permute-start.9 = (bf16[16,16,128]{2,1,0:T(8,128)(2,1)S(1)}, bf16[16,16,128]{2,1,0:T(8,128)(2,1)S(1)}, u32[]{:S(2)}, u32[]{:S(2)}) collective-permute-start(bf16[16,16,128]{2,1,0:T(8,128)(2,1)S(1)} %get-tuple-element.39), channel_id=1, source_target_pairs={{0,2},{1,3},{2,0},{3,1},{4,6},{5,7},{6,4},{7,5},{8,10},{9,11},{10,... | collective-permute-start | bytes 196616 | tf_op jit(solution)/shard_map/ppermute | solution.py:318
  29.5 3.8 %collective-permute-start.10 = (bf16[16,16,128]{2,1,0:T(8,128)(2,1)S(1)}, bf16[16,16,128]{2,1,0:T(8,128)(2,1)S(1)}, u32[]{:S(2)}, u32[]{:S(2)}) collective-permute-start(bf16[16,16,128]{2,1,0:T(8,128)(2,1)S(1)} %get-tuple-element.40), channel_id=1, source_target_pairs={{0,3},{1,2},{2,1},{3,0},{4,7},{5,6},{6,5},{7,4},{8,11},{9,10},{10,... | collective-permute-start | bytes 196616 | tf_op jit(solution)/shard_map/ppermute | solution.py:318
  29.5 3.8 %collective-permute-start.11 = (bf16[16,16,128]{2,1,0:T(8,128)(2,1)S(1)}, bf16[16,16,128]{2,1,0:T(8,128)(2,1)S(1)}, u32[]{:S(2)}, u32[]{:S(2)}) collective-permute-start(bf16[16,16,128]{2,1,0:T(8,128)(2,1)S(1)} %get-tuple-element.41), channel_id=1, source_target_pairs={{0,1},{1,0},{2,3},{3,2},{4,5},{5,4},{6,7},{7,6},{8,9},{9,8},{10,11... | collective-permute-start | bytes 196616 | tf_op jit(solution)/shard_map/ppermute | solution.py:318

commit v25 on v23

--- a/solution.py
+++ b/solution.py
@@ -387,15 +387,16 @@
             scratch=[pltpu.VMEM((pairs, channels), f32)], flops=work,
         )
         terms += before
+    last_steps = list(range(n - 1, 0, -1))
     total, *terms = call(
-        functools.partial(last_terms_kernel, [0] + gather_steps[:-1], gather_steps[-1], [0] + steps),
+        functools.partial(last_terms_kernel, [0] + gather_steps[:-1], gather_steps[-1], [0] + last_steps),
         (wide,) + (tile,) * (n - 1), grads[-1], right, *terms, flops=work,
         scratch=[pltpu.VMEM(tile.shape, bf16), pltpu.VMEM((pairs, channels), f32)],
     )
     last = []
-    for step, term in zip(steps, terms):
+    for step, term in zip(last_steps, terms):
         term = swap(term, "col", step)
-        if step in steps[-2:]:
+        if step in last_steps[-2:]:
             last.append(term)
         else:
             (total,) = call(add_kernel, (wide,), total, term, flops=wait)

time: 34.3 us -> 34.2 us (level)
  no operation moved by 1% of the time
where the time goes in v25:
time: 34.2 us; the launch traced here: 34 us
  starting transfers between devices  14 us (41%)
  waiting for transfers between devices  10.5 us (31%)
  Pallas kernels  7.5 us (22%)
  between operations  1.41 us (4%)
  local copies, waits for them, and re-layouts  0.6 us (2%)
    ppermute x12, starting transfers between devices, swap(): return lax.ppermute(values, axis, [(a, a ^ step) for a in range(n)])  14 us
    ppermute x12, waiting for transfers between devices, swap(): return lax.ppermute(values, axis, [(a, a ^ step) for a in range(n)])  10.5 us
    pallas_call x18, Pallas kernels, call(): pl.pallas_call(kernel, out_shape=tuple(outs), in_specs=specs, out_specs=(...  7.5 us
  transfers between devices with their start and end apart: 12, of which 8 were waited for; matrix products, arithmetic and copies ran while one was open for 0% of the time, Pallas kernels for 13%

profile of v25, /device:TPU:0, one launch (start us, length us, event | category | flops | bytes accessed | tf_op | source)
XLA Modules:
  0.0 34.0 jit_solution(4835351752356874572)
XLA Ops:
  0.6 1.3 %shard_map.77.refs_0_ = bf16[16,16,128]{2,1,0:T(8,128)(2,1)S(1)} custom-call(bf16[16,16,128]{2,1,0:T(8,128)(2,1)} %acts_in.3, s32[16,16]{1,0:T(8,128)} %mask_in.3, bf16[128,640]{1,0:T(8,128)(2,1)} %refs_8_.1), custom_call_target="tpu_custom_call" | custom-call | flops 16777216 | bytes 295936 | tf_op jit(solution)/shard_map/pallas_call | solution.py:289
  1.9 3.0 %collective-permute-start.2 = (bf16[16,16,128]{2,1,0:T(8,128)(2,1)S(1)}, bf16[16,16,128]{2,1,0:T(8,128)(2,1)S(1)}, u32[]{:S(2)}, u32[]{:S(2)}) collective-permute-start(bf16[16,16,128]{2,1,0:T(8,128)(2,1)S(1)} %shard_map.77.refs_0_), channel_id=1, source_target_pairs={{0,2},{1,3},{2,0},{3,1},{4,6},{5,7},{6,4},{7,5},{8,10},{9,11},{10,... | collective-permute-start | bytes 196616 | tf_op jit(solution)/shard_map/ppermute | solution.py:317
  5.8 1.6 %shard_map.78 = (f32[16,16,128]{2,1,0:T(8,128)S(1)}, f32[256,128]{1,0:T(8,128)S(1)}, f32[256,128]{1,0:T(8,128)S(1)}, f32[4,256,128]{2,1,0:T(8,128)S(1)}, f32[256...) custom-call(bf16[16,16,128]{2,1,0:T(8,128)(2,1)} %acts_in.3, s32[16,16]{1,0:T(8,128)} %mask_in.3, ...), custom_call_target="tpu_custom_call" | custom-call | flops 50331648 | bytes 1639428 | tf_op jit(solution)/shard_map/pallas_call | solution.py:289
  7.7 1.4 %collective-permute-done.refs_0_.refs_2_ = bf16[16,16,128]{2,1,0:T(8,128)(2,1)S(1)} collective-permute-done((bf16[16,16,128]{2,1,0:T(8,128)(2,1)S(1)}, bf16[16,16,128]{2,1,0:T(8,128)(2,1)S(1)}, u32[]{:S(2)}, u32[]{:S(2)}) %collective-permute-start) | collective-permute-done | bytes 65568 | tf_op jit(solution)/shard_map/ppermute | solution.py:317
  9.0 0.4 %shard_map.81 = (f32[16,16,128]{2,1,0:T(8,128)S(1)}, bf16[16,16,128]{2,1,0:T(8,128)(2,1)S(1)}, bf16[16,16,128]{2,1,0:T(8,128)(2,1)S(1)}, bf16[16,16,128]{2,1,0:T(8,128)(2,1)S(1)}) custom-call(s32[1]{0:T(128)S(6)} %copy.8.crop_ref, bf16[16,16,128]{2,1,0:T(8,128)(2,1)S(1)} %collective-permute-done.refs_0_.refs_2_, ...), custom_call_target="tpu_custom_call" | custom-call | flops 1048576 | bytes 720900 | tf_op jit(solution)/shard_map/pallas_call | solution.py:289
  9.4 2.7 %collective-permute-start.3 = (bf16[16,16,128]{2,1,0:T(8,128)(2,1)S(1)}, bf16[16,16,128]{2,1,0:T(8,128)(2,1)S(1)}, u32[]{:S(2)}, u32[]{:S(2)}) collective-permute-start(bf16[16,16,128]{2,1,0:T(8,128)(2,1)S(1)} %get-tuple-element.25), channel_id=1, source_target_pairs={{0,8},{4,12},{8,0},{12,4},{1,9},{5,13},{9,1},{13,5},{2,10},{6,14},... | collective-permute-start | bytes 196616 | tf_op jit(solution)/shard_map/ppermute | solution.py:317
  12.1 1.4 %collective-permute-start.4 = (bf16[16,16,128]{2,1,0:T(8,128)(2,1)S(1)}, bf16[16,16,128]{2,1,0:T(8,128)(2,1)S(1)}, u32[]{:S(2)}, u32[]{:S(2)}) collective-permute-start(bf16[16,16,128]{2,1,0:T(8,128)(2,1)S(1)} %get-tuple-element.26), channel_id=1, source_target_pairs={{0,12},{4,8},{8,4},{12,0},{1,13},{5,9},{9,5},{13,1},{2,14},{6,10},... | collective-permute-start | bytes 196616 | tf_op jit(solution)/shard_map/ppermute | solution.py:317
  13.5 0.2 collective-permute-start.5
  13.7 3.3 %collective-permute-done.3.tile_ref = bf16[16,16,128]{2,1,0:T(8,128)(2,1)S(1)} collective-permute-done((bf16[16,16,128]{2,1,0:T(8,128)(2,1)S(1)}, bf16[16,16,128]{2,1,0:T(8,128)(2,1)S(1)}, u32[]{:S(2)}, u32[]{:S(2)}) %collective-permute-start.3) | collective-permute-done | bytes 65568 | tf_op jit(solution)/shard_map/ppermute | solution.py:317
  17.1 1.3 %collective-permute-done.4.refs_0_ = bf16[16,16,128]{2,1,0:T(8,128)(2,1)S(1)} collective-permute-done((bf16[16,16,128]{2,1,0:T(8,128)(2,1)S(1)}, bf16[16,16,128]{2,1,0:T(8,128)(2,1)S(1)}, u32[]{:S(2)}, u32[]{:S(2)}) %collective-permute-start.4) | collective-permute-done | bytes 65568 | tf_op jit(solution)/shard_map/ppermute | solution.py:317
  18.8 3.0 %collective-permute-start.7 = (bf16[16,16,128]{2,1,0:T(8,128)(2,1)S(1)}, bf16[16,16,128]{2,1,0:T(8,128)(2,1)S(1)}, u32[]{:S(2)}, u32[]{:S(2)}) collective-permute-start(bf16[16,16,128]{2,1,0:T(8,128)(2,1)S(1)} %get-tuple-element.33.refs_0_.grad_ref), channel_id=1, source_target_pairs={{0,12},{4,8},{8,4},{12,0},{1,13},{5,9},{9,5},{13,1},{2,14},{6,10},... | collective-permute-start | bytes 196616 | tf_op jit(solution)/shard_map/ppermute | solution.py:317
  22.1 1.2 %collective-permute-start.6 = (bf16[16,16,128]{2,1,0:T(8,128)(2,1)S(1)}, bf16[16,16,128]{2,1,0:T(8,128)(2,1)S(1)}, u32[]{:S(2)}, u32[]{:S(2)}) collective-permute-start(bf16[16,16,128]{2,1,0:T(8,128)(2,1)S(1)} %get-tuple-element.33.refs_0_.grad_ref), channel_id=1, source_target_pairs={{0,8},{4,12},{8,0},{12,4},{1,9},{5,13},{9,1},{13,5},{2,10},{6,14},... | collective-permute-start | bytes 196616 | tf_op jit(solution)/shard_map/ppermute | solution.py:317
  23.3 0.4 %shard_map.87 = (f32[8,256]{1,0:T(8,128)S(1)}, f32[256,256]{1,0:T(8,128)S(1)}) custom-call(f32[256,128]{1,0:T(8,128)S(1)} %get-tuple-element.35.normed_ref.refs_7_.refs_2_, bf16[128,640]{1,0:T(8,128)(2,1)S(1)} %copy-done), custom_call_target="tpu_custom_call" | custom-call | tf_op jit(solution)/shard_map/pallas_call | solution.py:289
  23.9 0.6 %copy-done.1 = bf16[128,128]{1,0:T(8,128)(2,1)S(1)} copy-done((bf16[128,128]{1,0:T(8,128)(2,1)S(1)}, bf16[128,128]{1,0:T(8,128)(2,1)}, u32[]{:S(2)}) %copy-start.1) | copy-done | bytes 32792
  24.5 0.8 %shard_map.84 = (bf16[16,16,128]{2,1,0:T(8,128)(2,1)}, f32[256,128]{1,0:T(8,128)S(1)}) custom-call(f32[256,128]{1,0:T(8,128)S(1)} %get-tuple-element.29.tri_normed_ref, f32[256,128]{1,0:T(8,128)S(1)} %get-tuple-element.30.open_ref, f32[256,128]{1,0:T(8,128)S(1)} %get-tuple-element.31.gate_factor_ref, bf16[128,640]{1,0:T(8,128)(2,1)S(1)} %copy-done, ...), custom_call_target="tpu_custom_call" | custom-call | flops 16777216 | bytes 786432 | tf_op jit(solution)/shard_map/pallas_call | solution.py:289
  25.7 0.7 %collective-permute-done.8.grad_ref.refs_1_ = bf16[16,16,128]{2,1,0:T(8,128)(2,1)S(1)} collective-permute-done((bf16[16,16,128]{2,1,0:T(8,128)(2,1)S(1)}, bf16[16,16,128]{2,1,0:T(8,128)(2,1)S(1)}, u32[]{:S(2)}, u32[]{:S(2)}) %collective-permute-start.8) | collective-permute-done | bytes 65568 | tf_op jit(solution)/shard_map/ppermute | solution.py:317
  26.6 0.7 %collective-permute-done.6.grad_ref.refs_2_ = bf16[16,16,128]{2,1,0:T(8,128)(2,1)S(1)} collective-permute-done((bf16[16,16,128]{2,1,0:T(8,128)(2,1)S(1)}, bf16[16,16,128]{2,1,0:T(8,128)(2,1)S(1)}, u32[]{:S(2)}, u32[]{:S(2)}) %collective-permute-start.6) | collective-permute-done | bytes 65568 | tf_op jit(solution)/shard_map/ppermute | solution.py:317
  27.2 0.3 shard_map.91
  27.5 0.9 %collective-permute-start.9 = (bf16[16,16,128]{2,1,0:T(8,128)(2,1)S(1)}, bf16[16,16,128]{2,1,0:T(8,128)(2,1)S(1)}, u32[]{:S(2)}, u32[]{:S(2)}) collective-permute-start(bf16[16,16,128]{2,1,0:T(8,128)(2,1)S(1)} %get-tuple-element.38), channel_id=1, source_target_pairs={{0,3},{1,2},{2,1},{3,0},{4,7},{5,6},{6,5},{7,4},{8,11},{9,10},{10,... | collective-permute-start | bytes 196616 | tf_op jit(solution)/shard_map/ppermute | solution.py:317
  28.4 1.2 %collective-permute-start.10 = (bf16[16,16,128]{2,1,0:T(8,128)(2,1)S(1)}, bf16[16,16,128]{2,1,0:T(8,128)(2,1)S(1)}, u32[]{:S(2)}, u32[]{:S(2)}) collective-permute-start(bf16[16,16,128]{2,1,0:T(8,128)(2,1)S(1)} %get-tuple-element.39), channel_id=1, source_target_pairs={{0,2},{1,3},{2,0},{3,1},{4,6},{5,7},{6,4},{7,5},{8,10},{9,11},{10,... | collective-permute-start | bytes 196616 | tf_op jit(solution)/shard_map/ppermute | solution.py:317
  29.6 0.6 %shard_map.93.refs_5_ = f32[256,128]{1,0:T(8,128)S(1)} custom-call(f32[64,16,128]{2,1,0:T(8,128)S(1)} %shard_map.85.panel, bf16[16,16,128]{2,1,0:T(8,128)(2,1)S(1)} %collective-permute-done.7.grad_ref.refs_0_, bf16[16,16,128]{2,1,0:T(8,128)(2,1)S(1)} %collective-permute-done.8.grad_ref.refs_1_, ...), custom_call_target="tpu_custom_call" | custom-call | tf_op jit(solution)/shard_map/pallas_call | solution.py:289
  30.2 1.4 %collective-permute-done.9.tile_ref = bf16[16,16,128]{2,1,0:T(8,128)(2,1)S(1)} collective-permute-done((bf16[16,16,128]{2,1,0:T(8,128)(2,1)S(1)}, bf16[16,16,128]{2,1,0:T(8,128)(2,1)S(1)}, u32[]{:S(2)}, u32[]{:S(2)}) %collective-permute-start.9) | collective-permute-done | bytes 65568 | tf_op jit(solution)/shard_map/ppermute | solution.py:317
  31.6 1.5 %collective-permute-done.10.refs_0_ = bf16[16,16,128]{2,1,0:T(8,128)(2,1)S(1)} collective-permute-done((bf16[16,16,128]{2,1,0:T(8,128)(2,1)S(1)}, bf16[16,16,128]{2,1,0:T(8,128)(2,1)S(1)}, u32[]{:S(2)}, u32[]{:S(2)}) %collective-permute-start.10) | collective-permute-done | bytes 65568 | tf_op jit(solution)/shard_map/ppermute | solution.py:317
  33.1 0.8 %shard_map.94 = bf16[16,16,128]{2,1,0:T(8,128)(2,1)} custom-call(f32[16,16,128]{2,1,0:T(8,128)S(1)} %shard_map.92.base, bf16[16,16,128]{2,1,0:T(8,128)(2,1)S(1)} %collective-permute-done.10.refs_0_, bf16[16,16,128]{2,1,0:T(8,128)(2,1)S(1)} %collective-permute-done.11.refs_1_, f32[256,128]{1,0:T(8,128)S(1)} %get-tuple-element.35.normed_ref.refs_7_.refs_2_, ...), custom_call_target="tpu_custom_call" | custom-call | flops 16777216 | bytes 1679360 | tf_op jit(solution)/shard_map/pallas_call | solution.py:289
  (22 shorter events, 2.0 us)
Async XLA Ops:
  1.9 5.6 %collective-permute-start.2 = (bf16[16,16,128]{2,1,0:T(8,128)(2,1)S(1)}, bf16[16,16,128]{2,1,0:T(8,128)(2,1)S(1)}, u32[]{:S(2)}, u32[]{:S(2)}) collective-permute-start(bf16[16,16,128]{2,1,0:T(8,128)(2,1)S(1)} %shard_map.77.refs_0_), channel_id=1, source_target_pairs={{0,2},{1,3},{2,0},{3,1},{4,6},{5,7},{6,4},{7,5},{8,10},{9,11},{10,... | collective-permute-start | bytes 196616 | tf_op jit(solution)/shard_map/ppermute | solution.py:317
  4.9 4.1 %collective-permute-start = (bf16[16,16,128]{2,1,0:T(8,128)(2,1)S(1)}, bf16[16,16,128]{2,1,0:T(8,128)(2,1)S(1)}, u32[]{:S(2)}, u32[]{:S(2)}) collective-permute-start(bf16[16,16,128]{2,1,0:T(8,128)(2,1)S(1)} %shard_map.77.refs_0_), channel_id=1, source_target_pairs={{0,3},{1,2},{2,1},{3,0},{4,7},{5,6},{6,5},{7,4},{8,11},{9,10},{10,... | collective-permute-start | bytes 196616 | tf_op jit(solution)/shard_map/ppermute | solution.py:317
  4.9 4.1 %collective-permute-start.1 = (bf16[16,16,128]{2,1,0:T(8,128)(2,1)S(1)}, bf16[16,16,128]{2,1,0:T(8,128)(2,1)S(1)}, u32[]{:S(2)}, u32[]{:S(2)}) collective-permute-start(bf16[16,16,128]{2,1,0:T(8,128)(2,1)S(1)} %shard_map.77.refs_0_), channel_id=1, source_target_pairs={{0,1},{1,0},{2,3},{3,2},{4,5},{5,4},{6,7},{7,6},{8,9},{9,8},{10,11... | collective-permute-start | bytes 196616 | tf_op jit(solution)/shard_map/ppermute | solution.py:317
  9.4 7.6 %collective-permute-start.3 = (bf16[16,16,128]{2,1,0:T(8,128)(2,1)S(1)}, bf16[16,16,128]{2,1,0:T(8,128)(2,1)S(1)}, u32[]{:S(2)}, u32[]{:S(2)}) collective-permute-start(bf16[16,16,128]{2,1,0:T(8,128)(2,1)S(1)} %get-tuple-element.25), channel_id=1, source_target_pairs={{0,8},{4,12},{8,0},{12,4},{1,9},{5,13},{9,1},{13,5},{2,10},{6,14},... | collective-permute-start | bytes 196616 | tf_op jit(solution)/shard_map/ppermute | solution.py:317
  12.1 6.3 %collective-permute-start.4 = (bf16[16,16,128]{2,1,0:T(8,128)(2,1)S(1)}, bf16[16,16,128]{2,1,0:T(8,128)(2,1)S(1)}, u32[]{:S(2)}, u32[]{:S(2)}) collective-permute-start(bf16[16,16,128]{2,1,0:T(8,128)(2,1)S(1)} %get-tuple-element.26), channel_id=1, source_target_pairs={{0,12},{4,8},{8,4},{12,0},{1,13},{5,9},{9,5},{13,1},{2,14},{6,10},... | collective-permute-start | bytes 196616 | tf_op jit(solution)/shard_map/ppermute | solution.py:317
  13.5 5.1 %collective-permute-start.5 = (bf16[16,16,128]{2,1,0:T(8,128)(2,1)S(1)}, bf16[16,16,128]{2,1,0:T(8,128)(2,1)S(1)}, u32[]{:S(2)}, u32[]{:S(2)}) collective-permute-start(bf16[16,16,128]{2,1,0:T(8,128)(2,1)S(1)} %get-tuple-element.27), channel_id=1, source_target_pairs={{0,4},{4,0},{8,12},{12,8},{1,5},{5,1},{9,13},{13,9},{2,6},{6,2},{1... | collective-permute-start | bytes 196616 | tf_op jit(solution)/shard_map/ppermute | solution.py:317
  18.6 4.7 %copy-start = (bf16[128,640]{1,0:T(8,128)(2,1)S(1)}, bf16[128,640]{1,0:T(8,128)(2,1)}, u32[]{:S(2)}) copy-start(bf16[128,640]{1,0:T(8,128)(2,1)} %refs_8_.1) | copy-start | bytes 491524
  18.8 6.7 %collective-permute-start.7 = (bf16[16,16,128]{2,1,0:T(8,128)(2,1)S(1)}, bf16[16,16,128]{2,1,0:T(8,128)(2,1)S(1)}, u32[]{:S(2)}, u32[]{:S(2)}) collective-permute-start(bf16[16,16,128]{2,1,0:T(8,128)(2,1)S(1)} %get-tuple-element.33.refs_0_.grad_ref), channel_id=1, source_target_pairs={{0,12},{4,8},{8,4},{12,0},{1,13},{5,9},{9,5},{13,1},{2,14},{6,10},... | collective-permute-start | bytes 196616 | tf_op jit(solution)/shard_map/ppermute | solution.py:317
  21.9 4.5 %collective-permute-start.8 = (bf16[16,16,128]{2,1,0:T(8,128)(2,1)S(1)}, bf16[16,16,128]{2,1,0:T(8,128)(2,1)S(1)}, u32[]{:S(2)}, u32[]{:S(2)}) collective-permute-start(bf16[16,16,128]{2,1,0:T(8,128)(2,1)S(1)} %get-tuple-element.33.refs_0_.grad_ref), channel_id=1, source_target_pairs={{0,4},{4,0},{8,12},{12,8},{1,5},{5,1},{9,13},{13,9},{2,6},{6,2},{1... | collective-permute-start | bytes 196616 | tf_op jit(solution)/shard_map/ppermute | solution.py:317
  22.1 5.2 %collective-permute-start.6 = (bf16[16,16,128]{2,1,0:T(8,128)(2,1)S(1)}, bf16[16,16,128]{2,1,0:T(8,128)(2,1)S(1)}, u32[]{:S(2)}, u32[]{:S(2)}) collective-permute-start(bf16[16,16,128]{2,1,0:T(8,128)(2,1)S(1)} %get-tuple-element.33.refs_0_.grad_ref), channel_id=1, source_target_pairs={{0,8},{4,12},{8,0},{12,4},{1,9},{5,13},{9,1},{13,5},{2,10},{6,14},... | collective-permute-start | bytes 196616 | tf_op jit(solution)/shard_map/ppermute | solution.py:317
  23.8 0.8 %copy-start.1 = (bf16[128,128]{1,0:T(8,128)(2,1)S(1)}, bf16[128,128]{1,0:T(8,128)(2,1)}, u32[]{:S(2)}) copy-start(bf16[128,128]{1,0:T(8,128)(2,1)} %out_weight_ref.1) | copy-start | bytes 98308
  27.5 4.1 %collective-permute-start.9 = (bf16[16,16,128]{2,1,0:T(8,128)(2,1)S(1)}, bf16[16,16,128]{2,1,0:T(8,128)(2,1)S(1)}, u32[]{:S(2)}, u32[]{:S(2)}) collective-permute-start(bf16[16,16,128]{2,1,0:T(8,128)(2,1)S(1)} %get-tuple-element.38), channel_id=1, source_target_pairs={{0,3},{1,2},{2,1},{3,0},{4,7},{5,6},{6,5},{7,4},{8,11},{9,10},{10,... | collective-permute-start | bytes 196616 | tf_op jit(solution)/shard_map/ppermute | solution.py:317
  28.4 4.8 %collective-permute-start.10 = (bf16[16,16,128]{2,1,0:T(8,128)(2,1)S(1)}, bf16[16,16,128]{2,1,0:T(8,128)(2,1)S(1)}, u32[]{:S(2)}, u32[]{:S(2)}) collective-permute-start(bf16[16,16,128]{2,1,0:T(8,128)(2,1)S(1)} %get-tuple-element.39), channel_id=1, source_target_pairs={{0,2},{1,3},{2,0},{3,1},{4,6},{5,7},{6,4},{7,5},{8,10},{9,11},{10,... | collective-permute-start | bytes 196616 | tf_op jit(solution)/shard_map/ppermute | solution.py:317
  29.5 3.6 %collective-permute-start.11 = (bf16[16,16,128]{2,1,0:T(8,128)(2,1)S(1)}, bf16[16,16,128]{2,1,0:T(8,128)(2,1)S(1)}, u32[]{:S(2)}, u32[]{:S(2)}) collective-permute-start(bf16[16,16,128]{2,1,0:T(8,128)(2,1)S(1)} %get-tuple-element.40), channel_id=1, source_target_pairs={{0,1},{1,0},{2,3},{3,2},{4,5},{5,4},{6,7},{7,6},{8,9},{9,8},{10,11... | collective-permute-start | bytes 196616 | tf_op jit(solution)/shard_map/ppermute | solution.py:317

commit v26 on v23

--- a/solution.py
+++ b/solution.py
@@ -345,17 +345,19 @@
         ],
     )
     order = [0] + steps
+    early = order[:-2] + order[-1:]
+    tile_at = dict(zip(order, lefts))
     parts = [
         call(
-            functools.partial(partial_kernel, [order[at]]), (tile,), crop_length, lefts[at], right, smem=(0,),
+            functools.partial(partial_kernel, [step]), (tile,), crop_length, tile_at[step], right, smem=(0,),
             flops=work, scratch=[pltpu.VMEM(wide.shape, f32)],
         )[0]
-        for at in range(n - 2)
+        for step in early
     ]
     total, *parts = call(
-        functools.partial(last_partial_kernel, order[-2:], order[:-2], [0] + row_steps),
-        (wide,) + (tile,) * (n - 1), crop_length, *lefts[-2:], right, *parts, smem=(0,), flops=work,
-        scratch=[pltpu.VMEM(wide.shape, f32), pltpu.VMEM((2,) + wide.shape, bf16)],
+        functools.partial(last_partial_kernel, order[-2:-1], early, [0] + row_steps),
+        (wide,) + (tile,) * (n - 1), crop_length, tile_at[order[-2]], right, *parts, smem=(0,), flops=work,
+        scratch=[pltpu.VMEM(wide.shape, f32), pltpu.VMEM((1,) + wide.shape, bf16)],
     )
     (left_panel,) = call(
         functools.partial(left_panel_kernel, [0] + steps), (panel,), crop_length, *lefts, smem=(0,)

time: 34.3 us -> 34.7 us (1.012)
  waiting for transfers between devices: 10.4 us -> 10.8 us
    pallas_call x18 -> x19, Pallas kernels: 7.5 us -> 7.52 us  [call(): pl.pallas_call(kernel, out_shape=tuple(outs), in_specs=specs, out_specs=(...]
  transfers between devices with their start and end apart: 12 -> 12, of which waited for: 8 -> 8; matrix products, arithmetic and copies ran while one was open for 0% -> 0% of each run, Pallas kernels for 13% -> 14%
where the time goes in v26:
time: 34.7 us; the launch traced here: 34.4 us
  starting transfers between devices  14.1 us (41%)
  waiting for transfers between devices  10.8 us (31%)
  Pallas kernels  7.52 us (22%)
  between operations  1.42 us (4%)
  local copies, waits for them, and re-layouts  0.6 us (2%)
    ppermute x12, starting transfers between devices, swap(): return lax.ppermute(values, axis, [(a, a ^ step) for a in range(n)])  14.1 us
    ppermute x12, waiting for transfers between devices, swap(): return lax.ppermute(values, axis, [(a, a ^ step) for a in range(n)])  10.8 us
    pallas_call x19, Pallas kernels, call(): pl.pallas_call(kernel, out_shape=tuple(outs), in_specs=specs, out_specs=(...  7.52 us
  transfers between devices with their start and end apart: 12, of which 8 were waited for; matrix products, arithmetic and copies ran while one was open for 0% of the time, Pallas kernels for 14%

profile of v26, /device:TPU:0, one launch (start us, length us, event | category | flops | bytes accessed | tf_op | source)
XLA Modules:
  0.0 34.4 jit_solution(7455671093593588637)
XLA Ops:
  0.6 1.3 %shard_map.77.refs_0_ = bf16[16,16,128]{2,1,0:T(8,128)(2,1)S(1)} custom-call(bf16[16,16,128]{2,1,0:T(8,128)(2,1)} %acts_in.3, s32[16,16]{1,0:T(8,128)} %mask_in.3, bf16[128,640]{1,0:T(8,128)(2,1)} %refs_8_.1), custom_call_target="tpu_custom_call" | custom-call | flops 16777216 | bytes 295936 | tf_op jit(solution)/shard_map/pallas_call | solution.py:289
  1.9 3.0 %collective-permute-start.1 = (bf16[16,16,128]{2,1,0:T(8,128)(2,1)S(1)}, bf16[16,16,128]{2,1,0:T(8,128)(2,1)S(1)}, u32[]{:S(2)}, u32[]{:S(2)}) collective-permute-start(bf16[16,16,128]{2,1,0:T(8,128)(2,1)S(1)} %shard_map.77.refs_0_), channel_id=1, source_target_pairs={{0,2},{1,3},{2,0},{3,1},{4,6},{5,7},{6,4},{7,5},{8,10},{9,11},{10,... | collective-permute-start | bytes 196616 | tf_op jit(solution)/shard_map/ppermute | solution.py:317
  5.8 1.6 %shard_map.78 = (f32[16,16,128]{2,1,0:T(8,128)S(1)}, f32[256,128]{1,0:T(8,128)S(1)}, f32[256,128]{1,0:T(8,128)S(1)}, f32[4,256,128]{2,1,0:T(8,128)S(1)}, f32[256...) custom-call(bf16[16,16,128]{2,1,0:T(8,128)(2,1)} %acts_in.3, s32[16,16]{1,0:T(8,128)} %mask_in.3, ...), custom_call_target="tpu_custom_call" | custom-call | flops 50331648 | bytes 1639428 | tf_op jit(solution)/shard_map/pallas_call | solution.py:289
  7.9 0.8 %collective-permute-done.refs_0_.refs_2_ = bf16[16,16,128]{2,1,0:T(8,128)(2,1)S(1)} collective-permute-done((bf16[16,16,128]{2,1,0:T(8,128)(2,1)S(1)}, bf16[16,16,128]{2,1,0:T(8,128)(2,1)S(1)}, u32[]{:S(2)}, u32[]{:S(2)}) %collective-permute-start) | collective-permute-done | bytes 65568 | tf_op jit(solution)/shard_map/ppermute | solution.py:317
  8.7 0.2 shard_map.82
  8.9 2.7 %collective-permute-start.3 = (bf16[16,16,128]{2,1,0:T(8,128)(2,1)S(1)}, bf16[16,16,128]{2,1,0:T(8,128)(2,1)S(1)}, u32[]{:S(2)}, u32[]{:S(2)}) collective-permute-start(bf16[16,16,128]{2,1,0:T(8,128)(2,1)S(1)} %get-tuple-element.25), channel_id=1, source_target_pairs={{0,8},{4,12},{8,0},{12,4},{1,9},{5,13},{9,1},{13,5},{2,10},{6,14},... | collective-permute-start | bytes 196616 | tf_op jit(solution)/shard_map/ppermute | solution.py:317
  11.6 1.3 %collective-permute-start.4 = (bf16[16,16,128]{2,1,0:T(8,128)(2,1)S(1)}, bf16[16,16,128]{2,1,0:T(8,128)(2,1)S(1)}, u32[]{:S(2)}, u32[]{:S(2)}) collective-permute-start(bf16[16,16,128]{2,1,0:T(8,128)(2,1)S(1)} %get-tuple-element.26), channel_id=1, source_target_pairs={{0,12},{4,8},{8,4},{12,0},{1,13},{5,9},{9,5},{13,1},{2,14},{6,10},... | collective-permute-start | bytes 196616 | tf_op jit(solution)/shard_map/ppermute | solution.py:317
  13.1 2.8 %collective-permute-done.3.tile_ref = bf16[16,16,128]{2,1,0:T(8,128)(2,1)S(1)} collective-permute-done((bf16[16,16,128]{2,1,0:T(8,128)(2,1)S(1)}, bf16[16,16,128]{2,1,0:T(8,128)(2,1)S(1)}, u32[]{:S(2)}, u32[]{:S(2)}) %collective-permute-start.3) | collective-permute-done | bytes 65568 | tf_op jit(solution)/shard_map/ppermute | solution.py:317
  16.0 2.3 %collective-permute-done.4.refs_0_ = bf16[16,16,128]{2,1,0:T(8,128)(2,1)S(1)} collective-permute-done((bf16[16,16,128]{2,1,0:T(8,128)(2,1)S(1)}, bf16[16,16,128]{2,1,0:T(8,128)(2,1)S(1)}, u32[]{:S(2)}, u32[]{:S(2)}) %collective-permute-start.4) | collective-permute-done | bytes 65568 | tf_op jit(solution)/shard_map/ppermute | solution.py:317
  18.2 0.3 collective-permute-done.5.refs_1_
  18.8 3.4 %collective-permute-start.7 = (bf16[16,16,128]{2,1,0:T(8,128)(2,1)S(1)}, bf16[16,16,128]{2,1,0:T(8,128)(2,1)S(1)}, u32[]{:S(2)}, u32[]{:S(2)}) collective-permute-start(bf16[16,16,128]{2,1,0:T(8,128)(2,1)S(1)} %get-tuple-element.33.refs_0_.grad_ref), channel_id=1, source_target_pairs={{0,12},{4,8},{8,4},{12,0},{1,13},{5,9},{9,5},{13,1},{2,14},{6,10},... | collective-permute-start | bytes 196616 | tf_op jit(solution)/shard_map/ppermute | solution.py:317
  22.1 1.1 %collective-permute-start.6 = (bf16[16,16,128]{2,1,0:T(8,128)(2,1)S(1)}, bf16[16,16,128]{2,1,0:T(8,128)(2,1)S(1)}, u32[]{:S(2)}, u32[]{:S(2)}) collective-permute-start(bf16[16,16,128]{2,1,0:T(8,128)(2,1)S(1)} %get-tuple-element.33.refs_0_.grad_ref), channel_id=1, source_target_pairs={{0,8},{4,12},{8,0},{12,4},{1,9},{5,13},{9,1},{13,5},{2,10},{6,14},... | collective-permute-start | bytes 196616 | tf_op jit(solution)/shard_map/ppermute | solution.py:317
  23.2 0.4 %shard_map.88 = (f32[8,256]{1,0:T(8,128)S(1)}, f32[256,256]{1,0:T(8,128)S(1)}) custom-call(f32[256,128]{1,0:T(8,128)S(1)} %get-tuple-element.35.normed_ref.refs_7_.refs_2_, bf16[128,640]{1,0:T(8,128)(2,1)S(1)} %copy-done), custom_call_target="tpu_custom_call" | custom-call | tf_op jit(solution)/shard_map/pallas_call | solution.py:289
  23.9 0.6 %copy-done.1 = bf16[128,128]{1,0:T(8,128)(2,1)S(1)} copy-done((bf16[128,128]{1,0:T(8,128)(2,1)S(1)}, bf16[128,128]{1,0:T(8,128)(2,1)}, u32[]{:S(2)}) %copy-start.1) | copy-done | bytes 32792
  24.4 0.8 %shard_map.85 = (bf16[16,16,128]{2,1,0:T(8,128)(2,1)}, f32[256,128]{1,0:T(8,128)S(1)}) custom-call(f32[256,128]{1,0:T(8,128)S(1)} %get-tuple-element.29.tri_normed_ref, f32[256,128]{1,0:T(8,128)S(1)} %get-tuple-element.30.open_ref, f32[256,128]{1,0:T(8,128)S(1)} %get-tuple-element.31.gate_factor_ref, bf16[128,640]{1,0:T(8,128)(2,1)S(1)} %copy-done, ...), custom_call_target="tpu_custom_call" | custom-call | flops 16777216 | bytes 786432 | tf_op jit(solution)/shard_map/pallas_call | solution.py:289
  25.6 1.5 %collective-permute-done.8.grad_ref.refs_1_ = bf16[16,16,128]{2,1,0:T(8,128)(2,1)S(1)} collective-permute-done((bf16[16,16,128]{2,1,0:T(8,128)(2,1)S(1)}, bf16[16,16,128]{2,1,0:T(8,128)(2,1)S(1)}, u32[]{:S(2)}, u32[]{:S(2)}) %collective-permute-start.8) | collective-permute-done | bytes 65568 | tf_op jit(solution)/shard_map/ppermute | solution.py:317
  27.3 0.5 %collective-permute-done.6.grad_ref.refs_2_ = bf16[16,16,128]{2,1,0:T(8,128)(2,1)S(1)} collective-permute-done((bf16[16,16,128]{2,1,0:T(8,128)(2,1)S(1)}, bf16[16,16,128]{2,1,0:T(8,128)(2,1)S(1)}, u32[]{:S(2)}, u32[]{:S(2)}) %collective-permute-start.6) | collective-permute-done | bytes 65568 | tf_op jit(solution)/shard_map/ppermute | solution.py:317
  27.7 0.3 shard_map.92
  28.0 1.2 %collective-permute-start.9 = (bf16[16,16,128]{2,1,0:T(8,128)(2,1)S(1)}, bf16[16,16,128]{2,1,0:T(8,128)(2,1)S(1)}, u32[]{:S(2)}, u32[]{:S(2)}) collective-permute-start(bf16[16,16,128]{2,1,0:T(8,128)(2,1)S(1)} %get-tuple-element.38), channel_id=1, source_target_pairs={{0,2},{1,3},{2,0},{3,1},{4,6},{5,7},{6,4},{7,5},{8,10},{9,11},{10,... | collective-permute-start | bytes 196616 | tf_op jit(solution)/shard_map/ppermute | solution.py:317
  29.2 1.0 %collective-permute-start.11 = (bf16[16,16,128]{2,1,0:T(8,128)(2,1)S(1)}, bf16[16,16,128]{2,1,0:T(8,128)(2,1)S(1)}, u32[]{:S(2)}, u32[]{:S(2)}) collective-permute-start(bf16[16,16,128]{2,1,0:T(8,128)(2,1)S(1)} %get-tuple-element.40), channel_id=1, source_target_pairs={{0,1},{1,0},{2,3},{3,2},{4,5},{5,4},{6,7},{7,6},{8,9},{9,8},{10,11... | collective-permute-start | bytes 196616 | tf_op jit(solution)/shard_map/ppermute | solution.py:317
  30.2 0.6 %shard_map.94.refs_5_ = f32[256,128]{1,0:T(8,128)S(1)} custom-call(f32[64,16,128]{2,1,0:T(8,128)S(1)} %shard_map.86.panel, bf16[16,16,128]{2,1,0:T(8,128)(2,1)S(1)} %collective-permute-done.7.grad_ref.refs_0_, bf16[16,16,128]{2,1,0:T(8,128)(2,1)S(1)} %collective-permute-done.8.grad_ref.refs_1_, ...), custom_call_target="tpu_custom_call" | custom-call | tf_op jit(solution)/shard_map/pallas_call | solution.py:289
  30.9 1.7 %collective-permute-done.9.tile_ref = bf16[16,16,128]{2,1,0:T(8,128)(2,1)S(1)} collective-permute-done((bf16[16,16,128]{2,1,0:T(8,128)(2,1)S(1)}, bf16[16,16,128]{2,1,0:T(8,128)(2,1)S(1)}, u32[]{:S(2)}, u32[]{:S(2)}) %collective-permute-start.9) | collective-permute-done | bytes 65568 | tf_op jit(solution)/shard_map/ppermute | solution.py:317
  32.5 1.0 %collective-permute-done.10.refs_0_ = bf16[16,16,128]{2,1,0:T(8,128)(2,1)S(1)} collective-permute-done((bf16[16,16,128]{2,1,0:T(8,128)(2,1)S(1)}, bf16[16,16,128]{2,1,0:T(8,128)(2,1)S(1)}, u32[]{:S(2)}, u32[]{:S(2)}) %collective-permute-start.10) | collective-permute-done | bytes 65568 | tf_op jit(solution)/shard_map/ppermute | solution.py:317
  33.6 0.8 %shard_map.95 = bf16[16,16,128]{2,1,0:T(8,128)(2,1)} custom-call(f32[16,16,128]{2,1,0:T(8,128)S(1)} %shard_map.93.base, bf16[16,16,128]{2,1,0:T(8,128)(2,1)S(1)} %collective-permute-done.10.refs_0_, bf16[16,16,128]{2,1,0:T(8,128)(2,1)S(1)} %collective-permute-done.11.refs_1_, f32[256,128]{1,0:T(8,128)S(1)} %get-tuple-element.35.normed_ref.refs_7_.refs_2_, ...), custom_call_target="tpu_custom_call" | custom-call | flops 16777216 | bytes 1679360 | tf_op jit(solution)/shard_map/pallas_call | solution.py:289
  (23 shorter events, 2.0 us)
Async XLA Ops:
  1.9 5.6 %collective-permute-start.1 = (bf16[16,16,128]{2,1,0:T(8,128)(2,1)S(1)}, bf16[16,16,128]{2,1,0:T(8,128)(2,1)S(1)}, u32[]{:S(2)}, u32[]{:S(2)}) collective-permute-start(bf16[16,16,128]{2,1,0:T(8,128)(2,1)S(1)} %shard_map.77.refs_0_), channel_id=1, source_target_pairs={{0,2},{1,3},{2,0},{3,1},{4,6},{5,7},{6,4},{7,5},{8,10},{9,11},{10,... | collective-permute-start | bytes 196616 | tf_op jit(solution)/shard_map/ppermute | solution.py:317
  4.9 2.8 %collective-permute-start.2 = (bf16[16,16,128]{2,1,0:T(8,128)(2,1)S(1)}, bf16[16,16,128]{2,1,0:T(8,128)(2,1)S(1)}, u32[]{:S(2)}, u32[]{:S(2)}) collective-permute-start(bf16[16,16,128]{2,1,0:T(8,128)(2,1)S(1)} %shard_map.77.refs_0_), channel_id=1, source_target_pairs={{0,1},{1,0},{2,3},{3,2},{4,5},{5,4},{6,7},{7,6},{8,9},{9,8},{10,11... | collective-permute-start | bytes 196616 | tf_op jit(solution)/shard_map/ppermute | solution.py:317
  4.9 3.7 %collective-permute-start = (bf16[16,16,128]{2,1,0:T(8,128)(2,1)S(1)}, bf16[16,16,128]{2,1,0:T(8,128)(2,1)S(1)}, u32[]{:S(2)}, u32[]{:S(2)}) collective-permute-start(bf16[16,16,128]{2,1,0:T(8,128)(2,1)S(1)} %shard_map.77.refs_0_), channel_id=1, source_target_pairs={{0,3},{1,2},{2,1},{3,0},{4,7},{5,6},{6,5},{7,4},{8,11},{9,10},{10,... | collective-permute-start | bytes 196616 | tf_op jit(solution)/shard_map/ppermute | solution.py:317
  8.9 7.1 %collective-permute-start.3 = (bf16[16,16,128]{2,1,0:T(8,128)(2,1)S(1)}, bf16[16,16,128]{2,1,0:T(8,128)(2,1)S(1)}, u32[]{:S(2)}, u32[]{:S(2)}) collective-permute-start(bf16[16,16,128]{2,1,0:T(8,128)(2,1)S(1)} %get-tuple-element.25), channel_id=1, source_target_pairs={{0,8},{4,12},{8,0},{12,4},{1,9},{5,13},{9,1},{13,5},{2,10},{6,14},... | collective-permute-start | bytes 196616 | tf_op jit(solution)/shard_map/ppermute | solution.py:317
  11.6 6.7 %collective-permute-start.4 = (bf16[16,16,128]{2,1,0:T(8,128)(2,1)S(1)}, bf16[16,16,128]{2,1,0:T(8,128)(2,1)S(1)}, u32[]{:S(2)}, u32[]{:S(2)}) collective-permute-start(bf16[16,16,128]{2,1,0:T(8,128)(2,1)S(1)} %get-tuple-element.26), channel_id=1, source_target_pairs={{0,12},{4,8},{8,4},{12,0},{1,13},{5,9},{9,5},{13,1},{2,14},{6,10},... | collective-permute-start | bytes 196616 | tf_op jit(solution)/shard_map/ppermute | solution.py:317
  12.9 5.6 %collective-permute-start.5 = (bf16[16,16,128]{2,1,0:T(8,128)(2,1)S(1)}, bf16[16,16,128]{2,1,0:T(8,128)(2,1)S(1)}, u32[]{:S(2)}, u32[]{:S(2)}) collective-permute-start(bf16[16,16,128]{2,1,0:T(8,128)(2,1)S(1)} %get-tuple-element.27), channel_id=1, source_target_pairs={{0,4},{4,0},{8,12},{12,8},{1,5},{5,1},{9,13},{13,9},{2,6},{6,2},{1... | collective-permute-start | bytes 196616 | tf_op jit(solution)/shard_map/ppermute | solution.py:317
  18.5 4.7 %copy-start = (bf16[128,640]{1,0:T(8,128)(2,1)S(1)}, bf16[128,640]{1,0:T(8,128)(2,1)}, u32[]{:S(2)}) copy-start(bf16[128,640]{1,0:T(8,128)(2,1)} %refs_8_.1) | copy-start | bytes 491524
  18.8 6.7 %collective-permute-start.7 = (bf16[16,16,128]{2,1,0:T(8,128)(2,1)S(1)}, bf16[16,16,128]{2,1,0:T(8,128)(2,1)S(1)}, u32[]{:S(2)}, u32[]{:S(2)}) collective-permute-start(bf16[16,16,128]{2,1,0:T(8,128)(2,1)S(1)} %get-tuple-element.33.refs_0_.grad_ref), channel_id=1, source_target_pairs={{0,12},{4,8},{8,4},{12,0},{1,13},{5,9},{9,5},{13,1},{2,14},{6,10},... | collective-permute-start | bytes 196616 | tf_op jit(solution)/shard_map/ppermute | solution.py:317
  22.1 5.0 %collective-permute-start.8 = (bf16[16,16,128]{2,1,0:T(8,128)(2,1)S(1)}, bf16[16,16,128]{2,1,0:T(8,128)(2,1)S(1)}, u32[]{:S(2)}, u32[]{:S(2)}) collective-permute-start(bf16[16,16,128]{2,1,0:T(8,128)(2,1)S(1)} %get-tuple-element.33.refs_0_.grad_ref), channel_id=1, source_target_pairs={{0,4},{4,0},{8,12},{12,8},{1,5},{5,1},{9,13},{13,9},{2,6},{6,2},{1... | collective-permute-start | bytes 196616 | tf_op jit(solution)/shard_map/ppermute | solution.py:317
  22.1 5.6 %collective-permute-start.6 = (bf16[16,16,128]{2,1,0:T(8,128)(2,1)S(1)}, bf16[16,16,128]{2,1,0:T(8,128)(2,1)S(1)}, u32[]{:S(2)}, u32[]{:S(2)}) collective-permute-start(bf16[16,16,128]{2,1,0:T(8,128)(2,1)S(1)} %get-tuple-element.33.refs_0_.grad_ref), channel_id=1, source_target_pairs={{0,8},{4,12},{8,0},{12,4},{1,9},{5,13},{9,1},{13,5},{2,10},{6,14},... | collective-permute-start | bytes 196616 | tf_op jit(solution)/shard_map/ppermute | solution.py:317
  23.7 0.8 %copy-start.1 = (bf16[128,128]{1,0:T(8,128)(2,1)S(1)}, bf16[128,128]{1,0:T(8,128)(2,1)}, u32[]{:S(2)}) copy-start(bf16[128,128]{1,0:T(8,128)(2,1)} %out_weight_ref.1) | copy-start | bytes 98308
  28.0 4.5 %collective-permute-start.9 = (bf16[16,16,128]{2,1,0:T(8,128)(2,1)S(1)}, bf16[16,16,128]{2,1,0:T(8,128)(2,1)S(1)}, u32[]{:S(2)}, u32[]{:S(2)}) collective-permute-start(bf16[16,16,128]{2,1,0:T(8,128)(2,1)S(1)} %get-tuple-element.38), channel_id=1, source_target_pairs={{0,2},{1,3},{2,0},{3,1},{4,6},{5,7},{6,4},{7,5},{8,10},{9,11},{10,... | collective-permute-start | bytes 196616 | tf_op jit(solution)/shard_map/ppermute | solution.py:317
  29.2 4.3 %collective-permute-start.10 = (bf16[16,16,128]{2,1,0:T(8,128)(2,1)S(1)}, bf16[16,16,128]{2,1,0:T(8,128)(2,1)S(1)}, u32[]{:S(2)}, u32[]{:S(2)}) collective-permute-start(bf16[16,16,128]{2,1,0:T(8,128)(2,1)S(1)} %get-tuple-element.39), channel_id=1, source_target_pairs={{0,3},{1,2},{2,1},{3,0},{4,7},{5,6},{6,5},{7,4},{8,11},{9,10},{10,... | collective-permute-start | bytes 196616 | tf_op jit(solution)/shard_map/ppermute | solution.py:317
  29.2 4.3 %collective-permute-start.11 = (bf16[16,16,128]{2,1,0:T(8,128)(2,1)S(1)}, bf16[16,16,128]{2,1,0:T(8,128)(2,1)S(1)}, u32[]{:S(2)}, u32[]{:S(2)}) collective-permute-start(bf16[16,16,128]{2,1,0:T(8,128)(2,1)S(1)} %get-tuple-element.40), channel_id=1, source_target_pairs={{0,1},{1,0},{2,3},{3,2},{4,5},{5,4},{6,7},{7,6},{8,9},{9,8},{10,11... | collective-permute-start | bytes 196616 | tf_op jit(solution)/shard_map/ppermute | solution.py:317

commit v27 on v23

--- a/solution.py
+++ b/solution.py
@@ -329,7 +329,8 @@
             pltpu.SemaphoreType.DMA((3,)),
         ],
     )
-    lefts = gather(left, "col", steps)
+    first_steps = list(range(n - 1, 0, -1))
+    lefts = gather(left, "col", first_steps)
     right, normed, scale, factors, out_open, gate_factor, upstream = call(
         factors_kernel,
         (wide, flat, flat, jax.ShapeDtypeStruct((4, pairs, channels), f32), flat, flat, flat),
@@ -344,7 +345,7 @@
             pltpu.SemaphoreType.DMA((5,)),
         ],
     )
-    order = [0] + steps
+    order = [0] + first_steps
     parts = [
         call(
             functools.partial(partial_kernel, [order[at]]), (tile,), crop_length, lefts[at], right, smem=(0,),
@@ -358,7 +359,7 @@
         scratch=[pltpu.VMEM(wide.shape, f32), pltpu.VMEM((2,) + wide.shape, bf16)],
     )
     (left_panel,) = call(
-        functools.partial(left_panel_kernel, [0] + steps), (panel,), crop_length, *lefts, smem=(0,)
+        functools.partial(left_panel_kernel, [0] + first_steps), (panel,), crop_length, *lefts, smem=(0,)
     )
     last = []
     for step, part in zip(row_steps, parts):

time: 34.3 us -> 34.5 us (level)
  transfers between devices with their start and end apart: 12 -> 12, of which waited for: 8 -> 7; matrix products, arithmetic and copies ran while one was open for 0% -> 0% of each run, Pallas kernels for 13% -> 13%
where the time goes in v27:
time: 34.5 us; the launch traced here: 34.2 us
  starting transfers between devices  14.2 us (41%)
  waiting for transfers between devices  10.5 us (30%)
  Pallas kernels  7.5 us (22%)
  between operations  1.41 us (4%)
  local copies, waits for them, and re-layouts  0.6 us (2%)
    ppermute x12, starting transfers between devices, swap(): return lax.ppermute(values, axis, [(a, a ^ step) for a in range(n)])  14.2 us
    ppermute x12, waiting for transfers between devices, swap(): return lax.ppermute(values, axis, [(a, a ^ step) for a in range(n)])  10.5 us
    pallas_call x18, Pallas kernels, call(): pl.pallas_call(kernel, out_shape=tuple(outs), in_specs=specs, out_specs=(...  7.5 us
  transfers between devices with their start and end apart: 12, of which 7 were waited for; matrix products, arithmetic and copies ran while one was open for 0% of the time, Pallas kernels for 13%

profile of v27, /device:TPU:0, one launch (start us, length us, event | category | flops | bytes accessed | tf_op | source)
XLA Modules:
  0.0 34.2 jit_solution(10107632414823942830)
XLA Ops:
  0.6 1.3 %shard_map.77.refs_0_ = bf16[16,16,128]{2,1,0:T(8,128)(2,1)S(1)} custom-call(bf16[16,16,128]{2,1,0:T(8,128)(2,1)} %acts_in.3, s32[16,16]{1,0:T(8,128)} %mask_in.3, bf16[128,640]{1,0:T(8,128)(2,1)} %refs_8_.1), custom_call_target="tpu_custom_call" | custom-call | flops 16777216 | bytes 295936 | tf_op jit(solution)/shard_map/pallas_call | solution.py:289
  1.9 2.4 %collective-permute-start.2 = (bf16[16,16,128]{2,1,0:T(8,128)(2,1)S(1)}, bf16[16,16,128]{2,1,0:T(8,128)(2,1)S(1)}, u32[]{:S(2)}, u32[]{:S(2)}) collective-permute-start(bf16[16,16,128]{2,1,0:T(8,128)(2,1)S(1)} %shard_map.77.refs_0_), channel_id=1, source_target_pairs={{0,3},{1,2},{2,1},{3,0},{4,7},{5,6},{6,5},{7,4},{8,11},{9,10},{10,... | collective-permute-start | bytes 196616 | tf_op jit(solution)/shard_map/ppermute | solution.py:317
  4.3 0.6 %collective-permute-start = (bf16[16,16,128]{2,1,0:T(8,128)(2,1)S(1)}, bf16[16,16,128]{2,1,0:T(8,128)(2,1)S(1)}, u32[]{:S(2)}, u32[]{:S(2)}) collective-permute-start(bf16[16,16,128]{2,1,0:T(8,128)(2,1)S(1)} %shard_map.77.refs_0_), channel_id=1, source_target_pairs={{0,2},{1,3},{2,0},{3,1},{4,6},{5,7},{6,4},{7,5},{8,10},{9,11},{10,... | collective-permute-start | bytes 196616 | tf_op jit(solution)/shard_map/ppermute | solution.py:317
  5.7 1.6 %shard_map.78 = (f32[16,16,128]{2,1,0:T(8,128)S(1)}, f32[256,128]{1,0:T(8,128)S(1)}, f32[256,128]{1,0:T(8,128)S(1)}, f32[4,256,128]{2,1,0:T(8,128)S(1)}, f32[256...) custom-call(bf16[16,16,128]{2,1,0:T(8,128)(2,1)} %acts_in.3, s32[16,16]{1,0:T(8,128)} %mask_in.3, ...), custom_call_target="tpu_custom_call" | custom-call | flops 50331648 | bytes 1639428 | tf_op jit(solution)/shard_map/pallas_call | solution.py:289
  7.6 1.4 %collective-permute-done.refs_0_.refs_2_ = bf16[16,16,128]{2,1,0:T(8,128)(2,1)S(1)} collective-permute-done((bf16[16,16,128]{2,1,0:T(8,128)(2,1)S(1)}, bf16[16,16,128]{2,1,0:T(8,128)(2,1)S(1)}, u32[]{:S(2)}, u32[]{:S(2)}) %collective-permute-start) | collective-permute-done | bytes 65568 | tf_op jit(solution)/shard_map/ppermute | solution.py:317
  9.0 0.4 %shard_map.81 = (f32[16,16,128]{2,1,0:T(8,128)S(1)}, bf16[16,16,128]{2,1,0:T(8,128)(2,1)S(1)}, bf16[16,16,128]{2,1,0:T(8,128)(2,1)S(1)}, bf16[16,16,128]{2,1,0:T(8,128)(2,1)S(1)}) custom-call(s32[1]{0:T(128)S(6)} %copy.8.crop_ref, bf16[16,16,128]{2,1,0:T(8,128)(2,1)S(1)} %collective-permute-done.refs_0_.refs_2_, ...), custom_call_target="tpu_custom_call" | custom-call | flops 1048576 | bytes 720900 | tf_op jit(solution)/shard_map/pallas_call | solution.py:289
  9.4 2.8 %collective-permute-start.3 = (bf16[16,16,128]{2,1,0:T(8,128)(2,1)S(1)}, bf16[16,16,128]{2,1,0:T(8,128)(2,1)S(1)}, u32[]{:S(2)}, u32[]{:S(2)}) collective-permute-start(bf16[16,16,128]{2,1,0:T(8,128)(2,1)S(1)} %get-tuple-element.25), channel_id=1, source_target_pairs={{0,8},{4,12},{8,0},{12,4},{1,9},{5,13},{9,1},{13,5},{2,10},{6,14},... | collective-permute-start | bytes 196616 | tf_op jit(solution)/shard_map/ppermute | solution.py:317
  12.3 1.4 %collective-permute-start.4 = (bf16[16,16,128]{2,1,0:T(8,128)(2,1)S(1)}, bf16[16,16,128]{2,1,0:T(8,128)(2,1)S(1)}, u32[]{:S(2)}, u32[]{:S(2)}) collective-permute-start(bf16[16,16,128]{2,1,0:T(8,128)(2,1)S(1)} %get-tuple-element.26), channel_id=1, source_target_pairs={{0,12},{4,8},{8,4},{12,0},{1,13},{5,9},{9,5},{13,1},{2,14},{6,10},... | collective-permute-start | bytes 196616 | tf_op jit(solution)/shard_map/ppermute | solution.py:317
  13.6 0.2 collective-permute-start.5
  13.8 2.3 %collective-permute-done.3.tile_ref = bf16[16,16,128]{2,1,0:T(8,128)(2,1)S(1)} collective-permute-done((bf16[16,16,128]{2,1,0:T(8,128)(2,1)S(1)}, bf16[16,16,128]{2,1,0:T(8,128)(2,1)S(1)}, u32[]{:S(2)}, u32[]{:S(2)}) %collective-permute-start.3) | collective-permute-done | bytes 65568 | tf_op jit(solution)/shard_map/ppermute | solution.py:317
  16.2 2.4 %collective-permute-done.4.refs_0_ = bf16[16,16,128]{2,1,0:T(8,128)(2,1)S(1)} collective-permute-done((bf16[16,16,128]{2,1,0:T(8,128)(2,1)S(1)}, bf16[16,16,128]{2,1,0:T(8,128)(2,1)S(1)}, u32[]{:S(2)}, u32[]{:S(2)}) %collective-permute-start.4) | collective-permute-done | bytes 65568 | tf_op jit(solution)/shard_map/ppermute | solution.py:317
  18.9 3.2 %collective-permute-start.7 = (bf16[16,16,128]{2,1,0:T(8,128)(2,1)S(1)}, bf16[16,16,128]{2,1,0:T(8,128)(2,1)S(1)}, u32[]{:S(2)}, u32[]{:S(2)}) collective-permute-start(bf16[16,16,128]{2,1,0:T(8,128)(2,1)S(1)} %get-tuple-element.33.refs_0_.grad_ref), channel_id=1, source_target_pairs={{0,12},{4,8},{8,4},{12,0},{1,13},{5,9},{9,5},{13,1},{2,14},{6,10},... | collective-permute-start | bytes 196616 | tf_op jit(solution)/shard_map/ppermute | solution.py:317
  22.2 1.1 %collective-permute-start.6 = (bf16[16,16,128]{2,1,0:T(8,128)(2,1)S(1)}, bf16[16,16,128]{2,1,0:T(8,128)(2,1)S(1)}, u32[]{:S(2)}, u32[]{:S(2)}) collective-permute-start(bf16[16,16,128]{2,1,0:T(8,128)(2,1)S(1)} %get-tuple-element.33.refs_0_.grad_ref), channel_id=1, source_target_pairs={{0,8},{4,12},{8,0},{12,4},{1,9},{5,13},{9,1},{13,5},{2,10},{6,14},... | collective-permute-start | bytes 196616 | tf_op jit(solution)/shard_map/ppermute | solution.py:317
  23.3 0.4 %shard_map.87 = (f32[8,256]{1,0:T(8,128)S(1)}, f32[256,256]{1,0:T(8,128)S(1)}) custom-call(f32[256,128]{1,0:T(8,128)S(1)} %get-tuple-element.35.normed_ref.refs_7_.refs_2_, bf16[128,640]{1,0:T(8,128)(2,1)S(1)} %copy-done), custom_call_target="tpu_custom_call" | custom-call | tf_op jit(solution)/shard_map/pallas_call | solution.py:289
  24.0 0.6 %copy-done.1 = bf16[128,128]{1,0:T(8,128)(2,1)S(1)} copy-done((bf16[128,128]{1,0:T(8,128)(2,1)S(1)}, bf16[128,128]{1,0:T(8,128)(2,1)}, u32[]{:S(2)}) %copy-start.1) | copy-done | bytes 32792
  24.6 0.8 %shard_map.84 = (bf16[16,16,128]{2,1,0:T(8,128)(2,1)}, f32[256,128]{1,0:T(8,128)S(1)}) custom-call(f32[256,128]{1,0:T(8,128)S(1)} %get-tuple-element.29.tri_normed_ref, f32[256,128]{1,0:T(8,128)S(1)} %get-tuple-element.30.open_ref, f32[256,128]{1,0:T(8,128)S(1)} %get-tuple-element.31.gate_factor_ref, bf16[128,640]{1,0:T(8,128)(2,1)S(1)} %copy-done, ...), custom_call_target="tpu_custom_call" | custom-call | flops 16777216 | bytes 786432 | tf_op jit(solution)/shard_map/pallas_call | solution.py:289
  25.7 0.9 %collective-permute-done.8.grad_ref.refs_1_ = bf16[16,16,128]{2,1,0:T(8,128)(2,1)S(1)} collective-permute-done((bf16[16,16,128]{2,1,0:T(8,128)(2,1)S(1)}, bf16[16,16,128]{2,1,0:T(8,128)(2,1)S(1)}, u32[]{:S(2)}, u32[]{:S(2)}) %collective-permute-start.8) | collective-permute-done | bytes 65568 | tf_op jit(solution)/shard_map/ppermute | solution.py:317
  26.9 0.5 %collective-permute-done.6.grad_ref.refs_2_ = bf16[16,16,128]{2,1,0:T(8,128)(2,1)S(1)} collective-permute-done((bf16[16,16,128]{2,1,0:T(8,128)(2,1)S(1)}, bf16[16,16,128]{2,1,0:T(8,128)(2,1)S(1)}, u32[]{:S(2)}, u32[]{:S(2)}) %collective-permute-start.6) | collective-permute-done | bytes 65568 | tf_op jit(solution)/shard_map/ppermute | solution.py:317
  27.4 0.3 shard_map.91
  27.7 2.0 %collective-permute-start.9 = (bf16[16,16,128]{2,1,0:T(8,128)(2,1)S(1)}, bf16[16,16,128]{2,1,0:T(8,128)(2,1)S(1)}, u32[]{:S(2)}, u32[]{:S(2)}) collective-permute-start(bf16[16,16,128]{2,1,0:T(8,128)(2,1)S(1)} %get-tuple-element.38), channel_id=1, source_target_pairs={{0,2},{1,3},{2,0},{3,1},{4,6},{5,7},{6,4},{7,5},{8,10},{9,11},{10,... | collective-permute-start | bytes 196616 | tf_op jit(solution)/shard_map/ppermute | solution.py:317
  29.9 0.6 %shard_map.93.refs_5_ = f32[256,128]{1,0:T(8,128)S(1)} custom-call(f32[64,16,128]{2,1,0:T(8,128)S(1)} %shard_map.85.panel, bf16[16,16,128]{2,1,0:T(8,128)(2,1)S(1)} %collective-permute-done.7.grad_ref.refs_0_, bf16[16,16,128]{2,1,0:T(8,128)(2,1)S(1)} %collective-permute-done.8.grad_ref.refs_1_, ...), custom_call_target="tpu_custom_call" | custom-call | tf_op jit(solution)/shard_map/pallas_call | solution.py:289
  30.5 1.5 %collective-permute-done.9.tile_ref = bf16[16,16,128]{2,1,0:T(8,128)(2,1)S(1)} collective-permute-done((bf16[16,16,128]{2,1,0:T(8,128)(2,1)S(1)}, bf16[16,16,128]{2,1,0:T(8,128)(2,1)S(1)}, u32[]{:S(2)}, u32[]{:S(2)}) %collective-permute-start.9) | collective-permute-done | bytes 65568 | tf_op jit(solution)/shard_map/ppermute | solution.py:317
  32.0 1.4 %collective-permute-done.10.refs_0_ = bf16[16,16,128]{2,1,0:T(8,128)(2,1)S(1)} collective-permute-done((bf16[16,16,128]{2,1,0:T(8,128)(2,1)S(1)}, bf16[16,16,128]{2,1,0:T(8,128)(2,1)S(1)}, u32[]{:S(2)}, u32[]{:S(2)}) %collective-permute-start.10) | collective-permute-done | bytes 65568 | tf_op jit(solution)/shard_map/ppermute | solution.py:317
  33.4 0.8 %shard_map.94 = bf16[16,16,128]{2,1,0:T(8,128)(2,1)} custom-call(f32[16,16,128]{2,1,0:T(8,128)S(1)} %shard_map.92.base, bf16[16,16,128]{2,1,0:T(8,128)(2,1)S(1)} %collective-permute-done.10.refs_0_, bf16[16,16,128]{2,1,0:T(8,128)(2,1)S(1)} %collective-permute-done.11.refs_1_, f32[256,128]{1,0:T(8,128)S(1)} %get-tuple-element.35.normed_ref.refs_7_.refs_2_, ...), custom_call_target="tpu_custom_call" | custom-call | flops 16777216 | bytes 1679360 | tf_op jit(solution)/shard_map/pallas_call | solution.py:289
  (22 shorter events, 1.8 us)
Async XLA Ops:
  1.9 5.5 %collective-permute-start.2 = (bf16[16,16,128]{2,1,0:T(8,128)(2,1)S(1)}, bf16[16,16,128]{2,1,0:T(8,128)(2,1)S(1)}, u32[]{:S(2)}, u32[]{:S(2)}) collective-permute-start(bf16[16,16,128]{2,1,0:T(8,128)(2,1)S(1)} %shard_map.77.refs_0_), channel_id=1, source_target_pairs={{0,3},{1,2},{2,1},{3,0},{4,7},{5,6},{6,5},{7,4},{8,11},{9,10},{10,... | collective-permute-start | bytes 196616 | tf_op jit(solution)/shard_map/ppermute | solution.py:317
  4.3 4.7 %collective-permute-start = (bf16[16,16,128]{2,1,0:T(8,128)(2,1)S(1)}, bf16[16,16,128]{2,1,0:T(8,128)(2,1)S(1)}, u32[]{:S(2)}, u32[]{:S(2)}) collective-permute-start(bf16[16,16,128]{2,1,0:T(8,128)(2,1)S(1)} %shard_map.77.refs_0_), channel_id=1, source_target_pairs={{0,2},{1,3},{2,0},{3,1},{4,6},{5,7},{6,4},{7,5},{8,10},{9,11},{10,... | collective-permute-start | bytes 196616 | tf_op jit(solution)/shard_map/ppermute | solution.py:317
  5.0 4.0 %collective-permute-start.1 = (bf16[16,16,128]{2,1,0:T(8,128)(2,1)S(1)}, bf16[16,16,128]{2,1,0:T(8,128)(2,1)S(1)}, u32[]{:S(2)}, u32[]{:S(2)}) collective-permute-start(bf16[16,16,128]{2,1,0:T(8,128)(2,1)S(1)} %shard_map.77.refs_0_), channel_id=1, source_target_pairs={{0,1},{1,0},{2,3},{3,2},{4,5},{5,4},{6,7},{7,6},{8,9},{9,8},{10,11... | collective-permute-start | bytes 196616 | tf_op jit(solution)/shard_map/ppermute | solution.py:317
  9.4 6.8 %collective-permute-start.3 = (bf16[16,16,128]{2,1,0:T(8,128)(2,1)S(1)}, bf16[16,16,128]{2,1,0:T(8,128)(2,1)S(1)}, u32[]{:S(2)}, u32[]{:S(2)}) collective-permute-start(bf16[16,16,128]{2,1,0:T(8,128)(2,1)S(1)} %get-tuple-element.25), channel_id=1, source_target_pairs={{0,8},{4,12},{8,0},{12,4},{1,9},{5,13},{9,1},{13,5},{2,10},{6,14},... | collective-permute-start | bytes 196616 | tf_op jit(solution)/shard_map/ppermute | solution.py:317
  12.3 6.3 %collective-permute-start.4 = (bf16[16,16,128]{2,1,0:T(8,128)(2,1)S(1)}, bf16[16,16,128]{2,1,0:T(8,128)(2,1)S(1)}, u32[]{:S(2)}, u32[]{:S(2)}) collective-permute-start(bf16[16,16,128]{2,1,0:T(8,128)(2,1)S(1)} %get-tuple-element.26), channel_id=1, source_target_pairs={{0,12},{4,8},{8,4},{12,0},{1,13},{5,9},{9,5},{13,1},{2,14},{6,10},... | collective-permute-start | bytes 196616 | tf_op jit(solution)/shard_map/ppermute | solution.py:317
  13.6 5.0 %collective-permute-start.5 = (bf16[16,16,128]{2,1,0:T(8,128)(2,1)S(1)}, bf16[16,16,128]{2,1,0:T(8,128)(2,1)S(1)}, u32[]{:S(2)}, u32[]{:S(2)}) collective-permute-start(bf16[16,16,128]{2,1,0:T(8,128)(2,1)S(1)} %get-tuple-element.27), channel_id=1, source_target_pairs={{0,4},{4,0},{8,12},{12,8},{1,5},{5,1},{9,13},{13,9},{2,6},{6,2},{1... | collective-permute-start | bytes 196616 | tf_op jit(solution)/shard_map/ppermute | solution.py:317
  18.6 4.7 %copy-start = (bf16[128,640]{1,0:T(8,128)(2,1)S(1)}, bf16[128,640]{1,0:T(8,128)(2,1)}, u32[]{:S(2)}) copy-start(bf16[128,640]{1,0:T(8,128)(2,1)} %refs_8_.1) | copy-start | bytes 491524
  18.9 6.7 %collective-permute-start.7 = (bf16[16,16,128]{2,1,0:T(8,128)(2,1)S(1)}, bf16[16,16,128]{2,1,0:T(8,128)(2,1)S(1)}, u32[]{:S(2)}, u32[]{:S(2)}) collective-permute-start(bf16[16,16,128]{2,1,0:T(8,128)(2,1)S(1)} %get-tuple-element.33.refs_0_.grad_ref), channel_id=1, source_target_pairs={{0,12},{4,8},{8,4},{12,0},{1,13},{5,9},{9,5},{13,1},{2,14},{6,10},... | collective-permute-start | bytes 196616 | tf_op jit(solution)/shard_map/ppermute | solution.py:317
  22.1 4.6 %collective-permute-start.8 = (bf16[16,16,128]{2,1,0:T(8,128)(2,1)S(1)}, bf16[16,16,128]{2,1,0:T(8,128)(2,1)S(1)}, u32[]{:S(2)}, u32[]{:S(2)}) collective-permute-start(bf16[16,16,128]{2,1,0:T(8,128)(2,1)S(1)} %get-tuple-element.33.refs_0_.grad_ref), channel_id=1, source_target_pairs={{0,4},{4,0},{8,12},{12,8},{1,5},{5,1},{9,13},{13,9},{2,6},{6,2},{1... | collective-permute-start | bytes 196616 | tf_op jit(solution)/shard_map/ppermute | solution.py:317
  22.2 5.2 %collective-permute-start.6 = (bf16[16,16,128]{2,1,0:T(8,128)(2,1)S(1)}, bf16[16,16,128]{2,1,0:T(8,128)(2,1)S(1)}, u32[]{:S(2)}, u32[]{:S(2)}) collective-permute-start(bf16[16,16,128]{2,1,0:T(8,128)(2,1)S(1)} %get-tuple-element.33.refs_0_.grad_ref), channel_id=1, source_target_pairs={{0,8},{4,12},{8,0},{12,4},{1,9},{5,13},{9,1},{13,5},{2,10},{6,14},... | collective-permute-start | bytes 196616 | tf_op jit(solution)/shard_map/ppermute | solution.py:317
  23.8 0.8 %copy-start.1 = (bf16[128,128]{1,0:T(8,128)(2,1)S(1)}, bf16[128,128]{1,0:T(8,128)(2,1)}, u32[]{:S(2)}) copy-start(bf16[128,128]{1,0:T(8,128)(2,1)} %out_weight_ref.1) | copy-start | bytes 98308
  27.7 4.3 %collective-permute-start.9 = (bf16[16,16,128]{2,1,0:T(8,128)(2,1)S(1)}, bf16[16,16,128]{2,1,0:T(8,128)(2,1)S(1)}, u32[]{:S(2)}, u32[]{:S(2)}) collective-permute-start(bf16[16,16,128]{2,1,0:T(8,128)(2,1)S(1)} %get-tuple-element.38), channel_id=1, source_target_pairs={{0,2},{1,3},{2,0},{3,1},{4,6},{5,7},{6,4},{7,5},{8,10},{9,11},{10,... | collective-permute-start | bytes 196616 | tf_op jit(solution)/shard_map/ppermute | solution.py:317
  29.7 3.7 %collective-permute-start.10 = (bf16[16,16,128]{2,1,0:T(8,128)(2,1)S(1)}, bf16[16,16,128]{2,1,0:T(8,128)(2,1)S(1)}, u32[]{:S(2)}, u32[]{:S(2)}) collective-permute-start(bf16[16,16,128]{2,1,0:T(8,128)(2,1)S(1)} %get-tuple-element.39), channel_id=1, source_target_pairs={{0,3},{1,2},{2,1},{3,0},{4,7},{5,6},{6,5},{7,4},{8,11},{9,10},{10,... | collective-permute-start | bytes 196616 | tf_op jit(solution)/shard_map/ppermute | solution.py:317
  29.7 3.7 %collective-permute-start.11 = (bf16[16,16,128]{2,1,0:T(8,128)(2,1)S(1)}, bf16[16,16,128]{2,1,0:T(8,128)(2,1)S(1)}, u32[]{:S(2)}, u32[]{:S(2)}) collective-permute-start(bf16[16,16,128]{2,1,0:T(8,128)(2,1)S(1)} %get-tuple-element.40), channel_id=1, source_target_pairs={{0,1},{1,0},{2,3},{3,2},{4,5},{5,4},{6,7},{7,6},{8,9},{9,8},{10,11... | collective-permute-start | bytes 196616 | tf_op jit(solution)/shard_map/ppermute | solution.py:317

commit v28 on v25

--- a/solution.py
+++ b/solution.py
@@ -195,7 +195,7 @@
         center = total - mean_lanes(total)
         scale = lax.rsqrt(mean_lanes(center * center) + epsilon)
         tri_normed = center * scale
-        tri_normed_ref[here, :] = tri_normed
+        tri_normed_ref[i] = tri_normed.astype(bf16)
         project = mean_lanes(center * upstream) * scale
         grad_ref[i] = (scale * (upstream - tri_normed * project)).astype(bf16)
 
@@ -252,7 +252,7 @@
     tri_normed_ref, open_ref, gate_factor_ref, weights_ref, out_weight_ref, update_ref, normed_grad_ref
 ):
     size, _, channels = update_ref.shape
-    linear = dot(tri_normed_ref[...].astype(bf16), out_weight_ref[...])
+    linear = dot(tri_normed_ref[...].reshape(size * size, channels), out_weight_ref[...])
     update = (open_ref[...] * linear).astype(bf16)
     update_ref[...] = update.reshape(size, size, channels)
     out_gate_grad = (gate_factor_ref[...] * linear).astype(bf16)
@@ -368,7 +368,7 @@
         else:
             (total,) = call(add_kernel, (wide,), total, part, flops=wait)
     tri_normed, tri_grad = call(
-        triangle_kernel, (flat, tile), total, *last, upstream, flops=20 * pairs * channels,
+        triangle_kernel, (tile, tile), total, *last, upstream, flops=20 * pairs * channels,
     )
     grads = gather(tri_grad, "row", gather_steps)
     update, partial = call(

time: 34.2 us -> 34.2 us (level)
  no operation moved by 1% of the time
where the time goes in v28:
time: 34.2 us; the launch traced here: 34 us
  starting transfers between devices  14 us (41%)
  waiting for transfers between devices  10.5 us (31%)
  Pallas kernels  7.5 us (22%)
  between operations  1.41 us (4%)
  local copies, waits for them, and re-layouts  0.6 us (2%)
    ppermute x12, starting transfers between devices, swap(): return lax.ppermute(values, axis, [(a, a ^ step) for a in range(n)])  14 us
    ppermute x12, waiting for transfers between devices, swap(): return lax.ppermute(values, axis, [(a, a ^ step) for a in range(n)])  10.5 us
    pallas_call x18, Pallas kernels, call(): pl.pallas_call(kernel, out_shape=tuple(outs), in_specs=specs, out_specs=(...  7.5 us
  transfers between devices with their start and end apart: 12, of which 8 were waited for; matrix products, arithmetic and copies ran while one was open for 0% of the time, Pallas kernels for 13%

profile of v28, /device:TPU:0, one launch (start us, length us, event | category | flops | bytes accessed | tf_op | source)
XLA Modules:
  0.0 34.0 jit_solution(11724399503506624997)
XLA Ops:
  0.6 1.3 %shard_map.77.refs_0_ = bf16[16,16,128]{2,1,0:T(8,128)(2,1)S(1)} custom-call(bf16[16,16,128]{2,1,0:T(8,128)(2,1)} %acts_in.3, s32[16,16]{1,0:T(8,128)} %mask_in.3, bf16[128,640]{1,0:T(8,128)(2,1)} %refs_8_.1), custom_call_target="tpu_custom_call" | custom-call | flops 16777216 | bytes 295936 | tf_op jit(solution)/shard_map/pallas_call | solution.py:289
  1.9 3.0 %collective-permute-start.2 = (bf16[16,16,128]{2,1,0:T(8,128)(2,1)S(1)}, bf16[16,16,128]{2,1,0:T(8,128)(2,1)S(1)}, u32[]{:S(2)}, u32[]{:S(2)}) collective-permute-start(bf16[16,16,128]{2,1,0:T(8,128)(2,1)S(1)} %shard_map.77.refs_0_), channel_id=1, source_target_pairs={{0,2},{1,3},{2,0},{3,1},{4,6},{5,7},{6,4},{7,5},{8,10},{9,11},{10,... | collective-permute-start | bytes 196616 | tf_op jit(solution)/shard_map/ppermute | solution.py:317
  5.8 1.6 %shard_map.78 = (f32[16,16,128]{2,1,0:T(8,128)S(1)}, f32[256,128]{1,0:T(8,128)S(1)}, f32[256,128]{1,0:T(8,128)S(1)}, f32[4,256,128]{2,1,0:T(8,128)S(1)}, f32[256...) custom-call(bf16[16,16,128]{2,1,0:T(8,128)(2,1)} %acts_in.3, s32[16,16]{1,0:T(8,128)} %mask_in.3, ...), custom_call_target="tpu_custom_call" | custom-call | flops 50331648 | bytes 1639428 | tf_op jit(solution)/shard_map/pallas_call | solution.py:289
  7.7 1.4 %collective-permute-done.refs_0_.refs_2_ = bf16[16,16,128]{2,1,0:T(8,128)(2,1)S(1)} collective-permute-done((bf16[16,16,128]{2,1,0:T(8,128)(2,1)S(1)}, bf16[16,16,128]{2,1,0:T(8,128)(2,1)S(1)}, u32[]{:S(2)}, u32[]{:S(2)}) %collective-permute-start) | collective-permute-done | bytes 65568 | tf_op jit(solution)/shard_map/ppermute | solution.py:317
  9.0 0.4 %shard_map.81 = (f32[16,16,128]{2,1,0:T(8,128)S(1)}, bf16[16,16,128]{2,1,0:T(8,128)(2,1)S(1)}, bf16[16,16,128]{2,1,0:T(8,128)(2,1)S(1)}, bf16[16,16,128]{2,1,0:T(8,128)(2,1)S(1)}) custom-call(s32[1]{0:T(128)S(6)} %copy.8.crop_ref, bf16[16,16,128]{2,1,0:T(8,128)(2,1)S(1)} %collective-permute-done.refs_0_.refs_2_, ...), custom_call_target="tpu_custom_call" | custom-call | flops 1048576 | bytes 720900 | tf_op jit(solution)/shard_map/pallas_call | solution.py:289
  9.4 2.7 %collective-permute-start.3 = (bf16[16,16,128]{2,1,0:T(8,128)(2,1)S(1)}, bf16[16,16,128]{2,1,0:T(8,128)(2,1)S(1)}, u32[]{:S(2)}, u32[]{:S(2)}) collective-permute-start(bf16[16,16,128]{2,1,0:T(8,128)(2,1)S(1)} %get-tuple-element.25), channel_id=1, source_target_pairs={{0,8},{4,12},{8,0},{12,4},{1,9},{5,13},{9,1},{13,5},{2,10},{6,14},... | collective-permute-start | bytes 196616 | tf_op jit(solution)/shard_map/ppermute | solution.py:317
  12.1 1.4 %collective-permute-start.4 = (bf16[16,16,128]{2,1,0:T(8,128)(2,1)S(1)}, bf16[16,16,128]{2,1,0:T(8,128)(2,1)S(1)}, u32[]{:S(2)}, u32[]{:S(2)}) collective-permute-start(bf16[16,16,128]{2,1,0:T(8,128)(2,1)S(1)} %get-tuple-element.26), channel_id=1, source_target_pairs={{0,12},{4,8},{8,4},{12,0},{1,13},{5,9},{9,5},{13,1},{2,14},{6,10},... | collective-permute-start | bytes 196616 | tf_op jit(solution)/shard_map/ppermute | solution.py:317
  13.5 0.2 collective-permute-start.5
  13.7 3.3 %collective-permute-done.3.tile_ref = bf16[16,16,128]{2,1,0:T(8,128)(2,1)S(1)} collective-permute-done((bf16[16,16,128]{2,1,0:T(8,128)(2,1)S(1)}, bf16[16,16,128]{2,1,0:T(8,128)(2,1)S(1)}, u32[]{:S(2)}, u32[]{:S(2)}) %collective-permute-start.3) | collective-permute-done | bytes 65568 | tf_op jit(solution)/shard_map/ppermute | solution.py:317
  17.1 1.3 %collective-permute-done.4.refs_0_ = bf16[16,16,128]{2,1,0:T(8,128)(2,1)S(1)} collective-permute-done((bf16[16,16,128]{2,1,0:T(8,128)(2,1)S(1)}, bf16[16,16,128]{2,1,0:T(8,128)(2,1)S(1)}, u32[]{:S(2)}, u32[]{:S(2)}) %collective-permute-start.4) | collective-permute-done | bytes 65568 | tf_op jit(solution)/shard_map/ppermute | solution.py:317
  18.8 3.0 %collective-permute-start.7 = (bf16[16,16,128]{2,1,0:T(8,128)(2,1)S(1)}, bf16[16,16,128]{2,1,0:T(8,128)(2,1)S(1)}, u32[]{:S(2)}, u32[]{:S(2)}) collective-permute-start(bf16[16,16,128]{2,1,0:T(8,128)(2,1)S(1)} %get-tuple-element.33.refs_0_.grad_ref), channel_id=1, source_target_pairs={{0,12},{4,8},{8,4},{12,0},{1,13},{5,9},{9,5},{13,1},{2,14},{6,10},... | collective-permute-start | bytes 196616 | tf_op jit(solution)/shard_map/ppermute | solution.py:317
  22.1 1.2 %collective-permute-start.6 = (bf16[16,16,128]{2,1,0:T(8,128)(2,1)S(1)}, bf16[16,16,128]{2,1,0:T(8,128)(2,1)S(1)}, u32[]{:S(2)}, u32[]{:S(2)}) collective-permute-start(bf16[16,16,128]{2,1,0:T(8,128)(2,1)S(1)} %get-tuple-element.33.refs_0_.grad_ref), channel_id=1, source_target_pairs={{0,8},{4,12},{8,0},{12,4},{1,9},{5,13},{9,1},{13,5},{2,10},{6,14},... | collective-permute-start | bytes 196616 | tf_op jit(solution)/shard_map/ppermute | solution.py:317
  23.3 0.4 %shard_map.87 = (f32[8,256]{1,0:T(8,128)S(1)}, f32[256,256]{1,0:T(8,128)S(1)}) custom-call(f32[256,128]{1,0:T(8,128)S(1)} %get-tuple-element.35.normed_ref.refs_7_.refs_2_, bf16[128,640]{1,0:T(8,128)(2,1)S(1)} %copy-done), custom_call_target="tpu_custom_call" | custom-call | tf_op jit(solution)/shard_map/pallas_call | solution.py:289
  23.9 0.6 %copy-done.1 = bf16[128,128]{1,0:T(8,128)(2,1)S(1)} copy-done((bf16[128,128]{1,0:T(8,128)(2,1)S(1)}, bf16[128,128]{1,0:T(8,128)(2,1)}, u32[]{:S(2)}) %copy-start.1) | copy-done | bytes 32792
  24.5 0.8 %shard_map.84 = (bf16[16,16,128]{2,1,0:T(8,128)(2,1)}, f32[256,128]{1,0:T(8,128)S(1)}) custom-call(bf16[16,16,128]{2,1,0:T(8,128)(2,1)S(1)} %get-tuple-element.29.tri_normed_ref, f32[256,128]{1,0:T(8,128)S(1)} %get-tuple-element.30.open_ref, f32[256,128]{1,0:T(8,128)S(1)} %get-tuple-element.31.gate_factor_ref, bf16[128,640]{1,0:T(8,128)(2,1)S(1)} %copy-done, ...), custom_call_target="tpu_custom_call" | custom-call | flops 16777216 | bytes 720896 | tf_op jit(solution)/shard_map/pallas_call | solution.py:289
  25.7 0.7 %collective-permute-done.8.grad_ref.refs_1_ = bf16[16,16,128]{2,1,0:T(8,128)(2,1)S(1)} collective-permute-done((bf16[16,16,128]{2,1,0:T(8,128)(2,1)S(1)}, bf16[16,16,128]{2,1,0:T(8,128)(2,1)S(1)}, u32[]{:S(2)}, u32[]{:S(2)}) %collective-permute-start.8) | collective-permute-done | bytes 65568 | tf_op jit(solution)/shard_map/ppermute | solution.py:317
  26.6 0.7 %collective-permute-done.6.grad_ref.refs_2_ = bf16[16,16,128]{2,1,0:T(8,128)(2,1)S(1)} collective-permute-done((bf16[16,16,128]{2,1,0:T(8,128)(2,1)S(1)}, bf16[16,16,128]{2,1,0:T(8,128)(2,1)S(1)}, u32[]{:S(2)}, u32[]{:S(2)}) %collective-permute-start.6) | collective-permute-done | bytes 65568 | tf_op jit(solution)/shard_map/ppermute | solution.py:317
  27.2 0.3 shard_map.91
  27.5 0.9 %collective-permute-start.9 = (bf16[16,16,128]{2,1,0:T(8,128)(2,1)S(1)}, bf16[16,16,128]{2,1,0:T(8,128)(2,1)S(1)}, u32[]{:S(2)}, u32[]{:S(2)}) collective-permute-start(bf16[16,16,128]{2,1,0:T(8,128)(2,1)S(1)} %get-tuple-element.38), channel_id=1, source_target_pairs={{0,3},{1,2},{2,1},{3,0},{4,7},{5,6},{6,5},{7,4},{8,11},{9,10},{10,... | collective-permute-start | bytes 196616 | tf_op jit(solution)/shard_map/ppermute | solution.py:317
  28.4 1.2 %collective-permute-start.10 = (bf16[16,16,128]{2,1,0:T(8,128)(2,1)S(1)}, bf16[16,16,128]{2,1,0:T(8,128)(2,1)S(1)}, u32[]{:S(2)}, u32[]{:S(2)}) collective-permute-start(bf16[16,16,128]{2,1,0:T(8,128)(2,1)S(1)} %get-tuple-element.39), channel_id=1, source_target_pairs={{0,2},{1,3},{2,0},{3,1},{4,6},{5,7},{6,4},{7,5},{8,10},{9,11},{10,... | collective-permute-start | bytes 196616 | tf_op jit(solution)/shard_map/ppermute | solution.py:317
  29.6 0.6 %shard_map.93.refs_5_ = f32[256,128]{1,0:T(8,128)S(1)} custom-call(f32[64,16,128]{2,1,0:T(8,128)S(1)} %shard_map.85.panel, bf16[16,16,128]{2,1,0:T(8,128)(2,1)S(1)} %collective-permute-done.7.grad_ref.refs_0_, bf16[16,16,128]{2,1,0:T(8,128)(2,1)S(1)} %collective-permute-done.8.grad_ref.refs_1_, ...), custom_call_target="tpu_custom_call" | custom-call | tf_op jit(solution)/shard_map/pallas_call | solution.py:289
  30.2 1.4 %collective-permute-done.9.tile_ref = bf16[16,16,128]{2,1,0:T(8,128)(2,1)S(1)} collective-permute-done((bf16[16,16,128]{2,1,0:T(8,128)(2,1)S(1)}, bf16[16,16,128]{2,1,0:T(8,128)(2,1)S(1)}, u32[]{:S(2)}, u32[]{:S(2)}) %collective-permute-start.9) | collective-permute-done | bytes 65568 | tf_op jit(solution)/shard_map/ppermute | solution.py:317
  31.6 1.5 %collective-permute-done.10.refs_0_ = bf16[16,16,128]{2,1,0:T(8,128)(2,1)S(1)} collective-permute-done((bf16[16,16,128]{2,1,0:T(8,128)(2,1)S(1)}, bf16[16,16,128]{2,1,0:T(8,128)(2,1)S(1)}, u32[]{:S(2)}, u32[]{:S(2)}) %collective-permute-start.10) | collective-permute-done | bytes 65568 | tf_op jit(solution)/shard_map/ppermute | solution.py:317
  33.1 0.8 %shard_map.94 = bf16[16,16,128]{2,1,0:T(8,128)(2,1)} custom-call(f32[16,16,128]{2,1,0:T(8,128)S(1)} %shard_map.92.base, bf16[16,16,128]{2,1,0:T(8,128)(2,1)S(1)} %collective-permute-done.10.refs_0_, bf16[16,16,128]{2,1,0:T(8,128)(2,1)S(1)} %collective-permute-done.11.refs_1_, f32[256,128]{1,0:T(8,128)S(1)} %get-tuple-element.35.normed_ref.refs_7_.refs_2_, ...), custom_call_target="tpu_custom_call" | custom-call | flops 16777216 | bytes 1679360 | tf_op jit(solution)/shard_map/pallas_call | solution.py:289
  (22 shorter events, 2.0 us)
Async XLA Ops:
  1.9 5.6 %collective-permute-start.2 = (bf16[16,16,128]{2,1,0:T(8,128)(2,1)S(1)}, bf16[16,16,128]{2,1,0:T(8,128)(2,1)S(1)}, u32[]{:S(2)}, u32[]{:S(2)}) collective-permute-start(bf16[16,16,128]{2,1,0:T(8,128)(2,1)S(1)} %shard_map.77.refs_0_), channel_id=1, source_target_pairs={{0,2},{1,3},{2,0},{3,1},{4,6},{5,7},{6,4},{7,5},{8,10},{9,11},{10,... | collective-permute-start | bytes 196616 | tf_op jit(solution)/shard_map/ppermute | solution.py:317
  4.9 4.1 %collective-permute-start = (bf16[16,16,128]{2,1,0:T(8,128)(2,1)S(1)}, bf16[16,16,128]{2,1,0:T(8,128)(2,1)S(1)}, u32[]{:S(2)}, u32[]{:S(2)}) collective-permute-start(bf16[16,16,128]{2,1,0:T(8,128)(2,1)S(1)} %shard_map.77.refs_0_), channel_id=1, source_target_pairs={{0,3},{1,2},{2,1},{3,0},{4,7},{5,6},{6,5},{7,4},{8,11},{9,10},{10,... | collective-permute-start | bytes 196616 | tf_op jit(solution)/shard_map/ppermute | solution.py:317
  4.9 4.1 %collective-permute-start.1 = (bf16[16,16,128]{2,1,0:T(8,128)(2,1)S(1)}, bf16[16,16,128]{2,1,0:T(8,128)(2,1)S(1)}, u32[]{:S(2)}, u32[]{:S(2)}) collective-permute-start(bf16[16,16,128]{2,1,0:T(8,128)(2,1)S(1)} %shard_map.77.refs_0_), channel_id=1, source_target_pairs={{0,1},{1,0},{2,3},{3,2},{4,5},{5,4},{6,7},{7,6},{8,9},{9,8},{10,11... | collective-permute-start | bytes 196616 | tf_op jit(solution)/shard_map/ppermute | solution.py:317
  9.4 7.6 %collective-permute-start.3 = (bf16[16,16,128]{2,1,0:T(8,128)(2,1)S(1)}, bf16[16,16,128]{2,1,0:T(8,128)(2,1)S(1)}, u32[]{:S(2)}, u32[]{:S(2)}) collective-permute-start(bf16[16,16,128]{2,1,0:T(8,128)(2,1)S(1)} %get-tuple-element.25), channel_id=1, source_target_pairs={{0,8},{4,12},{8,0},{12,4},{1,9},{5,13},{9,1},{13,5},{2,10},{6,14},... | collective-permute-start | bytes 196616 | tf_op jit(solution)/shard_map/ppermute | solution.py:317
  12.1 6.3 %collective-permute-start.4 = (bf16[16,16,128]{2,1,0:T(8,128)(2,1)S(1)}, bf16[16,16,128]{2,1,0:T(8,128)(2,1)S(1)}, u32[]{:S(2)}, u32[]{:S(2)}) collective-permute-start(bf16[16,16,128]{2,1,0:T(8,128)(2,1)S(1)} %get-tuple-element.26), channel_id=1, source_target_pairs={{0,12},{4,8},{8,4},{12,0},{1,13},{5,9},{9,5},{13,1},{2,14},{6,10},... | collective-permute-start | bytes 196616 | tf_op jit(solution)/shard_map/ppermute | solution.py:317
  13.5 5.1 %collective-permute-start.5 = (bf16[16,16,128]{2,1,0:T(8,128)(2,1)S(1)}, bf16[16,16,128]{2,1,0:T(8,128)(2,1)S(1)}, u32[]{:S(2)}, u32[]{:S(2)}) collective-permute-start(bf16[16,16,128]{2,1,0:T(8,128)(2,1)S(1)} %get-tuple-element.27), channel_id=1, source_target_pairs={{0,4},{4,0},{8,12},{12,8},{1,5},{5,1},{9,13},{13,9},{2,6},{6,2},{1... | collective-permute-start | bytes 196616 | tf_op jit(solution)/shard_map/ppermute | solution.py:317
  18.6 4.7 %copy-start = (bf16[128,640]{1,0:T(8,128)(2,1)S(1)}, bf16[128,640]{1,0:T(8,128)(2,1)}, u32[]{:S(2)}) copy-start(bf16[128,640]{1,0:T(8,128)(2,1)} %refs_8_.1) | copy-start | bytes 491524
  18.8 6.7 %collective-permute-start.7 = (bf16[16,16,128]{2,1,0:T(8,128)(2,1)S(1)}, bf16[16,16,128]{2,1,0:T(8,128)(2,1)S(1)}, u32[]{:S(2)}, u32[]{:S(2)}) collective-permute-start(bf16[16,16,128]{2,1,0:T(8,128)(2,1)S(1)} %get-tuple-element.33.refs_0_.grad_ref), channel_id=1, source_target_pairs={{0,12},{4,8},{8,4},{12,0},{1,13},{5,9},{9,5},{13,1},{2,14},{6,10},... | collective-permute-start | bytes 196616 | tf_op jit(solution)/shard_map/ppermute | solution.py:317
  21.9 4.5 %collective-permute-start.8 = (bf16[16,16,128]{2,1,0:T(8,128)(2,1)S(1)}, bf16[16,16,128]{2,1,0:T(8,128)(2,1)S(1)}, u32[]{:S(2)}, u32[]{:S(2)}) collective-permute-start(bf16[16,16,128]{2,1,0:T(8,128)(2,1)S(1)} %get-tuple-element.33.refs_0_.grad_ref), channel_id=1, source_target_pairs={{0,4},{4,0},{8,12},{12,8},{1,5},{5,1},{9,13},{13,9},{2,6},{6,2},{1... | collective-permute-start | bytes 196616 | tf_op jit(solution)/shard_map/ppermute | solution.py:317
  22.1 5.2 %collective-permute-start.6 = (bf16[16,16,128]{2,1,0:T(8,128)(2,1)S(1)}, bf16[16,16,128]{2,1,0:T(8,128)(2,1)S(1)}, u32[]{:S(2)}, u32[]{:S(2)}) collective-permute-start(bf16[16,16,128]{2,1,0:T(8,128)(2,1)S(1)} %get-tuple-element.33.refs_0_.grad_ref), channel_id=1, source_target_pairs={{0,8},{4,12},{8,0},{12,4},{1,9},{5,13},{9,1},{13,5},{2,10},{6,14},... | collective-permute-start | bytes 196616 | tf_op jit(solution)/shard_map/ppermute | solution.py:317
  23.8 0.8 %copy-start.1 = (bf16[128,128]{1,0:T(8,128)(2,1)S(1)}, bf16[128,128]{1,0:T(8,128)(2,1)}, u32[]{:S(2)}) copy-start(bf16[128,128]{1,0:T(8,128)(2,1)} %out_weight_ref.1) | copy-start | bytes 98308
  27.5 4.1 %collective-permute-start.9 = (bf16[16,16,128]{2,1,0:T(8,128)(2,1)S(1)}, bf16[16,16,128]{2,1,0:T(8,128)(2,1)S(1)}, u32[]{:S(2)}, u32[]{:S(2)}) collective-permute-start(bf16[16,16,128]{2,1,0:T(8,128)(2,1)S(1)} %get-tuple-element.38), channel_id=1, source_target_pairs={{0,3},{1,2},{2,1},{3,0},{4,7},{5,6},{6,5},{7,4},{8,11},{9,10},{10,... | collective-permute-start | bytes 196616 | tf_op jit(solution)/shard_map/ppermute | solution.py:317
  28.4 4.8 %collective-permute-start.10 = (bf16[16,16,128]{2,1,0:T(8,128)(2,1)S(1)}, bf16[16,16,128]{2,1,0:T(8,128)(2,1)S(1)}, u32[]{:S(2)}, u32[]{:S(2)}) collective-permute-start(bf16[16,16,128]{2,1,0:T(8,128)(2,1)S(1)} %get-tuple-element.39), channel_id=1, source_target_pairs={{0,2},{1,3},{2,0},{3,1},{4,6},{5,7},{6,4},{7,5},{8,10},{9,11},{10,... | collective-permute-start | bytes 196616 | tf_op jit(solution)/shard_map/ppermute | solution.py:317
  29.5 3.6 %collective-permute-start.11 = (bf16[16,16,128]{2,1,0:T(8,128)(2,1)S(1)}, bf16[16,16,128]{2,1,0:T(8,128)(2,1)S(1)}, u32[]{:S(2)}, u32[]{:S(2)}) collective-permute-start(bf16[16,16,128]{2,1,0:T(8,128)(2,1)S(1)} %get-tuple-element.40), channel_id=1, source_target_pairs={{0,1},{1,0},{2,3},{3,2},{4,5},{5,4},{6,7},{7,6},{8,9},{9,8},{10,11... | collective-permute-start | bytes 196616 | tf_op jit(solution)/shard_map/ppermute | solution.py:317
